TPU v7x, 32 devices: a whole 2x2x4 slice. The times are simulated.
32 devices in a mesh: seq: 16 (over z, y, x), exp: 2 (over core).
Axes of the slice: x: 2, y: 2, z: 4, core: 2. Of those that a mesh axis runs over, the one named last changes fastest.
Arguments:
- queries: bfloat16 [4096, 1024], P('seq', 'exp'), may hold values from -170 to 170
- keys: bfloat16 [4096, 1024], P('seq', 'exp'), may hold values from -5 to 5
- values: bfloat16 [4096, 1024], P('seq', 'exp'), may hold values from -6 to 6
- resid: bfloat16 [4096, 2048], P(('seq', 'exp')), may hold values from -6 to 6
- pair_ids: int32 [4096], replicated, may hold values from 0 to 15, never falling along the last dimension, each value on 1 to 512 neighbouring positions
- out_weight: bfloat16 [1024, 2048], P('exp'), may hold values from -0.1875 to 0.1875
- norm_gain: float32 [2048], replicated, may hold values from 0.5 to 1.5
- experts: int32 [4096, 6], P(('seq', 'exp')), may hold values from 0 to 15, all different within a row; in each aligned block of 128 rows (0 to 127, 128 to 255, ...) at most 96 rows name the same one
- gates: float32 [4096, 6], P(('seq', 'exp')), may hold values from 0.05 to 0.5
- w_gate: bfloat16 [16, 2048, 704], P('seq', None, 'exp'), may hold values from -0.125 to 0.125
- w_up: bfloat16 [16, 2048, 704], P('seq', None, 'exp'), may hold values from -0.125 to 0.125
- w_down: bfloat16 [16, 704, 2048], P('seq', 'exp'), may hold values from -0.21875 to 0.21875
Outputs:
- mixed: bfloat16 [4096, 2048], P(('seq', 'exp'))
Inputs may be any that keep to these rules, and one draw needn't show every extreme that they name: In the aligned blocks of 128 rows no expert is named more than 96 times, a bound that some block reaches; each row names 6 different experts. `pair_ids`: pair numbers never fall along the sequence; each pair has 1 to 512 tokens, one exactly that many.
All inputs are finite; a program needn't handle non-finite values.
Results may differ from a plain program's by a relative error of at most 0.012.
Values may be sent and summed in bfloat16 or wider, within the bound.
No kernel may reach another device: no remote copies, remote signals or barrier semaphores. Data moves between devices by JAX's collectives and lax.ppermute only.
A program may use at most 128 MiB of HBM per device.

v0:
```python
import math

import jax
import jax.numpy as jnp
from jax import lax
from jax.sharding import PartitionSpec as P

HD = 128
TOP = 6


def with_halo(cells, sides, width):
    for axis, dim in sides:
        count = lax.axis_size(axis)
        ends = count - 1
        head = lax.slice_in_dim(cells, 0, width, axis=dim)
        tail = lax.slice_in_dim(cells, cells.shape[dim] - width, cells.shape[dim], axis=dim)
        cells = jnp.concatenate(
            [
                lax.ppermute(tail, axis, [(i, (i + 1) % count) for i in range(ends)]),
                cells,
                lax.ppermute(head, axis, [((i + 1) % count, i) for i in range(ends)]),
            ],
            axis=dim,
        )
    return cells


def send_back(result):
    return lax.all_to_all(result, "seq", split_axis=0, concat_axis=0, tiled=True)


def shards(
    queries,
    keys,
    values,
    resid,
    pair_ids,
    out_weight,
    norm_gain,
    experts,
    gates,
    w_gate,
    w_up,
    w_down,
):
    tok_rows = queries.shape[0]
    local_width = queries.shape[1]
    local_heads = local_width // HD
    shard = lax.axis_index("seq")
    stacked = jnp.stack([keys, values])
    widened = with_halo(stacked, (("seq", 1),), tok_rows)
    id_pad = jnp.pad(pair_ids, (tok_rows, tok_rows), constant_values=-1)
    key_ids = lax.dynamic_slice_in_dim(id_pad, shard * tok_rows, 3 * tok_rows, 0)
    query_ids = lax.dynamic_slice_in_dim(id_pad, shard * tok_rows + tok_rows, tok_rows, 0)
    query_pos = jnp.arange(tok_rows, dtype=jnp.int32) + tok_rows
    key_pos = jnp.arange(3 * tok_rows, dtype=jnp.int32)
    allowed = (query_ids[:, None] == key_ids[None, :]) & (
        jnp.abs(query_pos[:, None] - key_pos[None, :]) < tok_rows
    )
    query_heads = queries.reshape(tok_rows, local_heads, HD)
    key_heads = widened[0].reshape(3 * tok_rows, local_heads, HD)
    value_heads = widened[1].reshape(3 * tok_rows, local_heads, HD)
    score = jnp.einsum(
        "qhd,khd->hqk", query_heads, key_heads, preferred_element_type=jnp.float32
    ) / math.sqrt(HD)
    score = jnp.where(allowed[None], score, -jnp.inf)
    top = jnp.max(score, axis=-1, keepdims=True)
    weights = jnp.exp(score - top)
    probs = (weights / jnp.sum(weights, axis=-1, keepdims=True)).astype(jnp.bfloat16)
    attended = jnp.einsum("hqk,khd->qhd", probs, value_heads, preferred_element_type=jnp.float32)
    attended = attended.reshape(tok_rows, local_width).astype(jnp.bfloat16)
    moe_rows = resid.shape[0]
    projected = lax.psum(
        jnp.dot(attended, out_weight, preferred_element_type=jnp.float32).astype(jnp.bfloat16),
        "exp",
    ).astype(jnp.float32)
    projected = lax.dynamic_slice_in_dim(projected, lax.axis_index("exp") * moe_rows, moe_rows, 0)
    stream = resid.astype(jnp.float32) + projected
    meansq = jnp.mean(stream * stream, axis=-1, keepdims=True)
    normed = (stream * lax.rsqrt(meansq + 1e-05) * norm_gain).astype(jnp.bfloat16)
    n_experts = lax.axis_size("seq") * w_gate.shape[0]
    capacity = 2 * moe_rows * TOP // n_experts
    flat_experts = experts.reshape(-1)
    onehot = (flat_experts[:, None] == jnp.arange(n_experts, dtype=jnp.int32)[None, :]).astype(
        jnp.int32
    )
    ranks = jnp.cumsum(onehot, axis=0) - onehot
    slot_index = jnp.sum(ranks * onehot, axis=1)
    destination = flat_experts * capacity + slot_index
    token_of = jnp.arange(moe_rows * TOP, dtype=jnp.int32) // TOP
    outgoing = (
        jnp.zeros((n_experts * capacity, normed.shape[1]), jnp.bfloat16)
        .at[destination]
        .set(normed[token_of])
    )
    outgoing = outgoing.reshape(n_experts, capacity, normed.shape[1])
    arrived = lax.all_to_all(outgoing, "seq", split_axis=0, concat_axis=0, tiled=True)
    sources = arrived.shape[0]
    slots = arrived.shape[1]
    inputs = arrived.reshape(sources * slots, arrived.shape[2])
    group = lax.all_gather(inputs, "exp", axis=0, tiled=True)
    gate_part = jnp.dot(group, w_gate[0], preferred_element_type=jnp.float32)
    up_part = jnp.dot(group, w_up[0], preferred_element_type=jnp.float32)
    act = (jax.nn.silu(gate_part) * up_part).astype(jnp.bfloat16)
    result = lax.psum_scatter(
        jnp.dot(act, w_down[0], preferred_element_type=jnp.float32).astype(jnp.bfloat16),
        "exp",
        scatter_dimension=0,
        tiled=True,
    )
    result = result.reshape(sources, slots, result.shape[1])
    back = send_back(result)
    gathered = back.reshape(n_experts * capacity, back.shape[2])[destination]
    gathered = gathered.reshape(moe_rows, TOP, gathered.shape[1]).astype(jnp.float32)
    mixture = jnp.einsum("mk,mkd->md", gates, gathered)
    return (stream + mixture).astype(jnp.bfloat16)


def solution(mesh):
    in_specs = (
        P("seq", "exp"),
        P("seq", "exp"),
        P("seq", "exp"),
        P(("seq", "exp"), None),
        P(),
        P("exp", None),
        P(),
        P(("seq", "exp"), None),
        P(("seq", "exp"), None),
        P("seq", None, "exp"),
        P("seq", None, "exp"),
        P("seq", "exp", None),
    )
    out_specs = P(("seq", "exp"), None)
    return jax.shard_map(shards, mesh=mesh, in_specs=in_specs, out_specs=out_specs, check_vma=False)
```

profile of v0, /device:TPU:10, one launch (start us, length us, event | category | flops | bytes accessed | tf_op | source)
XLA Modules:
  0.0 487.5 jit_solution(12842179673673021849)
XLA Ops:
  6.5 1.2 copy.16
  7.8 1.1 copy.17
  8.9 0.1 pad_maximum_fusion.1
  8.9 3.4 collective-permute-start
  12.3 2.4 collective-permute-start.1
  14.8 0.8 pad_dynamic-slice_fusion.1
  15.6 0.8 pad_dynamic-slice_fusion
  16.4 0.3 fusion.18
  16.6 0.0 copy-start.4
  16.6 19.2 %collective-permute-done = bf16[2,256,512]{1,2,0:T(8,128)(2,1)} collective-permute-done((bf16[2,256,512]{1,2,0:T(8,128)(2,1)S(1)}, bf16[2,256,512]{1,2,0:T(8,128)(2,1)}, u32[]{:S(2)}, u32[]{:S(2)}) %collective-permute-start) | collective-permute-done | bytes 524320 | tf_op jit(solution)/shard_map/ppermute | solution.py:20
  35.8 1.0 collective-permute-done.1
  36.8 1.3 pad_maximum_fusion
  38.1 0.1 fusion.31
  38.2 0.6 fusion.19
  38.8 1.6 fusion.32
  40.5 0.4 fusion.16
  40.8 0.0 copy-start.5
  40.9 0.0 copy-start.6
  40.9 1.7 convolution_convert_fusion.1
  42.6 0.0 all-reduce.3.cloned.1.call-update
  42.6 0.0 all-gather.2.cloned.1.call-start
  42.7 0.1 copy.22
  42.8 0.1 eq.49
  43.0 0.1 eq.45
  43.1 1.9 reduce-window.6
  45.0 0.3 slice_reduce_fusion
  45.3 0.1 copy.21
  45.4 0.1 mul.56
  45.6 0.1 fusion.24
  45.7 17.1 %all-reduce.3.cloned.1.call-done = bf16[256,2048]{1,0:T(8,128)(2,1)} async-done(((bf16[256,2048]{1,0:T(8,128)(2,1)}), bf16[256,2048]{1,0:T(8,128)(2,1)}) %all-reduce.3.cloned.1.call-update) | async-done | bytes 1048592 | tf_op jit(solution)/shard_map/psum | solution.py:74
  62.9 1.3 multiply_reduce_fusion
  64.2 1.3 multiply_convert_fusion
  65.5 24.2 %scatter_custom_fusion = bf16[1536,2048]{1,0:T(8,128)(2,1)} fusion(s32[768]{0:T(1024)S(1)} %fusion.26, bf16[128,2048]{1,0:T(8,128)(2,1)S(1)} %multiply_convert_fusion, s32[1024]{0:T(1024)S(1)} %pad_clamp_fusion.1, bf16[]{:T(256)} %constant.50.clone.1), kind=kCustom, calls=%fused_computation.8 | custom fusion | bytes 6291458 | tf_op jit(solution)/shard_map/scatter | solution.py:95
  89.7 144.7 %all_to_all.10 = bf16[16,96,2048]{2,1,0:T(8,128)(2,1)} all-to-all(bf16[16,96,2048]{2,1,0:T(8,128)(2,1)} %bitcast.73), channel_id=1, replica_groups=mesh['seq'=16,'exp'=2] {'seq'}, dimensions={0} | all-to-all | bytes 12582912 | tf_op jit(solution)/shard_map/all_to_all | solution.py:98
  234.4 0.0 all-gather.2.cloned.1.call-update
  234.4 0.0 reduce-scatter.2.cloned.1.call-start
  234.4 24.7 %all-gather.2.cloned.1.call-done = bf16[3072,2048]{1,0:T(8,128)(2,1)} async-done(((bf16[1536,2048]{1,0:T(8,128)(2,1)}), bf16[3072,2048]{1,0:T(8,128)(2,1)}) %all-gather.2.cloned.1.call-update) | async-done | bytes 12582928 | tf_op jit(solution)/shard_map/all_gather | solution.py:102
  259.1 9.8 %fusion.14 = f32[3072,352]{0,1:T(8,128)} fusion(bf16[3072,2048]{1,0:T(8,128)(2,1)} %all-gather.2.cloned.1.call-done, bf16[1,2048,352]{1,2,0:T(8,128)(2,1)S(1)} %copy-done.8), kind=kOutput, calls=%fused_computation.23 | convolution fusion | flops 4429185024 | bytes 18350080 | tf_op jit(solution)/shard_map/dot_general | solution.py:103
  268.9 18.6 %convolution_convert_fusion = bf16[3072,2048]{1,0:T(8,128)(2,1)} fusion(bf16[3072,2048]{1,0:T(8,128)(2,1)} %all-gather.2.cloned.1.call-done, f32[3072,352]{0,1:T(8,128)} %fusion.14, bf16[1,352,2048]{2,1,0:T(8,128)(2,1)} %param.23, bf16[1,2048,352]{1,2,0:T(8,128)(2,1)} %param.22), kind=kOutput, calls=%fused_computation.4 | convolution fusion | flops 8871149568 | bytes 32374784 | tf_op jit(solution)/shard_map/dot_general | solution.py:107
  287.5 0.0 reduce-scatter.2.cloned.1.call-update
  287.5 22.8 %reduce-scatter.2.cloned.1.call-done = bf16[1536,2048]{1,0:T(8,128)(2,1)} async-done(((bf16[3072,2048]{1,0:T(8,128)(2,1)}), bf16[1536,2048]{1,0:T(8,128)(2,1)}) %reduce-scatter.2.cloned.1.call-update) | async-done | bytes 6291472 | tf_op jit(solution)/shard_map/reduce_scatter | solution.py:106
  310.3 7.1 %all-to-all-start.1 = ((bf16[16,96,2048]{2,1,0:T(8,128)(2,1)}), bf16[16,96,2048]{2,1,0:T(8,128)(2,1)}, u32[]{:S(2)}, u32[]{:S(2)}) async-start(bf16[16,96,2048]{2,1,0:T(8,128)(2,1)} %bitcast.74), calls=%async_computation.2 | async-start | bytes 12582912 | tf_op jit(solution)/shard_map/all_to_all | solution.py:30
  317.4 0.2 copy.27
  317.6 141.4 %all-to-all-done.1 = bf16[16,96,2048]{2,1,0:T(8,128)(2,1)} async-done(((bf16[16,96,2048]{2,1,0:T(8,128)(2,1)}), bf16[16,96,2048]{2,1,0:T(8,128)(2,1)}, u32[]{:S(2)}, u32[]{:S(2)}) %all-to-all-start.1) | async-done | bytes 6291488 | tf_op jit(solution)/shard_map/all_to_all | solution.py:30
  459.0 10.8 %gather_fusion = bf16[768,2048]{1,0:T(8,128)(2,1)} fusion(bf16[1536,2048]{1,0:T(8,128)(2,1)} %bitcast.14, s32[1024]{0:T(1024)S(1)} %pad_clamp_fusion), kind=kCustom, calls=%fused_computation.1 | custom fusion | bytes 6294528 | tf_op jit(solution)/shard_map/gather | solution.py:114
  469.7 6.4 %reshape.179 = bf16[128,6,2048]{2,1,0:T(8,128)(2,1)} reshape(bf16[768,2048]{1,0:T(8,128)(2,1)} %gather_fusion) | data formatting | bytes 6291456 | tf_op jit(solution)/shard_map/reshape | solution.py:115
  476.1 3.5 fusion.33
  479.7 1.3 fusion.17
  (24 shorter events, 0.1 us)
Async XLA Ops:
  6.5 34.4 %copy-start = (bf16[512,2048]{1,0:T(8,128)(2,1)S(1)}, bf16[512,2048]{1,0:T(8,128)(2,1)}, u32[]{:S(2)}) copy-start(bf16[512,2048]{1,0:T(8,128)(2,1)} %param.17) | copy-start | bytes 6291460
  6.5 56.3 %all-reduce.3.cloned.1.call-start = ((), (), s32[]{:S(2)}) async-start(), calls=%async_computation.3 | async-start | bytes 2097152 | tf_op jit(solution)/shard_map/psum | solution.py:74
  8.9 26.9 %collective-permute-start = (bf16[2,256,512]{1,2,0:T(8,128)(2,1)S(1)}, bf16[2,256,512]{1,2,0:T(8,128)(2,1)}, u32[]{:S(2)}, u32[]{:S(2)}) collective-permute-start(bf16[2,256,512]{1,2,0:T(8,128)(2,1)S(1)} %pad_maximum_fusion.1), channel_id=1, source_target_pairs={{0,2},{2,4},{4,6},{6,8},{8,10},{10,12},{12,14},{14,16},{16,18},{18... | collective-permute-start | bytes 1572872 | tf_op jit(solution)/shard_map/ppermute | solution.py:20
  12.3 24.4 %collective-permute-start.1 = (bf16[2,256,512]{1,2,0:T(8,128)(2,1)S(1)}, bf16[2,256,512]{1,2,0:T(8,128)(2,1)}, u32[]{:S(2)}, u32[]{:S(2)}) collective-permute-start(bf16[2,256,512]{1,2,0:T(8,128)(2,1)S(1)} %pad_maximum_fusion.1), channel_id=1, source_target_pairs={{2,0},{4,2},{6,4},{8,6},{10,8},{12,10},{14,12},{16,14},{18,16},{20... | collective-permute-start | bytes 1572872 | tf_op jit(solution)/shard_map/ppermute | solution.py:22
  16.6 21.6 %copy-start.4 = (bf16[256,512]{1,0:T(8,128)(2,1)S(1)}, bf16[256,512]{1,0:T(8,128)(2,1)}, u32[]{:S(2)}) copy-start(bf16[256,512]{1,0:T(8,128)(2,1)} %param.12) | copy-start | bytes 786436
  40.8 1.9 copy-start.5
  40.9 22.0 %copy-start.2 = (bf16[128,2048]{1,0:T(8,128)(2,1)S(1)}, bf16[128,2048]{1,0:T(8,128)(2,1)}, u32[]{:S(2)}) copy-start(bf16[128,2048]{1,0:T(8,128)(2,1)} %param.15) | copy-start | bytes 1572868
  40.9 23.3 %copy-start.6 = (f32[2048]{0:T(1024)S(1)}, f32[2048]{0:T(1024)}, u32[]{:S(2)}) copy-start(f32[2048]{0:T(1024)} %param.18) | copy-start | bytes 24580
  42.6 216.5 %all-gather.2.cloned.1.call-start = ((), (), s32[]{:S(2)}) async-start(), calls=%async_computation.4 | async-start | bytes 18874368 | tf_op jit(solution)/shard_map/all_gather | solution.py:102
  234.4 24.8 %copy-start.8 = (bf16[1,2048,352]{1,2,0:T(8,128)(2,1)S(1)}, bf16[1,2048,352]{1,2,0:T(8,128)(2,1)}, u32[]{:S(2)}) copy-start(bf16[1,2048,352]{1,2,0:T(8,128)(2,1)} %param.21) | copy-start | bytes 4325380
  234.4 75.9 %reduce-scatter.2.cloned.1.call-start = ((), (), s32[]{:S(2)}) async-start(), calls=%async_computation.5 | async-start | bytes 18874368 | tf_op jit(solution)/shard_map/reduce_scatter | solution.py:106
  310.3 7.1 %copy-start.7 = (f32[128,6]{0,1:T(8,128)S(1)}, f32[128,6]{0,1:T(8,128)}, u32[]{:S(2)}) copy-start(f32[128,6]{0,1:T(8,128)} %param.20) | copy-start | bytes 9220
  310.3 148.6 %all-to-all-start.1 = ((bf16[16,96,2048]{2,1,0:T(8,128)(2,1)}), bf16[16,96,2048]{2,1,0:T(8,128)(2,1)}, u32[]{:S(2)}, u32[]{:S(2)}) async-start(bf16[16,96,2048]{2,1,0:T(8,128)(2,1)} %bitcast.74), calls=%async_computation.2 | async-start | bytes 12582912 | tf_op jit(solution)/shard_map/all_to_all | solution.py:30
  469.7 11.2 %copy-start.1 = (bf16[512,2048]{1,0:T(8,128)(2,1)S(1)}, bf16[512,2048]{1,0:T(8,128)(2,1)}, u32[]{:S(2)}) copy-start(bf16[512,2048]{1,0:T(8,128)(2,1)} %param.17) | copy-start | bytes 6291460
  476.1 3.5 copy-start.3
Sparse Core Ops, SparseCore 0:
  42.8 20.0 all-reduce.2
  234.5 24.5 all-gather.1
  287.6 22.6 reduce-scatter.1
where the time goes:
time: 490 us; the launch traced here: 487 us
  waiting for transfers between devices  226 us (46%)
  blocking collectives  145 us (30%)
  local copies, waits for them, and re-layouts  45.7 us (9%)
  matrix products  34.6 us (7%)
  between operations  13.4 us (3%)
  starting transfers between devices  13 us (3%)
  other arithmetic  9.94 us (2%)
    all_to_all x1, blocking collectives, shards(): lax.all_to_all(outgoing, 'seq', split_axis=0, concat_axis=0, tiled=True)  145 us
    all_to_all x1, waiting for transfers between devices, send_back(): lax.all_to_all(result, 'seq', split_axis=0, concat_axis=0, tiled=True)  141 us
    all_gather x1, waiting for transfers between devices, shards(): group = lax.all_gather(inputs, 'exp', axis=0, tiled=True)  24.7 us
    scatter x1, local copies, waits for them, and re-layouts, shards(): outgoing = jnp.zeros((n_experts * capacity, normed.shape[1]), jnp.bfloat1...  24.2 us
    reduce_scatter x1, waiting for transfers between devices, shards(): lax.psum_scatter(jnp.dot(act, w_down[0], preferred_element_type=jnp.float...  22.8 us
    ppermute x1, waiting for transfers between devices, with_halo(): lax.ppermute(tail, axis, [(i, (i + 1) % count) for i in range(ends)])  19.2 us
    dot_general x1, matrix products, shards(): jnp.dot(act, w_down[0], preferred_element_type=jnp.float32)  18.6 us
    psum x1, waiting for transfers between devices, shards(): lax.psum(jnp.dot(attended, out_weight, preferred_element_type=jnp.float32...  17.1 us
  transfers between devices with their start and end apart: 6, of which 6 were waited for; matrix products, arithmetic and copies ran while one was open for 1% of the time, Pallas kernels for 0%

commit v1 on v0

v1 whole, which is shorter than its diff:
```python
import math

import jax
import jax.numpy as jnp
from jax import lax
from jax.sharding import PartitionSpec as P

HD = 128
TOP = 6
SWAP = [(0, 1), (1, 0)]


def with_halo(cells, width):
    count = lax.axis_size("seq")
    ends = count - 1
    before = lax.ppermute(cells, "seq", [(i, i + 1) for i in range(ends)])
    after = lax.ppermute(cells, "seq", [(i + 1, i) for i in range(ends)])
    return jnp.concatenate([before, cells, after], axis=1)


def both_halves(part, core, axis):
    other = lax.ppermute(part, "exp", SWAP)
    low = jnp.where(core == 0, part, other)
    high = jnp.where(core == 0, other, part)
    return jnp.concatenate([low, high], axis=axis)


def shards(
    queries,
    keys,
    values,
    resid,
    pair_ids,
    out_weight,
    norm_gain,
    experts,
    gates,
    w_gate,
    w_up,
    w_down,
):
    tok_rows = queries.shape[0]
    local_width = queries.shape[1]
    local_heads = local_width // HD
    moe_rows = resid.shape[0]
    shard = lax.axis_index("seq")
    core = lax.axis_index("exp")
    widened = with_halo(jnp.stack([keys, values]), tok_rows)
    n_experts = lax.axis_size("seq")
    per_expert = jnp.sum(
        jnp.where(
            experts[:, :, None] == jnp.arange(n_experts, dtype=jnp.int32)[None, None, :],
            gates[:, :, None],
            0.0,
        ),
        axis=1,
    )
    all_gates = lax.all_gather(per_expert, "seq", axis=0, tiled=True)
    my_gate = lax.dynamic_slice_in_dim(all_gates, shard, 1, 1)
    out_other = lax.ppermute(out_weight, "exp", SWAP)
    gate_w = both_halves(w_gate[0], core, 1)
    up_w = both_halves(w_up[0], core, 1)
    down_w = both_halves(w_down[0], core, 0)

    id_pad = jnp.pad(pair_ids, (tok_rows, tok_rows), constant_values=-1)
    key_ids = lax.dynamic_slice_in_dim(id_pad, shard * tok_rows, 3 * tok_rows, 0)
    query_ids = lax.dynamic_slice_in_dim(id_pad, shard * tok_rows + tok_rows, tok_rows, 0)
    query_pos = jnp.arange(tok_rows, dtype=jnp.int32) + tok_rows
    key_pos = jnp.arange(3 * tok_rows, dtype=jnp.int32)
    allowed = (query_ids[:, None] == key_ids[None, :]) & (
        jnp.abs(query_pos[:, None] - key_pos[None, :]) < tok_rows
    )
    query_heads = queries.reshape(tok_rows, local_heads, HD)
    key_heads = widened[0].reshape(3 * tok_rows, local_heads, HD)
    value_heads = widened[1].reshape(3 * tok_rows, local_heads, HD)
    score = jnp.einsum(
        "qhd,khd->hqk", query_heads, key_heads, preferred_element_type=jnp.float32
    ) / math.sqrt(HD)
    score = jnp.where(allowed[None], score, -jnp.inf)
    top = jnp.max(score, axis=-1, keepdims=True)
    weights = jnp.exp(score - top)
    probs = (weights / jnp.sum(weights, axis=-1, keepdims=True)).astype(jnp.bfloat16)
    attended = jnp.einsum("hqk,khd->qhd", probs, value_heads, preferred_element_type=jnp.float32)
    attended = attended.reshape(tok_rows, local_width).astype(jnp.bfloat16)
    mine = lax.dynamic_slice_in_dim(attended, core * moe_rows, moe_rows, 0)
    theirs = lax.dynamic_slice_in_dim(attended, (1 - core) * moe_rows, moe_rows, 0)
    received = lax.ppermute(theirs, "exp", SWAP)
    projected = jnp.dot(mine, out_weight, preferred_element_type=jnp.float32) + jnp.dot(
        received, out_other, preferred_element_type=jnp.float32
    )
    stream = resid.astype(jnp.float32) + projected
    meansq = jnp.mean(stream * stream, axis=-1, keepdims=True)
    normed = (stream * lax.rsqrt(meansq + 1e-05) * norm_gain).astype(jnp.bfloat16)

    group = lax.all_gather(normed, "seq", axis=0, tiled=True)
    gate_part = jnp.dot(group, gate_w, preferred_element_type=jnp.float32)
    up_part = jnp.dot(group, up_w, preferred_element_type=jnp.float32)
    act = (jax.nn.silu(gate_part) * up_part).astype(jnp.bfloat16)
    result = jnp.dot(act, down_w, preferred_element_type=jnp.float32) * my_gate
    mixture = lax.psum_scatter(
        result.astype(jnp.bfloat16), "seq", scatter_dimension=0, tiled=True
    )
    return (stream + mixture.astype(jnp.float32)).astype(jnp.bfloat16)


def solution(mesh):
    in_specs = (
        P("seq", "exp"),
        P("seq", "exp"),
        P("seq", "exp"),
        P(("seq", "exp"), None),
        P(),
        P("exp", None),
        P(),
        P(("seq", "exp"), None),
        P(("seq", "exp"), None),
        P("seq", None, "exp"),
        P("seq", None, "exp"),
        P("seq", "exp", None),
    )
    out_specs = P(("seq", "exp"), None)
    return jax.shard_map(shards, mesh=mesh, in_specs=in_specs, out_specs=out_specs, check_vma=False)
```

time: 490 us -> 378 us (0.77)
  blocking collectives: 145 us -> 29.4 us
  waiting for transfers between devices: 226 us -> 273 us
  local copies, waits for them, and re-layouts: 45.7 us -> 4.55 us
  other arithmetic: 9.94 us -> 16.4 us
  starting transfers between devices: 13 us -> 7.6 us
    reduce_scatter x1, waiting for transfers between devices: 22.8 us -> 181 us  [shards(): lax.psum_scatter(result.astype(jnp.bfloat16), 'seq', scatter_dimension=0,...]
    all_to_all x1 -> x0, blocking collectives: 145 us -> none  [shards(): lax.all_to_all(outgoing, 'seq', split_axis=0, concat_axis=0, tiled=True)]
    all_to_all x1 -> x0, waiting for transfers between devices: 141 us -> none  [send_back(): lax.all_to_all(result, 'seq', split_axis=0, concat_axis=0, tiled=True)]
    all_gather x1, waiting for transfers between devices: 24.7 us -> 72.8 us  [shards(): group = lax.all_gather(normed, 'seq', axis=0, tiled=True)]
    all_gather x0 -> x1, blocking collectives: none -> 29.4 us  [shards(): all_gates = lax.all_gather(per_expert, 'seq', axis=0, tiled=True)]
    scatter x1 -> x0, local copies, waits for them, and re-layouts: 24.2 us -> none  [shards(): outgoing = jnp.zeros((n_experts * capacity, normed.shape[1]), jnp.bfloat1...]
    psum x1 -> x0, waiting for transfers between devices: 17.1 us -> none  [shards(): lax.psum(jnp.dot(attended, out_weight, preferred_element_type=jnp.float32...]
    gather x1 -> x0, local copies, waits for them, and re-layouts: 10.8 us -> none  [shards(): gathered = back.reshape(n_experts * capacity, back.shape[2])[destination]]
  transfers between devices with their start and end apart: 6 -> 9, of which waited for: 6 -> 4; matrix products, arithmetic and copies ran while one was open for 1% -> 4% of each run, Pallas kernels for 0% -> 0%
where the time goes in v1:
time: 378 us; the launch traced here: 377 us
  waiting for transfers between devices  273 us (72%)
  matrix products  32.9 us (9%)
  blocking collectives  29.4 us (8%)
  other arithmetic  16.4 us (4%)
  between operations  13.6 us (4%)
  starting transfers between devices  7.6 us (2%)
  local copies, waits for them, and re-layouts  4.55 us (1%)
    reduce_scatter x1, waiting for transfers between devices, shards(): lax.psum_scatter(result.astype(jnp.bfloat16), 'seq', scatter_dimension=0,...  181 us
    all_gather x1, waiting for transfers between devices, shards(): group = lax.all_gather(normed, 'seq', axis=0, tiled=True)  72.8 us
    all_gather x1, blocking collectives, shards(): all_gates = lax.all_gather(per_expert, 'seq', axis=0, tiled=True)  29.4 us
    dot_general x1, matrix products, shards(): result = jnp.dot(act, down_w, preferred_element_type=jnp.float32) * my_gate  19.7 us
    dot_general x1, matrix products, shards(): up_part = jnp.dot(group, up_w, preferred_element_type=jnp.float32)  11.1 us
    ppermute x1, waiting for transfers between devices, with_halo(): before = lax.ppermute(cells, 'seq', [(i, i + 1) for i in range(ends)])  11 us
    select_n x3, other arithmetic, both_halves(): low = jnp.where(core == 0, part, other)  8.82 us
    ppermute x1, waiting for transfers between devices, with_halo(): after = lax.ppermute(cells, 'seq', [(i + 1, i) for i in range(ends)])  8.35 us
  transfers between devices with their start and end apart: 9, of which 4 were waited for; matrix products, arithmetic and copies ran while one was open for 4% of the time, Pallas kernels for 0%

profile of v1, /device:TPU:10, one launch (start us, length us, event | category | flops | bytes accessed | tf_op | source)
XLA Modules:
  0.0 377.3 jit_solution(9950768803270788607)
XLA Ops:
  6.5 1.1 copy.25
  7.7 1.1 copy.26
  8.8 0.1 pad_maximum_fusion.1
  8.8 2.4 collective-permute-start.1
  11.3 4.3 %collective-permute-start = (bf16[2,256,512]{1,2,0:T(8,128)(2,1)S(1)}, bf16[2,256,512]{1,2,0:T(8,128)(2,1)}, u32[]{:S(2)}, u32[]{:S(2)}) collective-permute-start(bf16[2,256,512]{1,2,0:T(8,128)(2,1)S(1)} %pad_maximum_fusion.1), channel_id=1, source_target_pairs={{0,2},{2,4},{4,6},{6,8},{8,10},{10,12},{12,14},{14,16},{16,18},{18... | collective-permute-start | bytes 1572872 | tf_op jit(solution)/shard_map/ppermute | solution.py:16
  15.6 0.1 collective-permute-start.3
  15.7 0.8 pad_dynamic-slice_fusion.1
  16.4 0.8 pad_dynamic-slice_fusion
  17.2 1.0 fusion.26
  18.2 8.3 %collective-permute-done.1 = bf16[2,256,512]{1,2,0:T(8,128)(2,1)} collective-permute-done((bf16[2,256,512]{1,2,0:T(8,128)(2,1)S(1)}, bf16[2,256,512]{1,2,0:T(8,128)(2,1)}, u32[]{:S(2)}, u32[]{:S(2)}) %collective-permute-start.1) | collective-permute-done | bytes 524320 | tf_op jit(solution)/shard_map/ppermute | solution.py:17
  26.5 11.0 %collective-permute-done = bf16[2,256,512]{1,2,0:T(8,128)(2,1)} collective-permute-done((bf16[2,256,512]{1,2,0:T(8,128)(2,1)S(1)}, bf16[2,256,512]{1,2,0:T(8,128)(2,1)}, u32[]{:S(2)}, u32[]{:S(2)}) %collective-permute-start) | collective-permute-done | bytes 524320 | tf_op jit(solution)/shard_map/ppermute | solution.py:16
  37.6 1.3 pad_maximum_fusion
  38.9 0.1 fusion.39
  39.0 0.0 copy-start.6
  39.0 0.6 fusion.27
  39.6 0.3 copy-done.6
  39.9 1.6 fusion.40
  41.5 0.0 copy-start.1
  41.5 0.4 fusion.25
  41.9 0.0 copy-start.5
  42.0 0.1 collective-permute-start.2
  42.0 1.1 copy-done.1
  43.1 0.5 fusion.30
  43.6 0.0 copy-start.7
  43.6 0.0 copy-start.8
  43.6 0.0 copy-start.9
  43.6 0.0 collective-permute-done.2
  43.6 0.0 collective-permute-done.3
  43.7 0.6 multiply_reduce_fusion
  44.3 0.0 copy-done.7
  44.3 0.9 multiply_convert_fusion.3
  45.2 0.0 all-gather.2.cloned.1.call-update
  45.3 0.0 reduce-scatter.2.cloned.1.call-start
  45.3 0.1 collective-permute-start.6
  45.4 0.5 collective-permute-start.5
  45.9 0.1 collective-permute-start.4
  46.0 29.4 %all_gather.7 = f32[2048,16]{0,1:T(8,128)S(1)} all-gather(f32[128,16]{0,1:T(8,128)S(1)} %select_reduce_fusion), channel_id=1, replica_groups=mesh['seq'=16,'exp'=2] {'seq'}, dimensions={0}, use_global_device_ids=true | all-gather | bytes 139264 | tf_op jit(solution)/shard_map/all_gather | solution.py:58
  75.4 0.0 copy-start.2
  75.4 0.0 collective-permute-done.6
  75.4 3.7 broadcast_select_fusion.1
  79.1 3.3 broadcast_select_fusion.3
  82.4 1.8 broadcast_select_fusion.5
  84.3 72.8 %all-gather.2.cloned.1.call-done = bf16[2048,2048]{1,0:T(8,128)(2,1)} async-done(((bf16[128,2048]{1,0:T(8,128)(2,1)}), bf16[2048,2048]{1,0:T(8,128)(2,1)}) %all-gather.2.cloned.1.call-update) | async-done | bytes 8388624 | tf_op jit(solution)/shard_map/all_gather | solution.py:95
  157.0 11.1 %fusion.11 = f32[2048,704]{0,1:T(8,128)} fusion(bf16[2048,2048]{1,0:T(8,128)(2,1)} %all-gather.2.cloned.1.call-done, bf16[2048,352]{0,1:T(8,128)(2,1)} %get-tuple-element.10, bf16[2048,352]{0,1:T(8,128)(2,1)} %get-tuple-element.9), kind=kOutput, calls=%fused_computation.10 | convolution fusion | flops 5911347200 | bytes 17039360 | tf_op jit(solution)/shard_map/dot_general | solution.py:97
  168.1 19.7 %multiply_convert_fusion = bf16[2048,2048]{1,0:T(8,128)(2,1)} fusion(f32[2048]{0:T(1024)S(1)} %bitcast.53, f32[2048,704]{0,1:T(8,128)} %fusion.11, bf16[2048,2048]{1,0:T(8,128)(2,1)} %all-gather.2.cloned.1.call-done, bf16[2048,352]{0,1:T(8,128)(2,1)} %get-tuple-element.8, bf16[2048,352]{0,1:T(8,128)(2,1)} %get-tuple-element.7, ...), kind=kOutput, calls=%fused_computation.1 | convolution fusion | flops 11839733760 | bytes 28319744 | tf_op jit(solution)/shard_map/dot_general | solution.py:99
  187.9 0.0 reduce-scatter.2.cloned.1.call-update
  187.9 180.6 %reduce-scatter.2.cloned.1.call-done = bf16[128,2048]{1,0:T(8,128)(2,1)} async-done(((bf16[2048,2048]{1,0:T(8,128)(2,1)}), bf16[128,2048]{1,0:T(8,128)(2,1)}) %reduce-scatter.2.cloned.1.call-update) | async-done | bytes 524304 | tf_op jit(solution)/shard_map/reduce_scatter | solution.py:100
  368.5 1.9 add_convert_fusion
  (17 shorter events, 0.1 us)
Async XLA Ops:
  6.5 32.5 %copy-start = (bf16[256,512]{1,0:T(8,128)(2,1)S(1)}, bf16[256,512]{1,0:T(8,128)(2,1)}, u32[]{:S(2)}) copy-start(bf16[256,512]{1,0:T(8,128)(2,1)} %param.12) | copy-start | bytes 786436
  6.5 150.5 %all-gather.2.cloned.1.call-start = ((), (), s32[]{:S(2)}) async-start(), calls=%async_computation.1 | async-start | bytes 8912896 | tf_op jit(solution)/shard_map/all_gather | solution.py:95
  8.8 17.7 %collective-permute-start.1 = (bf16[2,256,512]{1,2,0:T(8,128)(2,1)S(1)}, bf16[2,256,512]{1,2,0:T(8,128)(2,1)}, u32[]{:S(2)}, u32[]{:S(2)}) collective-permute-start(bf16[2,256,512]{1,2,0:T(8,128)(2,1)S(1)} %pad_maximum_fusion.1), channel_id=1, source_target_pairs={{2,0},{4,2},{6,4},{8,6},{10,8},{12,10},{14,12},{16,14},{18,16},{20... | collective-permute-start | bytes 1572872 | tf_op jit(solution)/shard_map/ppermute | solution.py:17
  11.3 26.3 %collective-permute-start = (bf16[2,256,512]{1,2,0:T(8,128)(2,1)S(1)}, bf16[2,256,512]{1,2,0:T(8,128)(2,1)}, u32[]{:S(2)}, u32[]{:S(2)}) collective-permute-start(bf16[2,256,512]{1,2,0:T(8,128)(2,1)S(1)} %pad_maximum_fusion.1), channel_id=1, source_target_pairs={{0,2},{2,4},{4,6},{6,8},{8,10},{10,12},{12,14},{14,16},{16,18},{18... | collective-permute-start | bytes 1572872 | tf_op jit(solution)/shard_map/ppermute | solution.py:16
  15.6 28.1 %collective-permute-start.3 = (bf16[512,2048]{1,0:T(8,128)(2,1)}, bf16[512,2048]{1,0:T(8,128)(2,1)S(1)}, u32[]{:S(2)}, u32[]{:S(2)}) collective-permute-start(bf16[512,2048]{1,0:T(8,128)(2,1)} %param.17), channel_id=1, source_target_pairs={{0,1},{1,0},{2,3},{3,2},{4,5},{5,4},{6,7},{7,6},{8,9},{9,8},{10,11... | collective-permute-start | bytes 6291464 | tf_op jit(solution)/shard_map/ppermute | solution.py:60
  39.0 0.9 copy-start.6
  41.5 1.6 copy-start.1
  41.9 1.7 copy-start.5
  42.0 1.7 collective-permute-start.2
  43.6 0.7 copy-start.7
  43.6 2.4 copy-start.8
  43.6 2.4 copy-start.9
  45.3 323.3 %reduce-scatter.2.cloned.1.call-start = ((), (), s32[]{:S(2)}) async-start(), calls=%async_computation.2 | async-start | bytes 8912896 | tf_op jit(solution)/shard_map/reduce_scatter | solution.py:100
  45.3 30.1 %collective-permute-start.6 = (bf16[352,2048]{1,0:T(8,128)(2,1)}, bf16[352,2048]{1,0:T(8,128)(2,1)}, u32[]{:S(2)}, u32[]{:S(2)}) collective-permute-start(bf16[352,2048]{1,0:T(8,128)(2,1)} %bitcast.47), channel_id=1, source_target_pairs={{0,1},{1,0},{2,3},{3,2},{4,5},{5,4},{6,7},{7,6},{8,9},{9,8},{10,11... | collective-permute-start | bytes 4325384 | tf_op jit(solution)/shard_map/ppermute | solution.py:22
  45.4 33.7 %collective-permute-start.5 = (bf16[2048,352]{0,1:T(8,128)(2,1)}, bf16[2048,352]{0,1:T(8,128)(2,1)}, u32[]{:S(2)}, u32[]{:S(2)}) collective-permute-start(bf16[2048,352]{0,1:T(8,128)(2,1)} %bitcast.48), channel_id=1, source_target_pairs={{0,1},{1,0},{2,3},{3,2},{4,5},{5,4},{6,7},{7,6},{8,9},{9,8},{10,11... | collective-permute-start | bytes 4325384 | tf_op jit(solution)/shard_map/ppermute | solution.py:22
  45.9 36.6 %collective-permute-start.4 = (bf16[2048,352]{0,1:T(8,128)(2,1)}, bf16[2048,352]{0,1:T(8,128)(2,1)S(1)}, u32[]{:S(2)}, u32[]{:S(2)}) collective-permute-start(bf16[2048,352]{0,1:T(8,128)(2,1)} %bitcast.49), channel_id=1, source_target_pairs={{0,1},{1,0},{2,3},{3,2},{4,5},{5,4},{6,7},{7,6},{8,9},{9,8},{10,11... | collective-permute-start | bytes 4325384 | tf_op jit(solution)/shard_map/ppermute | solution.py:22
  75.4 3.7 copy-start.2
  79.1 3.4 copy-start.3
  157.0 11.1 %copy-start.4 = (bf16[352,2048]{1,0:T(8,128)(2,1)S(1)}, bf16[352,2048]{1,0:T(8,128)(2,1)}, u32[]{:S(2)}) copy-start(bf16[352,2048]{1,0:T(8,128)(2,1)} %get-tuple-element.5) | copy-start | bytes 4325380
Sparse Core Ops, SparseCore 0:
  45.4 111.5 all-gather.1
  188.0 180.4 reduce-scatter.1

commit v2 on v1

--- a/solution.py
+++ b/solution.py
@@ -18,11 +18,82 @@
     return jnp.concatenate([before, cells, after], axis=1)
 
 
-def both_halves(part, core, axis):
-    other = lax.ppermute(part, "exp", SWAP)
-    low = jnp.where(core == 0, part, other)
-    high = jnp.where(core == 0, other, part)
-    return jnp.concatenate([low, high], axis=axis)
+def flip(block, mask):
+    count = lax.axis_size("seq")
+    return lax.ppermute(block, "seq", [(i, i ^ mask) for i in range(count)])
+
+
+def gather_small(block):
+    mask = 1
+    while mask < lax.axis_size("seq"):
+        block = jnp.concatenate([block, flip(block, mask)], axis=0)
+        mask *= 2
+    return block
+
+
+def expert(tokens, weight, gate_up, down):
+    hidden = lax.dot_general(
+        tokens, gate_up, (((1,), (1,)), ((), ())), preferred_element_type=jnp.float32
+    )
+    units = down.shape[0]
+    act = (jax.nn.silu(hidden[:, :units]) * hidden[:, units:]).astype(jnp.bfloat16)
+    result = jnp.dot(act, down, preferred_element_type=jnp.float32)
+    return (result * weight).astype(jnp.bfloat16)
+
+
+def plane_gather(block):
+    half = block.shape[1] // 2
+    beside_x = flip(block, 1)
+    beside_y = flip(block, 2)
+    left = flip(beside_x[:, :half], 2)
+    right = flip(beside_y[:, half:], 1)
+    return [block, beside_x, beside_y, jnp.concatenate([left, right], axis=1)]
+
+
+def add(*terms):
+    total = terms[0].astype(jnp.float32)
+    for term in terms[1:]:
+        total = total + term.astype(jnp.float32)
+    return total
+
+
+def plane_scatter(own, for_x, for_y, for_both):
+    half = own.shape[1] // 2
+    left = flip(for_both[:, :half], 2)
+    right = flip(for_both[:, half:], 1)
+    for_x = jnp.concatenate([add(for_x[:, :half], left).astype(jnp.bfloat16), for_x[:, half:]], axis=1)
+    for_y = jnp.concatenate([for_y[:, :half], add(for_y[:, half:], right).astype(jnp.bfloat16)], axis=1)
+    return add(own, flip(for_x, 1), flip(for_y, 2))
+
+
+def expert_layer(normed, weights, gate_up, down):
+    count = lax.axis_size("seq")
+    rows = normed.shape[0]
+
+    def run(blocks, first):
+        tokens = jnp.concatenate(blocks, axis=0)
+        part = weights[first * rows : first * rows + tokens.shape[0]]
+        result = expert(tokens, part, gate_up, down)
+        return [result[i * rows : (i + 1) * rows] for i in range(len(blocks))]
+
+    if count == 16:
+        layers = [normed] + [flip(normed, 4 * k) for k in range(1, 4)]
+        gathered = [plane_gather(layer) for layer in layers]
+        results = [run(blocks, 4 * k) for k, blocks in enumerate(gathered)]
+        sums = [plane_scatter(*result) for result in results]
+        return add(sums[0], *[flip(sums[k].astype(jnp.bfloat16), 4 * k) for k in range(1, 4)])
+    blocks, mask = [normed], 1
+    while mask < count:
+        blocks = blocks + [flip(block, mask) for block in blocks]
+        mask *= 2
+    step = 8
+    parts = []
+    for first in range(0, count, step):
+        parts += run(blocks[first : first + step], first)
+    while mask > 1:
+        mask //= 2
+        parts = [add(parts[i], flip(parts[i + mask], mask)).astype(jnp.bfloat16) for i in range(mask)]
+    return add(parts[0])
 
 
 def shards(
@@ -55,12 +126,18 @@
         ),
         axis=1,
     )
-    all_gates = lax.all_gather(per_expert, "seq", axis=0, tiled=True)
+    all_gates = gather_small(per_expert)
     my_gate = lax.dynamic_slice_in_dim(all_gates, shard, 1, 1)
     out_other = lax.ppermute(out_weight, "exp", SWAP)
-    gate_w = both_halves(w_gate[0], core, 1)
-    up_w = both_halves(w_up[0], core, 1)
-    down_w = both_halves(w_down[0], core, 0)
+    own_up = jnp.swapaxes(w_up[0], 0, 1)
+    own_gate = jnp.swapaxes(w_gate[0], 0, 1)
+    units = own_gate.shape[0]
+    own = jnp.concatenate([own_gate, own_up, w_down[0]], axis=0)
+    other = lax.ppermute(own, "exp", SWAP)
+    gate_up = jnp.concatenate(
+        [own_gate, other[:units], own_up, other[units : 2 * units]], axis=0
+    )
+    down = jnp.concatenate([w_down[0], other[2 * units :]], axis=0)
 
     id_pad = jnp.pad(pair_ids, (tok_rows, tok_rows), constant_values=-1)
     key_ids = lax.dynamic_slice_in_dim(id_pad, shard * tok_rows, 3 * tok_rows, 0)
@@ -92,15 +169,8 @@
     meansq = jnp.mean(stream * stream, axis=-1, keepdims=True)
     normed = (stream * lax.rsqrt(meansq + 1e-05) * norm_gain).astype(jnp.bfloat16)
 
-    group = lax.all_gather(normed, "seq", axis=0, tiled=True)
-    gate_part = jnp.dot(group, gate_w, preferred_element_type=jnp.float32)
-    up_part = jnp.dot(group, up_w, preferred_element_type=jnp.float32)
-    act = (jax.nn.silu(gate_part) * up_part).astype(jnp.bfloat16)
-    result = jnp.dot(act, down_w, preferred_element_type=jnp.float32) * my_gate
-    mixture = lax.psum_scatter(
-        result.astype(jnp.bfloat16), "seq", scatter_dimension=0, tiled=True
-    )
-    return (stream + mixture.astype(jnp.float32)).astype(jnp.bfloat16)
+    mixture = expert_layer(normed, my_gate, gate_up, down)
+    return (stream + mixture).astype(jnp.bfloat16)
 
 
 def solution(mesh):

time: 378 us -> 276 us (0.73); the launches traced: 377 us -> 270 us
  waiting for transfers between devices: 273 us -> 153 us
  starting transfers between devices: 7.6 us -> 50.9 us
  blocking collectives: 29.4 us -> 0 us
  between operations: 13.6 us -> 0.56 us
  matrix products: 32.9 us -> 41.5 us
  local copies, waits for them, and re-layouts: 4.55 us -> 12.1 us
  other arithmetic: 16.4 us -> 12.2 us
    reduce_scatter x1 -> x0, waiting for transfers between devices: 181 us -> none  [shards(): lax.psum_scatter(result.astype(jnp.bfloat16), 'seq', scatter_dimension=0,...]
    ppermute x3 -> x43, waiting for transfers between devices: 0.01 us -> 137 us  [the longest x42 137 us: flip(): return lax.ppermute(block, 'seq', [(i, i ^ mask) for i in range(count)])]
    all_gather x1 -> x0, waiting for transfers between devices: 72.8 us -> none  [shards(): group = lax.all_gather(normed, 'seq', axis=0, tiled=True)]
    ppermute x3 -> x43, starting transfers between devices: 0.65 us -> 44 us  [the longest x42 43.5 us: flip(): return lax.ppermute(block, 'seq', [(i, i ^ mask) for i in range(count)])]
    all_gather x1 -> x0, blocking collectives: 29.4 us -> none  [shards(): all_gates = lax.all_gather(per_expert, 'seq', axis=0, tiled=True)]
    select_n x3 -> x0, other arithmetic: 8.82 us -> none  [both_halves(): low = jnp.where(core == 0, part, other)]
    dot_general x2 -> x8, matrix products: 30.8 us -> 39.4 us  [the longest x4 23.8 us: expert(): lax.dot_general(tokens, gate_up, (((1,), (1,)), ((), ())), preferred_elem...]
    slice x0 -> x14, local copies, waits for them, and re-layouts: none -> 7.33 us  [the longest x4 2.64 us: plane_scatter(): left = flip(for_both[:, :half], 2)]
  transfers between devices with their start and end apart: 9 -> 47, of which waited for: 4 -> 25; matrix products, arithmetic and copies ran while one was open for 4% -> 22% of each run, Pallas kernels for 0% -> 0%
where the time goes in v2:
time: 276 us; the launch traced here: 270 us
  waiting for transfers between devices  153 us (55%)
  starting transfers between devices  50.9 us (18%)
  matrix products  41.5 us (15%)
  other arithmetic  12.2 us (4%)
  local copies, waits for them, and re-layouts  12.1 us (4%)
    ppermute x42, waiting for transfers between devices, flip(): return lax.ppermute(block, 'seq', [(i, i ^ mask) for i in range(count)])  137 us
    ppermute x42, starting transfers between devices, flip(): return lax.ppermute(block, 'seq', [(i, i ^ mask) for i in range(count)])  43.5 us
    dot_general x4, matrix products, expert(): lax.dot_general(tokens, gate_up, (((1,), (1,)), ((), ())), preferred_elem...  23.8 us
    dot_general x4, matrix products, expert(): result = jnp.dot(act, down, preferred_element_type=jnp.float32)  15.6 us
    ppermute x1, waiting for transfers between devices, with_halo(): before = lax.ppermute(cells, 'seq', [(i, i + 1) for i in range(ends)])  11 us
  transfers between devices with their start and end apart: 47, of which 25 were waited for; matrix products, arithmetic and copies ran while one was open for 22% of the time, Pallas kernels for 0%

profile of v2, /device:TPU:10, one launch (start us, length us, event | category | flops | bytes accessed | tf_op | source)
XLA Modules:
  0.0 270.4 jit_solution(9025246961317298739)
XLA Ops:
  2.3 2.4 collective-permute-start.1
  4.7 4.3 %collective-permute-start = (bf16[2,256,512]{1,2,0:T(8,128)(2,1)S(1)}, bf16[2,256,512]{1,2,0:T(8,128)(2,1)}, u32[]{:S(2)}, u32[]{:S(2)}) collective-permute-start(bf16[2,256,512]{1,2,0:T(8,128)(2,1)S(1)} %pad_maximum_fusion.4), channel_id=1, source_target_pairs={{0,2},{2,4},{4,6},{6,8},{8,10},{10,12},{12,14},{14,16},{16,18},{18... | collective-permute-start | bytes 1572872 | tf_op jit(solution)/shard_map/ppermute | solution.py:16
  9.1 3.8 %pad_maximum_fusion.1 = bf16[1056,2048]{1,0:T(8,128)(2,1)} fusion(bf16[352,2048]{1,0:T(8,128)(2,1)} %bitcast.56, bf16[352,2048]{1,0:T(8,128)(2,1)} %bitcast.46, bf16[352,2048]{1,0:T(8,128)(2,1)} %bitcast.51), kind=kLoop, calls=%fused_computation.2 | loop fusion | flops 12976128 | bytes 8650752 | tf_op jit(solution)/shard_map/concatenate | solution.py:135
  14.5 5.4 %collective-permute-done.1 = bf16[2,256,512]{1,2,0:T(8,128)(2,1)} collective-permute-done((bf16[2,256,512]{1,2,0:T(8,128)(2,1)S(1)}, bf16[2,256,512]{1,2,0:T(8,128)(2,1)}, u32[]{:S(2)}, u32[]{:S(2)}) %collective-permute-start.1) | collective-permute-done | bytes 524320 | tf_op jit(solution)/shard_map/ppermute | solution.py:17
  20.0 11.0 %collective-permute-done = bf16[2,256,512]{1,2,0:T(8,128)(2,1)} collective-permute-done((bf16[2,256,512]{1,2,0:T(8,128)(2,1)S(1)}, bf16[2,256,512]{1,2,0:T(8,128)(2,1)}, u32[]{:S(2)}, u32[]{:S(2)}) %collective-permute-start) | collective-permute-done | bytes 524320 | tf_op jit(solution)/shard_map/ppermute | solution.py:16
  31.0 1.3 pad_maximum_fusion.3
  33.4 1.8 fusion.83
  38.1 1.6 collective-permute-start.37
  41.8 3.6 %collective-permute-done.9 = f32[128,16]{0,1:T(8,128)S(1)} collective-permute-done((f32[128,16]{0,1:T(8,128)S(1)}, f32[128,16]{0,1:T(8,128)S(1)}, u32[]{:S(2)}, u32[]{:S(2)}) %collective-permute-start.9) | collective-permute-done | bytes 8224 | tf_op jit(solution)/shard_map/ppermute | solution.py:23
  45.6 3.6 %collective-permute-done.10 = f32[256,16]{0,1:T(8,128)S(1)} collective-permute-done((f32[256,16]{0,1:T(8,128)S(1)}, f32[256,16]{0,1:T(8,128)S(1)}, u32[]{:S(2)}, u32[]{:S(2)}) %collective-permute-start.10) | collective-permute-done | bytes 16416 | tf_op jit(solution)/shard_map/ppermute | solution.py:23
  49.1 1.3 collective-permute-start.11
  50.5 23.5 %collective-permute-done.11 = f32[512,16]{0,1:T(8,128)S(1)} collective-permute-done((f32[512,16]{0,1:T(8,128)S(1)}, f32[512,16]{0,1:T(8,128)S(1)}, u32[]{:S(2)}, u32[]{:S(2)}) %collective-permute-start.11) | collective-permute-done | bytes 32800 | tf_op jit(solution)/shard_map/ppermute | solution.py:23
  74.0 1.6 collective-permute-start.12
  75.6 10.6 %collective-permute-done.12 = f32[1024,16]{0,1:T(8,128)S(1)} collective-permute-done((f32[1024,16]{0,1:T(8,128)S(1)}, f32[1024,16]{0,1:T(8,128)S(1)}, u32[]{:S(2)}, u32[]{:S(2)}) %collective-permute-start.12) | collective-permute-done | bytes 65568 | tf_op jit(solution)/shard_map/ppermute | solution.py:23
  89.3 1.8 collective-permute-start.38
  91.1 9.9 %collective-permute-done.5 = bf16[128,2048]{1,0:T(8,128)(2,1)S(1)} collective-permute-done((bf16[128,2048]{1,0:T(8,128)(2,1)S(1)}, bf16[128,2048]{1,0:T(8,128)(2,1)S(1)}, u32[]{:S(2)}, u32[]{:S(2)}) %collective-permute-start.5) | collective-permute-done | bytes 524320 | tf_op jit(solution)/shard_map/ppermute | solution.py:23
  102.5 9.8 %collective-permute-done.39 = bf16[128,2048]{1,0:T(8,128)(2,1)} collective-permute-done((bf16[128,2048]{1,0:T(8,128)(2,1)}, bf16[128,2048]{1,0:T(8,128)(2,1)}, u32[]{:S(2)}, u32[]{:S(2)}) %collective-permute-start.39) | collective-permute-done | bytes 524320 | tf_op jit(solution)/shard_map/ppermute | solution.py:23
  116.0 7.5 %collective-permute-done.29 = bf16[128,2048]{1,0:T(8,128)(2,1)S(1)} collective-permute-done((bf16[128,2048]{1,0:T(8,128)(2,1)}, bf16[128,2048]{1,0:T(8,128)(2,1)S(1)}, u32[]{:S(2)}, u32[]{:S(2)}) %collective-permute-start.29) | collective-permute-done | bytes 524320 | tf_op jit(solution)/shard_map/ppermute | solution.py:23
  125.6 9.1 %collective-permute-done.19 = bf16[128,2048]{1,0:T(8,128)(2,1)S(1)} collective-permute-done((bf16[128,2048]{1,0:T(8,128)(2,1)}, bf16[128,2048]{1,0:T(8,128)(2,1)S(1)}, u32[]{:S(2)}, u32[]{:S(2)}) %collective-permute-start.19) | collective-permute-done | bytes 524320 | tf_op jit(solution)/shard_map/ppermute | solution.py:23
  137.9 2.6 fusion.77
  140.4 6.4 %collective-permute-done.41 = bf16[128,1024]{1,0:T(8,128)(2,1)S(1)} collective-permute-done((bf16[128,1024]{1,0:T(8,128)(2,1)S(1)}, bf16[128,1024]{1,0:T(8,128)(2,1)S(1)}, u32[]{:S(2)}, u32[]{:S(2)}) %collective-permute-start.41) | collective-permute-done | bytes 262176 | tf_op jit(solution)/shard_map/ppermute | solution.py:23
  148.0 6.5 %fusion.33 = f32[512,1408]{1,0:T(8,128)} fusion(bf16[128,1024]{1,0:T(8,128)(2,1)S(1)} %collective-permute-done.41, bf16[128,1024]{1,0:T(8,128)(2,1)S(1)} %collective-permute-done.40, bf16[128,2048]{1,0:T(8,128)(2,1)} %collective-permute-done.39, bf16[128,2048]{1,0:T(8,128)(2,1)} %collective-permute-done.38, bf16[128,2048]{1,0:T(8,128)(2,1)} %collective-permute-done.37, ...), kind=kOutput, calls=%fused_computation.44 | convolution fusion | flops 2986344448 | bytes 10747904 | tf_op jit(solution)/shard_map/dot_general | solution.py:35
  154.5 3.9 %multiply_convert_fusion = bf16[512,2048]{1,0:T(8,128)(2,1)S(1)} fusion(f32[512]{0:T(512)S(1)} %bitcast.67, f32[512,1408]{1,0:T(8,128)} %fusion.33, bf16[352,2048]{1,0:T(8,128)(2,1)S(1)} %get-tuple-element.5, bf16[352,2048]{1,0:T(8,128)(2,1)S(1)} %bitcast.57), kind=kOutput, calls=%fused_computation.3 | convolution fusion | flops 1486422016 | bytes 8128512 | tf_op jit(solution)/shard_map/dot_general | solution.py:40
  159.2 1.5 collective-permute-start.20
  161.3 5.0 %fusion.23 = f32[512,1408]{1,0:T(8,128)} fusion(bf16[128,1024]{1,0:T(8,128)(2,1)S(1)} %collective-permute-done.31, bf16[128,1024]{1,0:T(8,128)(2,1)S(1)} %collective-permute-done.30, bf16[128,2048]{1,0:T(8,128)(2,1)S(1)} %collective-permute-done.29, bf16[128,2048]{1,0:T(8,128)(2,1)S(1)} %collective-permute-done.28, bf16[128,2048]{1,0:T(8,128)(2,1)S(1)} %copy-done.18, ...), kind=kOutput, calls=%fused_computation.34 | convolution fusion | flops 2986344448 | bytes 10747904 | tf_op jit(solution)/shard_map/dot_general | solution.py:35
  166.3 4.1 %multiply_convert_fusion.1 = bf16[512,2048]{1,0:T(8,128)(2,1)S(1)} fusion(f32[512]{0:T(512)S(1)} %bitcast.66, f32[512,1408]{1,0:T(8,128)} %fusion.23, bf16[352,2048]{1,0:T(8,128)(2,1)S(1)} %get-tuple-element.5, bf16[352,2048]{1,0:T(8,128)(2,1)S(1)} %bitcast.58), kind=kOutput, calls=%fused_computation.4 | convolution fusion | flops 1486422016 | bytes 8128512 | tf_op jit(solution)/shard_map/dot_general | solution.py:40
  171.2 2.0 collective-permute-start.44
  174.1 6.0 %fusion.13 = f32[512,1408]{1,0:T(8,128)} fusion(bf16[128,1024]{1,0:T(8,128)(2,1)} %copy-done.19, bf16[128,1024]{1,0:T(8,128)(2,1)} %collective-permute-done.20, bf16[128,2048]{1,0:T(8,128)(2,1)S(1)} %collective-permute-done.19, bf16[128,2048]{1,0:T(8,128)(2,1)S(1)} %collective-permute-done.18, bf16[128,2048]{1,0:T(8,128)(2,1)S(1)} %copy-done.16, ...), kind=kOutput, calls=%fused_computation.24 | convolution fusion | flops 2986344448 | bytes 10747904 | tf_op jit(solution)/shard_map/dot_general | solution.py:35
  180.1 3.8 %multiply_convert_fusion.2 = bf16[512,2048]{1,0:T(8,128)(2,1)S(1)} fusion(f32[512]{0:T(512)S(1)} %bitcast.65, f32[512,1408]{1,0:T(8,128)} %fusion.13, bf16[352,2048]{1,0:T(8,128)(2,1)S(1)} %get-tuple-element.5, bf16[352,2048]{1,0:T(8,128)(2,1)S(1)} %bitcast.59), kind=kOutput, calls=%fused_computation.5 | convolution fusion | flops 1486422016 | bytes 8128512 | tf_op jit(solution)/shard_map/dot_general | solution.py:40
  186.6 6.4 %fusion.3 = f32[512,1408]{1,0:T(8,128)} fusion(bf16[128,1024]{1,0:T(8,128)(2,1)} %collective-permute-done.7, bf16[128,1024]{1,0:T(8,128)(2,1)} %collective-permute-done.6, bf16[128,2048]{1,0:T(8,128)(2,1)} %copy-done.9, bf16[128,2048]{1,0:T(8,128)(2,1)} %copy-done.10, bf16[128,2048]{1,0:T(8,128)(2,1)S(1)} %multiply_convert_fusion.4, ...), kind=kOutput, calls=%fused_computation.14 | convolution fusion | flops 2986344448 | bytes 10747904 | tf_op jit(solution)/shard_map/dot_general | solution.py:35
  193.0 3.8 %multiply_convert_fusion.3 = bf16[512,2048]{1,0:T(8,128)(2,1)S(1)} fusion(f32[512]{0:T(512)S(1)} %bitcast.64, f32[512,1408]{1,0:T(8,128)} %fusion.3, bf16[352,2048]{1,0:T(8,128)(2,1)S(1)} %get-tuple-element.5, bf16[352,2048]{1,0:T(8,128)(2,1)S(1)} %bitcast.60), kind=kOutput, calls=%fused_computation.6 | convolution fusion | flops 1486422016 | bytes 8128512 | tf_op jit(solution)/shard_map/dot_general | solution.py:40
  196.9 1.4 collective-permute-start.24
  202.6 1.4 collective-permute-start.43
  204.0 2.2 collective-permute-done.24
  207.6 1.3 collective-permute-start.33
  208.8 3.0 %collective-permute-done.15 = bf16[128,1024]{1,0:T(8,128)(2,1)S(1)} collective-permute-done((bf16[128,1024]{1,0:T(8,128)(2,1)S(1)}, bf16[128,1024]{1,0:T(8,128)(2,1)S(1)}, u32[]{:S(2)}, u32[]{:S(2)}) %collective-permute-start.15) | collective-permute-done | bytes 262176 | tf_op jit(solution)/shard_map/ppermute | solution.py:23
  213.1 5.7 %collective-permute-done.45 = bf16[128,2048]{1,0:T(8,128)(2,1)S(1)} collective-permute-done((bf16[128,2048]{1,0:T(8,128)(2,1)S(1)}, bf16[128,2048]{1,0:T(8,128)(2,1)S(1)}, u32[]{:S(2)}, u32[]{:S(2)}) %collective-permute-start.45) | collective-permute-done | bytes 524320 | tf_op jit(solution)/shard_map/ppermute | solution.py:23
  219.5 3.6 %collective-permute-done.43 = bf16[128,2048]{1,0:T(8,128)(2,1)S(1)} collective-permute-done((bf16[128,2048]{1,0:T(8,128)(2,1)S(1)}, bf16[128,2048]{1,0:T(8,128)(2,1)S(1)}, u32[]{:S(2)}, u32[]{:S(2)}) %collective-permute-start.43) | collective-permute-done | bytes 524320 | tf_op jit(solution)/shard_map/ppermute | solution.py:23
  224.2 5.8 %collective-permute-done.35 = bf16[128,2048]{1,0:T(8,128)(2,1)S(1)} collective-permute-done((bf16[128,2048]{1,0:T(8,128)(2,1)S(1)}, bf16[128,2048]{1,0:T(8,128)(2,1)S(1)}, u32[]{:S(2)}, u32[]{:S(2)}) %collective-permute-start.35) | collective-permute-done | bytes 524320 | tf_op jit(solution)/shard_map/ppermute | solution.py:23
  230.8 3.6 %collective-permute-done.33 = bf16[128,2048]{1,0:T(8,128)(2,1)S(1)} collective-permute-done((bf16[128,2048]{1,0:T(8,128)(2,1)S(1)}, bf16[128,2048]{1,0:T(8,128)(2,1)S(1)}, u32[]{:S(2)}, u32[]{:S(2)}) %collective-permute-start.33) | collective-permute-done | bytes 524320 | tf_op jit(solution)/shard_map/ppermute | solution.py:23
  234.3 1.9 collective-permute-start.46
  236.5 4.5 %collective-permute-done.25 = bf16[128,2048]{1,0:T(8,128)(2,1)S(1)} collective-permute-done((bf16[128,2048]{1,0:T(8,128)(2,1)S(1)}, bf16[128,2048]{1,0:T(8,128)(2,1)S(1)}, u32[]{:S(2)}, u32[]{:S(2)}) %collective-permute-start.25) | collective-permute-done | bytes 524320 | tf_op jit(solution)/shard_map/ppermute | solution.py:23
  241.0 3.4 %collective-permute-start.36 = (bf16[128,2048]{1,0:T(8,128)(2,1)S(1)}, bf16[128,2048]{1,0:T(8,128)(2,1)S(1)}, u32[]{:S(2)}, u32[]{:S(2)}) collective-permute-start(bf16[128,2048]{1,0:T(8,128)(2,1)S(1)} %add_convert_fusion.2), channel_id=1, source_target_pairs={{0,16},{2,18},{4,20},{6,22},{8,24},{10,26},{12,28},{14,30},{16,0},... | collective-permute-start | bytes 1572872 | tf_op jit(solution)/shard_map/ppermute | solution.py:23
  245.8 2.5 collective-permute-start.26
  248.3 3.1 %collective-permute-done.14 = bf16[128,2048]{1,0:T(8,128)(2,1)S(1)} collective-permute-done((bf16[128,2048]{1,0:T(8,128)(2,1)S(1)}, bf16[128,2048]{1,0:T(8,128)(2,1)S(1)}, u32[]{:S(2)}, u32[]{:S(2)}) %collective-permute-start.14) | collective-permute-done | bytes 524320 | tf_op jit(solution)/shard_map/ppermute | solution.py:23
  251.4 10.5 %collective-permute-done.46 = bf16[128,2048]{1,0:T(8,128)(2,1)S(1)} collective-permute-done((bf16[128,2048]{1,0:T(8,128)(2,1)S(1)}, bf16[128,2048]{1,0:T(8,128)(2,1)S(1)}, u32[]{:S(2)}, u32[]{:S(2)}) %collective-permute-start.46) | collective-permute-done | bytes 524320 | tf_op jit(solution)/shard_map/ppermute | solution.py:23
  262.0 7.1 %collective-permute-done.36 = bf16[128,2048]{1,0:T(8,128)(2,1)S(1)} collective-permute-done((bf16[128,2048]{1,0:T(8,128)(2,1)S(1)}, bf16[128,2048]{1,0:T(8,128)(2,1)S(1)}, u32[]{:S(2)}, u32[]{:S(2)}) %collective-permute-start.36) | collective-permute-done | bytes 524320 | tf_op jit(solution)/shard_map/ppermute | solution.py:23
  269.0 1.4 add_convert_fusion
  (150 shorter events, 41.4 us)
Async XLA Ops:
  2.3 17.7 %collective-permute-start.1 = (bf16[2,256,512]{1,2,0:T(8,128)(2,1)S(1)}, bf16[2,256,512]{1,2,0:T(8,128)(2,1)}, u32[]{:S(2)}, u32[]{:S(2)}) collective-permute-start(bf16[2,256,512]{1,2,0:T(8,128)(2,1)S(1)} %pad_maximum_fusion.4), channel_id=1, source_target_pairs={{2,0},{4,2},{6,4},{8,6},{10,8},{12,10},{14,12},{16,14},{18,16},{20... | collective-permute-start | bytes 1572872 | tf_op jit(solution)/shard_map/ppermute | solution.py:17
  4.7 26.3 %collective-permute-start = (bf16[2,256,512]{1,2,0:T(8,128)(2,1)S(1)}, bf16[2,256,512]{1,2,0:T(8,128)(2,1)}, u32[]{:S(2)}, u32[]{:S(2)}) collective-permute-start(bf16[2,256,512]{1,2,0:T(8,128)(2,1)S(1)} %pad_maximum_fusion.4), channel_id=1, source_target_pairs={{0,2},{2,4},{4,6},{6,8},{8,10},{10,12},{12,14},{14,16},{16,18},{18... | collective-permute-start | bytes 1572872 | tf_op jit(solution)/shard_map/ppermute | solution.py:16
  9.0 28.2 %collective-permute-start.3 = (bf16[512,2048]{1,0:T(8,128)(2,1)}, bf16[512,2048]{1,0:T(8,128)(2,1)S(1)}, u32[]{:S(2)}, u32[]{:S(2)}) collective-permute-start(bf16[512,2048]{1,0:T(8,128)(2,1)} %param.17), channel_id=1, source_target_pairs={{0,1},{1,0},{2,3},{3,2},{4,5},{5,4},{6,7},{7,6},{8,9},{9,8},{10,11... | collective-permute-start | bytes 6291464 | tf_op jit(solution)/shard_map/ppermute | solution.py:131
  13.0 123.9 %collective-permute-start.8 = (bf16[1056,2048]{1,0:T(8,128)(2,1)}, bf16[1056,2048]{1,0:T(8,128)(2,1)}, u32[]{:S(2)}, u32[]{:S(2)}) collective-permute-start(bf16[1056,2048]{1,0:T(8,128)(2,1)} %pad_maximum_fusion.1), channel_id=1, source_target_pairs={{0,1},{1,0},{2,3},{3,2},{4,5},{5,4},{6,7},{7,6},{8,9},{9,8},{10,11... | collective-permute-start | bytes 12976136 | tf_op jit(solution)/shard_map/ppermute | solution.py:136
  35.6 1.7 collective-permute-start.2
  38.1 49.0 %collective-permute-start.37 = (bf16[128,2048]{1,0:T(8,128)(2,1)S(1)}, bf16[128,2048]{1,0:T(8,128)(2,1)}, u32[]{:S(2)}, u32[]{:S(2)}) collective-permute-start(bf16[128,2048]{1,0:T(8,128)(2,1)S(1)} %multiply_convert_fusion.4), channel_id=1, source_target_pairs={{0,24},{2,26},{4,28},{6,30},{8,16},{10,18},{12,20},{14,22},{16,8},... | collective-permute-start | bytes 1572872 | tf_op jit(solution)/shard_map/ppermute | solution.py:23
  39.7 47.9 %collective-permute-start.27 = (bf16[128,2048]{1,0:T(8,128)(2,1)S(1)}, bf16[128,2048]{1,0:T(8,128)(2,1)S(1)}, u32[]{:S(2)}, u32[]{:S(2)}) collective-permute-start(bf16[128,2048]{1,0:T(8,128)(2,1)S(1)} %multiply_convert_fusion.4), channel_id=1, source_target_pairs={{0,16},{2,18},{4,20},{6,22},{8,24},{10,26},{12,28},{14,30},{16,0},... | collective-permute-start | bytes 1572872 | tf_op jit(solution)/shard_map/ppermute | solution.py:23
  41.0 47.4 %collective-permute-start.17 = (bf16[128,2048]{1,0:T(8,128)(2,1)S(1)}, bf16[128,2048]{1,0:T(8,128)(2,1)S(1)}, u32[]{:S(2)}, u32[]{:S(2)}) collective-permute-start(bf16[128,2048]{1,0:T(8,128)(2,1)S(1)} %multiply_convert_fusion.4), channel_id=1, source_target_pairs={{0,8},{2,10},{4,12},{6,14},{8,0},{10,2},{12,4},{14,6},{16,24},{18,... | collective-permute-start | bytes 1572872 | tf_op jit(solution)/shard_map/ppermute | solution.py:23
  41.7 3.7 %collective-permute-start.9 = (f32[128,16]{0,1:T(8,128)S(1)}, f32[128,16]{0,1:T(8,128)S(1)}, u32[]{:S(2)}, u32[]{:S(2)}) collective-permute-start(f32[128,16]{0,1:T(8,128)S(1)} %select_reduce_fusion), channel_id=1, source_target_pairs={{0,2},{2,0},{4,6},{6,4},{8,10},{10,8},{12,14},{14,12},{16,18},{18,... | collective-permute-start | bytes 24584 | tf_op jit(solution)/shard_map/ppermute | solution.py:23
  45.4 3.7 %collective-permute-start.10 = (f32[256,16]{0,1:T(8,128)S(1)}, f32[256,16]{0,1:T(8,128)S(1)}, u32[]{:S(2)}, u32[]{:S(2)}) collective-permute-start(f32[256,16]{0,1:T(8,128)S(1)} %pad_maximum_fusion.15), channel_id=1, source_target_pairs={{0,4},{2,6},{4,0},{6,2},{8,12},{10,14},{12,8},{14,10},{16,20},{18,... | collective-permute-start | bytes 49160 | tf_op jit(solution)/shard_map/ppermute | solution.py:23
  49.1 24.8 %collective-permute-start.11 = (f32[512,16]{0,1:T(8,128)S(1)}, f32[512,16]{0,1:T(8,128)S(1)}, u32[]{:S(2)}, u32[]{:S(2)}) collective-permute-start(f32[512,16]{0,1:T(8,128)S(1)} %pad_maximum_fusion.14), channel_id=1, source_target_pairs={{0,8},{2,10},{4,12},{6,14},{8,0},{10,2},{12,4},{14,6},{16,24},{18,... | collective-permute-start | bytes 98312 | tf_op jit(solution)/shard_map/ppermute | solution.py:23
  74.0 12.2 %collective-permute-start.12 = (f32[1024,16]{0,1:T(8,128)S(1)}, f32[1024,16]{0,1:T(8,128)S(1)}, u32[]{:S(2)}, u32[]{:S(2)}) collective-permute-start(f32[1024,16]{0,1:T(8,128)S(1)} %pad_maximum_fusion.13), channel_id=1, source_target_pairs={{0,16},{2,18},{4,20},{6,22},{8,24},{10,26},{12,28},{14,30},{16,0},... | collective-permute-start | bytes 196616 | tf_op jit(solution)/shard_map/ppermute | solution.py:23
  86.2 14.8 %collective-permute-start.5 = (bf16[128,2048]{1,0:T(8,128)(2,1)S(1)}, bf16[128,2048]{1,0:T(8,128)(2,1)S(1)}, u32[]{:S(2)}, u32[]{:S(2)}) collective-permute-start(bf16[128,2048]{1,0:T(8,128)(2,1)S(1)} %multiply_convert_fusion.4), channel_id=1, source_target_pairs={{0,4},{2,6},{4,0},{6,2},{8,12},{10,14},{12,8},{14,10},{16,20},{18,... | collective-permute-start | bytes 1572872 | tf_op jit(solution)/shard_map/ppermute | solution.py:23
  87.1 14.9 %collective-permute-start.4 = (bf16[128,2048]{1,0:T(8,128)(2,1)S(1)}, bf16[128,2048]{1,0:T(8,128)(2,1)S(1)}, u32[]{:S(2)}, u32[]{:S(2)}) collective-permute-start(bf16[128,2048]{1,0:T(8,128)(2,1)S(1)} %multiply_convert_fusion.4), channel_id=1, source_target_pairs={{0,2},{2,0},{4,6},{6,4},{8,10},{10,8},{12,14},{14,12},{16,18},{18,... | collective-permute-start | bytes 1572872 | tf_op jit(solution)/shard_map/ppermute | solution.py:23
  87.7 24.7 %collective-permute-start.39 = (bf16[128,2048]{1,0:T(8,128)(2,1)}, bf16[128,2048]{1,0:T(8,128)(2,1)}, u32[]{:S(2)}, u32[]{:S(2)}) collective-permute-start(bf16[128,2048]{1,0:T(8,128)(2,1)} %collective-permute-done.37), channel_id=1, source_target_pairs={{0,4},{2,6},{4,0},{6,2},{8,12},{10,14},{12,8},{14,10},{16,20},{18,... | collective-permute-start | bytes 1572872 | tf_op jit(solution)/shard_map/ppermute | solution.py:23
  89.3 24.0 %collective-permute-start.38 = (bf16[128,2048]{1,0:T(8,128)(2,1)}, bf16[128,2048]{1,0:T(8,128)(2,1)}, u32[]{:S(2)}, u32[]{:S(2)}) collective-permute-start(bf16[128,2048]{1,0:T(8,128)(2,1)} %collective-permute-done.37), channel_id=1, source_target_pairs={{0,2},{2,0},{4,6},{6,4},{8,10},{10,8},{12,14},{14,12},{16,18},{18,... | collective-permute-start | bytes 1572872 | tf_op jit(solution)/shard_map/ppermute | solution.py:23
  101.0 22.5 %collective-permute-start.29 = (bf16[128,2048]{1,0:T(8,128)(2,1)}, bf16[128,2048]{1,0:T(8,128)(2,1)S(1)}, u32[]{:S(2)}, u32[]{:S(2)}) collective-permute-start(bf16[128,2048]{1,0:T(8,128)(2,1)} %copy-done.17), channel_id=1, source_target_pairs={{0,4},{2,6},{4,0},{6,2},{8,12},{10,14},{12,8},{14,10},{16,20},{18,... | collective-permute-start | bytes 1572872 | tf_op jit(solution)/shard_map/ppermute | solution.py:23
  101.9 38.5 %copy-start.10 = (bf16[128,2048]{1,0:T(8,128)(2,1)}, bf16[128,2048]{1,0:T(8,128)(2,1)S(1)}, u32[]{:S(2)}) copy-start(bf16[128,2048]{1,0:T(8,128)(2,1)S(1)} %collective-permute-done.4) | copy-start | bytes 1572868
  101.9 22.5 %collective-permute-start.28 = (bf16[128,2048]{1,0:T(8,128)(2,1)}, bf16[128,2048]{1,0:T(8,128)(2,1)S(1)}, u32[]{:S(2)}, u32[]{:S(2)}) collective-permute-start(bf16[128,2048]{1,0:T(8,128)(2,1)} %copy-done.17), channel_id=1, source_target_pairs={{0,2},{2,0},{4,6},{6,4},{8,10},{10,8},{12,14},{14,12},{16,18},{18,... | collective-permute-start | bytes 1572872 | tf_op jit(solution)/shard_map/ppermute | solution.py:23
  112.3 22.4 %collective-permute-start.19 = (bf16[128,2048]{1,0:T(8,128)(2,1)}, bf16[128,2048]{1,0:T(8,128)(2,1)S(1)}, u32[]{:S(2)}, u32[]{:S(2)}) collective-permute-start(bf16[128,2048]{1,0:T(8,128)(2,1)} %copy-done.15), channel_id=1, source_target_pairs={{0,4},{2,6},{4,0},{6,2},{8,12},{10,14},{12,8},{14,10},{16,20},{18,... | collective-permute-start | bytes 1572872 | tf_op jit(solution)/shard_map/ppermute | solution.py:23
  113.3 22.4 %collective-permute-start.18 = (bf16[128,2048]{1,0:T(8,128)(2,1)}, bf16[128,2048]{1,0:T(8,128)(2,1)S(1)}, u32[]{:S(2)}, u32[]{:S(2)}) collective-permute-start(bf16[128,2048]{1,0:T(8,128)(2,1)} %copy-done.15), channel_id=1, source_target_pairs={{0,2},{2,0},{4,6},{6,4},{8,10},{10,8},{12,14},{14,12},{16,18},{18,... | collective-permute-start | bytes 1572872 | tf_op jit(solution)/shard_map/ppermute | solution.py:23
  123.5 61.3 %collective-permute-start.7 = (bf16[128,1024]{1,0:T(8,128)(2,1)S(1)}, bf16[128,1024]{1,0:T(8,128)(2,1)}, u32[]{:S(2)}, u32[]{:S(2)}) collective-permute-start(bf16[128,1024]{1,0:T(8,128)(2,1)S(1)} %slice.251), channel_id=1, source_target_pairs={{0,2},{2,0},{4,6},{6,4},{8,10},{10,8},{12,14},{14,12},{16,18},{18,... | collective-permute-start | bytes 786440 | tf_op jit(solution)/shard_map/ppermute | solution.py:23
  124.4 61.1 %collective-permute-start.6 = (bf16[128,1024]{1,0:T(8,128)(2,1)S(1)}, bf16[128,1024]{1,0:T(8,128)(2,1)}, u32[]{:S(2)}, u32[]{:S(2)}) collective-permute-start(bf16[128,1024]{1,0:T(8,128)(2,1)S(1)} %slice.250), channel_id=1, source_target_pairs={{0,4},{2,6},{4,0},{6,2},{8,12},{10,14},{12,8},{14,10},{16,20},{18,... | collective-permute-start | bytes 786440 | tf_op jit(solution)/shard_map/ppermute | solution.py:23
  134.7 12.2 %collective-permute-start.41 = (bf16[128,1024]{1,0:T(8,128)(2,1)S(1)}, bf16[128,1024]{1,0:T(8,128)(2,1)S(1)}, u32[]{:S(2)}, u32[]{:S(2)}) collective-permute-start(bf16[128,1024]{1,0:T(8,128)(2,1)S(1)} %slice.287), channel_id=1, source_target_pairs={{0,2},{2,0},{4,6},{6,4},{8,10},{10,8},{12,14},{14,12},{16,18},{18,... | collective-permute-start | bytes 786440 | tf_op jit(solution)/shard_map/ppermute | solution.py:23
  135.6 12.4 %collective-permute-start.40 = (bf16[128,1024]{1,0:T(8,128)(2,1)S(1)}, bf16[128,1024]{1,0:T(8,128)(2,1)S(1)}, u32[]{:S(2)}, u32[]{:S(2)}) collective-permute-start(bf16[128,1024]{1,0:T(8,128)(2,1)S(1)} %slice.286), channel_id=1, source_target_pairs={{0,4},{2,6},{4,0},{6,2},{8,12},{10,14},{12,8},{14,10},{16,20},{18,... | collective-permute-start | bytes 786440 | tf_op jit(solution)/shard_map/ppermute | solution.py:23
  136.8 22.4 %collective-permute-start.31 = (bf16[128,1024]{1,0:T(8,128)(2,1)S(1)}, bf16[128,1024]{1,0:T(8,128)(2,1)S(1)}, u32[]{:S(2)}, u32[]{:S(2)}) collective-permute-start(bf16[128,1024]{1,0:T(8,128)(2,1)S(1)} %slice.276), channel_id=1, source_target_pairs={{0,2},{2,0},{4,6},{6,4},{8,10},{10,8},{12,14},{14,12},{16,18},{18,... | collective-permute-start | bytes 786440 | tf_op jit(solution)/shard_map/ppermute | solution.py:23
  146.9 13.8 %collective-permute-start.30 = (bf16[128,1024]{1,0:T(8,128)(2,1)S(1)}, bf16[128,1024]{1,0:T(8,128)(2,1)S(1)}, u32[]{:S(2)}, u32[]{:S(2)}) collective-permute-start(bf16[128,1024]{1,0:T(8,128)(2,1)S(1)} %slice.275), channel_id=1, source_target_pairs={{0,4},{2,6},{4,0},{6,2},{8,12},{10,14},{12,8},{14,10},{16,20},{18,... | collective-permute-start | bytes 786440 | tf_op jit(solution)/shard_map/ppermute | solution.py:23
  148.0 23.2 %collective-permute-start.21 = (bf16[128,1024]{1,0:T(8,128)(2,1)S(1)}, bf16[128,1024]{1,0:T(8,128)(2,1)S(1)}, u32[]{:S(2)}, u32[]{:S(2)}) collective-permute-start(bf16[128,1024]{1,0:T(8,128)(2,1)S(1)} %slice.265), channel_id=1, source_target_pairs={{0,2},{2,0},{4,6},{6,4},{8,10},{10,8},{12,14},{14,12},{16,18},{18,... | collective-permute-start | bytes 786440 | tf_op jit(solution)/shard_map/ppermute | solution.py:23
  159.2 14.0 %collective-permute-start.20 = (bf16[128,1024]{1,0:T(8,128)(2,1)S(1)}, bf16[128,1024]{1,0:T(8,128)(2,1)}, u32[]{:S(2)}, u32[]{:S(2)}) collective-permute-start(bf16[128,1024]{1,0:T(8,128)(2,1)S(1)} %slice.264), channel_id=1, source_target_pairs={{0,4},{2,6},{4,0},{6,2},{8,12},{10,14},{12,8},{14,10},{16,20},{18,... | collective-permute-start | bytes 786440 | tf_op jit(solution)/shard_map/ppermute | solution.py:23
  160.7 36.2 %collective-permute-start.42 = (bf16[128,1024]{1,0:T(8,128)(2,1)}, bf16[128,1024]{1,0:T(8,128)(2,1)S(1)}, u32[]{:S(2)}, u32[]{:S(2)}) collective-permute-start(bf16[128,1024]{1,0:T(8,128)(2,1)} %get-tuple-element.28), channel_id=1, source_target_pairs={{0,4},{2,6},{4,0},{6,2},{8,12},{10,14},{12,8},{14,10},{16,20},{18,... | collective-permute-start | bytes 786440 | tf_op jit(solution)/shard_map/ppermute | solution.py:23
  171.2 27.1 %collective-permute-start.44 = (bf16[128,1024]{1,0:T(8,128)(2,1)}, bf16[128,1024]{1,0:T(8,128)(2,1)S(1)}, u32[]{:S(2)}, u32[]{:S(2)}) collective-permute-start(bf16[128,1024]{1,0:T(8,128)(2,1)} %get-tuple-element.29), channel_id=1, source_target_pairs={{0,2},{2,0},{4,6},{6,4},{8,10},{10,8},{12,14},{14,12},{16,18},{18,... | collective-permute-start | bytes 786440 | tf_op jit(solution)/shard_map/ppermute | solution.py:23
  173.2 26.3 %collective-permute-start.32 = (bf16[128,1024]{1,0:T(8,128)(2,1)}, bf16[128,1024]{1,0:T(8,128)(2,1)S(1)}, u32[]{:S(2)}, u32[]{:S(2)}) collective-permute-start(bf16[128,1024]{1,0:T(8,128)(2,1)} %get-tuple-element.22), channel_id=1, source_target_pairs={{0,4},{2,6},{4,0},{6,2},{8,12},{10,14},{12,8},{14,10},{16,20},{18,... | collective-permute-start | bytes 786440 | tf_op jit(solution)/shard_map/ppermute | solution.py:23
  184.8 15.4 %collective-permute-start.34 = (bf16[128,1024]{1,0:T(8,128)(2,1)}, bf16[128,1024]{1,0:T(8,128)(2,1)}, u32[]{:S(2)}, u32[]{:S(2)}) collective-permute-start(bf16[128,1024]{1,0:T(8,128)(2,1)} %get-tuple-element.23), channel_id=1, source_target_pairs={{0,2},{2,0},{4,6},{6,4},{8,10},{10,8},{12,14},{14,12},{16,18},{18,... | collective-permute-start | bytes 786440 | tf_op jit(solution)/shard_map/ppermute | solution.py:23
  185.5 17.1 %collective-permute-start.22 = (bf16[128,1024]{1,0:T(8,128)(2,1)}, bf16[128,1024]{1,0:T(8,128)(2,1)S(1)}, u32[]{:S(2)}, u32[]{:S(2)}) collective-permute-start(bf16[128,1024]{1,0:T(8,128)(2,1)} %get-tuple-element.16), channel_id=1, source_target_pairs={{0,4},{2,6},{4,0},{6,2},{8,12},{10,14},{12,8},{14,10},{16,20},{18,... | collective-permute-start | bytes 786440 | tf_op jit(solution)/shard_map/ppermute | solution.py:23
  196.9 9.3 %collective-permute-start.24 = (bf16[128,1024]{1,0:T(8,128)(2,1)S(1)}, bf16[128,1024]{1,0:T(8,128)(2,1)S(1)}, u32[]{:S(2)}, u32[]{:S(2)}) collective-permute-start(bf16[128,1024]{1,0:T(8,128)(2,1)S(1)} %copy-done.7), channel_id=1, source_target_pairs={{0,2},{2,0},{4,6},{6,4},{8,10},{10,8},{12,14},{14,12},{16,18},{18,... | collective-permute-start | bytes 786440 | tf_op jit(solution)/shard_map/ppermute | solution.py:23
  198.3 9.2 %collective-permute-start.13 = (bf16[128,1024]{1,0:T(8,128)(2,1)S(1)}, bf16[128,1024]{1,0:T(8,128)(2,1)S(1)}, u32[]{:S(2)}, u32[]{:S(2)}) collective-permute-start(bf16[128,1024]{1,0:T(8,128)(2,1)S(1)} %get-tuple-element.10), channel_id=1, source_target_pairs={{0,4},{2,6},{4,0},{6,2},{8,12},{10,14},{12,8},{14,10},{16,20},{18,... | collective-permute-start | bytes 786440 | tf_op jit(solution)/shard_map/ppermute | solution.py:23
  199.5 12.4 %collective-permute-start.15 = (bf16[128,1024]{1,0:T(8,128)(2,1)S(1)}, bf16[128,1024]{1,0:T(8,128)(2,1)S(1)}, u32[]{:S(2)}, u32[]{:S(2)}) collective-permute-start(bf16[128,1024]{1,0:T(8,128)(2,1)S(1)} %get-tuple-element.11), channel_id=1, source_target_pairs={{0,2},{2,0},{4,6},{6,4},{8,10},{10,8},{12,14},{14,12},{16,18},{18,... | collective-permute-start | bytes 786440 | tf_op jit(solution)/shard_map/ppermute | solution.py:23
  200.2 18.6 %collective-permute-start.45 = (bf16[128,2048]{1,0:T(8,128)(2,1)S(1)}, bf16[128,2048]{1,0:T(8,128)(2,1)S(1)}, u32[]{:S(2)}, u32[]{:S(2)}) collective-permute-start(bf16[128,2048]{1,0:T(8,128)(2,1)S(1)} %pad_maximum_fusion.12), channel_id=1, source_target_pairs={{0,4},{2,6},{4,0},{6,2},{8,12},{10,14},{12,8},{14,10},{16,20},{18,... | collective-permute-start | bytes 1572872 | tf_op jit(solution)/shard_map/ppermute | solution.py:23
  202.6 20.5 %collective-permute-start.43 = (bf16[128,2048]{1,0:T(8,128)(2,1)S(1)}, bf16[128,2048]{1,0:T(8,128)(2,1)S(1)}, u32[]{:S(2)}, u32[]{:S(2)}) collective-permute-start(bf16[128,2048]{1,0:T(8,128)(2,1)S(1)} %pad_maximum_fusion.11), channel_id=1, source_target_pairs={{0,2},{2,0},{4,6},{6,4},{8,10},{10,8},{12,14},{14,12},{16,18},{18,... | collective-permute-start | bytes 1572872 | tf_op jit(solution)/shard_map/ppermute | solution.py:23
  206.3 23.8 %collective-permute-start.35 = (bf16[128,2048]{1,0:T(8,128)(2,1)S(1)}, bf16[128,2048]{1,0:T(8,128)(2,1)S(1)}, u32[]{:S(2)}, u32[]{:S(2)}) collective-permute-start(bf16[128,2048]{1,0:T(8,128)(2,1)S(1)} %pad_maximum_fusion.10), channel_id=1, source_target_pairs={{0,4},{2,6},{4,0},{6,2},{8,12},{10,14},{12,8},{14,10},{16,20},{18,... | collective-permute-start | bytes 1572872 | tf_op jit(solution)/shard_map/ppermute | solution.py:23
  207.6 26.8 %collective-permute-start.33 = (bf16[128,2048]{1,0:T(8,128)(2,1)S(1)}, bf16[128,2048]{1,0:T(8,128)(2,1)S(1)}, u32[]{:S(2)}, u32[]{:S(2)}) collective-permute-start(bf16[128,2048]{1,0:T(8,128)(2,1)S(1)} %pad_maximum_fusion.9), channel_id=1, source_target_pairs={{0,2},{2,0},{4,6},{6,4},{8,10},{10,8},{12,14},{14,12},{16,18},{18,... | collective-permute-start | bytes 1572872 | tf_op jit(solution)/shard_map/ppermute | solution.py:23
  211.9 29.1 %collective-permute-start.25 = (bf16[128,2048]{1,0:T(8,128)(2,1)S(1)}, bf16[128,2048]{1,0:T(8,128)(2,1)S(1)}, u32[]{:S(2)}, u32[]{:S(2)}) collective-permute-start(bf16[128,2048]{1,0:T(8,128)(2,1)S(1)} %pad_maximum_fusion.8), channel_id=1, source_target_pairs={{0,4},{2,6},{4,0},{6,2},{8,12},{10,14},{12,8},{14,10},{16,20},{18,... | collective-permute-start | bytes 1572872 | tf_op jit(solution)/shard_map/ppermute | solution.py:23
  218.8 26.8 %collective-permute-start.23 = (bf16[128,2048]{1,0:T(8,128)(2,1)S(1)}, bf16[128,2048]{1,0:T(8,128)(2,1)S(1)}, u32[]{:S(2)}, u32[]{:S(2)}) collective-permute-start(bf16[128,2048]{1,0:T(8,128)(2,1)S(1)} %pad_maximum_fusion.7), channel_id=1, source_target_pairs={{0,2},{2,0},{4,6},{6,4},{8,10},{10,8},{12,14},{14,12},{16,18},{18,... | collective-permute-start | bytes 1572872 | tf_op jit(solution)/shard_map/ppermute | solution.py:23
  223.1 25.2 %collective-permute-start.16 = (bf16[128,2048]{1,0:T(8,128)(2,1)S(1)}, bf16[128,2048]{1,0:T(8,128)(2,1)S(1)}, u32[]{:S(2)}, u32[]{:S(2)}) collective-permute-start(bf16[128,2048]{1,0:T(8,128)(2,1)S(1)} %pad_maximum_fusion.6), channel_id=1, source_target_pairs={{0,4},{2,6},{4,0},{6,2},{8,12},{10,14},{12,8},{14,10},{16,20},{18,... | collective-permute-start | bytes 1572872 | tf_op jit(solution)/shard_map/ppermute | solution.py:23
  230.1 21.4 %collective-permute-start.14 = (bf16[128,2048]{1,0:T(8,128)(2,1)S(1)}, bf16[128,2048]{1,0:T(8,128)(2,1)S(1)}, u32[]{:S(2)}, u32[]{:S(2)}) collective-permute-start(bf16[128,2048]{1,0:T(8,128)(2,1)S(1)} %pad_maximum_fusion.5), channel_id=1, source_target_pairs={{0,2},{2,0},{4,6},{6,4},{8,10},{10,8},{12,14},{14,12},{16,18},{18,... | collective-permute-start | bytes 1572872 | tf_op jit(solution)/shard_map/ppermute | solution.py:23
  234.3 27.6 %collective-permute-start.46 = (bf16[128,2048]{1,0:T(8,128)(2,1)S(1)}, bf16[128,2048]{1,0:T(8,128)(2,1)S(1)}, u32[]{:S(2)}, u32[]{:S(2)}) collective-permute-start(bf16[128,2048]{1,0:T(8,128)(2,1)S(1)} %add_convert_fusion.1), channel_id=1, source_target_pairs={{0,24},{2,26},{4,28},{6,30},{8,16},{10,18},{12,20},{14,22},{16,8},... | collective-permute-start | bytes 1572872 | tf_op jit(solution)/shard_map/ppermute | solution.py:23
  241.0 28.0 %collective-permute-start.36 = (bf16[128,2048]{1,0:T(8,128)(2,1)S(1)}, bf16[128,2048]{1,0:T(8,128)(2,1)S(1)}, u32[]{:S(2)}, u32[]{:S(2)}) collective-permute-start(bf16[128,2048]{1,0:T(8,128)(2,1)S(1)} %add_convert_fusion.2), channel_id=1, source_target_pairs={{0,16},{2,18},{4,20},{6,22},{8,24},{10,26},{12,28},{14,30},{16,0},... | collective-permute-start | bytes 1572872 | tf_op jit(solution)/shard_map/ppermute | solution.py:23
  245.8 23.2 %collective-permute-start.26 = (bf16[128,2048]{1,0:T(8,128)(2,1)S(1)}, bf16[128,2048]{1,0:T(8,128)(2,1)S(1)}, u32[]{:S(2)}, u32[]{:S(2)}) collective-permute-start(bf16[128,2048]{1,0:T(8,128)(2,1)S(1)} %add_convert_fusion.3), channel_id=1, source_target_pairs={{0,8},{2,10},{4,12},{6,14},{8,0},{10,2},{12,4},{14,6},{16,24},{18,... | collective-permute-start | bytes 1572872 | tf_op jit(solution)/shard_map/ppermute | solution.py:23
  (19 other events, 139.4 us)

commit v3 on v2

v3 whole, which is shorter than its diff:
```python
import functools
import math

import jax
import jax.numpy as jnp
from jax import lax
from jax.experimental import pallas as pl
from jax.experimental.pallas import tpu as pltpu
from jax.sharding import PartitionSpec as P

HD = 128
SWAP = [(0, 1), (1, 0)]
VMEM = pl.BlockSpec(memory_space=pltpu.VMEM)
ANY = pl.BlockSpec(memory_space=pl.ANY)
NT = (((1,), (1,)), ((), ()))


def flip(block, mask):
    count = lax.axis_size("seq")
    return lax.ppermute(block, "seq", [(i, i ^ mask) for i in range(count)])


def gather_small(block):
    mask = 1
    while mask < lax.axis_size("seq"):
        block = jnp.concatenate([block, flip(block, mask)], axis=0)
        mask *= 2
    return block


def attention_kernel(q_ref, own_ref, before_ref, after_ref, qid_ref, kid_ref, _0, _1, _2, _3, out_ref):
    rows = q_ref.shape[0]
    query_pos = lax.broadcasted_iota(jnp.int32, (rows, 3 * rows), 0) + rows
    key_pos = lax.broadcasted_iota(jnp.int32, (rows, 3 * rows), 1)
    allowed = (qid_ref[...] == kid_ref[...]) & (jnp.abs(query_pos - key_pos) < rows)
    for head in range(q_ref.shape[1] // HD):
        cols = slice(head * HD, (head + 1) * HD)
        query = q_ref[:, cols]
        score = jnp.concatenate(
            [
                lax.dot_general(query, ref[:rows, cols], NT, preferred_element_type=jnp.float32)
                for ref in (before_ref, own_ref, after_ref)
            ],
            axis=1,
        ) / math.sqrt(HD)
        score = jnp.where(allowed, score, -jnp.inf)
        weights = jnp.exp(score - jnp.max(score, axis=-1, keepdims=True))
        probs = (weights / jnp.sum(weights, axis=-1, keepdims=True)).astype(jnp.bfloat16)
        total = jnp.zeros((rows, HD), jnp.float32)
        for place, ref in enumerate((before_ref, own_ref, after_ref)):
            total += jnp.dot(
                probs[:, place * rows : (place + 1) * rows],
                ref[rows:, cols],
                preferred_element_type=jnp.float32,
            )
        out_ref[:, cols] = total.astype(jnp.bfloat16)


def attention(queries, own, before, after, query_ids, key_ids, *ahead):
    rows, width = queries.shape
    return pl.pallas_call(
        attention_kernel,
        out_shape=jax.ShapeDtypeStruct(queries.shape, jnp.bfloat16),
        in_specs=[VMEM] * 6 + [ANY] * len(ahead),
        out_specs=VMEM,
        cost_estimate=pl.CostEstimate(
            flops=12 * rows * rows * width, bytes_accessed=5 * 1024 * 1024, transcendentals=0
        ),
        name="window_attention",
    )(queries, own, before, after, query_ids, key_ids, *ahead)


def norm_kernel(mine_ref, theirs_ref, own_w, other_w, resid_ref, gain_ref, stream_ref, normed_ref):
    stream = resid_ref[...].astype(jnp.float32)
    stream += jnp.dot(mine_ref[...], own_w[...], preferred_element_type=jnp.float32)
    stream += jnp.dot(theirs_ref[...], other_w[...], preferred_element_type=jnp.float32)
    meansq = jnp.mean(stream * stream, axis=-1, keepdims=True)
    stream_ref[...] = stream
    normed_ref[...] = (stream * lax.rsqrt(meansq + 1e-05) * gain_ref[...]).astype(jnp.bfloat16)


def project_and_norm(mine, theirs, own_w, other_w, resid, gain):
    rows, width = resid.shape
    return pl.pallas_call(
        norm_kernel,
        out_shape=(
            jax.ShapeDtypeStruct((rows, width), jnp.float32),
            jax.ShapeDtypeStruct((rows, width), jnp.bfloat16),
        ),
        in_specs=[VMEM] * 6,
        out_specs=(VMEM, VMEM),
        cost_estimate=pl.CostEstimate(
            flops=4 * rows * width * mine.shape[1], bytes_accessed=8 * 1024 * 1024, transcendentals=0
        ),
        compiler_params=pltpu.CompilerParams(vmem_limit_bytes=24 * 1024 * 1024),
        name="project_and_norm",
    )(mine, theirs, own_w, other_w, resid, gain)


def expert_kernel(count, *refs):
    blocks, (weight_ref, gate_up, down), outs = refs[:count], refs[count : count + 3], refs[count + 3 :]
    units = down.shape[0]
    for half in range(0, count, 2):
        part = min(2, count - half)
        rows = blocks[0].shape[0]
        tokens = jnp.concatenate([ref[...] for ref in blocks[half : half + part]], axis=0)
        gate = lax.dot_general(tokens, gate_up[:units, :], NT, preferred_element_type=jnp.float32)
        up = lax.dot_general(tokens, gate_up[units:, :], NT, preferred_element_type=jnp.float32)
        act = (gate / (1.0 + jnp.exp(-gate)) * up).astype(jnp.bfloat16)
        result = jnp.dot(act, down[...], preferred_element_type=jnp.float32)
        result = result * weight_ref[half * rows : (half + part) * rows, :]
        for i in range(part):
            outs[half + i][...] = result[i * rows : (i + 1) * rows].astype(jnp.bfloat16)


def expert(blocks, weight, gate_up, down):
    rows, width = blocks[0].shape
    count = len(blocks)
    return pl.pallas_call(
        functools.partial(expert_kernel, count),
        out_shape=[jax.ShapeDtypeStruct((rows, width), jnp.bfloat16)] * count,
        in_specs=[VMEM] * (count + 3),
        out_specs=[VMEM] * count,
        cost_estimate=pl.CostEstimate(
            flops=6 * count * rows * width * down.shape[0],
            bytes_accessed=13 * 1024 * 1024,
            transcendentals=0,
        ),
        compiler_params=pltpu.CompilerParams(vmem_limit_bytes=40 * 1024 * 1024),
        name="expert_rows",
    )(*blocks, weight, gate_up, down)


def add(*terms):
    total = terms[0].astype(jnp.float32)
    for term in terms[1:]:
        total = total + term.astype(jnp.float32)
    return total


def add_small(*terms):
    return add(*terms).astype(jnp.bfloat16)


def expert_layer(normed, stream, weights, gate_up, down):
    count = lax.axis_size("seq")
    rows = normed.shape[0]

    def run(blocks, first):
        part = weights[first * rows : (first + len(blocks)) * rows]
        return expert(blocks, part, gate_up, down)

    if count == 16:
        o0 = normed
        o2, x0, y0, o1, o3 = flip(o0, 8), flip(o0, 1), flip(o0, 2), flip(o0, 4), flip(o0, 12)
        d0 = flip(y0, 1)
        x1 = flip(x0, 4)
        y1 = flip(o1, 2)
        x2, y2 = flip(o2, 1), flip(o2, 2)
        d1 = flip(d0, 4)
        d2 = flip(x2, 2)
        x3, y3 = flip(o3, 1), flip(o3, 2)
        d3 = flip(y3, 1)
        o0, x0, y0, d0 = run([o0, x0, y0, d0], 0)
        o1, x1, y1, d1 = run([o1, x1, y1, d1], 4)
        o2, x2, y2, d2 = run([o2, x2, y2, d2], 8)
        o3, x3, y3, d3 = run([o3, x3, y3, d3], 12)
        d0 = add_small(d0, flip(d1, 4))
        x0 = add_small(x0, flip(x1, 4))
        o1 = add_small(o1, flip(y1, 2))
        x2 = add_small(x2, flip(d2, 2))
        o2 = add_small(o2, flip(x2, 1), flip(y2, 2))
        y3 = add_small(y3, flip(d3, 1))
        o3 = add_small(o3, flip(x3, 1), flip(y3, 2))
        y0 = add_small(y0, flip(d0, 1))
        return add(
            stream, o0, flip(x0, 1), flip(y0, 2), flip(o1, 4), flip(o2, 8), flip(o3, 12)
        )
    blocks, mask = [normed], 1
    while mask < count:
        blocks = blocks + [flip(block, mask) for block in blocks]
        mask *= 2
    parts = []
    for first in range(0, count, 4):
        parts += run(blocks[first : first + 4], first)
    while mask > 1:
        mask //= 2
        parts = [add_small(parts[i], flip(parts[i + mask], mask)) for i in range(mask)]
    return add(stream, parts[0])


def shards(
    queries,
    keys,
    values,
    resid,
    pair_ids,
    out_weight,
    norm_gain,
    experts,
    gates,
    w_gate,
    w_up,
    w_down,
):
    tok_rows = queries.shape[0]
    moe_rows = resid.shape[0]
    shard = lax.axis_index("seq")
    core = lax.axis_index("exp")
    count = lax.axis_size("seq")

    own = jnp.concatenate([keys, values], axis=0)
    before = lax.ppermute(own, "seq", [(i, i + 1) for i in range(count - 1)])
    after = lax.ppermute(own, "seq", [(i + 1, i) for i in range(count - 1)])
    per_expert = jnp.sum(
        jnp.where(
            experts[:, :, None] == jnp.arange(count, dtype=jnp.int32)[None, None, :],
            gates[:, :, None],
            0.0,
        ),
        axis=1,
    )
    my_gate = lax.dynamic_slice_in_dim(gather_small(per_expert), shard, 1, 1)
    out_other = lax.ppermute(out_weight, "exp", SWAP)
    own_up = jnp.swapaxes(w_up[0], 0, 1)
    own_gate = jnp.swapaxes(w_gate[0], 0, 1)
    units = own_gate.shape[0]
    own_w = jnp.concatenate([own_gate, own_up, w_down[0]], axis=0)
    other_w = lax.ppermute(own_w, "exp", SWAP)
    gate_up = jnp.concatenate(
        [own_gate, other_w[:units], own_up, other_w[units : 2 * units]], axis=0
    )
    down = jnp.concatenate([w_down[0], other_w[2 * units :]], axis=0)

    id_pad = jnp.pad(pair_ids, (tok_rows, tok_rows), constant_values=-1)
    key_ids = lax.dynamic_slice_in_dim(id_pad, shard * tok_rows, 3 * tok_rows, 0)
    query_ids = lax.dynamic_slice_in_dim(pair_ids, shard * tok_rows, tok_rows, 0)
    attended = attention(
        queries,
        own,
        before,
        after,
        query_ids[:, None],
        key_ids[None, :],
        my_gate,
        out_other,
        gate_up,
        down,
    )
    mine = lax.dynamic_slice_in_dim(attended, core * moe_rows, moe_rows, 0)
    theirs = lax.dynamic_slice_in_dim(attended, (1 - core) * moe_rows, moe_rows, 0)
    received = lax.ppermute(theirs, "exp", SWAP)
    stream, normed = project_and_norm(
        mine, received, out_weight, out_other, resid, norm_gain[None, :]
    )
    return expert_layer(normed, stream, my_gate, gate_up, down).astype(jnp.bfloat16)


def solution(mesh):
    in_specs = (
        P("seq", "exp"),
        P("seq", "exp"),
        P("seq", "exp"),
        P(("seq", "exp"), None),
        P(),
        P("exp", None),
        P(),
        P(("seq", "exp"), None),
        P(("seq", "exp"), None),
        P("seq", None, "exp"),
        P("seq", None, "exp"),
        P("seq", "exp", None),
    )
    out_specs = P(("seq", "exp"), None)
    return jax.shard_map(shards, mesh=mesh, in_specs=in_specs, out_specs=out_specs, check_vma=False)
```

time: 276 us -> 282 us (1.022); the launches traced: 270 us -> 281 us
  matrix products: 41.5 us -> 0 us
  Pallas kernels: 0 us -> 27.6 us
  waiting for transfers between devices: 153 us -> 179 us
  starting transfers between devices: 50.9 us -> 40.8 us
  other arithmetic: 12.2 us -> 20.9 us
    dot_general x12 -> x0, matrix products: 41.5 us -> none  [the longest x4 23.8 us: expert(): lax.dot_general(tokens, gate_up, (((1,), (1,)), ((), ())), preferred_elem...]
    ppermute x42 -> x34, waiting for transfers between devices: 137 us -> 177 us  [flip(): return lax.ppermute(block, 'seq', [(i, i ^ mask) for i in range(count)])]
    pallas_call x0 -> x6, Pallas kernels: none -> 27.6 us  [the longest x4 20.5 us: expert(): pl.pallas_call(functools.partial(expert_kernel, count), out_shape=[jax.Sh...]
    ppermute x3, waiting for transfers between devices: 16.5 us -> 0.01 us  [the longest x1 0.01 us: shards(): other_w = lax.ppermute(own_w, 'exp', SWAP)]
    concatenate x10 -> x3, other arithmetic: 5.41 us -> 18.3 us  [the longest x1 12.6 us: shards(): jnp.concatenate([own_gate, other_w[:units], own_up, other_w[units:2 * uni...]
    ppermute x42 -> x34, starting transfers between devices: 43.5 us -> 34.8 us  [flip(): return lax.ppermute(block, 'seq', [(i, i ^ mask) for i in range(count)])]
    slice x15 -> x2, local copies, waits for them, and re-layouts: 7.44 us -> 2.78 us  [the longest x1 2.71 us: shards(): down = jnp.concatenate([w_down[0], other_w[2 * units:]], axis=0)]
    unnamed x46 -> x38, local copies, waits for them, and re-layouts: 4.61 us -> 7.33 us
  transfers between devices with their start and end apart: 47 -> 39, of which waited for: 25 -> 20; matrix products, arithmetic and copies ran while one was open for 22% -> 8% of each run, Pallas kernels for 0% -> 7%
where the time goes in v3:
time: 282 us; the launch traced here: 281 us
  waiting for transfers between devices  179 us (63%)
  starting transfers between devices  40.8 us (14%)
  Pallas kernels  27.6 us (10%)
  other arithmetic  20.9 us (7%)
  local copies, waits for them, and re-layouts  12.8 us (5%)
    ppermute x34, waiting for transfers between devices, flip(): return lax.ppermute(block, 'seq', [(i, i ^ mask) for i in range(count)])  177 us
    ppermute x34, starting transfers between devices, flip(): return lax.ppermute(block, 'seq', [(i, i ^ mask) for i in range(count)])  34.8 us
    pallas_call x4, Pallas kernels, expert(): pl.pallas_call(functools.partial(expert_kernel, count), out_shape=[jax.Sh...  20.5 us
    concatenate x1, other arithmetic, shards(): jnp.concatenate([own_gate, other_w[:units], own_up, other_w[units:2 * uni...  12.6 us
    unnamed x38, local copies, waits for them, and re-layouts  7.33 us
  transfers between devices with their start and end apart: 39, of which 20 were waited for; matrix products, arithmetic and copies ran while one was open for 8% of the time, Pallas kernels for 7%

profile of v3, /device:TPU:10, one launch (start us, length us, event | category | flops | bytes accessed | tf_op | source)
XLA Modules:
  0.0 281.0 jit_solution(16574489011387633622)
XLA Ops:
  0.0 3.8 %pad_maximum_fusion.1 = bf16[1056,2048]{1,0:T(8,128)(2,1)} fusion(bf16[352,2048]{1,0:T(8,128)(2,1)} %bitcast.14, bf16[352,2048]{1,0:T(8,128)(2,1)} %bitcast.10, bf16[352,2048]{1,0:T(8,128)(2,1)} %bitcast.12), kind=kLoop, calls=%fused_computation.1 | loop fusion | flops 12976128 | bytes 8650752 | tf_op jit(solution)/shard_map/concatenate | solution.py:228
  4.0 3.4 %collective-permute-start = (bf16[512,512]{1,0:T(8,128)(2,1)S(1)}, bf16[512,512]{1,0:T(8,128)(2,1)}, u32[]{:S(2)}, u32[]{:S(2)}) collective-permute-start(bf16[512,512]{1,0:T(8,128)(2,1)S(1)} %constant_dynamic-update-slice_fusion.own_ref), channel_id=1, source_target_pairs={{0,2},{2,4},{4,6},{6,8},{8,10},{10,12},{12,14},{14,16},{16,18},{18... | collective-permute-start | bytes 1572872 | tf_op jit(solution)/shard_map/ppermute | solution.py:213
  7.4 2.4 collective-permute-start.1
  9.9 2.4 collective-permute-start.2
  13.8 17.8 %collective-permute-done.2 = f32[128,16]{0,1:T(8,128)S(1)} collective-permute-done((f32[128,16]{0,1:T(8,128)S(1)}, f32[128,16]{0,1:T(8,128)S(1)}, u32[]{:S(2)}, u32[]{:S(2)}) %collective-permute-start.2) | collective-permute-done | bytes 8224 | tf_op jit(solution)/shard_map/ppermute | solution.py:20
  31.6 1.5 collective-permute-start.3
  33.1 2.2 collective-permute-done.3
  35.8 3.5 %collective-permute-done.4 = f32[512,16]{0,1:T(8,128)S(1)} collective-permute-done((f32[512,16]{0,1:T(8,128)S(1)}, f32[512,16]{0,1:T(8,128)S(1)}, u32[]{:S(2)}, u32[]{:S(2)}) %collective-permute-start.4) | collective-permute-done | bytes 32800 | tf_op jit(solution)/shard_map/ppermute | solution.py:20
  39.3 2.1 collective-permute-start.5
  41.4 3.1 %collective-permute-done.5 = f32[1024,16]{0,1:T(8,128)S(1)} collective-permute-done((f32[1024,16]{0,1:T(8,128)S(1)}, f32[1024,16]{0,1:T(8,128)S(1)}, u32[]{:S(2)}, u32[]{:S(2)}) %collective-permute-start.5) | collective-permute-done | bytes 65568 | tf_op jit(solution)/shard_map/ppermute | solution.py:20
  44.5 1.4 copy.24._0
  45.8 2.7 fusion
  48.9 12.6 %pad_maximum_fusion._2.refs_5_ = bf16[1408,2048]{1,0:T(8,128)(2,1)} fusion(bf16[352,2048]{1,0:T(8,128)(2,1)S(1)} %get-tuple-element.42, bf16[352,2048]{1,0:T(8,128)(2,1)S(1)} %bitcast.11, bf16[352,2048]{1,0:T(8,128)(2,1)S(1)} %get-tuple-element.43, bf16[352,2048]{1,0:T(8,128)(2,1)S(1)} %bitcast.13), kind=kLoop, calls=%fused_computation | loop fusion | flops 23068672 | bytes 11534336 | tf_op jit(solution)/shard_map/concatenate | solution.py:230
  61.5 1.8 pad_maximum_fusion.2._3.refs_6_
  63.4 1.3 copy-done.2
  64.7 4.5 %window_attention.1 = bf16[256,512]{1,0:T(8,128)(2,1)} custom-call(bf16[256,512]{1,0:T(8,128)(2,1)} %q_ref.1, bf16[512,512]{1,0:T(8,128)(2,1)} %copy-done.10, bf16[512,512]{1,0:T(8,128)(2,1)} %collective-permute-done.before_ref, bf16[512,512]{1,0:T(8,128)(2,1)} %collective-permute-done.1.after_ref, s32[256,1]{1,0:T(8,128)} %copy.23.qid_ref, ...), custom_call_target="tpu_custom_call" | custom-call | flops 402653184 | bytes 5242880 | tf_op jit(solution)/shard_map/window_attention/pallas_call | solution.py:61
  69.2 1.1 constant_dynamic-slice_fusion
  70.4 1.3 collective-permute-done.8.theirs_ref
  71.8 1.6 copy-done.3
  73.4 2.6 project_and_norm.1
  75.9 1.6 collective-permute-start.10
  77.5 1.4 collective-permute-start.9
  78.9 3.2 %collective-permute-start.23 = (bf16[128,2048]{1,0:T(8,128)(2,1)S(1)}, bf16[128,2048]{1,0:T(8,128)(2,1)S(1)}, u32[]{:S(2)}, u32[]{:S(2)}) collective-permute-start(bf16[128,2048]{1,0:T(8,128)(2,1)S(1)} %get-tuple-element.24.refs_0_), channel_id=1, source_target_pairs={{0,16},{2,18},{4,20},{6,22},{8,24},{10,26},{12,28},{14,30},{16,0},... | collective-permute-start | bytes 1572872 | tf_op jit(solution)/shard_map/ppermute | solution.py:20
  82.6 7.4 %collective-permute-done.10.refs_2_ = bf16[128,2048]{1,0:T(8,128)(2,1)S(1)} collective-permute-done((bf16[128,2048]{1,0:T(8,128)(2,1)S(1)}, bf16[128,2048]{1,0:T(8,128)(2,1)S(1)}, u32[]{:S(2)}, u32[]{:S(2)}) %collective-permute-start.10) | collective-permute-done | bytes 524320 | tf_op jit(solution)/shard_map/ppermute | solution.py:20
  90.0 1.5 collective-permute-start.11
  91.9 13.0 %collective-permute-done.23.refs_0_ = bf16[128,2048]{1,0:T(8,128)(2,1)S(1)} collective-permute-done((bf16[128,2048]{1,0:T(8,128)(2,1)S(1)}, bf16[128,2048]{1,0:T(8,128)(2,1)S(1)}, u32[]{:S(2)}, u32[]{:S(2)}) %collective-permute-start.23) | collective-permute-done | bytes 524320 | tf_op jit(solution)/shard_map/ppermute | solution.py:20
  106.7 19.4 %collective-permute-done.31.refs_0_ = bf16[128,2048]{1,0:T(8,128)(2,1)S(1)} collective-permute-done((bf16[128,2048]{1,0:T(8,128)(2,1)S(1)}, bf16[128,2048]{1,0:T(8,128)(2,1)S(1)}, u32[]{:S(2)}, u32[]{:S(2)}) %collective-permute-start.31) | collective-permute-done | bytes 524320 | tf_op jit(solution)/shard_map/ppermute | solution.py:20
  127.2 1.1 collective-permute-start.25
  129.2 2.6 copy-done
  131.8 5.1 %expert_rows.4 = (bf16[128,2048]{1,0:T(8,128)(2,1)S(1)}, bf16[128,2048]{1,0:T(8,128)(2,1)S(1)}, bf16[128,2048]{1,0:T(8,128)(2,1)S(1)}, bf16[128,2048]{1,0:T(8,128)(2,1)S(1)}) custom-call(bf16[128,2048]{1,0:T(8,128)(2,1)S(1)} %get-tuple-element.24.refs_0_, bf16[128,2048]{1,0:T(8,128)(2,1)S(1)} %collective-permute-done.9.refs_1_, ...), custom_call_target="tpu_custom_call" | custom-call | flops 4429185024 | bytes 13631488 | tf_op jit(solution)/shard_map/expert_rows/pallas_call | solution.py:119
  138.0 2.9 %collective-permute-done.33.refs_2_ = bf16[128,2048]{1,0:T(8,128)(2,1)S(1)} collective-permute-done((bf16[128,2048]{1,0:T(8,128)(2,1)S(1)}, bf16[128,2048]{1,0:T(8,128)(2,1)S(1)}, u32[]{:S(2)}, u32[]{:S(2)}) %collective-permute-start.33) | collective-permute-done | bytes 524320 | tf_op jit(solution)/shard_map/ppermute | solution.py:20
  141.9 5.3 %expert_rows.5 = (bf16[128,2048]{1,0:T(8,128)(2,1)S(1)}, bf16[128,2048]{1,0:T(8,128)(2,1)S(1)}, bf16[128,2048]{1,0:T(8,128)(2,1)S(1)}, bf16[128,2048]{1,0:T(8,128)(2,1)S(1)}) custom-call(bf16[128,2048]{1,0:T(8,128)(2,1)S(1)} %collective-permute-done.12.refs_0_, bf16[128,2048]{1,0:T(8,128)(2,1)S(1)} %collective-permute-done.13.refs_1_, ...), custom_call_target="tpu_custom_call" | custom-call | flops 4429185024 | bytes 13631488 | tf_op jit(solution)/shard_map/expert_rows/pallas_call | solution.py:119
  147.6 4.5 %collective-permute-done.25.refs_2_ = bf16[128,2048]{1,0:T(8,128)(2,1)S(1)} collective-permute-done((bf16[128,2048]{1,0:T(8,128)(2,1)S(1)}, bf16[128,2048]{1,0:T(8,128)(2,1)S(1)}, u32[]{:S(2)}, u32[]{:S(2)}) %collective-permute-start.25) | collective-permute-done | bytes 524320 | tf_op jit(solution)/shard_map/ppermute | solution.py:20
  152.1 10.3 %collective-permute-done.26.refs_3_ = bf16[128,2048]{1,0:T(8,128)(2,1)S(1)} collective-permute-done((bf16[128,2048]{1,0:T(8,128)(2,1)S(1)}, bf16[128,2048]{1,0:T(8,128)(2,1)S(1)}, u32[]{:S(2)}, u32[]{:S(2)}) %collective-permute-start.26) | collective-permute-done | bytes 524320 | tf_op jit(solution)/shard_map/ppermute | solution.py:20
  163.1 5.1 %expert_rows.6 = (bf16[128,2048]{1,0:T(8,128)(2,1)S(1)}, bf16[128,2048]{1,0:T(8,128)(2,1)S(1)}, bf16[128,2048]{1,0:T(8,128)(2,1)S(1)}, bf16[128,2048]{1,0:T(8,128)(2,1)S(1)}) custom-call(bf16[128,2048]{1,0:T(8,128)(2,1)S(1)} %collective-permute-done.23.refs_0_, bf16[128,2048]{1,0:T(8,128)(2,1)S(1)} %collective-permute-done.24.refs_1_, ...), custom_call_target="tpu_custom_call" | custom-call | flops 4429185024 | bytes 13631488 | tf_op jit(solution)/shard_map/expert_rows/pallas_call | solution.py:119
  168.2 1.5 collective-permute-start.27
  170.3 5.1 %expert_rows.7 = (bf16[128,2048]{1,0:T(8,128)(2,1)S(1)}, bf16[128,2048]{1,0:T(8,128)(2,1)S(1)}, bf16[128,2048]{1,0:T(8,128)(2,1)S(1)}, bf16[128,2048]{1,0:T(8,128)(2,1)S(1)}) custom-call(bf16[128,2048]{1,0:T(8,128)(2,1)S(1)} %collective-permute-done.31.refs_0_, bf16[128,2048]{1,0:T(8,128)(2,1)S(1)} %collective-permute-done.32.refs_1_, ...), custom_call_target="tpu_custom_call" | custom-call | flops 4429185024 | bytes 13631488 | tf_op jit(solution)/shard_map/expert_rows/pallas_call | solution.py:119
  176.3 1.3 collective-permute-start.35
  178.8 9.8 %collective-permute-done.27 = bf16[128,2048]{1,0:T(8,128)(2,1)S(1)} collective-permute-done((bf16[128,2048]{1,0:T(8,128)(2,1)S(1)}, bf16[128,2048]{1,0:T(8,128)(2,1)S(1)}, u32[]{:S(2)}, u32[]{:S(2)}) %collective-permute-start.27) | collective-permute-done | bytes 524320 | tf_op jit(solution)/shard_map/ppermute | solution.py:20
  191.2 32.8 %collective-permute-done.19 = bf16[128,2048]{1,0:T(8,128)(2,1)S(1)} collective-permute-done((bf16[128,2048]{1,0:T(8,128)(2,1)S(1)}, bf16[128,2048]{1,0:T(8,128)(2,1)S(1)}, u32[]{:S(2)}, u32[]{:S(2)}) %collective-permute-start.19) | collective-permute-done | bytes 524320 | tf_op jit(solution)/shard_map/ppermute | solution.py:20
  224.0 1.4 collective-permute-start.37
  225.6 6.9 %collective-permute-done.28 = bf16[128,2048]{1,0:T(8,128)(2,1)S(1)} collective-permute-done((bf16[128,2048]{1,0:T(8,128)(2,1)S(1)}, bf16[128,2048]{1,0:T(8,128)(2,1)S(1)}, u32[]{:S(2)}, u32[]{:S(2)}) %collective-permute-start.28) | collective-permute-done | bytes 524320 | tf_op jit(solution)/shard_map/ppermute | solution.py:20
  232.5 1.4 collective-permute-start.20
  234.5 2.5 collective-permute-start.38
  237.1 7.3 %collective-permute-done.20 = bf16[128,2048]{1,0:T(8,128)(2,1)S(1)} collective-permute-done((bf16[128,2048]{1,0:T(8,128)(2,1)S(1)}, bf16[128,2048]{1,0:T(8,128)(2,1)S(1)}, u32[]{:S(2)}, u32[]{:S(2)}) %collective-permute-start.20) | collective-permute-done | bytes 524320 | tf_op jit(solution)/shard_map/ppermute | solution.py:20
  244.4 24.3 %collective-permute-done.30 = bf16[128,2048]{1,0:T(8,128)(2,1)S(1)} collective-permute-done((bf16[128,2048]{1,0:T(8,128)(2,1)S(1)}, bf16[128,2048]{1,0:T(8,128)(2,1)S(1)}, u32[]{:S(2)}, u32[]{:S(2)}) %collective-permute-start.30) | collective-permute-done | bytes 524320 | tf_op jit(solution)/shard_map/ppermute | solution.py:20
  268.7 10.9 %collective-permute-done.38 = bf16[128,2048]{1,0:T(8,128)(2,1)S(1)} collective-permute-done((bf16[128,2048]{1,0:T(8,128)(2,1)S(1)}, bf16[128,2048]{1,0:T(8,128)(2,1)S(1)}, u32[]{:S(2)}, u32[]{:S(2)}) %collective-permute-start.38) | collective-permute-done | bytes 524320 | tf_op jit(solution)/shard_map/ppermute | solution.py:20
  279.6 1.3 add_convert_fusion
  (100 shorter events, 16.5 us)
Async XLA Ops:
  0.0 9.8 %copy-start.14 = (f32[128,6]{0,1:T(8,128)S(1)}, f32[128,6]{0,1:T(8,128)}, u32[]{:S(2)}) copy-start(f32[128,6]{0,1:T(8,128)} %param.20) | copy-start | bytes 9220
  0.0 9.8 %copy-start.15 = (s32[128,6]{0,1:T(8,128)S(1)}, s32[128,6]{0,1:T(8,128)}, u32[]{:S(2)}) copy-start(s32[128,6]{0,1:T(8,128)} %param.19) | copy-start | bytes 9220
  0.0 12.2 %copy-start.13 = (s32[4096]{0:T(1024)S(1)}, s32[4096]{0:T(1024)}, u32[]{:S(2)}) copy-start(s32[4096]{0:T(1024)} %param.16) | copy-start | bytes 49156
  3.9 42.0 %collective-permute-start.7 = (bf16[1056,2048]{1,0:T(8,128)(2,1)}, bf16[1056,2048]{1,0:T(8,128)(2,1)}, u32[]{:S(2)}, u32[]{:S(2)}) collective-permute-start(bf16[1056,2048]{1,0:T(8,128)(2,1)} %pad_maximum_fusion.1), channel_id=1, source_target_pairs={{0,1},{1,0},{2,3},{3,2},{4,5},{5,4},{6,7},{7,6},{8,9},{9,8},{10,11... | collective-permute-start | bytes 12976136 | tf_op jit(solution)/shard_map/ppermute | solution.py:229
  4.0 44.6 %copy-start.10 = (bf16[512,512]{1,0:T(8,128)(2,1)}, bf16[512,512]{1,0:T(8,128)(2,1)S(1)}, u32[]{:S(2)}) copy-start(bf16[512,512]{1,0:T(8,128)(2,1)S(1)} %constant_dynamic-update-slice_fusion.own_ref) | copy-start | bytes 1572868
  4.0 59.4 %collective-permute-start = (bf16[512,512]{1,0:T(8,128)(2,1)S(1)}, bf16[512,512]{1,0:T(8,128)(2,1)}, u32[]{:S(2)}, u32[]{:S(2)}) collective-permute-start(bf16[512,512]{1,0:T(8,128)(2,1)S(1)} %constant_dynamic-update-slice_fusion.own_ref), channel_id=1, source_target_pairs={{0,2},{2,4},{4,6},{6,8},{8,10},{10,12},{12,14},{14,16},{16,18},{18... | collective-permute-start | bytes 1572872 | tf_op jit(solution)/shard_map/ppermute | solution.py:213
  7.4 56.0 %collective-permute-start.1 = (bf16[512,512]{1,0:T(8,128)(2,1)S(1)}, bf16[512,512]{1,0:T(8,128)(2,1)}, u32[]{:S(2)}, u32[]{:S(2)}) collective-permute-start(bf16[512,512]{1,0:T(8,128)(2,1)S(1)} %constant_dynamic-update-slice_fusion.own_ref), channel_id=1, source_target_pairs={{2,0},{4,2},{6,4},{8,6},{10,8},{12,10},{14,12},{16,14},{18,16},{20... | collective-permute-start | bytes 1572872 | tf_op jit(solution)/shard_map/ppermute | solution.py:214
  9.9 21.8 %collective-permute-start.2 = (f32[128,16]{0,1:T(8,128)S(1)}, f32[128,16]{0,1:T(8,128)S(1)}, u32[]{:S(2)}, u32[]{:S(2)}) collective-permute-start(f32[128,16]{0,1:T(8,128)S(1)} %select_reduce_fusion), channel_id=1, source_target_pairs={{0,2},{2,0},{4,6},{6,4},{8,10},{10,8},{12,14},{14,12},{16,18},{18,... | collective-permute-start | bytes 24584 | tf_op jit(solution)/shard_map/ppermute | solution.py:20
  12.3 51.1 %collective-permute-start.6 = (bf16[512,2048]{1,0:T(8,128)(2,1)}, bf16[512,2048]{1,0:T(8,128)(2,1)S(1)}, u32[]{:S(2)}, u32[]{:S(2)}) collective-permute-start(bf16[512,2048]{1,0:T(8,128)(2,1)} %own_w.1), channel_id=1, source_target_pairs={{0,1},{1,0},{2,3},{3,2},{4,5},{5,4},{6,7},{7,6},{8,9},{9,8},{10,11... | collective-permute-start | bytes 6291464 | tf_op jit(solution)/shard_map/ppermute | solution.py:224
  31.6 3.7 %collective-permute-start.3 = (f32[256,16]{0,1:T(8,128)S(1)}, f32[256,16]{0,1:T(8,128)S(1)}, u32[]{:S(2)}, u32[]{:S(2)}) collective-permute-start(f32[256,16]{0,1:T(8,128)S(1)} %pad_maximum_fusion.5), channel_id=1, source_target_pairs={{0,4},{2,6},{4,0},{6,2},{8,12},{10,14},{12,8},{14,10},{16,20},{18,... | collective-permute-start | bytes 49160 | tf_op jit(solution)/shard_map/ppermute | solution.py:20
  35.4 3.9 %collective-permute-start.4 = (f32[512,16]{0,1:T(8,128)S(1)}, f32[512,16]{0,1:T(8,128)S(1)}, u32[]{:S(2)}, u32[]{:S(2)}) collective-permute-start(f32[512,16]{0,1:T(8,128)S(1)} %pad_maximum_fusion.4), channel_id=1, source_target_pairs={{0,8},{2,10},{4,12},{6,14},{8,0},{10,2},{12,4},{14,6},{16,24},{18,... | collective-permute-start | bytes 98312 | tf_op jit(solution)/shard_map/ppermute | solution.py:20
  39.3 5.2 %collective-permute-start.5 = (f32[1024,16]{0,1:T(8,128)S(1)}, f32[1024,16]{0,1:T(8,128)S(1)}, u32[]{:S(2)}, u32[]{:S(2)}) collective-permute-start(f32[1024,16]{0,1:T(8,128)S(1)} %pad_maximum_fusion.3), channel_id=1, source_target_pairs={{0,16},{2,18},{4,20},{6,22},{8,24},{10,26},{12,28},{14,30},{16,0},... | collective-permute-start | bytes 196616 | tf_op jit(solution)/shard_map/ppermute | solution.py:20
  48.9 12.6 %copy-start.9 = (bf16[1,352,2048]{2,1,0:T(8,128)(2,1)S(1)}, bf16[1,352,2048]{2,1,0:T(8,128)(2,1)}, u32[]{:S(2)}) copy-start(bf16[1,352,2048]{2,1,0:T(8,128)(2,1)} %param.23) | copy-start | bytes 4325380
  63.4 8.4 %copy-start.4 = (bf16[128,2048]{1,0:T(8,128)(2,1)S(1)}, bf16[128,2048]{1,0:T(8,128)(2,1)}, u32[]{:S(2)}) copy-start(bf16[128,2048]{1,0:T(8,128)(2,1)} %resid_ref.1) | copy-start | bytes 1572868
  63.4 8.4 %copy-start.5 = (f32[2048]{0:T(1024)S(1)}, f32[2048]{0:T(1024)}, u32[]{:S(2)}) copy-start(f32[2048]{0:T(1024)} %param.18) | copy-start | bytes 24580
  69.2 60.0 %copy-start.1 = (bf16[704,2048]{1,0:T(8,128)(2,1)S(1)}, bf16[704,2048]{1,0:T(8,128)(2,1)}, u32[]{:S(2)}) copy-start(bf16[704,2048]{1,0:T(8,128)(2,1)} %pad_maximum_fusion.2._3.refs_6_) | copy-start | bytes 8650756
  70.4 1.4 collective-permute-start.8
  73.4 53.4 %copy-start.6 = (f32[2048,1]{1,0:T(8,128)S(1)}, f32[2048,1]{1,0:T(8,128)}, u32[]{:S(2)}) copy-start(f32[2048,1]{1,0:T(8,128)} %copy.24._0) | copy-start | bytes 24580
  75.9 14.0 %collective-permute-start.10 = (bf16[128,2048]{1,0:T(8,128)(2,1)S(1)}, bf16[128,2048]{1,0:T(8,128)(2,1)S(1)}, u32[]{:S(2)}, u32[]{:S(2)}) collective-permute-start(bf16[128,2048]{1,0:T(8,128)(2,1)S(1)} %get-tuple-element.24.refs_0_), channel_id=1, source_target_pairs={{0,4},{2,6},{4,0},{6,2},{8,12},{10,14},{12,8},{14,10},{16,20},{18,... | collective-permute-start | bytes 1572872 | tf_op jit(solution)/shard_map/ppermute | solution.py:20
  77.5 14.0 %collective-permute-start.9 = (bf16[128,2048]{1,0:T(8,128)(2,1)S(1)}, bf16[128,2048]{1,0:T(8,128)(2,1)S(1)}, u32[]{:S(2)}, u32[]{:S(2)}) collective-permute-start(bf16[128,2048]{1,0:T(8,128)(2,1)S(1)} %get-tuple-element.24.refs_0_), channel_id=1, source_target_pairs={{0,2},{2,0},{4,6},{6,4},{8,10},{10,8},{12,14},{14,12},{16,18},{18,... | collective-permute-start | bytes 1572872 | tf_op jit(solution)/shard_map/ppermute | solution.py:20
  78.9 26.0 %collective-permute-start.23 = (bf16[128,2048]{1,0:T(8,128)(2,1)S(1)}, bf16[128,2048]{1,0:T(8,128)(2,1)S(1)}, u32[]{:S(2)}, u32[]{:S(2)}) collective-permute-start(bf16[128,2048]{1,0:T(8,128)(2,1)S(1)} %get-tuple-element.24.refs_0_), channel_id=1, source_target_pairs={{0,16},{2,18},{4,20},{6,22},{8,24},{10,26},{12,28},{14,30},{16,0},... | collective-permute-start | bytes 1572872 | tf_op jit(solution)/shard_map/ppermute | solution.py:20
  82.1 24.0 %collective-permute-start.12 = (bf16[128,2048]{1,0:T(8,128)(2,1)S(1)}, bf16[128,2048]{1,0:T(8,128)(2,1)S(1)}, u32[]{:S(2)}, u32[]{:S(2)}) collective-permute-start(bf16[128,2048]{1,0:T(8,128)(2,1)S(1)} %get-tuple-element.24.refs_0_), channel_id=1, source_target_pairs={{0,8},{2,10},{4,12},{6,14},{8,0},{10,2},{12,4},{14,6},{16,24},{18,... | collective-permute-start | bytes 1572872 | tf_op jit(solution)/shard_map/ppermute | solution.py:20
  82.1 44.0 %collective-permute-start.31 = (bf16[128,2048]{1,0:T(8,128)(2,1)S(1)}, bf16[128,2048]{1,0:T(8,128)(2,1)S(1)}, u32[]{:S(2)}, u32[]{:S(2)}) collective-permute-start(bf16[128,2048]{1,0:T(8,128)(2,1)S(1)} %get-tuple-element.24.refs_0_), channel_id=1, source_target_pairs={{0,24},{2,26},{4,28},{6,30},{8,16},{10,18},{12,20},{14,22},{16,8},... | collective-permute-start | bytes 1572872 | tf_op jit(solution)/shard_map/ppermute | solution.py:20
  90.0 36.8 %collective-permute-start.11 = (bf16[128,2048]{1,0:T(8,128)(2,1)S(1)}, bf16[128,2048]{1,0:T(8,128)(2,1)S(1)}, u32[]{:S(2)}, u32[]{:S(2)}) collective-permute-start(bf16[128,2048]{1,0:T(8,128)(2,1)S(1)} %collective-permute-done.10.refs_2_), channel_id=1, source_target_pairs={{0,2},{2,0},{4,6},{6,4},{8,10},{10,8},{12,14},{14,12},{16,18},{18,... | collective-permute-start | bytes 1572872 | tf_op jit(solution)/shard_map/ppermute | solution.py:20
  91.5 35.7 %collective-permute-start.13 = (bf16[128,2048]{1,0:T(8,128)(2,1)S(1)}, bf16[128,2048]{1,0:T(8,128)(2,1)S(1)}, u32[]{:S(2)}, u32[]{:S(2)}) collective-permute-start(bf16[128,2048]{1,0:T(8,128)(2,1)S(1)} %collective-permute-done.9.refs_1_), channel_id=1, source_target_pairs={{0,8},{2,10},{4,12},{6,14},{8,0},{10,2},{12,4},{14,6},{16,24},{18,... | collective-permute-start | bytes 1572872 | tf_op jit(solution)/shard_map/ppermute | solution.py:20
  104.9 23.4 %collective-permute-start.24 = (bf16[128,2048]{1,0:T(8,128)(2,1)S(1)}, bf16[128,2048]{1,0:T(8,128)(2,1)S(1)}, u32[]{:S(2)}, u32[]{:S(2)}) collective-permute-start(bf16[128,2048]{1,0:T(8,128)(2,1)S(1)} %collective-permute-done.23.refs_0_), channel_id=1, source_target_pairs={{0,2},{2,0},{4,6},{6,4},{8,10},{10,8},{12,14},{14,12},{16,18},{18,... | collective-permute-start | bytes 1572872 | tf_op jit(solution)/shard_map/ppermute | solution.py:20
  106.1 30.8 %collective-permute-start.14 = (bf16[128,2048]{1,0:T(8,128)(2,1)S(1)}, bf16[128,2048]{1,0:T(8,128)(2,1)S(1)}, u32[]{:S(2)}, u32[]{:S(2)}) collective-permute-start(bf16[128,2048]{1,0:T(8,128)(2,1)S(1)} %collective-permute-done.12.refs_0_), channel_id=1, source_target_pairs={{0,4},{2,6},{4,0},{6,2},{8,12},{10,14},{12,8},{14,10},{16,20},{18,... | collective-permute-start | bytes 1572872 | tf_op jit(solution)/shard_map/ppermute | solution.py:20
  126.1 14.8 %collective-permute-start.33 = (bf16[128,2048]{1,0:T(8,128)(2,1)S(1)}, bf16[128,2048]{1,0:T(8,128)(2,1)S(1)}, u32[]{:S(2)}, u32[]{:S(2)}) collective-permute-start(bf16[128,2048]{1,0:T(8,128)(2,1)S(1)} %collective-permute-done.31.refs_0_), channel_id=1, source_target_pairs={{0,4},{2,6},{4,0},{6,2},{8,12},{10,14},{12,8},{14,10},{16,20},{18,... | collective-permute-start | bytes 1572872 | tf_op jit(solution)/shard_map/ppermute | solution.py:20
  126.8 15.2 %collective-permute-start.15 = (bf16[128,2048]{1,0:T(8,128)(2,1)S(1)}, bf16[128,2048]{1,0:T(8,128)(2,1)S(1)}, u32[]{:S(2)}, u32[]{:S(2)}) collective-permute-start(bf16[128,2048]{1,0:T(8,128)(2,1)S(1)} %collective-permute-done.11.refs_3_), channel_id=1, source_target_pairs={{0,8},{2,10},{4,12},{6,14},{8,0},{10,2},{12,4},{14,6},{16,24},{18,... | collective-permute-start | bytes 1572872 | tf_op jit(solution)/shard_map/ppermute | solution.py:20
  127.2 25.0 %collective-permute-start.25 = (bf16[128,2048]{1,0:T(8,128)(2,1)S(1)}, bf16[128,2048]{1,0:T(8,128)(2,1)S(1)}, u32[]{:S(2)}, u32[]{:S(2)}) collective-permute-start(bf16[128,2048]{1,0:T(8,128)(2,1)S(1)} %collective-permute-done.23.refs_0_), channel_id=1, source_target_pairs={{0,4},{2,6},{4,0},{6,2},{8,12},{10,14},{12,8},{14,10},{16,20},{18,... | collective-permute-start | bytes 1572872 | tf_op jit(solution)/shard_map/ppermute | solution.py:20
  128.3 34.1 %collective-permute-start.26 = (bf16[128,2048]{1,0:T(8,128)(2,1)S(1)}, bf16[128,2048]{1,0:T(8,128)(2,1)S(1)}, u32[]{:S(2)}, u32[]{:S(2)}) collective-permute-start(bf16[128,2048]{1,0:T(8,128)(2,1)S(1)} %collective-permute-done.24.refs_1_), channel_id=1, source_target_pairs={{0,4},{2,6},{4,0},{6,2},{8,12},{10,14},{12,8},{14,10},{16,20},{18,... | collective-permute-start | bytes 1572872 | tf_op jit(solution)/shard_map/ppermute | solution.py:20
  136.9 31.2 %collective-permute-start.32 = (bf16[128,2048]{1,0:T(8,128)(2,1)S(1)}, bf16[128,2048]{1,0:T(8,128)(2,1)S(1)}, u32[]{:S(2)}, u32[]{:S(2)}) collective-permute-start(bf16[128,2048]{1,0:T(8,128)(2,1)S(1)} %collective-permute-done.31.refs_0_), channel_id=1, source_target_pairs={{0,2},{2,0},{4,6},{6,4},{8,10},{10,8},{12,14},{14,12},{16,18},{18,... | collective-permute-start | bytes 1572872 | tf_op jit(solution)/shard_map/ppermute | solution.py:20
  140.9 28.7 %collective-permute-start.34 = (bf16[128,2048]{1,0:T(8,128)(2,1)S(1)}, bf16[128,2048]{1,0:T(8,128)(2,1)S(1)}, u32[]{:S(2)}, u32[]{:S(2)}) collective-permute-start(bf16[128,2048]{1,0:T(8,128)(2,1)S(1)} %collective-permute-done.33.refs_2_), channel_id=1, source_target_pairs={{0,2},{2,0},{4,6},{6,4},{8,10},{10,8},{12,14},{14,12},{16,18},{18,... | collective-permute-start | bytes 1572872 | tf_op jit(solution)/shard_map/ppermute | solution.py:20
  147.3 28.1 %collective-permute-start.16 = (bf16[128,2048]{1,0:T(8,128)(2,1)S(1)}, bf16[128,2048]{1,0:T(8,128)(2,1)S(1)}, u32[]{:S(2)}, u32[]{:S(2)}) collective-permute-start(bf16[128,2048]{1,0:T(8,128)(2,1)S(1)} %get-tuple-element.27), channel_id=1, source_target_pairs={{0,8},{2,10},{4,12},{6,14},{8,0},{10,2},{12,4},{14,6},{16,24},{18,... | collective-permute-start | bytes 1572872 | tf_op jit(solution)/shard_map/ppermute | solution.py:20
  152.1 24.2 %collective-permute-start.18 = (bf16[128,2048]{1,0:T(8,128)(2,1)S(1)}, bf16[128,2048]{1,0:T(8,128)(2,1)S(1)}, u32[]{:S(2)}, u32[]{:S(2)}) collective-permute-start(bf16[128,2048]{1,0:T(8,128)(2,1)S(1)} %get-tuple-element.30), channel_id=1, source_target_pairs={{0,8},{2,10},{4,12},{6,14},{8,0},{10,2},{12,4},{14,6},{16,24},{18,... | collective-permute-start | bytes 1572872 | tf_op jit(solution)/shard_map/ppermute | solution.py:20
  162.4 15.4 %collective-permute-start.21 = (bf16[128,2048]{1,0:T(8,128)(2,1)S(1)}, bf16[128,2048]{1,0:T(8,128)(2,1)S(1)}, u32[]{:S(2)}, u32[]{:S(2)}) collective-permute-start(bf16[128,2048]{1,0:T(8,128)(2,1)S(1)} %get-tuple-element.32), channel_id=1, source_target_pairs={{0,4},{2,6},{4,0},{6,2},{8,12},{10,14},{12,8},{14,10},{16,20},{18,... | collective-permute-start | bytes 1572872 | tf_op jit(solution)/shard_map/ppermute | solution.py:20
  168.2 20.4 %collective-permute-start.27 = (bf16[128,2048]{1,0:T(8,128)(2,1)S(1)}, bf16[128,2048]{1,0:T(8,128)(2,1)S(1)}, u32[]{:S(2)}, u32[]{:S(2)}) collective-permute-start(bf16[128,2048]{1,0:T(8,128)(2,1)S(1)} %get-tuple-element.35), channel_id=1, source_target_pairs={{0,4},{2,6},{4,0},{6,2},{8,12},{10,14},{12,8},{14,10},{16,20},{18,... | collective-permute-start | bytes 1572872 | tf_op jit(solution)/shard_map/ppermute | solution.py:20
  169.6 55.9 %collective-permute-start.29 = (bf16[128,2048]{1,0:T(8,128)(2,1)S(1)}, bf16[128,2048]{1,0:T(8,128)(2,1)S(1)}, u32[]{:S(2)}, u32[]{:S(2)}) collective-permute-start(bf16[128,2048]{1,0:T(8,128)(2,1)S(1)} %get-tuple-element.36), channel_id=1, source_target_pairs={{0,4},{2,6},{4,0},{6,2},{8,12},{10,14},{12,8},{14,10},{16,20},{18,... | collective-permute-start | bytes 1572872 | tf_op jit(solution)/shard_map/ppermute | solution.py:20
  175.4 14.9 %collective-permute-start.36 = (bf16[128,2048]{1,0:T(8,128)(2,1)S(1)}, bf16[128,2048]{1,0:T(8,128)(2,1)S(1)}, u32[]{:S(2)}, u32[]{:S(2)}) collective-permute-start(bf16[128,2048]{1,0:T(8,128)(2,1)S(1)} %get-tuple-element.40), channel_id=1, source_target_pairs={{0,2},{2,0},{4,6},{6,4},{8,10},{10,8},{12,14},{14,12},{16,18},{18,... | collective-permute-start | bytes 1572872 | tf_op jit(solution)/shard_map/ppermute | solution.py:20
  176.3 57.8 %collective-permute-start.35 = (bf16[128,2048]{1,0:T(8,128)(2,1)S(1)}, bf16[128,2048]{1,0:T(8,128)(2,1)S(1)}, u32[]{:S(2)}, u32[]{:S(2)}) collective-permute-start(bf16[128,2048]{1,0:T(8,128)(2,1)S(1)} %get-tuple-element.38), channel_id=1, source_target_pairs={{0,2},{2,0},{4,6},{6,4},{8,10},{10,8},{12,14},{14,12},{16,18},{18,... | collective-permute-start | bytes 1572872 | tf_op jit(solution)/shard_map/ppermute | solution.py:20
  177.8 59.3 %collective-permute-start.17 = (bf16[128,2048]{1,0:T(8,128)(2,1)S(1)}, bf16[128,2048]{1,0:T(8,128)(2,1)S(1)}, u32[]{:S(2)}, u32[]{:S(2)}) collective-permute-start(bf16[128,2048]{1,0:T(8,128)(2,1)S(1)} %add_convert_fusion.8), channel_id=1, source_target_pairs={{0,2},{2,0},{4,6},{6,4},{8,10},{10,8},{12,14},{14,12},{16,18},{18,... | collective-permute-start | bytes 1572872 | tf_op jit(solution)/shard_map/ppermute | solution.py:20
  188.5 35.5 %collective-permute-start.19 = (bf16[128,2048]{1,0:T(8,128)(2,1)S(1)}, bf16[128,2048]{1,0:T(8,128)(2,1)S(1)}, u32[]{:S(2)}, u32[]{:S(2)}) collective-permute-start(bf16[128,2048]{1,0:T(8,128)(2,1)S(1)} %add_convert_fusion.7), channel_id=1, source_target_pairs={{0,2},{2,0},{4,6},{6,4},{8,10},{10,8},{12,14},{14,12},{16,18},{18,... | collective-permute-start | bytes 1572872 | tf_op jit(solution)/shard_map/ppermute | solution.py:20
  190.3 42.2 %collective-permute-start.28 = (bf16[128,2048]{1,0:T(8,128)(2,1)S(1)}, bf16[128,2048]{1,0:T(8,128)(2,1)S(1)}, u32[]{:S(2)}, u32[]{:S(2)}) collective-permute-start(bf16[128,2048]{1,0:T(8,128)(2,1)S(1)} %add_convert_fusion.4), channel_id=1, source_target_pairs={{0,2},{2,0},{4,6},{6,4},{8,10},{10,8},{12,14},{14,12},{16,18},{18,... | collective-permute-start | bytes 1572872 | tf_op jit(solution)/shard_map/ppermute | solution.py:20
  224.0 10.3 %collective-permute-start.37 = (bf16[128,2048]{1,0:T(8,128)(2,1)S(1)}, bf16[128,2048]{1,0:T(8,128)(2,1)S(1)}, u32[]{:S(2)}, u32[]{:S(2)}) collective-permute-start(bf16[128,2048]{1,0:T(8,128)(2,1)S(1)} %add_convert_fusion.2), channel_id=1, source_target_pairs={{0,4},{2,6},{4,0},{6,2},{8,12},{10,14},{12,8},{14,10},{16,20},{18,... | collective-permute-start | bytes 1572872 | tf_op jit(solution)/shard_map/ppermute | solution.py:20
  225.5 11.5 %collective-permute-start.22 = (bf16[128,2048]{1,0:T(8,128)(2,1)S(1)}, bf16[128,2048]{1,0:T(8,128)(2,1)S(1)}, u32[]{:S(2)}, u32[]{:S(2)}) collective-permute-start(bf16[128,2048]{1,0:T(8,128)(2,1)S(1)} %add_convert_fusion.5), channel_id=1, source_target_pairs={{0,8},{2,10},{4,12},{6,14},{8,0},{10,2},{12,4},{14,6},{16,24},{18,... | collective-permute-start | bytes 1572872 | tf_op jit(solution)/shard_map/ppermute | solution.py:20
  232.5 11.9 %collective-permute-start.20 = (bf16[128,2048]{1,0:T(8,128)(2,1)S(1)}, bf16[128,2048]{1,0:T(8,128)(2,1)S(1)}, u32[]{:S(2)}, u32[]{:S(2)}) collective-permute-start(bf16[128,2048]{1,0:T(8,128)(2,1)S(1)} %add_convert_fusion.6), channel_id=1, source_target_pairs={{0,4},{2,6},{4,0},{6,2},{8,12},{10,14},{12,8},{14,10},{16,20},{18,... | collective-permute-start | bytes 1572872 | tf_op jit(solution)/shard_map/ppermute | solution.py:20
  234.2 34.6 %collective-permute-start.30 = (bf16[128,2048]{1,0:T(8,128)(2,1)S(1)}, bf16[128,2048]{1,0:T(8,128)(2,1)S(1)}, u32[]{:S(2)}, u32[]{:S(2)}) collective-permute-start(bf16[128,2048]{1,0:T(8,128)(2,1)S(1)} %add_convert_fusion.3), channel_id=1, source_target_pairs={{0,16},{2,18},{4,20},{6,22},{8,24},{10,26},{12,28},{14,30},{16,0},... | collective-permute-start | bytes 1572872 | tf_op jit(solution)/shard_map/ppermute | solution.py:20
  234.5 45.1 %collective-permute-start.38 = (bf16[128,2048]{1,0:T(8,128)(2,1)S(1)}, bf16[128,2048]{1,0:T(8,128)(2,1)S(1)}, u32[]{:S(2)}, u32[]{:S(2)}) collective-permute-start(bf16[128,2048]{1,0:T(8,128)(2,1)S(1)} %add_convert_fusion.1), channel_id=1, source_target_pairs={{0,24},{2,26},{4,28},{6,30},{8,16},{10,18},{12,20},{14,22},{16,8},... | collective-permute-start | bytes 1572872 | tf_op jit(solution)/shard_map/ppermute | solution.py:20
  (7 other events, 19.2 us)

commit v4 on v3

v4 whole, which is shorter than its diff:
```python
import functools
import math

import jax
import jax.numpy as jnp
from jax import lax
from jax.experimental import pallas as pl
from jax.experimental.pallas import tpu as pltpu
from jax.sharding import PartitionSpec as P

HD = 128
SWAP = [(0, 1), (1, 0)]
VMEM = pl.BlockSpec(memory_space=pltpu.VMEM)
ANY = pl.BlockSpec(memory_space=pl.ANY)
NT = (((1,), (1,)), ((), ()))


def flip(block, mask):
    count = lax.axis_size("seq")
    return lax.ppermute(block, "seq", [(i, i ^ mask) for i in range(count)])


def after(block, *arrays):
    return lax.optimization_barrier((block, *arrays))[0]


def gate_order(count):
    masks = [1 << bit for bit in range(count.bit_length() - 1)]
    return masks[2:] + masks[1::-1]


def gather_gates(block):
    for mask in gate_order(lax.axis_size("seq")):
        block = jnp.concatenate([block, flip(block, mask)], axis=0)
    return block


def place_of(j):
    return sum(1 << bit for bit, mask in enumerate(gate_order(lax.axis_size("seq"))) if j & mask)


def attention_kernel(start_ref, q_ref, own_ref, before_ref, after_ref, qid_ref, kid_ref, *refs):
    out_ref = refs[-1]
    rows, some = q_ref.shape[0], out_ref.shape[0]
    start = pl.multiple_of(start_ref[0], some)
    query_pos = lax.broadcasted_iota(jnp.int32, (some, 3 * rows), 0) + (start + rows)
    key_pos = lax.broadcasted_iota(jnp.int32, (some, 3 * rows), 1)
    allowed = (qid_ref[pl.ds(start, some), :] == kid_ref[...]) & (
        jnp.abs(query_pos - key_pos) < rows
    )
    for head in range(q_ref.shape[1] // HD):
        cols = slice(head * HD, (head + 1) * HD)
        query = q_ref[pl.ds(start, some), cols]
        score = jnp.concatenate(
            [
                lax.dot_general(query, ref[:rows, cols], NT, preferred_element_type=jnp.float32)
                for ref in (before_ref, own_ref, after_ref)
            ],
            axis=1,
        ) / math.sqrt(HD)
        score = jnp.where(allowed, score, -jnp.inf)
        weights = jnp.exp(score - jnp.max(score, axis=-1, keepdims=True))
        probs = (weights / jnp.sum(weights, axis=-1, keepdims=True)).astype(jnp.bfloat16)
        total = jnp.zeros((some, HD), jnp.float32)
        for place, ref in enumerate((before_ref, own_ref, after_ref)):
            total += jnp.dot(
                probs[:, place * rows : (place + 1) * rows],
                ref[rows:, cols],
                preferred_element_type=jnp.float32,
            )
        out_ref[:, cols] = total.astype(jnp.bfloat16)


def attention(start, some, queries, own, before, after_own, query_ids, key_ids, ahead):
    rows, width = queries.shape
    return pl.pallas_call(
        attention_kernel,
        out_shape=jax.ShapeDtypeStruct((some, width), jnp.bfloat16),
        in_specs=[pl.BlockSpec(memory_space=pltpu.SMEM)] + [VMEM] * 6 + [ANY] * len(ahead),
        out_specs=VMEM,
        cost_estimate=pl.CostEstimate(
            flops=12 * some * rows * width, bytes_accessed=4 * 1024 * 1024, transcendentals=0
        ),
        name="window_attention",
    )(start, queries, own, before, after_own, query_ids, key_ids, *ahead)


def norm_kernel(mine_ref, theirs_ref, own_w, other_w, resid_ref, gain_ref, *refs):
    stream_ref, normed_ref = refs[-2:]
    stream = resid_ref[...].astype(jnp.float32)
    stream += jnp.dot(mine_ref[...], own_w[...], preferred_element_type=jnp.float32)
    stream += jnp.dot(theirs_ref[...], other_w[...], preferred_element_type=jnp.float32)
    meansq = jnp.mean(stream * stream, axis=-1, keepdims=True)
    stream_ref[...] = stream
    normed_ref[...] = (stream * lax.rsqrt(meansq + 1e-05) * gain_ref[...]).astype(jnp.bfloat16)


def project_and_norm(mine, theirs, own_w, other_w, resid, gain, *ahead):
    rows, width = resid.shape
    return pl.pallas_call(
        norm_kernel,
        out_shape=(
            jax.ShapeDtypeStruct((rows, width), jnp.float32),
            jax.ShapeDtypeStruct((rows, width), jnp.bfloat16),
        ),
        in_specs=[VMEM] * 6 + [ANY] * len(ahead),
        out_specs=(VMEM, VMEM),
        cost_estimate=pl.CostEstimate(
            flops=4 * rows * width * mine.shape[1], bytes_accessed=8 * 1024 * 1024, transcendentals=0
        ),
        compiler_params=pltpu.CompilerParams(vmem_limit_bytes=24 * 1024 * 1024),
        name="project_and_norm",
    )(mine, theirs, own_w, other_w, resid, gain, *ahead)


def expert_kernel(places, shard_ref, *refs):
    count = len(places)
    blocks, gates_ref, halves = refs[:count], refs[count], refs[count + 1 : count + 7]
    outs, (gate_w, up_w, down_w, sems) = refs[count + 7 : -4], refs[-4:]
    units = halves[0].shape[0]
    copies = []
    for i, half in enumerate(halves):
        target = (gate_w, up_w, down_w)[i // 2].at[pl.ds(i % 2 * units, units), :]
        copies.append(pltpu.make_async_copy(half, target, sems.at[i]))
        copies[-1].start()
    rows = blocks[0].shape[0]
    tokens = jnp.concatenate([ref[...] for ref in blocks], axis=0)
    copies[0].wait()
    copies[1].wait()
    gate = lax.dot_general(tokens, gate_w[...], NT, preferred_element_type=jnp.float32)
    copies[2].wait()
    copies[3].wait()
    up = lax.dot_general(tokens, up_w[...], NT, preferred_element_type=jnp.float32)
    act = (gate / (1.0 + jnp.exp(-gate)) * up).astype(jnp.bfloat16)
    copies[4].wait()
    copies[5].wait()
    for i, place in enumerate(places):
        gates = gates_ref[place * rows : (place + 1) * rows, :]
        expert = lax.broadcasted_iota(jnp.int32, gates.shape, 1)
        chosen = jnp.sum(jnp.where(expert == shard_ref[0], gates, 0.0), axis=1, keepdims=True)
        result = jnp.dot(
            act[i * rows : (i + 1) * rows], down_w[...], preferred_element_type=jnp.float32
        )
        outs[i][...] = (result * chosen).astype(jnp.bfloat16)


def expert(blocks, places, shard, gates, halves):
    rows, width = blocks[0].shape
    units = halves[0].shape[0]
    count = len(blocks)
    return pl.pallas_call(
        functools.partial(expert_kernel, places),
        out_shape=[jax.ShapeDtypeStruct((rows, width), jnp.bfloat16)] * count,
        in_specs=[pl.BlockSpec(memory_space=pltpu.SMEM)] + [VMEM] * (count + 1) + [ANY] * 6,
        out_specs=[VMEM] * count,
        scratch_shapes=[pltpu.VMEM((2 * units, width), jnp.bfloat16)] * 3
        + [pltpu.SemaphoreType.DMA((6,))],
        cost_estimate=pl.CostEstimate(
            flops=12 * count * rows * width * units,
            bytes_accessed=13 * 1024 * 1024,
            transcendentals=0,
        ),
        compiler_params=pltpu.CompilerParams(vmem_limit_bytes=40 * 1024 * 1024),
        name="expert_rows",
    )(shard, *blocks, gates, *halves)


def add(*terms):
    total = terms[0].astype(jnp.float32)
    for term in terms[1:]:
        total = total + term.astype(jnp.float32)
    return total


def add_small(*terms):
    return add(*terms).astype(jnp.bfloat16)


def expert_layer(normed, stream, shard, gates, halves):
    count = lax.axis_size("seq")

    def run(blocks, first):
        places = tuple(place_of(first + i) for i in range(len(blocks)))
        return expert(blocks, places, shard, gates, halves)

    if count == 16:
        o0 = normed
        o2, x0, y0, o1 = flip(o0, 8), flip(o0, 1), flip(o0, 2), flip(o0, 4)
        d0, x1, y1 = flip(y0, 1), flip(x0, 4), flip(o1, 2)
        o3 = flip(after(o0, o2), 12)
        x2, y2 = flip(o2, 1), flip(after(o2, y1), 2)
        d1 = flip(d0, 4)
        d2 = flip(x2, 2)
        x3, y3 = flip(o3, 1), flip(o3, 2)
        d3 = flip(y3, 1)
        o0, x0, y0, d0 = run([o0, x0, y0, d0], 0)
        o1, x1, y1, d1 = run([o1, x1, y1, d1], 4)
        o2, x2, y2, d2 = run([o2, x2, y2, d2], 8)
        o3, x3, y3, d3 = run([o3, x3, y3, d3], 12)
        d0 = add_small(d0, flip(d1, 4))
        x0 = add_small(x0, flip(x1, 4))
        o1 = add_small(o1, flip(y1, 2))
        x2 = add_small(x2, flip(d2, 2))
        o2 = add_small(o2, flip(x2, 1), flip(y2, 2))
        o2 = flip(o2, 8)
        y3 = add_small(y3, flip(d3, 1))
        o3 = add_small(o3, flip(x3, 1), flip(y3, 2))
        o3 = flip(o3, 12)
        y0 = add_small(y0, flip(d0, 1))
        return add(stream, o0, flip(x0, 1), flip(y0, 2), flip(o1, 4), o2, o3)
    blocks, mask = [normed], 1
    while mask < count:
        blocks = blocks + [flip(block, mask) for block in blocks]
        mask *= 2
    parts = []
    for first in range(0, count, 4):
        parts += run(blocks[first : first + 4], first)
    while mask > 1:
        mask //= 2
        parts = [add_small(parts[i], flip(parts[i + mask], mask)) for i in range(mask)]
    return add(stream, parts[0])


def shards(
    queries,
    keys,
    values,
    resid,
    pair_ids,
    out_weight,
    norm_gain,
    experts,
    gates,
    w_gate,
    w_up,
    w_down,
):
    tok_rows = queries.shape[0]
    moe_rows = resid.shape[0]
    shard = lax.axis_index("seq")
    core = lax.axis_index("exp")
    count = lax.axis_size("seq")

    own = jnp.concatenate([keys, values], axis=0)
    before = lax.ppermute(own, "seq", [(i, i + 1) for i in range(count - 1)])
    after_own = lax.ppermute(own, "seq", [(i + 1, i) for i in range(count - 1)])
    per_expert = jnp.sum(
        jnp.where(
            experts[:, :, None] == jnp.arange(count, dtype=jnp.int32)[None, None, :],
            gates[:, :, None],
            0.0,
        ),
        axis=1,
    )
    all_gates = gather_gates(per_expert)
    out_other = lax.ppermute(out_weight, "exp", SWAP)
    gate_w, up_w = jnp.swapaxes(w_gate[0], 0, 1), jnp.swapaxes(w_up[0], 0, 1)
    gate_other = lax.ppermute(gate_w, "exp", SWAP)
    id_pad = jnp.pad(pair_ids, (tok_rows, tok_rows), constant_values=-1)
    key_ids = lax.dynamic_slice_in_dim(id_pad, shard * tok_rows, 3 * tok_rows, 0)
    query_ids = lax.dynamic_slice_in_dim(pair_ids, shard * tok_rows, tok_rows, 0)
    ids = (query_ids[:, None], key_ids[None, :])
    ready = (before, after_own, all_gates, *ids)
    up_other = lax.ppermute(after(up_w, *ready), "exp", SWAP)
    down_other = lax.ppermute(after(w_down[0], *ready), "exp", SWAP)
    halves = [gate_w, gate_other, up_w, up_other, w_down[0], down_other]

    def attend(half, ahead):
        start = (half * moe_rows).reshape(1)
        return attention(start, moe_rows, queries, own, before, after_own, *ids, ahead)

    theirs = attend(1 - core, [out_other, gate_other])
    received = lax.ppermute(theirs, "exp", SWAP)
    mine = attend(core, [theirs])
    stream, normed = project_and_norm(
        mine, received, out_weight, out_other, resid, norm_gain[None, :], up_other, down_other
    )
    mixed = expert_layer(normed, stream, shard.reshape(1), all_gates, halves)
    return mixed.astype(jnp.bfloat16)


def solution(mesh):
    in_specs = (
        P("seq", "exp"),
        P("seq", "exp"),
        P("seq", "exp"),
        P(("seq", "exp"), None),
        P(),
        P("exp", None),
        P(),
        P(("seq", "exp"), None),
        P(("seq", "exp"), None),
        P("seq", None, "exp"),
        P("seq", None, "exp"),
        P("seq", "exp", None),
    )
    out_specs = P(("seq", "exp"), None)
    return jax.shard_map(shards, mesh=mesh, in_specs=in_specs, out_specs=out_specs, check_vma=False)
```

time: 282 us -> 275 us (0.975)
  waiting for transfers between devices: 179 us -> 149 us
  Pallas kernels: 27.6 us -> 45.2 us
  other arithmetic: 20.9 us -> 3.3 us
  local copies, waits for them, and re-layouts: 12.8 us -> 24.5 us
  starting transfers between devices: 40.8 us -> 52.1 us
    ppermute x34, waiting for transfers between devices: 177 us -> 149 us  [flip(): return lax.ppermute(block, 'seq', [(i, i ^ mask) for i in range(count)])]
    pallas_call x5 -> x6, Pallas kernels: 25.1 us -> 43.6 us  [the longest x4 35.5 us: expert(): pl.pallas_call(functools.partial(expert_kernel, places), out_shape=[jax.S...]
    concatenate x6 -> x3, other arithmetic: 18.3 us -> 0.01 us  [gather_gates(): block = jnp.concatenate([block, flip(block, mask)], axis=0)]
    ppermute x34, starting transfers between devices: 34.8 us -> 45.2 us  [flip(): return lax.ppermute(block, 'seq', [(i, i ^ mask) for i in range(count)])]
    unnamed x38 -> x45, local copies, waits for them, and re-layouts: 7.33 us -> 16.9 us
  transfers between devices with their start and end apart: 39 -> 41, of which waited for: 20 -> 17; matrix products, arithmetic and copies ran while one was open for 8% -> 4% of each run, Pallas kernels for 7% -> 16%
where the time goes in v4:
time: 275 us; the launch traced here: 274 us
  waiting for transfers between devices  149 us (54%)
  starting transfers between devices  52.1 us (19%)
  Pallas kernels  45.2 us (16%)
  local copies, waits for them, and re-layouts  24.5 us (9%)
  other arithmetic  3.3 us (1%)
    ppermute x34, waiting for transfers between devices, flip(): return lax.ppermute(block, 'seq', [(i, i ^ mask) for i in range(count)])  149 us
    ppermute x34, starting transfers between devices, flip(): return lax.ppermute(block, 'seq', [(i, i ^ mask) for i in range(count)])  45.2 us
    pallas_call x4, Pallas kernels, expert(): pl.pallas_call(functools.partial(expert_kernel, places), out_shape=[jax.S...  35.5 us
    unnamed x45, local copies, waits for them, and re-layouts  16.9 us
    pallas_call x2, Pallas kernels, attention(): pl.pallas_call(attention_kernel, out_shape=jax.ShapeDtypeStruct((some, wi...  8.06 us
  transfers between devices with their start and end apart: 41, of which 17 were waited for; matrix products, arithmetic and copies ran while one was open for 4% of the time, Pallas kernels for 16%

profile of v4, /device:TPU:10, one launch (start us, length us, event | category | flops | bytes accessed | tf_op | source)
XLA Modules:
  0.0 274.1 jit_solution(2870456818563479801)
XLA Ops:
  0.0 1.7 constant_dynamic-update-slice_fusion.1
  1.7 1.7 constant_dynamic-update-slice_fusion.own_ref
  3.3 3.4 %collective-permute-start = (bf16[512,512]{1,0:T(8,128)(2,1)}, bf16[512,512]{1,0:T(8,128)(2,1)}, u32[]{:S(2)}, u32[]{:S(2)}) collective-permute-start(bf16[512,512]{1,0:T(8,128)(2,1)} %constant_dynamic-update-slice_fusion.own_ref), channel_id=1, source_target_pairs={{0,2},{2,4},{4,6},{6,8},{8,10},{10,12},{12,14},{14,16},{16,18},{18... | collective-permute-start | bytes 1572872 | tf_op jit(solution)/shard_map/ppermute | solution.py:245
  6.7 2.4 collective-permute-start.1
  14.9 1.8 collective-permute-start.6
  17.3 2.2 collective-permute-done.6
  19.6 5.8 %collective-permute-start.7 = (f32[512,16]{0,1:T(8,128)S(1)}, f32[512,16]{0,1:T(8,128)S(1)}, u32[]{:S(2)}, u32[]{:S(2)}) collective-permute-start(f32[512,16]{0,1:T(8,128)S(1)} %pad_maximum_fusion.1), channel_id=1, source_target_pairs={{0,4},{2,6},{4,0},{6,2},{8,12},{10,14},{12,8},{14,10},{16,20},{18,... | collective-permute-start | bytes 98312 | tf_op jit(solution)/shard_map/ppermute | solution.py:20
  26.0 6.0 %collective-permute-done.7 = f32[512,16]{0,1:T(8,128)S(1)} collective-permute-done((f32[512,16]{0,1:T(8,128)S(1)}, f32[512,16]{0,1:T(8,128)S(1)}, u32[]{:S(2)}, u32[]{:S(2)}) %collective-permute-start.7) | collective-permute-done | bytes 32800 | tf_op jit(solution)/shard_map/ppermute | solution.py:20
  32.6 3.6 %collective-permute-done.8 = f32[1024,16]{0,1:T(8,128)S(1)} collective-permute-done((f32[1024,16]{0,1:T(8,128)S(1)}, f32[1024,16]{0,1:T(8,128)S(1)}, u32[]{:S(2)}, u32[]{:S(2)}) %collective-permute-start.8) | collective-permute-done | bytes 65568 | tf_op jit(solution)/shard_map/ppermute | solution.py:20
  40.6 4.0 %window_attention.2.refs_0_ = bf16[128,512]{1,0:T(8,128)(2,1)} custom-call(s32[1]{0:T(128)} %bitcast.2.start_ref, bf16[256,512]{1,0:T(8,128)(2,1)} %q_ref.3, bf16[512,512]{1,0:T(8,128)(2,1)} %constant_dynamic-update-slice_fusion.own_ref, bf16[512,512]{1,0:T(8,128)(2,1)} %collective-permute-done.before_ref, ...), custom_call_target="tpu_custom_call" | custom-call | flops 201326592 | bytes 4194304 | tf_op jit(solution)/shard_map/window_attention/pallas_call | solution.py:76
  44.7 4.1 %window_attention.3.mine_ref = bf16[128,512]{1,0:T(8,128)(2,1)} custom-call(s32[1]{0:T(128)} %bitcast.start_ref, bf16[256,512]{1,0:T(8,128)(2,1)} %q_ref.3, bf16[512,512]{1,0:T(8,128)(2,1)} %constant_dynamic-update-slice_fusion.own_ref, bf16[512,512]{1,0:T(8,128)(2,1)} %collective-permute-done.before_ref, bf16[512,512]{1,0:T(8,128)(2,1)} %collective-permute-done.1.after_ref, ...), custom_call_target="tpu_custom_call" | custom-call | flops 201326592 | bytes 4194304 | tf_op jit(solution)/shard_map/window_attention/pallas_call | solution.py:76
  49.4 1.6 copy-done.2
  53.9 1.7 project_and_norm.1
  57.0 2.6 collective-permute-start.25
  59.6 1.6 collective-permute-start.11
  61.2 9.9 %collective-permute-done.12.refs_2_ = bf16[128,2048]{1,0:T(8,128)(2,1)S(1)} collective-permute-done((bf16[128,2048]{1,0:T(8,128)(2,1)}, bf16[128,2048]{1,0:T(8,128)(2,1)S(1)}, u32[]{:S(2)}, u32[]{:S(2)}) %collective-permute-start.12) | collective-permute-done | bytes 524320 | tf_op jit(solution)/shard_map/ppermute | solution.py:20
  72.0 8.3 %collective-permute-done.14.refs_0_ = bf16[128,2048]{1,0:T(8,128)(2,1)} collective-permute-done((bf16[128,2048]{1,0:T(8,128)(2,1)}, bf16[128,2048]{1,0:T(8,128)(2,1)}, u32[]{:S(2)}, u32[]{:S(2)}) %collective-permute-start.14) | collective-permute-done | bytes 524320 | tf_op jit(solution)/shard_map/ppermute | solution.py:20
  80.3 1.7 collective-permute-start.16
  82.1 1.4 collective-permute-done.25.refs_0_
  83.5 1.5 collective-permute-start.26
  85.0 4.2 %collective-permute-start.15 = (bf16[128,2048]{1,0:T(8,128)(2,1)}, bf16[128,2048]{1,0:T(8,128)(2,1)}, u32[]{:S(2)}, u32[]{:S(2)}) collective-permute-start(bf16[128,2048]{1,0:T(8,128)(2,1)} %collective-permute-done.11.refs_1_), channel_id=1, source_target_pairs={{0,8},{2,10},{4,12},{6,14},{8,0},{10,2},{12,4},{14,6},{16,24},{18,... | collective-permute-start | bytes 1572872 | tf_op jit(solution)/shard_map/ppermute | solution.py:20
  90.5 3.7 %collective-permute-done.16.refs_2_ = bf16[128,2048]{1,0:T(8,128)(2,1)} collective-permute-done((bf16[128,2048]{1,0:T(8,128)(2,1)}, bf16[128,2048]{1,0:T(8,128)(2,1)}, u32[]{:S(2)}, u32[]{:S(2)}) %collective-permute-start.16) | collective-permute-done | bytes 524320 | tf_op jit(solution)/shard_map/ppermute | solution.py:20
  94.2 1.4 collective-permute-start.27
  95.6 1.5 collective-permute-done.26.refs_1_
  97.1 1.4 collective-permute-start.28
  98.5 11.2 %collective-permute-done.33.refs_0_ = bf16[128,2048]{1,0:T(8,128)(2,1)S(1)} collective-permute-done((bf16[128,2048]{1,0:T(8,128)(2,1)}, bf16[128,2048]{1,0:T(8,128)(2,1)S(1)}, u32[]{:S(2)}, u32[]{:S(2)}) %collective-permute-start.33) | collective-permute-done | bytes 524320 | tf_op jit(solution)/shard_map/ppermute | solution.py:20
  109.7 1.4 collective-permute-start.35
  111.1 2.4 collective-permute-done.15.refs_1_
  113.5 9.4 %collective-permute-done.17.refs_3_ = bf16[128,2048]{1,0:T(8,128)(2,1)} collective-permute-done((bf16[128,2048]{1,0:T(8,128)(2,1)}, bf16[128,2048]{1,0:T(8,128)(2,1)}, u32[]{:S(2)}, u32[]{:S(2)}) %collective-permute-start.17) | collective-permute-done | bytes 524320 | tf_op jit(solution)/shard_map/ppermute | solution.py:20
  127.0 9.4 %expert_rows.5 = (bf16[128,2048]{1,0:T(8,128)(2,1)S(1)}, bf16[128,2048]{1,0:T(8,128)(2,1)S(1)}, bf16[128,2048]{1,0:T(8,128)(2,1)S(1)}, bf16[128,2048]{1,0:T(8,128)(2,1)S(1)}) custom-call(s32[1]{0:T(128)} %bitcast.9.shard_ref, bf16[128,2048]{1,0:T(8,128)(2,1)} %collective-permute-done.14.refs_0_, bf16[128,2048]{1,0:T(8,128)(2,1)} %collective-permute-done.15.refs_1_, ...), custom_call_target="tpu_custom_call" | custom-call | flops 4429185024 | bytes 13631488 | tf_op jit(solution)/shard_map/expert_rows/pallas_call | solution.py:151
  137.1 9.1 %expert_rows.4 = (bf16[128,2048]{1,0:T(8,128)(2,1)S(1)}, bf16[128,2048]{1,0:T(8,128)(2,1)S(1)}, bf16[128,2048]{1,0:T(8,128)(2,1)S(1)}, bf16[128,2048]{1,0:T(8,128)(2,1)S(1)}) custom-call(s32[1]{0:T(128)} %bitcast.9.shard_ref, bf16[128,2048]{1,0:T(8,128)(2,1)} %get-tuple-element.44.refs_0_, bf16[128,2048]{1,0:T(8,128)(2,1)} %collective-permute-done.11.refs_1_, ...), custom_call_target="tpu_custom_call" | custom-call | flops 4429185024 | bytes 13631488 | tf_op jit(solution)/shard_map/expert_rows/pallas_call | solution.py:151
  148.1 1.5 collective-permute-start.23
  149.6 9.0 %expert_rows.6 = (bf16[128,2048]{1,0:T(8,128)(2,1)S(1)}, bf16[128,2048]{1,0:T(8,128)(2,1)S(1)}, bf16[128,2048]{1,0:T(8,128)(2,1)S(1)}, bf16[128,2048]{1,0:T(8,128)(2,1)S(1)}) custom-call(s32[1]{0:T(128)} %bitcast.9.shard_ref, bf16[128,2048]{1,0:T(8,128)(2,1)S(1)} %collective-permute-done.25.refs_0_, bf16[128,2048]{1,0:T(8,128)(2,1)} %collective-permute-done.26.refs_1_, ...), custom_call_target="tpu_custom_call" | custom-call | flops 4429185024 | bytes 13631488 | tf_op jit(solution)/shard_map/expert_rows/pallas_call | solution.py:151
  159.3 1.6 collective-permute-start.36
  161.0 1.5 collective-permute-start.31
  163.2 10.9 %collective-permute-done.36.refs_3_ = bf16[128,2048]{1,0:T(8,128)(2,1)S(1)} collective-permute-done((bf16[128,2048]{1,0:T(8,128)(2,1)S(1)}, bf16[128,2048]{1,0:T(8,128)(2,1)S(1)}, u32[]{:S(2)}, u32[]{:S(2)}) %collective-permute-start.36) | collective-permute-done | bytes 524320 | tf_op jit(solution)/shard_map/ppermute | solution.py:20
  174.1 1.6 collective-permute-start.21
  175.7 8.0 %expert_rows.7 = (bf16[128,2048]{1,0:T(8,128)(2,1)S(1)}, bf16[128,2048]{1,0:T(8,128)(2,1)S(1)}, bf16[128,2048]{1,0:T(8,128)(2,1)S(1)}, bf16[128,2048]{1,0:T(8,128)(2,1)S(1)}) custom-call(s32[1]{0:T(128)} %bitcast.9.shard_ref, bf16[128,2048]{1,0:T(8,128)(2,1)S(1)} %collective-permute-done.33.refs_0_, bf16[128,2048]{1,0:T(8,128)(2,1)S(1)} %collective-permute-done.34.refs_1_, ...), custom_call_target="tpu_custom_call" | custom-call | flops 4429185024 | bytes 13631488 | tf_op jit(solution)/shard_map/expert_rows/pallas_call | solution.py:151
  184.4 1.7 collective-permute-start.30
  186.2 21.6 %collective-permute-done.38 = bf16[128,2048]{1,0:T(8,128)(2,1)S(1)} collective-permute-done((bf16[128,2048]{1,0:T(8,128)(2,1)S(1)}, bf16[128,2048]{1,0:T(8,128)(2,1)S(1)}, u32[]{:S(2)}, u32[]{:S(2)}) %collective-permute-start.38) | collective-permute-done | bytes 524320 | tf_op jit(solution)/shard_map/ppermute | solution.py:20
  207.8 1.6 collective-permute-start.37
  209.6 1.5 collective-permute-start.39
  211.7 7.4 %collective-permute-done.30 = bf16[128,2048]{1,0:T(8,128)(2,1)S(1)} collective-permute-done((bf16[128,2048]{1,0:T(8,128)(2,1)S(1)}, bf16[128,2048]{1,0:T(8,128)(2,1)S(1)}, u32[]{:S(2)}, u32[]{:S(2)}) %collective-permute-start.30) | collective-permute-done | bytes 524320 | tf_op jit(solution)/shard_map/ppermute | solution.py:20
  219.1 1.5 collective-permute-start.22
  220.8 6.4 %collective-permute-done.37 = bf16[128,2048]{1,0:T(8,128)(2,1)S(1)} collective-permute-done((bf16[128,2048]{1,0:T(8,128)(2,1)S(1)}, bf16[128,2048]{1,0:T(8,128)(2,1)S(1)}, u32[]{:S(2)}, u32[]{:S(2)}) %collective-permute-start.37) | collective-permute-done | bytes 524320 | tf_op jit(solution)/shard_map/ppermute | solution.py:20
  227.5 2.8 %collective-permute-start.40 = (bf16[128,2048]{1,0:T(8,128)(2,1)S(1)}, bf16[128,2048]{1,0:T(8,128)(2,1)S(1)}, u32[]{:S(2)}, u32[]{:S(2)}) collective-permute-start(bf16[128,2048]{1,0:T(8,128)(2,1)S(1)} %add_convert_fusion.1), channel_id=1, source_target_pairs={{0,24},{2,26},{4,28},{6,30},{8,16},{10,18},{12,20},{14,22},{16,8},... | collective-permute-start | bytes 1572872 | tf_op jit(solution)/shard_map/ppermute | solution.py:20
  230.3 29.6 %collective-permute-done.32 = bf16[128,2048]{1,0:T(8,128)(2,1)S(1)} collective-permute-done((bf16[128,2048]{1,0:T(8,128)(2,1)S(1)}, bf16[128,2048]{1,0:T(8,128)(2,1)S(1)}, u32[]{:S(2)}, u32[]{:S(2)}) %collective-permute-start.32) | collective-permute-done | bytes 524320 | tf_op jit(solution)/shard_map/ppermute | solution.py:20
  259.9 12.8 %collective-permute-done.40 = bf16[128,2048]{1,0:T(8,128)(2,1)S(1)} collective-permute-done((bf16[128,2048]{1,0:T(8,128)(2,1)S(1)}, bf16[128,2048]{1,0:T(8,128)(2,1)S(1)}, u32[]{:S(2)}, u32[]{:S(2)}) %collective-permute-start.40) | collective-permute-done | bytes 524320 | tf_op jit(solution)/shard_map/ppermute | solution.py:20
  (106 shorter events, 30.4 us)
Async XLA Ops:
  3.3 33.6 %collective-permute-start = (bf16[512,512]{1,0:T(8,128)(2,1)}, bf16[512,512]{1,0:T(8,128)(2,1)}, u32[]{:S(2)}, u32[]{:S(2)}) collective-permute-start(bf16[512,512]{1,0:T(8,128)(2,1)} %constant_dynamic-update-slice_fusion.own_ref), channel_id=1, source_target_pairs={{0,2},{2,4},{4,6},{6,8},{8,10},{10,12},{12,14},{14,16},{16,18},{18... | collective-permute-start | bytes 1572872 | tf_op jit(solution)/shard_map/ppermute | solution.py:245
  6.7 30.2 %collective-permute-start.1 = (bf16[512,512]{1,0:T(8,128)(2,1)}, bf16[512,512]{1,0:T(8,128)(2,1)}, u32[]{:S(2)}, u32[]{:S(2)}) collective-permute-start(bf16[512,512]{1,0:T(8,128)(2,1)} %constant_dynamic-update-slice_fusion.own_ref), channel_id=1, source_target_pairs={{2,0},{4,2},{6,4},{8,6},{10,8},{12,10},{14,12},{16,14},{18,16},{20... | collective-permute-start | bytes 1572872 | tf_op jit(solution)/shard_map/ppermute | solution.py:246
  9.9 5.0 %collective-permute-start.5 = (f32[128,16]{0,1:T(8,128)S(1)}, f32[128,16]{0,1:T(8,128)S(1)}, u32[]{:S(2)}, u32[]{:S(2)}) collective-permute-start(f32[128,16]{0,1:T(8,128)S(1)} %select_reduce_fusion), channel_id=1, source_target_pairs={{0,8},{2,10},{4,12},{6,14},{8,0},{10,2},{12,4},{14,6},{16,24},{18,... | collective-permute-start | bytes 24584 | tf_op jit(solution)/shard_map/ppermute | solution.py:20
  11.2 27.6 %collective-permute-start.3 = (bf16[352,2048]{1,0:T(8,128)(2,1)}, bf16[352,2048]{1,0:T(8,128)(2,1)S(1)}, u32[]{:S(2)}, u32[]{:S(2)}) collective-permute-start(bf16[352,2048]{1,0:T(8,128)(2,1)} %bitcast.13), channel_id=1, source_target_pairs={{0,1},{1,0},{2,3},{3,2},{4,5},{5,4},{6,7},{7,6},{8,9},{9,8},{10,11... | collective-permute-start | bytes 4325384 | tf_op jit(solution)/shard_map/ppermute | solution.py:258
  11.2 27.6 %collective-permute-start.2 = (bf16[512,2048]{1,0:T(8,128)(2,1)}, bf16[512,2048]{1,0:T(8,128)(2,1)S(1)}, u32[]{:S(2)}, u32[]{:S(2)}) collective-permute-start(bf16[512,2048]{1,0:T(8,128)(2,1)} %own_w.1), channel_id=1, source_target_pairs={{0,1},{1,0},{2,3},{3,2},{4,5},{5,4},{6,7},{7,6},{8,9},{9,8},{10,11... | collective-permute-start | bytes 6291464 | tf_op jit(solution)/shard_map/ppermute | solution.py:256
  14.9 4.6 %collective-permute-start.6 = (f32[256,16]{0,1:T(8,128)S(1)}, f32[256,16]{0,1:T(8,128)S(1)}, u32[]{:S(2)}, u32[]{:S(2)}) collective-permute-start(f32[256,16]{0,1:T(8,128)S(1)} %pad_maximum_fusion.2), channel_id=1, source_target_pairs={{0,16},{2,18},{4,20},{6,22},{8,24},{10,26},{12,28},{14,30},{16,0},... | collective-permute-start | bytes 49160 | tf_op jit(solution)/shard_map/ppermute | solution.py:20
  19.6 12.4 %collective-permute-start.7 = (f32[512,16]{0,1:T(8,128)S(1)}, f32[512,16]{0,1:T(8,128)S(1)}, u32[]{:S(2)}, u32[]{:S(2)}) collective-permute-start(f32[512,16]{0,1:T(8,128)S(1)} %pad_maximum_fusion.1), channel_id=1, source_target_pairs={{0,4},{2,6},{4,0},{6,2},{8,12},{10,14},{12,8},{14,10},{16,20},{18,... | collective-permute-start | bytes 98312 | tf_op jit(solution)/shard_map/ppermute | solution.py:20
  32.0 4.3 %collective-permute-start.8 = (f32[1024,16]{0,1:T(8,128)S(1)}, f32[1024,16]{0,1:T(8,128)S(1)}, u32[]{:S(2)}, u32[]{:S(2)}) collective-permute-start(f32[1024,16]{0,1:T(8,128)S(1)} %pad_maximum_fusion), channel_id=1, source_target_pairs={{0,2},{2,0},{4,6},{6,4},{8,10},{10,8},{12,14},{14,12},{16,18},{18,... | collective-permute-start | bytes 196616 | tf_op jit(solution)/shard_map/ppermute | solution.py:20
  36.9 11.9 %collective-permute-start.10 = (bf16[352,2048]{1,0:T(8,128)(2,1)}, bf16[352,2048]{1,0:T(8,128)(2,1)}, u32[]{:S(2)}, u32[]{:S(2)}) collective-permute-start(bf16[352,2048]{1,0:T(8,128)(2,1)} %bitcast.23), channel_id=1, source_target_pairs={{0,1},{1,0},{2,3},{3,2},{4,5},{5,4},{6,7},{7,6},{8,9},{9,8},{10,11... | collective-permute-start | bytes 4325384 | tf_op jit(solution)/shard_map/ppermute | solution.py:265
  36.9 11.8 %collective-permute-start.9 = (bf16[352,2048]{1,0:T(8,128)(2,1)}, bf16[352,2048]{1,0:T(8,128)(2,1)}, u32[]{:S(2)}, u32[]{:S(2)}) collective-permute-start(bf16[352,2048]{1,0:T(8,128)(2,1)} %bitcast.18), channel_id=1, source_target_pairs={{0,1},{1,0},{2,3},{3,2},{4,5},{5,4},{6,7},{7,6},{8,9},{9,8},{10,11... | collective-permute-start | bytes 4325384 | tf_op jit(solution)/shard_map/ppermute | solution.py:264
  44.6 4.9 %copy-start.11 = (f32[2048]{0:T(1024)S(1)}, f32[2048]{0:T(1024)}, u32[]{:S(2)}) copy-start(f32[2048]{0:T(1024)} %param.18) | copy-start | bytes 24580
  44.6 4.2 %collective-permute-start.4 = (bf16[128,512]{1,0:T(8,128)(2,1)}, bf16[128,512]{1,0:T(8,128)(2,1)S(1)}, u32[]{:S(2)}, u32[]{:S(2)}) collective-permute-start(bf16[128,512]{1,0:T(8,128)(2,1)} %window_attention.2.refs_0_), channel_id=1, source_target_pairs={{0,1},{1,0},{2,3},{3,2},{4,5},{5,4},{6,7},{7,6},{8,9},{9,8},{10,11... | collective-permute-start | bytes 393224 | tf_op jit(solution)/shard_map/ppermute | solution.py:273
  53.9 69.0 %copy-start.4 = (bf16[352,2048]{1,0:T(8,128)(2,1)S(1)}, bf16[352,2048]{1,0:T(8,128)(2,1)}, u32[]{:S(2)}) copy-start(bf16[352,2048]{1,0:T(8,128)(2,1)} %copy-done.3) | copy-start | bytes 4325380
  56.6 14.5 %collective-permute-start.12 = (bf16[128,2048]{1,0:T(8,128)(2,1)}, bf16[128,2048]{1,0:T(8,128)(2,1)S(1)}, u32[]{:S(2)}, u32[]{:S(2)}) collective-permute-start(bf16[128,2048]{1,0:T(8,128)(2,1)} %get-tuple-element.44.refs_0_), channel_id=1, source_target_pairs={{0,4},{2,6},{4,0},{6,2},{8,12},{10,14},{12,8},{14,10},{16,20},{18,... | collective-permute-start | bytes 1572872 | tf_op jit(solution)/shard_map/ppermute | solution.py:20
  56.6 23.7 %collective-permute-start.14 = (bf16[128,2048]{1,0:T(8,128)(2,1)}, bf16[128,2048]{1,0:T(8,128)(2,1)}, u32[]{:S(2)}, u32[]{:S(2)}) collective-permute-start(bf16[128,2048]{1,0:T(8,128)(2,1)} %get-tuple-element.44.refs_0_), channel_id=1, source_target_pairs={{0,8},{2,10},{4,12},{6,14},{8,0},{10,2},{12,4},{14,6},{16,24},{18,... | collective-permute-start | bytes 1572872 | tf_op jit(solution)/shard_map/ppermute | solution.py:20
  57.0 26.4 %collective-permute-start.25 = (bf16[128,2048]{1,0:T(8,128)(2,1)}, bf16[128,2048]{1,0:T(8,128)(2,1)S(1)}, u32[]{:S(2)}, u32[]{:S(2)}) collective-permute-start(bf16[128,2048]{1,0:T(8,128)(2,1)} %get-tuple-element.44.refs_0_), channel_id=1, source_target_pairs={{0,16},{2,18},{4,20},{6,22},{8,24},{10,26},{12,28},{14,30},{16,0},... | collective-permute-start | bytes 1572872 | tf_op jit(solution)/shard_map/ppermute | solution.py:20
  59.6 25.4 %collective-permute-start.11 = (bf16[128,2048]{1,0:T(8,128)(2,1)}, bf16[128,2048]{1,0:T(8,128)(2,1)}, u32[]{:S(2)}, u32[]{:S(2)}) collective-permute-start(bf16[128,2048]{1,0:T(8,128)(2,1)} %get-tuple-element.44.refs_0_), channel_id=1, source_target_pairs={{0,2},{2,0},{4,6},{6,4},{8,10},{10,8},{12,14},{14,12},{16,18},{18,... | collective-permute-start | bytes 1572872 | tf_op jit(solution)/shard_map/ppermute | solution.py:20
  71.1 18.0 %collective-permute-start.13 = (bf16[128,2048]{1,0:T(8,128)(2,1)S(1)}, bf16[128,2048]{1,0:T(8,128)(2,1)}, u32[]{:S(2)}, u32[]{:S(2)}) collective-permute-start(bf16[128,2048]{1,0:T(8,128)(2,1)S(1)} %collective-permute-done.12.refs_2_), channel_id=1, source_target_pairs={{0,2},{2,0},{4,6},{6,4},{8,10},{10,8},{12,14},{14,12},{16,18},{18,... | collective-permute-start | bytes 1572872 | tf_op jit(solution)/shard_map/ppermute | solution.py:20
  80.3 13.9 %collective-permute-start.16 = (bf16[128,2048]{1,0:T(8,128)(2,1)}, bf16[128,2048]{1,0:T(8,128)(2,1)}, u32[]{:S(2)}, u32[]{:S(2)}) collective-permute-start(bf16[128,2048]{1,0:T(8,128)(2,1)} %collective-permute-done.14.refs_0_), channel_id=1, source_target_pairs={{0,4},{2,6},{4,0},{6,2},{8,12},{10,14},{12,8},{14,10},{16,20},{18,... | collective-permute-start | bytes 1572872 | tf_op jit(solution)/shard_map/ppermute | solution.py:20
  83.5 13.6 %collective-permute-start.26 = (bf16[128,2048]{1,0:T(8,128)(2,1)S(1)}, bf16[128,2048]{1,0:T(8,128)(2,1)}, u32[]{:S(2)}, u32[]{:S(2)}) collective-permute-start(bf16[128,2048]{1,0:T(8,128)(2,1)S(1)} %collective-permute-done.25.refs_0_), channel_id=1, source_target_pairs={{0,2},{2,0},{4,6},{6,4},{8,10},{10,8},{12,14},{14,12},{16,18},{18,... | collective-permute-start | bytes 1572872 | tf_op jit(solution)/shard_map/ppermute | solution.py:20
  85.0 24.7 %collective-permute-start.33 = (bf16[128,2048]{1,0:T(8,128)(2,1)}, bf16[128,2048]{1,0:T(8,128)(2,1)S(1)}, u32[]{:S(2)}, u32[]{:S(2)}) collective-permute-start(bf16[128,2048]{1,0:T(8,128)(2,1)} %get-tuple-element.44.refs_0_), channel_id=1, source_target_pairs={{0,24},{2,26},{4,28},{6,30},{8,16},{10,18},{12,20},{14,22},{16,8},... | collective-permute-start | bytes 1572872 | tf_op jit(solution)/shard_map/ppermute | solution.py:20
  85.0 28.5 %collective-permute-start.15 = (bf16[128,2048]{1,0:T(8,128)(2,1)}, bf16[128,2048]{1,0:T(8,128)(2,1)}, u32[]{:S(2)}, u32[]{:S(2)}) collective-permute-start(bf16[128,2048]{1,0:T(8,128)(2,1)} %collective-permute-done.11.refs_1_), channel_id=1, source_target_pairs={{0,8},{2,10},{4,12},{6,14},{8,0},{10,2},{12,4},{14,6},{16,24},{18,... | collective-permute-start | bytes 1572872 | tf_op jit(solution)/shard_map/ppermute | solution.py:20
  89.2 33.8 %collective-permute-start.17 = (bf16[128,2048]{1,0:T(8,128)(2,1)}, bf16[128,2048]{1,0:T(8,128)(2,1)}, u32[]{:S(2)}, u32[]{:S(2)}) collective-permute-start(bf16[128,2048]{1,0:T(8,128)(2,1)} %collective-permute-done.13.refs_3_), channel_id=1, source_target_pairs={{0,8},{2,10},{4,12},{6,14},{8,0},{10,2},{12,4},{14,6},{16,24},{18,... | collective-permute-start | bytes 1572872 | tf_op jit(solution)/shard_map/ppermute | solution.py:20
  94.2 52.5 %collective-permute-start.27 = (bf16[128,2048]{1,0:T(8,128)(2,1)S(1)}, bf16[128,2048]{1,0:T(8,128)(2,1)S(1)}, u32[]{:S(2)}, u32[]{:S(2)}) collective-permute-start(bf16[128,2048]{1,0:T(8,128)(2,1)S(1)} %collective-permute-done.25.refs_0_), channel_id=1, source_target_pairs={{0,4},{2,6},{4,0},{6,2},{8,12},{10,14},{12,8},{14,10},{16,20},{18,... | collective-permute-start | bytes 1572872 | tf_op jit(solution)/shard_map/ppermute | solution.py:20
  97.1 51.0 %collective-permute-start.28 = (bf16[128,2048]{1,0:T(8,128)(2,1)}, bf16[128,2048]{1,0:T(8,128)(2,1)S(1)}, u32[]{:S(2)}, u32[]{:S(2)}) collective-permute-start(bf16[128,2048]{1,0:T(8,128)(2,1)} %collective-permute-done.26.refs_1_), channel_id=1, source_target_pairs={{0,4},{2,6},{4,0},{6,2},{8,12},{10,14},{12,8},{14,10},{16,20},{18,... | collective-permute-start | bytes 1572872 | tf_op jit(solution)/shard_map/ppermute | solution.py:20
  109.7 48.9 %collective-permute-start.35 = (bf16[128,2048]{1,0:T(8,128)(2,1)S(1)}, bf16[128,2048]{1,0:T(8,128)(2,1)S(1)}, u32[]{:S(2)}, u32[]{:S(2)}) collective-permute-start(bf16[128,2048]{1,0:T(8,128)(2,1)S(1)} %collective-permute-done.33.refs_0_), channel_id=1, source_target_pairs={{0,4},{2,6},{4,0},{6,2},{8,12},{10,14},{12,8},{14,10},{16,20},{18,... | collective-permute-start | bytes 1572872 | tf_op jit(solution)/shard_map/ppermute | solution.py:20
  127.0 10.1 %copy-start.13 = (bf16[1,2048,352]{1,2,0:T(8,128)(2,1)S(1)}, bf16[1,2048,352]{1,2,0:T(8,128)(2,1)}, u32[]{:S(2)}) copy-start(bf16[1,2048,352]{1,2,0:T(8,128)(2,1)} %param.21) | copy-start | bytes 4325380
  127.0 10.1 %copy-start.15 = (bf16[1,2048,352]{1,2,0:T(8,128)(2,1)S(1)}, bf16[1,2048,352]{1,2,0:T(8,128)(2,1)}, u32[]{:S(2)}) copy-start(bf16[1,2048,352]{1,2,0:T(8,128)(2,1)} %param.22) | copy-start | bytes 4325380
  127.0 10.1 %copy-start.17 = (bf16[1,352,2048]{2,1,0:T(8,128)(2,1)S(1)}, bf16[1,352,2048]{2,1,0:T(8,128)(2,1)}, u32[]{:S(2)}) copy-start(bf16[1,352,2048]{2,1,0:T(8,128)(2,1)} %param.23) | copy-start | bytes 4325380
  127.0 10.1 %copy-start.19 = (bf16[128,2048]{1,0:T(8,128)(2,1)S(1)}, bf16[128,2048]{1,0:T(8,128)(2,1)}, u32[]{:S(2)}) copy-start(bf16[128,2048]{1,0:T(8,128)(2,1)} %copy-done.18) | copy-start | bytes 1572868
  136.4 22.8 %collective-permute-start.18 = (bf16[128,2048]{1,0:T(8,128)(2,1)S(1)}, bf16[128,2048]{1,0:T(8,128)(2,1)S(1)}, u32[]{:S(2)}, u32[]{:S(2)}) collective-permute-start(bf16[128,2048]{1,0:T(8,128)(2,1)S(1)} %get-tuple-element.33), channel_id=1, source_target_pairs={{0,8},{2,10},{4,12},{6,14},{8,0},{10,2},{12,4},{14,6},{16,24},{18,... | collective-permute-start | bytes 1572872 | tf_op jit(solution)/shard_map/ppermute | solution.py:20
  146.2 16.5 %collective-permute-start.34 = (bf16[128,2048]{1,0:T(8,128)(2,1)S(1)}, bf16[128,2048]{1,0:T(8,128)(2,1)S(1)}, u32[]{:S(2)}, u32[]{:S(2)}) collective-permute-start(bf16[128,2048]{1,0:T(8,128)(2,1)S(1)} %collective-permute-done.33.refs_0_), channel_id=1, source_target_pairs={{0,2},{2,0},{4,6},{6,4},{8,10},{10,8},{12,14},{14,12},{16,18},{18,... | collective-permute-start | bytes 1572872 | tf_op jit(solution)/shard_map/ppermute | solution.py:20
  146.7 14.3 %collective-permute-start.20 = (bf16[128,2048]{1,0:T(8,128)(2,1)S(1)}, bf16[128,2048]{1,0:T(8,128)(2,1)S(1)}, u32[]{:S(2)}, u32[]{:S(2)}) collective-permute-start(bf16[128,2048]{1,0:T(8,128)(2,1)S(1)} %get-tuple-element.36), channel_id=1, source_target_pairs={{0,8},{2,10},{4,12},{6,14},{8,0},{10,2},{12,4},{14,6},{16,24},{18,... | collective-permute-start | bytes 1572872 | tf_op jit(solution)/shard_map/ppermute | solution.py:20
  148.1 36.2 %collective-permute-start.23 = (bf16[128,2048]{1,0:T(8,128)(2,1)S(1)}, bf16[128,2048]{1,0:T(8,128)(2,1)S(1)}, u32[]{:S(2)}, u32[]{:S(2)}) collective-permute-start(bf16[128,2048]{1,0:T(8,128)(2,1)S(1)} %get-tuple-element.38), channel_id=1, source_target_pairs={{0,4},{2,6},{4,0},{6,2},{8,12},{10,14},{12,8},{14,10},{16,20},{18,... | collective-permute-start | bytes 1572872 | tf_op jit(solution)/shard_map/ppermute | solution.py:20
  158.6 25.1 %collective-permute-start.29 = (bf16[128,2048]{1,0:T(8,128)(2,1)S(1)}, bf16[128,2048]{1,0:T(8,128)(2,1)S(1)}, u32[]{:S(2)}, u32[]{:S(2)}) collective-permute-start(bf16[128,2048]{1,0:T(8,128)(2,1)S(1)} %get-tuple-element.42), channel_id=1, source_target_pairs={{0,4},{2,6},{4,0},{6,2},{8,12},{10,14},{12,8},{14,10},{16,20},{18,... | collective-permute-start | bytes 1572872 | tf_op jit(solution)/shard_map/ppermute | solution.py:20
  159.3 14.9 %collective-permute-start.36 = (bf16[128,2048]{1,0:T(8,128)(2,1)S(1)}, bf16[128,2048]{1,0:T(8,128)(2,1)S(1)}, u32[]{:S(2)}, u32[]{:S(2)}) collective-permute-start(bf16[128,2048]{1,0:T(8,128)(2,1)S(1)} %collective-permute-done.35.refs_2_), channel_id=1, source_target_pairs={{0,2},{2,0},{4,6},{6,4},{8,10},{10,8},{12,14},{14,12},{16,18},{18,... | collective-permute-start | bytes 1572872 | tf_op jit(solution)/shard_map/ppermute | solution.py:20
  161.0 50.2 %collective-permute-start.31 = (bf16[128,2048]{1,0:T(8,128)(2,1)S(1)}, bf16[128,2048]{1,0:T(8,128)(2,1)S(1)}, u32[]{:S(2)}, u32[]{:S(2)}) collective-permute-start(bf16[128,2048]{1,0:T(8,128)(2,1)S(1)} %get-tuple-element.43), channel_id=1, source_target_pairs={{0,4},{2,6},{4,0},{6,2},{8,12},{10,14},{12,8},{14,10},{16,20},{18,... | collective-permute-start | bytes 1572872 | tf_op jit(solution)/shard_map/ppermute | solution.py:20
  162.7 67.6 %collective-permute-start.19 = (bf16[128,2048]{1,0:T(8,128)(2,1)S(1)}, bf16[128,2048]{1,0:T(8,128)(2,1)S(1)}, u32[]{:S(2)}, u32[]{:S(2)}) collective-permute-start(bf16[128,2048]{1,0:T(8,128)(2,1)S(1)} %add_convert_fusion.8), channel_id=1, source_target_pairs={{0,2},{2,0},{4,6},{6,4},{8,10},{10,8},{12,14},{14,12},{16,18},{18,... | collective-permute-start | bytes 1572872 | tf_op jit(solution)/shard_map/ppermute | solution.py:20
  174.1 35.5 %collective-permute-start.21 = (bf16[128,2048]{1,0:T(8,128)(2,1)S(1)}, bf16[128,2048]{1,0:T(8,128)(2,1)S(1)}, u32[]{:S(2)}, u32[]{:S(2)}) collective-permute-start(bf16[128,2048]{1,0:T(8,128)(2,1)S(1)} %add_convert_fusion.7), channel_id=1, source_target_pairs={{0,2},{2,0},{4,6},{6,4},{8,10},{10,8},{12,14},{14,12},{16,18},{18,... | collective-permute-start | bytes 1572872 | tf_op jit(solution)/shard_map/ppermute | solution.py:20
  183.7 24.1 %collective-permute-start.38 = (bf16[128,2048]{1,0:T(8,128)(2,1)S(1)}, bf16[128,2048]{1,0:T(8,128)(2,1)S(1)}, u32[]{:S(2)}, u32[]{:S(2)}) collective-permute-start(bf16[128,2048]{1,0:T(8,128)(2,1)S(1)} %get-tuple-element.48), channel_id=1, source_target_pairs={{0,2},{2,0},{4,6},{6,4},{8,10},{10,8},{12,14},{14,12},{16,18},{18,... | collective-permute-start | bytes 1572872 | tf_op jit(solution)/shard_map/ppermute | solution.py:20
  184.4 34.7 %collective-permute-start.30 = (bf16[128,2048]{1,0:T(8,128)(2,1)S(1)}, bf16[128,2048]{1,0:T(8,128)(2,1)S(1)}, u32[]{:S(2)}, u32[]{:S(2)}) collective-permute-start(bf16[128,2048]{1,0:T(8,128)(2,1)S(1)} %add_convert_fusion.4), channel_id=1, source_target_pairs={{0,2},{2,0},{4,6},{6,4},{8,10},{10,8},{12,14},{14,12},{16,18},{18,... | collective-permute-start | bytes 1572872 | tf_op jit(solution)/shard_map/ppermute | solution.py:20
  207.8 19.4 %collective-permute-start.37 = (bf16[128,2048]{1,0:T(8,128)(2,1)S(1)}, bf16[128,2048]{1,0:T(8,128)(2,1)S(1)}, u32[]{:S(2)}, u32[]{:S(2)}) collective-permute-start(bf16[128,2048]{1,0:T(8,128)(2,1)S(1)} %get-tuple-element.46), channel_id=1, source_target_pairs={{0,2},{2,0},{4,6},{6,4},{8,10},{10,8},{12,14},{14,12},{16,18},{18,... | collective-permute-start | bytes 1572872 | tf_op jit(solution)/shard_map/ppermute | solution.py:20
  209.6 17.7 %collective-permute-start.39 = (bf16[128,2048]{1,0:T(8,128)(2,1)S(1)}, bf16[128,2048]{1,0:T(8,128)(2,1)S(1)}, u32[]{:S(2)}, u32[]{:S(2)}) collective-permute-start(bf16[128,2048]{1,0:T(8,128)(2,1)S(1)} %add_convert_fusion.2), channel_id=1, source_target_pairs={{0,4},{2,6},{4,0},{6,2},{8,12},{10,14},{12,8},{14,10},{16,20},{18,... | collective-permute-start | bytes 1572872 | tf_op jit(solution)/shard_map/ppermute | solution.py:20
  211.3 19.0 %collective-permute-start.24 = (bf16[128,2048]{1,0:T(8,128)(2,1)S(1)}, bf16[128,2048]{1,0:T(8,128)(2,1)S(1)}, u32[]{:S(2)}, u32[]{:S(2)}) collective-permute-start(bf16[128,2048]{1,0:T(8,128)(2,1)S(1)} %add_convert_fusion.5), channel_id=1, source_target_pairs={{0,8},{2,10},{4,12},{6,14},{8,0},{10,2},{12,4},{14,6},{16,24},{18,... | collective-permute-start | bytes 1572872 | tf_op jit(solution)/shard_map/ppermute | solution.py:20
  219.1 11.2 %collective-permute-start.22 = (bf16[128,2048]{1,0:T(8,128)(2,1)S(1)}, bf16[128,2048]{1,0:T(8,128)(2,1)S(1)}, u32[]{:S(2)}, u32[]{:S(2)}) collective-permute-start(bf16[128,2048]{1,0:T(8,128)(2,1)S(1)} %add_convert_fusion.6), channel_id=1, source_target_pairs={{0,4},{2,6},{4,0},{6,2},{8,12},{10,14},{12,8},{14,10},{16,20},{18,... | collective-permute-start | bytes 1572872 | tf_op jit(solution)/shard_map/ppermute | solution.py:20
  220.8 51.9 %copy-start.6 = (f32[128,2048]{1,0:T(8,128)S(1)}, f32[128,2048]{1,0:T(8,128)}, u32[]{:S(2)}) copy-start(f32[128,2048]{1,0:T(8,128)} %copy-done.5) | copy-start | bytes 3145732
  227.2 32.6 %collective-permute-start.32 = (bf16[128,2048]{1,0:T(8,128)(2,1)S(1)}, bf16[128,2048]{1,0:T(8,128)(2,1)S(1)}, u32[]{:S(2)}, u32[]{:S(2)}) collective-permute-start(bf16[128,2048]{1,0:T(8,128)(2,1)S(1)} %add_convert_fusion.3), channel_id=1, source_target_pairs={{0,16},{2,18},{4,20},{6,22},{8,24},{10,26},{12,28},{14,30},{16,0},... | collective-permute-start | bytes 1572872 | tf_op jit(solution)/shard_map/ppermute | solution.py:20
  227.5 45.2 %collective-permute-start.40 = (bf16[128,2048]{1,0:T(8,128)(2,1)S(1)}, bf16[128,2048]{1,0:T(8,128)(2,1)S(1)}, u32[]{:S(2)}, u32[]{:S(2)}) collective-permute-start(bf16[128,2048]{1,0:T(8,128)(2,1)S(1)} %add_convert_fusion.1), channel_id=1, source_target_pairs={{0,24},{2,26},{4,28},{6,30},{8,16},{10,18},{12,20},{14,22},{16,8},... | collective-permute-start | bytes 1572872 | tf_op jit(solution)/shard_map/ppermute | solution.py:20
  (13 other events, 18.8 us)

commit v5 on v4

v5 whole, which is shorter than its diff:
```python
import functools
import math

import jax
import jax.numpy as jnp
from jax import lax
from jax.experimental import pallas as pl
from jax.experimental.pallas import tpu as pltpu
from jax.sharding import PartitionSpec as P

HD = 128
SWAP = [(0, 1), (1, 0)]
VMEM = pl.BlockSpec(memory_space=pltpu.VMEM)
ANY = pl.BlockSpec(memory_space=pl.ANY)
NT = (((1,), (1,)), ((), ()))


def flip(block, mask):
    count = lax.axis_size("seq")
    return lax.ppermute(block, "seq", [(i, i ^ mask) for i in range(count)])


def after(block, *arrays):
    return lax.optimization_barrier((block, *arrays))[0]


def gate_order(count):
    masks = [1 << bit for bit in range(count.bit_length() - 1)]
    return masks[2:] + masks[1::-1]


def gather_gates(block):
    for mask in gate_order(lax.axis_size("seq")):
        half = block
        block = jnp.concatenate([half, flip(half, mask)], axis=0)
    return half, block


def place_of(j):
    return sum(1 << bit for bit, mask in enumerate(gate_order(lax.axis_size("seq"))) if j & mask)


def stack_kernel(keys_ref, values_ref, out_ref, sems):
    rows = keys_ref.shape[0]
    copies = [
        pltpu.make_async_copy(ref, out_ref.at[pl.ds(i * rows, rows), :], sems.at[i])
        for i, ref in enumerate((keys_ref, values_ref))
    ]
    for copy in copies:
        copy.start()
    for copy in copies:
        copy.wait()


def stack(keys, values):
    rows, width = keys.shape
    return pl.pallas_call(
        stack_kernel,
        out_shape=jax.ShapeDtypeStruct((2 * rows, width), keys.dtype),
        in_specs=[ANY, ANY],
        out_specs=ANY,
        scratch_shapes=[pltpu.SemaphoreType.DMA((2,))],
        name="stack_keys_values",
    )(keys, values)


def attention_kernel(core_ref, q_ref, before_ref, own_ref, after_ref, ids_ref, *refs):
    theirs_ref, mine_ref = refs[-2:]
    rows = q_ref.shape[0]
    some = rows // 2
    scale = 1.0 / math.sqrt(HD)
    column = jnp.transpose(jnp.broadcast_to(ids_ref[:, rows : 2 * rows], (HD, rows)))[:, :1]
    for half in range(2):
        first = half * some
        spans = [
            (before_ref, half * some, rows),
            (own_ref, 0, rows),
            (after_ref, 0, some + half * some),
        ]
        keys = 2 * rows + some
        query_pos = lax.broadcasted_iota(jnp.int32, (some, keys), 0) + (first + rows)
        key_pos = lax.broadcasted_iota(jnp.int32, (some, keys), 1) + first
        allowed = (column[first : first + some] == ids_ref[:, first : first + keys]) & (
            jnp.abs(query_pos - key_pos) < rows
        )
        for head in range(q_ref.shape[1] // HD):
            cols = slice(head * HD, (head + 1) * HD)
            query = q_ref[first : first + some, cols]
            score = jnp.concatenate(
                [
                    lax.dot_general(query, ref[lo:hi, cols], NT, preferred_element_type=jnp.float32)
                    for ref, lo, hi in spans
                ],
                axis=1,
            )
            score = jnp.where(allowed, score * scale, -jnp.inf)
            weights = jnp.exp(score - jnp.max(score, axis=-1, keepdims=True))
            share = 1.0 / jnp.sum(weights, axis=-1, keepdims=True)
            probs = (weights * share).astype(jnp.bfloat16)
            total, at = jnp.zeros((some, HD), jnp.float32), 0
            for ref, lo, hi in spans:
                total += jnp.dot(
                    probs[:, at : at + hi - lo],
                    ref[rows + lo : rows + hi, cols],
                    preferred_element_type=jnp.float32,
                )
                at += hi - lo
            total = total.astype(jnp.bfloat16)

            @pl.when(core_ref[0] == half)
            def _():
                mine_ref[:, cols] = total

            @pl.when(core_ref[0] != half)
            def _():
                theirs_ref[:, cols] = total


def attention(core, queries, near, ids, *ahead):
    rows, width = queries.shape
    half = jax.ShapeDtypeStruct((rows // 2, width), jnp.bfloat16)
    return pl.pallas_call(
        attention_kernel,
        out_shape=(half, half),
        in_specs=[pl.BlockSpec(memory_space=pltpu.SMEM)] + [VMEM] * 5 + [ANY] * len(ahead),
        out_specs=(VMEM, VMEM),
        compiler_params=pltpu.CompilerParams(vmem_limit_bytes=16 * 1024 * 1024),
        name="window_attention",
    )(core, queries, *near, ids, *ahead)


def norm_kernel(mine_ref, theirs_ref, own_w, other_w, resid_ref, gain_ref, *refs):
    stream_ref, normed_ref = refs[-2:]
    stream = resid_ref[...].astype(jnp.float32)
    stream += jnp.dot(mine_ref[...], own_w[...], preferred_element_type=jnp.float32)
    stream += jnp.dot(theirs_ref[...], other_w[...], preferred_element_type=jnp.float32)
    meansq = jnp.mean(stream * stream, axis=-1, keepdims=True)
    stream_ref[...] = stream
    normed_ref[...] = (stream * lax.rsqrt(meansq + 1e-05) * gain_ref[...]).astype(jnp.bfloat16)


def project_and_norm(mine, theirs, own_w, other_w, resid, gain, *ahead):
    rows, width = resid.shape
    return pl.pallas_call(
        norm_kernel,
        out_shape=(
            jax.ShapeDtypeStruct((rows, width), jnp.float32),
            jax.ShapeDtypeStruct((rows, width), jnp.bfloat16),
        ),
        in_specs=[VMEM] * 6 + [ANY] * len(ahead),
        out_specs=(VMEM, VMEM),
        compiler_params=pltpu.CompilerParams(vmem_limit_bytes=16 * 1024 * 1024),
        name="project_and_norm",
    )(mine, theirs, own_w, other_w, resid, gain, *ahead)


def expert_kernel(places, shard_ref, *refs):
    count = len(places)
    blocks, gates_ref, halves = refs[:count], refs[count], refs[count + 1 : count + 7]
    outs, (gate_w, up_w, down_w, sems) = refs[count + 7 : -4], refs[-4:]
    units = halves[0].shape[0]
    copies = []
    for i, half in enumerate(halves):
        target = (gate_w, up_w, down_w)[i // 2].at[pl.ds(i % 2 * units, units), :]
        copies.append(pltpu.make_async_copy(half, target, sems.at[i]))
        copies[-1].start()
    rows = blocks[0].shape[0]
    tokens = jnp.concatenate([ref[...] for ref in blocks], axis=0)
    copies[0].wait()
    copies[1].wait()
    gate = lax.dot_general(tokens, gate_w[...], NT, preferred_element_type=jnp.float32)
    copies[2].wait()
    copies[3].wait()
    up = lax.dot_general(tokens, up_w[...], NT, preferred_element_type=jnp.float32)
    act = (gate / (1.0 + jnp.exp(-gate)) * up).astype(jnp.bfloat16)
    copies[4].wait()
    copies[5].wait()
    result = jnp.dot(act, down_w[...], preferred_element_type=jnp.float32)
    for i, place in enumerate(places):
        gates = gates_ref[place * rows : (place + 1) * rows, :]
        expert = lax.broadcasted_iota(jnp.int32, gates.shape, 1)
        chosen = jnp.sum(jnp.where(expert == shard_ref[0], gates, 0.0), axis=1, keepdims=True)
        outs[i][...] = (result[i * rows : (i + 1) * rows] * chosen).astype(jnp.bfloat16)


def expert(blocks, places, shard, gates, halves):
    rows, width = blocks[0].shape
    units = halves[0].shape[0]
    count = len(blocks)
    return pl.pallas_call(
        functools.partial(expert_kernel, places),
        out_shape=[jax.ShapeDtypeStruct((rows, width), jnp.bfloat16)] * count,
        in_specs=[pl.BlockSpec(memory_space=pltpu.SMEM)] + [VMEM] * (count + 1) + [ANY] * 6,
        out_specs=[VMEM] * count,
        scratch_shapes=[pltpu.VMEM((2 * units, width), jnp.bfloat16)] * 3
        + [pltpu.SemaphoreType.DMA((6,))],
        compiler_params=pltpu.CompilerParams(vmem_limit_bytes=40 * 1024 * 1024),
        name="expert_rows",
    )(shard, *blocks, gates, *halves)


def add(*terms):
    total = terms[0].astype(jnp.float32)
    for term in terms[1:]:
        total = total + term.astype(jnp.float32)
    return total


def add_small(*terms):
    return add(*terms).astype(jnp.bfloat16)


def shift(block, pairs):
    return lax.ppermute(block, "seq", [(4 * a + i, 4 * b + i) for a, b in pairs for i in range(4)])


OUTWARD, INWARD, MIDDLE = [(1, 0), (2, 3)], [(0, 1), (3, 2)], [(1, 2), (2, 1)]


def step_layer(normed, stream, run):
    z = lax.axis_index("seq") // 4
    inner = (z == 1) | (z == 2)

    def step(arrays, *waits):
        return lax.optimization_barrier((*arrays, *waits))[: len(arrays)]

    o0 = normed
    x0, y0, o1, near3 = flip(o0, 1), flip(o0, 2), flip(o0, 4), shift(o0, MIDDLE)

    x0, y0, o1, near3 = step([x0, y0, o1, near3])
    d0, y1 = flip(y0, 1), flip(o1, 2)
    ends2, near2 = shift(near3, OUTWARD), shift(o1, MIDDLE)

    d0, y1, ends2, near2 = step([d0, y1, ends2, near2])
    o2 = jnp.where(inner, near2, ends2)
    ends3, x2, y2 = shift(near2, OUTWARD), flip(o2, 1), flip(o2, 2)
    p0, px0, py0, pd0 = run([o0, x0, y0, d0], (0, 1, 2, 3))

    ends3, x2, y2, x0, near3 = step([ends3, x2, y2, x0, near3], p0)
    o3 = jnp.where(inner, near3, ends3)
    x3, y3, x1 = flip(o3, 1), flip(o3, 2), flip(x0, 4)
    p1, py1, p2, px2, py2, p3 = run([o1, y1, o2, x2, y2, o3], (4, 6, 8, 9, 10, 12))

    x3, y3, x1, y2, d0 = step([x3, y3, x1, y2, d0], p1)
    d2, d3, d1 = flip(y2, 1), flip(x3, 2), flip(d0, 4)
    px3, py3, px1 = run([x3, y3, x1], (13, 14, 5))

    d2, d3, d1 = step([d2, d3, d1], px3)
    pd2, pd3, pd1 = run([d2, d3, d1], (11, 15, 7))
    to_y2, to_x3, to_d0 = flip(pd2, 1), flip(pd3, 2), flip(pd1, 4)

    px3, py2, pd0 = add_small(px3, to_x3), add_small(py2, to_y2), add_small(pd0, to_d0)
    px3, py3, px1, py2, pd0 = step([px3, py3, px1, py2, pd0])
    by_x, by_y, to_x0 = flip(px3, 1), flip(py3, 2), flip(px1, 4)

    p3, px0 = add_small(p3, by_x, by_y), add_small(px0, to_x0)
    p3, px0, px2, py2 = step([p3, px0, px2, py2])
    to_2, by_x, by_y = shift(p3, INWARD), flip(px2, 1), flip(py2, 2)

    p2 = add_small(p2, by_x, by_y, to_2)
    p2, pd0, py1 = step([p2, pd0, py1])
    to_3, to_1, to_y0, by_y = shift(p2, INWARD), shift(p2, MIDDLE), flip(pd0, 1), flip(py1, 2)

    p3, p1, py0 = add_small(p3, to_3), add_small(p1, by_y, to_1), add_small(py0, to_y0)
    p3, p1, py0, px0 = step([p3, p1, py0, px0])
    by_z, by_middle, by_x, by_y = flip(p1, 4), shift(p3, MIDDLE), flip(px0, 1), flip(py0, 2)
    return add(stream, p0, by_z, by_middle, by_x, by_y)


def expert_layer(normed, stream, shard, gates, halves):
    count = lax.axis_size("seq")

    def run(blocks, masks):
        places = tuple(place_of(mask) for mask in masks)
        return expert(blocks, places, shard, gates, halves)

    if count == 16:
        return step_layer(normed, stream, run)
    blocks, mask = [normed], 1
    while mask < count:
        blocks = blocks + [flip(block, mask) for block in blocks]
        mask *= 2
    parts = []
    for first in range(0, count, 4):
        parts += run(blocks[first : first + 4], range(first, first + 4))
    while mask > 1:
        mask //= 2
        parts = [add_small(parts[i], flip(parts[i + mask], mask)) for i in range(mask)]
    return add(stream, parts[0])


def shards(
    queries,
    keys,
    values,
    resid,
    pair_ids,
    out_weight,
    norm_gain,
    experts,
    gates,
    w_gate,
    w_up,
    w_down,
):
    tok_rows = queries.shape[0]
    moe_rows = resid.shape[0]
    shard = lax.axis_index("seq")
    core = lax.axis_index("exp")
    count = lax.axis_size("seq")

    own = stack(keys, values)
    before = lax.ppermute(own, "seq", [(i, i + 1) for i in range(count - 1)])
    after_own = lax.ppermute(own, "seq", [(i + 1, i) for i in range(count - 1)])
    per_expert = jnp.sum(
        jnp.where(
            experts[:, :, None] == jnp.arange(count, dtype=jnp.int32)[None, None, :],
            gates[:, :, None],
            0.0,
        ),
        axis=1,
    )
    some_gates, all_gates = gather_gates(per_expert)
    id_pad = jnp.pad(pair_ids, (tok_rows, tok_rows), constant_values=-1)
    ids = lax.dynamic_slice_in_dim(id_pad, shard * tok_rows, 3 * tok_rows, 0)[None, :]
    out_other = lax.ppermute(out_weight, "exp", SWAP)
    gate_w, up_w = jnp.swapaxes(w_gate[0], 0, 1), jnp.swapaxes(w_up[0], 0, 1)
    gate_other = lax.ppermute(gate_w, "exp", SWAP)
    ready = (before, after_own, some_gates, ids)
    up_other = lax.ppermute(after(up_w, *ready), "exp", SWAP)
    down_other = lax.ppermute(after(w_down[0], *ready), "exp", SWAP)
    halves = [gate_w, gate_other, up_w, up_other, w_down[0], down_other]

    theirs, mine = attention(
        core.reshape(1), queries, (before, own, after_own), ids, out_other, gate_other
    )
    received = lax.ppermute(theirs, "exp", SWAP)
    ahead = (up_other, down_other, all_gates)
    stream, normed = project_and_norm(
        mine, received, out_weight, out_other, resid, norm_gain[None, :], *ahead
    )
    mixed = expert_layer(normed, stream, shard.reshape(1), all_gates, halves)
    return mixed.astype(jnp.bfloat16)


def solution(mesh):
    in_specs = (
        P("seq", "exp"),
        P("seq", "exp"),
        P("seq", "exp"),
        P(("seq", "exp"), None),
        P(),
        P("exp", None),
        P(),
        P(("seq", "exp"), None),
        P(("seq", "exp"), None),
        P("seq", None, "exp"),
        P("seq", None, "exp"),
        P("seq", "exp", None),
    )
    out_specs = P(("seq", "exp"), None)
    return jax.shard_map(shards, mesh=mesh, in_specs=in_specs, out_specs=out_specs, check_vma=False)
```

time: 275 us -> 247 us (0.90)
  waiting for transfers between devices: 149 us -> 93 us
  Pallas kernels: 45.2 us -> 58.4 us
  starting transfers between devices: 52.1 us -> 61.9 us
  other arithmetic: 3.3 us -> 6.53 us
    ppermute x34 -> x30, waiting for transfers between devices: 149 us -> 73.7 us  [flip(): return lax.ppermute(block, 'seq', [(i, i ^ mask) for i in range(count)])]
    ppermute x0 -> x8, starting transfers between devices: none -> 19.8 us  [shift(): lax.ppermute(block, 'seq', [(4 * a + i, 4 * b + i) for a, b in pairs for...]
    ppermute x0 -> x8, waiting for transfers between devices: none -> 19.3 us  [shift(): lax.ppermute(block, 'seq', [(4 * a + i, 4 * b + i) for a, b in pairs for...]
    pallas_call x2, Pallas kernels: 8.06 us -> 22.3 us  [the longest x1 17 us: stack(): pl.pallas_call(stack_kernel, out_shape=jax.ShapeDtypeStruct((2 * rows, wi...]
    ppermute x34 -> x30, starting transfers between devices: 45.2 us -> 35.7 us  [flip(): return lax.ppermute(block, 'seq', [(i, i ^ mask) for i in range(count)])]
    unnamed x45 -> x54, local copies, waits for them, and re-layouts: 16.9 us -> 21.8 us
  transfers between devices with their start and end apart: 41 -> 45, of which waited for: 17 -> 26; matrix products, arithmetic and copies ran while one was open for 4% -> 3% of each run, Pallas kernels for 16% -> 21%
where the time goes in v5:
time: 247 us; the launch traced here: 245 us
  waiting for transfers between devices  93 us (38%)
  starting transfers between devices  61.9 us (25%)
  Pallas kernels  58.4 us (24%)
  local copies, waits for them, and re-layouts  24.4 us (10%)
  other arithmetic  6.53 us (3%)
    ppermute x30, waiting for transfers between devices, flip(): return lax.ppermute(block, 'seq', [(i, i ^ mask) for i in range(count)])  73.7 us
    ppermute x30, starting transfers between devices, flip(): return lax.ppermute(block, 'seq', [(i, i ^ mask) for i in range(count)])  35.7 us
    pallas_call x4, Pallas kernels, expert(): pl.pallas_call(functools.partial(expert_kernel, places), out_shape=[jax.S...  35.2 us
    unnamed x54, local copies, waits for them, and re-layouts  21.8 us
    ppermute x8, starting transfers between devices, shift(): lax.ppermute(block, 'seq', [(4 * a + i, 4 * b + i) for a, b in pairs for...  19.8 us
    ppermute x8, waiting for transfers between devices, shift(): lax.ppermute(block, 'seq', [(4 * a + i, 4 * b + i) for a, b in pairs for...  19.3 us
    pallas_call x1, Pallas kernels, stack(): pl.pallas_call(stack_kernel, out_shape=jax.ShapeDtypeStruct((2 * rows, wi...  17 us
    pallas_call x1, Pallas kernels, attention(): pl.pallas_call(attention_kernel, out_shape=(half, half), in_specs=[pl.Blo...  5.28 us
  transfers between devices with their start and end apart: 45, of which 26 were waited for; matrix products, arithmetic and copies ran while one was open for 3% of the time, Pallas kernels for 21%

profile of v5, /device:TPU:10, one launch (start us, length us, event | category | flops | bytes accessed | tf_op | source)
XLA Modules:
  0.0 244.7 jit_solution(5122523303642873119)
XLA Ops:
  0.0 17.0 %stack_keys_values.1.own_ref = bf16[512,512]{1,0:T(8,128)(2,1)} custom-call(bf16[256,512]{1,0:T(8,128)(2,1)} %keys_ref.1, bf16[256,512]{1,0:T(8,128)(2,1)} %values_ref.1), custom_call_target="tpu_custom_call" | custom-call | tf_op jit(solution)/shard_map/stack_keys_values/pallas_call | solution.py:57
  17.0 3.4 %collective-permute-start = (bf16[512,512]{1,0:T(8,128)(2,1)}, bf16[512,512]{1,0:T(8,128)(2,1)S(1)}, u32[]{:S(2)}, u32[]{:S(2)}) collective-permute-start(bf16[512,512]{1,0:T(8,128)(2,1)} %stack_keys_values.1.own_ref), channel_id=1, source_target_pairs={{0,2},{2,4},{4,6},{6,8},{8,10},{10,12},{12,14},{14,16},{16,18},{18... | collective-permute-start | bytes 1572872 | tf_op jit(solution)/shard_map/ppermute | solution.py:313
  20.4 2.4 collective-permute-start.1
  24.1 3.2 %collective-permute-done.5 = f32[128,16]{0,1:T(8,128)S(1)} collective-permute-done((f32[128,16]{0,1:T(8,128)S(1)}, f32[128,16]{0,1:T(8,128)S(1)}, u32[]{:S(2)}, u32[]{:S(2)}) %collective-permute-start.5) | collective-permute-done | bytes 8224 | tf_op jit(solution)/shard_map/ppermute | solution.py:20
  27.3 2.6 %collective-permute-start.6 = (f32[256,16]{0,1:T(8,128)S(1)}, f32[256,16]{0,1:T(8,128)S(1)}, u32[]{:S(2)}, u32[]{:S(2)}) collective-permute-start(f32[256,16]{0,1:T(8,128)S(1)} %pad_maximum_fusion.2), channel_id=1, source_target_pairs={{0,16},{2,18},{4,20},{6,22},{8,24},{10,26},{12,28},{14,30},{16,0},... | collective-permute-start | bytes 49160 | tf_op jit(solution)/shard_map/ppermute | solution.py:20
  29.9 2.0 collective-permute-done.6
  32.0 7.8 %collective-permute-start.7 = (f32[512,16]{0,1:T(8,128)S(1)}, f32[512,16]{0,1:T(8,128)S(1)}, u32[]{:S(2)}, u32[]{:S(2)}) collective-permute-start(f32[512,16]{0,1:T(8,128)S(1)} %pad_maximum_fusion.1), channel_id=1, source_target_pairs={{0,4},{2,6},{4,0},{6,2},{8,12},{10,14},{12,8},{14,10},{16,20},{18,... | collective-permute-start | bytes 98312 | tf_op jit(solution)/shard_map/ppermute | solution.py:20
  40.5 5.8 %collective-permute-done.7 = f32[512,16]{0,1:T(8,128)S(1)} collective-permute-done((f32[512,16]{0,1:T(8,128)S(1)}, f32[512,16]{0,1:T(8,128)S(1)}, u32[]{:S(2)}, u32[]{:S(2)}) %collective-permute-start.7) | collective-permute-done | bytes 32800 | tf_op jit(solution)/shard_map/ppermute | solution.py:20
  52.4 1.4 copy-done.7
  56.8 5.3 %window_attention.1 = (bf16[128,512]{1,0:T(8,128)(2,1)}, bf16[128,512]{1,0:T(8,128)(2,1)S(1)}) custom-call(s32[1]{0:T(128)} %bitcast.core_ref, bf16[256,512]{1,0:T(8,128)(2,1)S(1)} %copy-done.15, bf16[512,512]{1,0:T(8,128)(2,1)S(1)} %copy-done.12, bf16[512,512]{1,0:T(8,128)(2,1)S(1)} %copy-done.7, bf16[512,512]{1,0:T(8,128)(2,1)S(1)} %copy-done.14, ...), custom_call_target="tpu_custom_call" | custom-call | tf_op jit(solution)/shard_map/window_attention/pallas_call | solution.py:122
  66.0 1.6 copy-done.5
  67.5 1.6 copy-done.6
  72.9 2.1 collective-permute-start.11
  75.4 4.6 %collective-permute-start.14 = (bf16[128,2048]{1,0:T(8,128)(2,1)S(1)}, bf16[128,2048]{1,0:T(8,128)(2,1)}, u32[]{:S(2)}, u32[]{:S(2)}) collective-permute-start(bf16[128,2048]{1,0:T(8,128)(2,1)S(1)} %get-tuple-element.69.refs_0_), channel_id=1, source_target_pairs={{8,16},{10,18},{12,20},{14,22},{16,8},{18,10},{20,12},{22,14},{9,1... | collective-permute-start | bytes 1572872 | tf_op jit(solution)/shard_map/ppermute | solution.py:214
  80.8 6.8 %collective-permute-done.11.refs_1_ = bf16[128,2048]{1,0:T(8,128)(2,1)} collective-permute-done((bf16[128,2048]{1,0:T(8,128)(2,1)S(1)}, bf16[128,2048]{1,0:T(8,128)(2,1)}, u32[]{:S(2)}, u32[]{:S(2)}) %collective-permute-start.11) | collective-permute-done | bytes 524320 | tf_op jit(solution)/shard_map/ppermute | solution.py:20
  87.6 1.5 collective-permute-done.12.refs_2_
  89.1 3.0 %collective-permute-done.14 = bf16[128,2048]{1,0:T(8,128)(2,1)} collective-permute-done((bf16[128,2048]{1,0:T(8,128)(2,1)S(1)}, bf16[128,2048]{1,0:T(8,128)(2,1)}, u32[]{:S(2)}, u32[]{:S(2)}) %collective-permute-start.14) | collective-permute-done | bytes 524320 | tf_op jit(solution)/shard_map/ppermute | solution.py:214
  92.6 1.7 collective-permute-start.16
  94.3 2.1 collective-permute-start.17
  96.4 3.5 %collective-permute-start.18 = (bf16[128,2048]{1,0:T(8,128)(2,1)}, bf16[128,2048]{1,0:T(8,128)(2,1)}, u32[]{:S(2)}, u32[]{:S(2)}) collective-permute-start(bf16[128,2048]{1,0:T(8,128)(2,1)} %collective-permute-done.13.refs_0_), channel_id=1, source_target_pairs={{8,16},{10,18},{12,20},{14,22},{16,8},{18,10},{20,12},{22,14},{9,1... | collective-permute-start | bytes 1572872 | tf_op jit(solution)/shard_map/ppermute | solution.py:214
  100.0 5.7 %collective-permute-done.15.refs_3_ = bf16[128,2048]{1,0:T(8,128)(2,1)} collective-permute-done((bf16[128,2048]{1,0:T(8,128)(2,1)}, bf16[128,2048]{1,0:T(8,128)(2,1)}, u32[]{:S(2)}, u32[]{:S(2)}) %collective-permute-start.15) | collective-permute-done | bytes 524320 | tf_op jit(solution)/shard_map/ppermute | solution.py:20
  105.9 5.0 %collective-permute-done.18 = bf16[128,2048]{1,0:T(8,128)(2,1)} collective-permute-done((bf16[128,2048]{1,0:T(8,128)(2,1)}, bf16[128,2048]{1,0:T(8,128)(2,1)}, u32[]{:S(2)}, u32[]{:S(2)}) %collective-permute-start.18) | collective-permute-done | bytes 524320 | tf_op jit(solution)/shard_map/ppermute | solution.py:214
  112.0 1.7 collective-permute-start.20
  114.3 1.5 collective-permute-start.19
  119.6 9.5 %expert_rows.4 = (bf16[128,2048]{1,0:T(8,128)(2,1)S(1)}, bf16[128,2048]{1,0:T(8,128)(2,1)S(1)}, bf16[128,2048]{1,0:T(8,128)(2,1)S(1)}, bf16[128,2048]{1,0:T(8,128)(2,1)S(1)}) custom-call(s32[1]{0:T(128)} %bitcast.7.shard_ref, bf16[128,2048]{1,0:T(8,128)(2,1)S(1)} %copy-done.10, bf16[128,2048]{1,0:T(8,128)(2,1)} %collective-permute-done.11.refs_1_, ...), custom_call_target="tpu_custom_call" | custom-call | tf_op jit(solution)/shard_map/expert_rows/pallas_call | solution.py:190
  132.2 12.3 %expert_rows.5 = (bf16[128,2048]{1,0:T(8,128)(2,1)S(1)}, bf16[128,2048]{1,0:T(8,128)(2,1)S(1)}, bf16[128,2048]{1,0:T(8,128)(2,1)S(1)}, bf16[128,2048]{1,0:T(8,12...) custom-call(s32[1]{0:T(128)} %bitcast.7.shard_ref, ...), custom_call_target="tpu_custom_call" | custom-call | tf_op jit(solution)/shard_map/expert_rows/pallas_call | solution.py:190
  144.6 1.7 collective-permute-start.25
  146.9 2.0 collective-permute-start.27
  149.0 6.7 %expert_rows.6 = (bf16[128,2048]{1,0:T(8,128)(2,1)S(1)}, bf16[128,2048]{1,0:T(8,128)(2,1)S(1)}, bf16[128,2048]{1,0:T(8,128)(2,1)S(1)}) custom-call(s32[1]{0:T(128)} %bitcast.7.shard_ref, bf16[128,2048]{1,0:T(8,128)(2,1)S(1)} %collective-permute-done.22.refs_0_, bf16[128,2048]{1,0:T(8,128)(2,1)S(1)} %collective-permute-done.23.refs_1_, ...), custom_call_target="tpu_custom_call" | custom-call | tf_op jit(solution)/shard_map/expert_rows/pallas_call | solution.py:190
  157.2 6.7 %expert_rows.7 = (bf16[128,2048]{1,0:T(8,128)(2,1)S(1)}, bf16[128,2048]{1,0:T(8,128)(2,1)S(1)}, bf16[128,2048]{1,0:T(8,128)(2,1)S(1)}) custom-call(s32[1]{0:T(128)} %bitcast.7.shard_ref, bf16[128,2048]{1,0:T(8,128)(2,1)S(1)} %collective-permute-done.25.refs_0_, bf16[128,2048]{1,0:T(8,128)(2,1)S(1)} %collective-permute-done.26.refs_1_, ...), custom_call_target="tpu_custom_call" | custom-call | tf_op jit(solution)/shard_map/expert_rows/pallas_call | solution.py:190
  165.1 1.7 collective-permute-start.30
  167.2 6.6 %collective-permute-done.28 = bf16[128,2048]{1,0:T(8,128)(2,1)S(1)} collective-permute-done((bf16[128,2048]{1,0:T(8,128)(2,1)S(1)}, bf16[128,2048]{1,0:T(8,128)(2,1)S(1)}, u32[]{:S(2)}, u32[]{:S(2)}) %collective-permute-start.28) | collective-permute-done | bytes 524320 | tf_op jit(solution)/shard_map/ppermute | solution.py:20
  173.9 2.9 %collective-permute-done.30 = bf16[128,2048]{1,0:T(8,128)(2,1)S(1)} collective-permute-done((bf16[128,2048]{1,0:T(8,128)(2,1)S(1)}, bf16[128,2048]{1,0:T(8,128)(2,1)S(1)}, u32[]{:S(2)}, u32[]{:S(2)}) %collective-permute-start.30) | collective-permute-done | bytes 524320 | tf_op jit(solution)/shard_map/ppermute | solution.py:20
  176.9 2.6 %collective-permute-done.29 = bf16[128,2048]{1,0:T(8,128)(2,1)S(1)} collective-permute-done((bf16[128,2048]{1,0:T(8,128)(2,1)S(1)}, bf16[128,2048]{1,0:T(8,128)(2,1)S(1)}, u32[]{:S(2)}, u32[]{:S(2)}) %collective-permute-start.29) | collective-permute-done | bytes 524320 | tf_op jit(solution)/shard_map/ppermute | solution.py:20
  180.9 9.9 %collective-permute-done.33 = bf16[128,2048]{1,0:T(8,128)(2,1)S(1)} collective-permute-done((bf16[128,2048]{1,0:T(8,128)(2,1)S(1)}, bf16[128,2048]{1,0:T(8,128)(2,1)S(1)}, u32[]{:S(2)}, u32[]{:S(2)}) %collective-permute-start.33) | collective-permute-done | bytes 524320 | tf_op jit(solution)/shard_map/ppermute | solution.py:20
  190.9 2.7 %collective-permute-done.31 = bf16[128,2048]{1,0:T(8,128)(2,1)S(1)} collective-permute-done((bf16[128,2048]{1,0:T(8,128)(2,1)S(1)}, bf16[128,2048]{1,0:T(8,128)(2,1)S(1)}, u32[]{:S(2)}, u32[]{:S(2)}) %collective-permute-start.31) | collective-permute-done | bytes 524320 | tf_op jit(solution)/shard_map/ppermute | solution.py:20
  194.6 1.7 collective-permute-start.34
  197.9 10.7 %collective-permute-done.34 = bf16[128,2048]{1,0:T(8,128)(2,1)S(1)} collective-permute-done((bf16[128,2048]{1,0:T(8,128)(2,1)S(1)}, bf16[128,2048]{1,0:T(8,128)(2,1)S(1)}, u32[]{:S(2)}, u32[]{:S(2)}) %collective-permute-start.34) | collective-permute-done | bytes 524320 | tf_op jit(solution)/shard_map/ppermute | solution.py:20
  208.6 2.3 collective-permute-done.36
  212.5 1.7 collective-permute-start.40
  214.3 3.4 %collective-permute-start.39 = (bf16[128,2048]{1,0:T(8,128)(2,1)S(1)}, bf16[128,2048]{1,0:T(8,128)(2,1)S(1)}, u32[]{:S(2)}, u32[]{:S(2)}) collective-permute-start(bf16[128,2048]{1,0:T(8,128)(2,1)S(1)} %add_convert_fusion.4), channel_id=1, source_target_pairs={{8,16},{10,18},{12,20},{14,22},{16,8},{18,10},{20,12},{22,14},{9,1... | collective-permute-start | bytes 1572872 | tf_op jit(solution)/shard_map/ppermute | solution.py:214
  218.2 6.9 %collective-permute-done.37 = bf16[128,2048]{1,0:T(8,128)(2,1)S(1)} collective-permute-done((bf16[128,2048]{1,0:T(8,128)(2,1)S(1)}, bf16[128,2048]{1,0:T(8,128)(2,1)S(1)}, u32[]{:S(2)}, u32[]{:S(2)}) %collective-permute-start.37) | collective-permute-done | bytes 524320 | tf_op jit(solution)/shard_map/ppermute | solution.py:214
  225.6 4.3 %collective-permute-done.38 = bf16[128,2048]{1,0:T(8,128)(2,1)S(1)} collective-permute-done((bf16[128,2048]{1,0:T(8,128)(2,1)S(1)}, bf16[128,2048]{1,0:T(8,128)(2,1)S(1)}, u32[]{:S(2)}, u32[]{:S(2)}) %collective-permute-start.38) | collective-permute-done | bytes 524320 | tf_op jit(solution)/shard_map/ppermute | solution.py:20
  230.3 2.2 collective-permute-start.42
  232.5 1.7 collective-permute-start.43
  235.1 4.3 %collective-permute-done.41 = bf16[128,2048]{1,0:T(8,128)(2,1)S(1)} collective-permute-done((bf16[128,2048]{1,0:T(8,128)(2,1)S(1)}, bf16[128,2048]{1,0:T(8,128)(2,1)S(1)}, u32[]{:S(2)}, u32[]{:S(2)}) %collective-permute-start.41) | collective-permute-done | bytes 524320 | tf_op jit(solution)/shard_map/ppermute | solution.py:20
  239.4 1.9 collective-permute-done.42
  241.7 1.7 collective-permute-done.44
  (123 shorter events, 42.5 us)
Async XLA Ops:
  0.0 52.4 %collective-permute-start.2 = (bf16[512,2048]{1,0:T(8,128)(2,1)}, bf16[512,2048]{1,0:T(8,128)(2,1)S(1)}, u32[]{:S(2)}, u32[]{:S(2)}) collective-permute-start(bf16[512,2048]{1,0:T(8,128)(2,1)} %own_w.1), channel_id=1, source_target_pairs={{0,1},{1,0},{2,3},{3,2},{4,5},{5,4},{6,7},{7,6},{8,9},{9,8},{10,11... | collective-permute-start | bytes 6291464 | tf_op jit(solution)/shard_map/ppermute | solution.py:326
  17.0 30.0 %collective-permute-start = (bf16[512,512]{1,0:T(8,128)(2,1)}, bf16[512,512]{1,0:T(8,128)(2,1)S(1)}, u32[]{:S(2)}, u32[]{:S(2)}) collective-permute-start(bf16[512,512]{1,0:T(8,128)(2,1)} %stack_keys_values.1.own_ref), channel_id=1, source_target_pairs={{0,2},{2,4},{4,6},{6,8},{8,10},{10,12},{12,14},{14,16},{16,18},{18... | collective-permute-start | bytes 1572872 | tf_op jit(solution)/shard_map/ppermute | solution.py:313
  20.4 27.4 %collective-permute-start.1 = (bf16[512,512]{1,0:T(8,128)(2,1)}, bf16[512,512]{1,0:T(8,128)(2,1)S(1)}, u32[]{:S(2)}, u32[]{:S(2)}) collective-permute-start(bf16[512,512]{1,0:T(8,128)(2,1)} %stack_keys_values.1.own_ref), channel_id=1, source_target_pairs={{2,0},{4,2},{6,4},{8,6},{10,8},{12,10},{14,12},{16,14},{18,16},{20... | collective-permute-start | bytes 1572872 | tf_op jit(solution)/shard_map/ppermute | solution.py:314
  23.6 3.7 %collective-permute-start.5 = (f32[128,16]{0,1:T(8,128)S(1)}, f32[128,16]{0,1:T(8,128)S(1)}, u32[]{:S(2)}, u32[]{:S(2)}) collective-permute-start(f32[128,16]{0,1:T(8,128)S(1)} %select_reduce_fusion), channel_id=1, source_target_pairs={{0,8},{2,10},{4,12},{6,14},{8,0},{10,2},{12,4},{14,6},{16,24},{18,... | collective-permute-start | bytes 24584 | tf_op jit(solution)/shard_map/ppermute | solution.py:20
  27.3 20.5 %copy-start.24 = (f32[128,16]{0,1:T(8,128)}, f32[128,16]{0,1:T(8,128)S(1)}, u32[]{:S(2)}) copy-start(f32[128,16]{0,1:T(8,128)S(1)} %collective-permute-done.5) | copy-start | bytes 24580
  27.3 4.6 %collective-permute-start.6 = (f32[256,16]{0,1:T(8,128)S(1)}, f32[256,16]{0,1:T(8,128)S(1)}, u32[]{:S(2)}, u32[]{:S(2)}) collective-permute-start(f32[256,16]{0,1:T(8,128)S(1)} %pad_maximum_fusion.2), channel_id=1, source_target_pairs={{0,16},{2,18},{4,20},{6,22},{8,24},{10,26},{12,28},{14,30},{16,0},... | collective-permute-start | bytes 49160 | tf_op jit(solution)/shard_map/ppermute | solution.py:20
  29.9 22.5 %collective-permute-start.3 = (bf16[352,2048]{1,0:T(8,128)(2,1)}, bf16[352,2048]{1,0:T(8,128)(2,1)}, u32[]{:S(2)}, u32[]{:S(2)}) collective-permute-start(bf16[352,2048]{1,0:T(8,128)(2,1)} %bitcast.10), channel_id=1, source_target_pairs={{0,1},{1,0},{2,3},{3,2},{4,5},{5,4},{6,7},{7,6},{8,9},{9,8},{10,11... | collective-permute-start | bytes 4325384 | tf_op jit(solution)/shard_map/ppermute | solution.py:328
  31.9 15.9 %copy-start.21 = (f32[256,16]{0,1:T(8,128)}, f32[256,16]{0,1:T(8,128)S(1)}, u32[]{:S(2)}) copy-start(f32[256,16]{0,1:T(8,128)S(1)} %collective-permute-done.6) | copy-start | bytes 49156
  32.0 14.4 %collective-permute-start.7 = (f32[512,16]{0,1:T(8,128)S(1)}, f32[512,16]{0,1:T(8,128)S(1)}, u32[]{:S(2)}, u32[]{:S(2)}) collective-permute-start(f32[512,16]{0,1:T(8,128)S(1)} %pad_maximum_fusion.1), channel_id=1, source_target_pairs={{0,4},{2,6},{4,0},{6,2},{8,12},{10,14},{12,8},{14,10},{16,20},{18,... | collective-permute-start | bytes 98312 | tf_op jit(solution)/shard_map/ppermute | solution.py:20
  48.6 16.6 %collective-permute-start.8 = (bf16[352,2048]{1,0:T(8,128)(2,1)}, bf16[352,2048]{1,0:T(8,128)(2,1)S(1)}, u32[]{:S(2)}, u32[]{:S(2)}) collective-permute-start(bf16[352,2048]{1,0:T(8,128)(2,1)} %bitcast.15), channel_id=1, source_target_pairs={{0,1},{1,0},{2,3},{3,2},{4,5},{5,4},{6,7},{7,6},{8,9},{9,8},{10,11... | collective-permute-start | bytes 4325384 | tf_op jit(solution)/shard_map/ppermute | solution.py:330
  48.6 16.6 %collective-permute-start.9 = (bf16[352,2048]{1,0:T(8,128)(2,1)}, bf16[352,2048]{1,0:T(8,128)(2,1)}, u32[]{:S(2)}, u32[]{:S(2)}) collective-permute-start(bf16[352,2048]{1,0:T(8,128)(2,1)} %bitcast.20), channel_id=1, source_target_pairs={{0,1},{1,0},{2,3},{3,2},{4,5},{5,4},{6,7},{7,6},{8,9},{9,8},{10,11... | collective-permute-start | bytes 4325384 | tf_op jit(solution)/shard_map/ppermute | solution.py:331
  52.4 11.0 %collective-permute-start.10 = (f32[1024,16]{0,1:T(8,128)}, f32[1024,16]{0,1:T(8,128)S(1)}, u32[]{:S(2)}, u32[]{:S(2)}) collective-permute-start(f32[1024,16]{0,1:T(8,128)} %pad_maximum_fusion), channel_id=1, source_target_pairs={{0,2},{2,0},{4,6},{6,4},{8,10},{10,8},{12,14},{14,12},{16,18},{18,... | collective-permute-start | bytes 196616 | tf_op jit(solution)/shard_map/ppermute | solution.py:20
  62.8 2.5 %collective-permute-start.4 = (bf16[128,512]{1,0:T(8,128)(2,1)}, bf16[128,512]{1,0:T(8,128)(2,1)S(1)}, u32[]{:S(2)}, u32[]{:S(2)}) collective-permute-start(bf16[128,512]{1,0:T(8,128)(2,1)} %get-tuple-element.65), channel_id=1, source_target_pairs={{0,1},{1,0},{2,3},{3,2},{4,5},{5,4},{6,7},{7,6},{8,9},{9,8},{10,11... | collective-permute-start | bytes 393224 | tf_op jit(solution)/shard_map/ppermute | solution.py:337
  72.9 14.8 %collective-permute-start.11 = (bf16[128,2048]{1,0:T(8,128)(2,1)S(1)}, bf16[128,2048]{1,0:T(8,128)(2,1)}, u32[]{:S(2)}, u32[]{:S(2)}) collective-permute-start(bf16[128,2048]{1,0:T(8,128)(2,1)S(1)} %get-tuple-element.69.refs_0_), channel_id=1, source_target_pairs={{0,2},{2,0},{4,6},{6,4},{8,10},{10,8},{12,14},{14,12},{16,18},{18,... | collective-permute-start | bytes 1572872 | tf_op jit(solution)/shard_map/ppermute | solution.py:20
  74.9 14.2 %collective-permute-start.12 = (bf16[128,2048]{1,0:T(8,128)(2,1)S(1)}, bf16[128,2048]{1,0:T(8,128)(2,1)}, u32[]{:S(2)}, u32[]{:S(2)}) collective-permute-start(bf16[128,2048]{1,0:T(8,128)(2,1)S(1)} %get-tuple-element.69.refs_0_), channel_id=1, source_target_pairs={{0,4},{2,6},{4,0},{6,2},{8,12},{10,14},{12,8},{14,10},{16,20},{18,... | collective-permute-start | bytes 1572872 | tf_op jit(solution)/shard_map/ppermute | solution.py:20
  74.9 14.2 %collective-permute-start.13 = (bf16[128,2048]{1,0:T(8,128)(2,1)S(1)}, bf16[128,2048]{1,0:T(8,128)(2,1)}, u32[]{:S(2)}, u32[]{:S(2)}) collective-permute-start(bf16[128,2048]{1,0:T(8,128)(2,1)S(1)} %get-tuple-element.69.refs_0_), channel_id=1, source_target_pairs={{0,8},{2,10},{4,12},{6,14},{8,0},{10,2},{12,4},{14,6},{16,24},{18,... | collective-permute-start | bytes 1572872 | tf_op jit(solution)/shard_map/ppermute | solution.py:20
  75.4 16.7 %collective-permute-start.14 = (bf16[128,2048]{1,0:T(8,128)(2,1)S(1)}, bf16[128,2048]{1,0:T(8,128)(2,1)}, u32[]{:S(2)}, u32[]{:S(2)}) collective-permute-start(bf16[128,2048]{1,0:T(8,128)(2,1)S(1)} %get-tuple-element.69.refs_0_), channel_id=1, source_target_pairs={{8,16},{10,18},{12,20},{14,22},{16,8},{18,10},{20,12},{22,14},{9,1... | collective-permute-start | bytes 1572872 | tf_op jit(solution)/shard_map/ppermute | solution.py:214
  92.1 13.6 %collective-permute-start.15 = (bf16[128,2048]{1,0:T(8,128)(2,1)}, bf16[128,2048]{1,0:T(8,128)(2,1)}, u32[]{:S(2)}, u32[]{:S(2)}) collective-permute-start(bf16[128,2048]{1,0:T(8,128)(2,1)} %collective-permute-done.12.refs_2_), channel_id=1, source_target_pairs={{0,2},{2,0},{4,6},{6,4},{8,10},{10,8},{12,14},{14,12},{16,18},{18,... | collective-permute-start | bytes 1572872 | tf_op jit(solution)/shard_map/ppermute | solution.py:20
  92.6 13.1 %collective-permute-start.16 = (bf16[128,2048]{1,0:T(8,128)(2,1)}, bf16[128,2048]{1,0:T(8,128)(2,1)}, u32[]{:S(2)}, u32[]{:S(2)}) collective-permute-start(bf16[128,2048]{1,0:T(8,128)(2,1)} %collective-permute-done.13.refs_0_), channel_id=1, source_target_pairs={{0,4},{2,6},{4,0},{6,2},{8,12},{10,14},{12,8},{14,10},{16,20},{18,... | collective-permute-start | bytes 1572872 | tf_op jit(solution)/shard_map/ppermute | solution.py:20
  94.3 11.6 %collective-permute-start.17 = (bf16[128,2048]{1,0:T(8,128)(2,1)}, bf16[128,2048]{1,0:T(8,128)(2,1)}, u32[]{:S(2)}, u32[]{:S(2)}) collective-permute-start(bf16[128,2048]{1,0:T(8,128)(2,1)} %collective-permute-done.14), channel_id=1, source_target_pairs={{8,0},{10,2},{12,4},{14,6},{16,24},{18,26},{20,28},{22,30},{9,1},{... | collective-permute-start | bytes 1572872 | tf_op jit(solution)/shard_map/ppermute | solution.py:214
  96.4 14.5 %collective-permute-start.18 = (bf16[128,2048]{1,0:T(8,128)(2,1)}, bf16[128,2048]{1,0:T(8,128)(2,1)}, u32[]{:S(2)}, u32[]{:S(2)}) collective-permute-start(bf16[128,2048]{1,0:T(8,128)(2,1)} %collective-permute-done.13.refs_0_), channel_id=1, source_target_pairs={{8,16},{10,18},{12,20},{14,22},{16,8},{18,10},{20,12},{22,14},{9,1... | collective-permute-start | bytes 1572872 | tf_op jit(solution)/shard_map/ppermute | solution.py:214
  99.9 15.8 %copy-start = (bf16[1,2048,352]{1,2,0:T(8,128)(2,1)S(1)}, bf16[1,2048,352]{1,2,0:T(8,128)(2,1)}, u32[]{:S(2)}) copy-start(bf16[1,2048,352]{1,2,0:T(8,128)(2,1)} %param.21) | copy-start | bytes 4325380
  112.0 17.2 %collective-permute-start.20 = (bf16[128,2048]{1,0:T(8,128)(2,1)S(1)}, bf16[128,2048]{1,0:T(8,128)(2,1)S(1)}, u32[]{:S(2)}, u32[]{:S(2)}) collective-permute-start(bf16[128,2048]{1,0:T(8,128)(2,1)S(1)} %broadcast_select_fusion.1.refs_2_), channel_id=1, source_target_pairs={{0,2},{2,0},{4,6},{6,4},{8,10},{10,8},{12,14},{14,12},{16,18},{18,... | collective-permute-start | bytes 1572872 | tf_op jit(solution)/shard_map/ppermute | solution.py:20
  113.7 15.4 %collective-permute-start.21 = (bf16[128,2048]{1,0:T(8,128)(2,1)S(1)}, bf16[128,2048]{1,0:T(8,128)(2,1)S(1)}, u32[]{:S(2)}, u32[]{:S(2)}) collective-permute-start(bf16[128,2048]{1,0:T(8,128)(2,1)S(1)} %broadcast_select_fusion.1.refs_2_), channel_id=1, source_target_pairs={{0,4},{2,6},{4,0},{6,2},{8,12},{10,14},{12,8},{14,10},{16,20},{18,... | collective-permute-start | bytes 1572872 | tf_op jit(solution)/shard_map/ppermute | solution.py:20
  114.3 14.8 %collective-permute-start.19 = (bf16[128,2048]{1,0:T(8,128)(2,1)}, bf16[128,2048]{1,0:T(8,128)(2,1)S(1)}, u32[]{:S(2)}, u32[]{:S(2)}) collective-permute-start(bf16[128,2048]{1,0:T(8,128)(2,1)} %collective-permute-done.18), channel_id=1, source_target_pairs={{8,0},{10,2},{12,4},{14,6},{16,24},{18,26},{20,28},{22,30},{9,1},{... | collective-permute-start | bytes 1572872 | tf_op jit(solution)/shard_map/ppermute | solution.py:214
  130.4 14.2 %collective-permute-start.22 = (bf16[128,2048]{1,0:T(8,128)(2,1)S(1)}, bf16[128,2048]{1,0:T(8,128)(2,1)S(1)}, u32[]{:S(2)}, u32[]{:S(2)}) collective-permute-start(bf16[128,2048]{1,0:T(8,128)(2,1)S(1)} %broadcast_select_fusion.refs_5_), channel_id=1, source_target_pairs={{0,2},{2,0},{4,6},{6,4},{8,10},{10,8},{12,14},{14,12},{16,18},{18,... | collective-permute-start | bytes 1572872 | tf_op jit(solution)/shard_map/ppermute | solution.py:20
  130.9 13.7 %collective-permute-start.23 = (bf16[128,2048]{1,0:T(8,128)(2,1)S(1)}, bf16[128,2048]{1,0:T(8,128)(2,1)S(1)}, u32[]{:S(2)}, u32[]{:S(2)}) collective-permute-start(bf16[128,2048]{1,0:T(8,128)(2,1)S(1)} %broadcast_select_fusion.refs_5_), channel_id=1, source_target_pairs={{0,4},{2,6},{4,0},{6,2},{8,12},{10,14},{12,8},{14,10},{16,20},{18,... | collective-permute-start | bytes 1572872 | tf_op jit(solution)/shard_map/ppermute | solution.py:20
  132.2 12.4 %collective-permute-start.24 = (bf16[128,2048]{1,0:T(8,128)(2,1)}, bf16[128,2048]{1,0:T(8,128)(2,1)S(1)}, u32[]{:S(2)}, u32[]{:S(2)}) collective-permute-start(bf16[128,2048]{1,0:T(8,128)(2,1)} %collective-permute-done.11.refs_1_), channel_id=1, source_target_pairs={{0,8},{2,10},{4,12},{6,14},{8,0},{10,2},{12,4},{14,6},{16,24},{18,... | collective-permute-start | bytes 1572872 | tf_op jit(solution)/shard_map/ppermute | solution.py:20
  144.6 11.0 %collective-permute-start.25 = (bf16[128,2048]{1,0:T(8,128)(2,1)S(1)}, bf16[128,2048]{1,0:T(8,128)(2,1)S(1)}, u32[]{:S(2)}, u32[]{:S(2)}) collective-permute-start(bf16[128,2048]{1,0:T(8,128)(2,1)S(1)} %collective-permute-done.21.refs_4_), channel_id=1, source_target_pairs={{0,2},{2,0},{4,6},{6,4},{8,10},{10,8},{12,14},{14,12},{16,18},{18,... | collective-permute-start | bytes 1572872 | tf_op jit(solution)/shard_map/ppermute | solution.py:20
  146.3 10.0 %collective-permute-start.26 = (bf16[128,2048]{1,0:T(8,128)(2,1)S(1)}, bf16[128,2048]{1,0:T(8,128)(2,1)S(1)}, u32[]{:S(2)}, u32[]{:S(2)}) collective-permute-start(bf16[128,2048]{1,0:T(8,128)(2,1)S(1)} %collective-permute-done.22.refs_0_), channel_id=1, source_target_pairs={{0,4},{2,6},{4,0},{6,2},{8,12},{10,14},{12,8},{14,10},{16,20},{18,... | collective-permute-start | bytes 1572872 | tf_op jit(solution)/shard_map/ppermute | solution.py:20
  146.9 10.3 %collective-permute-start.27 = (bf16[128,2048]{1,0:T(8,128)(2,1)}, bf16[128,2048]{1,0:T(8,128)(2,1)S(1)}, u32[]{:S(2)}, u32[]{:S(2)}) collective-permute-start(bf16[128,2048]{1,0:T(8,128)(2,1)} %collective-permute-done.15.refs_3_), channel_id=1, source_target_pairs={{0,8},{2,10},{4,12},{6,14},{8,0},{10,2},{12,4},{14,6},{16,24},{18,... | collective-permute-start | bytes 1572872 | tf_op jit(solution)/shard_map/ppermute | solution.py:20
  163.9 9.9 %collective-permute-start.28 = (bf16[128,2048]{1,0:T(8,128)(2,1)S(1)}, bf16[128,2048]{1,0:T(8,128)(2,1)S(1)}, u32[]{:S(2)}, u32[]{:S(2)}) collective-permute-start(bf16[128,2048]{1,0:T(8,128)(2,1)S(1)} %get-tuple-element.95), channel_id=1, source_target_pairs={{0,4},{2,6},{4,0},{6,2},{8,12},{10,14},{12,8},{14,10},{16,20},{18,... | collective-permute-start | bytes 1572872 | tf_op jit(solution)/shard_map/ppermute | solution.py:20
  165.1 11.7 %collective-permute-start.30 = (bf16[128,2048]{1,0:T(8,128)(2,1)S(1)}, bf16[128,2048]{1,0:T(8,128)(2,1)S(1)}, u32[]{:S(2)}, u32[]{:S(2)}) collective-permute-start(bf16[128,2048]{1,0:T(8,128)(2,1)S(1)} %get-tuple-element.101), channel_id=1, source_target_pairs={{0,8},{2,10},{4,12},{6,14},{8,0},{10,2},{12,4},{14,6},{16,24},{18,... | collective-permute-start | bytes 1572872 | tf_op jit(solution)/shard_map/ppermute | solution.py:20
  166.8 12.7 %collective-permute-start.29 = (bf16[128,2048]{1,0:T(8,128)(2,1)S(1)}, bf16[128,2048]{1,0:T(8,128)(2,1)S(1)}, u32[]{:S(2)}, u32[]{:S(2)}) collective-permute-start(bf16[128,2048]{1,0:T(8,128)(2,1)S(1)} %get-tuple-element.99), channel_id=1, source_target_pairs={{0,2},{2,0},{4,6},{6,4},{8,10},{10,8},{12,14},{14,12},{16,18},{18,... | collective-permute-start | bytes 1572872 | tf_op jit(solution)/shard_map/ppermute | solution.py:20
  179.7 11.1 %collective-permute-start.33 = (bf16[128,2048]{1,0:T(8,128)(2,1)S(1)}, bf16[128,2048]{1,0:T(8,128)(2,1)S(1)}, u32[]{:S(2)}, u32[]{:S(2)}) collective-permute-start(bf16[128,2048]{1,0:T(8,128)(2,1)S(1)} %get-tuple-element.105), channel_id=1, source_target_pairs={{0,8},{2,10},{4,12},{6,14},{8,0},{10,2},{12,4},{14,6},{16,24},{18,... | collective-permute-start | bytes 1572872 | tf_op jit(solution)/shard_map/ppermute | solution.py:20
  179.8 13.9 %collective-permute-start.31 = (bf16[128,2048]{1,0:T(8,128)(2,1)S(1)}, bf16[128,2048]{1,0:T(8,128)(2,1)S(1)}, u32[]{:S(2)}, u32[]{:S(2)}) collective-permute-start(bf16[128,2048]{1,0:T(8,128)(2,1)S(1)} %add_convert_fusion.9), channel_id=1, source_target_pairs={{0,2},{2,0},{4,6},{6,4},{8,10},{10,8},{12,14},{14,12},{16,18},{18,... | collective-permute-start | bytes 1572872 | tf_op jit(solution)/shard_map/ppermute | solution.py:20
  180.2 14.2 %collective-permute-start.32 = (bf16[128,2048]{1,0:T(8,128)(2,1)S(1)}, bf16[128,2048]{1,0:T(8,128)(2,1)S(1)}, u32[]{:S(2)}, u32[]{:S(2)}) collective-permute-start(bf16[128,2048]{1,0:T(8,128)(2,1)S(1)} %get-tuple-element.103), channel_id=1, source_target_pairs={{0,4},{2,6},{4,0},{6,2},{8,12},{10,14},{12,8},{14,10},{16,20},{18,... | collective-permute-start | bytes 1572872 | tf_op jit(solution)/shard_map/ppermute | solution.py:20
  194.6 14.0 %collective-permute-start.34 = (bf16[128,2048]{1,0:T(8,128)(2,1)S(1)}, bf16[128,2048]{1,0:T(8,128)(2,1)S(1)}, u32[]{:S(2)}, u32[]{:S(2)}) collective-permute-start(bf16[128,2048]{1,0:T(8,128)(2,1)S(1)} %get-tuple-element.110), channel_id=1, source_target_pairs={{0,2},{2,0},{4,6},{6,4},{8,10},{10,8},{12,14},{14,12},{16,18},{18,... | collective-permute-start | bytes 1572872 | tf_op jit(solution)/shard_map/ppermute | solution.py:20
  196.3 12.3 %collective-permute-start.35 = (bf16[128,2048]{1,0:T(8,128)(2,1)S(1)}, bf16[128,2048]{1,0:T(8,128)(2,1)S(1)}, u32[]{:S(2)}, u32[]{:S(2)}) collective-permute-start(bf16[128,2048]{1,0:T(8,128)(2,1)S(1)} %add_convert_fusion.8), channel_id=1, source_target_pairs={{0,4},{2,6},{4,0},{6,2},{8,12},{10,14},{12,8},{14,10},{16,20},{18,... | collective-permute-start | bytes 1572872 | tf_op jit(solution)/shard_map/ppermute | solution.py:20
  196.6 14.3 %collective-permute-start.36 = (bf16[128,2048]{1,0:T(8,128)(2,1)S(1)}, bf16[128,2048]{1,0:T(8,128)(2,1)S(1)}, u32[]{:S(2)}, u32[]{:S(2)}) collective-permute-start(bf16[128,2048]{1,0:T(8,128)(2,1)S(1)} %add_convert_fusion.6), channel_id=1, source_target_pairs={{0,8},{2,10},{4,12},{6,14},{24,16},{26,18},{28,20},{30,22},{1,9},{... | collective-permute-start | bytes 1572872 | tf_op jit(solution)/shard_map/ppermute | solution.py:214
  211.2 13.9 %collective-permute-start.37 = (bf16[128,2048]{1,0:T(8,128)(2,1)S(1)}, bf16[128,2048]{1,0:T(8,128)(2,1)S(1)}, u32[]{:S(2)}, u32[]{:S(2)}) collective-permute-start(bf16[128,2048]{1,0:T(8,128)(2,1)S(1)} %add_convert_fusion.4), channel_id=1, source_target_pairs={{0,8},{2,10},{4,12},{6,14},{24,16},{26,18},{28,20},{30,22},{1,9},{... | collective-permute-start | bytes 1572872 | tf_op jit(solution)/shard_map/ppermute | solution.py:214
  212.5 13.0 %collective-permute-start.40 = (bf16[128,2048]{1,0:T(8,128)(2,1)S(1)}, bf16[128,2048]{1,0:T(8,128)(2,1)S(1)}, u32[]{:S(2)}, u32[]{:S(2)}) collective-permute-start(bf16[128,2048]{1,0:T(8,128)(2,1)S(1)} %add_convert_fusion.7), channel_id=1, source_target_pairs={{0,2},{2,0},{4,6},{6,4},{8,10},{10,8},{12,14},{14,12},{16,18},{18,... | collective-permute-start | bytes 1572872 | tf_op jit(solution)/shard_map/ppermute | solution.py:20
  214.3 15.7 %collective-permute-start.39 = (bf16[128,2048]{1,0:T(8,128)(2,1)S(1)}, bf16[128,2048]{1,0:T(8,128)(2,1)S(1)}, u32[]{:S(2)}, u32[]{:S(2)}) collective-permute-start(bf16[128,2048]{1,0:T(8,128)(2,1)S(1)} %add_convert_fusion.4), channel_id=1, source_target_pairs={{8,16},{10,18},{12,20},{14,22},{16,8},{18,10},{20,12},{22,14},{9,1... | collective-permute-start | bytes 1572872 | tf_op jit(solution)/shard_map/ppermute | solution.py:214
  217.6 12.3 %collective-permute-start.38 = (bf16[128,2048]{1,0:T(8,128)(2,1)S(1)}, bf16[128,2048]{1,0:T(8,128)(2,1)S(1)}, u32[]{:S(2)}, u32[]{:S(2)}) collective-permute-start(bf16[128,2048]{1,0:T(8,128)(2,1)S(1)} %get-tuple-element.115), channel_id=1, source_target_pairs={{0,4},{2,6},{4,0},{6,2},{8,12},{10,14},{12,8},{14,10},{16,20},{18,... | collective-permute-start | bytes 1572872 | tf_op jit(solution)/shard_map/ppermute | solution.py:20
  230.2 9.2 %collective-permute-start.41 = (bf16[128,2048]{1,0:T(8,128)(2,1)S(1)}, bf16[128,2048]{1,0:T(8,128)(2,1)S(1)}, u32[]{:S(2)}, u32[]{:S(2)}) collective-permute-start(bf16[128,2048]{1,0:T(8,128)(2,1)S(1)} %add_convert_fusion.2), channel_id=1, source_target_pairs={{0,8},{2,10},{4,12},{6,14},{8,0},{10,2},{12,4},{14,6},{16,24},{18,... | collective-permute-start | bytes 1572872 | tf_op jit(solution)/shard_map/ppermute | solution.py:20
  230.3 11.1 %collective-permute-start.42 = (bf16[128,2048]{1,0:T(8,128)(2,1)S(1)}, bf16[128,2048]{1,0:T(8,128)(2,1)S(1)}, u32[]{:S(2)}, u32[]{:S(2)}) collective-permute-start(bf16[128,2048]{1,0:T(8,128)(2,1)S(1)} %add_convert_fusion.3), channel_id=1, source_target_pairs={{8,16},{10,18},{12,20},{14,22},{16,8},{18,10},{20,12},{22,14},{9,1... | collective-permute-start | bytes 1572872 | tf_op jit(solution)/shard_map/ppermute | solution.py:214
  232.5 9.2 %collective-permute-start.43 = (bf16[128,2048]{1,0:T(8,128)(2,1)S(1)}, bf16[128,2048]{1,0:T(8,128)(2,1)S(1)}, u32[]{:S(2)}, u32[]{:S(2)}) collective-permute-start(bf16[128,2048]{1,0:T(8,128)(2,1)S(1)} %add_convert_fusion.5), channel_id=1, source_target_pairs={{0,2},{2,0},{4,6},{6,4},{8,10},{10,8},{12,14},{14,12},{16,18},{18,... | collective-permute-start | bytes 1572872 | tf_op jit(solution)/shard_map/ppermute | solution.py:20
  234.2 9.2 %collective-permute-start.44 = (bf16[128,2048]{1,0:T(8,128)(2,1)S(1)}, bf16[128,2048]{1,0:T(8,128)(2,1)S(1)}, u32[]{:S(2)}, u32[]{:S(2)}) collective-permute-start(bf16[128,2048]{1,0:T(8,128)(2,1)S(1)} %add_convert_fusion.1), channel_id=1, source_target_pairs={{0,4},{2,6},{4,0},{6,2},{8,12},{10,14},{12,8},{14,10},{16,20},{18,... | collective-permute-start | bytes 1572872 | tf_op jit(solution)/shard_map/ppermute | solution.py:20
  (22 other events, 47.4 us)

commit v6 on v5

v6 whole, which is shorter than its diff:
```python
import functools
import math

import jax
import jax.numpy as jnp
from jax import lax
from jax.experimental import pallas as pl
from jax.experimental.pallas import tpu as pltpu
from jax.sharding import PartitionSpec as P

HD = 128
SWAP = [(0, 1), (1, 0)]
VMEM = pl.BlockSpec(memory_space=pltpu.VMEM)
ANY = pl.BlockSpec(memory_space=pl.ANY)
NT = (((1,), (1,)), ((), ()))


def flip(block, mask):
    count = lax.axis_size("seq")
    return lax.ppermute(block, "seq", [(i, i ^ mask) for i in range(count)])


def after(block, *arrays):
    return lax.optimization_barrier((block, *arrays))[0]


def gate_order(count):
    masks = [1 << bit for bit in range(count.bit_length() - 1)]
    return masks[2:] + masks[1::-1]


def gather_gates(block):
    pieces = [block]
    for mask in gate_order(lax.axis_size("seq")):
        pieces.append(flip(block, mask))
        block = jnp.concatenate([block, pieces[-1]], axis=1)
    return pieces


def place_of(j):
    return sum(1 << bit for bit, mask in enumerate(gate_order(lax.axis_size("seq"))) if j & mask)


def stack_kernel(keys_ref, values_ref, out_ref):
    rows = keys_ref.shape[0]
    out_ref[:rows] = keys_ref[...]
    out_ref[rows:] = values_ref[...]


def stack(keys, values):
    rows, width = keys.shape
    return pl.pallas_call(
        stack_kernel,
        out_shape=jax.ShapeDtypeStruct((2 * rows, width), keys.dtype),
        in_specs=[VMEM, VMEM],
        out_specs=VMEM,
        compiler_params=pltpu.CompilerParams(vmem_limit_bytes=63 * 1024 * 1024),
        name="stack_keys_values",
    )(keys, values)


def attention_kernel(core_ref, q_ref, before_ref, own_ref, after_ref, ids_ref, *refs):
    theirs_ref, mine_ref, both = refs[-3:]
    rows = q_ref.shape[0]
    some = rows // 2
    scale = 1.0 / math.sqrt(HD)
    column = jnp.transpose(jnp.broadcast_to(ids_ref[:, rows : 2 * rows], (HD, rows)))[:, :1]
    for half in range(2):
        first = half * some
        spans = [
            (before_ref, half * some, rows),
            (own_ref, 0, rows),
            (after_ref, 0, some + half * some),
        ]
        keys = 2 * rows + some
        query_pos = lax.broadcasted_iota(jnp.int32, (some, keys), 0) + (first + rows)
        key_pos = lax.broadcasted_iota(jnp.int32, (some, keys), 1) + first
        allowed = (column[first : first + some] == ids_ref[:, first : first + keys]) & (
            jnp.abs(query_pos - key_pos) < rows
        )
        for head in range(q_ref.shape[1] // HD):
            cols = slice(head * HD, (head + 1) * HD)
            query = q_ref[first : first + some, cols]
            score = jnp.concatenate(
                [
                    lax.dot_general(query, ref[lo:hi, cols], NT, preferred_element_type=jnp.float32)
                    for ref, lo, hi in spans
                ],
                axis=1,
            )
            score = jnp.where(allowed, score * scale, -jnp.inf)
            weights = jnp.exp(score - jnp.max(score, axis=-1, keepdims=True))
            share = 1.0 / jnp.sum(weights, axis=-1, keepdims=True)
            probs = (weights * share).astype(jnp.bfloat16)
            total, at = jnp.zeros((some, HD), jnp.float32), 0
            for ref, lo, hi in spans:
                total += jnp.dot(
                    probs[:, at : at + hi - lo],
                    ref[rows + lo : rows + hi, cols],
                    preferred_element_type=jnp.float32,
                )
                at += hi - lo
            both[first : first + some, cols] = total.astype(jnp.bfloat16)
    at = pl.multiple_of(core_ref[0] * some, some)
    mine_ref[...] = both[pl.ds(at, some), :]
    theirs_ref[...] = both[pl.ds(some - at, some), :]


def attention(core, queries, near, ids, *ahead):
    rows, width = queries.shape
    half = jax.ShapeDtypeStruct((rows // 2, width), jnp.bfloat16)
    return pl.pallas_call(
        attention_kernel,
        out_shape=(half, half),
        in_specs=[pl.BlockSpec(memory_space=pltpu.SMEM)] + [VMEM] * 5 + [ANY] * len(ahead),
        out_specs=(VMEM, VMEM),
        scratch_shapes=[pltpu.VMEM((rows, width), jnp.bfloat16)],
        compiler_params=pltpu.CompilerParams(vmem_limit_bytes=63 * 1024 * 1024),
        name="window_attention",
    )(core, queries, *near, ids, *ahead)


def norm_kernel(mine_ref, theirs_ref, own_w, other_w, resid_ref, gain_ref, *refs):
    stream_ref, normed_ref = refs[-2:]
    stream = resid_ref[...].astype(jnp.float32)
    stream += jnp.dot(mine_ref[...], own_w[...], preferred_element_type=jnp.float32)
    stream += jnp.dot(theirs_ref[...], other_w[...], preferred_element_type=jnp.float32)
    meansq = jnp.mean(stream * stream, axis=-1, keepdims=True)
    stream_ref[...] = stream
    normed_ref[...] = (stream * lax.rsqrt(meansq + 1e-05) * gain_ref[...]).astype(jnp.bfloat16)


def project_and_norm(mine, theirs, own_w, other_w, resid, gain, *ahead):
    rows, width = resid.shape
    return pl.pallas_call(
        norm_kernel,
        out_shape=(
            jax.ShapeDtypeStruct((rows, width), jnp.float32),
            jax.ShapeDtypeStruct((rows, width), jnp.bfloat16),
        ),
        in_specs=[VMEM] * 6 + [ANY] * len(ahead),
        out_specs=(VMEM, VMEM),
        compiler_params=pltpu.CompilerParams(vmem_limit_bytes=63 * 1024 * 1024),
        name="project_and_norm",
    )(mine, theirs, own_w, other_w, resid, gain, *ahead)


def assemble_kernel(*refs):
    halves, (gate_up, down, sems) = refs[:6], refs[6:]
    units = halves[0].shape[0]
    copies = []
    for i, half in enumerate(halves):
        target, at = (gate_up, i * units) if i < 4 else (down, (i - 4) * units)
        copies.append(pltpu.make_async_copy(half, target.at[pl.ds(at, units), :], sems.at[i]))
    for copy in copies:
        copy.start()
    for copy in copies:
        copy.wait()


def assemble(halves):
    units, width = halves[0].shape
    return pl.pallas_call(
        assemble_kernel,
        out_shape=(
            jax.ShapeDtypeStruct((4 * units, width), jnp.bfloat16),
            jax.ShapeDtypeStruct((2 * units, width), jnp.bfloat16),
        ),
        in_specs=[ANY] * 6,
        out_specs=(VMEM, VMEM),
        scratch_shapes=[pltpu.SemaphoreType.DMA((6,))],
        compiler_params=pltpu.CompilerParams(vmem_limit_bytes=36 * 1024 * 1024),
        name="assemble_weights",
    )(*halves)


def expert_kernel(places, pieces, shard_ref, *refs):
    count = len(places)
    blocks, gates, (gate_up, down) = refs[:count], refs[count : count + pieces], refs[count + pieces :][:2]
    outs = refs[count + pieces + 2 :]
    units = down.shape[0]
    rows = blocks[0].shape[0]
    for first in range(0, count, 2):
        group = range(first, min(first + 2, count))
        tokens = jnp.concatenate([blocks[i][...] for i in group], axis=0)
        gate = lax.dot_general(tokens, gate_up[:units, :], NT, preferred_element_type=jnp.float32)
        up = lax.dot_general(tokens, gate_up[units:, :], NT, preferred_element_type=jnp.float32)
        act = (gate / (1.0 + jnp.exp(-gate)) * up).astype(jnp.bfloat16)
        result = jnp.dot(act, down[...], preferred_element_type=jnp.float32)
        for i in group:
            piece = places[i].bit_length()
            at = (places[i] - (1 << piece >> 1)) * rows
            here = gates[piece][:, at : at + rows]
            expert = lax.broadcasted_iota(jnp.int32, here.shape, 0)
            chosen = jnp.sum(jnp.where(expert == shard_ref[0], here, 0.0), axis=0, keepdims=True)
            chosen = jnp.transpose(jnp.broadcast_to(chosen, (rows, rows)))[:, :1]
            part = result[(i - first) * rows : (i - first + 1) * rows]
            outs[i][...] = (part * chosen).astype(jnp.bfloat16)


def expert(blocks, places, shard, gates, weights):
    rows, width = blocks[0].shape
    count = len(blocks)
    return pl.pallas_call(
        functools.partial(expert_kernel, places, len(gates)),
        out_shape=[jax.ShapeDtypeStruct((rows, width), jnp.bfloat16)] * count,
        in_specs=[pl.BlockSpec(memory_space=pltpu.SMEM)] + [VMEM] * (count + len(gates) + 2),
        out_specs=[VMEM] * count,
        compiler_params=pltpu.CompilerParams(vmem_limit_bytes=36 * 1024 * 1024),
        name="expert_rows",
    )(shard, *blocks, *gates, *weights)


def add(*terms):
    total = terms[0].astype(jnp.float32)
    for term in terms[1:]:
        total = total + term.astype(jnp.float32)
    return total


def add_small(*terms):
    return add(*terms).astype(jnp.bfloat16)


def shift(block, pairs):
    return lax.ppermute(block, "seq", [(4 * a + i, 4 * b + i) for a, b in pairs for i in range(4)])


OUTWARD, INWARD, MIDDLE = [(1, 0), (2, 3)], [(0, 1), (3, 2)], [(1, 2), (2, 1)]


def step_layer(normed, stream, run, weights):
    z = lax.axis_index("seq") // 4
    inner = (z == 1) | (z == 2)

    o0 = normed
    o1, near3, x0, y0 = flip(o0, 4), shift(o0, MIDDLE), flip(o0, 1), flip(o0, 2)

    ends2, near2 = shift(after(near3, o1), OUTWARD), shift(after(o1, near3), MIDDLE)
    d0, y1 = flip(after(y0, x0), 1), flip(after(o1, y0), 2)

    ends3 = shift(after(near2, ends2), OUTWARD)
    o2 = jnp.where(inner, near2, ends2)
    x2, y2 = flip(after(o2, d0, weights[0]), 1), flip(after(o2, y1, weights[0]), 2)
    p0, px0, py0, pd0 = run([after(o0, o2), x0, y0, d0], (0, 1, 2, 3))

    x1 = flip(after(x0, ends3, p0), 4)
    o3 = jnp.where(inner, near3, ends3)
    x3, y3 = flip(after(o3, x2, p0), 1), flip(after(o3, y2, p0), 2)
    p1, py1, p2, px2, py2, p3 = run([after(o1, p0), y1, o2, x2, y2, o3], (4, 6, 8, 9, 10, 12))

    d1 = flip(after(d0, x1, p1), 4)
    d2, d3 = flip(after(y2, x3, p1), 1), flip(after(x3, y3, p1), 2)
    px3, py3, px1 = run([after(x3, p1), y3, x1], (13, 14, 5))

    pd2, pd3 = run([after(d2, px3), d3], (11, 15))
    (pd1,) = run([after(d1, pd2)], (7,))
    to_x3, to_y2, to_d0 = flip(pd3, 2), flip(pd2, 1), flip(pd1, 4)

    px3, py2, pd0 = add_small(px3, to_x3), add_small(py2, to_y2), add_small(pd0, to_d0)
    by_x, by_y = flip(after(px3, to_y2), 1), flip(after(py3, to_x3), 2)
    to_x0 = flip(after(px1, to_d0), 4)

    p3, px0 = add_small(p3, by_x, by_y), add_small(px0, to_x0)
    to_2 = shift(after(p3, to_x0), INWARD)
    by_x, by_y = flip(after(px2, by_x), 1), flip(after(py2, by_y), 2)

    p2 = add_small(p2, by_x, by_y, to_2)
    to_3, to_1 = shift(after(p2, to_2), INWARD), shift(p2, MIDDLE)
    to_y0, by_y = flip(after(pd0, by_x), 1), flip(after(py1, by_y), 2)

    p3, p1, py0 = add_small(p3, to_3), add_small(p1, by_y, to_1), add_small(py0, to_y0)
    by_z, by_middle = flip(after(p1, to_3), 4), shift(after(p3, to_1), MIDDLE)
    by_x, by_y = flip(after(px0, to_y0), 1), flip(after(py0, by_y), 2)
    return add(stream, p0, by_z, by_middle, by_x, by_y)


def expert_layer(normed, stream, shard, gates, weights):
    count = lax.axis_size("seq")

    def run(blocks, masks):
        places = tuple(place_of(mask) for mask in masks)
        return expert(blocks, places, shard, gates, weights)

    if count == 16:
        return step_layer(normed, stream, run, weights)
    blocks, mask = [normed], 1
    while mask < count:
        blocks = blocks + [flip(block, mask) for block in blocks]
        mask *= 2
    parts = []
    for first in range(0, count, 4):
        parts += run(blocks[first : first + 4], range(first, first + 4))
    while mask > 1:
        mask //= 2
        parts = [add_small(parts[i], flip(parts[i + mask], mask)) for i in range(mask)]
    return add(stream, parts[0])


def shards(
    queries,
    keys,
    values,
    resid,
    pair_ids,
    out_weight,
    norm_gain,
    experts,
    gates,
    w_gate,
    w_up,
    w_down,
):
    tok_rows = queries.shape[0]
    moe_rows = resid.shape[0]
    shard = lax.axis_index("seq")
    core = lax.axis_index("exp")
    count = lax.axis_size("seq")

    own = stack(keys, values)
    before = lax.ppermute(own, "seq", [(i, i + 1) for i in range(count - 1)])
    after_own = lax.ppermute(own, "seq", [(i + 1, i) for i in range(count - 1)])
    chosen = experts.T[:, None, :] == jnp.arange(count, dtype=jnp.int32)[None, :, None]
    all_gates = gather_gates(jnp.sum(jnp.where(chosen, gates.T[:, None, :], 0.0), axis=0))
    some_gates = all_gates[-2]
    id_pad = jnp.pad(pair_ids, (tok_rows, tok_rows), constant_values=-1)
    ids = lax.dynamic_slice_in_dim(id_pad, shard * tok_rows, 3 * tok_rows, 0)[None, :]
    out_other = lax.ppermute(out_weight, "exp", SWAP)
    gate_w, up_w = jnp.swapaxes(w_gate[0], 0, 1), jnp.swapaxes(w_up[0], 0, 1)
    gate_other = lax.ppermute(gate_w, "exp", SWAP)
    ready = (before, after_own, some_gates, ids)
    up_other = lax.ppermute(after(up_w, *ready), "exp", SWAP)
    down_other = lax.ppermute(after(w_down[0], *ready), "exp", SWAP)
    halves = [gate_w, gate_other, up_w, up_other, w_down[0], down_other]

    theirs, mine = attention(
        core.reshape(1), queries, (before, own, after_own), ids, out_other, gate_other
    )
    received = lax.ppermute(theirs, "exp", SWAP)
    ahead = (up_other, down_other, all_gates[-1])
    stream, normed = project_and_norm(
        mine, received, out_weight, out_other, resid, norm_gain[None, :], *ahead
    )
    mixed = expert_layer(normed, stream, shard.reshape(1), all_gates, assemble(halves))
    return mixed.astype(jnp.bfloat16)


def solution(mesh):
    in_specs = (
        P("seq", "exp"),
        P("seq", "exp"),
        P("seq", "exp"),
        P(("seq", "exp"), None),
        P(),
        P("exp", None),
        P(),
        P(("seq", "exp"), None),
        P(("seq", "exp"), None),
        P("seq", None, "exp"),
        P("seq", None, "exp"),
        P("seq", "exp", None),
    )
    out_specs = P(("seq", "exp"), None)
    return jax.shard_map(shards, mesh=mesh, in_specs=in_specs, out_specs=out_specs, check_vma=False)
```

time: 247 us -> 201 us (0.81)
  Pallas kernels: 58.4 us -> 37 us
  local copies, waits for them, and re-layouts: 24.4 us -> 6.38 us
  waiting for transfers between devices: 93 us -> 90 us
    unnamed x54 -> x18, local copies, waits for them, and re-layouts: 21.8 us -> 5.01 us
    pallas_call x1, Pallas kernels: 17 us -> 1.86 us  [stack(): pl.pallas_call(stack_kernel, out_shape=jax.ShapeDtypeStruct((2 * rows, wi...]
    pallas_call x4 -> x6, Pallas kernels: 35.2 us -> 25.3 us  [the longest x5 22.7 us: expert(): pl.pallas_call(functools.partial(expert_kernel, places, len(gates)), out_...]
    ppermute x30, waiting for transfers between devices: 73.7 us -> 68.2 us  [flip(): return lax.ppermute(block, 'seq', [(i, i ^ mask) for i in range(count)])]
    ppermute x30, starting transfers between devices: 35.7 us -> 31.9 us  [flip(): return lax.ppermute(block, 'seq', [(i, i ^ mask) for i in range(count)])]
    pallas_call x1, Pallas kernels: 0.88 us -> 4.29 us  [project_and_norm(): pl.pallas_call(norm_kernel, out_shape=(jax.ShapeDtypeStruct((rows, width)...]
  transfers between devices with their start and end apart: 45 -> 45, of which waited for: 26 -> 27; matrix products, arithmetic and copies ran while one was open for 3% -> 3% of each run, Pallas kernels for 21% -> 16%
where the time goes in v6:
time: 201 us; the launch traced here: 199 us
  waiting for transfers between devices  90 us (45%)
  starting transfers between devices  59.9 us (30%)
  Pallas kernels  37 us (18%)
  local copies, waits for them, and re-layouts  6.38 us (3%)
  other arithmetic  5.77 us (3%)
    ppermute x30, waiting for transfers between devices, flip(): return lax.ppermute(block, 'seq', [(i, i ^ mask) for i in range(count)])  68.2 us
    ppermute x30, starting transfers between devices, flip(): return lax.ppermute(block, 'seq', [(i, i ^ mask) for i in range(count)])  31.9 us
    pallas_call x5, Pallas kernels, expert(): pl.pallas_call(functools.partial(expert_kernel, places, len(gates)), out_...  22.7 us
    ppermute x8, waiting for transfers between devices, shift(): lax.ppermute(block, 'seq', [(4 * a + i, 4 * b + i) for a, b in pairs for...  21.7 us
    ppermute x8, starting transfers between devices, shift(): lax.ppermute(block, 'seq', [(4 * a + i, 4 * b + i) for a, b in pairs for...  21.5 us
    pallas_call x1, Pallas kernels, attention(): pl.pallas_call(attention_kernel, out_shape=(half, half), in_specs=[pl.Blo...  5.5 us
    unnamed x18, local copies, waits for them, and re-layouts  5.01 us
    pallas_call x1, Pallas kernels, project_and_norm(): pl.pallas_call(norm_kernel, out_shape=(jax.ShapeDtypeStruct((rows, width)...  4.29 us
  transfers between devices with their start and end apart: 45, of which 27 were waited for; matrix products, arithmetic and copies ran while one was open for 3% of the time, Pallas kernels for 16%

profile of v6, /device:TPU:10, one launch (start us, length us, event | category | flops | bytes accessed | tf_op | source)
XLA Modules:
  0.0 199.3 jit_solution(7776369564060662042)
XLA Ops:
  0.0 1.9 stack_keys_values.1.own_ref
  1.9 3.4 %collective-permute-start = (bf16[512,512]{1,0:T(8,128)(2,1)}, bf16[512,512]{1,0:T(8,128)(2,1)S(1)}, u32[]{:S(2)}, u32[]{:S(2)}) collective-permute-start(bf16[512,512]{1,0:T(8,128)(2,1)} %stack_keys_values.1.own_ref), channel_id=1, source_target_pairs={{0,2},{2,4},{4,6},{6,8},{8,10},{10,12},{12,14},{14,16},{16,18},{18... | collective-permute-start | bytes 1572872 | tf_op jit(solution)/shard_map/ppermute | solution.py:321
  5.3 2.4 %collective-permute-start.1 = (bf16[512,512]{1,0:T(8,128)(2,1)}, bf16[512,512]{1,0:T(8,128)(2,1)}, u32[]{:S(2)}, u32[]{:S(2)}) collective-permute-start(bf16[512,512]{1,0:T(8,128)(2,1)} %stack_keys_values.1.own_ref), channel_id=1, source_target_pairs={{2,0},{4,2},{6,4},{8,6},{10,8},{12,10},{14,12},{16,14},{18,16},{20... | collective-permute-start | bytes 1572872 | tf_op jit(solution)/shard_map/ppermute | solution.py:322
  9.0 3.2 %collective-permute-done.5.refs_5_.refs_7_.refs_4_.refs_3_.refs_2_ = f32[16,128]{1,0:T(8,128)S(1)} collective-permute-done((f32[16,128]{1,0:T(8,128)S(1)}, f32[16,128]{1,0:T(8,128)S(1)}, u32[]{:S(2)}, u32[]{:S(2)}) %collective-permute-start.5) | collective-permute-done | bytes 8224 | tf_op jit(solution)/shard_map/ppermute | solution.py:20
  12.1 2.6 %collective-permute-start.6 = (f32[16,256]{1,0:T(8,128)S(1)}, f32[16,256]{1,0:T(8,128)S(1)}, u32[]{:S(2)}, u32[]{:S(2)}) collective-permute-start(f32[16,256]{1,0:T(8,128)S(1)} %pad_maximum_fusion.2), channel_id=1, source_target_pairs={{0,16},{2,18},{4,20},{6,22},{8,24},{10,26},{12,28},{14,30},{16,0},... | collective-permute-start | bytes 49160 | tf_op jit(solution)/shard_map/ppermute | solution.py:20
  14.7 2.0 %collective-permute-done.6.refs_6_.refs_8_.refs_5_.refs_4_.refs_3_ = f32[16,256]{1,0:T(8,128)S(1)} collective-permute-done((f32[16,256]{1,0:T(8,128)S(1)}, f32[16,256]{1,0:T(8,128)S(1)}, u32[]{:S(2)}, u32[]{:S(2)}) %collective-permute-start.6) | collective-permute-done | bytes 16416 | tf_op jit(solution)/shard_map/ppermute | solution.py:20
  16.8 7.8 %collective-permute-start.7 = (f32[16,512]{1,0:T(8,128)S(1)}, f32[16,512]{1,0:T(8,128)S(1)}, u32[]{:S(2)}, u32[]{:S(2)}) collective-permute-start(f32[16,512]{1,0:T(8,128)S(1)} %pad_maximum_fusion.1), channel_id=1, source_target_pairs={{0,4},{2,6},{4,0},{6,2},{8,12},{10,14},{12,8},{14,10},{16,20},{18,... | collective-permute-start | bytes 98312 | tf_op jit(solution)/shard_map/ppermute | solution.py:20
  26.0 5.2 %collective-permute-done.7.refs_7_.refs_9_.refs_6_.refs_5_.refs_4_ = f32[16,512]{1,0:T(8,128)S(1)} collective-permute-done((f32[16,512]{1,0:T(8,128)S(1)}, f32[16,512]{1,0:T(8,128)S(1)}, u32[]{:S(2)}, u32[]{:S(2)}) %collective-permute-start.7) | collective-permute-done | bytes 32800 | tf_op jit(solution)/shard_map/ppermute | solution.py:20
  32.0 5.5 %window_attention.1 = (bf16[128,512]{1,0:T(8,128)(2,1)}, bf16[128,512]{1,0:T(8,128)(2,1)}) custom-call(s32[1]{0:T(128)} %bitcast.core_ref, bf16[256,512]{1,0:T(8,128)(2,1)} %q_ref.1, bf16[512,512]{1,0:T(8,128)(2,1)} %copy-done.7, bf16[512,512]{1,0:T(8,128)(2,1)} %stack_keys_values.1.own_ref, bf16[512,512]{1,0:T(8,128)(2,1)} %collective-permute-done.1.after_ref, ...), custom_call_target="tpu_custom_call" | custom-call | tf_op jit(solution)/shard_map/window_attention/pallas_call | solution.py:112
  37.6 4.4 %collective-permute-done.10.refs_2_.refs_8_.refs_10_.refs_7_.refs_6_.refs_5_ = f32[16,1024]{1,0:T(8,128)S(1)} collective-permute-done((f32[16,1024]{1,0:T(8,128)S(1)}, f32[16,1024]{1,0:T(8,128)S(1)}, u32[]{:S(2)}, u32[]{:S(2)}) %collective-permute-start.10) | collective-permute-done | bytes 65568 | tf_op jit(solution)/shard_map/ppermute | solution.py:20
  42.7 4.3 %project_and_norm.1 = (f32[128,2048]{1,0:T(8,128)}, bf16[128,2048]{1,0:T(8,128)(2,1)}) custom-call(bf16[128,512]{1,0:T(8,128)(2,1)} %get-tuple-element.59.mine_ref, bf16[128,512]{1,0:T(8,128)(2,1)} %copy-done.8, bf16[512,2048]{1,0:T(8,128)(2,1)} %own_w.1, bf16[512,2048]{1,0:T(8,128)(2,1)} %collective-permute-done.2.refs_0_.other_w, ...), custom_call_target="tpu_custom_call" | custom-call | tf_op jit(solution)/shard_map/project_and_norm/pallas_call | solution.py:135
  47.5 4.6 %collective-permute-start.12 = (bf16[128,2048]{1,0:T(8,128)(2,1)}, bf16[128,2048]{1,0:T(8,128)(2,1)}, u32[]{:S(2)}, u32[]{:S(2)}) collective-permute-start(bf16[128,2048]{1,0:T(8,128)(2,1)} %get-tuple-element.67.refs_0_), channel_id=1, source_target_pairs={{8,16},{10,18},{12,20},{14,22},{16,8},{18,10},{20,12},{22,14},{9,1... | collective-permute-start | bytes 1572872 | tf_op jit(solution)/shard_map/ppermute | solution.py:226
  53.2 7.5 %collective-permute-done.11.refs_0_ = bf16[128,2048]{1,0:T(8,128)(2,1)S(1)} collective-permute-done((bf16[128,2048]{1,0:T(8,128)(2,1)}, bf16[128,2048]{1,0:T(8,128)(2,1)S(1)}, u32[]{:S(2)}, u32[]{:S(2)}) %collective-permute-start.11) | collective-permute-done | bytes 524320 | tf_op jit(solution)/shard_map/ppermute | solution.py:20
  60.7 3.1 %collective-permute-done.12 = bf16[128,2048]{1,0:T(8,128)(2,1)} collective-permute-done((bf16[128,2048]{1,0:T(8,128)(2,1)}, bf16[128,2048]{1,0:T(8,128)(2,1)}, u32[]{:S(2)}, u32[]{:S(2)}) %collective-permute-start.12) | collective-permute-done | bytes 524320 | tf_op jit(solution)/shard_map/ppermute | solution.py:226
  63.8 3.6 %collective-permute-start.13 = (bf16[128,2048]{1,0:T(8,128)(2,1)S(1)}, bf16[128,2048]{1,0:T(8,128)(2,1)}, u32[]{:S(2)}, u32[]{:S(2)}) collective-permute-start(bf16[128,2048]{1,0:T(8,128)(2,1)S(1)} %collective-permute-done.11.refs_0_), channel_id=1, source_target_pairs={{8,16},{10,18},{12,20},{14,22},{16,8},{18,10},{20,12},{22,14},{9,1... | collective-permute-start | bytes 1572872 | tf_op jit(solution)/shard_map/ppermute | solution.py:226
  67.5 2.1 %collective-permute-start.14 = (bf16[128,2048]{1,0:T(8,128)(2,1)}, bf16[128,2048]{1,0:T(8,128)(2,1)}, u32[]{:S(2)}, u32[]{:S(2)}) collective-permute-start(bf16[128,2048]{1,0:T(8,128)(2,1)} %collective-permute-done.12), channel_id=1, source_target_pairs={{8,0},{10,2},{12,4},{14,6},{16,24},{18,26},{20,28},{22,30},{9,1},{... | collective-permute-start | bytes 1572872 | tf_op jit(solution)/shard_map/ppermute | solution.py:226
  70.6 1.4 copy-done.2
  72.0 1.4 copy-done.3
  73.3 1.4 copy-done.4
  74.7 2.6 %assemble_weights.1 = (bf16[1408,2048]{1,0:T(8,128)(2,1)S(1)}, bf16[704,2048]{1,0:T(8,128)(2,1)S(1)}) custom-call(bf16[352,2048]{1,0:T(8,128)(2,1)S(1)} %bitcast.13, bf16[352,2048]{1,0:T(8,128)(2,1)} %collective-permute-done.3.refs_1_, bf16[352,2048]{1,0:T(8,128)(2,1)S(1)} %bitcast.15, bf16[352,2048]{1,0:T(8,128)(2,1)} %collective-permute-done.8.refs_0_.refs_3_, ...), custom_call_target="tpu_custom_call" | custom-call | tf_op jit(solution)/shard_map/assemble_weights/pallas_call | solution.py:163
  78.9 4.6 %collective-permute-start.21 = (bf16[128,2048]{1,0:T(8,128)(2,1)}, bf16[128,2048]{1,0:T(8,128)(2,1)S(1)}, u32[]{:S(2)}, u32[]{:S(2)}) collective-permute-start(bf16[128,2048]{1,0:T(8,128)(2,1)} %collective-permute-done.13), channel_id=1, source_target_pairs={{8,0},{10,2},{12,4},{14,6},{16,24},{18,26},{20,28},{22,30},{9,1},{... | collective-permute-start | bytes 1572872 | tf_op jit(solution)/shard_map/ppermute | solution.py:226
  85.7 5.1 %expert_rows.5 = (bf16[128,2048]{1,0:T(8,128)(2,1)S(1)}, bf16[128,2048]{1,0:T(8,128)(2,1)S(1)}, bf16[128,2048]{1,0:T(8,128)(2,1)S(1)}, bf16[128,2048]{1,0:T(8,128)(2,1)S(1)}) custom-call(s32[1]{0:T(128)} %bitcast.9.shard_ref, bf16[128,2048]{1,0:T(8,128)(2,1)S(1)} %copy-done.5, bf16[128,2048]{1,0:T(8,128)(2,1)S(1)} %collective-permute-done.15.refs_1_, ...), custom_call_target="tpu_custom_call" | custom-call | tf_op jit(solution)/shard_map/expert_rows/pallas_call | solution.py:204
  90.8 1.6 collective-permute-done.21
  93.5 3.2 %collective-permute-done.19.refs_3_ = bf16[128,2048]{1,0:T(8,128)(2,1)S(1)} collective-permute-done((bf16[128,2048]{1,0:T(8,128)(2,1)S(1)}, bf16[128,2048]{1,0:T(8,128)(2,1)S(1)}, u32[]{:S(2)}, u32[]{:S(2)}) %collective-permute-start.19) | collective-permute-done | bytes 524320 | tf_op jit(solution)/shard_map/ppermute | solution.py:20
  97.8 7.5 %expert_rows.6 = (bf16[128,2048]{1,0:T(8,128)(2,1)S(1)}, bf16[128,2048]{1,0:T(8,128)(2,1)S(1)}, bf16[128,2048]{1,0:T(8,128)(2,1)S(1)}, bf16[128,2048]{1,0:T(8,12...) custom-call(s32[1]{0:T(128)} %bitcast.9.shard_ref, ...), custom_call_target="tpu_custom_call" | custom-call | tf_op jit(solution)/shard_map/expert_rows/pallas_call | solution.py:204
  105.3 3.5 %collective-permute-done.22.refs_0_ = bf16[128,2048]{1,0:T(8,128)(2,1)S(1)} collective-permute-done((bf16[128,2048]{1,0:T(8,128)(2,1)S(1)}, bf16[128,2048]{1,0:T(8,128)(2,1)S(1)}, u32[]{:S(2)}, u32[]{:S(2)}) %collective-permute-start.22) | collective-permute-done | bytes 524320 | tf_op jit(solution)/shard_map/ppermute | solution.py:20
  110.4 5.1 %expert_rows.7 = (bf16[128,2048]{1,0:T(8,128)(2,1)S(1)}, bf16[128,2048]{1,0:T(8,128)(2,1)S(1)}, bf16[128,2048]{1,0:T(8,128)(2,1)S(1)}) custom-call(s32[1]{0:T(128)} %bitcast.9.shard_ref, bf16[128,2048]{1,0:T(8,128)(2,1)S(1)} %collective-permute-done.22.refs_0_, bf16[128,2048]{1,0:T(8,128)(2,1)S(1)} %collective-permute-done.24.refs_1_, ...), custom_call_target="tpu_custom_call" | custom-call | tf_op jit(solution)/shard_map/expert_rows/pallas_call | solution.py:204
  115.5 2.7 %collective-permute-done.23.refs_0_ = bf16[128,2048]{1,0:T(8,128)(2,1)S(1)} collective-permute-done((bf16[128,2048]{1,0:T(8,128)(2,1)S(1)}, bf16[128,2048]{1,0:T(8,128)(2,1)S(1)}, u32[]{:S(2)}, u32[]{:S(2)}) %collective-permute-start.23) | collective-permute-done | bytes 524320 | tf_op jit(solution)/shard_map/ppermute | solution.py:20
  118.9 2.6 %expert_rows.8 = (bf16[128,2048]{1,0:T(8,128)(2,1)S(1)}, bf16[128,2048]{1,0:T(8,128)(2,1)S(1)}) custom-call(s32[1]{0:T(128)} %bitcast.9.shard_ref, bf16[128,2048]{1,0:T(8,128)(2,1)S(1)} %collective-permute-done.23.refs_0_, bf16[128,2048]{1,0:T(8,128)(2,1)S(1)} %collective-permute-done.26.refs_1_, ...), custom_call_target="tpu_custom_call" | custom-call | tf_op jit(solution)/shard_map/expert_rows/pallas_call | solution.py:204
  123.1 2.4 %expert_rows.9 = bf16[128,2048]{1,0:T(8,128)(2,1)S(1)} custom-call(s32[1]{0:T(128)} %bitcast.9.shard_ref, bf16[128,2048]{1,0:T(8,128)(2,1)S(1)} %collective-permute-done.34.refs_0_, f32[16,128]{1,0:T(8,128)S(1)} %select_reduce_fusion.refs_4_.refs_6_.refs_3_.refs_2_.refs_1_, f32[16,128]{1,0:T(8,128)S(1)} %collective-permute-done.5.refs_5_.refs_7_.refs_4_.refs_3_.refs_2_, ...), custom_call_target="tpu_custom_call" | custom-call | tf_op jit(solution)/shard_map/expert_rows/pallas_call | solution.py:204
  126.0 7.6 %collective-permute-done.28 = bf16[128,2048]{1,0:T(8,128)(2,1)S(1)} collective-permute-done((bf16[128,2048]{1,0:T(8,128)(2,1)S(1)}, bf16[128,2048]{1,0:T(8,128)(2,1)S(1)}, u32[]{:S(2)}, u32[]{:S(2)}) %collective-permute-start.28) | collective-permute-done | bytes 524320 | tf_op jit(solution)/shard_map/ppermute | solution.py:20
  133.7 1.3 collective-permute-done.27
  136.1 2.4 %collective-permute-start.29 = (bf16[128,2048]{1,0:T(8,128)(2,1)S(1)}, bf16[128,2048]{1,0:T(8,128)(2,1)S(1)}, u32[]{:S(2)}, u32[]{:S(2)}) collective-permute-start(bf16[128,2048]{1,0:T(8,128)(2,1)S(1)} %get-tuple-element.91), channel_id=1, source_target_pairs={{0,4},{2,6},{4,0},{6,2},{8,12},{10,14},{12,8},{14,10},{16,20},{18,... | collective-permute-start | bytes 1572872 | tf_op jit(solution)/shard_map/ppermute | solution.py:20
  139.8 9.2 %collective-permute-done.32 = bf16[128,2048]{1,0:T(8,128)(2,1)S(1)} collective-permute-done((bf16[128,2048]{1,0:T(8,128)(2,1)S(1)}, bf16[128,2048]{1,0:T(8,128)(2,1)S(1)}, u32[]{:S(2)}, u32[]{:S(2)}) %collective-permute-start.32) | collective-permute-done | bytes 524320 | tf_op jit(solution)/shard_map/ppermute | solution.py:20
  151.0 2.2 %collective-permute-start.30 = (bf16[128,2048]{1,0:T(8,128)(2,1)S(1)}, bf16[128,2048]{1,0:T(8,128)(2,1)S(1)}, u32[]{:S(2)}, u32[]{:S(2)}) collective-permute-start(bf16[128,2048]{1,0:T(8,128)(2,1)S(1)} %add_convert_fusion.9), channel_id=1, source_target_pairs={{0,4},{2,6},{4,0},{6,2},{8,12},{10,14},{12,8},{14,10},{16,20},{18,... | collective-permute-start | bytes 1572872 | tf_op jit(solution)/shard_map/ppermute | solution.py:20
  153.5 1.3 collective-permute-start.37
  154.9 8.9 %collective-permute-done.33 = bf16[128,2048]{1,0:T(8,128)(2,1)S(1)} collective-permute-done((bf16[128,2048]{1,0:T(8,128)(2,1)S(1)}, bf16[128,2048]{1,0:T(8,128)(2,1)S(1)}, u32[]{:S(2)}, u32[]{:S(2)}) %collective-permute-start.33) | collective-permute-done | bytes 524320 | tf_op jit(solution)/shard_map/ppermute | solution.py:20
  165.5 1.7 collective-permute-start.31
  167.3 2.7 %collective-permute-done.37 = bf16[128,2048]{1,0:T(8,128)(2,1)S(1)} collective-permute-done((bf16[128,2048]{1,0:T(8,128)(2,1)S(1)}, bf16[128,2048]{1,0:T(8,128)(2,1)S(1)}, u32[]{:S(2)}, u32[]{:S(2)}) %collective-permute-start.37) | collective-permute-done | bytes 524320 | tf_op jit(solution)/shard_map/ppermute | solution.py:226
  170.3 1.3 collective-permute-start.39
  171.8 1.9 collective-permute-start.38
  173.7 3.1 %collective-permute-done.42 = bf16[128,2048]{1,0:T(8,128)(2,1)S(1)} collective-permute-done((bf16[128,2048]{1,0:T(8,128)(2,1)S(1)}, bf16[128,2048]{1,0:T(8,128)(2,1)S(1)}, u32[]{:S(2)}, u32[]{:S(2)}) %collective-permute-start.42) | collective-permute-done | bytes 524320 | tf_op jit(solution)/shard_map/ppermute | solution.py:20
  177.0 2.2 %collective-permute-done.31 = bf16[128,2048]{1,0:T(8,128)(2,1)S(1)} collective-permute-done((bf16[128,2048]{1,0:T(8,128)(2,1)S(1)}, bf16[128,2048]{1,0:T(8,128)(2,1)S(1)}, u32[]{:S(2)}, u32[]{:S(2)}) %collective-permute-start.31) | collective-permute-done | bytes 524320 | tf_op jit(solution)/shard_map/ppermute | solution.py:20
  179.1 1.4 collective-permute-start.44
  181.5 4.9 %collective-permute-done.39 = bf16[128,2048]{1,0:T(8,128)(2,1)S(1)} collective-permute-done((bf16[128,2048]{1,0:T(8,128)(2,1)S(1)}, bf16[128,2048]{1,0:T(8,128)(2,1)S(1)}, u32[]{:S(2)}, u32[]{:S(2)}) %collective-permute-start.39) | collective-permute-done | bytes 524320 | tf_op jit(solution)/shard_map/ppermute | solution.py:226
  186.5 2.1 %collective-permute-start.41 = (bf16[128,2048]{1,0:T(8,128)(2,1)S(1)}, bf16[128,2048]{1,0:T(8,128)(2,1)S(1)}, u32[]{:S(2)}, u32[]{:S(2)}) collective-permute-start(bf16[128,2048]{1,0:T(8,128)(2,1)S(1)} %add_convert_fusion.4), channel_id=1, source_target_pairs={{8,16},{10,18},{12,20},{14,22},{16,8},{18,10},{20,12},{22,14},{9,1... | collective-permute-start | bytes 1572872 | tf_op jit(solution)/shard_map/ppermute | solution.py:226
  189.7 7.9 %collective-permute-done.41 = bf16[128,2048]{1,0:T(8,128)(2,1)S(1)} collective-permute-done((bf16[128,2048]{1,0:T(8,128)(2,1)S(1)}, bf16[128,2048]{1,0:T(8,128)(2,1)S(1)}, u32[]{:S(2)}, u32[]{:S(2)}) %collective-permute-start.41) | collective-permute-done | bytes 524320 | tf_op jit(solution)/shard_map/ppermute | solution.py:226
  198.0 1.3 add_convert_fusion
  (87 shorter events, 26.7 us)
Async XLA Ops:
  0.0 31.8 %collective-permute-start.2 = (bf16[512,2048]{1,0:T(8,128)(2,1)}, bf16[512,2048]{1,0:T(8,128)(2,1)}, u32[]{:S(2)}, u32[]{:S(2)}) collective-permute-start(bf16[512,2048]{1,0:T(8,128)(2,1)} %own_w.1), channel_id=1, source_target_pairs={{0,1},{1,0},{2,3},{3,2},{4,5},{5,4},{6,7},{7,6},{8,9},{9,8},{10,11... | collective-permute-start | bytes 6291464 | tf_op jit(solution)/shard_map/ppermute | solution.py:328
  1.9 29.3 %collective-permute-start = (bf16[512,512]{1,0:T(8,128)(2,1)}, bf16[512,512]{1,0:T(8,128)(2,1)S(1)}, u32[]{:S(2)}, u32[]{:S(2)}) collective-permute-start(bf16[512,512]{1,0:T(8,128)(2,1)} %stack_keys_values.1.own_ref), channel_id=1, source_target_pairs={{0,2},{2,4},{4,6},{6,8},{8,10},{10,12},{12,14},{14,16},{16,18},{18... | collective-permute-start | bytes 1572872 | tf_op jit(solution)/shard_map/ppermute | solution.py:321
  5.3 25.9 %collective-permute-start.1 = (bf16[512,512]{1,0:T(8,128)(2,1)}, bf16[512,512]{1,0:T(8,128)(2,1)}, u32[]{:S(2)}, u32[]{:S(2)}) collective-permute-start(bf16[512,512]{1,0:T(8,128)(2,1)} %stack_keys_values.1.own_ref), channel_id=1, source_target_pairs={{2,0},{4,2},{6,4},{8,6},{10,8},{12,10},{14,12},{16,14},{18,16},{20... | collective-permute-start | bytes 1572872 | tf_op jit(solution)/shard_map/ppermute | solution.py:322
  8.4 3.7 %collective-permute-start.5 = (f32[16,128]{1,0:T(8,128)S(1)}, f32[16,128]{1,0:T(8,128)S(1)}, u32[]{:S(2)}, u32[]{:S(2)}) collective-permute-start(f32[16,128]{1,0:T(8,128)S(1)} %select_reduce_fusion.refs_4_.refs_6_.refs_3_.refs_2_.refs_1_), channel_id=1, source_target_pairs={{0,8},{2,10},{4,12},{6,14},{8,0},{10,2},{12,4},{14,6},{16,24},{18,... | collective-permute-start | bytes 24584 | tf_op jit(solution)/shard_map/ppermute | solution.py:20
  12.1 4.6 %collective-permute-start.6 = (f32[16,256]{1,0:T(8,128)S(1)}, f32[16,256]{1,0:T(8,128)S(1)}, u32[]{:S(2)}, u32[]{:S(2)}) collective-permute-start(f32[16,256]{1,0:T(8,128)S(1)} %pad_maximum_fusion.2), channel_id=1, source_target_pairs={{0,16},{2,18},{4,20},{6,22},{8,24},{10,26},{12,28},{14,30},{16,0},... | collective-permute-start | bytes 49160 | tf_op jit(solution)/shard_map/ppermute | solution.py:20
  14.7 17.0 %collective-permute-start.3 = (bf16[352,2048]{1,0:T(8,128)(2,1)}, bf16[352,2048]{1,0:T(8,128)(2,1)}, u32[]{:S(2)}, u32[]{:S(2)}) collective-permute-start(bf16[352,2048]{1,0:T(8,128)(2,1)} %bitcast.12), channel_id=1, source_target_pairs={{0,1},{1,0},{2,3},{3,2},{4,5},{5,4},{6,7},{7,6},{8,9},{9,8},{10,11... | collective-permute-start | bytes 4325384 | tf_op jit(solution)/shard_map/ppermute | solution.py:330
  16.8 14.4 %collective-permute-start.7 = (f32[16,512]{1,0:T(8,128)S(1)}, f32[16,512]{1,0:T(8,128)S(1)}, u32[]{:S(2)}, u32[]{:S(2)}) collective-permute-start(f32[16,512]{1,0:T(8,128)S(1)} %pad_maximum_fusion.1), channel_id=1, source_target_pairs={{0,4},{2,6},{4,0},{6,2},{8,12},{10,14},{12,8},{14,10},{16,20},{18,... | collective-permute-start | bytes 98312 | tf_op jit(solution)/shard_map/ppermute | solution.py:20
  31.2 10.8 %collective-permute-start.8 = (bf16[352,2048]{1,0:T(8,128)(2,1)}, bf16[352,2048]{1,0:T(8,128)(2,1)}, u32[]{:S(2)}, u32[]{:S(2)}) collective-permute-start(bf16[352,2048]{1,0:T(8,128)(2,1)} %bitcast.14), channel_id=1, source_target_pairs={{0,1},{1,0},{2,3},{3,2},{4,5},{5,4},{6,7},{7,6},{8,9},{9,8},{10,11... | collective-permute-start | bytes 4325384 | tf_op jit(solution)/shard_map/ppermute | solution.py:332
  31.3 10.8 %collective-permute-start.9 = (bf16[352,2048]{1,0:T(8,128)(2,1)}, bf16[352,2048]{1,0:T(8,128)(2,1)}, u32[]{:S(2)}, u32[]{:S(2)}) collective-permute-start(bf16[352,2048]{1,0:T(8,128)(2,1)} %bitcast.16), channel_id=1, source_target_pairs={{0,1},{1,0},{2,3},{3,2},{4,5},{5,4},{6,7},{7,6},{8,9},{9,8},{10,11... | collective-permute-start | bytes 4325384 | tf_op jit(solution)/shard_map/ppermute | solution.py:333
  37.5 4.5 %collective-permute-start.4 = (bf16[128,512]{1,0:T(8,128)(2,1)}, bf16[128,512]{1,0:T(8,128)(2,1)S(1)}, u32[]{:S(2)}, u32[]{:S(2)}) collective-permute-start(bf16[128,512]{1,0:T(8,128)(2,1)} %get-tuple-element.60), channel_id=1, source_target_pairs={{0,1},{1,0},{2,3},{3,2},{4,5},{5,4},{6,7},{7,6},{8,9},{9,8},{10,11... | collective-permute-start | bytes 393224 | tf_op jit(solution)/shard_map/ppermute | solution.py:339
  37.6 4.5 %collective-permute-start.10 = (f32[16,1024]{1,0:T(8,128)S(1)}, f32[16,1024]{1,0:T(8,128)S(1)}, u32[]{:S(2)}, u32[]{:S(2)}) collective-permute-start(f32[16,1024]{1,0:T(8,128)S(1)} %pad_maximum_fusion), channel_id=1, source_target_pairs={{0,2},{2,0},{4,6},{6,4},{8,10},{10,8},{12,14},{14,12},{16,18},{18,... | collective-permute-start | bytes 196616 | tf_op jit(solution)/shard_map/ppermute | solution.py:20
  47.0 13.7 %collective-permute-start.11 = (bf16[128,2048]{1,0:T(8,128)(2,1)}, bf16[128,2048]{1,0:T(8,128)(2,1)S(1)}, u32[]{:S(2)}, u32[]{:S(2)}) collective-permute-start(bf16[128,2048]{1,0:T(8,128)(2,1)} %get-tuple-element.67.refs_0_), channel_id=1, source_target_pairs={{0,8},{2,10},{4,12},{6,14},{8,0},{10,2},{12,4},{14,6},{16,24},{18,... | collective-permute-start | bytes 1572872 | tf_op jit(solution)/shard_map/ppermute | solution.py:20
  47.5 16.4 %collective-permute-start.12 = (bf16[128,2048]{1,0:T(8,128)(2,1)}, bf16[128,2048]{1,0:T(8,128)(2,1)}, u32[]{:S(2)}, u32[]{:S(2)}) collective-permute-start(bf16[128,2048]{1,0:T(8,128)(2,1)} %get-tuple-element.67.refs_0_), channel_id=1, source_target_pairs={{8,16},{10,18},{12,20},{14,22},{16,8},{18,10},{20,12},{22,14},{9,1... | collective-permute-start | bytes 1572872 | tf_op jit(solution)/shard_map/ppermute | solution.py:226
  52.1 17.5 %collective-permute-start.16 = (bf16[128,2048]{1,0:T(8,128)(2,1)}, bf16[128,2048]{1,0:T(8,128)(2,1)S(1)}, u32[]{:S(2)}, u32[]{:S(2)}) collective-permute-start(bf16[128,2048]{1,0:T(8,128)(2,1)} %get-tuple-element.67.refs_0_), channel_id=1, source_target_pairs={{0,4},{2,6},{4,0},{6,2},{8,12},{10,14},{12,8},{14,10},{16,20},{18,... | collective-permute-start | bytes 1572872 | tf_op jit(solution)/shard_map/ppermute | solution.py:20
  52.2 17.4 %collective-permute-start.15 = (bf16[128,2048]{1,0:T(8,128)(2,1)}, bf16[128,2048]{1,0:T(8,128)(2,1)S(1)}, u32[]{:S(2)}, u32[]{:S(2)}) collective-permute-start(bf16[128,2048]{1,0:T(8,128)(2,1)} %get-tuple-element.67.refs_0_), channel_id=1, source_target_pairs={{0,2},{2,0},{4,6},{6,4},{8,10},{10,8},{12,14},{14,12},{16,18},{18,... | collective-permute-start | bytes 1572872 | tf_op jit(solution)/shard_map/ppermute | solution.py:20
  63.8 14.6 %collective-permute-start.13 = (bf16[128,2048]{1,0:T(8,128)(2,1)S(1)}, bf16[128,2048]{1,0:T(8,128)(2,1)}, u32[]{:S(2)}, u32[]{:S(2)}) collective-permute-start(bf16[128,2048]{1,0:T(8,128)(2,1)S(1)} %collective-permute-done.11.refs_0_), channel_id=1, source_target_pairs={{8,16},{10,18},{12,20},{14,22},{16,8},{18,10},{20,12},{22,14},{9,1... | collective-permute-start | bytes 1572872 | tf_op jit(solution)/shard_map/ppermute | solution.py:226
  67.5 11.4 %collective-permute-start.14 = (bf16[128,2048]{1,0:T(8,128)(2,1)}, bf16[128,2048]{1,0:T(8,128)(2,1)}, u32[]{:S(2)}, u32[]{:S(2)}) collective-permute-start(bf16[128,2048]{1,0:T(8,128)(2,1)} %collective-permute-done.12), channel_id=1, source_target_pairs={{8,0},{10,2},{12,4},{14,6},{16,24},{18,26},{20,28},{22,30},{9,1},{... | collective-permute-start | bytes 1572872 | tf_op jit(solution)/shard_map/ppermute | solution.py:226
  69.6 15.0 %collective-permute-start.17 = (bf16[128,2048]{1,0:T(8,128)(2,1)S(1)}, bf16[128,2048]{1,0:T(8,128)(2,1)S(1)}, u32[]{:S(2)}, u32[]{:S(2)}) collective-permute-start(bf16[128,2048]{1,0:T(8,128)(2,1)S(1)} %collective-permute-done.16.refs_2_), channel_id=1, source_target_pairs={{0,2},{2,0},{4,6},{6,4},{8,10},{10,8},{12,14},{14,12},{16,18},{18,... | collective-permute-start | bytes 1572872 | tf_op jit(solution)/shard_map/ppermute | solution.py:20
  70.1 15.3 %collective-permute-start.18 = (bf16[128,2048]{1,0:T(8,128)(2,1)S(1)}, bf16[128,2048]{1,0:T(8,128)(2,1)S(1)}, u32[]{:S(2)}, u32[]{:S(2)}) collective-permute-start(bf16[128,2048]{1,0:T(8,128)(2,1)S(1)} %collective-permute-done.11.refs_0_), channel_id=1, source_target_pairs={{0,4},{2,6},{4,0},{6,2},{8,12},{10,14},{12,8},{14,10},{16,20},{18,... | collective-permute-start | bytes 1572872 | tf_op jit(solution)/shard_map/ppermute | solution.py:20
  77.4 8.3 %copy-start.1 = (f32[16,1024]{1,0:T(8,128)S(1)}, f32[16,1024]{1,0:T(8,128)}, u32[]{:S(2)}) copy-start(f32[16,1024]{1,0:T(8,128)} %copy-done) | copy-start | bytes 196612
  77.4 8.3 %copy-start.5 = (bf16[128,2048]{1,0:T(8,128)(2,1)S(1)}, bf16[128,2048]{1,0:T(8,128)(2,1)}, u32[]{:S(2)}) copy-start(bf16[128,2048]{1,0:T(8,128)(2,1)} %get-tuple-element.67.refs_0_) | copy-start | bytes 1572868
  78.9 13.5 %collective-permute-start.21 = (bf16[128,2048]{1,0:T(8,128)(2,1)}, bf16[128,2048]{1,0:T(8,128)(2,1)S(1)}, u32[]{:S(2)}, u32[]{:S(2)}) collective-permute-start(bf16[128,2048]{1,0:T(8,128)(2,1)} %collective-permute-done.13), channel_id=1, source_target_pairs={{8,0},{10,2},{12,4},{14,6},{16,24},{18,26},{20,28},{22,30},{9,1},{... | collective-permute-start | bytes 1572872 | tf_op jit(solution)/shard_map/ppermute | solution.py:226
  84.6 12.2 %collective-permute-start.19 = (bf16[128,2048]{1,0:T(8,128)(2,1)S(1)}, bf16[128,2048]{1,0:T(8,128)(2,1)S(1)}, u32[]{:S(2)}, u32[]{:S(2)}) collective-permute-start(bf16[128,2048]{1,0:T(8,128)(2,1)S(1)} %broadcast_select_fusion.1.refs_2_), channel_id=1, source_target_pairs={{0,2},{2,0},{4,6},{6,4},{8,10},{10,8},{12,14},{14,12},{16,18},{18,... | collective-permute-start | bytes 1572872 | tf_op jit(solution)/shard_map/ppermute | solution.py:20
  85.4 12.1 %collective-permute-start.20 = (bf16[128,2048]{1,0:T(8,128)(2,1)S(1)}, bf16[128,2048]{1,0:T(8,128)(2,1)S(1)}, u32[]{:S(2)}, u32[]{:S(2)}) collective-permute-start(bf16[128,2048]{1,0:T(8,128)(2,1)S(1)} %broadcast_select_fusion.1.refs_2_), channel_id=1, source_target_pairs={{0,4},{2,6},{4,0},{6,2},{8,12},{10,14},{12,8},{14,10},{16,20},{18,... | collective-permute-start | bytes 1572872 | tf_op jit(solution)/shard_map/ppermute | solution.py:20
  96.7 12.1 %collective-permute-start.22 = (bf16[128,2048]{1,0:T(8,128)(2,1)S(1)}, bf16[128,2048]{1,0:T(8,128)(2,1)S(1)}, u32[]{:S(2)}, u32[]{:S(2)}) collective-permute-start(bf16[128,2048]{1,0:T(8,128)(2,1)S(1)} %broadcast_select_fusion.refs_5_), channel_id=1, source_target_pairs={{0,2},{2,0},{4,6},{6,4},{8,10},{10,8},{12,14},{14,12},{16,18},{18,... | collective-permute-start | bytes 1572872 | tf_op jit(solution)/shard_map/ppermute | solution.py:20
  97.5 12.1 %collective-permute-start.24 = (bf16[128,2048]{1,0:T(8,128)(2,1)S(1)}, bf16[128,2048]{1,0:T(8,128)(2,1)S(1)}, u32[]{:S(2)}, u32[]{:S(2)}) collective-permute-start(bf16[128,2048]{1,0:T(8,128)(2,1)S(1)} %broadcast_select_fusion.refs_5_), channel_id=1, source_target_pairs={{0,4},{2,6},{4,0},{6,2},{8,12},{10,14},{12,8},{14,10},{16,20},{18,... | collective-permute-start | bytes 1572872 | tf_op jit(solution)/shard_map/ppermute | solution.py:20
  97.8 12.1 %collective-permute-start.25 = (bf16[128,2048]{1,0:T(8,128)(2,1)S(1)}, bf16[128,2048]{1,0:T(8,128)(2,1)S(1)}, u32[]{:S(2)}, u32[]{:S(2)}) collective-permute-start(bf16[128,2048]{1,0:T(8,128)(2,1)S(1)} %collective-permute-done.15.refs_1_), channel_id=1, source_target_pairs={{0,8},{2,10},{4,12},{6,14},{8,0},{10,2},{12,4},{14,6},{16,24},{18,... | collective-permute-start | bytes 1572872 | tf_op jit(solution)/shard_map/ppermute | solution.py:20
  108.8 9.4 %collective-permute-start.23 = (bf16[128,2048]{1,0:T(8,128)(2,1)S(1)}, bf16[128,2048]{1,0:T(8,128)(2,1)S(1)}, u32[]{:S(2)}, u32[]{:S(2)}) collective-permute-start(bf16[128,2048]{1,0:T(8,128)(2,1)S(1)} %collective-permute-done.20.refs_4_), channel_id=1, source_target_pairs={{0,2},{2,0},{4,6},{6,4},{8,10},{10,8},{12,14},{14,12},{16,18},{18,... | collective-permute-start | bytes 1572872 | tf_op jit(solution)/shard_map/ppermute | solution.py:20
  109.6 9.4 %collective-permute-start.26 = (bf16[128,2048]{1,0:T(8,128)(2,1)S(1)}, bf16[128,2048]{1,0:T(8,128)(2,1)S(1)}, u32[]{:S(2)}, u32[]{:S(2)}) collective-permute-start(bf16[128,2048]{1,0:T(8,128)(2,1)S(1)} %collective-permute-done.22.refs_0_), channel_id=1, source_target_pairs={{0,4},{2,6},{4,0},{6,2},{8,12},{10,14},{12,8},{14,10},{16,20},{18,... | collective-permute-start | bytes 1572872 | tf_op jit(solution)/shard_map/ppermute | solution.py:20
  109.9 13.2 %collective-permute-start.34 = (bf16[128,2048]{1,0:T(8,128)(2,1)S(1)}, bf16[128,2048]{1,0:T(8,128)(2,1)S(1)}, u32[]{:S(2)}, u32[]{:S(2)}) collective-permute-start(bf16[128,2048]{1,0:T(8,128)(2,1)S(1)} %collective-permute-done.17.refs_3_), channel_id=1, source_target_pairs={{0,8},{2,10},{4,12},{6,14},{8,0},{10,2},{12,4},{14,6},{16,24},{18,... | collective-permute-start | bytes 1572872 | tf_op jit(solution)/shard_map/ppermute | solution.py:20
  121.6 12.0 %collective-permute-start.28 = (bf16[128,2048]{1,0:T(8,128)(2,1)S(1)}, bf16[128,2048]{1,0:T(8,128)(2,1)S(1)}, u32[]{:S(2)}, u32[]{:S(2)}) collective-permute-start(bf16[128,2048]{1,0:T(8,128)(2,1)S(1)} %get-tuple-element.90), channel_id=1, source_target_pairs={{0,4},{2,6},{4,0},{6,2},{8,12},{10,14},{12,8},{14,10},{16,20},{18,... | collective-permute-start | bytes 1572872 | tf_op jit(solution)/shard_map/ppermute | solution.py:20
  121.9 13.1 %collective-permute-start.27 = (bf16[128,2048]{1,0:T(8,128)(2,1)S(1)}, bf16[128,2048]{1,0:T(8,128)(2,1)S(1)}, u32[]{:S(2)}, u32[]{:S(2)}) collective-permute-start(bf16[128,2048]{1,0:T(8,128)(2,1)S(1)} %get-tuple-element.88), channel_id=1, source_target_pairs={{0,2},{2,0},{4,6},{6,4},{8,10},{10,8},{12,14},{14,12},{16,18},{18,... | collective-permute-start | bytes 1572872 | tf_op jit(solution)/shard_map/ppermute | solution.py:20
  125.5 13.5 %collective-permute-start.35 = (bf16[128,2048]{1,0:T(8,128)(2,1)S(1)}, bf16[128,2048]{1,0:T(8,128)(2,1)S(1)}, u32[]{:S(2)}, u32[]{:S(2)}) collective-permute-start(bf16[128,2048]{1,0:T(8,128)(2,1)S(1)} %expert_rows.9), channel_id=1, source_target_pairs={{0,8},{2,10},{4,12},{6,14},{8,0},{10,2},{12,4},{14,6},{16,24},{18,... | collective-permute-start | bytes 1572872 | tf_op jit(solution)/shard_map/ppermute | solution.py:20
  135.1 14.0 %collective-permute-start.32 = (bf16[128,2048]{1,0:T(8,128)(2,1)S(1)}, bf16[128,2048]{1,0:T(8,128)(2,1)S(1)}, u32[]{:S(2)}, u32[]{:S(2)}) collective-permute-start(bf16[128,2048]{1,0:T(8,128)(2,1)S(1)} %add_convert_fusion.8), channel_id=1, source_target_pairs={{0,2},{2,0},{4,6},{6,4},{8,10},{10,8},{12,14},{14,12},{16,18},{18,... | collective-permute-start | bytes 1572872 | tf_op jit(solution)/shard_map/ppermute | solution.py:20
  136.1 14.8 %collective-permute-start.29 = (bf16[128,2048]{1,0:T(8,128)(2,1)S(1)}, bf16[128,2048]{1,0:T(8,128)(2,1)S(1)}, u32[]{:S(2)}, u32[]{:S(2)}) collective-permute-start(bf16[128,2048]{1,0:T(8,128)(2,1)S(1)} %get-tuple-element.91), channel_id=1, source_target_pairs={{0,4},{2,6},{4,0},{6,2},{8,12},{10,14},{12,8},{14,10},{16,20},{18,... | collective-permute-start | bytes 1572872 | tf_op jit(solution)/shard_map/ppermute | solution.py:20
  139.0 14.4 %collective-permute-start.36 = (bf16[128,2048]{1,0:T(8,128)(2,1)S(1)}, bf16[128,2048]{1,0:T(8,128)(2,1)S(1)}, u32[]{:S(2)}, u32[]{:S(2)}) collective-permute-start(bf16[128,2048]{1,0:T(8,128)(2,1)S(1)} %get-tuple-element.102), channel_id=1, source_target_pairs={{0,8},{2,10},{4,12},{6,14},{8,0},{10,2},{12,4},{14,6},{16,24},{18,... | collective-permute-start | bytes 1572872 | tf_op jit(solution)/shard_map/ppermute | solution.py:20
  149.1 14.7 %collective-permute-start.33 = (bf16[128,2048]{1,0:T(8,128)(2,1)S(1)}, bf16[128,2048]{1,0:T(8,128)(2,1)S(1)}, u32[]{:S(2)}, u32[]{:S(2)}) collective-permute-start(bf16[128,2048]{1,0:T(8,128)(2,1)S(1)} %get-tuple-element.97), channel_id=1, source_target_pairs={{0,2},{2,0},{4,6},{6,4},{8,10},{10,8},{12,14},{14,12},{16,18},{18,... | collective-permute-start | bytes 1572872 | tf_op jit(solution)/shard_map/ppermute | solution.py:20
  151.0 14.6 %collective-permute-start.30 = (bf16[128,2048]{1,0:T(8,128)(2,1)S(1)}, bf16[128,2048]{1,0:T(8,128)(2,1)S(1)}, u32[]{:S(2)}, u32[]{:S(2)}) collective-permute-start(bf16[128,2048]{1,0:T(8,128)(2,1)S(1)} %add_convert_fusion.9), channel_id=1, source_target_pairs={{0,4},{2,6},{4,0},{6,2},{8,12},{10,14},{12,8},{14,10},{16,20},{18,... | collective-permute-start | bytes 1572872 | tf_op jit(solution)/shard_map/ppermute | solution.py:20
  153.5 16.5 %collective-permute-start.37 = (bf16[128,2048]{1,0:T(8,128)(2,1)S(1)}, bf16[128,2048]{1,0:T(8,128)(2,1)S(1)}, u32[]{:S(2)}, u32[]{:S(2)}) collective-permute-start(bf16[128,2048]{1,0:T(8,128)(2,1)S(1)} %add_convert_fusion.7), channel_id=1, source_target_pairs={{0,8},{2,10},{4,12},{6,14},{24,16},{26,18},{28,20},{30,22},{1,9},{... | collective-permute-start | bytes 1572872 | tf_op jit(solution)/shard_map/ppermute | solution.py:226
  163.8 13.0 %collective-permute-start.42 = (bf16[128,2048]{1,0:T(8,128)(2,1)S(1)}, bf16[128,2048]{1,0:T(8,128)(2,1)S(1)}, u32[]{:S(2)}, u32[]{:S(2)}) collective-permute-start(bf16[128,2048]{1,0:T(8,128)(2,1)S(1)} %add_convert_fusion.2), channel_id=1, source_target_pairs={{0,2},{2,0},{4,6},{6,4},{8,10},{10,8},{12,14},{14,12},{16,18},{18,... | collective-permute-start | bytes 1572872 | tf_op jit(solution)/shard_map/ppermute | solution.py:20
  165.5 13.6 %collective-permute-start.31 = (bf16[128,2048]{1,0:T(8,128)(2,1)S(1)}, bf16[128,2048]{1,0:T(8,128)(2,1)S(1)}, u32[]{:S(2)}, u32[]{:S(2)}) collective-permute-start(bf16[128,2048]{1,0:T(8,128)(2,1)S(1)} %get-tuple-element.93), channel_id=1, source_target_pairs={{0,4},{2,6},{4,0},{6,2},{8,12},{10,14},{12,8},{14,10},{16,20},{18,... | collective-permute-start | bytes 1572872 | tf_op jit(solution)/shard_map/ppermute | solution.py:20
  170.3 16.0 %collective-permute-start.39 = (bf16[128,2048]{1,0:T(8,128)(2,1)S(1)}, bf16[128,2048]{1,0:T(8,128)(2,1)S(1)}, u32[]{:S(2)}, u32[]{:S(2)}) collective-permute-start(bf16[128,2048]{1,0:T(8,128)(2,1)S(1)} %add_convert_fusion.6), channel_id=1, source_target_pairs={{0,8},{2,10},{4,12},{6,14},{24,16},{26,18},{28,20},{30,22},{1,9},{... | collective-permute-start | bytes 1572872 | tf_op jit(solution)/shard_map/ppermute | solution.py:226
  171.8 14.7 %collective-permute-start.38 = (bf16[128,2048]{1,0:T(8,128)(2,1)S(1)}, bf16[128,2048]{1,0:T(8,128)(2,1)S(1)}, u32[]{:S(2)}, u32[]{:S(2)}) collective-permute-start(bf16[128,2048]{1,0:T(8,128)(2,1)S(1)} %add_convert_fusion.6), channel_id=1, source_target_pairs={{8,16},{10,18},{12,20},{14,22},{16,8},{18,10},{20,12},{22,14},{9,1... | collective-permute-start | bytes 1572872 | tf_op jit(solution)/shard_map/ppermute | solution.py:226
  179.1 9.7 %collective-permute-start.44 = (bf16[128,2048]{1,0:T(8,128)(2,1)S(1)}, bf16[128,2048]{1,0:T(8,128)(2,1)S(1)}, u32[]{:S(2)}, u32[]{:S(2)}) collective-permute-start(bf16[128,2048]{1,0:T(8,128)(2,1)S(1)} %add_convert_fusion.1), channel_id=1, source_target_pairs={{0,4},{2,6},{4,0},{6,2},{8,12},{10,14},{12,8},{14,10},{16,20},{18,... | collective-permute-start | bytes 1572872 | tf_op jit(solution)/shard_map/ppermute | solution.py:20
  180.6 9.2 %collective-permute-start.43 = (bf16[128,2048]{1,0:T(8,128)(2,1)S(1)}, bf16[128,2048]{1,0:T(8,128)(2,1)S(1)}, u32[]{:S(2)}, u32[]{:S(2)}) collective-permute-start(bf16[128,2048]{1,0:T(8,128)(2,1)S(1)} %add_convert_fusion.3), channel_id=1, source_target_pairs={{0,2},{2,0},{4,6},{6,4},{8,10},{10,8},{12,14},{14,12},{16,18},{18,... | collective-permute-start | bytes 1572872 | tf_op jit(solution)/shard_map/ppermute | solution.py:20
  186.5 11.6 %copy-start.6 = (f32[128,2048]{1,0:T(8,128)S(1)}, f32[128,2048]{1,0:T(8,128)}, u32[]{:S(2)}) copy-start(f32[128,2048]{1,0:T(8,128)} %get-tuple-element.63) | copy-start | bytes 3145732
  186.5 11.2 %collective-permute-start.41 = (bf16[128,2048]{1,0:T(8,128)(2,1)S(1)}, bf16[128,2048]{1,0:T(8,128)(2,1)S(1)}, u32[]{:S(2)}, u32[]{:S(2)}) collective-permute-start(bf16[128,2048]{1,0:T(8,128)(2,1)S(1)} %add_convert_fusion.4), channel_id=1, source_target_pairs={{8,16},{10,18},{12,20},{14,22},{16,8},{18,10},{20,12},{22,14},{9,1... | collective-permute-start | bytes 1572872 | tf_op jit(solution)/shard_map/ppermute | solution.py:226
  188.8 9.2 %collective-permute-start.40 = (bf16[128,2048]{1,0:T(8,128)(2,1)S(1)}, bf16[128,2048]{1,0:T(8,128)(2,1)S(1)}, u32[]{:S(2)}, u32[]{:S(2)}) collective-permute-start(bf16[128,2048]{1,0:T(8,128)(2,1)S(1)} %add_convert_fusion.5), channel_id=1, source_target_pairs={{0,8},{2,10},{4,12},{6,14},{8,0},{10,2},{12,4},{14,6},{16,24},{18,... | collective-permute-start | bytes 1572872 | tf_op jit(solution)/shard_map/ppermute | solution.py:20
  (6 other events, 6.2 us)

commit v7 on v6

--- a/solution.py
+++ b/solution.py
@@ -41,83 +41,88 @@
     return sum(1 << bit for bit, mask in enumerate(gate_order(lax.axis_size("seq"))) if j & mask)
 
 
-def stack_kernel(keys_ref, values_ref, out_ref):
-    rows = keys_ref.shape[0]
-    out_ref[:rows] = keys_ref[...]
-    out_ref[rows:] = values_ref[...]
-
-
-def stack(keys, values):
-    rows, width = keys.shape
-    return pl.pallas_call(
-        stack_kernel,
-        out_shape=jax.ShapeDtypeStruct((2 * rows, width), keys.dtype),
-        in_specs=[VMEM, VMEM],
-        out_specs=VMEM,
-        compiler_params=pltpu.CompilerParams(vmem_limit_bytes=63 * 1024 * 1024),
-        name="stack_keys_values",
-    )(keys, values)
-
-
-def attention_kernel(core_ref, q_ref, before_ref, own_ref, after_ref, ids_ref, *refs):
-    theirs_ref, mine_ref, both = refs[-3:]
+def fetch_kernel(own_ref, other_ref, resid_ref, *refs):
+    outs, sems = refs[:-1], refs[-1]
+    copies = [
+        pltpu.make_async_copy(ref, out, sems.at[i])
+        for i, (ref, out) in enumerate(zip((own_ref, other_ref, resid_ref), outs))
+    ]
+    for copy in copies:
+        copy.start()
+    for copy in copies:
+        copy.wait()
+
+
+def fetch(*arrays):
+    return pl.pallas_call(
+        fetch_kernel,
+        out_shape=[jax.ShapeDtypeStruct(array.shape, array.dtype) for array in arrays],
+        in_specs=[ANY] * len(arrays),
+        out_specs=[VMEM] * len(arrays),
+        scratch_shapes=[pltpu.SemaphoreType.DMA((len(arrays),))],
+        compiler_params=pltpu.CompilerParams(vmem_limit_bytes=8 * 1024 * 1024),
+        name="fetch_projection",
+    )(*arrays)
+
+
+def attention_kernel(where_ref, q_ref, ids_ref, *refs):
+    blocks, (theirs_ref, mine_ref, keys, values, both, sems) = refs[:6], refs[-6:]
     rows = q_ref.shape[0]
     some = rows // 2
+    core, odd = where_ref[0], where_ref[1]
+    starts = (2 * rows * (1 - odd), rows, 2 * rows * odd)
+    copies = []
+    for i, block in enumerate(blocks):
+        target = (keys, values)[i // 3].at[pl.ds(pl.multiple_of(starts[i % 3], rows), rows), :]
+        copies.append(pltpu.make_async_copy(block, target, sems.at[i]))
+        copies[-1].start()
     scale = 1.0 / math.sqrt(HD)
     column = jnp.transpose(jnp.broadcast_to(ids_ref[:, rows : 2 * rows], (HD, rows)))[:, :1]
-    for half in range(2):
-        first = half * some
-        spans = [
-            (before_ref, half * some, rows),
-            (own_ref, 0, rows),
-            (after_ref, 0, some + half * some),
-        ]
-        keys = 2 * rows + some
-        query_pos = lax.broadcasted_iota(jnp.int32, (some, keys), 0) + (first + rows)
-        key_pos = lax.broadcasted_iota(jnp.int32, (some, keys), 1) + first
-        allowed = (column[first : first + some] == ids_ref[:, first : first + keys]) & (
-            jnp.abs(query_pos - key_pos) < rows
+    span = 2 * rows + some
+    allowed = []
+    for first in (0, some):
+        query_pos = lax.broadcasted_iota(jnp.int32, (some, span), 0) + (first + rows)
+        key_pos = lax.broadcasted_iota(jnp.int32, (some, span), 1) + first
+        allowed.append(
+            (column[first : first + some] == ids_ref[:, first : first + span])
+            & (jnp.abs(query_pos - key_pos) < rows)
         )
+    for copy in copies:
+        copy.wait()
+    for half, first in enumerate((0, some)):
         for head in range(q_ref.shape[1] // HD):
             cols = slice(head * HD, (head + 1) * HD)
-            query = q_ref[first : first + some, cols]
-            score = jnp.concatenate(
-                [
-                    lax.dot_general(query, ref[lo:hi, cols], NT, preferred_element_type=jnp.float32)
-                    for ref, lo, hi in spans
-                ],
-                axis=1,
+            score = lax.dot_general(
+                q_ref[first : first + some, cols],
+                keys[first : first + span, cols],
+                NT,
+                preferred_element_type=jnp.float32,
             )
-            score = jnp.where(allowed, score * scale, -jnp.inf)
+            score = jnp.where(allowed[half], score * scale, -jnp.inf)
             weights = jnp.exp(score - jnp.max(score, axis=-1, keepdims=True))
             share = 1.0 / jnp.sum(weights, axis=-1, keepdims=True)
             probs = (weights * share).astype(jnp.bfloat16)
-            total, at = jnp.zeros((some, HD), jnp.float32), 0
-            for ref, lo, hi in spans:
-                total += jnp.dot(
-                    probs[:, at : at + hi - lo],
-                    ref[rows + lo : rows + hi, cols],
-                    preferred_element_type=jnp.float32,
-                )
-                at += hi - lo
-            both[first : first + some, cols] = total.astype(jnp.bfloat16)
-    at = pl.multiple_of(core_ref[0] * some, some)
+            both[first : first + some, cols] = jnp.dot(
+                probs, values[first : first + span, cols], preferred_element_type=jnp.float32
+            ).astype(jnp.bfloat16)
+    at = pl.multiple_of(core * some, some)
     mine_ref[...] = both[pl.ds(at, some), :]
     theirs_ref[...] = both[pl.ds(some - at, some), :]
 
 
-def attention(core, queries, near, ids, *ahead):
+def attention(where, queries, ids, near_keys, near_values, *ahead):
     rows, width = queries.shape
     half = jax.ShapeDtypeStruct((rows // 2, width), jnp.bfloat16)
     return pl.pallas_call(
         attention_kernel,
         out_shape=(half, half),
-        in_specs=[pl.BlockSpec(memory_space=pltpu.SMEM)] + [VMEM] * 5 + [ANY] * len(ahead),
+        in_specs=[pl.BlockSpec(memory_space=pltpu.SMEM), VMEM, VMEM] + [ANY] * (6 + len(ahead)),
         out_specs=(VMEM, VMEM),
-        scratch_shapes=[pltpu.VMEM((rows, width), jnp.bfloat16)],
-        compiler_params=pltpu.CompilerParams(vmem_limit_bytes=63 * 1024 * 1024),
+        scratch_shapes=[pltpu.VMEM((3 * rows, width), jnp.bfloat16)] * 2
+        + [pltpu.VMEM((rows, width), jnp.bfloat16), pltpu.SemaphoreType.DMA((6,))],
+        compiler_params=pltpu.CompilerParams(vmem_limit_bytes=16 * 1024 * 1024),
         name="window_attention",
-    )(core, queries, *near, ids, *ahead)
+    )(where, queries, ids, *near_keys, *near_values, *ahead)
 
 
 def norm_kernel(mine_ref, theirs_ref, own_w, other_w, resid_ref, gain_ref, *refs):
@@ -140,7 +145,7 @@
         ),
         in_specs=[VMEM] * 6 + [ANY] * len(ahead),
         out_specs=(VMEM, VMEM),
-        compiler_params=pltpu.CompilerParams(vmem_limit_bytes=63 * 1024 * 1024),
+        compiler_params=pltpu.CompilerParams(vmem_limit_bytes=16 * 1024 * 1024),
         name="project_and_norm",
     )(mine, theirs, own_w, other_w, resid, gain, *ahead)
 
@@ -169,7 +174,7 @@
         in_specs=[ANY] * 6,
         out_specs=(VMEM, VMEM),
         scratch_shapes=[pltpu.SemaphoreType.DMA((6,))],
-        compiler_params=pltpu.CompilerParams(vmem_limit_bytes=36 * 1024 * 1024),
+        compiler_params=pltpu.CompilerParams(vmem_limit_bytes=12 * 1024 * 1024),
         name="assemble_weights",
     )(*halves)
 
@@ -206,7 +211,7 @@
         out_shape=[jax.ShapeDtypeStruct((rows, width), jnp.bfloat16)] * count,
         in_specs=[pl.BlockSpec(memory_space=pltpu.SMEM)] + [VMEM] * (count + len(gates) + 2),
         out_specs=[VMEM] * count,
-        compiler_params=pltpu.CompilerParams(vmem_limit_bytes=36 * 1024 * 1024),
+        compiler_params=pltpu.CompilerParams(vmem_limit_bytes=24 * 1024 * 1024),
         name="expert_rows",
     )(shard, *blocks, *gates, *weights)
 
@@ -253,25 +258,22 @@
     d2, d3 = flip(after(y2, x3, p1), 1), flip(after(x3, y3, p1), 2)
     px3, py3, px1 = run([after(x3, p1), y3, x1], (13, 14, 5))
 
-    pd2, pd3 = run([after(d2, px3), d3], (11, 15))
+    pd2, pd3 = run([after(d2, px3, d1), d3], (11, 15))
     (pd1,) = run([after(d1, pd2)], (7,))
     to_x3, to_y2, to_d0 = flip(pd3, 2), flip(pd2, 1), flip(pd1, 4)
 
     px3, py2, pd0 = add_small(px3, to_x3), add_small(py2, to_y2), add_small(pd0, to_d0)
-    by_x, by_y = flip(after(px3, to_y2), 1), flip(after(py3, to_x3), 2)
-    to_x0 = flip(after(px1, to_d0), 4)
+    by_x, by_y, to_x0 = flip(px3, 1), flip(py3, 2), flip(px1, 4)
 
     p3, px0 = add_small(p3, by_x, by_y), add_small(px0, to_x0)
-    to_2 = shift(after(p3, to_x0), INWARD)
-    by_x, by_y = flip(after(px2, by_x), 1), flip(after(py2, by_y), 2)
+    to_2, by_x, by_y = shift(p3, INWARD), flip(px2, 1), flip(py2, 2)
 
     p2 = add_small(p2, by_x, by_y, to_2)
-    to_3, to_1 = shift(after(p2, to_2), INWARD), shift(p2, MIDDLE)
-    to_y0, by_y = flip(after(pd0, by_x), 1), flip(after(py1, by_y), 2)
+    to_3, to_1 = shift(p2, INWARD), shift(p2, MIDDLE)
+    to_y0, by_y = flip(pd0, 1), flip(py1, 2)
 
     p3, p1, py0 = add_small(p3, to_3), add_small(p1, by_y, to_1), add_small(py0, to_y0)
-    by_z, by_middle = flip(after(p1, to_3), 4), shift(after(p3, to_1), MIDDLE)
-    by_x, by_y = flip(after(px0, to_y0), 1), flip(after(py0, by_y), 2)
+    by_z, by_middle, by_x, by_y = flip(p1, 4), shift(p3, MIDDLE), flip(px0, 1), flip(py0, 2)
     return add(stream, p0, by_z, by_middle, by_x, by_y)
 
 
@@ -317,29 +319,33 @@
     core = lax.axis_index("exp")
     count = lax.axis_size("seq")
 
-    own = stack(keys, values)
-    before = lax.ppermute(own, "seq", [(i, i + 1) for i in range(count - 1)])
-    after_own = lax.ppermute(own, "seq", [(i + 1, i) for i in range(count - 1)])
+    def halo(part, *arrays):
+        beside = after(flip(part, 1), *arrays)
+        ahead = [(i, i + 2) for i in range(0, count - 2, 2)]
+        back = [(i + 2, i) for i in range(1, count - 2, 2)]
+        return beside, part, lax.ppermute(beside, "seq", ahead + back)
+
+    out_other = lax.ppermute(out_weight, "exp", SWAP)
+    out_own, out_other, stream = fetch(out_weight, out_other, resid)
+    near_keys, near_values = halo(keys), halo(values, out_own)
     chosen = experts.T[:, None, :] == jnp.arange(count, dtype=jnp.int32)[None, :, None]
     all_gates = gather_gates(jnp.sum(jnp.where(chosen, gates.T[:, None, :], 0.0), axis=0))
-    some_gates = all_gates[-2]
     id_pad = jnp.pad(pair_ids, (tok_rows, tok_rows), constant_values=-1)
     ids = lax.dynamic_slice_in_dim(id_pad, shard * tok_rows, 3 * tok_rows, 0)[None, :]
-    out_other = lax.ppermute(out_weight, "exp", SWAP)
     gate_w, up_w = jnp.swapaxes(w_gate[0], 0, 1), jnp.swapaxes(w_up[0], 0, 1)
     gate_other = lax.ppermute(gate_w, "exp", SWAP)
-    ready = (before, after_own, some_gates, ids)
+    ready = (*near_keys, *near_values, all_gates[-1], ids)
     up_other = lax.ppermute(after(up_w, *ready), "exp", SWAP)
     down_other = lax.ppermute(after(w_down[0], *ready), "exp", SWAP)
     halves = [gate_w, gate_other, up_w, up_other, w_down[0], down_other]
 
+    where = jnp.stack([core, shard % 2])
     theirs, mine = attention(
-        core.reshape(1), queries, (before, own, after_own), ids, out_other, gate_other
+        where, queries, ids, near_keys, near_values, gate_other
     )
     received = lax.ppermute(theirs, "exp", SWAP)
-    ahead = (up_other, down_other, all_gates[-1])
     stream, normed = project_and_norm(
-        mine, received, out_weight, out_other, resid, norm_gain[None, :], *ahead
+        mine, received, out_own, out_other, stream, norm_gain[None, :], up_other, down_other
     )
     mixed = expert_layer(normed, stream, shard.reshape(1), all_gates, assemble(halves))
     return mixed.astype(jnp.bfloat16)

time: 201 us -> 207 us (1.030)
  local copies, waits for them, and re-layouts: 6.38 us -> 21.2 us
  waiting for transfers between devices: 90 us -> 84.5 us
  Pallas kernels: 37 us -> 33.1 us
    unnamed x18 -> x54, local copies, waits for them, and re-layouts: 5.01 us -> 21.1 us
    ppermute x30 -> x32, waiting for transfers between devices: 68.2 us -> 59.4 us  [flip(): return lax.ppermute(block, 'seq', [(i, i ^ mask) for i in range(count)])]
    pallas_call x1, Pallas kernels: 4.29 us -> 0.89 us  [project_and_norm(): pl.pallas_call(norm_kernel, out_shape=(jax.ShapeDtypeStruct((rows, width)...]
    ppermute x30 -> x32, starting transfers between devices: 31.9 us -> 29.5 us  [flip(): return lax.ppermute(block, 'seq', [(i, i ^ mask) for i in range(count)])]
    pallas_call x5, Pallas kernels: 22.7 us -> 25.1 us  [expert(): pl.pallas_call(functools.partial(expert_kernel, places, len(gates)), out_...]
  transfers between devices with their start and end apart: 45 -> 47, of which waited for: 27 -> 26; matrix products, arithmetic and copies ran while one was open for 3% -> 2% of each run, Pallas kernels for 16% -> 14%
where the time goes in v7:
time: 207 us; the launch traced here: 204 us
  waiting for transfers between devices  84.5 us (41%)
  starting transfers between devices  59 us (29%)
  Pallas kernels  33.1 us (16%)
  local copies, waits for them, and re-layouts  21.2 us (10%)
  other arithmetic  5.9 us (3%)
    ppermute x32, waiting for transfers between devices, flip(): return lax.ppermute(block, 'seq', [(i, i ^ mask) for i in range(count)])  59.4 us
    ppermute x32, starting transfers between devices, flip(): return lax.ppermute(block, 'seq', [(i, i ^ mask) for i in range(count)])  29.5 us
    pallas_call x5, Pallas kernels, expert(): pl.pallas_call(functools.partial(expert_kernel, places, len(gates)), out_...  25.1 us
    ppermute x8, waiting for transfers between devices, shift(): lax.ppermute(block, 'seq', [(4 * a + i, 4 * b + i) for a, b in pairs for...  23.7 us
    ppermute x8, starting transfers between devices, shift(): lax.ppermute(block, 'seq', [(4 * a + i, 4 * b + i) for a, b in pairs for...  23.1 us
    unnamed x54, local copies, waits for them, and re-layouts  21.1 us
    ppermute x2, starting transfers between devices, halo(): return (beside, part, lax.ppermute(beside, 'seq', ahead + back))  5.84 us
    pallas_call x1, Pallas kernels, attention(): pl.pallas_call(attention_kernel, out_shape=(half, half), in_specs=[pl.Blo...  4.26 us
  transfers between devices with their start and end apart: 47, of which 26 were waited for; matrix products, arithmetic and copies ran while one was open for 2% of the time, Pallas kernels for 14%

profile of v7, /device:TPU:10, one launch (start us, length us, event | category | flops | bytes accessed | tf_op | source)
XLA Modules:
  0.0 204.2 jit_solution(4012800579510903219)
XLA Ops:
  0.5 1.5 collective-permute-start.2
  3.3 3.2 %collective-permute-done.7.refs_5_.refs_7_.refs_4_.refs_3_.refs_2_ = f32[16,128]{1,0:T(8,128)S(1)} collective-permute-done((f32[16,128]{1,0:T(8,128)S(1)}, f32[16,128]{1,0:T(8,128)S(1)}, u32[]{:S(2)}, u32[]{:S(2)}) %collective-permute-start.7) | collective-permute-done | bytes 8224 | tf_op jit(solution)/shard_map/ppermute | solution.py:20
  6.5 2.6 %collective-permute-start.8 = (f32[16,256]{1,0:T(8,128)S(1)}, f32[16,256]{1,0:T(8,128)S(1)}, u32[]{:S(2)}, u32[]{:S(2)}) collective-permute-start(f32[16,256]{1,0:T(8,128)S(1)} %pad_maximum_fusion.2), channel_id=1, source_target_pairs={{0,16},{2,18},{4,20},{6,22},{8,24},{10,26},{12,28},{14,30},{16,0},... | collective-permute-start | bytes 49160 | tf_op jit(solution)/shard_map/ppermute | solution.py:20
  9.3 3.3 %collective-permute-start.1 = (bf16[256,512]{1,0:T(8,128)(2,1)S(1)}, bf16[256,512]{1,0:T(8,128)(2,1)S(1)}, u32[]{:S(2)}, u32[]{:S(2)}) collective-permute-start(bf16[256,512]{1,0:T(8,128)(2,1)S(1)} %collective-permute-done.refs_0_), channel_id=1, source_target_pairs={{0,4},{4,8},{8,12},{12,16},{16,20},{20,24},{24,28},{6,2},{10,6},{1... | collective-permute-start | bytes 786440 | tf_op jit(solution)/shard_map/ppermute | solution.py:326
  12.7 1.6 copy-done.4
  17.0 1.4 copy-done.2
  18.3 2.5 %collective-permute-start.4 = (bf16[256,512]{1,0:T(8,128)(2,1)S(1)}, bf16[256,512]{1,0:T(8,128)(2,1)S(1)}, u32[]{:S(2)}, u32[]{:S(2)}) collective-permute-start(bf16[256,512]{1,0:T(8,128)(2,1)S(1)} %collective-permute-done.2.refs_3_), channel_id=1, source_target_pairs={{0,4},{4,8},{8,12},{12,16},{16,20},{20,24},{24,28},{6,2},{10,6},{1... | collective-permute-start | bytes 786440 | tf_op jit(solution)/shard_map/ppermute | solution.py:326
  21.6 1.5 collective-permute-start.9
  23.1 5.2 %collective-permute-done.9.refs_7_.refs_9_.refs_6_.refs_5_.refs_4_ = f32[16,512]{1,0:T(8,128)S(1)} collective-permute-done((f32[16,512]{1,0:T(8,128)S(1)}, f32[16,512]{1,0:T(8,128)S(1)}, u32[]{:S(2)}, u32[]{:S(2)}) %collective-permute-start.9) | collective-permute-done | bytes 32800 | tf_op jit(solution)/shard_map/ppermute | solution.py:20
  28.3 1.5 collective-permute-start.10
  30.0 2.6 %collective-permute-done.10.refs_8_.refs_10_.refs_7_.refs_6_.refs_5_ = f32[16,1024]{1,0:T(8,128)S(1)} collective-permute-done((f32[16,1024]{1,0:T(8,128)S(1)}, f32[16,1024]{1,0:T(8,128)S(1)}, u32[]{:S(2)}, u32[]{:S(2)}) %collective-permute-start.10) | collective-permute-done | bytes 65568 | tf_op jit(solution)/shard_map/ppermute | solution.py:20
  41.4 4.3 %window_attention.1 = (bf16[128,512]{1,0:T(8,128)(2,1)S(1)}, bf16[128,512]{1,0:T(8,128)(2,1)S(1)}) custom-call(s32[2]{0:T(128)S(1)} %pad_add_fusion.where_ref, bf16[256,512]{1,0:T(8,128)(2,1)S(1)} %copy-done.14, s32[1,768]{1,0:T(1,128)S(1)} %broadcast_in_dim.21.ids_ref, bf16[256,512]{1,0:T(8,128)(2,1)S(1)} %copy-done.18, bf16[256,512]{1,0:T(8,128)(2,1)S(1)} %copy-done.15, ...), custom_call_target="tpu_custom_call" | custom-call | tf_op jit(solution)/shard_map/window_attention/pallas_call | solution.py:116
  47.1 1.6 copy-done.3
  50.6 5.0 %collective-permute-start.14 = (bf16[128,2048]{1,0:T(8,128)(2,1)S(1)}, bf16[128,2048]{1,0:T(8,128)(2,1)}, u32[]{:S(2)}, u32[]{:S(2)}) collective-permute-start(bf16[128,2048]{1,0:T(8,128)(2,1)S(1)} %get-tuple-element.62.refs_0_), channel_id=1, source_target_pairs={{8,16},{10,18},{12,20},{14,22},{16,8},{18,10},{20,12},{22,14},{9,1... | collective-permute-start | bytes 1572872 | tf_op jit(solution)/shard_map/ppermute | solution.py:231
  55.7 1.5 collective-permute-start.17
  58.0 6.6 %collective-permute-done.13.refs_0_ = bf16[128,2048]{1,0:T(8,128)(2,1)S(1)} collective-permute-done((bf16[128,2048]{1,0:T(8,128)(2,1)S(1)}, bf16[128,2048]{1,0:T(8,128)(2,1)S(1)}, u32[]{:S(2)}, u32[]{:S(2)}) %collective-permute-start.13) | collective-permute-done | bytes 524320 | tf_op jit(solution)/shard_map/ppermute | solution.py:20
  64.5 3.1 %collective-permute-done.14 = bf16[128,2048]{1,0:T(8,128)(2,1)} collective-permute-done((bf16[128,2048]{1,0:T(8,128)(2,1)S(1)}, bf16[128,2048]{1,0:T(8,128)(2,1)}, u32[]{:S(2)}, u32[]{:S(2)}) %collective-permute-start.14) | collective-permute-done | bytes 524320 | tf_op jit(solution)/shard_map/ppermute | solution.py:231
  67.7 3.6 %collective-permute-start.15 = (bf16[128,2048]{1,0:T(8,128)(2,1)S(1)}, bf16[128,2048]{1,0:T(8,128)(2,1)}, u32[]{:S(2)}, u32[]{:S(2)}) collective-permute-start(bf16[128,2048]{1,0:T(8,128)(2,1)S(1)} %collective-permute-done.13.refs_0_), channel_id=1, source_target_pairs={{8,16},{10,18},{12,20},{14,22},{16,8},{18,10},{20,12},{22,14},{9,1... | collective-permute-start | bytes 1572872 | tf_op jit(solution)/shard_map/ppermute | solution.py:231
  71.3 2.1 %collective-permute-start.16 = (bf16[128,2048]{1,0:T(8,128)(2,1)}, bf16[128,2048]{1,0:T(8,128)(2,1)}, u32[]{:S(2)}, u32[]{:S(2)}) collective-permute-start(bf16[128,2048]{1,0:T(8,128)(2,1)} %collective-permute-done.14), channel_id=1, source_target_pairs={{8,0},{10,2},{12,4},{14,6},{16,24},{18,26},{20,28},{22,30},{9,1},{... | collective-permute-start | bytes 1572872 | tf_op jit(solution)/shard_map/ppermute | solution.py:231
  74.2 1.4 collective-permute-start.19
  78.3 2.5 %assemble_weights.1 = (bf16[1408,2048]{1,0:T(8,128)(2,1)S(1)}, bf16[704,2048]{1,0:T(8,128)(2,1)S(1)}) custom-call(bf16[352,2048]{1,0:T(8,128)(2,1)} %bitcast.3.refs_0_, bf16[352,2048]{1,0:T(8,128)(2,1)S(1)} %collective-permute-done.5.refs_6_.refs_1_, bf16[352,2048]{1,0:T(8,128)(2,1)S(1)} %bitcast.14, ...), custom_call_target="tpu_custom_call" | custom-call | tf_op jit(solution)/shard_map/assemble_weights/pallas_call | solution.py:168
  80.9 1.9 collective-permute-done.15
  83.2 4.6 %collective-permute-start.23 = (bf16[128,2048]{1,0:T(8,128)(2,1)}, bf16[128,2048]{1,0:T(8,128)(2,1)S(1)}, u32[]{:S(2)}, u32[]{:S(2)}) collective-permute-start(bf16[128,2048]{1,0:T(8,128)(2,1)} %collective-permute-done.15), channel_id=1, source_target_pairs={{8,0},{10,2},{12,4},{14,6},{16,24},{18,26},{20,28},{22,30},{9,1},{... | collective-permute-start | bytes 1572872 | tf_op jit(solution)/shard_map/ppermute | solution.py:231
  89.0 1.5 collective-permute-start.21
  90.5 6.3 %expert_rows.5 = (bf16[128,2048]{1,0:T(8,128)(2,1)S(1)}, bf16[128,2048]{1,0:T(8,128)(2,1)S(1)}, bf16[128,2048]{1,0:T(8,128)(2,1)S(1)}, bf16[128,2048]{1,0:T(8,128)(2,1)S(1)}) custom-call(s32[1]{0:T(128)} %bitcast.10.shard_ref, bf16[128,2048]{1,0:T(8,128)(2,1)S(1)} %copy-done.13, bf16[128,2048]{1,0:T(8,128)(2,1)S(1)} %copy-done.11, ...), custom_call_target="tpu_custom_call" | custom-call | tf_op jit(solution)/shard_map/expert_rows/pallas_call | solution.py:209
  97.5 2.4 %collective-permute-start.29 = (bf16[128,2048]{1,0:T(8,128)(2,1)S(1)}, bf16[128,2048]{1,0:T(8,128)(2,1)S(1)}, u32[]{:S(2)}, u32[]{:S(2)}) collective-permute-start(bf16[128,2048]{1,0:T(8,128)(2,1)S(1)} %copy-done.11), channel_id=1, source_target_pairs={{0,8},{2,10},{4,12},{6,14},{8,0},{10,2},{12,4},{14,6},{16,24},{18,... | collective-permute-start | bytes 1572872 | tf_op jit(solution)/shard_map/ppermute | solution.py:20
  101.0 1.5 collective-permute-start.26
  102.5 8.6 %expert_rows.6 = (bf16[128,2048]{1,0:T(8,128)(2,1)S(1)}, bf16[128,2048]{1,0:T(8,128)(2,1)S(1)}, bf16[128,2048]{1,0:T(8,128)(2,1)S(1)}, bf16[128,2048]{1,0:T(8,12...) custom-call(s32[1]{0:T(128)} %bitcast.10.shard_ref, ...), custom_call_target="tpu_custom_call" | custom-call | tf_op jit(solution)/shard_map/expert_rows/pallas_call | solution.py:209
  111.2 2.0 collective-permute-done.26.refs_0_
  113.2 1.4 collective-permute-start.27
  114.6 5.1 %expert_rows.7 = (bf16[128,2048]{1,0:T(8,128)(2,1)S(1)}, bf16[128,2048]{1,0:T(8,128)(2,1)S(1)}, bf16[128,2048]{1,0:T(8,128)(2,1)S(1)}) custom-call(s32[1]{0:T(128)} %bitcast.10.shard_ref, bf16[128,2048]{1,0:T(8,128)(2,1)S(1)} %collective-permute-done.26.refs_0_, bf16[128,2048]{1,0:T(8,128)(2,1)S(1)} %collective-permute-done.28.refs_1_, ...), custom_call_target="tpu_custom_call" | custom-call | tf_op jit(solution)/shard_map/expert_rows/pallas_call | solution.py:209
  119.7 1.9 collective-permute-done.30.refs_0_
  121.6 1.5 collective-permute-done.27.refs_0_
  124.3 2.7 %expert_rows.8 = (bf16[128,2048]{1,0:T(8,128)(2,1)S(1)}, bf16[128,2048]{1,0:T(8,128)(2,1)S(1)}) custom-call(s32[1]{0:T(128)} %bitcast.10.shard_ref, bf16[128,2048]{1,0:T(8,128)(2,1)S(1)} %collective-permute-done.27.refs_0_, bf16[128,2048]{1,0:T(8,128)(2,1)S(1)} %collective-permute-done.31.refs_1_, ...), custom_call_target="tpu_custom_call" | custom-call | tf_op jit(solution)/shard_map/expert_rows/pallas_call | solution.py:209
  129.7 12.2 %collective-permute-done.34 = bf16[128,2048]{1,0:T(8,128)(2,1)S(1)} collective-permute-done((bf16[128,2048]{1,0:T(8,128)(2,1)S(1)}, bf16[128,2048]{1,0:T(8,128)(2,1)S(1)}, u32[]{:S(2)}, u32[]{:S(2)}) %collective-permute-start.34) | collective-permute-done | bytes 524320 | tf_op jit(solution)/shard_map/ppermute | solution.py:20
  142.7 1.4 collective-permute-start.25
  144.1 2.4 %expert_rows.9 = bf16[128,2048]{1,0:T(8,128)(2,1)S(1)} custom-call(s32[1]{0:T(128)} %bitcast.10.shard_ref, bf16[128,2048]{1,0:T(8,128)(2,1)S(1)} %collective-permute-done.30.refs_0_, f32[16,128]{1,0:T(8,128)S(1)} %select_reduce_fusion.refs_4_.refs_6_.refs_3_.refs_2_.refs_1_, f32[16,128]{1,0:T(8,128)S(1)} %collective-permute-done.7.refs_5_.refs_7_.refs_4_.refs_3_.refs_2_, ...), custom_call_target="tpu_custom_call" | custom-call | tf_op jit(solution)/shard_map/expert_rows/pallas_call | solution.py:209
  147.8 5.3 %collective-permute-done.36 = bf16[128,2048]{1,0:T(8,128)(2,1)S(1)} collective-permute-done((bf16[128,2048]{1,0:T(8,128)(2,1)S(1)}, bf16[128,2048]{1,0:T(8,128)(2,1)S(1)}, u32[]{:S(2)}, u32[]{:S(2)}) %collective-permute-start.36) | collective-permute-done | bytes 524320 | tf_op jit(solution)/shard_map/ppermute | solution.py:20
  156.7 4.7 %collective-permute-done.44 = bf16[128,2048]{1,0:T(8,128)(2,1)S(1)} collective-permute-done((bf16[128,2048]{1,0:T(8,128)(2,1)S(1)}, bf16[128,2048]{1,0:T(8,128)(2,1)S(1)}, u32[]{:S(2)}, u32[]{:S(2)}) %collective-permute-start.44) | collective-permute-done | bytes 524320 | tf_op jit(solution)/shard_map/ppermute | solution.py:20
  161.6 2.9 %collective-permute-done.25 = bf16[128,2048]{1,0:T(8,128)(2,1)S(1)} collective-permute-done((bf16[128,2048]{1,0:T(8,128)(2,1)S(1)}, bf16[128,2048]{1,0:T(8,128)(2,1)S(1)}, u32[]{:S(2)}, u32[]{:S(2)}) %collective-permute-start.25) | collective-permute-done | bytes 524320 | tf_op jit(solution)/shard_map/ppermute | solution.py:20
  165.8 6.8 %collective-permute-done.37 = bf16[128,2048]{1,0:T(8,128)(2,1)S(1)} collective-permute-done((bf16[128,2048]{1,0:T(8,128)(2,1)S(1)}, bf16[128,2048]{1,0:T(8,128)(2,1)S(1)}, u32[]{:S(2)}, u32[]{:S(2)}) %collective-permute-start.37) | collective-permute-done | bytes 524320 | tf_op jit(solution)/shard_map/ppermute | solution.py:231
  174.3 6.4 %collective-permute-done.42 = bf16[128,2048]{1,0:T(8,128)(2,1)S(1)} collective-permute-done((bf16[128,2048]{1,0:T(8,128)(2,1)S(1)}, bf16[128,2048]{1,0:T(8,128)(2,1)S(1)}, u32[]{:S(2)}, u32[]{:S(2)}) %collective-permute-start.42) | collective-permute-done | bytes 524320 | tf_op jit(solution)/shard_map/ppermute | solution.py:20
  182.1 2.4 %collective-permute-start.38 = (bf16[128,2048]{1,0:T(8,128)(2,1)S(1)}, bf16[128,2048]{1,0:T(8,128)(2,1)S(1)}, u32[]{:S(2)}, u32[]{:S(2)}) collective-permute-start(bf16[128,2048]{1,0:T(8,128)(2,1)S(1)} %add_convert_fusion.6), channel_id=1, source_target_pairs={{8,16},{10,18},{12,20},{14,22},{16,8},{18,10},{20,12},{22,14},{9,1... | collective-permute-start | bytes 1572872 | tf_op jit(solution)/shard_map/ppermute | solution.py:231
  184.6 1.7 collective-permute-start.46
  186.3 2.9 %collective-permute-done.40 = bf16[128,2048]{1,0:T(8,128)(2,1)S(1)} collective-permute-done((bf16[128,2048]{1,0:T(8,128)(2,1)S(1)}, bf16[128,2048]{1,0:T(8,128)(2,1)S(1)}, u32[]{:S(2)}, u32[]{:S(2)}) %collective-permute-start.40) | collective-permute-done | bytes 524320 | tf_op jit(solution)/shard_map/ppermute | solution.py:231
  189.4 2.8 %collective-permute-start.41 = (bf16[128,2048]{1,0:T(8,128)(2,1)S(1)}, bf16[128,2048]{1,0:T(8,128)(2,1)S(1)}, u32[]{:S(2)}, u32[]{:S(2)}) collective-permute-start(bf16[128,2048]{1,0:T(8,128)(2,1)S(1)} %add_convert_fusion.4), channel_id=1, source_target_pairs={{8,16},{10,18},{12,20},{14,22},{16,8},{18,10},{20,12},{22,14},{9,1... | collective-permute-start | bytes 1572872 | tf_op jit(solution)/shard_map/ppermute | solution.py:231
  193.9 6.6 %collective-permute-done.41 = bf16[128,2048]{1,0:T(8,128)(2,1)S(1)} collective-permute-done((bf16[128,2048]{1,0:T(8,128)(2,1)S(1)}, bf16[128,2048]{1,0:T(8,128)(2,1)S(1)}, u32[]{:S(2)}, u32[]{:S(2)}) %collective-permute-start.41) | collective-permute-done | bytes 524320 | tf_op jit(solution)/shard_map/ppermute | solution.py:231
  200.5 2.4 %collective-permute-done.39 = bf16[128,2048]{1,0:T(8,128)(2,1)S(1)} collective-permute-done((bf16[128,2048]{1,0:T(8,128)(2,1)S(1)}, bf16[128,2048]{1,0:T(8,128)(2,1)S(1)}, u32[]{:S(2)}, u32[]{:S(2)}) %collective-permute-start.39) | collective-permute-done | bytes 524320 | tf_op jit(solution)/shard_map/ppermute | solution.py:20
  (128 shorter events, 42.8 us)
Async XLA Ops:
  0.0 12.6 %collective-permute-start.3 = (bf16[512,2048]{1,0:T(8,128)(2,1)}, bf16[512,2048]{1,0:T(8,128)(2,1)S(1)}, u32[]{:S(2)}, u32[]{:S(2)}) collective-permute-start(bf16[512,2048]{1,0:T(8,128)(2,1)} %own_ref.1), channel_id=1, source_target_pairs={{0,1},{1,0},{2,3},{3,2},{4,5},{5,4},{6,7},{7,6},{8,9},{9,8},{10,11... | collective-permute-start | bytes 6291464 | tf_op jit(solution)/shard_map/ppermute | solution.py:328
  0.0 9.3 %collective-permute-start = (bf16[256,512]{1,0:T(8,128)(2,1)}, bf16[256,512]{1,0:T(8,128)(2,1)S(1)}, u32[]{:S(2)}, u32[]{:S(2)}) collective-permute-start(bf16[256,512]{1,0:T(8,128)(2,1)} %refs_1_.1), channel_id=1, source_target_pairs={{0,2},{2,0},{4,6},{6,4},{8,10},{10,8},{12,14},{14,12},{16,18},{18,... | collective-permute-start | bytes 786440 | tf_op jit(solution)/shard_map/ppermute | solution.py:20
  0.5 17.8 %collective-permute-start.2 = (bf16[256,512]{1,0:T(8,128)(2,1)}, bf16[256,512]{1,0:T(8,128)(2,1)S(1)}, u32[]{:S(2)}, u32[]{:S(2)}) collective-permute-start(bf16[256,512]{1,0:T(8,128)(2,1)} %refs_4_.1), channel_id=1, source_target_pairs={{0,2},{2,0},{4,6},{6,4},{8,10},{10,8},{12,14},{14,12},{16,18},{18,... | collective-permute-start | bytes 786440 | tf_op jit(solution)/shard_map/ppermute | solution.py:20
  2.7 3.7 %collective-permute-start.7 = (f32[16,128]{1,0:T(8,128)S(1)}, f32[16,128]{1,0:T(8,128)S(1)}, u32[]{:S(2)}, u32[]{:S(2)}) collective-permute-start(f32[16,128]{1,0:T(8,128)S(1)} %select_reduce_fusion.refs_4_.refs_6_.refs_3_.refs_2_.refs_1_), channel_id=1, source_target_pairs={{0,8},{2,10},{4,12},{6,14},{8,0},{10,2},{12,4},{14,6},{16,24},{18,... | collective-permute-start | bytes 24584 | tf_op jit(solution)/shard_map/ppermute | solution.py:20
  6.5 15.1 %collective-permute-start.8 = (f32[16,256]{1,0:T(8,128)S(1)}, f32[16,256]{1,0:T(8,128)S(1)}, u32[]{:S(2)}, u32[]{:S(2)}) collective-permute-start(f32[16,256]{1,0:T(8,128)S(1)} %pad_maximum_fusion.2), channel_id=1, source_target_pairs={{0,16},{2,18},{4,20},{6,22},{8,24},{10,26},{12,28},{14,30},{16,0},... | collective-permute-start | bytes 49160 | tf_op jit(solution)/shard_map/ppermute | solution.py:20
  9.3 23.3 %collective-permute-start.1 = (bf16[256,512]{1,0:T(8,128)(2,1)S(1)}, bf16[256,512]{1,0:T(8,128)(2,1)S(1)}, u32[]{:S(2)}, u32[]{:S(2)}) collective-permute-start(bf16[256,512]{1,0:T(8,128)(2,1)S(1)} %collective-permute-done.refs_0_), channel_id=1, source_target_pairs={{0,4},{4,8},{8,12},{12,16},{16,20},{20,24},{24,28},{6,2},{10,6},{1... | collective-permute-start | bytes 786440 | tf_op jit(solution)/shard_map/ppermute | solution.py:326
  18.3 28.8 %copy-start.25 = (f32[2048]{0:T(1024)S(1)}, f32[2048]{0:T(1024)}, u32[]{:S(2)}) copy-start(f32[2048]{0:T(1024)} %param.18) | copy-start | bytes 24580
  18.3 15.0 %collective-permute-start.4 = (bf16[256,512]{1,0:T(8,128)(2,1)S(1)}, bf16[256,512]{1,0:T(8,128)(2,1)S(1)}, u32[]{:S(2)}, u32[]{:S(2)}) collective-permute-start(bf16[256,512]{1,0:T(8,128)(2,1)S(1)} %collective-permute-done.2.refs_3_), channel_id=1, source_target_pairs={{0,4},{4,8},{8,12},{12,16},{16,20},{20,24},{24,28},{6,2},{10,6},{1... | collective-permute-start | bytes 786440 | tf_op jit(solution)/shard_map/ppermute | solution.py:326
  21.6 6.7 %collective-permute-start.9 = (f32[16,512]{1,0:T(8,128)S(1)}, f32[16,512]{1,0:T(8,128)S(1)}, u32[]{:S(2)}, u32[]{:S(2)}) collective-permute-start(f32[16,512]{1,0:T(8,128)S(1)} %pad_maximum_fusion.1), channel_id=1, source_target_pairs={{0,4},{2,6},{4,0},{6,2},{8,12},{10,14},{12,8},{14,10},{16,20},{18,... | collective-permute-start | bytes 98312 | tf_op jit(solution)/shard_map/ppermute | solution.py:20
  23.1 11.5 %collective-permute-start.5 = (bf16[352,2048]{1,0:T(8,128)(2,1)}, bf16[352,2048]{1,0:T(8,128)(2,1)S(1)}, u32[]{:S(2)}, u32[]{:S(2)}) collective-permute-start(bf16[352,2048]{1,0:T(8,128)(2,1)} %bitcast.3.refs_0_), channel_id=1, source_target_pairs={{0,1},{1,0},{2,3},{3,2},{4,5},{5,4},{6,7},{7,6},{8,9},{9,8},{10,11... | collective-permute-start | bytes 4325384 | tf_op jit(solution)/shard_map/ppermute | solution.py:336
  28.3 4.3 %collective-permute-start.10 = (f32[16,1024]{1,0:T(8,128)S(1)}, f32[16,1024]{1,0:T(8,128)S(1)}, u32[]{:S(2)}, u32[]{:S(2)}) collective-permute-start(f32[16,1024]{1,0:T(8,128)S(1)} %pad_maximum_fusion), channel_id=1, source_target_pairs={{0,2},{2,0},{4,6},{6,4},{8,10},{10,8},{12,14},{14,12},{16,18},{18,... | collective-permute-start | bytes 196616 | tf_op jit(solution)/shard_map/ppermute | solution.py:20
  34.0 13.1 %collective-permute-start.11 = (bf16[352,2048]{1,0:T(8,128)(2,1)}, bf16[352,2048]{1,0:T(8,128)(2,1)S(1)}, u32[]{:S(2)}, u32[]{:S(2)}) collective-permute-start(bf16[352,2048]{1,0:T(8,128)(2,1)} %bitcast.13), channel_id=1, source_target_pairs={{0,1},{1,0},{2,3},{3,2},{4,5},{5,4},{6,7},{7,6},{8,9},{9,8},{10,11... | collective-permute-start | bytes 4325384 | tf_op jit(solution)/shard_map/ppermute | solution.py:338
  34.0 13.1 %collective-permute-start.12 = (bf16[352,2048]{1,0:T(8,128)(2,1)}, bf16[352,2048]{1,0:T(8,128)(2,1)}, u32[]{:S(2)}, u32[]{:S(2)}) collective-permute-start(bf16[352,2048]{1,0:T(8,128)(2,1)} %bitcast.15), channel_id=1, source_target_pairs={{0,1},{1,0},{2,3},{3,2},{4,5},{5,4},{6,7},{7,6},{8,9},{9,8},{10,11... | collective-permute-start | bytes 4325384 | tf_op jit(solution)/shard_map/ppermute | solution.py:339
  45.6 1.4 collective-permute-start.6
  50.6 14.0 %collective-permute-start.13 = (bf16[128,2048]{1,0:T(8,128)(2,1)S(1)}, bf16[128,2048]{1,0:T(8,128)(2,1)S(1)}, u32[]{:S(2)}, u32[]{:S(2)}) collective-permute-start(bf16[128,2048]{1,0:T(8,128)(2,1)S(1)} %get-tuple-element.62.refs_0_), channel_id=1, source_target_pairs={{0,8},{2,10},{4,12},{6,14},{8,0},{10,2},{12,4},{14,6},{16,24},{18,... | collective-permute-start | bytes 1572872 | tf_op jit(solution)/shard_map/ppermute | solution.py:20
  50.6 17.1 %collective-permute-start.14 = (bf16[128,2048]{1,0:T(8,128)(2,1)S(1)}, bf16[128,2048]{1,0:T(8,128)(2,1)}, u32[]{:S(2)}, u32[]{:S(2)}) collective-permute-start(bf16[128,2048]{1,0:T(8,128)(2,1)S(1)} %get-tuple-element.62.refs_0_), channel_id=1, source_target_pairs={{8,16},{10,18},{12,20},{14,22},{16,8},{18,10},{20,12},{22,14},{9,1... | collective-permute-start | bytes 1572872 | tf_op jit(solution)/shard_map/ppermute | solution.py:231
  55.6 17.8 %collective-permute-start.18 = (bf16[128,2048]{1,0:T(8,128)(2,1)S(1)}, bf16[128,2048]{1,0:T(8,128)(2,1)}, u32[]{:S(2)}, u32[]{:S(2)}) collective-permute-start(bf16[128,2048]{1,0:T(8,128)(2,1)S(1)} %get-tuple-element.62.refs_0_), channel_id=1, source_target_pairs={{0,4},{2,6},{4,0},{6,2},{8,12},{10,14},{12,8},{14,10},{16,20},{18,... | collective-permute-start | bytes 1572872 | tf_op jit(solution)/shard_map/ppermute | solution.py:20
  55.7 17.7 %collective-permute-start.17 = (bf16[128,2048]{1,0:T(8,128)(2,1)S(1)}, bf16[128,2048]{1,0:T(8,128)(2,1)S(1)}, u32[]{:S(2)}, u32[]{:S(2)}) collective-permute-start(bf16[128,2048]{1,0:T(8,128)(2,1)S(1)} %get-tuple-element.62.refs_0_), channel_id=1, source_target_pairs={{0,2},{2,0},{4,6},{6,4},{8,10},{10,8},{12,14},{14,12},{16,18},{18,... | collective-permute-start | bytes 1572872 | tf_op jit(solution)/shard_map/ppermute | solution.py:20
  67.7 15.1 %collective-permute-start.15 = (bf16[128,2048]{1,0:T(8,128)(2,1)S(1)}, bf16[128,2048]{1,0:T(8,128)(2,1)}, u32[]{:S(2)}, u32[]{:S(2)}) collective-permute-start(bf16[128,2048]{1,0:T(8,128)(2,1)S(1)} %collective-permute-done.13.refs_0_), channel_id=1, source_target_pairs={{8,16},{10,18},{12,20},{14,22},{16,8},{18,10},{20,12},{22,14},{9,1... | collective-permute-start | bytes 1572872 | tf_op jit(solution)/shard_map/ppermute | solution.py:231
  71.3 11.9 %collective-permute-start.16 = (bf16[128,2048]{1,0:T(8,128)(2,1)}, bf16[128,2048]{1,0:T(8,128)(2,1)}, u32[]{:S(2)}, u32[]{:S(2)}) collective-permute-start(bf16[128,2048]{1,0:T(8,128)(2,1)} %collective-permute-done.14), channel_id=1, source_target_pairs={{8,0},{10,2},{12,4},{14,6},{16,24},{18,26},{20,28},{22,30},{9,1},{... | collective-permute-start | bytes 1572872 | tf_op jit(solution)/shard_map/ppermute | solution.py:231
  74.2 14.7 %collective-permute-start.19 = (bf16[128,2048]{1,0:T(8,128)(2,1)}, bf16[128,2048]{1,0:T(8,128)(2,1)}, u32[]{:S(2)}, u32[]{:S(2)}) collective-permute-start(bf16[128,2048]{1,0:T(8,128)(2,1)} %collective-permute-done.18.refs_2_), channel_id=1, source_target_pairs={{0,2},{2,0},{4,6},{6,4},{8,10},{10,8},{12,14},{14,12},{16,18},{18,... | collective-permute-start | bytes 1572872 | tf_op jit(solution)/shard_map/ppermute | solution.py:20
  75.6 14.8 %collective-permute-start.20 = (bf16[128,2048]{1,0:T(8,128)(2,1)S(1)}, bf16[128,2048]{1,0:T(8,128)(2,1)}, u32[]{:S(2)}, u32[]{:S(2)}) collective-permute-start(bf16[128,2048]{1,0:T(8,128)(2,1)S(1)} %collective-permute-done.13.refs_0_), channel_id=1, source_target_pairs={{0,4},{2,6},{4,0},{6,2},{8,12},{10,14},{12,8},{14,10},{16,20},{18,... | collective-permute-start | bytes 1572872 | tf_op jit(solution)/shard_map/ppermute | solution.py:20
  83.2 14.3 %collective-permute-start.23 = (bf16[128,2048]{1,0:T(8,128)(2,1)}, bf16[128,2048]{1,0:T(8,128)(2,1)S(1)}, u32[]{:S(2)}, u32[]{:S(2)}) collective-permute-start(bf16[128,2048]{1,0:T(8,128)(2,1)} %collective-permute-done.15), channel_id=1, source_target_pairs={{8,0},{10,2},{12,4},{14,6},{16,24},{18,26},{20,28},{22,30},{9,1},{... | collective-permute-start | bytes 1572872 | tf_op jit(solution)/shard_map/ppermute | solution.py:231
  89.0 12.1 %collective-permute-start.21 = (bf16[128,2048]{1,0:T(8,128)(2,1)S(1)}, bf16[128,2048]{1,0:T(8,128)(2,1)S(1)}, u32[]{:S(2)}, u32[]{:S(2)}) collective-permute-start(bf16[128,2048]{1,0:T(8,128)(2,1)S(1)} %broadcast_select_fusion.1.refs_2_), channel_id=1, source_target_pairs={{0,2},{2,0},{4,6},{6,4},{8,10},{10,8},{12,14},{14,12},{16,18},{18,... | collective-permute-start | bytes 1572872 | tf_op jit(solution)/shard_map/ppermute | solution.py:20
  90.4 12.1 %collective-permute-start.22 = (bf16[128,2048]{1,0:T(8,128)(2,1)S(1)}, bf16[128,2048]{1,0:T(8,128)(2,1)S(1)}, u32[]{:S(2)}, u32[]{:S(2)}) collective-permute-start(bf16[128,2048]{1,0:T(8,128)(2,1)S(1)} %broadcast_select_fusion.1.refs_2_), channel_id=1, source_target_pairs={{0,4},{2,6},{4,0},{6,2},{8,12},{10,14},{12,8},{14,10},{16,20},{18,... | collective-permute-start | bytes 1572872 | tf_op jit(solution)/shard_map/ppermute | solution.py:20
  97.5 13.6 %collective-permute-start.29 = (bf16[128,2048]{1,0:T(8,128)(2,1)S(1)}, bf16[128,2048]{1,0:T(8,128)(2,1)S(1)}, u32[]{:S(2)}, u32[]{:S(2)}) collective-permute-start(bf16[128,2048]{1,0:T(8,128)(2,1)S(1)} %copy-done.11), channel_id=1, source_target_pairs={{0,8},{2,10},{4,12},{6,14},{8,0},{10,2},{12,4},{14,6},{16,24},{18,... | collective-permute-start | bytes 1572872 | tf_op jit(solution)/shard_map/ppermute | solution.py:20
  101.0 12.2 %collective-permute-start.26 = (bf16[128,2048]{1,0:T(8,128)(2,1)S(1)}, bf16[128,2048]{1,0:T(8,128)(2,1)S(1)}, u32[]{:S(2)}, u32[]{:S(2)}) collective-permute-start(bf16[128,2048]{1,0:T(8,128)(2,1)S(1)} %broadcast_select_fusion.refs_5_), channel_id=1, source_target_pairs={{0,2},{2,0},{4,6},{6,4},{8,10},{10,8},{12,14},{14,12},{16,18},{18,... | collective-permute-start | bytes 1572872 | tf_op jit(solution)/shard_map/ppermute | solution.py:20
  102.5 12.1 %collective-permute-start.28 = (bf16[128,2048]{1,0:T(8,128)(2,1)S(1)}, bf16[128,2048]{1,0:T(8,128)(2,1)S(1)}, u32[]{:S(2)}, u32[]{:S(2)}) collective-permute-start(bf16[128,2048]{1,0:T(8,128)(2,1)S(1)} %broadcast_select_fusion.refs_5_), channel_id=1, source_target_pairs={{0,4},{2,6},{4,0},{6,2},{8,12},{10,14},{12,8},{14,10},{16,20},{18,... | collective-permute-start | bytes 1572872 | tf_op jit(solution)/shard_map/ppermute | solution.py:20
  111.1 10.5 %collective-permute-start.30 = (bf16[128,2048]{1,0:T(8,128)(2,1)}, bf16[128,2048]{1,0:T(8,128)(2,1)S(1)}, u32[]{:S(2)}, u32[]{:S(2)}) collective-permute-start(bf16[128,2048]{1,0:T(8,128)(2,1)} %collective-permute-done.19.refs_3_), channel_id=1, source_target_pairs={{0,8},{2,10},{4,12},{6,14},{8,0},{10,2},{12,4},{14,6},{16,24},{18,... | collective-permute-start | bytes 1572872 | tf_op jit(solution)/shard_map/ppermute | solution.py:20
  113.2 9.9 %collective-permute-start.27 = (bf16[128,2048]{1,0:T(8,128)(2,1)S(1)}, bf16[128,2048]{1,0:T(8,128)(2,1)S(1)}, u32[]{:S(2)}, u32[]{:S(2)}) collective-permute-start(bf16[128,2048]{1,0:T(8,128)(2,1)S(1)} %collective-permute-done.22.refs_4_), channel_id=1, source_target_pairs={{0,2},{2,0},{4,6},{6,4},{8,10},{10,8},{12,14},{14,12},{16,18},{18,... | collective-permute-start | bytes 1572872 | tf_op jit(solution)/shard_map/ppermute | solution.py:20
  114.6 9.7 %collective-permute-start.31 = (bf16[128,2048]{1,0:T(8,128)(2,1)S(1)}, bf16[128,2048]{1,0:T(8,128)(2,1)S(1)}, u32[]{:S(2)}, u32[]{:S(2)}) collective-permute-start(bf16[128,2048]{1,0:T(8,128)(2,1)S(1)} %collective-permute-done.26.refs_0_), channel_id=1, source_target_pairs={{0,4},{2,6},{4,0},{6,2},{8,12},{10,14},{12,8},{14,10},{16,20},{18,... | collective-permute-start | bytes 1572872 | tf_op jit(solution)/shard_map/ppermute | solution.py:20
  127.0 14.9 %collective-permute-start.34 = (bf16[128,2048]{1,0:T(8,128)(2,1)S(1)}, bf16[128,2048]{1,0:T(8,128)(2,1)S(1)}, u32[]{:S(2)}, u32[]{:S(2)}) collective-permute-start(bf16[128,2048]{1,0:T(8,128)(2,1)S(1)} %get-tuple-element.88), channel_id=1, source_target_pairs={{0,4},{2,6},{4,0},{6,2},{8,12},{10,14},{12,8},{14,10},{16,20},{18,... | collective-permute-start | bytes 1572872 | tf_op jit(solution)/shard_map/ppermute | solution.py:20
  127.3 19.5 %collective-permute-start.32 = (bf16[128,2048]{1,0:T(8,128)(2,1)S(1)}, bf16[128,2048]{1,0:T(8,128)(2,1)S(1)}, u32[]{:S(2)}, u32[]{:S(2)}) collective-permute-start(bf16[128,2048]{1,0:T(8,128)(2,1)S(1)} %get-tuple-element.86), channel_id=1, source_target_pairs={{0,2},{2,0},{4,6},{6,4},{8,10},{10,8},{12,14},{14,12},{16,18},{18,... | collective-permute-start | bytes 1572872 | tf_op jit(solution)/shard_map/ppermute | solution.py:20
  128.6 24.6 %collective-permute-start.36 = (bf16[128,2048]{1,0:T(8,128)(2,1)S(1)}, bf16[128,2048]{1,0:T(8,128)(2,1)S(1)}, u32[]{:S(2)}, u32[]{:S(2)}) collective-permute-start(bf16[128,2048]{1,0:T(8,128)(2,1)S(1)} %get-tuple-element.89), channel_id=1, source_target_pairs={{0,4},{2,6},{4,0},{6,2},{8,12},{10,14},{12,8},{14,10},{16,20},{18,... | collective-permute-start | bytes 1572872 | tf_op jit(solution)/shard_map/ppermute | solution.py:20
  142.0 12.0 %collective-permute-start.35 = (bf16[128,2048]{1,0:T(8,128)(2,1)S(1)}, bf16[128,2048]{1,0:T(8,128)(2,1)S(1)}, u32[]{:S(2)}, u32[]{:S(2)}) collective-permute-start(bf16[128,2048]{1,0:T(8,128)(2,1)S(1)} %add_convert_fusion.8), channel_id=1, source_target_pairs={{0,2},{2,0},{4,6},{6,4},{8,10},{10,8},{12,14},{14,12},{16,18},{18,... | collective-permute-start | bytes 1572872 | tf_op jit(solution)/shard_map/ppermute | solution.py:20
  142.7 21.9 %collective-permute-start.25 = (bf16[128,2048]{1,0:T(8,128)(2,1)S(1)}, bf16[128,2048]{1,0:T(8,128)(2,1)S(1)}, u32[]{:S(2)}, u32[]{:S(2)}) collective-permute-start(bf16[128,2048]{1,0:T(8,128)(2,1)S(1)} %get-tuple-element.75), channel_id=1, source_target_pairs={{0,2},{2,0},{4,6},{6,4},{8,10},{10,8},{12,14},{14,12},{16,18},{18,... | collective-permute-start | bytes 1572872 | tf_op jit(solution)/shard_map/ppermute | solution.py:20
  146.5 14.9 %collective-permute-start.44 = (bf16[128,2048]{1,0:T(8,128)(2,1)S(1)}, bf16[128,2048]{1,0:T(8,128)(2,1)S(1)}, u32[]{:S(2)}, u32[]{:S(2)}) collective-permute-start(bf16[128,2048]{1,0:T(8,128)(2,1)S(1)} %expert_rows.9), channel_id=1, source_target_pairs={{0,8},{2,10},{4,12},{6,14},{8,0},{10,2},{12,4},{14,6},{16,24},{18,... | collective-permute-start | bytes 1572872 | tf_op jit(solution)/shard_map/ppermute | solution.py:20
  146.9 18.9 %collective-permute-start.33 = (bf16[128,2048]{1,0:T(8,128)(2,1)S(1)}, bf16[128,2048]{1,0:T(8,128)(2,1)S(1)}, u32[]{:S(2)}, u32[]{:S(2)}) collective-permute-start(bf16[128,2048]{1,0:T(8,128)(2,1)S(1)} %add_convert_fusion.9), channel_id=1, source_target_pairs={{0,4},{2,6},{4,0},{6,2},{8,12},{10,14},{12,8},{14,10},{16,20},{18,... | collective-permute-start | bytes 1572872 | tf_op jit(solution)/shard_map/ppermute | solution.py:20
  154.3 18.4 %collective-permute-start.37 = (bf16[128,2048]{1,0:T(8,128)(2,1)S(1)}, bf16[128,2048]{1,0:T(8,128)(2,1)S(1)}, u32[]{:S(2)}, u32[]{:S(2)}) collective-permute-start(bf16[128,2048]{1,0:T(8,128)(2,1)S(1)} %add_convert_fusion.7), channel_id=1, source_target_pairs={{0,8},{2,10},{4,12},{6,14},{24,16},{26,18},{28,20},{30,22},{1,9},{... | collective-permute-start | bytes 1572872 | tf_op jit(solution)/shard_map/ppermute | solution.py:231
  155.6 36.7 %collective-permute-start.24 = (bf16[128,2048]{1,0:T(8,128)(2,1)S(1)}, bf16[128,2048]{1,0:T(8,128)(2,1)S(1)}, u32[]{:S(2)}, u32[]{:S(2)}) collective-permute-start(bf16[128,2048]{1,0:T(8,128)(2,1)S(1)} %get-tuple-element.73), channel_id=1, source_target_pairs={{0,4},{2,6},{4,0},{6,2},{8,12},{10,14},{12,8},{14,10},{16,20},{18,... | collective-permute-start | bytes 1572872 | tf_op jit(solution)/shard_map/ppermute | solution.py:20
  161.4 19.2 %collective-permute-start.42 = (bf16[128,2048]{1,0:T(8,128)(2,1)S(1)}, bf16[128,2048]{1,0:T(8,128)(2,1)S(1)}, u32[]{:S(2)}, u32[]{:S(2)}) collective-permute-start(bf16[128,2048]{1,0:T(8,128)(2,1)S(1)} %get-tuple-element.91), channel_id=1, source_target_pairs={{0,8},{2,10},{4,12},{6,14},{8,0},{10,2},{12,4},{14,6},{16,24},{18,... | collective-permute-start | bytes 1572872 | tf_op jit(solution)/shard_map/ppermute | solution.py:20
  164.6 19.9 %collective-permute-start.45 = (bf16[128,2048]{1,0:T(8,128)(2,1)S(1)}, bf16[128,2048]{1,0:T(8,128)(2,1)S(1)}, u32[]{:S(2)}, u32[]{:S(2)}) collective-permute-start(bf16[128,2048]{1,0:T(8,128)(2,1)S(1)} %add_convert_fusion.2), channel_id=1, source_target_pairs={{0,2},{2,0},{4,6},{6,4},{8,10},{10,8},{12,14},{14,12},{16,18},{18,... | collective-permute-start | bytes 1572872 | tf_op jit(solution)/shard_map/ppermute | solution.py:20
  173.0 16.3 %collective-permute-start.40 = (bf16[128,2048]{1,0:T(8,128)(2,1)S(1)}, bf16[128,2048]{1,0:T(8,128)(2,1)S(1)}, u32[]{:S(2)}, u32[]{:S(2)}) collective-permute-start(bf16[128,2048]{1,0:T(8,128)(2,1)S(1)} %add_convert_fusion.6), channel_id=1, source_target_pairs={{0,8},{2,10},{4,12},{6,14},{24,16},{26,18},{28,20},{30,22},{1,9},{... | collective-permute-start | bytes 1572872 | tf_op jit(solution)/shard_map/ppermute | solution.py:231
  180.8 12.9 %collective-permute-start.43 = (bf16[128,2048]{1,0:T(8,128)(2,1)S(1)}, bf16[128,2048]{1,0:T(8,128)(2,1)S(1)}, u32[]{:S(2)}, u32[]{:S(2)}) collective-permute-start(bf16[128,2048]{1,0:T(8,128)(2,1)S(1)} %add_convert_fusion.3), channel_id=1, source_target_pairs={{0,2},{2,0},{4,6},{6,4},{8,10},{10,8},{12,14},{14,12},{16,18},{18,... | collective-permute-start | bytes 1572872 | tf_op jit(solution)/shard_map/ppermute | solution.py:20
  182.1 11.3 %collective-permute-start.38 = (bf16[128,2048]{1,0:T(8,128)(2,1)S(1)}, bf16[128,2048]{1,0:T(8,128)(2,1)S(1)}, u32[]{:S(2)}, u32[]{:S(2)}) collective-permute-start(bf16[128,2048]{1,0:T(8,128)(2,1)S(1)} %add_convert_fusion.6), channel_id=1, source_target_pairs={{8,16},{10,18},{12,20},{14,22},{16,8},{18,10},{20,12},{22,14},{9,1... | collective-permute-start | bytes 1572872 | tf_op jit(solution)/shard_map/ppermute | solution.py:231
  184.6 9.2 %collective-permute-start.46 = (bf16[128,2048]{1,0:T(8,128)(2,1)S(1)}, bf16[128,2048]{1,0:T(8,128)(2,1)S(1)}, u32[]{:S(2)}, u32[]{:S(2)}) collective-permute-start(bf16[128,2048]{1,0:T(8,128)(2,1)S(1)} %add_convert_fusion.1), channel_id=1, source_target_pairs={{0,4},{2,6},{4,0},{6,2},{8,12},{10,14},{12,8},{14,10},{16,20},{18,... | collective-permute-start | bytes 1572872 | tf_op jit(solution)/shard_map/ppermute | solution.py:20
  189.4 11.1 %collective-permute-start.41 = (bf16[128,2048]{1,0:T(8,128)(2,1)S(1)}, bf16[128,2048]{1,0:T(8,128)(2,1)S(1)}, u32[]{:S(2)}, u32[]{:S(2)}) collective-permute-start(bf16[128,2048]{1,0:T(8,128)(2,1)S(1)} %add_convert_fusion.4), channel_id=1, source_target_pairs={{8,16},{10,18},{12,20},{14,22},{16,8},{18,10},{20,12},{22,14},{9,1... | collective-permute-start | bytes 1572872 | tf_op jit(solution)/shard_map/ppermute | solution.py:231
  193.6 9.2 %collective-permute-start.39 = (bf16[128,2048]{1,0:T(8,128)(2,1)S(1)}, bf16[128,2048]{1,0:T(8,128)(2,1)S(1)}, u32[]{:S(2)}, u32[]{:S(2)}) collective-permute-start(bf16[128,2048]{1,0:T(8,128)(2,1)S(1)} %add_convert_fusion.5), channel_id=1, source_target_pairs={{0,8},{2,10},{4,12},{6,14},{8,0},{10,2},{12,4},{14,6},{16,24},{18,... | collective-permute-start | bytes 1572872 | tf_op jit(solution)/shard_map/ppermute | solution.py:20
  (26 other events, 105.9 us)

commit v8 on v7

--- a/solution.py
+++ b/solution.py
@@ -39,30 +39,6 @@
 
 def place_of(j):
     return sum(1 << bit for bit, mask in enumerate(gate_order(lax.axis_size("seq"))) if j & mask)
-
-
-def fetch_kernel(own_ref, other_ref, resid_ref, *refs):
-    outs, sems = refs[:-1], refs[-1]
-    copies = [
-        pltpu.make_async_copy(ref, out, sems.at[i])
-        for i, (ref, out) in enumerate(zip((own_ref, other_ref, resid_ref), outs))
-    ]
-    for copy in copies:
-        copy.start()
-    for copy in copies:
-        copy.wait()
-
-
-def fetch(*arrays):
-    return pl.pallas_call(
-        fetch_kernel,
-        out_shape=[jax.ShapeDtypeStruct(array.shape, array.dtype) for array in arrays],
-        in_specs=[ANY] * len(arrays),
-        out_specs=[VMEM] * len(arrays),
-        scratch_shapes=[pltpu.SemaphoreType.DMA((len(arrays),))],
-        compiler_params=pltpu.CompilerParams(vmem_limit_bytes=8 * 1024 * 1024),
-        name="fetch_projection",
-    )(*arrays)
 
 
 def attention_kernel(where_ref, q_ref, ids_ref, *refs):
@@ -120,7 +96,7 @@
         out_specs=(VMEM, VMEM),
         scratch_shapes=[pltpu.VMEM((3 * rows, width), jnp.bfloat16)] * 2
         + [pltpu.VMEM((rows, width), jnp.bfloat16), pltpu.SemaphoreType.DMA((6,))],
-        compiler_params=pltpu.CompilerParams(vmem_limit_bytes=16 * 1024 * 1024),
+        compiler_params=pltpu.CompilerParams(vmem_limit_bytes=63 * 1024 * 1024),
         name="window_attention",
     )(where, queries, ids, *near_keys, *near_values, *ahead)
 
@@ -145,7 +121,7 @@
         ),
         in_specs=[VMEM] * 6 + [ANY] * len(ahead),
         out_specs=(VMEM, VMEM),
-        compiler_params=pltpu.CompilerParams(vmem_limit_bytes=16 * 1024 * 1024),
+        compiler_params=pltpu.CompilerParams(vmem_limit_bytes=63 * 1024 * 1024),
         name="project_and_norm",
     )(mine, theirs, own_w, other_w, resid, gain, *ahead)
 
@@ -174,12 +150,18 @@
         in_specs=[ANY] * 6,
         out_specs=(VMEM, VMEM),
         scratch_shapes=[pltpu.SemaphoreType.DMA((6,))],
-        compiler_params=pltpu.CompilerParams(vmem_limit_bytes=12 * 1024 * 1024),
+        compiler_params=pltpu.CompilerParams(vmem_limit_bytes=36 * 1024 * 1024),
         name="assemble_weights",
     )(*halves)
 
 
-def expert_kernel(places, pieces, shard_ref, *refs):
+def gates_at(place, rows, pieces):
+    piece = place.bit_length()
+    at = (place - (1 << piece >> 1)) * rows
+    return pieces[piece][:, at : at + rows]
+
+
+def expert_kernel(places, pieces, where_ref, *refs):
     count = len(places)
     blocks, gates, (gate_up, down) = refs[:count], refs[count : count + pieces], refs[count + pieces :][:2]
     outs = refs[count + pieces + 2 :]
@@ -193,17 +175,18 @@
         act = (gate / (1.0 + jnp.exp(-gate)) * up).astype(jnp.bfloat16)
         result = jnp.dot(act, down[...], preferred_element_type=jnp.float32)
         for i in group:
-            piece = places[i].bit_length()
-            at = (places[i] - (1 << piece >> 1)) * rows
-            here = gates[piece][:, at : at + rows]
+            here, *other = [gates_at(place, rows, gates) for place in sorted(set(places[i]))]
+            if other:
+                swap = where_ref[1] == (1 if places[i][0] < places[i][1] else 0)
+                here = jnp.where(swap, other[0], here)
             expert = lax.broadcasted_iota(jnp.int32, here.shape, 0)
-            chosen = jnp.sum(jnp.where(expert == shard_ref[0], here, 0.0), axis=0, keepdims=True)
+            chosen = jnp.sum(jnp.where(expert == where_ref[0], here, 0.0), axis=0, keepdims=True)
             chosen = jnp.transpose(jnp.broadcast_to(chosen, (rows, rows)))[:, :1]
             part = result[(i - first) * rows : (i - first + 1) * rows]
             outs[i][...] = (part * chosen).astype(jnp.bfloat16)
 
 
-def expert(blocks, places, shard, gates, weights):
+def expert(blocks, places, where, gates, weights):
     rows, width = blocks[0].shape
     count = len(blocks)
     return pl.pallas_call(
@@ -213,7 +196,7 @@
         out_specs=[VMEM] * count,
         compiler_params=pltpu.CompilerParams(vmem_limit_bytes=24 * 1024 * 1024),
         name="expert_rows",
-    )(shard, *blocks, *gates, *weights)
+    )(where, *blocks, *gates, *weights)
 
 
 def add(*terms):
@@ -227,62 +210,62 @@
     return add(*terms).astype(jnp.bfloat16)
 
 
-def shift(block, pairs):
-    return lax.ppermute(block, "seq", [(4 * a + i, 4 * b + i) for a, b in pairs for i in range(4)])
-
-
-OUTWARD, INWARD, MIDDLE = [(1, 0), (2, 3)], [(0, 1), (3, 2)], [(1, 2), (2, 1)]
+UP, DOWN = 16, 32
+
+
+def ring(block, hops):
+    count = lax.axis_size("seq")
+    return lax.ppermute(block, "seq", [((i + 4 * hops) % count, i) for i in range(count)])
 
 
 def step_layer(normed, stream, run, weights):
-    z = lax.axis_index("seq") // 4
-    inner = (z == 1) | (z == 2)
-
-    o0 = normed
-    o1, near3, x0, y0 = flip(o0, 4), shift(o0, MIDDLE), flip(o0, 1), flip(o0, 2)
-
-    ends2, near2 = shift(after(near3, o1), OUTWARD), shift(after(o1, near3), MIDDLE)
-    d0, y1 = flip(after(y0, x0), 1), flip(after(o1, y0), 2)
-
-    ends3 = shift(after(near2, ends2), OUTWARD)
-    o2 = jnp.where(inner, near2, ends2)
-    x2, y2 = flip(after(o2, d0, weights[0]), 1), flip(after(o2, y1, weights[0]), 2)
-    p0, px0, py0, pd0 = run([after(o0, o2), x0, y0, d0], (0, 1, 2, 3))
-
-    x1 = flip(after(x0, ends3, p0), 4)
-    o3 = jnp.where(inner, near3, ends3)
-    x3, y3 = flip(after(o3, x2, p0), 1), flip(after(o3, y2, p0), 2)
-    p1, py1, p2, px2, py2, p3 = run([after(o1, p0), y1, o2, x2, y2, o3], (4, 6, 8, 9, 10, 12))
-
-    d1 = flip(after(d0, x1, p1), 4)
-    d2, d3 = flip(after(y2, x3, p1), 1), flip(after(x3, y3, p1), 2)
-    px3, py3, px1 = run([after(x3, p1), y3, x1], (13, 14, 5))
-
-    pd2, pd3 = run([after(d2, px3, d1), d3], (11, 15))
-    (pd1,) = run([after(d1, pd2)], (7,))
-    to_x3, to_y2, to_d0 = flip(pd3, 2), flip(pd2, 1), flip(pd1, 4)
-
-    px3, py2, pd0 = add_small(px3, to_x3), add_small(py2, to_y2), add_small(pd0, to_d0)
-    by_x, by_y, to_x0 = flip(px3, 1), flip(py3, 2), flip(px1, 4)
-
-    p3, px0 = add_small(p3, by_x, by_y), add_small(px0, to_x0)
-    to_2, by_x, by_y = shift(p3, INWARD), flip(px2, 1), flip(py2, 2)
-
-    p2 = add_small(p2, by_x, by_y, to_2)
-    to_3, to_1 = shift(p2, INWARD), shift(p2, MIDDLE)
-    to_y0, by_y = flip(pd0, 1), flip(py1, 2)
-
-    p3, p1, py0 = add_small(p3, to_3), add_small(p1, by_y, to_1), add_small(py0, to_y0)
-    by_z, by_middle, by_x, by_y = flip(p1, 4), shift(p3, MIDDLE), flip(px0, 1), flip(py0, 2)
-    return add(stream, p0, by_z, by_middle, by_x, by_y)
-
-
-def expert_layer(normed, stream, shard, gates, weights):
+    o = normed
+    uo, wo, xo, yo = ring(o, 1), ring(o, -1), flip(o, 1), flip(o, 2)
+
+    fo = ring(after(uo, weights[0]), 1)
+    wx = ring(after(xo, wo, weights[0]), -1)
+    do, uy = flip(after(yo, xo, weights[0]), 1), flip(after(uo, yo, weights[0]), 2)
+    po, pxo, pyo, puo = run([after(o, wo), xo, yo, uo], (0, 1, 2, UP))
+
+    ux, wy = ring(after(xo, fo, po), 1), ring(after(yo, wx, po), -1)
+    fx, fy = flip(after(fo, do, po), 1), flip(after(fo, uy, po), 2)
+    pwo, pfo, pwx, puy, pdo = run([after(wo, po), fo, wx, uy, do], (DOWN, 8, DOWN + 1, UP + 2, 3))
+
+    ud, wd = ring(after(do, ux, pwo), 1), ring(after(do, wy, pwo), -1)
+    fd = flip(after(fy, fx, pwo), 1)
+    pux, pwy, pfx, pfy = run([after(ux, pwo), wy, fx, fy], (UP + 1, DOWN + 2, 9, 10))
+
+    pfd, pud = run([after(fd, pux, wd), ud], (11, UP + 3))
+    (pwd,) = run([after(wd, pfd)], (DOWN + 3,))
+    to_fy, down, up = flip(pfd, 1), ring(pud, -1), ring(pwd, 1)
+
+    pfy, pdo = add_small(pfy, to_fy), add_small(pdo, down, up)
+    by_x, by_y = flip(after(pfx, to_fy), 1), flip(pfy, 2)
+    to_xo, to_yo = ring(after(pux, down), -1), ring(after(pwy, up), 1)
+
+    pfo, pxo, pyo = add_small(pfo, by_x, by_y), add_small(pxo, to_xo), add_small(pyo, to_yo)
+    to_uo, to_xo = ring(after(pfo, to_xo), -1), ring(after(pwx, to_yo), 1)
+    to_yo, by_y = flip(after(pdo, by_x), 1), flip(after(puy, by_y), 2)
+
+    puo = add_small(puo, to_uo, by_y)
+    pxo, pyo = add_small(pxo, to_xo), add_small(pyo, to_yo)
+    down, up = ring(after(puo, to_uo), -1), ring(after(pwo, to_xo), 1)
+    by_x, by_y = flip(after(pxo, to_yo), 1), flip(after(pyo, by_y), 2)
+    return add(stream, po, down, up, by_x, by_y)
+
+
+def expert_layer(normed, stream, where, gates, weights):
     count = lax.axis_size("seq")
 
     def run(blocks, masks):
-        places = tuple(place_of(mask) for mask in masks)
-        return expert(blocks, places, shard, gates, weights)
+        places = []
+        for mask in masks:
+            even = odd = mask
+            if count == 16 and mask >= UP:
+                even, odd = (4, 12) if mask < DOWN else (12, 4)
+                even, odd = even + mask % 4, odd + mask % 4
+            places.append((place_of(even), place_of(odd)))
+        return expert(blocks, tuple(places), where, gates, weights)
 
     if count == 16:
         return step_layer(normed, stream, run, weights)
@@ -319,15 +302,14 @@
     core = lax.axis_index("exp")
     count = lax.axis_size("seq")
 
-    def halo(part, *arrays):
-        beside = after(flip(part, 1), *arrays)
+    def halo(part):
+        beside = flip(part, 1)
         ahead = [(i, i + 2) for i in range(0, count - 2, 2)]
         back = [(i + 2, i) for i in range(1, count - 2, 2)]
         return beside, part, lax.ppermute(beside, "seq", ahead + back)
 
     out_other = lax.ppermute(out_weight, "exp", SWAP)
-    out_own, out_other, stream = fetch(out_weight, out_other, resid)
-    near_keys, near_values = halo(keys), halo(values, out_own)
+    near_keys, near_values = halo(keys), halo(values)
     chosen = experts.T[:, None, :] == jnp.arange(count, dtype=jnp.int32)[None, :, None]
     all_gates = gather_gates(jnp.sum(jnp.where(chosen, gates.T[:, None, :], 0.0), axis=0))
     id_pad = jnp.pad(pair_ids, (tok_rows, tok_rows), constant_values=-1)
@@ -340,14 +322,13 @@
     halves = [gate_w, gate_other, up_w, up_other, w_down[0], down_other]
 
     where = jnp.stack([core, shard % 2])
-    theirs, mine = attention(
-        where, queries, ids, near_keys, near_values, gate_other
-    )
+    place = jnp.stack([shard, shard // 4 % 2])
+    theirs, mine = attention(where, queries, ids, near_keys, near_values, out_other, gate_other)
     received = lax.ppermute(theirs, "exp", SWAP)
     stream, normed = project_and_norm(
-        mine, received, out_own, out_other, stream, norm_gain[None, :], up_other, down_other
+        mine, received, out_weight, out_other, resid, norm_gain[None, :], up_other, down_other
     )
-    mixed = expert_layer(normed, stream, shard.reshape(1), all_gates, assemble(halves))
+    mixed = expert_layer(normed, stream, place, all_gates, assemble(halves))
     return mixed.astype(jnp.bfloat16)
 
 

time: 207 us -> 247 us (1.19)
  waiting for transfers between devices: 84.5 us -> 135 us
  starting transfers between devices: 59 us -> 51.2 us
  local copies, waits for them, and re-layouts: 21.2 us -> 13.8 us
  Pallas kernels: 33.1 us -> 40.4 us
    ppermute x8 -> x16, waiting for transfers between devices: 23.7 us -> 119 us  [ring(): lax.ppermute(block, 'seq', [((i + 4 * hops) % count, i) for i in range(co...]
    ppermute x32 -> x20, waiting for transfers between devices: 59.4 us -> 14.2 us  [flip(): return lax.ppermute(block, 'seq', [(i, i ^ mask) for i in range(count)])]
    unnamed x54 -> x30, local copies, waits for them, and re-layouts: 21.1 us -> 12.4 us
    ppermute x32 -> x20, starting transfers between devices: 29.5 us -> 23.8 us  [flip(): return lax.ppermute(block, 'seq', [(i, i ^ mask) for i in range(count)])]
    pallas_call x1, Pallas kernels: 0.89 us -> 4.29 us  [project_and_norm(): pl.pallas_call(norm_kernel, out_shape=(jax.ShapeDtypeStruct((rows, width)...]
    ppermute x8 -> x16, starting transfers between devices: 23.1 us -> 20.2 us  [ring(): lax.ppermute(block, 'seq', [((i + 4 * hops) % count, i) for i in range(co...]
  transfers between devices with their start and end apart: 47 -> 43, of which waited for: 26 -> 17; matrix products, arithmetic and copies ran while one was open for 2% -> 2% of each run, Pallas kernels for 14% -> 12%
where the time goes in v8:
time: 247 us; the launch traced here: 244 us
  waiting for transfers between devices  135 us (55%)
  starting transfers between devices  51.2 us (21%)
  Pallas kernels  40.4 us (16%)
  local copies, waits for them, and re-layouts  13.8 us (6%)
  other arithmetic  3.96 us (2%)
    ppermute x16, waiting for transfers between devices, ring(): lax.ppermute(block, 'seq', [((i + 4 * hops) % count, i) for i in range(co...  119 us
    pallas_call x5, Pallas kernels, expert(): pl.pallas_call(functools.partial(expert_kernel, places, len(gates)), out_...  27.1 us
    ppermute x20, starting transfers between devices, flip(): return lax.ppermute(block, 'seq', [(i, i ^ mask) for i in range(count)])  23.8 us
    ppermute x16, starting transfers between devices, ring(): lax.ppermute(block, 'seq', [((i + 4 * hops) % count, i) for i in range(co...  20.2 us
    ppermute x20, waiting for transfers between devices, flip(): return lax.ppermute(block, 'seq', [(i, i ^ mask) for i in range(count)])  14.2 us
    unnamed x30, local copies, waits for them, and re-layouts  12.4 us
    ppermute x2, starting transfers between devices, halo(): return (beside, part, lax.ppermute(beside, 'seq', ahead + back))  6.6 us
    pallas_call x1, Pallas kernels, attention(): pl.pallas_call(attention_kernel, out_shape=(half, half), in_specs=[pl.Blo...  6.4 us
  transfers between devices with their start and end apart: 43, of which 17 were waited for; matrix products, arithmetic and copies ran while one was open for 2% of the time, Pallas kernels for 12%

profile of v8, /device:TPU:10, one launch (start us, length us, event | category | flops | bytes accessed | tf_op | source)
XLA Modules:
  0.0 244.3 jit_solution(8954575569918558632)
XLA Ops:
  0.5 1.5 collective-permute-start.2
  3.3 3.2 %collective-permute-done.7.refs_5_.refs_6_.refs_3_.refs_2_ = f32[16,128]{1,0:T(8,128)S(1)} collective-permute-done((f32[16,128]{1,0:T(8,128)S(1)}, f32[16,128]{1,0:T(8,128)S(1)}, u32[]{:S(2)}, u32[]{:S(2)}) %collective-permute-start.7) | collective-permute-done | bytes 8224 | tf_op jit(solution)/shard_map/ppermute | solution.py:20
  6.5 2.6 %collective-permute-start.8 = (f32[16,256]{1,0:T(8,128)S(1)}, f32[16,256]{1,0:T(8,128)S(1)}, u32[]{:S(2)}, u32[]{:S(2)}) collective-permute-start(f32[16,256]{1,0:T(8,128)S(1)} %pad_maximum_fusion.2), channel_id=1, source_target_pairs={{0,16},{2,18},{4,20},{6,22},{8,24},{10,26},{12,28},{14,30},{16,0},... | collective-permute-start | bytes 49160 | tf_op jit(solution)/shard_map/ppermute | solution.py:20
  9.3 3.3 %collective-permute-start.1 = (bf16[256,512]{1,0:T(8,128)(2,1)S(1)}, bf16[256,512]{1,0:T(8,128)(2,1)S(1)}, u32[]{:S(2)}, u32[]{:S(2)}) collective-permute-start(bf16[256,512]{1,0:T(8,128)(2,1)S(1)} %collective-permute-done.refs_0_), channel_id=1, source_target_pairs={{0,4},{4,8},{8,12},{12,16},{16,20},{20,24},{24,28},{6,2},{10,6},{1... | collective-permute-start | bytes 786440 | tf_op jit(solution)/shard_map/ppermute | solution.py:309
  12.6 1.9 collective-permute-done.2.refs_3_
  14.6 3.3 %collective-permute-start.3 = (bf16[256,512]{1,0:T(8,128)(2,1)S(1)}, bf16[256,512]{1,0:T(8,128)(2,1)S(1)}, u32[]{:S(2)}, u32[]{:S(2)}) collective-permute-start(bf16[256,512]{1,0:T(8,128)(2,1)S(1)} %collective-permute-done.2.refs_3_), channel_id=1, source_target_pairs={{0,4},{4,8},{8,12},{12,16},{16,20},{20,24},{24,28},{6,2},{10,6},{1... | collective-permute-start | bytes 786440 | tf_op jit(solution)/shard_map/ppermute | solution.py:309
  18.6 6.5 %collective-permute-done.9.refs_7_.refs_8_.refs_5_.refs_4_ = f32[16,512]{1,0:T(8,128)S(1)} collective-permute-done((f32[16,512]{1,0:T(8,128)S(1)}, f32[16,512]{1,0:T(8,128)S(1)}, u32[]{:S(2)}, u32[]{:S(2)}) %collective-permute-start.9) | collective-permute-done | bytes 32800 | tf_op jit(solution)/shard_map/ppermute | solution.py:20
  25.1 1.4 collective-permute-start.10
  27.9 1.5 collective-permute-done.10.refs_8_.refs_9_.refs_6_.refs_5_
  31.2 6.4 %window_attention.1 = (bf16[128,512]{1,0:T(8,128)(2,1)}, bf16[128,512]{1,0:T(8,128)(2,1)}) custom-call(s32[2]{0:T(128)} %pad_add_fusion.where_ref, bf16[256,512]{1,0:T(8,128)(2,1)} %q_ref.1, s32[1,768]{1,0:T(1,128)} %broadcast_in_dim.21.ids_ref, bf16[256,512]{1,0:T(8,128)(2,1)} %copy-done.10, bf16[256,512]{1,0:T(8,128)(2,1)} %refs_1_.1, ...), custom_call_target="tpu_custom_call" | custom-call | tf_op jit(solution)/shard_map/window_attention/pallas_call | solution.py:92
  37.7 1.5 collective-permute-done.6.theirs_ref
  39.9 4.3 %project_and_norm.1 = (f32[128,2048]{1,0:T(8,128)}, bf16[128,2048]{1,0:T(8,128)(2,1)}) custom-call(bf16[128,512]{1,0:T(8,128)(2,1)} %get-tuple-element.55.mine_ref, bf16[128,512]{1,0:T(8,128)(2,1)} %copy-done.14, bf16[512,2048]{1,0:T(8,128)(2,1)} %own_w.1, bf16[512,2048]{1,0:T(8,128)(2,1)} %collective-permute-done.4.refs_6_.other_w, ...), custom_call_target="tpu_custom_call" | custom-call | tf_op jit(solution)/shard_map/project_and_norm/pallas_call | solution.py:116
  44.6 2.4 collective-permute-start.15
  47.1 1.6 collective-permute-start.13
  48.7 1.4 copy-done.3
  50.0 1.4 copy-done.4
  51.4 1.4 copy-done.5
  52.7 2.6 %assemble_weights.1 = (bf16[1408,2048]{1,0:T(8,128)(2,1)S(1)}, bf16[704,2048]{1,0:T(8,128)(2,1)S(1)}) custom-call(bf16[352,2048]{1,0:T(8,128)(2,1)S(1)} %bitcast.15, bf16[352,2048]{1,0:T(8,128)(2,1)} %collective-permute-done.5.refs_7_.refs_1_, bf16[352,2048]{1,0:T(8,128)(2,1)S(1)} %bitcast.17, bf16[352,2048]{1,0:T(8,128)(2,1)} %collective-permute-done.11.refs_0_.refs_3_, ...), custom_call_target="tpu_custom_call" | custom-call | tf_op jit(solution)/shard_map/assemble_weights/pallas_call | solution.py:144
  55.4 2.5 %copy-done = bf16[1408,2048]{1,0:T(8,128)(2,1)} copy-done((bf16[1408,2048]{1,0:T(8,128)(2,1)}, bf16[1408,2048]{1,0:T(8,128)(2,1)S(1)}, u32[]{:S(2)}) %copy-start) | copy-done | bytes 5767192
  59.3 2.9 %collective-permute-start.17 = (bf16[128,2048]{1,0:T(8,128)(2,1)}, bf16[128,2048]{1,0:T(8,128)(2,1)}, u32[]{:S(2)}, u32[]{:S(2)}) collective-permute-start(bf16[128,2048]{1,0:T(8,128)(2,1)} %collective-permute-done.16.refs_3_), channel_id=1, source_target_pairs={{8,0},{10,2},{12,4},{14,6},{16,8},{18,10},{20,12},{22,14},{24,16},... | collective-permute-start | bytes 1572872 | tf_op jit(solution)/shard_map/ppermute | solution.py:218
  62.6 9.9 %collective-permute-done.13.refs_0_ = bf16[128,2048]{1,0:T(8,128)(2,1)S(1)} collective-permute-done((bf16[128,2048]{1,0:T(8,128)(2,1)}, bf16[128,2048]{1,0:T(8,128)(2,1)S(1)}, u32[]{:S(2)}, u32[]{:S(2)}) %collective-permute-start.13) | collective-permute-done | bytes 524320 | tf_op jit(solution)/shard_map/ppermute | solution.py:218
  73.2 1.4 collective-permute-start.18
  74.6 1.4 collective-permute-start.20
  76.1 2.6 %copy-done.1 = bf16[1408,2048]{1,0:T(8,128)(2,1)S(1)} copy-done((bf16[1408,2048]{1,0:T(8,128)(2,1)S(1)}, bf16[1408,2048]{1,0:T(8,128)(2,1)}, u32[]{:S(2)}) %copy-start.1) | copy-done | bytes 5767192
  79.8 6.5 %expert_rows.5 = (bf16[128,2048]{1,0:T(8,128)(2,1)S(1)}, bf16[128,2048]{1,0:T(8,128)(2,1)S(1)}, bf16[128,2048]{1,0:T(8,128)(2,1)S(1)}, bf16[128,2048]{1,0:T(8,128)(2,1)S(1)}) custom-call(s32[2]{0:T(128)S(1)} %pad_add_fusion.1.where_ref, bf16[128,2048]{1,0:T(8,128)(2,1)S(1)} %copy-done.8, bf16[128,2048]{1,0:T(8,128)(2,1)S(1)} %collective-permute-done.14.refs_1_, ...), custom_call_target="tpu_custom_call" | custom-call | tf_op jit(solution)/shard_map/expert_rows/pallas_call | solution.py:192
  86.3 8.0 %collective-permute-done.18.refs_2_ = bf16[128,2048]{1,0:T(8,128)(2,1)} collective-permute-done((bf16[128,2048]{1,0:T(8,128)(2,1)S(1)}, bf16[128,2048]{1,0:T(8,128)(2,1)}, u32[]{:S(2)}, u32[]{:S(2)}) %collective-permute-start.18) | collective-permute-done | bytes 524320 | tf_op jit(solution)/shard_map/ppermute | solution.py:218
  94.3 1.4 collective-permute-start.22
  95.7 1.4 collective-permute-start.23
  98.4 8.8 %expert_rows.6 = (bf16[128,2048]{1,0:T(8,128)(2,1)S(1)}, bf16[128,2048]{1,0:T(8,128)(2,1)S(1)}, bf16[128,2048]{1,0:T(8,128)(2,1)S(1)}, bf16[128,2048]{1,0:T(8,128)(2,1)S(1)}, bf16[128,2048]{1,0:T(8,128)(2,1)S(1)}) custom-call(s32[2]{0:T(128)S(1)} %pad_add_fusion.1.where_ref, bf16[128,2048]{1,0:T(8,128)(2,1)S(1)} %copy-done.7, ...), custom_call_target="tpu_custom_call" | custom-call | tf_op jit(solution)/shard_map/expert_rows/pallas_call | solution.py:192
  107.2 10.8 %collective-permute-done.22.refs_1_ = bf16[128,2048]{1,0:T(8,128)(2,1)S(1)} collective-permute-done((bf16[128,2048]{1,0:T(8,128)(2,1)}, bf16[128,2048]{1,0:T(8,128)(2,1)S(1)}, u32[]{:S(2)}, u32[]{:S(2)}) %collective-permute-start.22) | collective-permute-done | bytes 524320 | tf_op jit(solution)/shard_map/ppermute | solution.py:218
  118.0 1.4 collective-permute-start.25
  119.5 2.9 %collective-permute-start.26 = (bf16[128,2048]{1,0:T(8,128)(2,1)}, bf16[128,2048]{1,0:T(8,128)(2,1)S(1)}, u32[]{:S(2)}, u32[]{:S(2)}) collective-permute-start(bf16[128,2048]{1,0:T(8,128)(2,1)} %collective-permute-done.20.refs_4_), channel_id=1, source_target_pairs={{24,0},{26,2},{28,4},{30,6},{0,8},{2,10},{4,12},{6,14},{8,16},{10,... | collective-permute-start | bytes 1572872 | tf_op jit(solution)/shard_map/ppermute | solution.py:218
  122.8 5.6 %expert_rows.7 = (bf16[128,2048]{1,0:T(8,128)(2,1)S(1)}, bf16[128,2048]{1,0:T(8,128)(2,1)S(1)}, bf16[128,2048]{1,0:T(8,128)(2,1)S(1)}, bf16[128,2048]{1,0:T(8,128)(2,1)S(1)}) custom-call(s32[2]{0:T(128)S(1)} %pad_add_fusion.1.where_ref, bf16[128,2048]{1,0:T(8,128)(2,1)S(1)} %collective-permute-done.21.refs_0_, ...), custom_call_target="tpu_custom_call" | custom-call | tf_op jit(solution)/shard_map/expert_rows/pallas_call | solution.py:192
  128.4 12.7 %collective-permute-done.26.refs_0_ = bf16[128,2048]{1,0:T(8,128)(2,1)S(1)} collective-permute-done((bf16[128,2048]{1,0:T(8,128)(2,1)}, bf16[128,2048]{1,0:T(8,128)(2,1)S(1)}, u32[]{:S(2)}, u32[]{:S(2)}) %collective-permute-start.26) | collective-permute-done | bytes 524320 | tf_op jit(solution)/shard_map/ppermute | solution.py:218
  141.1 1.5 collective-permute-done.27.refs_1_
  142.7 3.2 %expert_rows.8 = (bf16[128,2048]{1,0:T(8,128)(2,1)S(1)}, bf16[128,2048]{1,0:T(8,128)(2,1)S(1)}) custom-call(s32[2]{0:T(128)S(1)} %pad_add_fusion.1.where_ref, bf16[128,2048]{1,0:T(8,128)(2,1)S(1)} %collective-permute-done.25.refs_0_, bf16[128,2048]{1,0:T(8,128)(2,1)S(1)} %collective-permute-done.27.refs_1_, ...), custom_call_target="tpu_custom_call" | custom-call | tf_op jit(solution)/shard_map/expert_rows/pallas_call | solution.py:192
  145.9 2.9 %expert_rows.9 = bf16[128,2048]{1,0:T(8,128)(2,1)S(1)} custom-call(s32[2]{0:T(128)S(1)} %pad_add_fusion.1.where_ref, bf16[128,2048]{1,0:T(8,128)(2,1)S(1)} %collective-permute-done.26.refs_0_, f32[16,128]{1,0:T(8,128)S(1)} %select_reduce_fusion.refs_4_.refs_5_.refs_2_.refs_1_, f32[16,128]{1,0:T(8,128)S(1)} %collective-permute-done.7.refs_5_.refs_6_.refs_3_.refs_2_, ...), custom_call_target="tpu_custom_call" | custom-call | tf_op jit(solution)/shard_map/expert_rows/pallas_call | solution.py:192
  148.8 1.5 collective-permute-start.36
  150.3 1.4 collective-permute-start.28
  152.3 21.8 %collective-permute-done.36 = bf16[128,2048]{1,0:T(8,128)(2,1)S(1)} collective-permute-done((bf16[128,2048]{1,0:T(8,128)(2,1)S(1)}, bf16[128,2048]{1,0:T(8,128)(2,1)S(1)}, u32[]{:S(2)}, u32[]{:S(2)}) %collective-permute-start.36) | collective-permute-done | bytes 524320 | tf_op jit(solution)/shard_map/ppermute | solution.py:218
  174.1 1.3 collective-permute-start.37
  175.4 1.3 collective-permute-start.29
  178.5 20.4 %collective-permute-done.37 = bf16[128,2048]{1,0:T(8,128)(2,1)S(1)} collective-permute-done((bf16[128,2048]{1,0:T(8,128)(2,1)S(1)}, bf16[128,2048]{1,0:T(8,128)(2,1)S(1)}, u32[]{:S(2)}, u32[]{:S(2)}) %collective-permute-start.37) | collective-permute-done | bytes 524320 | tf_op jit(solution)/shard_map/ppermute | solution.py:218
  200.3 1.3 collective-permute-start.40
  203.6 18.9 %collective-permute-done.38 = bf16[128,2048]{1,0:T(8,128)(2,1)S(1)} collective-permute-done((bf16[128,2048]{1,0:T(8,128)(2,1)S(1)}, bf16[128,2048]{1,0:T(8,128)(2,1)S(1)}, u32[]{:S(2)}, u32[]{:S(2)}) %collective-permute-start.38) | collective-permute-done | bytes 524320 | tf_op jit(solution)/shard_map/ppermute | solution.py:218
  224.0 1.9 collective-permute-start.41
  228.8 14.1 %collective-permute-done.39 = bf16[128,2048]{1,0:T(8,128)(2,1)S(1)} collective-permute-done((bf16[128,2048]{1,0:T(8,128)(2,1)S(1)}, bf16[128,2048]{1,0:T(8,128)(2,1)S(1)}, u32[]{:S(2)}, u32[]{:S(2)}) %collective-permute-start.39) | collective-permute-done | bytes 524320 | tf_op jit(solution)/shard_map/ppermute | solution.py:218
  243.0 1.3 add_convert_fusion
  (91 shorter events, 22.5 us)
Async XLA Ops:
  0.0 31.2 %collective-permute-start.4 = (bf16[512,2048]{1,0:T(8,128)(2,1)}, bf16[512,2048]{1,0:T(8,128)(2,1)}, u32[]{:S(2)}, u32[]{:S(2)}) collective-permute-start(bf16[512,2048]{1,0:T(8,128)(2,1)} %own_w.1), channel_id=1, source_target_pairs={{0,1},{1,0},{2,3},{3,2},{4,5},{5,4},{6,7},{7,6},{8,9},{9,8},{10,11... | collective-permute-start | bytes 6291464 | tf_op jit(solution)/shard_map/ppermute | solution.py:311
  0.0 9.3 %collective-permute-start = (bf16[256,512]{1,0:T(8,128)(2,1)}, bf16[256,512]{1,0:T(8,128)(2,1)S(1)}, u32[]{:S(2)}, u32[]{:S(2)}) collective-permute-start(bf16[256,512]{1,0:T(8,128)(2,1)} %refs_1_.1), channel_id=1, source_target_pairs={{0,2},{2,0},{4,6},{6,4},{8,10},{10,8},{12,14},{14,12},{16,18},{18,... | collective-permute-start | bytes 786440 | tf_op jit(solution)/shard_map/ppermute | solution.py:20
  0.5 14.0 %collective-permute-start.2 = (bf16[256,512]{1,0:T(8,128)(2,1)}, bf16[256,512]{1,0:T(8,128)(2,1)S(1)}, u32[]{:S(2)}, u32[]{:S(2)}) collective-permute-start(bf16[256,512]{1,0:T(8,128)(2,1)} %refs_4_.1), channel_id=1, source_target_pairs={{0,2},{2,0},{4,6},{6,4},{8,10},{10,8},{12,14},{14,12},{16,18},{18,... | collective-permute-start | bytes 786440 | tf_op jit(solution)/shard_map/ppermute | solution.py:20
  2.7 3.7 %collective-permute-start.7 = (f32[16,128]{1,0:T(8,128)S(1)}, f32[16,128]{1,0:T(8,128)S(1)}, u32[]{:S(2)}, u32[]{:S(2)}) collective-permute-start(f32[16,128]{1,0:T(8,128)S(1)} %select_reduce_fusion.refs_4_.refs_5_.refs_2_.refs_1_), channel_id=1, source_target_pairs={{0,8},{2,10},{4,12},{6,14},{8,0},{10,2},{12,4},{14,6},{16,24},{18,... | collective-permute-start | bytes 24584 | tf_op jit(solution)/shard_map/ppermute | solution.py:20
  6.5 11.4 %collective-permute-start.8 = (f32[16,256]{1,0:T(8,128)S(1)}, f32[16,256]{1,0:T(8,128)S(1)}, u32[]{:S(2)}, u32[]{:S(2)}) collective-permute-start(f32[16,256]{1,0:T(8,128)S(1)} %pad_maximum_fusion.2), channel_id=1, source_target_pairs={{0,16},{2,18},{4,20},{6,22},{8,24},{10,26},{12,28},{14,30},{16,0},... | collective-permute-start | bytes 49160 | tf_op jit(solution)/shard_map/ppermute | solution.py:20
  9.3 21.9 %copy-start.10 = (bf16[256,512]{1,0:T(8,128)(2,1)}, bf16[256,512]{1,0:T(8,128)(2,1)S(1)}, u32[]{:S(2)}) copy-start(bf16[256,512]{1,0:T(8,128)(2,1)S(1)} %collective-permute-done.refs_0_) | copy-start | bytes 786436
  9.3 20.0 %collective-permute-start.1 = (bf16[256,512]{1,0:T(8,128)(2,1)S(1)}, bf16[256,512]{1,0:T(8,128)(2,1)S(1)}, u32[]{:S(2)}, u32[]{:S(2)}) collective-permute-start(bf16[256,512]{1,0:T(8,128)(2,1)S(1)} %collective-permute-done.refs_0_), channel_id=1, source_target_pairs={{0,4},{4,8},{8,12},{12,16},{16,20},{20,24},{24,28},{6,2},{10,6},{1... | collective-permute-start | bytes 786440 | tf_op jit(solution)/shard_map/ppermute | solution.py:309
  14.6 16.6 %copy-start.11 = (bf16[256,512]{1,0:T(8,128)(2,1)}, bf16[256,512]{1,0:T(8,128)(2,1)S(1)}, u32[]{:S(2)}) copy-start(bf16[256,512]{1,0:T(8,128)(2,1)S(1)} %collective-permute-done.2.refs_3_) | copy-start | bytes 786436
  14.6 14.8 %collective-permute-start.3 = (bf16[256,512]{1,0:T(8,128)(2,1)S(1)}, bf16[256,512]{1,0:T(8,128)(2,1)S(1)}, u32[]{:S(2)}, u32[]{:S(2)}) collective-permute-start(bf16[256,512]{1,0:T(8,128)(2,1)S(1)} %collective-permute-done.2.refs_3_), channel_id=1, source_target_pairs={{0,4},{4,8},{8,12},{12,16},{16,20},{20,24},{24,28},{6,2},{10,6},{1... | collective-permute-start | bytes 786440 | tf_op jit(solution)/shard_map/ppermute | solution.py:309
  17.9 7.2 %collective-permute-start.9 = (f32[16,512]{1,0:T(8,128)S(1)}, f32[16,512]{1,0:T(8,128)S(1)}, u32[]{:S(2)}, u32[]{:S(2)}) collective-permute-start(f32[16,512]{1,0:T(8,128)S(1)} %pad_maximum_fusion.1), channel_id=1, source_target_pairs={{0,4},{2,6},{4,0},{6,2},{8,12},{10,14},{12,8},{14,10},{16,20},{18,... | collective-permute-start | bytes 98312 | tf_op jit(solution)/shard_map/ppermute | solution.py:20
  18.6 12.6 %collective-permute-start.5 = (bf16[352,2048]{1,0:T(8,128)(2,1)}, bf16[352,2048]{1,0:T(8,128)(2,1)}, u32[]{:S(2)}, u32[]{:S(2)}) collective-permute-start(bf16[352,2048]{1,0:T(8,128)(2,1)} %bitcast.14), channel_id=1, source_target_pairs={{0,1},{1,0},{2,3},{3,2},{4,5},{5,4},{6,7},{7,6},{8,9},{9,8},{10,11... | collective-permute-start | bytes 4325384 | tf_op jit(solution)/shard_map/ppermute | solution.py:318
  25.1 4.3 %collective-permute-start.10 = (f32[16,1024]{1,0:T(8,128)S(1)}, f32[16,1024]{1,0:T(8,128)S(1)}, u32[]{:S(2)}, u32[]{:S(2)}) collective-permute-start(f32[16,1024]{1,0:T(8,128)S(1)} %pad_maximum_fusion), channel_id=1, source_target_pairs={{0,2},{2,0},{4,6},{6,4},{8,10},{10,8},{12,14},{14,12},{16,18},{18,... | collective-permute-start | bytes 196616 | tf_op jit(solution)/shard_map/ppermute | solution.py:20
  30.1 7.6 %collective-permute-start.11 = (bf16[352,2048]{1,0:T(8,128)(2,1)}, bf16[352,2048]{1,0:T(8,128)(2,1)}, u32[]{:S(2)}, u32[]{:S(2)}) collective-permute-start(bf16[352,2048]{1,0:T(8,128)(2,1)} %bitcast.16), channel_id=1, source_target_pairs={{0,1},{1,0},{2,3},{3,2},{4,5},{5,4},{6,7},{7,6},{8,9},{9,8},{10,11... | collective-permute-start | bytes 4325384 | tf_op jit(solution)/shard_map/ppermute | solution.py:320
  30.1 7.6 %collective-permute-start.12 = (bf16[352,2048]{1,0:T(8,128)(2,1)}, bf16[352,2048]{1,0:T(8,128)(2,1)}, u32[]{:S(2)}, u32[]{:S(2)}) collective-permute-start(bf16[352,2048]{1,0:T(8,128)(2,1)} %bitcast.18), channel_id=1, source_target_pairs={{0,1},{1,0},{2,3},{3,2},{4,5},{5,4},{6,7},{7,6},{8,9},{9,8},{10,11... | collective-permute-start | bytes 4325384 | tf_op jit(solution)/shard_map/ppermute | solution.py:321
  37.6 1.6 collective-permute-start.6
  44.2 14.3 %collective-permute-start.16 = (bf16[128,2048]{1,0:T(8,128)(2,1)}, bf16[128,2048]{1,0:T(8,128)(2,1)}, u32[]{:S(2)}, u32[]{:S(2)}) collective-permute-start(bf16[128,2048]{1,0:T(8,128)(2,1)} %get-tuple-element.61.refs_0_), channel_id=1, source_target_pairs={{8,0},{10,2},{12,4},{14,6},{16,8},{18,10},{20,12},{22,14},{24,16},... | collective-permute-start | bytes 1572872 | tf_op jit(solution)/shard_map/ppermute | solution.py:218
  44.6 14.7 %collective-permute-start.15 = (bf16[128,2048]{1,0:T(8,128)(2,1)}, bf16[128,2048]{1,0:T(8,128)(2,1)}, u32[]{:S(2)}, u32[]{:S(2)}) collective-permute-start(bf16[128,2048]{1,0:T(8,128)(2,1)} %get-tuple-element.61.refs_0_), channel_id=1, source_target_pairs={{0,4},{2,6},{4,0},{6,2},{8,12},{10,14},{12,8},{14,10},{16,20},{18,... | collective-permute-start | bytes 1572872 | tf_op jit(solution)/shard_map/ppermute | solution.py:20
  47.0 15.5 %collective-permute-start.14 = (bf16[128,2048]{1,0:T(8,128)(2,1)}, bf16[128,2048]{1,0:T(8,128)(2,1)S(1)}, u32[]{:S(2)}, u32[]{:S(2)}) collective-permute-start(bf16[128,2048]{1,0:T(8,128)(2,1)} %get-tuple-element.61.refs_0_), channel_id=1, source_target_pairs={{0,2},{2,0},{4,6},{6,4},{8,10},{10,8},{12,14},{14,12},{16,18},{18,... | collective-permute-start | bytes 1572872 | tf_op jit(solution)/shard_map/ppermute | solution.py:20
  47.1 25.4 %collective-permute-start.13 = (bf16[128,2048]{1,0:T(8,128)(2,1)}, bf16[128,2048]{1,0:T(8,128)(2,1)S(1)}, u32[]{:S(2)}, u32[]{:S(2)}) collective-permute-start(bf16[128,2048]{1,0:T(8,128)(2,1)} %get-tuple-element.61.refs_0_), channel_id=1, source_target_pairs={{24,0},{26,2},{28,4},{30,6},{0,8},{2,10},{4,12},{6,14},{8,16},{10,... | collective-permute-start | bytes 1572872 | tf_op jit(solution)/shard_map/ppermute | solution.py:218
  59.3 26.9 %collective-permute-start.17 = (bf16[128,2048]{1,0:T(8,128)(2,1)}, bf16[128,2048]{1,0:T(8,128)(2,1)}, u32[]{:S(2)}, u32[]{:S(2)}) collective-permute-start(bf16[128,2048]{1,0:T(8,128)(2,1)} %collective-permute-done.16.refs_3_), channel_id=1, source_target_pairs={{8,0},{10,2},{12,4},{14,6},{16,8},{18,10},{20,12},{22,14},{24,16},... | collective-permute-start | bytes 1572872 | tf_op jit(solution)/shard_map/ppermute | solution.py:218
  62.2 24.1 %collective-permute-start.19 = (bf16[128,2048]{1,0:T(8,128)(2,1)}, bf16[128,2048]{1,0:T(8,128)(2,1)}, u32[]{:S(2)}, u32[]{:S(2)}) collective-permute-start(bf16[128,2048]{1,0:T(8,128)(2,1)} %collective-permute-done.16.refs_3_), channel_id=1, source_target_pairs={{0,4},{2,6},{4,0},{6,2},{8,12},{10,14},{12,8},{14,10},{16,20},{18,... | collective-permute-start | bytes 1572872 | tf_op jit(solution)/shard_map/ppermute | solution.py:20
  73.2 21.0 %collective-permute-start.18 = (bf16[128,2048]{1,0:T(8,128)(2,1)S(1)}, bf16[128,2048]{1,0:T(8,128)(2,1)}, u32[]{:S(2)}, u32[]{:S(2)}) collective-permute-start(bf16[128,2048]{1,0:T(8,128)(2,1)S(1)} %collective-permute-done.14.refs_1_), channel_id=1, source_target_pairs={{24,0},{26,2},{28,4},{30,6},{0,8},{2,10},{4,12},{6,14},{8,16},{10,... | collective-permute-start | bytes 1572872 | tf_op jit(solution)/shard_map/ppermute | solution.py:218
  74.6 21.1 %collective-permute-start.20 = (bf16[128,2048]{1,0:T(8,128)(2,1)}, bf16[128,2048]{1,0:T(8,128)(2,1)}, u32[]{:S(2)}, u32[]{:S(2)}) collective-permute-start(bf16[128,2048]{1,0:T(8,128)(2,1)} %collective-permute-done.15.refs_2_), channel_id=1, source_target_pairs={{0,2},{2,0},{4,6},{6,4},{8,10},{10,8},{12,14},{14,12},{16,18},{18,... | collective-permute-start | bytes 1572872 | tf_op jit(solution)/shard_map/ppermute | solution.py:20
  79.8 18.6 %copy-start.2 = (bf16[1408,2048]{1,0:T(8,128)(2,1)S(1)}, bf16[1408,2048]{1,0:T(8,128)(2,1)}, u32[]{:S(2)}) copy-start(bf16[1408,2048]{1,0:T(8,128)(2,1)} %copy-done) | copy-start | bytes 17301508
  79.8 18.6 %copy-start.7 = (bf16[128,2048]{1,0:T(8,128)(2,1)S(1)}, bf16[128,2048]{1,0:T(8,128)(2,1)}, u32[]{:S(2)}) copy-start(bf16[128,2048]{1,0:T(8,128)(2,1)} %copy-done.6) | copy-start | bytes 1572868
  94.3 23.7 %collective-permute-start.22 = (bf16[128,2048]{1,0:T(8,128)(2,1)}, bf16[128,2048]{1,0:T(8,128)(2,1)S(1)}, u32[]{:S(2)}, u32[]{:S(2)}) collective-permute-start(bf16[128,2048]{1,0:T(8,128)(2,1)} %collective-permute-done.15.refs_2_), channel_id=1, source_target_pairs={{24,0},{26,2},{28,4},{30,6},{0,8},{2,10},{4,12},{6,14},{8,16},{10,... | collective-permute-start | bytes 1572872 | tf_op jit(solution)/shard_map/ppermute | solution.py:218
  95.7 22.3 %collective-permute-start.23 = (bf16[128,2048]{1,0:T(8,128)(2,1)}, bf16[128,2048]{1,0:T(8,128)(2,1)S(1)}, u32[]{:S(2)}, u32[]{:S(2)}) collective-permute-start(bf16[128,2048]{1,0:T(8,128)(2,1)} %collective-permute-done.17.refs_1_), channel_id=1, source_target_pairs={{0,2},{2,0},{4,6},{6,4},{8,10},{10,8},{12,14},{14,12},{16,18},{18,... | collective-permute-start | bytes 1572872 | tf_op jit(solution)/shard_map/ppermute | solution.py:20
  97.1 20.9 %collective-permute-start.24 = (bf16[128,2048]{1,0:T(8,128)(2,1)}, bf16[128,2048]{1,0:T(8,128)(2,1)S(1)}, u32[]{:S(2)}, u32[]{:S(2)}) collective-permute-start(bf16[128,2048]{1,0:T(8,128)(2,1)} %collective-permute-done.17.refs_1_), channel_id=1, source_target_pairs={{0,4},{2,6},{4,0},{6,2},{8,12},{10,14},{12,8},{14,10},{16,20},{18,... | collective-permute-start | bytes 1572872 | tf_op jit(solution)/shard_map/ppermute | solution.py:20
  97.8 24.6 %collective-permute-start.21 = (bf16[128,2048]{1,0:T(8,128)(2,1)S(1)}, bf16[128,2048]{1,0:T(8,128)(2,1)S(1)}, u32[]{:S(2)}, u32[]{:S(2)}) collective-permute-start(bf16[128,2048]{1,0:T(8,128)(2,1)S(1)} %collective-permute-done.14.refs_1_), channel_id=1, source_target_pairs={{8,0},{10,2},{12,4},{14,6},{16,8},{18,10},{20,12},{22,14},{24,16},... | collective-permute-start | bytes 1572872 | tf_op jit(solution)/shard_map/ppermute | solution.py:218
  118.0 10.4 %collective-permute-start.25 = (bf16[128,2048]{1,0:T(8,128)(2,1)S(1)}, bf16[128,2048]{1,0:T(8,128)(2,1)S(1)}, u32[]{:S(2)}, u32[]{:S(2)}) collective-permute-start(bf16[128,2048]{1,0:T(8,128)(2,1)S(1)} %collective-permute-done.24.refs_3_), channel_id=1, source_target_pairs={{0,2},{2,0},{4,6},{6,4},{8,10},{10,8},{12,14},{14,12},{16,18},{18,... | collective-permute-start | bytes 1572872 | tf_op jit(solution)/shard_map/ppermute | solution.py:20
  119.5 21.7 %collective-permute-start.26 = (bf16[128,2048]{1,0:T(8,128)(2,1)}, bf16[128,2048]{1,0:T(8,128)(2,1)S(1)}, u32[]{:S(2)}, u32[]{:S(2)}) collective-permute-start(bf16[128,2048]{1,0:T(8,128)(2,1)} %collective-permute-done.20.refs_4_), channel_id=1, source_target_pairs={{24,0},{26,2},{28,4},{30,6},{0,8},{2,10},{4,12},{6,14},{8,16},{10,... | collective-permute-start | bytes 1572872 | tf_op jit(solution)/shard_map/ppermute | solution.py:218
  122.3 20.3 %collective-permute-start.27 = (bf16[128,2048]{1,0:T(8,128)(2,1)}, bf16[128,2048]{1,0:T(8,128)(2,1)S(1)}, u32[]{:S(2)}, u32[]{:S(2)}) collective-permute-start(bf16[128,2048]{1,0:T(8,128)(2,1)} %collective-permute-done.20.refs_4_), channel_id=1, source_target_pairs={{8,0},{10,2},{12,4},{14,6},{16,8},{18,10},{20,12},{22,14},{24,16},... | collective-permute-start | bytes 1572872 | tf_op jit(solution)/shard_map/ppermute | solution.py:218
  148.8 25.3 %collective-permute-start.36 = (bf16[128,2048]{1,0:T(8,128)(2,1)S(1)}, bf16[128,2048]{1,0:T(8,128)(2,1)S(1)}, u32[]{:S(2)}, u32[]{:S(2)}) collective-permute-start(bf16[128,2048]{1,0:T(8,128)(2,1)S(1)} %expert_rows.9), channel_id=1, source_target_pairs={{8,0},{10,2},{12,4},{14,6},{16,8},{18,10},{20,12},{22,14},{24,16},... | collective-permute-start | bytes 1572872 | tf_op jit(solution)/shard_map/ppermute | solution.py:218
  150.3 25.1 %collective-permute-start.28 = (bf16[128,2048]{1,0:T(8,128)(2,1)S(1)}, bf16[128,2048]{1,0:T(8,128)(2,1)S(1)}, u32[]{:S(2)}, u32[]{:S(2)}) collective-permute-start(bf16[128,2048]{1,0:T(8,128)(2,1)S(1)} %get-tuple-element.84), channel_id=1, source_target_pairs={{0,2},{2,0},{4,6},{6,4},{8,10},{10,8},{12,14},{14,12},{16,18},{18,... | collective-permute-start | bytes 1572872 | tf_op jit(solution)/shard_map/ppermute | solution.py:20
  151.8 26.0 %collective-permute-start.31 = (bf16[128,2048]{1,0:T(8,128)(2,1)S(1)}, bf16[128,2048]{1,0:T(8,128)(2,1)S(1)}, u32[]{:S(2)}, u32[]{:S(2)}) collective-permute-start(bf16[128,2048]{1,0:T(8,128)(2,1)S(1)} %get-tuple-element.87), channel_id=1, source_target_pairs={{24,0},{26,2},{28,4},{30,6},{0,8},{2,10},{4,12},{6,14},{8,16},{10,... | collective-permute-start | bytes 1572872 | tf_op jit(solution)/shard_map/ppermute | solution.py:218
  174.1 24.7 %collective-permute-start.37 = (bf16[128,2048]{1,0:T(8,128)(2,1)S(1)}, bf16[128,2048]{1,0:T(8,128)(2,1)S(1)}, u32[]{:S(2)}, u32[]{:S(2)}) collective-permute-start(bf16[128,2048]{1,0:T(8,128)(2,1)S(1)} %get-tuple-element.96), channel_id=1, source_target_pairs={{8,0},{10,2},{12,4},{14,6},{16,8},{18,10},{20,12},{22,14},{24,16},... | collective-permute-start | bytes 1572872 | tf_op jit(solution)/shard_map/ppermute | solution.py:218
  175.4 24.8 %collective-permute-start.29 = (bf16[128,2048]{1,0:T(8,128)(2,1)S(1)}, bf16[128,2048]{1,0:T(8,128)(2,1)S(1)}, u32[]{:S(2)}, u32[]{:S(2)}) collective-permute-start(bf16[128,2048]{1,0:T(8,128)(2,1)S(1)} %get-tuple-element.85), channel_id=1, source_target_pairs={{0,2},{2,0},{4,6},{6,4},{8,10},{10,8},{12,14},{14,12},{16,18},{18,... | collective-permute-start | bytes 1572872 | tf_op jit(solution)/shard_map/ppermute | solution.py:20
  176.9 24.7 %collective-permute-start.30 = (bf16[128,2048]{1,0:T(8,128)(2,1)S(1)}, bf16[128,2048]{1,0:T(8,128)(2,1)S(1)}, u32[]{:S(2)}, u32[]{:S(2)}) collective-permute-start(bf16[128,2048]{1,0:T(8,128)(2,1)S(1)} %add_convert_fusion.8), channel_id=1, source_target_pairs={{0,4},{2,6},{4,0},{6,2},{8,12},{10,14},{12,8},{14,10},{16,20},{18,... | collective-permute-start | bytes 1572872 | tf_op jit(solution)/shard_map/ppermute | solution.py:20
  177.7 24.1 %collective-permute-start.32 = (bf16[128,2048]{1,0:T(8,128)(2,1)S(1)}, bf16[128,2048]{1,0:T(8,128)(2,1)S(1)}, u32[]{:S(2)}, u32[]{:S(2)}) collective-permute-start(bf16[128,2048]{1,0:T(8,128)(2,1)S(1)} %get-tuple-element.88), channel_id=1, source_target_pairs={{24,0},{26,2},{28,4},{30,6},{0,8},{2,10},{4,12},{6,14},{8,16},{10,... | collective-permute-start | bytes 1572872 | tf_op jit(solution)/shard_map/ppermute | solution.py:218
  198.8 23.7 %collective-permute-start.38 = (bf16[128,2048]{1,0:T(8,128)(2,1)S(1)}, bf16[128,2048]{1,0:T(8,128)(2,1)S(1)}, u32[]{:S(2)}, u32[]{:S(2)}) collective-permute-start(bf16[128,2048]{1,0:T(8,128)(2,1)S(1)} %get-tuple-element.97), channel_id=1, source_target_pairs={{8,0},{10,2},{12,4},{14,6},{16,8},{18,10},{20,12},{22,14},{24,16},... | collective-permute-start | bytes 1572872 | tf_op jit(solution)/shard_map/ppermute | solution.py:218
  200.3 23.7 %collective-permute-start.40 = (bf16[128,2048]{1,0:T(8,128)(2,1)S(1)}, bf16[128,2048]{1,0:T(8,128)(2,1)S(1)}, u32[]{:S(2)}, u32[]{:S(2)}) collective-permute-start(bf16[128,2048]{1,0:T(8,128)(2,1)S(1)} %add_convert_fusion.3), channel_id=1, source_target_pairs={{0,2},{2,0},{4,6},{6,4},{8,10},{10,8},{12,14},{14,12},{16,18},{18,... | collective-permute-start | bytes 1572872 | tf_op jit(solution)/shard_map/ppermute | solution.py:20
  201.9 24.3 %collective-permute-start.34 = (bf16[128,2048]{1,0:T(8,128)(2,1)S(1)}, bf16[128,2048]{1,0:T(8,128)(2,1)S(1)}, u32[]{:S(2)}, u32[]{:S(2)}) collective-permute-start(bf16[128,2048]{1,0:T(8,128)(2,1)S(1)} %get-tuple-element.91), channel_id=1, source_target_pairs={{0,4},{2,6},{4,0},{6,2},{8,12},{10,14},{12,8},{14,10},{16,20},{18,... | collective-permute-start | bytes 1572872 | tf_op jit(solution)/shard_map/ppermute | solution.py:20
  202.7 24.6 %collective-permute-start.33 = (bf16[128,2048]{1,0:T(8,128)(2,1)S(1)}, bf16[128,2048]{1,0:T(8,128)(2,1)S(1)}, u32[]{:S(2)}, u32[]{:S(2)}) collective-permute-start(bf16[128,2048]{1,0:T(8,128)(2,1)S(1)} %add_convert_fusion.7), channel_id=1, source_target_pairs={{24,0},{26,2},{28,4},{30,6},{0,8},{2,10},{4,12},{6,14},{8,16},{10,... | collective-permute-start | bytes 1572872 | tf_op jit(solution)/shard_map/ppermute | solution.py:218
  222.5 20.4 %collective-permute-start.39 = (bf16[128,2048]{1,0:T(8,128)(2,1)S(1)}, bf16[128,2048]{1,0:T(8,128)(2,1)S(1)}, u32[]{:S(2)}, u32[]{:S(2)}) collective-permute-start(bf16[128,2048]{1,0:T(8,128)(2,1)S(1)} %get-tuple-element.98), channel_id=1, source_target_pairs={{8,0},{10,2},{12,4},{14,6},{16,8},{18,10},{20,12},{22,14},{24,16},... | collective-permute-start | bytes 1572872 | tf_op jit(solution)/shard_map/ppermute | solution.py:218
  224.0 19.0 %collective-permute-start.41 = (bf16[128,2048]{1,0:T(8,128)(2,1)S(1)}, bf16[128,2048]{1,0:T(8,128)(2,1)S(1)}, u32[]{:S(2)}, u32[]{:S(2)}) collective-permute-start(bf16[128,2048]{1,0:T(8,128)(2,1)S(1)} %add_convert_fusion.4), channel_id=1, source_target_pairs={{0,2},{2,0},{4,6},{6,4},{8,10},{10,8},{12,14},{14,12},{16,18},{18,... | collective-permute-start | bytes 1572872 | tf_op jit(solution)/shard_map/ppermute | solution.py:20
  226.1 16.8 %copy-start.9 = (f32[128,2048]{1,0:T(8,128)S(1)}, f32[128,2048]{1,0:T(8,128)}, u32[]{:S(2)}) copy-start(f32[128,2048]{1,0:T(8,128)} %get-tuple-element.59) | copy-start | bytes 3145732
  226.2 16.8 %collective-permute-start.42 = (bf16[128,2048]{1,0:T(8,128)(2,1)S(1)}, bf16[128,2048]{1,0:T(8,128)(2,1)S(1)}, u32[]{:S(2)}, u32[]{:S(2)}) collective-permute-start(bf16[128,2048]{1,0:T(8,128)(2,1)S(1)} %add_convert_fusion.1), channel_id=1, source_target_pairs={{0,4},{2,6},{4,0},{6,2},{8,12},{10,14},{12,8},{14,10},{16,20},{18,... | collective-permute-start | bytes 1572872 | tf_op jit(solution)/shard_map/ppermute | solution.py:20
  227.6 15.4 %collective-permute-start.35 = (bf16[128,2048]{1,0:T(8,128)(2,1)S(1)}, bf16[128,2048]{1,0:T(8,128)(2,1)S(1)}, u32[]{:S(2)}, u32[]{:S(2)}) collective-permute-start(bf16[128,2048]{1,0:T(8,128)(2,1)S(1)} %add_convert_fusion.6), channel_id=1, source_target_pairs={{24,0},{26,2},{28,4},{30,6},{0,8},{2,10},{4,12},{6,14},{8,16},{10,... | collective-permute-start | bytes 1572872 | tf_op jit(solution)/shard_map/ppermute | solution.py:218
  (10 other events, 14.3 us)

commit v9 on v6

--- a/solution.py
+++ b/solution.py
@@ -29,105 +29,102 @@
     return masks[2:] + masks[1::-1]
 
 
-def gather_gates(block):
-    pieces = [block]
-    for mask in gate_order(lax.axis_size("seq")):
-        pieces.append(flip(block, mask))
-        block = jnp.concatenate([block, pieces[-1]], axis=1)
-    return pieces
+def gather_gates(pieces, *waits):
+    held = jnp.concatenate(pieces, axis=1) if len(pieces) > 1 else pieces[0]
+    mask = gate_order(lax.axis_size("seq"))[len(pieces) - 1]
+    return [*pieces, flip(after(held, *waits) if waits else held, mask)]
 
 
 def place_of(j):
     return sum(1 << bit for bit, mask in enumerate(gate_order(lax.axis_size("seq"))) if j & mask)
 
 
-def stack_kernel(keys_ref, values_ref, out_ref):
-    rows = keys_ref.shape[0]
-    out_ref[:rows] = keys_ref[...]
-    out_ref[rows:] = values_ref[...]
-
-
-def stack(keys, values):
-    rows, width = keys.shape
-    return pl.pallas_call(
-        stack_kernel,
-        out_shape=jax.ShapeDtypeStruct((2 * rows, width), keys.dtype),
-        in_specs=[VMEM, VMEM],
-        out_specs=VMEM,
-        compiler_params=pltpu.CompilerParams(vmem_limit_bytes=63 * 1024 * 1024),
-        name="stack_keys_values",
-    )(keys, values)
-
-
-def attention_kernel(core_ref, q_ref, before_ref, own_ref, after_ref, ids_ref, *refs):
-    theirs_ref, mine_ref, both = refs[-3:]
+def attention_kernel(where_ref, q_ref, ids_ref, *refs):
+    keys, values, (theirs_ref, mine_ref, both) = refs[:3], refs[3:6], refs[-3:]
     rows = q_ref.shape[0]
     some = rows // 2
+    core, odd = where_ref[0], where_ref[1]
     scale = 1.0 / math.sqrt(HD)
-    column = jnp.transpose(jnp.broadcast_to(ids_ref[:, rows : 2 * rows], (HD, rows)))[:, :1]
-    for half in range(2):
-        first = half * some
-        spans = [
-            (before_ref, half * some, rows),
-            (own_ref, 0, rows),
-            (after_ref, 0, some + half * some),
-        ]
-        keys = 2 * rows + some
-        query_pos = lax.broadcasted_iota(jnp.int32, (some, keys), 0) + (first + rows)
-        key_pos = lax.broadcasted_iota(jnp.int32, (some, keys), 1) + first
-        allowed = (column[first : first + some] == ids_ref[:, first : first + keys]) & (
-            jnp.abs(query_pos - key_pos) < rows
+    ids = [ids_ref[:, i * rows : (i + 1) * rows] for i in range(3)]
+    column = jnp.transpose(jnp.broadcast_to(ids[1], (HD, rows)))[:, :1]
+    back, front = jnp.where(odd == 1, ids[0], ids[2]), jnp.where(odd == 1, ids[2], ids[0])
+    apart = lax.broadcasted_iota(jnp.int32, (rows, rows), 0) - lax.broadcasted_iota(
+        jnp.int32, (rows, rows), 1
+    )
+    side = rows * (2 * odd - 1)
+    allowed = jnp.concatenate(
+        [
+            (column == back) & (jnp.abs(apart + side) < rows),
+            column == ids[1],
+            (column == front) & (jnp.abs(apart - side) < rows),
+        ],
+        axis=1,
+    )
+    for head in range(q_ref.shape[1] // HD):
+        cols = slice(head * HD, (head + 1) * HD)
+        query = q_ref[:, cols]
+        score = jnp.concatenate(
+            [
+                lax.dot_general(query, ref[:, cols], NT, preferred_element_type=jnp.float32)
+                for ref in keys
+            ],
+            axis=1,
         )
-        for head in range(q_ref.shape[1] // HD):
-            cols = slice(head * HD, (head + 1) * HD)
-            query = q_ref[first : first + some, cols]
-            score = jnp.concatenate(
-                [
-                    lax.dot_general(query, ref[lo:hi, cols], NT, preferred_element_type=jnp.float32)
-                    for ref, lo, hi in spans
-                ],
-                axis=1,
+        score = jnp.where(allowed, score * scale, -jnp.inf)
+        weights = jnp.exp(score - jnp.max(score, axis=-1, keepdims=True))
+        share = 1.0 / jnp.sum(weights, axis=-1, keepdims=True)
+        probs = (weights * share).astype(jnp.bfloat16)
+        total = jnp.zeros((rows, HD), jnp.float32)
+        for i, ref in enumerate(values):
+            total += jnp.dot(
+                probs[:, i * rows : (i + 1) * rows], ref[:, cols], preferred_element_type=jnp.float32
             )
-            score = jnp.where(allowed, score * scale, -jnp.inf)
-            weights = jnp.exp(score - jnp.max(score, axis=-1, keepdims=True))
-            share = 1.0 / jnp.sum(weights, axis=-1, keepdims=True)
-            probs = (weights * share).astype(jnp.bfloat16)
-            total, at = jnp.zeros((some, HD), jnp.float32), 0
-            for ref, lo, hi in spans:
-                total += jnp.dot(
-                    probs[:, at : at + hi - lo],
-                    ref[rows + lo : rows + hi, cols],
-                    preferred_element_type=jnp.float32,
-                )
-                at += hi - lo
-            both[first : first + some, cols] = total.astype(jnp.bfloat16)
-    at = pl.multiple_of(core_ref[0] * some, some)
+        both[:, cols] = total.astype(jnp.bfloat16)
+    at = pl.multiple_of(core * some, some)
     mine_ref[...] = both[pl.ds(at, some), :]
     theirs_ref[...] = both[pl.ds(some - at, some), :]
 
 
-def attention(core, queries, near, ids, *ahead):
+def attention(where, queries, ids, near_keys, near_values, *ahead):
     rows, width = queries.shape
     half = jax.ShapeDtypeStruct((rows // 2, width), jnp.bfloat16)
     return pl.pallas_call(
         attention_kernel,
         out_shape=(half, half),
-        in_specs=[pl.BlockSpec(memory_space=pltpu.SMEM)] + [VMEM] * 5 + [ANY] * len(ahead),
+        in_specs=[pl.BlockSpec(memory_space=pltpu.SMEM)] + [VMEM] * 8 + [ANY] * len(ahead),
         out_specs=(VMEM, VMEM),
         scratch_shapes=[pltpu.VMEM((rows, width), jnp.bfloat16)],
         compiler_params=pltpu.CompilerParams(vmem_limit_bytes=63 * 1024 * 1024),
         name="window_attention",
-    )(core, queries, *near, ids, *ahead)
+    )(where, queries, ids, *near_keys, *near_values, *ahead)
+
+
+PIECES = 4
 
 
 def norm_kernel(mine_ref, theirs_ref, own_w, other_w, resid_ref, gain_ref, *refs):
-    stream_ref, normed_ref = refs[-2:]
-    stream = resid_ref[...].astype(jnp.float32)
-    stream += jnp.dot(mine_ref[...], own_w[...], preferred_element_type=jnp.float32)
-    stream += jnp.dot(theirs_ref[...], other_w[...], preferred_element_type=jnp.float32)
-    meansq = jnp.mean(stream * stream, axis=-1, keepdims=True)
-    stream_ref[...] = stream
-    normed_ref[...] = (stream * lax.rsqrt(meansq + 1e-05) * gain_ref[...]).astype(jnp.bfloat16)
+    stream_ref, normed_ref, weights, sems = refs[-4:]
+    depth, piece = own_w.shape[0], own_w.shape[1] // PIECES
+    copies = []
+    for i in range(PIECES):
+        cols = pl.ds(i * piece, piece)
+        for half, ref in enumerate((own_w, other_w)):
+            target = weights.at[pl.ds(half * depth, depth), cols]
+            copies.append(pltpu.make_async_copy(ref.at[:, cols], target, sems.at[2 * i + half]))
+    for copy in copies:
+        copy.start()
+    both = jnp.concatenate([mine_ref[...], theirs_ref[...]], axis=1)
+    total = 0.0
+    for i in range(PIECES):
+        copies[2 * i].wait()
+        copies[2 * i + 1].wait()
+        cols = slice(i * piece, (i + 1) * piece)
+        part = resid_ref[:, cols].astype(jnp.float32)
+        part += jnp.dot(both, weights[:, cols], preferred_element_type=jnp.float32)
+        stream_ref[:, cols] = part
+        total += jnp.sum(part * part, axis=-1, keepdims=True)
+    scale = lax.rsqrt(total / own_w.shape[1] + 1e-05)
+    normed_ref[...] = (stream_ref[...] * scale * gain_ref[...]).astype(jnp.bfloat16)
 
 
 def project_and_norm(mine, theirs, own_w, other_w, resid, gain, *ahead):
@@ -138,8 +135,12 @@
             jax.ShapeDtypeStruct((rows, width), jnp.float32),
             jax.ShapeDtypeStruct((rows, width), jnp.bfloat16),
         ),
-        in_specs=[VMEM] * 6 + [ANY] * len(ahead),
+        in_specs=[VMEM] * 2 + [ANY] * 2 + [VMEM] * 2 + [ANY] * len(ahead),
         out_specs=(VMEM, VMEM),
+        scratch_shapes=[
+            pltpu.VMEM((2 * own_w.shape[0], width), jnp.bfloat16),
+            pltpu.SemaphoreType.DMA((2 * PIECES,)),
+        ],
         compiler_params=pltpu.CompilerParams(vmem_limit_bytes=63 * 1024 * 1024),
         name="project_and_norm",
     )(mine, theirs, own_w, other_w, resid, gain, *ahead)
@@ -229,15 +230,18 @@
 OUTWARD, INWARD, MIDDLE = [(1, 0), (2, 3)], [(0, 1), (3, 2)], [(1, 2), (2, 1)]
 
 
-def step_layer(normed, stream, run, weights):
+def step_layer(normed, stream, run, gates, weights):
     z = lax.axis_index("seq") // 4
     inner = (z == 1) | (z == 2)
 
     o0 = normed
     o1, near3, x0, y0 = flip(o0, 4), shift(o0, MIDDLE), flip(o0, 1), flip(o0, 2)
+    gates = gather_gates(gates, o0)
 
     ends2, near2 = shift(after(near3, o1), OUTWARD), shift(after(o1, near3), MIDDLE)
     d0, y1 = flip(after(y0, x0), 1), flip(after(o1, y0), 2)
+    gates = gather_gates(gates, o1, y0)
+    run = functools.partial(run, gates)
 
     ends3 = shift(after(near2, ends2), OUTWARD)
     o2 = jnp.where(inner, near2, ends2)
@@ -278,19 +282,21 @@
 def expert_layer(normed, stream, shard, gates, weights):
     count = lax.axis_size("seq")
 
-    def run(blocks, masks):
+    def run(gates, blocks, masks):
         places = tuple(place_of(mask) for mask in masks)
         return expert(blocks, places, shard, gates, weights)
 
     if count == 16:
-        return step_layer(normed, stream, run, weights)
+        return step_layer(normed, stream, run, gates, weights)
+    while len(gates) < count.bit_length():
+        gates = gather_gates(gates)
     blocks, mask = [normed], 1
     while mask < count:
         blocks = blocks + [flip(block, mask) for block in blocks]
         mask *= 2
     parts = []
     for first in range(0, count, 4):
-        parts += run(blocks[first : first + 4], range(first, first + 4))
+        parts += run(gates, blocks[first : first + 4], range(first, first + 4))
     while mask > 1:
         mask //= 2
         parts = [add_small(parts[i], flip(parts[i + mask], mask)) for i in range(mask)]
@@ -317,31 +323,33 @@
     core = lax.axis_index("exp")
     count = lax.axis_size("seq")
 
-    own = stack(keys, values)
-    before = lax.ppermute(own, "seq", [(i, i + 1) for i in range(count - 1)])
-    after_own = lax.ppermute(own, "seq", [(i + 1, i) for i in range(count - 1)])
+    def halo(part):
+        beside = flip(part, 1)
+        ahead = [(i, i + 2) for i in range(0, count - 2, 2)]
+        back = [(i + 2, i) for i in range(1, count - 2, 2)]
+        return beside, part, lax.ppermute(beside, "seq", ahead + back)
+
+    near_keys, near_values = halo(keys), halo(values)
     chosen = experts.T[:, None, :] == jnp.arange(count, dtype=jnp.int32)[None, :, None]
-    all_gates = gather_gates(jnp.sum(jnp.where(chosen, gates.T[:, None, :], 0.0), axis=0))
-    some_gates = all_gates[-2]
+    some_gates = [jnp.sum(jnp.where(chosen, gates.T[:, None, :], 0.0), axis=0)]
+    some_gates = gather_gates(gather_gates(some_gates))
     id_pad = jnp.pad(pair_ids, (tok_rows, tok_rows), constant_values=-1)
     ids = lax.dynamic_slice_in_dim(id_pad, shard * tok_rows, 3 * tok_rows, 0)[None, :]
     out_other = lax.ppermute(out_weight, "exp", SWAP)
     gate_w, up_w = jnp.swapaxes(w_gate[0], 0, 1), jnp.swapaxes(w_up[0], 0, 1)
     gate_other = lax.ppermute(gate_w, "exp", SWAP)
-    ready = (before, after_own, some_gates, ids)
+    ready = (*near_keys, *near_values, some_gates[-1], ids)
     up_other = lax.ppermute(after(up_w, *ready), "exp", SWAP)
     down_other = lax.ppermute(after(w_down[0], *ready), "exp", SWAP)
     halves = [gate_w, gate_other, up_w, up_other, w_down[0], down_other]
 
-    theirs, mine = attention(
-        core.reshape(1), queries, (before, own, after_own), ids, out_other, gate_other
+    where = jnp.stack([core, shard % 2])
+    theirs, mine = attention(where, queries, ids, near_keys, near_values, out_other, gate_other)
+    received = lax.ppermute(theirs, "exp", SWAP)
+    stream, normed = project_and_norm(
+        mine, received, out_weight, out_other, resid, norm_gain[None, :], up_other, down_other
     )
-    received = lax.ppermute(theirs, "exp", SWAP)
-    ahead = (up_other, down_other, all_gates[-1])
-    stream, normed = project_and_norm(
-        mine, received, out_weight, out_other, resid, norm_gain[None, :], *ahead
-    )
-    mixed = expert_layer(normed, stream, shard.reshape(1), all_gates, assemble(halves))
+    mixed = expert_layer(normed, stream, shard.reshape(1), some_gates, assemble(halves))
     return mixed.astype(jnp.bfloat16)
 
 

time: 201 us -> 204 us (1.015)
  waiting for transfers between devices: 90 us -> 94 us
    ppermute x30 -> x32, waiting for transfers between devices: 68.2 us -> 78.9 us  [flip(): return lax.ppermute(block, 'seq', [(i, i ^ mask) for i in range(count)])]
    ppermute x8, waiting for transfers between devices: 21.7 us -> 13.5 us  [shift(): lax.ppermute(block, 'seq', [(4 * a + i, 4 * b + i) for a, b in pairs for...]
    unnamed x18 -> x20, local copies, waits for them, and re-layouts: 5.01 us -> 5.49 us
    ppermute x30 -> x32, starting transfers between devices: 31.9 us -> 32.1 us  [flip(): return lax.ppermute(block, 'seq', [(i, i ^ mask) for i in range(count)])]
  transfers between devices with their start and end apart: 45 -> 47, of which waited for: 27 -> 29; matrix products, arithmetic and copies ran while one was open for 3% -> 3% of each run, Pallas kernels for 16% -> 15%
where the time goes in v9:
time: 204 us; the launch traced here: 201 us
  waiting for transfers between devices  94 us (46%)
  starting transfers between devices  58.9 us (29%)
  Pallas kernels  35.2 us (17%)
  local copies, waits for them, and re-layouts  6.86 us (3%)
  other arithmetic  5.39 us (3%)
    ppermute x32, waiting for transfers between devices, flip(): return lax.ppermute(block, 'seq', [(i, i ^ mask) for i in range(count)])  78.9 us
    ppermute x32, starting transfers between devices, flip(): return lax.ppermute(block, 'seq', [(i, i ^ mask) for i in range(count)])  32.1 us
    pallas_call x5, Pallas kernels, expert(): pl.pallas_call(functools.partial(expert_kernel, places, len(gates)), out_...  22.9 us
    ppermute x8, starting transfers between devices, shift(): lax.ppermute(block, 'seq', [(4 * a + i, 4 * b + i) for a, b in pairs for...  19.5 us
    ppermute x8, waiting for transfers between devices, shift(): lax.ppermute(block, 'seq', [(4 * a + i, 4 * b + i) for a, b in pairs for...  13.5 us
    ppermute x2, starting transfers between devices, halo(): return (beside, part, lax.ppermute(beside, 'seq', ahead + back))  6.6 us
    unnamed x20, local copies, waits for them, and re-layouts  5.49 us
    pallas_call x1, Pallas kernels, project_and_norm(): pl.pallas_call(norm_kernel, out_shape=(jax.ShapeDtypeStruct((rows, width)...  5.09 us
  transfers between devices with their start and end apart: 47, of which 29 were waited for; matrix products, arithmetic and copies ran while one was open for 3% of the time, Pallas kernels for 15%

profile of v9, /device:TPU:10, one launch (start us, length us, event | category | flops | bytes accessed | tf_op | source)
XLA Modules:
  0.0 200.6 jit_solution(347047620176159817)
XLA Ops:
  0.5 1.5 collective-permute-start.2
  2.0 7.3 %collective-permute-done.refs_0_ = bf16[256,512]{1,0:T(8,128)(2,1)S(1)} collective-permute-done((bf16[256,512]{1,0:T(8,128)(2,1)}, bf16[256,512]{1,0:T(8,128)(2,1)S(1)}, u32[]{:S(2)}, u32[]{:S(2)}) %collective-permute-start) | collective-permute-done | bytes 262176 | tf_op jit(solution)/shard_map/ppermute | solution.py:20
  9.3 3.3 %collective-permute-start.1 = (bf16[256,512]{1,0:T(8,128)(2,1)S(1)}, bf16[256,512]{1,0:T(8,128)(2,1)S(1)}, u32[]{:S(2)}, u32[]{:S(2)}) collective-permute-start(bf16[256,512]{1,0:T(8,128)(2,1)S(1)} %collective-permute-done.refs_0_), channel_id=1, source_target_pairs={{0,4},{4,8},{8,12},{12,16},{16,20},{20,24},{24,28},{6,2},{10,6},{1... | collective-permute-start | bytes 786440 | tf_op jit(solution)/shard_map/ppermute | solution.py:330
  12.6 1.9 collective-permute-done.2.refs_3_
  14.6 3.3 %collective-permute-start.3 = (bf16[256,512]{1,0:T(8,128)(2,1)S(1)}, bf16[256,512]{1,0:T(8,128)(2,1)S(1)}, u32[]{:S(2)}, u32[]{:S(2)}) collective-permute-start(bf16[256,512]{1,0:T(8,128)(2,1)S(1)} %collective-permute-done.2.refs_3_), channel_id=1, source_target_pairs={{0,4},{4,8},{8,12},{12,16},{16,20},{20,24},{24,28},{6,2},{10,6},{1... | collective-permute-start | bytes 786440 | tf_op jit(solution)/shard_map/ppermute | solution.py:330
  18.7 4.7 %collective-permute-done.7.refs_5_.refs_7_.refs_4_.refs_3_.refs_2_ = f32[16,128]{1,0:T(8,128)S(1)} collective-permute-done((f32[16,128]{1,0:T(8,128)S(1)}, f32[16,128]{1,0:T(8,128)S(1)}, u32[]{:S(2)}, u32[]{:S(2)}) %collective-permute-start.7) | collective-permute-done | bytes 8224 | tf_op jit(solution)/shard_map/ppermute | solution.py:20
  23.5 2.8 %collective-permute-start.8 = (f32[16,256]{1,0:T(8,128)S(1)}, f32[16,256]{1,0:T(8,128)S(1)}, u32[]{:S(2)}, u32[]{:S(2)}) collective-permute-start(f32[16,256]{1,0:T(8,128)S(1)} %pad_maximum_fusion.2), channel_id=1, source_target_pairs={{0,16},{2,18},{4,20},{6,22},{8,24},{10,26},{12,28},{14,30},{16,0},... | collective-permute-start | bytes 49160 | tf_op jit(solution)/shard_map/ppermute | solution.py:20
  30.0 4.6 %window_attention.1 = (bf16[128,512]{1,0:T(8,128)(2,1)}, bf16[128,512]{1,0:T(8,128)(2,1)}) custom-call(s32[2]{0:T(128)} %pad_add_fusion.where_ref, bf16[256,512]{1,0:T(8,128)(2,1)} %q_ref.1, s32[1,768]{1,0:T(1,128)} %broadcast_in_dim.21.ids_ref, bf16[256,512]{1,0:T(8,128)(2,1)} %copy-done.5, bf16[256,512]{1,0:T(8,128)(2,1)} %refs_1_.1, ...), custom_call_target="tpu_custom_call" | custom-call | tf_op jit(solution)/shard_map/window_attention/pallas_call | solution.py:91
  34.6 1.5 collective-permute-done.6.theirs_ref
  36.8 5.1 %project_and_norm.1 = (f32[128,2048]{1,0:T(8,128)}, bf16[128,2048]{1,0:T(8,128)(2,1)}) custom-call(bf16[128,512]{1,0:T(8,128)(2,1)} %get-tuple-element.61.mine_ref, bf16[128,512]{1,0:T(8,128)(2,1)} %copy-done.9, bf16[512,2048]{1,0:T(8,128)(2,1)} %own_w.1, bf16[512,2048]{1,0:T(8,128)(2,1)} %collective-permute-done.4.refs_6_.other_w, ...), custom_call_target="tpu_custom_call" | custom-call | tf_op jit(solution)/shard_map/project_and_norm/pallas_call | solution.py:132
  41.9 2.5 %collective-permute-start.11 = (bf16[128,2048]{1,0:T(8,128)(2,1)}, bf16[128,2048]{1,0:T(8,128)(2,1)S(1)}, u32[]{:S(2)}, u32[]{:S(2)}) collective-permute-start(bf16[128,2048]{1,0:T(8,128)(2,1)} %get-tuple-element.69.refs_0_), channel_id=1, source_target_pairs={{0,8},{2,10},{4,12},{6,14},{8,0},{10,2},{12,4},{14,6},{16,24},{18,... | collective-permute-start | bytes 1572872 | tf_op jit(solution)/shard_map/ppermute | solution.py:20
  44.5 3.2 %collective-permute-start.12 = (bf16[128,2048]{1,0:T(8,128)(2,1)}, bf16[128,2048]{1,0:T(8,128)(2,1)S(1)}, u32[]{:S(2)}, u32[]{:S(2)}) collective-permute-start(bf16[128,2048]{1,0:T(8,128)(2,1)} %get-tuple-element.69.refs_0_), channel_id=1, source_target_pairs={{8,16},{10,18},{12,20},{14,22},{16,8},{18,10},{20,12},{22,14},{9,1... | collective-permute-start | bytes 1572872 | tf_op jit(solution)/shard_map/ppermute | solution.py:227
  47.8 2.4 %collective-permute-start.15 = (bf16[128,2048]{1,0:T(8,128)(2,1)}, bf16[128,2048]{1,0:T(8,128)(2,1)S(1)}, u32[]{:S(2)}, u32[]{:S(2)}) collective-permute-start(bf16[128,2048]{1,0:T(8,128)(2,1)} %get-tuple-element.69.refs_0_), channel_id=1, source_target_pairs={{0,2},{2,0},{4,6},{6,4},{8,10},{10,8},{12,14},{14,12},{16,18},{18,... | collective-permute-start | bytes 1572872 | tf_op jit(solution)/shard_map/ppermute | solution.py:20
  50.2 6.7 %collective-permute-done.11.refs_0_ = bf16[128,2048]{1,0:T(8,128)(2,1)S(1)} collective-permute-done((bf16[128,2048]{1,0:T(8,128)(2,1)}, bf16[128,2048]{1,0:T(8,128)(2,1)S(1)}, u32[]{:S(2)}, u32[]{:S(2)}) %collective-permute-start.11) | collective-permute-done | bytes 524320 | tf_op jit(solution)/shard_map/ppermute | solution.py:20
  56.9 3.3 %collective-permute-done.12 = bf16[128,2048]{1,0:T(8,128)(2,1)S(1)} collective-permute-done((bf16[128,2048]{1,0:T(8,128)(2,1)}, bf16[128,2048]{1,0:T(8,128)(2,1)S(1)}, u32[]{:S(2)}, u32[]{:S(2)}) %collective-permute-start.12) | collective-permute-done | bytes 524320 | tf_op jit(solution)/shard_map/ppermute | solution.py:227
  60.3 3.5 %collective-permute-start.13 = (bf16[128,2048]{1,0:T(8,128)(2,1)S(1)}, bf16[128,2048]{1,0:T(8,128)(2,1)}, u32[]{:S(2)}, u32[]{:S(2)}) collective-permute-start(bf16[128,2048]{1,0:T(8,128)(2,1)S(1)} %collective-permute-done.11.refs_0_), channel_id=1, source_target_pairs={{8,16},{10,18},{12,20},{14,22},{16,8},{18,10},{20,12},{22,14},{9,1... | collective-permute-start | bytes 1572872 | tf_op jit(solution)/shard_map/ppermute | solution.py:227
  63.8 2.1 %collective-permute-start.14 = (bf16[128,2048]{1,0:T(8,128)(2,1)S(1)}, bf16[128,2048]{1,0:T(8,128)(2,1)}, u32[]{:S(2)}, u32[]{:S(2)}) collective-permute-start(bf16[128,2048]{1,0:T(8,128)(2,1)S(1)} %collective-permute-done.12), channel_id=1, source_target_pairs={{8,0},{10,2},{12,4},{14,6},{16,24},{18,26},{20,28},{22,30},{9,1},{... | collective-permute-start | bytes 1572872 | tf_op jit(solution)/shard_map/ppermute | solution.py:227
  67.3 1.4 copy-done.1
  68.6 1.4 copy-done.2
  70.0 2.6 %assemble_weights.1 = (bf16[1408,2048]{1,0:T(8,128)(2,1)S(1)}, bf16[704,2048]{1,0:T(8,128)(2,1)S(1)}) custom-call(bf16[352,2048]{1,0:T(8,128)(2,1)S(1)} %bitcast.14, bf16[352,2048]{1,0:T(8,128)(2,1)} %collective-permute-done.5.refs_7_.refs_1_, bf16[352,2048]{1,0:T(8,128)(2,1)S(1)} %bitcast.16, bf16[352,2048]{1,0:T(8,128)(2,1)} %collective-permute-done.9.refs_0_.refs_3_, ...), custom_call_target="tpu_custom_call" | custom-call | tf_op jit(solution)/shard_map/assemble_weights/pallas_call | solution.py:164
  72.7 2.2 %collective-permute-start.17 = (bf16[128,2048]{1,0:T(8,128)(2,1)S(1)}, bf16[128,2048]{1,0:T(8,128)(2,1)S(1)}, u32[]{:S(2)}, u32[]{:S(2)}) collective-permute-start(bf16[128,2048]{1,0:T(8,128)(2,1)S(1)} %collective-permute-done.16.refs_2_), channel_id=1, source_target_pairs={{0,2},{2,0},{4,6},{6,4},{8,10},{10,8},{12,14},{14,12},{16,18},{18,... | collective-permute-start | bytes 1572872 | tf_op jit(solution)/shard_map/ppermute | solution.py:20
  74.9 2.0 collective-permute-start.19
  76.9 3.6 %collective-permute-start.23 = (bf16[128,2048]{1,0:T(8,128)(2,1)}, bf16[128,2048]{1,0:T(8,128)(2,1)S(1)}, u32[]{:S(2)}, u32[]{:S(2)}) collective-permute-start(bf16[128,2048]{1,0:T(8,128)(2,1)} %collective-permute-done.13), channel_id=1, source_target_pairs={{8,0},{10,2},{12,4},{14,6},{16,24},{18,26},{20,28},{22,30},{9,1},{... | collective-permute-start | bytes 1572872 | tf_op jit(solution)/shard_map/ppermute | solution.py:227
  81.5 4.8 %collective-permute-done.17.refs_3_ = bf16[128,2048]{1,0:T(8,128)(2,1)S(1)} collective-permute-done((bf16[128,2048]{1,0:T(8,128)(2,1)S(1)}, bf16[128,2048]{1,0:T(8,128)(2,1)S(1)}, u32[]{:S(2)}, u32[]{:S(2)}) %collective-permute-start.17) | collective-permute-done | bytes 524320 | tf_op jit(solution)/shard_map/ppermute | solution.py:20
  86.3 2.0 %collective-permute-start.21 = (bf16[128,2048]{1,0:T(8,128)(2,1)S(1)}, bf16[128,2048]{1,0:T(8,128)(2,1)S(1)}, u32[]{:S(2)}, u32[]{:S(2)}) collective-permute-start(bf16[128,2048]{1,0:T(8,128)(2,1)S(1)} %broadcast_select_fusion.1.refs_2_), channel_id=1, source_target_pairs={{0,2},{2,0},{4,6},{6,4},{8,10},{10,8},{12,14},{14,12},{16,18},{18,... | collective-permute-start | bytes 1572872 | tf_op jit(solution)/shard_map/ppermute | solution.py:20
  88.4 5.1 %expert_rows.5 = (bf16[128,2048]{1,0:T(8,128)(2,1)S(1)}, bf16[128,2048]{1,0:T(8,128)(2,1)S(1)}, bf16[128,2048]{1,0:T(8,128)(2,1)S(1)}, bf16[128,2048]{1,0:T(8,128)(2,1)S(1)}) custom-call(s32[1]{0:T(128)} %bitcast.10.shard_ref, bf16[128,2048]{1,0:T(8,128)(2,1)S(1)} %copy-done.3, bf16[128,2048]{1,0:T(8,128)(2,1)S(1)} %collective-permute-done.15.refs_1_, ...), custom_call_target="tpu_custom_call" | custom-call | tf_op jit(solution)/shard_map/expert_rows/pallas_call | solution.py:205
  93.6 4.9 %collective-permute-done.21.refs_3_ = bf16[128,2048]{1,0:T(8,128)(2,1)S(1)} collective-permute-done((bf16[128,2048]{1,0:T(8,128)(2,1)S(1)}, bf16[128,2048]{1,0:T(8,128)(2,1)S(1)}, u32[]{:S(2)}, u32[]{:S(2)}) %collective-permute-start.21) | collective-permute-done | bytes 524320 | tf_op jit(solution)/shard_map/ppermute | solution.py:20
  98.4 2.0 %collective-permute-start.24 = (bf16[128,2048]{1,0:T(8,128)(2,1)S(1)}, bf16[128,2048]{1,0:T(8,128)(2,1)S(1)}, u32[]{:S(2)}, u32[]{:S(2)}) collective-permute-start(bf16[128,2048]{1,0:T(8,128)(2,1)S(1)} %broadcast_select_fusion.refs_5_), channel_id=1, source_target_pairs={{0,2},{2,0},{4,6},{6,4},{8,10},{10,8},{12,14},{14,12},{16,18},{18,... | collective-permute-start | bytes 1572872 | tf_op jit(solution)/shard_map/ppermute | solution.py:20
  100.5 7.6 %expert_rows.6 = (bf16[128,2048]{1,0:T(8,128)(2,1)S(1)}, bf16[128,2048]{1,0:T(8,128)(2,1)S(1)}, bf16[128,2048]{1,0:T(8,128)(2,1)S(1)}, bf16[128,2048]{1,0:T(8,12...) custom-call(s32[1]{0:T(128)} %bitcast.10.shard_ref, ...), custom_call_target="tpu_custom_call" | custom-call | tf_op jit(solution)/shard_map/expert_rows/pallas_call | solution.py:205
  108.0 2.5 %collective-permute-done.24.refs_0_ = bf16[128,2048]{1,0:T(8,128)(2,1)S(1)} collective-permute-done((bf16[128,2048]{1,0:T(8,128)(2,1)S(1)}, bf16[128,2048]{1,0:T(8,128)(2,1)S(1)}, u32[]{:S(2)}, u32[]{:S(2)}) %collective-permute-start.24) | collective-permute-done | bytes 524320 | tf_op jit(solution)/shard_map/ppermute | solution.py:20
  110.5 2.0 %collective-permute-start.25 = (bf16[128,2048]{1,0:T(8,128)(2,1)S(1)}, bf16[128,2048]{1,0:T(8,128)(2,1)S(1)}, u32[]{:S(2)}, u32[]{:S(2)}) collective-permute-start(bf16[128,2048]{1,0:T(8,128)(2,1)S(1)} %collective-permute-done.22.refs_4_), channel_id=1, source_target_pairs={{0,2},{2,0},{4,6},{6,4},{8,10},{10,8},{12,14},{14,12},{16,18},{18,... | collective-permute-start | bytes 1572872 | tf_op jit(solution)/shard_map/ppermute | solution.py:20
  112.6 5.1 %expert_rows.7 = (bf16[128,2048]{1,0:T(8,128)(2,1)S(1)}, bf16[128,2048]{1,0:T(8,128)(2,1)S(1)}, bf16[128,2048]{1,0:T(8,128)(2,1)S(1)}) custom-call(s32[1]{0:T(128)} %bitcast.10.shard_ref, bf16[128,2048]{1,0:T(8,128)(2,1)S(1)} %collective-permute-done.24.refs_0_, bf16[128,2048]{1,0:T(8,128)(2,1)S(1)} %collective-permute-done.26.refs_1_, ...), custom_call_target="tpu_custom_call" | custom-call | tf_op jit(solution)/shard_map/expert_rows/pallas_call | solution.py:205
  117.8 3.0 %collective-permute-done.25.refs_0_ = bf16[128,2048]{1,0:T(8,128)(2,1)S(1)} collective-permute-done((bf16[128,2048]{1,0:T(8,128)(2,1)S(1)}, bf16[128,2048]{1,0:T(8,128)(2,1)S(1)}, u32[]{:S(2)}, u32[]{:S(2)}) %collective-permute-start.25) | collective-permute-done | bytes 524320 | tf_op jit(solution)/shard_map/ppermute | solution.py:20
  121.9 2.7 %expert_rows.8 = (bf16[128,2048]{1,0:T(8,128)(2,1)S(1)}, bf16[128,2048]{1,0:T(8,128)(2,1)S(1)}) custom-call(s32[1]{0:T(128)} %bitcast.10.shard_ref, bf16[128,2048]{1,0:T(8,128)(2,1)S(1)} %collective-permute-done.25.refs_0_, bf16[128,2048]{1,0:T(8,128)(2,1)S(1)} %collective-permute-done.28.refs_1_, ...), custom_call_target="tpu_custom_call" | custom-call | tf_op jit(solution)/shard_map/expert_rows/pallas_call | solution.py:205
  126.6 2.4 %expert_rows.9 = bf16[128,2048]{1,0:T(8,128)(2,1)S(1)} custom-call(s32[1]{0:T(128)} %bitcast.10.shard_ref, bf16[128,2048]{1,0:T(8,128)(2,1)S(1)} %collective-permute-done.36.refs_0_, f32[16,128]{1,0:T(8,128)S(1)} %select_reduce_fusion.refs_4_.refs_6_.refs_3_.refs_2_.refs_1_, f32[16,128]{1,0:T(8,128)S(1)} %collective-permute-done.7.refs_5_.refs_7_.refs_4_.refs_3_.refs_2_, ...), custom_call_target="tpu_custom_call" | custom-call | tf_op jit(solution)/shard_map/expert_rows/pallas_call | solution.py:205
  129.1 7.0 %collective-permute-done.30 = bf16[128,2048]{1,0:T(8,128)(2,1)S(1)} collective-permute-done((bf16[128,2048]{1,0:T(8,128)(2,1)S(1)}, bf16[128,2048]{1,0:T(8,128)(2,1)S(1)}, u32[]{:S(2)}, u32[]{:S(2)}) %collective-permute-start.30) | collective-permute-done | bytes 524320 | tf_op jit(solution)/shard_map/ppermute | solution.py:20
  137.6 2.1 %collective-permute-start.34 = (bf16[128,2048]{1,0:T(8,128)(2,1)S(1)}, bf16[128,2048]{1,0:T(8,128)(2,1)S(1)}, u32[]{:S(2)}, u32[]{:S(2)}) collective-permute-start(bf16[128,2048]{1,0:T(8,128)(2,1)S(1)} %add_convert_fusion.8), channel_id=1, source_target_pairs={{0,2},{2,0},{4,6},{6,4},{8,10},{10,8},{12,14},{14,12},{16,18},{18,... | collective-permute-start | bytes 1572872 | tf_op jit(solution)/shard_map/ppermute | solution.py:20
  140.1 2.4 %collective-permute-done.37 = bf16[128,2048]{1,0:T(8,128)(2,1)S(1)} collective-permute-done((bf16[128,2048]{1,0:T(8,128)(2,1)S(1)}, bf16[128,2048]{1,0:T(8,128)(2,1)S(1)}, u32[]{:S(2)}, u32[]{:S(2)}) %collective-permute-start.37) | collective-permute-done | bytes 524320 | tf_op jit(solution)/shard_map/ppermute | solution.py:20
  142.6 8.6 %collective-permute-done.34 = bf16[128,2048]{1,0:T(8,128)(2,1)S(1)} collective-permute-done((bf16[128,2048]{1,0:T(8,128)(2,1)S(1)}, bf16[128,2048]{1,0:T(8,128)(2,1)S(1)}, u32[]{:S(2)}, u32[]{:S(2)}) %collective-permute-start.34) | collective-permute-done | bytes 524320 | tf_op jit(solution)/shard_map/ppermute | solution.py:20
  151.2 2.5 %collective-permute-start.35 = (bf16[128,2048]{1,0:T(8,128)(2,1)S(1)}, bf16[128,2048]{1,0:T(8,128)(2,1)S(1)}, u32[]{:S(2)}, u32[]{:S(2)}) collective-permute-start(bf16[128,2048]{1,0:T(8,128)(2,1)S(1)} %get-tuple-element.101), channel_id=1, source_target_pairs={{0,2},{2,0},{4,6},{6,4},{8,10},{10,8},{12,14},{14,12},{16,18},{18,... | collective-permute-start | bytes 1572872 | tf_op jit(solution)/shard_map/ppermute | solution.py:20
  156.2 10.2 %collective-permute-done.35 = bf16[128,2048]{1,0:T(8,128)(2,1)S(1)} collective-permute-done((bf16[128,2048]{1,0:T(8,128)(2,1)S(1)}, bf16[128,2048]{1,0:T(8,128)(2,1)S(1)}, u32[]{:S(2)}, u32[]{:S(2)}) %collective-permute-start.35) | collective-permute-done | bytes 524320 | tf_op jit(solution)/shard_map/ppermute | solution.py:20
  166.4 1.7 collective-permute-start.44
  171.2 2.3 %collective-permute-start.40 = (bf16[128,2048]{1,0:T(8,128)(2,1)S(1)}, bf16[128,2048]{1,0:T(8,128)(2,1)S(1)}, u32[]{:S(2)}, u32[]{:S(2)}) collective-permute-start(bf16[128,2048]{1,0:T(8,128)(2,1)S(1)} %add_convert_fusion.6), channel_id=1, source_target_pairs={{8,16},{10,18},{12,20},{14,22},{16,8},{18,10},{20,12},{22,14},{9,1... | collective-permute-start | bytes 1572872 | tf_op jit(solution)/shard_map/ppermute | solution.py:227
  173.5 6.7 %collective-permute-done.44 = bf16[128,2048]{1,0:T(8,128)(2,1)S(1)} collective-permute-done((bf16[128,2048]{1,0:T(8,128)(2,1)S(1)}, bf16[128,2048]{1,0:T(8,128)(2,1)S(1)}, u32[]{:S(2)}, u32[]{:S(2)}) %collective-permute-start.44) | collective-permute-done | bytes 524320 | tf_op jit(solution)/shard_map/ppermute | solution.py:20
  180.3 1.8 collective-permute-done.33
  185.0 2.6 %collective-permute-done.40 = bf16[128,2048]{1,0:T(8,128)(2,1)S(1)} collective-permute-done((bf16[128,2048]{1,0:T(8,128)(2,1)S(1)}, bf16[128,2048]{1,0:T(8,128)(2,1)S(1)}, u32[]{:S(2)}, u32[]{:S(2)}) %collective-permute-start.40) | collective-permute-done | bytes 524320 | tf_op jit(solution)/shard_map/ppermute | solution.py:227
  187.6 2.3 %collective-permute-start.43 = (bf16[128,2048]{1,0:T(8,128)(2,1)S(1)}, bf16[128,2048]{1,0:T(8,128)(2,1)S(1)}, u32[]{:S(2)}, u32[]{:S(2)}) collective-permute-start(bf16[128,2048]{1,0:T(8,128)(2,1)S(1)} %add_convert_fusion.4), channel_id=1, source_target_pairs={{8,16},{10,18},{12,20},{14,22},{16,8},{18,10},{20,12},{22,14},{9,1... | collective-permute-start | bytes 1572872 | tf_op jit(solution)/shard_map/ppermute | solution.py:227
  192.3 6.4 %collective-permute-done.43 = bf16[128,2048]{1,0:T(8,128)(2,1)S(1)} collective-permute-done((bf16[128,2048]{1,0:T(8,128)(2,1)S(1)}, bf16[128,2048]{1,0:T(8,128)(2,1)S(1)}, u32[]{:S(2)}, u32[]{:S(2)}) %collective-permute-start.43) | collective-permute-done | bytes 524320 | tf_op jit(solution)/shard_map/ppermute | solution.py:227
  (93 shorter events, 26.9 us)
Async XLA Ops:
  0.0 30.0 %collective-permute-start.4 = (bf16[512,2048]{1,0:T(8,128)(2,1)}, bf16[512,2048]{1,0:T(8,128)(2,1)}, u32[]{:S(2)}, u32[]{:S(2)}) collective-permute-start(bf16[512,2048]{1,0:T(8,128)(2,1)} %own_w.1), channel_id=1, source_target_pairs={{0,1},{1,0},{2,3},{3,2},{4,5},{5,4},{6,7},{7,6},{8,9},{9,8},{10,11... | collective-permute-start | bytes 6291464 | tf_op jit(solution)/shard_map/ppermute | solution.py:338
  0.0 9.3 %collective-permute-start = (bf16[256,512]{1,0:T(8,128)(2,1)}, bf16[256,512]{1,0:T(8,128)(2,1)S(1)}, u32[]{:S(2)}, u32[]{:S(2)}) collective-permute-start(bf16[256,512]{1,0:T(8,128)(2,1)} %refs_1_.1), channel_id=1, source_target_pairs={{0,2},{2,0},{4,6},{6,4},{8,10},{10,8},{12,14},{14,12},{16,18},{18,... | collective-permute-start | bytes 786440 | tf_op jit(solution)/shard_map/ppermute | solution.py:20
  0.5 14.0 %collective-permute-start.2 = (bf16[256,512]{1,0:T(8,128)(2,1)}, bf16[256,512]{1,0:T(8,128)(2,1)S(1)}, u32[]{:S(2)}, u32[]{:S(2)}) collective-permute-start(bf16[256,512]{1,0:T(8,128)(2,1)} %refs_4_.1), channel_id=1, source_target_pairs={{0,2},{2,0},{4,6},{6,4},{8,10},{10,8},{12,14},{14,12},{16,18},{18,... | collective-permute-start | bytes 786440 | tf_op jit(solution)/shard_map/ppermute | solution.py:20
  9.3 20.7 %copy-start.5 = (bf16[256,512]{1,0:T(8,128)(2,1)}, bf16[256,512]{1,0:T(8,128)(2,1)S(1)}, u32[]{:S(2)}) copy-start(bf16[256,512]{1,0:T(8,128)(2,1)S(1)} %collective-permute-done.refs_0_) | copy-start | bytes 786436
  9.3 18.8 %collective-permute-start.1 = (bf16[256,512]{1,0:T(8,128)(2,1)S(1)}, bf16[256,512]{1,0:T(8,128)(2,1)S(1)}, u32[]{:S(2)}, u32[]{:S(2)}) collective-permute-start(bf16[256,512]{1,0:T(8,128)(2,1)S(1)} %collective-permute-done.refs_0_), channel_id=1, source_target_pairs={{0,4},{4,8},{8,12},{12,16},{16,20},{20,24},{24,28},{6,2},{10,6},{1... | collective-permute-start | bytes 786440 | tf_op jit(solution)/shard_map/ppermute | solution.py:330
  14.6 13.6 %collective-permute-start.3 = (bf16[256,512]{1,0:T(8,128)(2,1)S(1)}, bf16[256,512]{1,0:T(8,128)(2,1)S(1)}, u32[]{:S(2)}, u32[]{:S(2)}) collective-permute-start(bf16[256,512]{1,0:T(8,128)(2,1)S(1)} %collective-permute-done.2.refs_3_), channel_id=1, source_target_pairs={{0,4},{4,8},{8,12},{12,16},{16,20},{20,24},{24,28},{6,2},{10,6},{1... | collective-permute-start | bytes 786440 | tf_op jit(solution)/shard_map/ppermute | solution.py:330
  18.6 4.9 %collective-permute-start.7 = (f32[16,128]{1,0:T(8,128)S(1)}, f32[16,128]{1,0:T(8,128)S(1)}, u32[]{:S(2)}, u32[]{:S(2)}) collective-permute-start(f32[16,128]{1,0:T(8,128)S(1)} %select_reduce_fusion.refs_4_.refs_6_.refs_3_.refs_2_.refs_1_), channel_id=1, source_target_pairs={{0,8},{2,10},{4,12},{6,14},{8,0},{10,2},{12,4},{14,6},{16,24},{18,... | collective-permute-start | bytes 24584 | tf_op jit(solution)/shard_map/ppermute | solution.py:20
  18.7 11.4 %collective-permute-start.5 = (bf16[352,2048]{1,0:T(8,128)(2,1)}, bf16[352,2048]{1,0:T(8,128)(2,1)}, u32[]{:S(2)}, u32[]{:S(2)}) collective-permute-start(bf16[352,2048]{1,0:T(8,128)(2,1)} %bitcast.13), channel_id=1, source_target_pairs={{0,1},{1,0},{2,3},{3,2},{4,5},{5,4},{6,7},{7,6},{8,9},{9,8},{10,11... | collective-permute-start | bytes 4325384 | tf_op jit(solution)/shard_map/ppermute | solution.py:340
  23.5 4.6 %collective-permute-start.8 = (f32[16,256]{1,0:T(8,128)S(1)}, f32[16,256]{1,0:T(8,128)S(1)}, u32[]{:S(2)}, u32[]{:S(2)}) collective-permute-start(f32[16,256]{1,0:T(8,128)S(1)} %pad_maximum_fusion.2), channel_id=1, source_target_pairs={{0,16},{2,18},{4,20},{6,22},{8,24},{10,26},{12,28},{14,30},{16,0},... | collective-permute-start | bytes 49160 | tf_op jit(solution)/shard_map/ppermute | solution.py:20
  28.9 5.8 %collective-permute-start.9 = (bf16[352,2048]{1,0:T(8,128)(2,1)}, bf16[352,2048]{1,0:T(8,128)(2,1)}, u32[]{:S(2)}, u32[]{:S(2)}) collective-permute-start(bf16[352,2048]{1,0:T(8,128)(2,1)} %bitcast.15), channel_id=1, source_target_pairs={{0,1},{1,0},{2,3},{3,2},{4,5},{5,4},{6,7},{7,6},{8,9},{9,8},{10,11... | collective-permute-start | bytes 4325384 | tf_op jit(solution)/shard_map/ppermute | solution.py:342
  28.9 5.8 %collective-permute-start.10 = (bf16[352,2048]{1,0:T(8,128)(2,1)}, bf16[352,2048]{1,0:T(8,128)(2,1)}, u32[]{:S(2)}, u32[]{:S(2)}) collective-permute-start(bf16[352,2048]{1,0:T(8,128)(2,1)} %bitcast.17), channel_id=1, source_target_pairs={{0,1},{1,0},{2,3},{3,2},{4,5},{5,4},{6,7},{7,6},{8,9},{9,8},{10,11... | collective-permute-start | bytes 4325384 | tf_op jit(solution)/shard_map/ppermute | solution.py:343
  34.6 1.6 collective-permute-start.6
  41.9 15.0 %collective-permute-start.11 = (bf16[128,2048]{1,0:T(8,128)(2,1)}, bf16[128,2048]{1,0:T(8,128)(2,1)S(1)}, u32[]{:S(2)}, u32[]{:S(2)}) collective-permute-start(bf16[128,2048]{1,0:T(8,128)(2,1)} %get-tuple-element.69.refs_0_), channel_id=1, source_target_pairs={{0,8},{2,10},{4,12},{6,14},{8,0},{10,2},{12,4},{14,6},{16,24},{18,... | collective-permute-start | bytes 1572872 | tf_op jit(solution)/shard_map/ppermute | solution.py:20
  44.5 15.8 %collective-permute-start.12 = (bf16[128,2048]{1,0:T(8,128)(2,1)}, bf16[128,2048]{1,0:T(8,128)(2,1)S(1)}, u32[]{:S(2)}, u32[]{:S(2)}) collective-permute-start(bf16[128,2048]{1,0:T(8,128)(2,1)} %get-tuple-element.69.refs_0_), channel_id=1, source_target_pairs={{8,16},{10,18},{12,20},{14,22},{16,8},{18,10},{20,12},{22,14},{9,1... | collective-permute-start | bytes 1572872 | tf_op jit(solution)/shard_map/ppermute | solution.py:227
  47.7 24.9 %collective-permute-start.16 = (bf16[128,2048]{1,0:T(8,128)(2,1)}, bf16[128,2048]{1,0:T(8,128)(2,1)S(1)}, u32[]{:S(2)}, u32[]{:S(2)}) collective-permute-start(bf16[128,2048]{1,0:T(8,128)(2,1)} %get-tuple-element.69.refs_0_), channel_id=1, source_target_pairs={{0,4},{2,6},{4,0},{6,2},{8,12},{10,14},{12,8},{14,10},{16,20},{18,... | collective-permute-start | bytes 1572872 | tf_op jit(solution)/shard_map/ppermute | solution.py:20
  47.8 24.9 %collective-permute-start.15 = (bf16[128,2048]{1,0:T(8,128)(2,1)}, bf16[128,2048]{1,0:T(8,128)(2,1)S(1)}, u32[]{:S(2)}, u32[]{:S(2)}) collective-permute-start(bf16[128,2048]{1,0:T(8,128)(2,1)} %get-tuple-element.69.refs_0_), channel_id=1, source_target_pairs={{0,2},{2,0},{4,6},{6,4},{8,10},{10,8},{12,14},{14,12},{16,18},{18,... | collective-permute-start | bytes 1572872 | tf_op jit(solution)/shard_map/ppermute | solution.py:20
  60.3 16.6 %collective-permute-start.13 = (bf16[128,2048]{1,0:T(8,128)(2,1)S(1)}, bf16[128,2048]{1,0:T(8,128)(2,1)}, u32[]{:S(2)}, u32[]{:S(2)}) collective-permute-start(bf16[128,2048]{1,0:T(8,128)(2,1)S(1)} %collective-permute-done.11.refs_0_), channel_id=1, source_target_pairs={{8,16},{10,18},{12,20},{14,22},{16,8},{18,10},{20,12},{22,14},{9,1... | collective-permute-start | bytes 1572872 | tf_op jit(solution)/shard_map/ppermute | solution.py:227
  63.8 13.1 %collective-permute-start.14 = (bf16[128,2048]{1,0:T(8,128)(2,1)S(1)}, bf16[128,2048]{1,0:T(8,128)(2,1)}, u32[]{:S(2)}, u32[]{:S(2)}) collective-permute-start(bf16[128,2048]{1,0:T(8,128)(2,1)S(1)} %collective-permute-done.12), channel_id=1, source_target_pairs={{8,0},{10,2},{12,4},{14,6},{16,24},{18,26},{20,28},{22,30},{9,1},{... | collective-permute-start | bytes 1572872 | tf_op jit(solution)/shard_map/ppermute | solution.py:227
  65.9 9.0 %collective-permute-start.18 = (f32[16,512]{1,0:T(8,128)S(1)}, f32[16,512]{1,0:T(8,128)S(1)}, u32[]{:S(2)}, u32[]{:S(2)}) collective-permute-start(f32[16,512]{1,0:T(8,128)S(1)} %pad_maximum_fusion.1), channel_id=1, source_target_pairs={{0,4},{2,6},{4,0},{6,2},{8,12},{10,14},{12,8},{14,10},{16,20},{18,... | collective-permute-start | bytes 98312 | tf_op jit(solution)/shard_map/ppermute | solution.py:20
  72.7 13.7 %collective-permute-start.17 = (bf16[128,2048]{1,0:T(8,128)(2,1)S(1)}, bf16[128,2048]{1,0:T(8,128)(2,1)S(1)}, u32[]{:S(2)}, u32[]{:S(2)}) collective-permute-start(bf16[128,2048]{1,0:T(8,128)(2,1)S(1)} %collective-permute-done.16.refs_2_), channel_id=1, source_target_pairs={{0,2},{2,0},{4,6},{6,4},{8,10},{10,8},{12,14},{14,12},{16,18},{18,... | collective-permute-start | bytes 1572872 | tf_op jit(solution)/shard_map/ppermute | solution.py:20
  74.9 13.5 %collective-permute-start.20 = (bf16[128,2048]{1,0:T(8,128)(2,1)S(1)}, bf16[128,2048]{1,0:T(8,128)(2,1)S(1)}, u32[]{:S(2)}, u32[]{:S(2)}) collective-permute-start(bf16[128,2048]{1,0:T(8,128)(2,1)S(1)} %collective-permute-done.11.refs_0_), channel_id=1, source_target_pairs={{0,4},{2,6},{4,0},{6,2},{8,12},{10,14},{12,8},{14,10},{16,20},{18,... | collective-permute-start | bytes 1572872 | tf_op jit(solution)/shard_map/ppermute | solution.py:20
  74.9 13.5 %collective-permute-start.19 = (f32[16,1024]{1,0:T(8,128)S(1)}, f32[16,1024]{1,0:T(8,128)S(1)}, u32[]{:S(2)}, u32[]{:S(2)}) collective-permute-start(f32[16,1024]{1,0:T(8,128)S(1)} %pad_maximum_fusion), channel_id=1, source_target_pairs={{0,2},{2,0},{4,6},{6,4},{8,10},{10,8},{12,14},{14,12},{16,18},{18,... | collective-permute-start | bytes 196616 | tf_op jit(solution)/shard_map/ppermute | solution.py:20
  76.9 16.6 %collective-permute-start.23 = (bf16[128,2048]{1,0:T(8,128)(2,1)}, bf16[128,2048]{1,0:T(8,128)(2,1)S(1)}, u32[]{:S(2)}, u32[]{:S(2)}) collective-permute-start(bf16[128,2048]{1,0:T(8,128)(2,1)} %collective-permute-done.13), channel_id=1, source_target_pairs={{8,0},{10,2},{12,4},{14,6},{16,24},{18,26},{20,28},{22,30},{9,1},{... | collective-permute-start | bytes 1572872 | tf_op jit(solution)/shard_map/ppermute | solution.py:227
  86.3 12.1 %collective-permute-start.21 = (bf16[128,2048]{1,0:T(8,128)(2,1)S(1)}, bf16[128,2048]{1,0:T(8,128)(2,1)S(1)}, u32[]{:S(2)}, u32[]{:S(2)}) collective-permute-start(bf16[128,2048]{1,0:T(8,128)(2,1)S(1)} %broadcast_select_fusion.1.refs_2_), channel_id=1, source_target_pairs={{0,2},{2,0},{4,6},{6,4},{8,10},{10,8},{12,14},{14,12},{16,18},{18,... | collective-permute-start | bytes 1572872 | tf_op jit(solution)/shard_map/ppermute | solution.py:20
  88.4 12.1 %collective-permute-start.22 = (bf16[128,2048]{1,0:T(8,128)(2,1)S(1)}, bf16[128,2048]{1,0:T(8,128)(2,1)S(1)}, u32[]{:S(2)}, u32[]{:S(2)}) collective-permute-start(bf16[128,2048]{1,0:T(8,128)(2,1)S(1)} %broadcast_select_fusion.1.refs_2_), channel_id=1, source_target_pairs={{0,4},{2,6},{4,0},{6,2},{8,12},{10,14},{12,8},{14,10},{16,20},{18,... | collective-permute-start | bytes 1572872 | tf_op jit(solution)/shard_map/ppermute | solution.py:20
  98.4 12.1 %collective-permute-start.24 = (bf16[128,2048]{1,0:T(8,128)(2,1)S(1)}, bf16[128,2048]{1,0:T(8,128)(2,1)S(1)}, u32[]{:S(2)}, u32[]{:S(2)}) collective-permute-start(bf16[128,2048]{1,0:T(8,128)(2,1)S(1)} %broadcast_select_fusion.refs_5_), channel_id=1, source_target_pairs={{0,2},{2,0},{4,6},{6,4},{8,10},{10,8},{12,14},{14,12},{16,18},{18,... | collective-permute-start | bytes 1572872 | tf_op jit(solution)/shard_map/ppermute | solution.py:20
  100.5 12.1 %collective-permute-start.26 = (bf16[128,2048]{1,0:T(8,128)(2,1)S(1)}, bf16[128,2048]{1,0:T(8,128)(2,1)S(1)}, u32[]{:S(2)}, u32[]{:S(2)}) collective-permute-start(bf16[128,2048]{1,0:T(8,128)(2,1)S(1)} %broadcast_select_fusion.refs_5_), channel_id=1, source_target_pairs={{0,4},{2,6},{4,0},{6,2},{8,12},{10,14},{12,8},{14,10},{16,20},{18,... | collective-permute-start | bytes 1572872 | tf_op jit(solution)/shard_map/ppermute | solution.py:20
  100.5 12.1 %collective-permute-start.27 = (bf16[128,2048]{1,0:T(8,128)(2,1)S(1)}, bf16[128,2048]{1,0:T(8,128)(2,1)S(1)}, u32[]{:S(2)}, u32[]{:S(2)}) collective-permute-start(bf16[128,2048]{1,0:T(8,128)(2,1)S(1)} %collective-permute-done.15.refs_1_), channel_id=1, source_target_pairs={{0,8},{2,10},{4,12},{6,14},{8,0},{10,2},{12,4},{14,6},{16,24},{18,... | collective-permute-start | bytes 1572872 | tf_op jit(solution)/shard_map/ppermute | solution.py:20
  110.5 10.2 %collective-permute-start.25 = (bf16[128,2048]{1,0:T(8,128)(2,1)S(1)}, bf16[128,2048]{1,0:T(8,128)(2,1)S(1)}, u32[]{:S(2)}, u32[]{:S(2)}) collective-permute-start(bf16[128,2048]{1,0:T(8,128)(2,1)S(1)} %collective-permute-done.22.refs_4_), channel_id=1, source_target_pairs={{0,2},{2,0},{4,6},{6,4},{8,10},{10,8},{12,14},{14,12},{16,18},{18,... | collective-permute-start | bytes 1572872 | tf_op jit(solution)/shard_map/ppermute | solution.py:20
  112.5 9.4 %collective-permute-start.28 = (bf16[128,2048]{1,0:T(8,128)(2,1)S(1)}, bf16[128,2048]{1,0:T(8,128)(2,1)S(1)}, u32[]{:S(2)}, u32[]{:S(2)}) collective-permute-start(bf16[128,2048]{1,0:T(8,128)(2,1)S(1)} %collective-permute-done.24.refs_0_), channel_id=1, source_target_pairs={{0,4},{2,6},{4,0},{6,2},{8,12},{10,14},{12,8},{14,10},{16,20},{18,... | collective-permute-start | bytes 1572872 | tf_op jit(solution)/shard_map/ppermute | solution.py:20
  112.6 14.0 %collective-permute-start.36 = (bf16[128,2048]{1,0:T(8,128)(2,1)S(1)}, bf16[128,2048]{1,0:T(8,128)(2,1)S(1)}, u32[]{:S(2)}, u32[]{:S(2)}) collective-permute-start(bf16[128,2048]{1,0:T(8,128)(2,1)S(1)} %collective-permute-done.17.refs_3_), channel_id=1, source_target_pairs={{0,8},{2,10},{4,12},{6,14},{8,0},{10,2},{12,4},{14,6},{16,24},{18,... | collective-permute-start | bytes 1572872 | tf_op jit(solution)/shard_map/ppermute | solution.py:20
  124.6 11.5 %collective-permute-start.30 = (bf16[128,2048]{1,0:T(8,128)(2,1)S(1)}, bf16[128,2048]{1,0:T(8,128)(2,1)S(1)}, u32[]{:S(2)}, u32[]{:S(2)}) collective-permute-start(bf16[128,2048]{1,0:T(8,128)(2,1)S(1)} %get-tuple-element.94), channel_id=1, source_target_pairs={{0,4},{2,6},{4,0},{6,2},{8,12},{10,14},{12,8},{14,10},{16,20},{18,... | collective-permute-start | bytes 1572872 | tf_op jit(solution)/shard_map/ppermute | solution.py:20
  125.2 12.4 %collective-permute-start.29 = (bf16[128,2048]{1,0:T(8,128)(2,1)S(1)}, bf16[128,2048]{1,0:T(8,128)(2,1)S(1)}, u32[]{:S(2)}, u32[]{:S(2)}) collective-permute-start(bf16[128,2048]{1,0:T(8,128)(2,1)S(1)} %get-tuple-element.92), channel_id=1, source_target_pairs={{0,2},{2,0},{4,6},{6,4},{8,10},{10,8},{12,14},{14,12},{16,18},{18,... | collective-permute-start | bytes 1572872 | tf_op jit(solution)/shard_map/ppermute | solution.py:20
  129.0 13.5 %collective-permute-start.37 = (bf16[128,2048]{1,0:T(8,128)(2,1)S(1)}, bf16[128,2048]{1,0:T(8,128)(2,1)S(1)}, u32[]{:S(2)}, u32[]{:S(2)}) collective-permute-start(bf16[128,2048]{1,0:T(8,128)(2,1)S(1)} %expert_rows.9), channel_id=1, source_target_pairs={{0,8},{2,10},{4,12},{6,14},{8,0},{10,2},{12,4},{14,6},{16,24},{18,... | collective-permute-start | bytes 1572872 | tf_op jit(solution)/shard_map/ppermute | solution.py:20
  137.6 13.6 %collective-permute-start.34 = (bf16[128,2048]{1,0:T(8,128)(2,1)S(1)}, bf16[128,2048]{1,0:T(8,128)(2,1)S(1)}, u32[]{:S(2)}, u32[]{:S(2)}) collective-permute-start(bf16[128,2048]{1,0:T(8,128)(2,1)S(1)} %add_convert_fusion.8), channel_id=1, source_target_pairs={{0,2},{2,0},{4,6},{6,4},{8,10},{10,8},{12,14},{14,12},{16,18},{18,... | collective-permute-start | bytes 1572872 | tf_op jit(solution)/shard_map/ppermute | solution.py:20
  139.7 14.3 %collective-permute-start.31 = (bf16[128,2048]{1,0:T(8,128)(2,1)S(1)}, bf16[128,2048]{1,0:T(8,128)(2,1)S(1)}, u32[]{:S(2)}, u32[]{:S(2)}) collective-permute-start(bf16[128,2048]{1,0:T(8,128)(2,1)S(1)} %get-tuple-element.95), channel_id=1, source_target_pairs={{0,4},{2,6},{4,0},{6,2},{8,12},{10,14},{12,8},{14,10},{16,20},{18,... | collective-permute-start | bytes 1572872 | tf_op jit(solution)/shard_map/ppermute | solution.py:20
  142.4 12.3 %collective-permute-start.38 = (bf16[128,2048]{1,0:T(8,128)(2,1)S(1)}, bf16[128,2048]{1,0:T(8,128)(2,1)S(1)}, u32[]{:S(2)}, u32[]{:S(2)}) collective-permute-start(bf16[128,2048]{1,0:T(8,128)(2,1)S(1)} %get-tuple-element.106), channel_id=1, source_target_pairs={{0,8},{2,10},{4,12},{6,14},{8,0},{10,2},{12,4},{14,6},{16,24},{18,... | collective-permute-start | bytes 1572872 | tf_op jit(solution)/shard_map/ppermute | solution.py:20
  151.2 15.2 %collective-permute-start.35 = (bf16[128,2048]{1,0:T(8,128)(2,1)S(1)}, bf16[128,2048]{1,0:T(8,128)(2,1)S(1)}, u32[]{:S(2)}, u32[]{:S(2)}) collective-permute-start(bf16[128,2048]{1,0:T(8,128)(2,1)S(1)} %get-tuple-element.101), channel_id=1, source_target_pairs={{0,2},{2,0},{4,6},{6,4},{8,10},{10,8},{12,14},{14,12},{16,18},{18,... | collective-permute-start | bytes 1572872 | tf_op jit(solution)/shard_map/ppermute | solution.py:20
  154.0 14.4 %collective-permute-start.32 = (bf16[128,2048]{1,0:T(8,128)(2,1)S(1)}, bf16[128,2048]{1,0:T(8,128)(2,1)S(1)}, u32[]{:S(2)}, u32[]{:S(2)}) collective-permute-start(bf16[128,2048]{1,0:T(8,128)(2,1)S(1)} %add_convert_fusion.9), channel_id=1, source_target_pairs={{0,4},{2,6},{4,0},{6,2},{8,12},{10,14},{12,8},{14,10},{16,20},{18,... | collective-permute-start | bytes 1572872 | tf_op jit(solution)/shard_map/ppermute | solution.py:20
  154.8 14.6 %collective-permute-start.39 = (bf16[128,2048]{1,0:T(8,128)(2,1)S(1)}, bf16[128,2048]{1,0:T(8,128)(2,1)S(1)}, u32[]{:S(2)}, u32[]{:S(2)}) collective-permute-start(bf16[128,2048]{1,0:T(8,128)(2,1)S(1)} %add_convert_fusion.7), channel_id=1, source_target_pairs={{0,8},{2,10},{4,12},{6,14},{24,16},{26,18},{28,20},{30,22},{1,9},{... | collective-permute-start | bytes 1572872 | tf_op jit(solution)/shard_map/ppermute | solution.py:227
  166.4 13.8 %collective-permute-start.44 = (bf16[128,2048]{1,0:T(8,128)(2,1)S(1)}, bf16[128,2048]{1,0:T(8,128)(2,1)S(1)}, u32[]{:S(2)}, u32[]{:S(2)}) collective-permute-start(bf16[128,2048]{1,0:T(8,128)(2,1)S(1)} %add_convert_fusion.2), channel_id=1, source_target_pairs={{0,2},{2,0},{4,6},{6,4},{8,10},{10,8},{12,14},{14,12},{16,18},{18,... | collective-permute-start | bytes 1572872 | tf_op jit(solution)/shard_map/ppermute | solution.py:20
  168.4 13.7 %collective-permute-start.33 = (bf16[128,2048]{1,0:T(8,128)(2,1)S(1)}, bf16[128,2048]{1,0:T(8,128)(2,1)S(1)}, u32[]{:S(2)}, u32[]{:S(2)}) collective-permute-start(bf16[128,2048]{1,0:T(8,128)(2,1)S(1)} %get-tuple-element.97), channel_id=1, source_target_pairs={{0,4},{2,6},{4,0},{6,2},{8,12},{10,14},{12,8},{14,10},{16,20},{18,... | collective-permute-start | bytes 1572872 | tf_op jit(solution)/shard_map/ppermute | solution.py:20
  169.8 15.1 %collective-permute-start.41 = (bf16[128,2048]{1,0:T(8,128)(2,1)S(1)}, bf16[128,2048]{1,0:T(8,128)(2,1)S(1)}, u32[]{:S(2)}, u32[]{:S(2)}) collective-permute-start(bf16[128,2048]{1,0:T(8,128)(2,1)S(1)} %add_convert_fusion.6), channel_id=1, source_target_pairs={{0,8},{2,10},{4,12},{6,14},{24,16},{26,18},{28,20},{30,22},{1,9},{... | collective-permute-start | bytes 1572872 | tf_op jit(solution)/shard_map/ppermute | solution.py:227
  171.2 16.4 %collective-permute-start.40 = (bf16[128,2048]{1,0:T(8,128)(2,1)S(1)}, bf16[128,2048]{1,0:T(8,128)(2,1)S(1)}, u32[]{:S(2)}, u32[]{:S(2)}) collective-permute-start(bf16[128,2048]{1,0:T(8,128)(2,1)S(1)} %add_convert_fusion.6), channel_id=1, source_target_pairs={{8,16},{10,18},{12,20},{14,22},{16,8},{18,10},{20,12},{22,14},{9,1... | collective-permute-start | bytes 1572872 | tf_op jit(solution)/shard_map/ppermute | solution.py:227
  182.1 9.2 %collective-permute-start.46 = (bf16[128,2048]{1,0:T(8,128)(2,1)S(1)}, bf16[128,2048]{1,0:T(8,128)(2,1)S(1)}, u32[]{:S(2)}, u32[]{:S(2)}) collective-permute-start(bf16[128,2048]{1,0:T(8,128)(2,1)S(1)} %add_convert_fusion.1), channel_id=1, source_target_pairs={{0,4},{2,6},{4,0},{6,2},{8,12},{10,14},{12,8},{14,10},{16,20},{18,... | collective-permute-start | bytes 1572872 | tf_op jit(solution)/shard_map/ppermute | solution.py:20
  183.1 9.2 %collective-permute-start.45 = (bf16[128,2048]{1,0:T(8,128)(2,1)S(1)}, bf16[128,2048]{1,0:T(8,128)(2,1)S(1)}, u32[]{:S(2)}, u32[]{:S(2)}) collective-permute-start(bf16[128,2048]{1,0:T(8,128)(2,1)S(1)} %add_convert_fusion.3), channel_id=1, source_target_pairs={{0,2},{2,0},{4,6},{6,4},{8,10},{10,8},{12,14},{14,12},{16,18},{18,... | collective-permute-start | bytes 1572872 | tf_op jit(solution)/shard_map/ppermute | solution.py:20
  187.6 11.1 %collective-permute-start.43 = (bf16[128,2048]{1,0:T(8,128)(2,1)S(1)}, bf16[128,2048]{1,0:T(8,128)(2,1)S(1)}, u32[]{:S(2)}, u32[]{:S(2)}) collective-permute-start(bf16[128,2048]{1,0:T(8,128)(2,1)S(1)} %add_convert_fusion.4), channel_id=1, source_target_pairs={{8,16},{10,18},{12,20},{14,22},{16,8},{18,10},{20,12},{22,14},{9,1... | collective-permute-start | bytes 1572872 | tf_op jit(solution)/shard_map/ppermute | solution.py:227
  190.1 9.2 %collective-permute-start.42 = (bf16[128,2048]{1,0:T(8,128)(2,1)S(1)}, bf16[128,2048]{1,0:T(8,128)(2,1)S(1)}, u32[]{:S(2)}, u32[]{:S(2)}) collective-permute-start(bf16[128,2048]{1,0:T(8,128)(2,1)S(1)} %add_convert_fusion.5), channel_id=1, source_target_pairs={{0,8},{2,10},{4,12},{6,14},{8,0},{10,2},{12,4},{14,6},{16,24},{18,... | collective-permute-start | bytes 1572872 | tf_op jit(solution)/shard_map/ppermute | solution.py:20
  (9 other events, 53.0 us)

commit v10 on v9

--- a/solution.py
+++ b/solution.py
@@ -18,6 +18,12 @@
 def flip(block, mask):
     count = lax.axis_size("seq")
     return lax.ppermute(block, "seq", [(i, i ^ mask) for i in range(count)])
+
+
+def cross(block, masks):
+    count = lax.axis_size("seq")
+    pairs = [(2 * i + c, 2 * (i ^ masks[c]) + c) for i in range(count) for c in range(2)]
+    return lax.ppermute(block, ("seq", "exp"), pairs)
 
 
 def after(block, *arrays):
@@ -99,32 +105,14 @@
     )(where, queries, ids, *near_keys, *near_values, *ahead)
 
 
-PIECES = 4
-
-
 def norm_kernel(mine_ref, theirs_ref, own_w, other_w, resid_ref, gain_ref, *refs):
-    stream_ref, normed_ref, weights, sems = refs[-4:]
-    depth, piece = own_w.shape[0], own_w.shape[1] // PIECES
-    copies = []
-    for i in range(PIECES):
-        cols = pl.ds(i * piece, piece)
-        for half, ref in enumerate((own_w, other_w)):
-            target = weights.at[pl.ds(half * depth, depth), cols]
-            copies.append(pltpu.make_async_copy(ref.at[:, cols], target, sems.at[2 * i + half]))
-    for copy in copies:
-        copy.start()
-    both = jnp.concatenate([mine_ref[...], theirs_ref[...]], axis=1)
-    total = 0.0
-    for i in range(PIECES):
-        copies[2 * i].wait()
-        copies[2 * i + 1].wait()
-        cols = slice(i * piece, (i + 1) * piece)
-        part = resid_ref[:, cols].astype(jnp.float32)
-        part += jnp.dot(both, weights[:, cols], preferred_element_type=jnp.float32)
-        stream_ref[:, cols] = part
-        total += jnp.sum(part * part, axis=-1, keepdims=True)
-    scale = lax.rsqrt(total / own_w.shape[1] + 1e-05)
-    normed_ref[...] = (stream_ref[...] * scale * gain_ref[...]).astype(jnp.bfloat16)
+    stream_ref, normed_ref = refs[-2:]
+    stream = resid_ref[...].astype(jnp.float32)
+    stream += jnp.dot(mine_ref[...], own_w[...], preferred_element_type=jnp.float32)
+    stream += jnp.dot(theirs_ref[...], other_w[...], preferred_element_type=jnp.float32)
+    meansq = jnp.mean(stream * stream, axis=-1, keepdims=True)
+    stream_ref[...] = stream
+    normed_ref[...] = (stream * lax.rsqrt(meansq + 1e-05) * gain_ref[...]).astype(jnp.bfloat16)
 
 
 def project_and_norm(mine, theirs, own_w, other_w, resid, gain, *ahead):
@@ -135,12 +123,8 @@
             jax.ShapeDtypeStruct((rows, width), jnp.float32),
             jax.ShapeDtypeStruct((rows, width), jnp.bfloat16),
         ),
-        in_specs=[VMEM] * 2 + [ANY] * 2 + [VMEM] * 2 + [ANY] * len(ahead),
+        in_specs=[VMEM] * 6 + [ANY] * len(ahead),
         out_specs=(VMEM, VMEM),
-        scratch_shapes=[
-            pltpu.VMEM((2 * own_w.shape[0], width), jnp.bfloat16),
-            pltpu.SemaphoreType.DMA((2 * PIECES,)),
-        ],
         compiler_params=pltpu.CompilerParams(vmem_limit_bytes=63 * 1024 * 1024),
         name="project_and_norm",
     )(mine, theirs, own_w, other_w, resid, gain, *ahead)
@@ -175,7 +159,13 @@
     )(*halves)
 
 
-def expert_kernel(places, pieces, shard_ref, *refs):
+def gates_at(place, rows, pieces):
+    piece = place.bit_length()
+    at = (place - (1 << piece >> 1)) * rows
+    return pieces[piece][:, at : at + rows]
+
+
+def expert_kernel(places, pieces, where_ref, *refs):
     count = len(places)
     blocks, gates, (gate_up, down) = refs[:count], refs[count : count + pieces], refs[count + pieces :][:2]
     outs = refs[count + pieces + 2 :]
@@ -189,17 +179,16 @@
         act = (gate / (1.0 + jnp.exp(-gate)) * up).astype(jnp.bfloat16)
         result = jnp.dot(act, down[...], preferred_element_type=jnp.float32)
         for i in group:
-            piece = places[i].bit_length()
-            at = (places[i] - (1 << piece >> 1)) * rows
-            here = gates[piece][:, at : at + rows]
+            here, other = (gates_at(place, rows, gates) for place in places[i])
+            here = jnp.where(where_ref[1] == 1, other, here)
             expert = lax.broadcasted_iota(jnp.int32, here.shape, 0)
-            chosen = jnp.sum(jnp.where(expert == shard_ref[0], here, 0.0), axis=0, keepdims=True)
+            chosen = jnp.sum(jnp.where(expert == where_ref[0], here, 0.0), axis=0, keepdims=True)
             chosen = jnp.transpose(jnp.broadcast_to(chosen, (rows, rows)))[:, :1]
             part = result[(i - first) * rows : (i - first + 1) * rows]
             outs[i][...] = (part * chosen).astype(jnp.bfloat16)
 
 
-def expert(blocks, places, shard, gates, weights):
+def expert(blocks, places, where, gates, weights):
     rows, width = blocks[0].shape
     count = len(blocks)
     return pl.pallas_call(
@@ -209,7 +198,7 @@
         out_specs=[VMEM] * count,
         compiler_params=pltpu.CompilerParams(vmem_limit_bytes=36 * 1024 * 1024),
         name="expert_rows",
-    )(shard, *blocks, *gates, *weights)
+    )(where, *blocks, *gates, *weights)
 
 
 def add(*terms):
@@ -228,75 +217,84 @@
 
 
 OUTWARD, INWARD, MIDDLE = [(1, 0), (2, 3)], [(0, 1), (3, 2)], [(1, 2), (2, 1)]
-
-
-def step_layer(normed, stream, run, gates, weights):
+X, Y = (1, 2), (2, 1)
+
+
+def step_layer(normed, stream, run, weights):
     z = lax.axis_index("seq") // 4
     inner = (z == 1) | (z == 2)
 
     o0 = normed
-    o1, near3, x0, y0 = flip(o0, 4), shift(o0, MIDDLE), flip(o0, 1), flip(o0, 2)
-    gates = gather_gates(gates, o0)
+    o1, near3, x0, y0 = flip(o0, 4), shift(o0, MIDDLE), cross(o0, X), cross(o0, Y)
+    weights = weights(x0, y0)
 
     ends2, near2 = shift(after(near3, o1), OUTWARD), shift(after(o1, near3), MIDDLE)
-    d0, y1 = flip(after(y0, x0), 1), flip(after(o1, y0), 2)
-    gates = gather_gates(gates, o1, y0)
-    run = functools.partial(run, gates)
+    d0, y1 = cross(after(y0, x0), X), cross(after(o1, y0), Y)
 
     ends3 = shift(after(near2, ends2), OUTWARD)
     o2 = jnp.where(inner, near2, ends2)
-    x2, y2 = flip(after(o2, d0, weights[0]), 1), flip(after(o2, y1, weights[0]), 2)
-    p0, px0, py0, pd0 = run([after(o0, o2), x0, y0, d0], (0, 1, 2, 3))
+    x2, y2 = cross(after(o2, d0, weights[0]), X), cross(after(o2, y1, weights[0]), Y)
+    run = functools.partial(run, weights)
+    p0, px0, py0, pd0 = run([after(o0, o2), x0, y0, d0], (0, X, Y, 3))
 
     x1 = flip(after(x0, ends3, p0), 4)
     o3 = jnp.where(inner, near3, ends3)
-    x3, y3 = flip(after(o3, x2, p0), 1), flip(after(o3, y2, p0), 2)
-    p1, py1, p2, px2, py2, p3 = run([after(o1, p0), y1, o2, x2, y2, o3], (4, 6, 8, 9, 10, 12))
+    x3, y3 = cross(after(o3, x2, p0), X), cross(after(o3, y2, p0), Y)
+    p1, py1, p2, px2, py2, p3 = run(
+        [after(o1, p0), y1, o2, x2, y2, o3], (4, plane(Y, 4), 8, plane(X, 8), plane(Y, 8), 12)
+    )
 
     d1 = flip(after(d0, x1, p1), 4)
-    d2, d3 = flip(after(y2, x3, p1), 1), flip(after(x3, y3, p1), 2)
-    px3, py3, px1 = run([after(x3, p1), y3, x1], (13, 14, 5))
+    d2, d3 = cross(after(y2, x3, p1), X), cross(after(x3, y3, p1), Y)
+    px3, py3, px1 = run([after(x3, p1), y3, x1], (plane(X, 12), plane(Y, 12), plane(X, 4)))
 
     pd2, pd3 = run([after(d2, px3), d3], (11, 15))
     (pd1,) = run([after(d1, pd2)], (7,))
-    to_x3, to_y2, to_d0 = flip(pd3, 2), flip(pd2, 1), flip(pd1, 4)
+    to_x3, to_y2, to_d0 = cross(pd3, Y), cross(pd2, X), flip(pd1, 4)
 
     px3, py2, pd0 = add_small(px3, to_x3), add_small(py2, to_y2), add_small(pd0, to_d0)
-    by_x, by_y = flip(after(px3, to_y2), 1), flip(after(py3, to_x3), 2)
+    by_x, by_y = cross(after(px3, to_y2), X), cross(after(py3, to_x3), Y)
     to_x0 = flip(after(px1, to_d0), 4)
 
     p3, px0 = add_small(p3, by_x, by_y), add_small(px0, to_x0)
     to_2 = shift(after(p3, to_x0), INWARD)
-    by_x, by_y = flip(after(px2, by_x), 1), flip(after(py2, by_y), 2)
+    by_x, by_y = cross(after(px2, by_x), X), cross(after(py2, by_y), Y)
 
     p2 = add_small(p2, by_x, by_y, to_2)
     to_3, to_1 = shift(after(p2, to_2), INWARD), shift(p2, MIDDLE)
-    to_y0, by_y = flip(after(pd0, by_x), 1), flip(after(py1, by_y), 2)
+    to_y0, by_y = cross(after(pd0, by_x), X), cross(after(py1, by_y), Y)
 
     p3, p1, py0 = add_small(p3, to_3), add_small(p1, by_y, to_1), add_small(py0, to_y0)
     by_z, by_middle = flip(after(p1, to_3), 4), shift(after(p3, to_1), MIDDLE)
-    by_x, by_y = flip(after(px0, to_y0), 1), flip(after(py0, by_y), 2)
+    by_x, by_y = cross(after(px0, to_y0), X), cross(after(py0, by_y), Y)
     return add(stream, p0, by_z, by_middle, by_x, by_y)
 
 
-def expert_layer(normed, stream, shard, gates, weights):
+def plane(masks, distance):
+    return tuple(mask + distance for mask in masks)
+
+
+def expert_layer(normed, stream, where, gates, halves):
     count = lax.axis_size("seq")
 
-    def run(gates, blocks, masks):
-        places = tuple(place_of(mask) for mask in masks)
-        return expert(blocks, places, shard, gates, weights)
+    def weights(*waits):
+        return assemble([after(half, *waits) for half in halves])
+
+    def run(weights, blocks, masks):
+        masks = [mask if isinstance(mask, tuple) else (mask, mask) for mask in masks]
+        places = tuple(tuple(place_of(j) for j in mask) for mask in masks)
+        return expert(blocks, places, where, gates, weights)
 
     if count == 16:
-        return step_layer(normed, stream, run, gates, weights)
-    while len(gates) < count.bit_length():
-        gates = gather_gates(gates)
+        return step_layer(normed, stream, run, weights)
+    held = weights()
     blocks, mask = [normed], 1
     while mask < count:
         blocks = blocks + [flip(block, mask) for block in blocks]
         mask *= 2
     parts = []
     for first in range(0, count, 4):
-        parts += run(gates, blocks[first : first + 4], range(first, first + 4))
+        parts += run(held, blocks[first : first + 4], range(first, first + 4))
     while mask > 1:
         mask //= 2
         parts = [add_small(parts[i], flip(parts[i + mask], mask)) for i in range(mask)]
@@ -332,7 +330,8 @@
     near_keys, near_values = halo(keys), halo(values)
     chosen = experts.T[:, None, :] == jnp.arange(count, dtype=jnp.int32)[None, :, None]
     some_gates = [jnp.sum(jnp.where(chosen, gates.T[:, None, :], 0.0), axis=0)]
-    some_gates = gather_gates(gather_gates(some_gates))
+    while len(some_gates) < count.bit_length() - 1:
+        some_gates = gather_gates(some_gates)
     id_pad = jnp.pad(pair_ids, (tok_rows, tok_rows), constant_values=-1)
     ids = lax.dynamic_slice_in_dim(id_pad, shard * tok_rows, 3 * tok_rows, 0)[None, :]
     out_other = lax.ppermute(out_weight, "exp", SWAP)
@@ -345,11 +344,12 @@
 
     where = jnp.stack([core, shard % 2])
     theirs, mine = attention(where, queries, ids, near_keys, near_values, out_other, gate_other)
+    all_gates = gather_gates(some_gates, theirs)
     received = lax.ppermute(theirs, "exp", SWAP)
     stream, normed = project_and_norm(
         mine, received, out_weight, out_other, resid, norm_gain[None, :], up_other, down_other
     )
-    mixed = expert_layer(normed, stream, shard.reshape(1), some_gates, assemble(halves))
+    mixed = expert_layer(normed, stream, jnp.stack([shard, core]), all_gates, halves)
     return mixed.astype(jnp.bfloat16)
 
 

time: 204 us -> 191 us (0.936)
  the two profiles are of different devices: /device:TPU:10 before, /device:TPU:0 now
where the time goes in v10:
time: 191 us
  starting transfers between devices  76.8 us (40%)
  waiting for transfers between devices  64.2 us (34%)
  Pallas kernels  37 us (19%)
  local copies, waits for them, and re-layouts  6.85 us (4%)
  other arithmetic  5.48 us (3%)
    ppermute x12, starting transfers between devices, flip(): return lax.ppermute(block, 'seq', [(i, i ^ mask) for i in range(count)])  28.6 us
    ppermute x20, waiting for transfers between devices, cross(): return lax.ppermute(block, ('seq', 'exp'), pairs)  26.5 us
    ppermute x12, waiting for transfers between devices, flip(): return lax.ppermute(block, 'seq', [(i, i ^ mask) for i in range(count)])  25.9 us
    ppermute x20, starting transfers between devices, cross(): return lax.ppermute(block, ('seq', 'exp'), pairs)  25.7 us
    pallas_call x5, Pallas kernels, expert(): pl.pallas_call(functools.partial(expert_kernel, places, len(gates)), out_...  25.5 us
    ppermute x8, starting transfers between devices, shift(): lax.ppermute(block, 'seq', [(4 * a + i, 4 * b + i) for a, b in pairs for...  14 us
    ppermute x8, waiting for transfers between devices, shift(): lax.ppermute(block, 'seq', [(4 * a + i, 4 * b + i) for a, b in pairs for...  10.2 us
    ppermute x2, starting transfers between devices, halo(): return (beside, part, lax.ppermute(beside, 'seq', ahead + back))  7.56 us
  transfers between devices with their start and end apart: 47, of which 19 were waited for; matrix products, arithmetic and copies ran while one was open for 3% of the time, Pallas kernels for 17%

profile of v10, /device:TPU:0, one launch (start us, length us, event | category | flops | bytes accessed | tf_op | source)
XLA Modules:
  0.0 190.7 jit_solution(11958098746279661899)
XLA Ops:
  0.5 2.5 %collective-permute-start = (bf16[256,512]{1,0:T(8,128)(2,1)}, bf16[256,512]{1,0:T(8,128)(2,1)S(1)}, u32[]{:S(2)}, u32[]{:S(2)}) collective-permute-start(bf16[256,512]{1,0:T(8,128)(2,1)} %refs_1_.1), channel_id=1, source_target_pairs={{0,2},{2,0},{4,6},{6,4},{8,10},{10,8},{12,14},{14,12},{16,18},{18,... | collective-permute-start | bytes 786440 | tf_op jit(solution)/shard_map/ppermute | solution.py:20
  3.7 2.1 %collective-permute-start.7 = (f32[16,128]{1,0:T(8,128)S(1)}, f32[16,128]{1,0:T(8,128)S(1)}, u32[]{:S(2)}, u32[]{:S(2)}) collective-permute-start(f32[16,128]{1,0:T(8,128)S(1)} %select_reduce_fusion.refs_4_.refs_6_.refs_3_.refs_2_.refs_1_), channel_id=1, source_target_pairs={{0,8},{2,10},{4,12},{6,14},{8,0},{10,2},{12,4},{14,6},{16,24},{18,... | collective-permute-start | bytes 24584 | tf_op jit(solution)/shard_map/ppermute | solution.py:20
  5.8 4.5 %collective-permute-done.refs_0_ = bf16[256,512]{1,0:T(8,128)(2,1)S(1)} collective-permute-done((bf16[256,512]{1,0:T(8,128)(2,1)}, bf16[256,512]{1,0:T(8,128)(2,1)S(1)}, u32[]{:S(2)}, u32[]{:S(2)}) %collective-permute-start) | collective-permute-done | bytes 262176 | tf_op jit(solution)/shard_map/ppermute | solution.py:20
  10.3 3.9 %collective-permute-start.1 = (bf16[256,512]{1,0:T(8,128)(2,1)S(1)}, bf16[256,512]{1,0:T(8,128)(2,1)S(1)}, u32[]{:S(2)}, u32[]{:S(2)}) collective-permute-start(bf16[256,512]{1,0:T(8,128)(2,1)S(1)} %collective-permute-done.refs_0_), channel_id=1, source_target_pairs={{0,4},{4,8},{8,12},{12,16},{16,20},{20,24},{24,28},{6,2},{10,6},{1... | collective-permute-start | bytes 786440 | tf_op jit(solution)/shard_map/ppermute | solution.py:328
  14.2 1.5 collective-permute-done.2.refs_3_
  15.7 3.7 %collective-permute-start.3 = (bf16[256,512]{1,0:T(8,128)(2,1)S(1)}, bf16[256,512]{1,0:T(8,128)(2,1)S(1)}, u32[]{:S(2)}, u32[]{:S(2)}) collective-permute-start(bf16[256,512]{1,0:T(8,128)(2,1)S(1)} %collective-permute-done.2.refs_3_), channel_id=1, source_target_pairs={{0,4},{4,8},{8,12},{12,16},{16,20},{20,24},{24,28},{6,2},{10,6},{1... | collective-permute-start | bytes 786440 | tf_op jit(solution)/shard_map/ppermute | solution.py:328
  19.5 2.6 %collective-permute-start.8 = (f32[16,256]{1,0:T(8,128)S(1)}, f32[16,256]{1,0:T(8,128)S(1)}, u32[]{:S(2)}, u32[]{:S(2)}) collective-permute-start(f32[16,256]{1,0:T(8,128)S(1)} %pad_maximum_fusion.2), channel_id=1, source_target_pairs={{0,16},{2,18},{4,20},{6,22},{8,24},{10,26},{12,28},{14,30},{16,0},... | collective-permute-start | bytes 49160 | tf_op jit(solution)/shard_map/ppermute | solution.py:20
  22.1 2.1 %collective-permute-done.8.refs_6_.refs_8_.refs_5_.refs_4_.refs_3_ = f32[16,256]{1,0:T(8,128)S(1)} collective-permute-done((f32[16,256]{1,0:T(8,128)S(1)}, f32[16,256]{1,0:T(8,128)S(1)}, u32[]{:S(2)}, u32[]{:S(2)}) %collective-permute-start.8) | collective-permute-done | bytes 16416 | tf_op jit(solution)/shard_map/ppermute | solution.py:20
  24.2 2.6 %collective-permute-start.9 = (f32[16,512]{1,0:T(8,128)S(1)}, f32[16,512]{1,0:T(8,128)S(1)}, u32[]{:S(2)}, u32[]{:S(2)}) collective-permute-start(f32[16,512]{1,0:T(8,128)S(1)} %pad_maximum_fusion.1), channel_id=1, source_target_pairs={{0,4},{2,6},{4,0},{6,2},{8,12},{10,14},{12,8},{14,10},{16,20},{18,... | collective-permute-start | bytes 98312 | tf_op jit(solution)/shard_map/ppermute | solution.py:20
  30.6 4.6 %window_attention.1 = (bf16[128,512]{1,0:T(8,128)(2,1)}, bf16[128,512]{1,0:T(8,128)(2,1)}) custom-call(s32[2]{0:T(128)} %pad_add_fusion.where_ref, bf16[256,512]{1,0:T(8,128)(2,1)} %q_ref.1, s32[1,768]{1,0:T(1,128)} %broadcast_in_dim.21.ids_ref, bf16[256,512]{1,0:T(8,128)(2,1)} %copy-done.5, bf16[256,512]{1,0:T(8,128)(2,1)} %refs_1_.1, ...), custom_call_target="tpu_custom_call" | custom-call | tf_op jit(solution)/shard_map/window_attention/pallas_call | solution.py:97
  35.1 1.5 collective-permute-done.6.theirs_ref
  37.3 4.3 %project_and_norm.1 = (f32[128,2048]{1,0:T(8,128)}, bf16[128,2048]{1,0:T(8,128)(2,1)}) custom-call(bf16[128,512]{1,0:T(8,128)(2,1)} %get-tuple-element.66.mine_ref, bf16[128,512]{1,0:T(8,128)(2,1)} %copy-done.9, bf16[512,2048]{1,0:T(8,128)(2,1)} %own_w.1, bf16[512,2048]{1,0:T(8,128)(2,1)} %collective-permute-done.4.refs_6_.other_w, ...), custom_call_target="tpu_custom_call" | custom-call | tf_op jit(solution)/shard_map/project_and_norm/pallas_call | solution.py:120
  41.6 2.0 %collective-permute-start.12 = (bf16[128,2048]{1,0:T(8,128)(2,1)}, bf16[128,2048]{1,0:T(8,128)(2,1)S(1)}, u32[]{:S(2)}, u32[]{:S(2)}) collective-permute-start(bf16[128,2048]{1,0:T(8,128)(2,1)} %get-tuple-element.74.refs_0_), channel_id=1, source_target_pairs={{0,8},{2,10},{4,12},{6,14},{8,0},{10,2},{12,4},{14,6},{16,24},{18,... | collective-permute-start | bytes 1572872 | tf_op jit(solution)/shard_map/ppermute | solution.py:20
  44.3 2.1 %collective-permute-start.17 = (bf16[128,2048]{1,0:T(8,128)(2,1)}, bf16[128,2048]{1,0:T(8,128)(2,1)S(1)}, u32[]{:S(2)}, u32[]{:S(2)}) collective-permute-start(bf16[128,2048]{1,0:T(8,128)(2,1)} %get-tuple-element.74.refs_0_), channel_id=1, source_target_pairs={{0,4},{1,3},{2,6},{3,1},{4,0},{5,7},{6,2},{7,5},{8,12},{9,11},{10,... | collective-permute-start | bytes 1572872 | tf_op jit(solution)/shard_map/ppermute | solution.py:26
  46.4 2.6 %collective-permute-start.16 = (bf16[128,2048]{1,0:T(8,128)(2,1)}, bf16[128,2048]{1,0:T(8,128)(2,1)S(1)}, u32[]{:S(2)}, u32[]{:S(2)}) collective-permute-start(bf16[128,2048]{1,0:T(8,128)(2,1)} %get-tuple-element.74.refs_0_), channel_id=1, source_target_pairs={{0,2},{1,5},{2,0},{3,7},{4,6},{5,1},{6,4},{7,3},{8,10},{9,13},{10,... | collective-permute-start | bytes 1572872 | tf_op jit(solution)/shard_map/ppermute | solution.py:26
  49.0 7.1 %collective-permute-done.12.refs_0_ = bf16[128,2048]{1,0:T(8,128)(2,1)S(1)} collective-permute-done((bf16[128,2048]{1,0:T(8,128)(2,1)}, bf16[128,2048]{1,0:T(8,128)(2,1)S(1)}, u32[]{:S(2)}, u32[]{:S(2)}) %collective-permute-start.12) | collective-permute-done | bytes 524320 | tf_op jit(solution)/shard_map/ppermute | solution.py:20
  58.8 2.2 %collective-permute-done.16.refs_1_ = bf16[128,2048]{1,0:T(8,128)(2,1)S(1)} collective-permute-done((bf16[128,2048]{1,0:T(8,128)(2,1)}, bf16[128,2048]{1,0:T(8,128)(2,1)S(1)}, u32[]{:S(2)}, u32[]{:S(2)}) %collective-permute-start.16) | collective-permute-done | bytes 524320 | tf_op jit(solution)/shard_map/ppermute | solution.py:26
  61.1 2.7 %collective-permute-start.18 = (bf16[128,2048]{1,0:T(8,128)(2,1)S(1)}, bf16[128,2048]{1,0:T(8,128)(2,1)S(1)}, u32[]{:S(2)}, u32[]{:S(2)}) collective-permute-start(bf16[128,2048]{1,0:T(8,128)(2,1)S(1)} %collective-permute-done.17.refs_2_), channel_id=1, source_target_pairs={{0,2},{1,5},{2,0},{3,7},{4,6},{5,1},{6,4},{7,3},{8,10},{9,13},{10,... | collective-permute-start | bytes 1572872 | tf_op jit(solution)/shard_map/ppermute | solution.py:26
  68.1 2.6 %assemble_weights.1 = (bf16[1408,2048]{1,0:T(8,128)(2,1)S(1)}, bf16[704,2048]{1,0:T(8,128)(2,1)S(1)}) custom-call(bf16[352,2048]{1,0:T(8,128)(2,1)S(1)} %bitcast.14, bf16[352,2048]{1,0:T(8,128)(2,1)} %collective-permute-done.5.refs_7_.refs_1_, bf16[352,2048]{1,0:T(8,128)(2,1)S(1)} %bitcast.16, bf16[352,2048]{1,0:T(8,128)(2,1)} %collective-permute-done.10.refs_0_.refs_3_, ...), custom_call_target="tpu_custom_call" | custom-call | tf_op jit(solution)/shard_map/assemble_weights/pallas_call | solution.py:148
  70.7 6.7 %collective-permute-done.15 = bf16[128,2048]{1,0:T(8,128)(2,1)} collective-permute-done((bf16[128,2048]{1,0:T(8,128)(2,1)S(1)}, bf16[128,2048]{1,0:T(8,128)(2,1)}, u32[]{:S(2)}, u32[]{:S(2)}) %collective-permute-start.15) | collective-permute-done | bytes 524320 | tf_op jit(solution)/shard_map/ppermute | solution.py:216
  80.0 1.9 %collective-permute-start.21 = (bf16[128,2048]{1,0:T(8,128)(2,1)S(1)}, bf16[128,2048]{1,0:T(8,128)(2,1)S(1)}, u32[]{:S(2)}, u32[]{:S(2)}) collective-permute-start(bf16[128,2048]{1,0:T(8,128)(2,1)S(1)} %broadcast_select_fusion.1.refs_2_), channel_id=1, source_target_pairs={{0,2},{1,5},{2,0},{3,7},{4,6},{5,1},{6,4},{7,3},{8,10},{9,13},{10,... | collective-permute-start | bytes 1572872 | tf_op jit(solution)/shard_map/ppermute | solution.py:26
  82.2 5.6 %expert_rows.5 = (bf16[128,2048]{1,0:T(8,128)(2,1)S(1)}, bf16[128,2048]{1,0:T(8,128)(2,1)S(1)}, bf16[128,2048]{1,0:T(8,128)(2,1)S(1)}, bf16[128,2048]{1,0:T(8,128)(2,1)S(1)}) custom-call(s32[2]{0:T(128)S(1)} %pad_add_fusion.1.where_ref, bf16[128,2048]{1,0:T(8,128)(2,1)S(1)} %copy-done.3, bf16[128,2048]{1,0:T(8,128)(2,1)S(1)} %collective-permute-done.16.refs_1_, ...), custom_call_target="tpu_custom_call" | custom-call | tf_op jit(solution)/shard_map/expert_rows/pallas_call | solution.py:194
  87.9 3.5 %collective-permute-done.23 = bf16[128,2048]{1,0:T(8,128)(2,1)S(1)} collective-permute-done((bf16[128,2048]{1,0:T(8,128)(2,1)}, bf16[128,2048]{1,0:T(8,128)(2,1)S(1)}, u32[]{:S(2)}, u32[]{:S(2)}) %collective-permute-start.23) | collective-permute-done | bytes 524320 | tf_op jit(solution)/shard_map/ppermute | solution.py:216
  91.5 2.3 %collective-permute-done.21.refs_3_ = bf16[128,2048]{1,0:T(8,128)(2,1)S(1)} collective-permute-done((bf16[128,2048]{1,0:T(8,128)(2,1)S(1)}, bf16[128,2048]{1,0:T(8,128)(2,1)S(1)}, u32[]{:S(2)}, u32[]{:S(2)}) %collective-permute-start.21) | collective-permute-done | bytes 524320 | tf_op jit(solution)/shard_map/ppermute | solution.py:26
  94.2 1.7 collective-permute-start.26
  95.9 2.4 %collective-permute-start.27 = (bf16[128,2048]{1,0:T(8,128)(2,1)S(1)}, bf16[128,2048]{1,0:T(8,128)(2,1)S(1)}, u32[]{:S(2)}, u32[]{:S(2)}) collective-permute-start(bf16[128,2048]{1,0:T(8,128)(2,1)S(1)} %collective-permute-done.16.refs_1_), channel_id=1, source_target_pairs={{0,8},{2,10},{4,12},{6,14},{8,0},{10,2},{12,4},{14,6},{16,24},{18,... | collective-permute-start | bytes 1572872 | tf_op jit(solution)/shard_map/ppermute | solution.py:20
  98.3 8.1 %expert_rows.6 = (bf16[128,2048]{1,0:T(8,128)(2,1)S(1)}, bf16[128,2048]{1,0:T(8,128)(2,1)S(1)}, bf16[128,2048]{1,0:T(8,128)(2,1)S(1)}, bf16[128,2048]{1,0:T(8,12...) custom-call(s32[2]{0:T(128)S(1)} %pad_add_fusion.1.where_ref, ...), custom_call_target="tpu_custom_call" | custom-call | tf_op jit(solution)/shard_map/expert_rows/pallas_call | solution.py:194
  106.8 2.1 %collective-permute-start.28 = (bf16[128,2048]{1,0:T(8,128)(2,1)S(1)}, bf16[128,2048]{1,0:T(8,128)(2,1)S(1)}, u32[]{:S(2)}, u32[]{:S(2)}) collective-permute-start(bf16[128,2048]{1,0:T(8,128)(2,1)S(1)} %collective-permute-done.24.refs_0_), channel_id=1, source_target_pairs={{0,4},{1,3},{2,6},{3,1},{4,0},{5,7},{6,2},{7,5},{8,12},{9,11},{10,... | collective-permute-start | bytes 1572872 | tf_op jit(solution)/shard_map/ppermute | solution.py:26
  108.9 2.1 %collective-permute-start.36 = (bf16[128,2048]{1,0:T(8,128)(2,1)S(1)}, bf16[128,2048]{1,0:T(8,128)(2,1)S(1)}, u32[]{:S(2)}, u32[]{:S(2)}) collective-permute-start(bf16[128,2048]{1,0:T(8,128)(2,1)S(1)} %collective-permute-done.18.refs_3_), channel_id=1, source_target_pairs={{0,8},{2,10},{4,12},{6,14},{8,0},{10,2},{12,4},{14,6},{16,24},{18,... | collective-permute-start | bytes 1572872 | tf_op jit(solution)/shard_map/ppermute | solution.py:20
  110.9 5.6 %expert_rows.7 = (bf16[128,2048]{1,0:T(8,128)(2,1)S(1)}, bf16[128,2048]{1,0:T(8,128)(2,1)S(1)}, bf16[128,2048]{1,0:T(8,128)(2,1)S(1)}) custom-call(s32[2]{0:T(128)S(1)} %pad_add_fusion.1.where_ref, bf16[128,2048]{1,0:T(8,128)(2,1)S(1)} %collective-permute-done.24.refs_0_, bf16[128,2048]{1,0:T(8,128)(2,1)S(1)} %collective-permute-done.26.refs_1_, ...), custom_call_target="tpu_custom_call" | custom-call | tf_op jit(solution)/shard_map/expert_rows/pallas_call | solution.py:194
  116.6 1.7 collective-permute-done.25.refs_0_
  118.3 3.2 %expert_rows.8 = (bf16[128,2048]{1,0:T(8,128)(2,1)S(1)}, bf16[128,2048]{1,0:T(8,128)(2,1)S(1)}) custom-call(s32[2]{0:T(128)S(1)} %pad_add_fusion.1.where_ref, bf16[128,2048]{1,0:T(8,128)(2,1)S(1)} %collective-permute-done.25.refs_0_, bf16[128,2048]{1,0:T(8,128)(2,1)S(1)} %collective-permute-done.28.refs_1_, ...), custom_call_target="tpu_custom_call" | custom-call | tf_op jit(solution)/shard_map/expert_rows/pallas_call | solution.py:194
  122.5 1.7 collective-permute-start.29
  124.2 2.9 %expert_rows.9 = bf16[128,2048]{1,0:T(8,128)(2,1)S(1)} custom-call(s32[2]{0:T(128)S(1)} %pad_add_fusion.1.where_ref, bf16[128,2048]{1,0:T(8,128)(2,1)S(1)} %collective-permute-done.36.refs_0_, f32[16,128]{1,0:T(8,128)S(1)} %select_reduce_fusion.refs_4_.refs_6_.refs_3_.refs_2_.refs_1_, ...), custom_call_target="tpu_custom_call" | custom-call | tf_op jit(solution)/shard_map/expert_rows/pallas_call | solution.py:194
  127.1 1.8 collective-permute-start.37
  128.9 4.3 %collective-permute-done.30 = bf16[128,2048]{1,0:T(8,128)(2,1)S(1)} collective-permute-done((bf16[128,2048]{1,0:T(8,128)(2,1)S(1)}, bf16[128,2048]{1,0:T(8,128)(2,1)S(1)}, u32[]{:S(2)}, u32[]{:S(2)}) %collective-permute-start.30) | collective-permute-done | bytes 524320 | tf_op jit(solution)/shard_map/ppermute | solution.py:26
  134.5 1.9 %collective-permute-start.31 = (bf16[128,2048]{1,0:T(8,128)(2,1)S(1)}, bf16[128,2048]{1,0:T(8,128)(2,1)S(1)}, u32[]{:S(2)}, u32[]{:S(2)}) collective-permute-start(bf16[128,2048]{1,0:T(8,128)(2,1)S(1)} %get-tuple-element.105), channel_id=1, source_target_pairs={{0,4},{1,3},{2,6},{3,1},{4,0},{5,7},{6,2},{7,5},{8,12},{9,11},{10,... | collective-permute-start | bytes 1572872 | tf_op jit(solution)/shard_map/ppermute | solution.py:26
  136.4 2.9 %collective-permute-done.37 = bf16[128,2048]{1,0:T(8,128)(2,1)S(1)} collective-permute-done((bf16[128,2048]{1,0:T(8,128)(2,1)S(1)}, bf16[128,2048]{1,0:T(8,128)(2,1)S(1)}, u32[]{:S(2)}, u32[]{:S(2)}) %collective-permute-start.37) | collective-permute-done | bytes 524320 | tf_op jit(solution)/shard_map/ppermute | solution.py:20
  139.3 1.7 collective-permute-start.38
  141.2 5.2 %collective-permute-done.34 = bf16[128,2048]{1,0:T(8,128)(2,1)S(1)} collective-permute-done((bf16[128,2048]{1,0:T(8,128)(2,1)S(1)}, bf16[128,2048]{1,0:T(8,128)(2,1)S(1)}, u32[]{:S(2)}, u32[]{:S(2)}) %collective-permute-start.34) | collective-permute-done | bytes 524320 | tf_op jit(solution)/shard_map/ppermute | solution.py:26
  146.7 1.8 collective-permute-start.32
  149.0 3.6 %collective-permute-start.39 = (bf16[128,2048]{1,0:T(8,128)(2,1)S(1)}, bf16[128,2048]{1,0:T(8,128)(2,1)S(1)}, u32[]{:S(2)}, u32[]{:S(2)}) collective-permute-start(bf16[128,2048]{1,0:T(8,128)(2,1)S(1)} %add_convert_fusion.7), channel_id=1, source_target_pairs={{0,8},{2,10},{4,12},{6,14},{24,16},{26,18},{28,20},{30,22},{1,9},{... | collective-permute-start | bytes 1572872 | tf_op jit(solution)/shard_map/ppermute | solution.py:216
  152.7 5.8 %collective-permute-done.35 = bf16[128,2048]{1,0:T(8,128)(2,1)S(1)} collective-permute-done((bf16[128,2048]{1,0:T(8,128)(2,1)S(1)}, bf16[128,2048]{1,0:T(8,128)(2,1)S(1)}, u32[]{:S(2)}, u32[]{:S(2)}) %collective-permute-start.35) | collective-permute-done | bytes 524320 | tf_op jit(solution)/shard_map/ppermute | solution.py:26
  158.8 1.8 collective-permute-start.33
  161.0 3.9 %collective-permute-start.41 = (bf16[128,2048]{1,0:T(8,128)(2,1)S(1)}, bf16[128,2048]{1,0:T(8,128)(2,1)S(1)}, u32[]{:S(2)}, u32[]{:S(2)}) collective-permute-start(bf16[128,2048]{1,0:T(8,128)(2,1)S(1)} %add_convert_fusion.6), channel_id=1, source_target_pairs={{0,8},{2,10},{4,12},{6,14},{24,16},{26,18},{28,20},{30,22},{1,9},{... | collective-permute-start | bytes 1572872 | tf_op jit(solution)/shard_map/ppermute | solution.py:216
  165.7 4.9 %collective-permute-done.44 = bf16[128,2048]{1,0:T(8,128)(2,1)S(1)} collective-permute-done((bf16[128,2048]{1,0:T(8,128)(2,1)S(1)}, bf16[128,2048]{1,0:T(8,128)(2,1)S(1)}, u32[]{:S(2)}, u32[]{:S(2)}) %collective-permute-start.44) | collective-permute-done | bytes 524320 | tf_op jit(solution)/shard_map/ppermute | solution.py:26
  173.6 8.6 %collective-permute-start.42 = (bf16[128,2048]{1,0:T(8,128)(2,1)S(1)}, bf16[128,2048]{1,0:T(8,128)(2,1)S(1)}, u32[]{:S(2)}, u32[]{:S(2)}) collective-permute-start(bf16[128,2048]{1,0:T(8,128)(2,1)S(1)} %add_convert_fusion.5), channel_id=1, source_target_pairs={{0,8},{2,10},{4,12},{6,14},{8,0},{10,2},{12,4},{14,6},{16,24},{18,... | collective-permute-start | bytes 1572872 | tf_op jit(solution)/shard_map/ppermute | solution.py:20
  182.3 7.1 %collective-permute-done.42 = bf16[128,2048]{1,0:T(8,128)(2,1)S(1)} collective-permute-done((bf16[128,2048]{1,0:T(8,128)(2,1)S(1)}, bf16[128,2048]{1,0:T(8,128)(2,1)S(1)}, u32[]{:S(2)}, u32[]{:S(2)}) %collective-permute-start.42) | collective-permute-done | bytes 524320 | tf_op jit(solution)/shard_map/ppermute | solution.py:20
  (94 shorter events, 26.1 us)
Async XLA Ops:
  0.0 30.5 %collective-permute-start.4 = (bf16[512,2048]{1,0:T(8,128)(2,1)}, bf16[512,2048]{1,0:T(8,128)(2,1)}, u32[]{:S(2)}, u32[]{:S(2)}) collective-permute-start(bf16[512,2048]{1,0:T(8,128)(2,1)} %own_w.1), channel_id=1, source_target_pairs={{0,1},{1,0},{2,3},{3,2},{4,5},{5,4},{6,7},{7,6},{8,9},{9,8},{10,11... | collective-permute-start | bytes 6291464 | tf_op jit(solution)/shard_map/ppermute | solution.py:337
  0.5 9.9 %collective-permute-start = (bf16[256,512]{1,0:T(8,128)(2,1)}, bf16[256,512]{1,0:T(8,128)(2,1)S(1)}, u32[]{:S(2)}, u32[]{:S(2)}) collective-permute-start(bf16[256,512]{1,0:T(8,128)(2,1)} %refs_1_.1), channel_id=1, source_target_pairs={{0,2},{2,0},{4,6},{6,4},{8,10},{10,8},{12,14},{14,12},{16,18},{18,... | collective-permute-start | bytes 786440 | tf_op jit(solution)/shard_map/ppermute | solution.py:20
  2.9 12.8 %collective-permute-start.2 = (bf16[256,512]{1,0:T(8,128)(2,1)}, bf16[256,512]{1,0:T(8,128)(2,1)S(1)}, u32[]{:S(2)}, u32[]{:S(2)}) collective-permute-start(bf16[256,512]{1,0:T(8,128)(2,1)} %refs_4_.1), channel_id=1, source_target_pairs={{0,2},{2,0},{4,6},{6,4},{8,10},{10,8},{12,14},{14,12},{16,18},{18,... | collective-permute-start | bytes 786440 | tf_op jit(solution)/shard_map/ppermute | solution.py:20
  3.7 15.7 %collective-permute-start.7 = (f32[16,128]{1,0:T(8,128)S(1)}, f32[16,128]{1,0:T(8,128)S(1)}, u32[]{:S(2)}, u32[]{:S(2)}) collective-permute-start(f32[16,128]{1,0:T(8,128)S(1)} %select_reduce_fusion.refs_4_.refs_6_.refs_3_.refs_2_.refs_1_), channel_id=1, source_target_pairs={{0,8},{2,10},{4,12},{6,14},{8,0},{10,2},{12,4},{14,6},{16,24},{18,... | collective-permute-start | bytes 24584 | tf_op jit(solution)/shard_map/ppermute | solution.py:20
  10.3 20.2 %copy-start.5 = (bf16[256,512]{1,0:T(8,128)(2,1)}, bf16[256,512]{1,0:T(8,128)(2,1)S(1)}, u32[]{:S(2)}) copy-start(bf16[256,512]{1,0:T(8,128)(2,1)S(1)} %collective-permute-done.refs_0_) | copy-start | bytes 786436
  10.3 18.3 %collective-permute-start.1 = (bf16[256,512]{1,0:T(8,128)(2,1)S(1)}, bf16[256,512]{1,0:T(8,128)(2,1)S(1)}, u32[]{:S(2)}, u32[]{:S(2)}) collective-permute-start(bf16[256,512]{1,0:T(8,128)(2,1)S(1)} %collective-permute-done.refs_0_), channel_id=1, source_target_pairs={{0,4},{4,8},{8,12},{12,16},{16,20},{20,24},{24,28},{6,2},{10,6},{1... | collective-permute-start | bytes 786440 | tf_op jit(solution)/shard_map/ppermute | solution.py:328
  15.7 12.9 %collective-permute-start.3 = (bf16[256,512]{1,0:T(8,128)(2,1)S(1)}, bf16[256,512]{1,0:T(8,128)(2,1)S(1)}, u32[]{:S(2)}, u32[]{:S(2)}) collective-permute-start(bf16[256,512]{1,0:T(8,128)(2,1)S(1)} %collective-permute-done.2.refs_3_), channel_id=1, source_target_pairs={{0,4},{4,8},{8,12},{12,16},{16,20},{20,24},{24,28},{6,2},{10,6},{1... | collective-permute-start | bytes 786440 | tf_op jit(solution)/shard_map/ppermute | solution.py:328
  19.5 4.7 %collective-permute-start.8 = (f32[16,256]{1,0:T(8,128)S(1)}, f32[16,256]{1,0:T(8,128)S(1)}, u32[]{:S(2)}, u32[]{:S(2)}) collective-permute-start(f32[16,256]{1,0:T(8,128)S(1)} %pad_maximum_fusion.2), channel_id=1, source_target_pairs={{0,16},{2,18},{4,20},{6,22},{8,24},{10,26},{12,28},{14,30},{16,0},... | collective-permute-start | bytes 49160 | tf_op jit(solution)/shard_map/ppermute | solution.py:20
  22.1 8.4 %collective-permute-start.5 = (bf16[352,2048]{1,0:T(8,128)(2,1)}, bf16[352,2048]{1,0:T(8,128)(2,1)}, u32[]{:S(2)}, u32[]{:S(2)}) collective-permute-start(bf16[352,2048]{1,0:T(8,128)(2,1)} %bitcast.13), channel_id=1, source_target_pairs={{0,1},{1,0},{2,3},{3,2},{4,5},{5,4},{6,7},{7,6},{8,9},{9,8},{10,11... | collective-permute-start | bytes 4325384 | tf_op jit(solution)/shard_map/ppermute | solution.py:339
  24.2 4.5 %collective-permute-start.9 = (f32[16,512]{1,0:T(8,128)S(1)}, f32[16,512]{1,0:T(8,128)S(1)}, u32[]{:S(2)}, u32[]{:S(2)}) collective-permute-start(f32[16,512]{1,0:T(8,128)S(1)} %pad_maximum_fusion.1), channel_id=1, source_target_pairs={{0,4},{2,6},{4,0},{6,2},{8,12},{10,14},{12,8},{14,10},{16,20},{18,... | collective-permute-start | bytes 98312 | tf_op jit(solution)/shard_map/ppermute | solution.py:20
  29.4 5.8 %collective-permute-start.10 = (bf16[352,2048]{1,0:T(8,128)(2,1)}, bf16[352,2048]{1,0:T(8,128)(2,1)}, u32[]{:S(2)}, u32[]{:S(2)}) collective-permute-start(bf16[352,2048]{1,0:T(8,128)(2,1)} %bitcast.15), channel_id=1, source_target_pairs={{0,1},{1,0},{2,3},{3,2},{4,5},{5,4},{6,7},{7,6},{8,9},{9,8},{10,11... | collective-permute-start | bytes 4325384 | tf_op jit(solution)/shard_map/ppermute | solution.py:341
  29.4 5.8 %collective-permute-start.11 = (bf16[352,2048]{1,0:T(8,128)(2,1)}, bf16[352,2048]{1,0:T(8,128)(2,1)}, u32[]{:S(2)}, u32[]{:S(2)}) collective-permute-start(bf16[352,2048]{1,0:T(8,128)(2,1)} %bitcast.17), channel_id=1, source_target_pairs={{0,1},{1,0},{2,3},{3,2},{4,5},{5,4},{6,7},{7,6},{8,9},{9,8},{10,11... | collective-permute-start | bytes 4325384 | tf_op jit(solution)/shard_map/ppermute | solution.py:342
  35.1 1.6 collective-permute-start.6
  41.6 14.4 %collective-permute-start.12 = (bf16[128,2048]{1,0:T(8,128)(2,1)}, bf16[128,2048]{1,0:T(8,128)(2,1)S(1)}, u32[]{:S(2)}, u32[]{:S(2)}) collective-permute-start(bf16[128,2048]{1,0:T(8,128)(2,1)} %get-tuple-element.74.refs_0_), channel_id=1, source_target_pairs={{0,8},{2,10},{4,12},{6,14},{8,0},{10,2},{12,4},{14,6},{16,24},{18,... | collective-permute-start | bytes 1572872 | tf_op jit(solution)/shard_map/ppermute | solution.py:20
  43.6 12.4 %collective-permute-start.13 = (bf16[128,2048]{1,0:T(8,128)(2,1)}, bf16[128,2048]{1,0:T(8,128)(2,1)S(1)}, u32[]{:S(2)}, u32[]{:S(2)}) collective-permute-start(bf16[128,2048]{1,0:T(8,128)(2,1)} %get-tuple-element.74.refs_0_), channel_id=1, source_target_pairs={{8,16},{10,18},{12,20},{14,22},{16,8},{18,10},{20,12},{22,14},{9,1... | collective-permute-start | bytes 1572872 | tf_op jit(solution)/shard_map/ppermute | solution.py:216
  44.3 14.5 %collective-permute-start.17 = (bf16[128,2048]{1,0:T(8,128)(2,1)}, bf16[128,2048]{1,0:T(8,128)(2,1)S(1)}, u32[]{:S(2)}, u32[]{:S(2)}) collective-permute-start(bf16[128,2048]{1,0:T(8,128)(2,1)} %get-tuple-element.74.refs_0_), channel_id=1, source_target_pairs={{0,4},{1,3},{2,6},{3,1},{4,0},{5,7},{6,2},{7,5},{8,12},{9,11},{10,... | collective-permute-start | bytes 1572872 | tf_op jit(solution)/shard_map/ppermute | solution.py:26
  46.4 14.7 %collective-permute-start.16 = (bf16[128,2048]{1,0:T(8,128)(2,1)}, bf16[128,2048]{1,0:T(8,128)(2,1)S(1)}, u32[]{:S(2)}, u32[]{:S(2)}) collective-permute-start(bf16[128,2048]{1,0:T(8,128)(2,1)} %get-tuple-element.74.refs_0_), channel_id=1, source_target_pairs={{0,2},{1,5},{2,0},{3,7},{4,6},{5,1},{6,4},{7,3},{8,10},{9,13},{10,... | collective-permute-start | bytes 1572872 | tf_op jit(solution)/shard_map/ppermute | solution.py:26
  56.0 14.7 %collective-permute-start.14 = (bf16[128,2048]{1,0:T(8,128)(2,1)S(1)}, bf16[128,2048]{1,0:T(8,128)(2,1)}, u32[]{:S(2)}, u32[]{:S(2)}) collective-permute-start(bf16[128,2048]{1,0:T(8,128)(2,1)S(1)} %collective-permute-done.12.refs_0_), channel_id=1, source_target_pairs={{8,16},{10,18},{12,20},{14,22},{16,8},{18,10},{20,12},{22,14},{9,1... | collective-permute-start | bytes 1572872 | tf_op jit(solution)/shard_map/ppermute | solution.py:216
  57.5 19.9 %collective-permute-start.15 = (bf16[128,2048]{1,0:T(8,128)(2,1)S(1)}, bf16[128,2048]{1,0:T(8,128)(2,1)}, u32[]{:S(2)}, u32[]{:S(2)}) collective-permute-start(bf16[128,2048]{1,0:T(8,128)(2,1)S(1)} %collective-permute-done.13), channel_id=1, source_target_pairs={{8,0},{10,2},{12,4},{14,6},{16,24},{18,26},{20,28},{22,30},{9,1},{... | collective-permute-start | bytes 1572872 | tf_op jit(solution)/shard_map/ppermute | solution.py:216
  61.1 18.9 %collective-permute-start.18 = (bf16[128,2048]{1,0:T(8,128)(2,1)S(1)}, bf16[128,2048]{1,0:T(8,128)(2,1)S(1)}, u32[]{:S(2)}, u32[]{:S(2)}) collective-permute-start(bf16[128,2048]{1,0:T(8,128)(2,1)S(1)} %collective-permute-done.17.refs_2_), channel_id=1, source_target_pairs={{0,2},{1,5},{2,0},{3,7},{4,6},{5,1},{6,4},{7,3},{8,10},{9,13},{10,... | collective-permute-start | bytes 1572872 | tf_op jit(solution)/shard_map/ppermute | solution.py:26
  63.8 18.1 %collective-permute-start.20 = (bf16[128,2048]{1,0:T(8,128)(2,1)S(1)}, bf16[128,2048]{1,0:T(8,128)(2,1)S(1)}, u32[]{:S(2)}, u32[]{:S(2)}) collective-permute-start(bf16[128,2048]{1,0:T(8,128)(2,1)S(1)} %collective-permute-done.12.refs_0_), channel_id=1, source_target_pairs={{0,4},{1,3},{2,6},{3,1},{4,0},{5,7},{6,2},{7,5},{8,12},{9,11},{10,... | collective-permute-start | bytes 1572872 | tf_op jit(solution)/shard_map/ppermute | solution.py:26
  63.8 18.4 %collective-permute-start.19 = (f32[16,1024]{1,0:T(8,128)S(1)}, f32[16,1024]{1,0:T(8,128)S(1)}, u32[]{:S(2)}, u32[]{:S(2)}) collective-permute-start(f32[16,1024]{1,0:T(8,128)S(1)} %pad_maximum_fusion), channel_id=1, source_target_pairs={{0,2},{2,0},{4,6},{6,4},{8,10},{10,8},{12,14},{14,12},{16,18},{18,... | collective-permute-start | bytes 196616 | tf_op jit(solution)/shard_map/ppermute | solution.py:20
  77.4 14.0 %collective-permute-start.23 = (bf16[128,2048]{1,0:T(8,128)(2,1)}, bf16[128,2048]{1,0:T(8,128)(2,1)S(1)}, u32[]{:S(2)}, u32[]{:S(2)}) collective-permute-start(bf16[128,2048]{1,0:T(8,128)(2,1)} %collective-permute-done.14), channel_id=1, source_target_pairs={{8,0},{10,2},{12,4},{14,6},{16,24},{18,26},{20,28},{22,30},{9,1},{... | collective-permute-start | bytes 1572872 | tf_op jit(solution)/shard_map/ppermute | solution.py:216
  80.0 13.7 %collective-permute-start.21 = (bf16[128,2048]{1,0:T(8,128)(2,1)S(1)}, bf16[128,2048]{1,0:T(8,128)(2,1)S(1)}, u32[]{:S(2)}, u32[]{:S(2)}) collective-permute-start(bf16[128,2048]{1,0:T(8,128)(2,1)S(1)} %broadcast_select_fusion.1.refs_2_), channel_id=1, source_target_pairs={{0,2},{1,5},{2,0},{3,7},{4,6},{5,1},{6,4},{7,3},{8,10},{9,13},{10,... | collective-permute-start | bytes 1572872 | tf_op jit(solution)/shard_map/ppermute | solution.py:26
  81.9 12.3 %collective-permute-start.22 = (bf16[128,2048]{1,0:T(8,128)(2,1)S(1)}, bf16[128,2048]{1,0:T(8,128)(2,1)S(1)}, u32[]{:S(2)}, u32[]{:S(2)}) collective-permute-start(bf16[128,2048]{1,0:T(8,128)(2,1)S(1)} %broadcast_select_fusion.1.refs_2_), channel_id=1, source_target_pairs={{0,4},{1,3},{2,6},{3,1},{4,0},{5,7},{6,2},{7,5},{8,12},{9,11},{10,... | collective-permute-start | bytes 1572872 | tf_op jit(solution)/shard_map/ppermute | solution.py:26
  93.7 12.8 %collective-permute-start.24 = (bf16[128,2048]{1,0:T(8,128)(2,1)S(1)}, bf16[128,2048]{1,0:T(8,128)(2,1)S(1)}, u32[]{:S(2)}, u32[]{:S(2)}) collective-permute-start(bf16[128,2048]{1,0:T(8,128)(2,1)S(1)} %broadcast_select_fusion.refs_5_), channel_id=1, source_target_pairs={{0,2},{1,5},{2,0},{3,7},{4,6},{5,1},{6,4},{7,3},{8,10},{9,13},{10,... | collective-permute-start | bytes 1572872 | tf_op jit(solution)/shard_map/ppermute | solution.py:26
  94.2 12.5 %collective-permute-start.26 = (bf16[128,2048]{1,0:T(8,128)(2,1)S(1)}, bf16[128,2048]{1,0:T(8,128)(2,1)S(1)}, u32[]{:S(2)}, u32[]{:S(2)}) collective-permute-start(bf16[128,2048]{1,0:T(8,128)(2,1)S(1)} %broadcast_select_fusion.refs_5_), channel_id=1, source_target_pairs={{0,4},{1,3},{2,6},{3,1},{4,0},{5,7},{6,2},{7,5},{8,12},{9,11},{10,... | collective-permute-start | bytes 1572872 | tf_op jit(solution)/shard_map/ppermute | solution.py:26
  95.9 13.0 %collective-permute-start.27 = (bf16[128,2048]{1,0:T(8,128)(2,1)S(1)}, bf16[128,2048]{1,0:T(8,128)(2,1)S(1)}, u32[]{:S(2)}, u32[]{:S(2)}) collective-permute-start(bf16[128,2048]{1,0:T(8,128)(2,1)S(1)} %collective-permute-done.16.refs_1_), channel_id=1, source_target_pairs={{0,8},{2,10},{4,12},{6,14},{8,0},{10,2},{12,4},{14,6},{16,24},{18,... | collective-permute-start | bytes 1572872 | tf_op jit(solution)/shard_map/ppermute | solution.py:20
  106.5 11.9 %collective-permute-start.25 = (bf16[128,2048]{1,0:T(8,128)(2,1)S(1)}, bf16[128,2048]{1,0:T(8,128)(2,1)S(1)}, u32[]{:S(2)}, u32[]{:S(2)}) collective-permute-start(bf16[128,2048]{1,0:T(8,128)(2,1)S(1)} %collective-permute-done.22.refs_4_), channel_id=1, source_target_pairs={{0,2},{1,5},{2,0},{3,7},{4,6},{5,1},{6,4},{7,3},{8,10},{9,13},{10,... | collective-permute-start | bytes 1572872 | tf_op jit(solution)/shard_map/ppermute | solution.py:26
  106.8 11.6 %collective-permute-start.28 = (bf16[128,2048]{1,0:T(8,128)(2,1)S(1)}, bf16[128,2048]{1,0:T(8,128)(2,1)S(1)}, u32[]{:S(2)}, u32[]{:S(2)}) collective-permute-start(bf16[128,2048]{1,0:T(8,128)(2,1)S(1)} %collective-permute-done.24.refs_0_), channel_id=1, source_target_pairs={{0,4},{1,3},{2,6},{3,1},{4,0},{5,7},{6,2},{7,5},{8,12},{9,11},{10,... | collective-permute-start | bytes 1572872 | tf_op jit(solution)/shard_map/ppermute | solution.py:26
  108.9 15.3 %collective-permute-start.36 = (bf16[128,2048]{1,0:T(8,128)(2,1)S(1)}, bf16[128,2048]{1,0:T(8,128)(2,1)S(1)}, u32[]{:S(2)}, u32[]{:S(2)}) collective-permute-start(bf16[128,2048]{1,0:T(8,128)(2,1)S(1)} %collective-permute-done.18.refs_3_), channel_id=1, source_target_pairs={{0,8},{2,10},{4,12},{6,14},{8,0},{10,2},{12,4},{14,6},{16,24},{18,... | collective-permute-start | bytes 1572872 | tf_op jit(solution)/shard_map/ppermute | solution.py:20
  121.6 11.7 %collective-permute-start.30 = (bf16[128,2048]{1,0:T(8,128)(2,1)S(1)}, bf16[128,2048]{1,0:T(8,128)(2,1)S(1)}, u32[]{:S(2)}, u32[]{:S(2)}) collective-permute-start(bf16[128,2048]{1,0:T(8,128)(2,1)S(1)} %get-tuple-element.104), channel_id=1, source_target_pairs={{0,4},{1,3},{2,6},{3,1},{4,0},{5,7},{6,2},{7,5},{8,12},{9,11},{10,... | collective-permute-start | bytes 1572872 | tf_op jit(solution)/shard_map/ppermute | solution.py:26
  122.5 11.0 %collective-permute-start.29 = (bf16[128,2048]{1,0:T(8,128)(2,1)S(1)}, bf16[128,2048]{1,0:T(8,128)(2,1)S(1)}, u32[]{:S(2)}, u32[]{:S(2)}) collective-permute-start(bf16[128,2048]{1,0:T(8,128)(2,1)S(1)} %get-tuple-element.102), channel_id=1, source_target_pairs={{0,2},{1,5},{2,0},{3,7},{4,6},{5,1},{6,4},{7,3},{8,10},{9,13},{10,... | collective-permute-start | bytes 1572872 | tf_op jit(solution)/shard_map/ppermute | solution.py:26
  127.1 12.2 %collective-permute-start.37 = (bf16[128,2048]{1,0:T(8,128)(2,1)S(1)}, bf16[128,2048]{1,0:T(8,128)(2,1)S(1)}, u32[]{:S(2)}, u32[]{:S(2)}) collective-permute-start(bf16[128,2048]{1,0:T(8,128)(2,1)S(1)} %expert_rows.9), channel_id=1, source_target_pairs={{0,8},{2,10},{4,12},{6,14},{8,0},{10,2},{12,4},{14,6},{16,24},{18,... | collective-permute-start | bytes 1572872 | tf_op jit(solution)/shard_map/ppermute | solution.py:20
  133.4 13.0 %collective-permute-start.34 = (bf16[128,2048]{1,0:T(8,128)(2,1)S(1)}, bf16[128,2048]{1,0:T(8,128)(2,1)S(1)}, u32[]{:S(2)}, u32[]{:S(2)}) collective-permute-start(bf16[128,2048]{1,0:T(8,128)(2,1)S(1)} %add_convert_fusion.8), channel_id=1, source_target_pairs={{0,2},{1,5},{2,0},{3,7},{4,6},{5,1},{6,4},{7,3},{8,10},{9,13},{10,... | collective-permute-start | bytes 1572872 | tf_op jit(solution)/shard_map/ppermute | solution.py:26
  134.5 12.2 %collective-permute-start.31 = (bf16[128,2048]{1,0:T(8,128)(2,1)S(1)}, bf16[128,2048]{1,0:T(8,128)(2,1)S(1)}, u32[]{:S(2)}, u32[]{:S(2)}) collective-permute-start(bf16[128,2048]{1,0:T(8,128)(2,1)S(1)} %get-tuple-element.105), channel_id=1, source_target_pairs={{0,4},{1,3},{2,6},{3,1},{4,0},{5,7},{6,2},{7,5},{8,12},{9,11},{10,... | collective-permute-start | bytes 1572872 | tf_op jit(solution)/shard_map/ppermute | solution.py:26
  139.3 9.7 %collective-permute-start.38 = (bf16[128,2048]{1,0:T(8,128)(2,1)S(1)}, bf16[128,2048]{1,0:T(8,128)(2,1)S(1)}, u32[]{:S(2)}, u32[]{:S(2)}) collective-permute-start(bf16[128,2048]{1,0:T(8,128)(2,1)S(1)} %get-tuple-element.116), channel_id=1, source_target_pairs={{0,8},{2,10},{4,12},{6,14},{8,0},{10,2},{12,4},{14,6},{16,24},{18,... | collective-permute-start | bytes 1572872 | tf_op jit(solution)/shard_map/ppermute | solution.py:20
  146.4 12.1 %collective-permute-start.35 = (bf16[128,2048]{1,0:T(8,128)(2,1)S(1)}, bf16[128,2048]{1,0:T(8,128)(2,1)S(1)}, u32[]{:S(2)}, u32[]{:S(2)}) collective-permute-start(bf16[128,2048]{1,0:T(8,128)(2,1)S(1)} %get-tuple-element.111), channel_id=1, source_target_pairs={{0,2},{1,5},{2,0},{3,7},{4,6},{5,1},{6,4},{7,3},{8,10},{9,13},{10,... | collective-permute-start | bytes 1572872 | tf_op jit(solution)/shard_map/ppermute | solution.py:26
  146.7 12.1 %collective-permute-start.32 = (bf16[128,2048]{1,0:T(8,128)(2,1)S(1)}, bf16[128,2048]{1,0:T(8,128)(2,1)S(1)}, u32[]{:S(2)}, u32[]{:S(2)}) collective-permute-start(bf16[128,2048]{1,0:T(8,128)(2,1)S(1)} %add_convert_fusion.9), channel_id=1, source_target_pairs={{0,4},{1,3},{2,6},{3,1},{4,0},{5,7},{6,2},{7,5},{8,12},{9,11},{10,... | collective-permute-start | bytes 1572872 | tf_op jit(solution)/shard_map/ppermute | solution.py:26
  149.0 11.6 %collective-permute-start.39 = (bf16[128,2048]{1,0:T(8,128)(2,1)S(1)}, bf16[128,2048]{1,0:T(8,128)(2,1)S(1)}, u32[]{:S(2)}, u32[]{:S(2)}) collective-permute-start(bf16[128,2048]{1,0:T(8,128)(2,1)S(1)} %add_convert_fusion.7), channel_id=1, source_target_pairs={{0,8},{2,10},{4,12},{6,14},{24,16},{26,18},{28,20},{30,22},{1,9},{... | collective-permute-start | bytes 1572872 | tf_op jit(solution)/shard_map/ppermute | solution.py:216
  158.5 12.1 %collective-permute-start.44 = (bf16[128,2048]{1,0:T(8,128)(2,1)S(1)}, bf16[128,2048]{1,0:T(8,128)(2,1)S(1)}, u32[]{:S(2)}, u32[]{:S(2)}) collective-permute-start(bf16[128,2048]{1,0:T(8,128)(2,1)S(1)} %add_convert_fusion.2), channel_id=1, source_target_pairs={{0,2},{1,5},{2,0},{3,7},{4,6},{5,1},{6,4},{7,3},{8,10},{9,13},{10,... | collective-permute-start | bytes 1572872 | tf_op jit(solution)/shard_map/ppermute | solution.py:26
  158.8 11.9 %collective-permute-start.33 = (bf16[128,2048]{1,0:T(8,128)(2,1)S(1)}, bf16[128,2048]{1,0:T(8,128)(2,1)S(1)}, u32[]{:S(2)}, u32[]{:S(2)}) collective-permute-start(bf16[128,2048]{1,0:T(8,128)(2,1)S(1)} %get-tuple-element.107), channel_id=1, source_target_pairs={{0,4},{1,3},{2,6},{3,1},{4,0},{5,7},{6,2},{7,5},{8,12},{9,11},{10,... | collective-permute-start | bytes 1572872 | tf_op jit(solution)/shard_map/ppermute | solution.py:26
  161.0 11.4 %collective-permute-start.41 = (bf16[128,2048]{1,0:T(8,128)(2,1)S(1)}, bf16[128,2048]{1,0:T(8,128)(2,1)S(1)}, u32[]{:S(2)}, u32[]{:S(2)}) collective-permute-start(bf16[128,2048]{1,0:T(8,128)(2,1)S(1)} %add_convert_fusion.6), channel_id=1, source_target_pairs={{0,8},{2,10},{4,12},{6,14},{24,16},{26,18},{28,20},{30,22},{1,9},{... | collective-permute-start | bytes 1572872 | tf_op jit(solution)/shard_map/ppermute | solution.py:216
  165.0 7.5 %collective-permute-start.40 = (bf16[128,2048]{1,0:T(8,128)(2,1)S(1)}, bf16[128,2048]{1,0:T(8,128)(2,1)S(1)}, u32[]{:S(2)}, u32[]{:S(2)}) collective-permute-start(bf16[128,2048]{1,0:T(8,128)(2,1)S(1)} %add_convert_fusion.6), channel_id=1, source_target_pairs={{8,16},{10,18},{12,20},{14,22},{16,8},{18,10},{20,12},{22,14},{9,1... | collective-permute-start | bytes 1572872 | tf_op jit(solution)/shard_map/ppermute | solution.py:216
  170.7 11.5 %collective-permute-start.46 = (bf16[128,2048]{1,0:T(8,128)(2,1)S(1)}, bf16[128,2048]{1,0:T(8,128)(2,1)S(1)}, u32[]{:S(2)}, u32[]{:S(2)}) collective-permute-start(bf16[128,2048]{1,0:T(8,128)(2,1)S(1)} %add_convert_fusion.1), channel_id=1, source_target_pairs={{0,4},{1,3},{2,6},{3,1},{4,0},{5,7},{6,2},{7,5},{8,12},{9,11},{10,... | collective-permute-start | bytes 1572872 | tf_op jit(solution)/shard_map/ppermute | solution.py:26
  171.7 10.5 %collective-permute-start.45 = (bf16[128,2048]{1,0:T(8,128)(2,1)S(1)}, bf16[128,2048]{1,0:T(8,128)(2,1)S(1)}, u32[]{:S(2)}, u32[]{:S(2)}) collective-permute-start(bf16[128,2048]{1,0:T(8,128)(2,1)S(1)} %add_convert_fusion.3), channel_id=1, source_target_pairs={{0,2},{1,5},{2,0},{3,7},{4,6},{5,1},{6,4},{7,3},{8,10},{9,13},{10,... | collective-permute-start | bytes 1572872 | tf_op jit(solution)/shard_map/ppermute | solution.py:26
  172.6 9.7 %collective-permute-start.43 = (bf16[128,2048]{1,0:T(8,128)(2,1)S(1)}, bf16[128,2048]{1,0:T(8,128)(2,1)S(1)}, u32[]{:S(2)}, u32[]{:S(2)}) collective-permute-start(bf16[128,2048]{1,0:T(8,128)(2,1)S(1)} %add_convert_fusion.4), channel_id=1, source_target_pairs={{8,16},{10,18},{12,20},{14,22},{16,8},{18,10},{20,12},{22,14},{9,1... | collective-permute-start | bytes 1572872 | tf_op jit(solution)/shard_map/ppermute | solution.py:216
  173.6 15.8 %collective-permute-start.42 = (bf16[128,2048]{1,0:T(8,128)(2,1)S(1)}, bf16[128,2048]{1,0:T(8,128)(2,1)S(1)}, u32[]{:S(2)}, u32[]{:S(2)}) collective-permute-start(bf16[128,2048]{1,0:T(8,128)(2,1)S(1)} %add_convert_fusion.5), channel_id=1, source_target_pairs={{0,8},{2,10},{4,12},{6,14},{8,0},{10,2},{12,4},{14,6},{16,24},{18,... | collective-permute-start | bytes 1572872 | tf_op jit(solution)/shard_map/ppermute | solution.py:20
  (9 other events, 50.6 us)

commit v11 on v10

--- a/solution.py
+++ b/solution.py
@@ -228,7 +228,7 @@
     o1, near3, x0, y0 = flip(o0, 4), shift(o0, MIDDLE), cross(o0, X), cross(o0, Y)
     weights = weights(x0, y0)
 
-    ends2, near2 = shift(after(near3, o1), OUTWARD), shift(after(o1, near3), MIDDLE)
+    ends2, near2 = shift(near3, OUTWARD), shift(o1, MIDDLE)
     d0, y1 = cross(after(y0, x0), X), cross(after(o1, y0), Y)
 
     ends3 = shift(after(near2, ends2), OUTWARD)
@@ -264,8 +264,9 @@
     to_3, to_1 = shift(after(p2, to_2), INWARD), shift(p2, MIDDLE)
     to_y0, by_y = cross(after(pd0, by_x), X), cross(after(py1, by_y), Y)
 
-    p3, p1, py0 = add_small(p3, to_3), add_small(p1, by_y, to_1), add_small(py0, to_y0)
-    by_z, by_middle = flip(after(p1, to_3), 4), shift(after(p3, to_1), MIDDLE)
+    p1, py0 = add_small(p1, by_y, to_1), add_small(py0, to_y0)
+    p3 = add_small(after(p3, p1), to_3)
+    by_z, by_middle = flip(after(p1, to_3), 4), shift(p3, MIDDLE)
     by_x, by_y = cross(after(px0, to_y0), X), cross(after(py0, by_y), Y)
     return add(stream, p0, by_z, by_middle, by_x, by_y)
 
@@ -337,12 +338,12 @@
     out_other = lax.ppermute(out_weight, "exp", SWAP)
     gate_w, up_w = jnp.swapaxes(w_gate[0], 0, 1), jnp.swapaxes(w_up[0], 0, 1)
     gate_other = lax.ppermute(gate_w, "exp", SWAP)
-    ready = (*near_keys, *near_values, some_gates[-1], ids)
+    where = jnp.stack([core, shard % 2])
+    ready = (where, *near_keys, *near_values, some_gates[-1], ids)
     up_other = lax.ppermute(after(up_w, *ready), "exp", SWAP)
     down_other = lax.ppermute(after(w_down[0], *ready), "exp", SWAP)
     halves = [gate_w, gate_other, up_w, up_other, w_down[0], down_other]
 
-    where = jnp.stack([core, shard % 2])
     theirs, mine = attention(where, queries, ids, near_keys, near_values, out_other, gate_other)
     all_gates = gather_gates(some_gates, theirs)
     received = lax.ppermute(theirs, "exp", SWAP)

time: 191 us -> 188 us (0.984)
  the two profiles are of different devices: /device:TPU:0 before, /device:TPU:10 now
where the time goes in v11:
time: 188 us
  waiting for transfers between devices  77.1 us (41%)
  starting transfers between devices  60.9 us (32%)
  Pallas kernels  37 us (20%)
  local copies, waits for them, and re-layouts  6.87 us (4%)
  other arithmetic  5.42 us (3%)
    ppermute x20, waiting for transfers between devices, cross(): return lax.ppermute(block, ('seq', 'exp'), pairs)  42.7 us
    pallas_call x5, Pallas kernels, expert(): pl.pallas_call(functools.partial(expert_kernel, places, len(gates)), out_...  25.5 us
    ppermute x8, starting transfers between devices, shift(): lax.ppermute(block, 'seq', [(4 * a + i, 4 * b + i) for a, b in pairs for...  22.4 us
    ppermute x20, starting transfers between devices, cross(): return lax.ppermute(block, ('seq', 'exp'), pairs)  21 us
    ppermute x12, waiting for transfers between devices, flip(): return lax.ppermute(block, 'seq', [(i, i ^ mask) for i in range(count)])  20.5 us
    ppermute x8, waiting for transfers between devices, shift(): lax.ppermute(block, 'seq', [(4 * a + i, 4 * b + i) for a, b in pairs for...  12.4 us
    ppermute x12, starting transfers between devices, flip(): return lax.ppermute(block, 'seq', [(i, i ^ mask) for i in range(count)])  10.4 us
    ppermute x2, starting transfers between devices, halo(): return (beside, part, lax.ppermute(beside, 'seq', ahead + back))  6.6 us
  transfers between devices with their start and end apart: 47, of which 22 were waited for; matrix products, arithmetic and copies ran while one was open for 3% of the time, Pallas kernels for 17%

profile of v11, /device:TPU:10, one launch (start us, length us, event | category | flops | bytes accessed | tf_op | source)
XLA Modules:
  0.0 187.7 jit_solution(11630924966127225390)
XLA Ops:
  0.5 1.5 collective-permute-start.2
  3.3 3.2 %collective-permute-done.7.refs_5_.refs_7_.refs_4_.refs_3_.refs_2_ = f32[16,128]{1,0:T(8,128)S(1)} collective-permute-done((f32[16,128]{1,0:T(8,128)S(1)}, f32[16,128]{1,0:T(8,128)S(1)}, u32[]{:S(2)}, u32[]{:S(2)}) %collective-permute-start.7) | collective-permute-done | bytes 8224 | tf_op jit(solution)/shard_map/ppermute | solution.py:20
  6.5 2.6 %collective-permute-start.8 = (f32[16,256]{1,0:T(8,128)S(1)}, f32[16,256]{1,0:T(8,128)S(1)}, u32[]{:S(2)}, u32[]{:S(2)}) collective-permute-start(f32[16,256]{1,0:T(8,128)S(1)} %pad_maximum_fusion.2), channel_id=1, source_target_pairs={{0,16},{2,18},{4,20},{6,22},{8,24},{10,26},{12,28},{14,30},{16,0},... | collective-permute-start | bytes 49160 | tf_op jit(solution)/shard_map/ppermute | solution.py:20
  9.3 3.3 %collective-permute-start.1 = (bf16[256,512]{1,0:T(8,128)(2,1)S(1)}, bf16[256,512]{1,0:T(8,128)(2,1)S(1)}, u32[]{:S(2)}, u32[]{:S(2)}) collective-permute-start(bf16[256,512]{1,0:T(8,128)(2,1)S(1)} %collective-permute-done.refs_0_), channel_id=1, source_target_pairs={{0,4},{4,8},{8,12},{12,16},{16,20},{20,24},{24,28},{6,2},{10,6},{1... | collective-permute-start | bytes 786440 | tf_op jit(solution)/shard_map/ppermute | solution.py:329
  12.6 1.9 %collective-permute-done.2.refs_3_ = bf16[256,512]{1,0:T(8,128)(2,1)S(1)} collective-permute-done((bf16[256,512]{1,0:T(8,128)(2,1)}, bf16[256,512]{1,0:T(8,128)(2,1)S(1)}, u32[]{:S(2)}, u32[]{:S(2)}) %collective-permute-start.2) | collective-permute-done | bytes 262176 | tf_op jit(solution)/shard_map/ppermute | solution.py:20
  14.6 3.3 %collective-permute-start.3 = (bf16[256,512]{1,0:T(8,128)(2,1)S(1)}, bf16[256,512]{1,0:T(8,128)(2,1)S(1)}, u32[]{:S(2)}, u32[]{:S(2)}) collective-permute-start(bf16[256,512]{1,0:T(8,128)(2,1)S(1)} %collective-permute-done.2.refs_3_), channel_id=1, source_target_pairs={{0,4},{4,8},{8,12},{12,16},{16,20},{20,24},{24,28},{6,2},{10,6},{1... | collective-permute-start | bytes 786440 | tf_op jit(solution)/shard_map/ppermute | solution.py:329
  20.5 4.5 %collective-permute-done.9.refs_7_.refs_9_.refs_6_.refs_5_.refs_4_ = f32[16,512]{1,0:T(8,128)S(1)} collective-permute-done((f32[16,512]{1,0:T(8,128)S(1)}, f32[16,512]{1,0:T(8,128)S(1)}, u32[]{:S(2)}, u32[]{:S(2)}) %collective-permute-start.9) | collective-permute-done | bytes 32800 | tf_op jit(solution)/shard_map/ppermute | solution.py:20
  26.4 4.6 %window_attention.1 = (bf16[128,512]{1,0:T(8,128)(2,1)}, bf16[128,512]{1,0:T(8,128)(2,1)}) custom-call(s32[2]{0:T(128)} %pad_add_fusion.where_ref, bf16[256,512]{1,0:T(8,128)(2,1)} %q_ref.1, s32[1,768]{1,0:T(1,128)} %broadcast_in_dim.21.ids_ref, bf16[256,512]{1,0:T(8,128)(2,1)} %copy-done.5, bf16[256,512]{1,0:T(8,128)(2,1)} %refs_1_.1, ...), custom_call_target="tpu_custom_call" | custom-call | tf_op jit(solution)/shard_map/window_attention/pallas_call | solution.py:97
  33.2 4.3 %project_and_norm.1 = (f32[128,2048]{1,0:T(8,128)}, bf16[128,2048]{1,0:T(8,128)(2,1)}) custom-call(bf16[128,512]{1,0:T(8,128)(2,1)} %get-tuple-element.64.mine_ref, bf16[128,512]{1,0:T(8,128)(2,1)} %copy-done.9, bf16[512,2048]{1,0:T(8,128)(2,1)} %own_w.1, bf16[512,2048]{1,0:T(8,128)(2,1)} %collective-permute-done.4.refs_6_.other_w, ...), custom_call_target="tpu_custom_call" | custom-call | tf_op jit(solution)/shard_map/project_and_norm/pallas_call | solution.py:120
  37.9 4.6 %collective-permute-start.14 = (bf16[128,2048]{1,0:T(8,128)(2,1)}, bf16[128,2048]{1,0:T(8,128)(2,1)S(1)}, u32[]{:S(2)}, u32[]{:S(2)}) collective-permute-start(bf16[128,2048]{1,0:T(8,128)(2,1)} %get-tuple-element.70.refs_0_), channel_id=1, source_target_pairs={{8,16},{10,18},{12,20},{14,22},{16,8},{18,10},{20,12},{22,14},{9,1... | collective-permute-start | bytes 1572872 | tf_op jit(solution)/shard_map/ppermute | solution.py:216
  44.6 7.0 %collective-permute-done.12.refs_0_ = bf16[128,2048]{1,0:T(8,128)(2,1)S(1)} collective-permute-done((bf16[128,2048]{1,0:T(8,128)(2,1)}, bf16[128,2048]{1,0:T(8,128)(2,1)S(1)}, u32[]{:S(2)}, u32[]{:S(2)}) %collective-permute-start.12) | collective-permute-done | bytes 524320 | tf_op jit(solution)/shard_map/ppermute | solution.py:20
  51.6 3.5 %collective-permute-start.13 = (bf16[128,2048]{1,0:T(8,128)(2,1)S(1)}, bf16[128,2048]{1,0:T(8,128)(2,1)}, u32[]{:S(2)}, u32[]{:S(2)}) collective-permute-start(bf16[128,2048]{1,0:T(8,128)(2,1)S(1)} %collective-permute-done.12.refs_0_), channel_id=1, source_target_pairs={{8,16},{10,18},{12,20},{14,22},{16,8},{18,10},{20,12},{22,14},{9,1... | collective-permute-start | bytes 1572872 | tf_op jit(solution)/shard_map/ppermute | solution.py:216
  55.1 2.1 %collective-permute-start.15 = (bf16[128,2048]{1,0:T(8,128)(2,1)S(1)}, bf16[128,2048]{1,0:T(8,128)(2,1)}, u32[]{:S(2)}, u32[]{:S(2)}) collective-permute-start(bf16[128,2048]{1,0:T(8,128)(2,1)S(1)} %collective-permute-done.14), channel_id=1, source_target_pairs={{8,0},{10,2},{12,4},{14,6},{16,24},{18,26},{20,28},{22,30},{9,1},{... | collective-permute-start | bytes 1572872 | tf_op jit(solution)/shard_map/ppermute | solution.py:216
  57.4 1.3 collective-permute-start.18
  59.7 2.0 %collective-permute-start.19 = (f32[16,1024]{1,0:T(8,128)S(1)}, f32[16,1024]{1,0:T(8,128)S(1)}, u32[]{:S(2)}, u32[]{:S(2)}) collective-permute-start(f32[16,1024]{1,0:T(8,128)S(1)} %pad_maximum_fusion), channel_id=1, source_target_pairs={{0,2},{2,0},{4,6},{6,4},{8,10},{10,8},{12,14},{14,12},{16,18},{18,... | collective-permute-start | bytes 196616 | tf_op jit(solution)/shard_map/ppermute | solution.py:20
  61.7 1.4 copy-done
  63.1 1.4 copy-done.1
  64.4 1.4 copy-done.2
  65.8 2.6 %assemble_weights.1 = (bf16[1408,2048]{1,0:T(8,128)(2,1)S(1)}, bf16[704,2048]{1,0:T(8,128)(2,1)S(1)}) custom-call(bf16[352,2048]{1,0:T(8,128)(2,1)S(1)} %bitcast.14, bf16[352,2048]{1,0:T(8,128)(2,1)} %collective-permute-done.5.refs_7_.refs_1_, bf16[352,2048]{1,0:T(8,128)(2,1)S(1)} %bitcast.16, bf16[352,2048]{1,0:T(8,128)(2,1)} %collective-permute-done.10.refs_0_.refs_3_, ...), custom_call_target="tpu_custom_call" | custom-call | tf_op jit(solution)/shard_map/assemble_weights/pallas_call | solution.py:148
  68.5 3.3 %collective-permute-start.23 = (bf16[128,2048]{1,0:T(8,128)(2,1)}, bf16[128,2048]{1,0:T(8,128)(2,1)S(1)}, u32[]{:S(2)}, u32[]{:S(2)}) collective-permute-start(bf16[128,2048]{1,0:T(8,128)(2,1)} %collective-permute-done.13), channel_id=1, source_target_pairs={{8,0},{10,2},{12,4},{14,6},{16,24},{18,26},{20,28},{22,30},{9,1},{... | collective-permute-start | bytes 1572872 | tf_op jit(solution)/shard_map/ppermute | solution.py:216
  72.9 1.5 collective-permute-start.21
  75.6 5.6 %expert_rows.5 = (bf16[128,2048]{1,0:T(8,128)(2,1)S(1)}, bf16[128,2048]{1,0:T(8,128)(2,1)S(1)}, bf16[128,2048]{1,0:T(8,128)(2,1)S(1)}, bf16[128,2048]{1,0:T(8,128)(2,1)S(1)}) custom-call(s32[2]{0:T(128)S(1)} %pad_add_fusion.1.where_ref, bf16[128,2048]{1,0:T(8,128)(2,1)S(1)} %copy-done.3, bf16[128,2048]{1,0:T(8,128)(2,1)S(1)} %collective-permute-done.16.refs_1_, ...), custom_call_target="tpu_custom_call" | custom-call | tf_op jit(solution)/shard_map/expert_rows/pallas_call | solution.py:194
  81.7 5.4 %collective-permute-done.21.refs_3_ = bf16[128,2048]{1,0:T(8,128)(2,1)S(1)} collective-permute-done((bf16[128,2048]{1,0:T(8,128)(2,1)S(1)}, bf16[128,2048]{1,0:T(8,128)(2,1)S(1)}, u32[]{:S(2)}, u32[]{:S(2)}) %collective-permute-start.21) | collective-permute-done | bytes 524320 | tf_op jit(solution)/shard_map/ppermute | solution.py:26
  88.1 8.1 %expert_rows.6 = (bf16[128,2048]{1,0:T(8,128)(2,1)S(1)}, bf16[128,2048]{1,0:T(8,128)(2,1)S(1)}, bf16[128,2048]{1,0:T(8,128)(2,1)S(1)}, bf16[128,2048]{1,0:T(8,12...) custom-call(s32[2]{0:T(128)S(1)} %pad_add_fusion.1.where_ref, ...), custom_call_target="tpu_custom_call" | custom-call | tf_op jit(solution)/shard_map/expert_rows/pallas_call | solution.py:194
  96.2 4.1 %collective-permute-done.24.refs_0_ = bf16[128,2048]{1,0:T(8,128)(2,1)S(1)} collective-permute-done((bf16[128,2048]{1,0:T(8,128)(2,1)S(1)}, bf16[128,2048]{1,0:T(8,128)(2,1)S(1)}, u32[]{:S(2)}, u32[]{:S(2)}) %collective-permute-start.24) | collective-permute-done | bytes 524320 | tf_op jit(solution)/shard_map/ppermute | solution.py:26
  101.4 5.6 %expert_rows.7 = (bf16[128,2048]{1,0:T(8,128)(2,1)S(1)}, bf16[128,2048]{1,0:T(8,128)(2,1)S(1)}, bf16[128,2048]{1,0:T(8,128)(2,1)S(1)}) custom-call(s32[2]{0:T(128)S(1)} %pad_add_fusion.1.where_ref, bf16[128,2048]{1,0:T(8,128)(2,1)S(1)} %collective-permute-done.24.refs_0_, bf16[128,2048]{1,0:T(8,128)(2,1)S(1)} %collective-permute-done.26.refs_1_, ...), custom_call_target="tpu_custom_call" | custom-call | tf_op jit(solution)/shard_map/expert_rows/pallas_call | solution.py:194
  107.0 5.7 %collective-permute-done.25.refs_0_ = bf16[128,2048]{1,0:T(8,128)(2,1)S(1)} collective-permute-done((bf16[128,2048]{1,0:T(8,128)(2,1)S(1)}, bf16[128,2048]{1,0:T(8,128)(2,1)S(1)}, u32[]{:S(2)}, u32[]{:S(2)}) %collective-permute-start.25) | collective-permute-done | bytes 524320 | tf_op jit(solution)/shard_map/ppermute | solution.py:26
  112.7 3.2 %expert_rows.8 = (bf16[128,2048]{1,0:T(8,128)(2,1)S(1)}, bf16[128,2048]{1,0:T(8,128)(2,1)S(1)}) custom-call(s32[2]{0:T(128)S(1)} %pad_add_fusion.1.where_ref, bf16[128,2048]{1,0:T(8,128)(2,1)S(1)} %collective-permute-done.25.refs_0_, bf16[128,2048]{1,0:T(8,128)(2,1)S(1)} %collective-permute-done.28.refs_1_, ...), custom_call_target="tpu_custom_call" | custom-call | tf_op jit(solution)/shard_map/expert_rows/pallas_call | solution.py:194
  116.3 2.9 %expert_rows.9 = bf16[128,2048]{1,0:T(8,128)(2,1)S(1)} custom-call(s32[2]{0:T(128)S(1)} %pad_add_fusion.1.where_ref, bf16[128,2048]{1,0:T(8,128)(2,1)S(1)} %collective-permute-done.36.refs_0_, f32[16,128]{1,0:T(8,128)S(1)} %select_reduce_fusion.refs_4_.refs_6_.refs_3_.refs_2_.refs_1_, ...), custom_call_target="tpu_custom_call" | custom-call | tf_op jit(solution)/shard_map/expert_rows/pallas_call | solution.py:194
  120.1 8.0 %collective-permute-done.30 = bf16[128,2048]{1,0:T(8,128)(2,1)S(1)} collective-permute-done((bf16[128,2048]{1,0:T(8,128)(2,1)S(1)}, bf16[128,2048]{1,0:T(8,128)(2,1)S(1)}, u32[]{:S(2)}, u32[]{:S(2)}) %collective-permute-start.30) | collective-permute-done | bytes 524320 | tf_op jit(solution)/shard_map/ppermute | solution.py:26
  129.6 1.4 collective-permute-done.37
  131.8 7.9 %collective-permute-done.34 = bf16[128,2048]{1,0:T(8,128)(2,1)S(1)} collective-permute-done((bf16[128,2048]{1,0:T(8,128)(2,1)S(1)}, bf16[128,2048]{1,0:T(8,128)(2,1)S(1)}, u32[]{:S(2)}, u32[]{:S(2)}) %collective-permute-start.34) | collective-permute-done | bytes 524320 | tf_op jit(solution)/shard_map/ppermute | solution.py:26
  139.7 1.7 collective-permute-start.35
  141.4 1.4 collective-permute-start.32
  143.1 1.3 collective-permute-start.39
  144.6 7.2 %collective-permute-done.35 = bf16[128,2048]{1,0:T(8,128)(2,1)S(1)} collective-permute-done((bf16[128,2048]{1,0:T(8,128)(2,1)S(1)}, bf16[128,2048]{1,0:T(8,128)(2,1)S(1)}, u32[]{:S(2)}, u32[]{:S(2)}) %collective-permute-start.35) | collective-permute-done | bytes 524320 | tf_op jit(solution)/shard_map/ppermute | solution.py:26
  151.8 1.7 collective-permute-start.44
  154.3 2.5 %collective-permute-start.33 = (bf16[128,2048]{1,0:T(8,128)(2,1)S(1)}, bf16[128,2048]{1,0:T(8,128)(2,1)S(1)}, u32[]{:S(2)}, u32[]{:S(2)}) collective-permute-start(bf16[128,2048]{1,0:T(8,128)(2,1)S(1)} %get-tuple-element.103), channel_id=1, source_target_pairs={{0,4},{1,3},{2,6},{3,1},{4,0},{5,7},{6,2},{7,5},{8,12},{9,11},{10,... | collective-permute-start | bytes 1572872 | tf_op jit(solution)/shard_map/ppermute | solution.py:26
  157.1 1.9 %collective-permute-start.40 = (bf16[128,2048]{1,0:T(8,128)(2,1)S(1)}, bf16[128,2048]{1,0:T(8,128)(2,1)S(1)}, u32[]{:S(2)}, u32[]{:S(2)}) collective-permute-start(bf16[128,2048]{1,0:T(8,128)(2,1)S(1)} %add_convert_fusion.6), channel_id=1, source_target_pairs={{8,16},{10,18},{12,20},{14,22},{16,8},{18,10},{20,12},{22,14},{9,1... | collective-permute-start | bytes 1572872 | tf_op jit(solution)/shard_map/ppermute | solution.py:216
  159.2 1.3 collective-permute-start.41
  160.5 3.4 %collective-permute-done.44 = bf16[128,2048]{1,0:T(8,128)(2,1)S(1)} collective-permute-done((bf16[128,2048]{1,0:T(8,128)(2,1)S(1)}, bf16[128,2048]{1,0:T(8,128)(2,1)S(1)}, u32[]{:S(2)}, u32[]{:S(2)}) %collective-permute-start.44) | collective-permute-done | bytes 524320 | tf_op jit(solution)/shard_map/ppermute | solution.py:26
  164.1 2.3 %collective-permute-start.46 = (bf16[128,2048]{1,0:T(8,128)(2,1)S(1)}, bf16[128,2048]{1,0:T(8,128)(2,1)S(1)}, u32[]{:S(2)}, u32[]{:S(2)}) collective-permute-start(bf16[128,2048]{1,0:T(8,128)(2,1)S(1)} %add_convert_fusion.1), channel_id=1, source_target_pairs={{0,4},{1,3},{2,6},{3,1},{4,0},{5,7},{6,2},{7,5},{8,12},{9,11},{10,... | collective-permute-start | bytes 1572872 | tf_op jit(solution)/shard_map/ppermute | solution.py:26
  167.5 1.4 collective-permute-done.40
  169.1 3.6 %collective-permute-done.41 = bf16[128,2048]{1,0:T(8,128)(2,1)S(1)} collective-permute-done((bf16[128,2048]{1,0:T(8,128)(2,1)S(1)}, bf16[128,2048]{1,0:T(8,128)(2,1)S(1)}, u32[]{:S(2)}, u32[]{:S(2)}) %collective-permute-start.41) | collective-permute-done | bytes 524320 | tf_op jit(solution)/shard_map/ppermute | solution.py:216
  172.8 4.4 %collective-permute-start.43 = (bf16[128,2048]{1,0:T(8,128)(2,1)S(1)}, bf16[128,2048]{1,0:T(8,128)(2,1)S(1)}, u32[]{:S(2)}, u32[]{:S(2)}) collective-permute-start(bf16[128,2048]{1,0:T(8,128)(2,1)S(1)} %add_convert_fusion.4), channel_id=1, source_target_pairs={{8,16},{10,18},{12,20},{14,22},{16,8},{18,10},{20,12},{22,14},{9,1... | collective-permute-start | bytes 1572872 | tf_op jit(solution)/shard_map/ppermute | solution.py:216
  177.3 7.0 %collective-permute-done.43 = bf16[128,2048]{1,0:T(8,128)(2,1)S(1)} collective-permute-done((bf16[128,2048]{1,0:T(8,128)(2,1)S(1)}, bf16[128,2048]{1,0:T(8,128)(2,1)S(1)}, u32[]{:S(2)}, u32[]{:S(2)}) %collective-permute-start.43) | collective-permute-done | bytes 524320 | tf_op jit(solution)/shard_map/ppermute | solution.py:216
  184.3 2.1 %collective-permute-done.42 = bf16[128,2048]{1,0:T(8,128)(2,1)S(1)} collective-permute-done((bf16[128,2048]{1,0:T(8,128)(2,1)S(1)}, bf16[128,2048]{1,0:T(8,128)(2,1)S(1)}, u32[]{:S(2)}, u32[]{:S(2)}) %collective-permute-start.42) | collective-permute-done | bytes 524320 | tf_op jit(solution)/shard_map/ppermute | solution.py:20
  186.4 1.2 add_convert_fusion
  (94 shorter events, 23.5 us)
Async XLA Ops:
  0.0 26.3 %collective-permute-start.4 = (bf16[512,2048]{1,0:T(8,128)(2,1)}, bf16[512,2048]{1,0:T(8,128)(2,1)}, u32[]{:S(2)}, u32[]{:S(2)}) collective-permute-start(bf16[512,2048]{1,0:T(8,128)(2,1)} %own_w.1), channel_id=1, source_target_pairs={{0,1},{1,0},{2,3},{3,2},{4,5},{5,4},{6,7},{7,6},{8,9},{9,8},{10,11... | collective-permute-start | bytes 6291464 | tf_op jit(solution)/shard_map/ppermute | solution.py:338
  0.0 9.3 %collective-permute-start = (bf16[256,512]{1,0:T(8,128)(2,1)}, bf16[256,512]{1,0:T(8,128)(2,1)S(1)}, u32[]{:S(2)}, u32[]{:S(2)}) collective-permute-start(bf16[256,512]{1,0:T(8,128)(2,1)} %refs_1_.1), channel_id=1, source_target_pairs={{0,2},{2,0},{4,6},{6,4},{8,10},{10,8},{12,14},{14,12},{16,18},{18,... | collective-permute-start | bytes 786440 | tf_op jit(solution)/shard_map/ppermute | solution.py:20
  0.5 14.0 %collective-permute-start.2 = (bf16[256,512]{1,0:T(8,128)(2,1)}, bf16[256,512]{1,0:T(8,128)(2,1)S(1)}, u32[]{:S(2)}, u32[]{:S(2)}) collective-permute-start(bf16[256,512]{1,0:T(8,128)(2,1)} %refs_4_.1), channel_id=1, source_target_pairs={{0,2},{2,0},{4,6},{6,4},{8,10},{10,8},{12,14},{14,12},{16,18},{18,... | collective-permute-start | bytes 786440 | tf_op jit(solution)/shard_map/ppermute | solution.py:20
  2.7 3.7 %collective-permute-start.7 = (f32[16,128]{1,0:T(8,128)S(1)}, f32[16,128]{1,0:T(8,128)S(1)}, u32[]{:S(2)}, u32[]{:S(2)}) collective-permute-start(f32[16,128]{1,0:T(8,128)S(1)} %select_reduce_fusion.refs_4_.refs_6_.refs_3_.refs_2_.refs_1_), channel_id=1, source_target_pairs={{0,8},{2,10},{4,12},{6,14},{8,0},{10,2},{12,4},{14,6},{16,24},{18,... | collective-permute-start | bytes 24584 | tf_op jit(solution)/shard_map/ppermute | solution.py:20
  3.3 23.1 %collective-permute-start.5 = (bf16[352,2048]{1,0:T(8,128)(2,1)}, bf16[352,2048]{1,0:T(8,128)(2,1)}, u32[]{:S(2)}, u32[]{:S(2)}) collective-permute-start(bf16[352,2048]{1,0:T(8,128)(2,1)} %bitcast.13), channel_id=1, source_target_pairs={{0,1},{1,0},{2,3},{3,2},{4,5},{5,4},{6,7},{7,6},{8,9},{9,8},{10,11... | collective-permute-start | bytes 4325384 | tf_op jit(solution)/shard_map/ppermute | solution.py:340
  6.5 12.2 %collective-permute-start.8 = (f32[16,256]{1,0:T(8,128)S(1)}, f32[16,256]{1,0:T(8,128)S(1)}, u32[]{:S(2)}, u32[]{:S(2)}) collective-permute-start(f32[16,256]{1,0:T(8,128)S(1)} %pad_maximum_fusion.2), channel_id=1, source_target_pairs={{0,16},{2,18},{4,20},{6,22},{8,24},{10,26},{12,28},{14,30},{16,0},... | collective-permute-start | bytes 49160 | tf_op jit(solution)/shard_map/ppermute | solution.py:20
  9.3 15.8 %collective-permute-start.1 = (bf16[256,512]{1,0:T(8,128)(2,1)S(1)}, bf16[256,512]{1,0:T(8,128)(2,1)S(1)}, u32[]{:S(2)}, u32[]{:S(2)}) collective-permute-start(bf16[256,512]{1,0:T(8,128)(2,1)S(1)} %collective-permute-done.refs_0_), channel_id=1, source_target_pairs={{0,4},{4,8},{8,12},{12,16},{16,20},{20,24},{24,28},{6,2},{10,6},{1... | collective-permute-start | bytes 786440 | tf_op jit(solution)/shard_map/ppermute | solution.py:329
  14.6 10.5 %collective-permute-start.3 = (bf16[256,512]{1,0:T(8,128)(2,1)S(1)}, bf16[256,512]{1,0:T(8,128)(2,1)S(1)}, u32[]{:S(2)}, u32[]{:S(2)}) collective-permute-start(bf16[256,512]{1,0:T(8,128)(2,1)S(1)} %collective-permute-done.2.refs_3_), channel_id=1, source_target_pairs={{0,4},{4,8},{8,12},{12,16},{16,20},{20,24},{24,28},{6,2},{10,6},{1... | collective-permute-start | bytes 786440 | tf_op jit(solution)/shard_map/ppermute | solution.py:329
  18.7 6.4 %collective-permute-start.9 = (f32[16,512]{1,0:T(8,128)S(1)}, f32[16,512]{1,0:T(8,128)S(1)}, u32[]{:S(2)}, u32[]{:S(2)}) collective-permute-start(f32[16,512]{1,0:T(8,128)S(1)} %pad_maximum_fusion.1), channel_id=1, source_target_pairs={{0,4},{2,6},{4,0},{6,2},{8,12},{10,14},{12,8},{14,10},{16,20},{18,... | collective-permute-start | bytes 98312 | tf_op jit(solution)/shard_map/ppermute | solution.py:20
  25.8 5.1 %collective-permute-start.10 = (bf16[352,2048]{1,0:T(8,128)(2,1)}, bf16[352,2048]{1,0:T(8,128)(2,1)}, u32[]{:S(2)}, u32[]{:S(2)}) collective-permute-start(bf16[352,2048]{1,0:T(8,128)(2,1)} %bitcast.15), channel_id=1, source_target_pairs={{0,1},{1,0},{2,3},{3,2},{4,5},{5,4},{6,7},{7,6},{8,9},{9,8},{10,11... | collective-permute-start | bytes 4325384 | tf_op jit(solution)/shard_map/ppermute | solution.py:343
  25.8 5.6 %collective-permute-start.11 = (bf16[352,2048]{1,0:T(8,128)(2,1)}, bf16[352,2048]{1,0:T(8,128)(2,1)}, u32[]{:S(2)}, u32[]{:S(2)}) collective-permute-start(bf16[352,2048]{1,0:T(8,128)(2,1)} %bitcast.17), channel_id=1, source_target_pairs={{0,1},{1,0},{2,3},{3,2},{4,5},{5,4},{6,7},{7,6},{8,9},{9,8},{10,11... | collective-permute-start | bytes 4325384 | tf_op jit(solution)/shard_map/ppermute | solution.py:344
  30.9 1.6 collective-permute-start.6
  37.5 14.2 %collective-permute-start.12 = (bf16[128,2048]{1,0:T(8,128)(2,1)}, bf16[128,2048]{1,0:T(8,128)(2,1)S(1)}, u32[]{:S(2)}, u32[]{:S(2)}) collective-permute-start(bf16[128,2048]{1,0:T(8,128)(2,1)} %get-tuple-element.70.refs_0_), channel_id=1, source_target_pairs={{0,8},{2,10},{4,12},{6,14},{8,0},{10,2},{12,4},{14,6},{16,24},{18,... | collective-permute-start | bytes 1572872 | tf_op jit(solution)/shard_map/ppermute | solution.py:20
  37.9 17.2 %collective-permute-start.14 = (bf16[128,2048]{1,0:T(8,128)(2,1)}, bf16[128,2048]{1,0:T(8,128)(2,1)S(1)}, u32[]{:S(2)}, u32[]{:S(2)}) collective-permute-start(bf16[128,2048]{1,0:T(8,128)(2,1)} %get-tuple-element.70.refs_0_), channel_id=1, source_target_pairs={{8,16},{10,18},{12,20},{14,22},{16,8},{18,10},{20,12},{22,14},{9,1... | collective-permute-start | bytes 1572872 | tf_op jit(solution)/shard_map/ppermute | solution.py:216
  42.5 14.8 %collective-permute-start.17 = (bf16[128,2048]{1,0:T(8,128)(2,1)}, bf16[128,2048]{1,0:T(8,128)(2,1)S(1)}, u32[]{:S(2)}, u32[]{:S(2)}) collective-permute-start(bf16[128,2048]{1,0:T(8,128)(2,1)} %get-tuple-element.70.refs_0_), channel_id=1, source_target_pairs={{0,4},{1,3},{2,6},{3,1},{4,0},{5,7},{6,2},{7,5},{8,12},{9,11},{10,... | collective-permute-start | bytes 1572872 | tf_op jit(solution)/shard_map/ppermute | solution.py:26
  43.4 13.9 %collective-permute-start.16 = (bf16[128,2048]{1,0:T(8,128)(2,1)}, bf16[128,2048]{1,0:T(8,128)(2,1)S(1)}, u32[]{:S(2)}, u32[]{:S(2)}) collective-permute-start(bf16[128,2048]{1,0:T(8,128)(2,1)} %get-tuple-element.70.refs_0_), channel_id=1, source_target_pairs={{0,2},{1,5},{2,0},{3,7},{4,6},{5,1},{6,4},{7,3},{8,10},{9,13},{10,... | collective-permute-start | bytes 1572872 | tf_op jit(solution)/shard_map/ppermute | solution.py:26
  51.6 16.8 %collective-permute-start.13 = (bf16[128,2048]{1,0:T(8,128)(2,1)S(1)}, bf16[128,2048]{1,0:T(8,128)(2,1)}, u32[]{:S(2)}, u32[]{:S(2)}) collective-permute-start(bf16[128,2048]{1,0:T(8,128)(2,1)S(1)} %collective-permute-done.12.refs_0_), channel_id=1, source_target_pairs={{8,16},{10,18},{12,20},{14,22},{16,8},{18,10},{20,12},{22,14},{9,1... | collective-permute-start | bytes 1572872 | tf_op jit(solution)/shard_map/ppermute | solution.py:216
  55.1 13.3 %collective-permute-start.15 = (bf16[128,2048]{1,0:T(8,128)(2,1)S(1)}, bf16[128,2048]{1,0:T(8,128)(2,1)}, u32[]{:S(2)}, u32[]{:S(2)}) collective-permute-start(bf16[128,2048]{1,0:T(8,128)(2,1)S(1)} %collective-permute-done.14), channel_id=1, source_target_pairs={{8,0},{10,2},{12,4},{14,6},{16,24},{18,26},{20,28},{22,30},{9,1},{... | collective-permute-start | bytes 1572872 | tf_op jit(solution)/shard_map/ppermute | solution.py:216
  57.4 15.5 %collective-permute-start.18 = (bf16[128,2048]{1,0:T(8,128)(2,1)S(1)}, bf16[128,2048]{1,0:T(8,128)(2,1)S(1)}, u32[]{:S(2)}, u32[]{:S(2)}) collective-permute-start(bf16[128,2048]{1,0:T(8,128)(2,1)S(1)} %collective-permute-done.17.refs_2_), channel_id=1, source_target_pairs={{0,2},{1,5},{2,0},{3,7},{4,6},{5,1},{6,4},{7,3},{8,10},{9,13},{10,... | collective-permute-start | bytes 1572872 | tf_op jit(solution)/shard_map/ppermute | solution.py:26
  58.7 15.7 %collective-permute-start.20 = (bf16[128,2048]{1,0:T(8,128)(2,1)S(1)}, bf16[128,2048]{1,0:T(8,128)(2,1)S(1)}, u32[]{:S(2)}, u32[]{:S(2)}) collective-permute-start(bf16[128,2048]{1,0:T(8,128)(2,1)S(1)} %collective-permute-done.12.refs_0_), channel_id=1, source_target_pairs={{0,4},{1,3},{2,6},{3,1},{4,0},{5,7},{6,2},{7,5},{8,12},{9,11},{10,... | collective-permute-start | bytes 1572872 | tf_op jit(solution)/shard_map/ppermute | solution.py:26
  59.7 15.8 %collective-permute-start.19 = (f32[16,1024]{1,0:T(8,128)S(1)}, f32[16,1024]{1,0:T(8,128)S(1)}, u32[]{:S(2)}, u32[]{:S(2)}) collective-permute-start(f32[16,1024]{1,0:T(8,128)S(1)} %pad_maximum_fusion), channel_id=1, source_target_pairs={{0,2},{2,0},{4,6},{6,4},{8,10},{10,8},{12,14},{14,12},{16,18},{18,... | collective-permute-start | bytes 196616 | tf_op jit(solution)/shard_map/ppermute | solution.py:20
  68.5 13.1 %collective-permute-start.23 = (bf16[128,2048]{1,0:T(8,128)(2,1)}, bf16[128,2048]{1,0:T(8,128)(2,1)S(1)}, u32[]{:S(2)}, u32[]{:S(2)}) collective-permute-start(bf16[128,2048]{1,0:T(8,128)(2,1)} %collective-permute-done.13), channel_id=1, source_target_pairs={{8,0},{10,2},{12,4},{14,6},{16,24},{18,26},{20,28},{22,30},{9,1},{... | collective-permute-start | bytes 1572872 | tf_op jit(solution)/shard_map/ppermute | solution.py:216
  72.9 14.2 %collective-permute-start.21 = (bf16[128,2048]{1,0:T(8,128)(2,1)S(1)}, bf16[128,2048]{1,0:T(8,128)(2,1)S(1)}, u32[]{:S(2)}, u32[]{:S(2)}) collective-permute-start(bf16[128,2048]{1,0:T(8,128)(2,1)S(1)} %broadcast_select_fusion.1.refs_2_), channel_id=1, source_target_pairs={{0,2},{1,5},{2,0},{3,7},{4,6},{5,1},{6,4},{7,3},{8,10},{9,13},{10,... | collective-permute-start | bytes 1572872 | tf_op jit(solution)/shard_map/ppermute | solution.py:26
  74.4 12.9 %collective-permute-start.22 = (bf16[128,2048]{1,0:T(8,128)(2,1)S(1)}, bf16[128,2048]{1,0:T(8,128)(2,1)S(1)}, u32[]{:S(2)}, u32[]{:S(2)}) collective-permute-start(bf16[128,2048]{1,0:T(8,128)(2,1)S(1)} %broadcast_select_fusion.1.refs_2_), channel_id=1, source_target_pairs={{0,4},{1,3},{2,6},{3,1},{4,0},{5,7},{6,2},{7,5},{8,12},{9,11},{10,... | collective-permute-start | bytes 1572872 | tf_op jit(solution)/shard_map/ppermute | solution.py:26
  87.1 13.3 %collective-permute-start.24 = (bf16[128,2048]{1,0:T(8,128)(2,1)S(1)}, bf16[128,2048]{1,0:T(8,128)(2,1)S(1)}, u32[]{:S(2)}, u32[]{:S(2)}) collective-permute-start(bf16[128,2048]{1,0:T(8,128)(2,1)S(1)} %broadcast_select_fusion.refs_5_), channel_id=1, source_target_pairs={{0,2},{1,5},{2,0},{3,7},{4,6},{5,1},{6,4},{7,3},{8,10},{9,13},{10,... | collective-permute-start | bytes 1572872 | tf_op jit(solution)/shard_map/ppermute | solution.py:26
  87.4 13.3 %collective-permute-start.26 = (bf16[128,2048]{1,0:T(8,128)(2,1)S(1)}, bf16[128,2048]{1,0:T(8,128)(2,1)S(1)}, u32[]{:S(2)}, u32[]{:S(2)}) collective-permute-start(bf16[128,2048]{1,0:T(8,128)(2,1)S(1)} %broadcast_select_fusion.refs_5_), channel_id=1, source_target_pairs={{0,4},{1,3},{2,6},{3,1},{4,0},{5,7},{6,2},{7,5},{8,12},{9,11},{10,... | collective-permute-start | bytes 1572872 | tf_op jit(solution)/shard_map/ppermute | solution.py:26
  88.1 12.5 %collective-permute-start.27 = (bf16[128,2048]{1,0:T(8,128)(2,1)S(1)}, bf16[128,2048]{1,0:T(8,128)(2,1)S(1)}, u32[]{:S(2)}, u32[]{:S(2)}) collective-permute-start(bf16[128,2048]{1,0:T(8,128)(2,1)S(1)} %collective-permute-done.16.refs_1_), channel_id=1, source_target_pairs={{0,8},{2,10},{4,12},{6,14},{8,0},{10,2},{12,4},{14,6},{16,24},{18,... | collective-permute-start | bytes 1572872 | tf_op jit(solution)/shard_map/ppermute | solution.py:20
  100.3 12.4 %collective-permute-start.25 = (bf16[128,2048]{1,0:T(8,128)(2,1)S(1)}, bf16[128,2048]{1,0:T(8,128)(2,1)S(1)}, u32[]{:S(2)}, u32[]{:S(2)}) collective-permute-start(bf16[128,2048]{1,0:T(8,128)(2,1)S(1)} %collective-permute-done.22.refs_4_), channel_id=1, source_target_pairs={{0,2},{1,5},{2,0},{3,7},{4,6},{5,1},{6,4},{7,3},{8,10},{9,13},{10,... | collective-permute-start | bytes 1572872 | tf_op jit(solution)/shard_map/ppermute | solution.py:26
  100.6 12.1 %collective-permute-start.28 = (bf16[128,2048]{1,0:T(8,128)(2,1)S(1)}, bf16[128,2048]{1,0:T(8,128)(2,1)S(1)}, u32[]{:S(2)}, u32[]{:S(2)}) collective-permute-start(bf16[128,2048]{1,0:T(8,128)(2,1)S(1)} %collective-permute-done.24.refs_0_), channel_id=1, source_target_pairs={{0,4},{1,3},{2,6},{3,1},{4,0},{5,7},{6,2},{7,5},{8,12},{9,11},{10,... | collective-permute-start | bytes 1572872 | tf_op jit(solution)/shard_map/ppermute | solution.py:26
  100.6 15.7 %collective-permute-start.36 = (bf16[128,2048]{1,0:T(8,128)(2,1)S(1)}, bf16[128,2048]{1,0:T(8,128)(2,1)S(1)}, u32[]{:S(2)}, u32[]{:S(2)}) collective-permute-start(bf16[128,2048]{1,0:T(8,128)(2,1)S(1)} %collective-permute-done.18.refs_3_), channel_id=1, source_target_pairs={{0,8},{2,10},{4,12},{6,14},{8,0},{10,2},{12,4},{14,6},{16,24},{18,... | collective-permute-start | bytes 1572872 | tf_op jit(solution)/shard_map/ppermute | solution.py:20
  115.9 12.2 %collective-permute-start.30 = (bf16[128,2048]{1,0:T(8,128)(2,1)S(1)}, bf16[128,2048]{1,0:T(8,128)(2,1)S(1)}, u32[]{:S(2)}, u32[]{:S(2)}) collective-permute-start(bf16[128,2048]{1,0:T(8,128)(2,1)S(1)} %get-tuple-element.100), channel_id=1, source_target_pairs={{0,4},{1,3},{2,6},{3,1},{4,0},{5,7},{6,2},{7,5},{8,12},{9,11},{10,... | collective-permute-start | bytes 1572872 | tf_op jit(solution)/shard_map/ppermute | solution.py:26
  116.0 12.2 %collective-permute-start.29 = (bf16[128,2048]{1,0:T(8,128)(2,1)S(1)}, bf16[128,2048]{1,0:T(8,128)(2,1)S(1)}, u32[]{:S(2)}, u32[]{:S(2)}) collective-permute-start(bf16[128,2048]{1,0:T(8,128)(2,1)S(1)} %get-tuple-element.98), channel_id=1, source_target_pairs={{0,2},{1,5},{2,0},{3,7},{4,6},{5,1},{6,4},{7,3},{8,10},{9,13},{10,... | collective-permute-start | bytes 1572872 | tf_op jit(solution)/shard_map/ppermute | solution.py:26
  119.3 11.8 %collective-permute-start.37 = (bf16[128,2048]{1,0:T(8,128)(2,1)S(1)}, bf16[128,2048]{1,0:T(8,128)(2,1)S(1)}, u32[]{:S(2)}, u32[]{:S(2)}) collective-permute-start(bf16[128,2048]{1,0:T(8,128)(2,1)S(1)} %expert_rows.9), channel_id=1, source_target_pairs={{0,8},{2,10},{4,12},{6,14},{8,0},{10,2},{12,4},{14,6},{16,24},{18,... | collective-permute-start | bytes 1572872 | tf_op jit(solution)/shard_map/ppermute | solution.py:20
  128.2 11.5 %collective-permute-start.34 = (bf16[128,2048]{1,0:T(8,128)(2,1)S(1)}, bf16[128,2048]{1,0:T(8,128)(2,1)S(1)}, u32[]{:S(2)}, u32[]{:S(2)}) collective-permute-start(bf16[128,2048]{1,0:T(8,128)(2,1)S(1)} %add_convert_fusion.8), channel_id=1, source_target_pairs={{0,2},{1,5},{2,0},{3,7},{4,6},{5,1},{6,4},{7,3},{8,10},{9,13},{10,... | collective-permute-start | bytes 1572872 | tf_op jit(solution)/shard_map/ppermute | solution.py:26
  129.4 12.1 %collective-permute-start.31 = (bf16[128,2048]{1,0:T(8,128)(2,1)S(1)}, bf16[128,2048]{1,0:T(8,128)(2,1)S(1)}, u32[]{:S(2)}, u32[]{:S(2)}) collective-permute-start(bf16[128,2048]{1,0:T(8,128)(2,1)S(1)} %get-tuple-element.101), channel_id=1, source_target_pairs={{0,4},{1,3},{2,6},{3,1},{4,0},{5,7},{6,2},{7,5},{8,12},{9,11},{10,... | collective-permute-start | bytes 1572872 | tf_op jit(solution)/shard_map/ppermute | solution.py:26
  131.1 12.1 %collective-permute-start.38 = (bf16[128,2048]{1,0:T(8,128)(2,1)S(1)}, bf16[128,2048]{1,0:T(8,128)(2,1)S(1)}, u32[]{:S(2)}, u32[]{:S(2)}) collective-permute-start(bf16[128,2048]{1,0:T(8,128)(2,1)S(1)} %get-tuple-element.112), channel_id=1, source_target_pairs={{0,8},{2,10},{4,12},{6,14},{8,0},{10,2},{12,4},{14,6},{16,24},{18,... | collective-permute-start | bytes 1572872 | tf_op jit(solution)/shard_map/ppermute | solution.py:20
  139.7 12.1 %collective-permute-start.35 = (bf16[128,2048]{1,0:T(8,128)(2,1)S(1)}, bf16[128,2048]{1,0:T(8,128)(2,1)S(1)}, u32[]{:S(2)}, u32[]{:S(2)}) collective-permute-start(bf16[128,2048]{1,0:T(8,128)(2,1)S(1)} %get-tuple-element.107), channel_id=1, source_target_pairs={{0,2},{1,5},{2,0},{3,7},{4,6},{5,1},{6,4},{7,3},{8,10},{9,13},{10,... | collective-permute-start | bytes 1572872 | tf_op jit(solution)/shard_map/ppermute | solution.py:26
  141.4 12.8 %collective-permute-start.32 = (bf16[128,2048]{1,0:T(8,128)(2,1)S(1)}, bf16[128,2048]{1,0:T(8,128)(2,1)S(1)}, u32[]{:S(2)}, u32[]{:S(2)}) collective-permute-start(bf16[128,2048]{1,0:T(8,128)(2,1)S(1)} %add_convert_fusion.9), channel_id=1, source_target_pairs={{0,4},{1,3},{2,6},{3,1},{4,0},{5,7},{6,2},{7,5},{8,12},{9,11},{10,... | collective-permute-start | bytes 1572872 | tf_op jit(solution)/shard_map/ppermute | solution.py:26
  143.1 13.7 %collective-permute-start.39 = (bf16[128,2048]{1,0:T(8,128)(2,1)S(1)}, bf16[128,2048]{1,0:T(8,128)(2,1)S(1)}, u32[]{:S(2)}, u32[]{:S(2)}) collective-permute-start(bf16[128,2048]{1,0:T(8,128)(2,1)S(1)} %add_convert_fusion.7), channel_id=1, source_target_pairs={{0,8},{2,10},{4,12},{6,14},{24,16},{26,18},{28,20},{30,22},{1,9},{... | collective-permute-start | bytes 1572872 | tf_op jit(solution)/shard_map/ppermute | solution.py:216
  151.8 12.1 %collective-permute-start.44 = (bf16[128,2048]{1,0:T(8,128)(2,1)S(1)}, bf16[128,2048]{1,0:T(8,128)(2,1)S(1)}, u32[]{:S(2)}, u32[]{:S(2)}) collective-permute-start(bf16[128,2048]{1,0:T(8,128)(2,1)S(1)} %add_convert_fusion.2), channel_id=1, source_target_pairs={{0,2},{1,5},{2,0},{3,7},{4,6},{5,1},{6,4},{7,3},{8,10},{9,13},{10,... | collective-permute-start | bytes 1572872 | tf_op jit(solution)/shard_map/ppermute | solution.py:26
  154.3 9.8 %collective-permute-start.33 = (bf16[128,2048]{1,0:T(8,128)(2,1)S(1)}, bf16[128,2048]{1,0:T(8,128)(2,1)S(1)}, u32[]{:S(2)}, u32[]{:S(2)}) collective-permute-start(bf16[128,2048]{1,0:T(8,128)(2,1)S(1)} %get-tuple-element.103), channel_id=1, source_target_pairs={{0,4},{1,3},{2,6},{3,1},{4,0},{5,7},{6,2},{7,5},{8,12},{9,11},{10,... | collective-permute-start | bytes 1572872 | tf_op jit(solution)/shard_map/ppermute | solution.py:26
  157.1 11.7 %collective-permute-start.40 = (bf16[128,2048]{1,0:T(8,128)(2,1)S(1)}, bf16[128,2048]{1,0:T(8,128)(2,1)S(1)}, u32[]{:S(2)}, u32[]{:S(2)}) collective-permute-start(bf16[128,2048]{1,0:T(8,128)(2,1)S(1)} %add_convert_fusion.6), channel_id=1, source_target_pairs={{8,16},{10,18},{12,20},{14,22},{16,8},{18,10},{20,12},{22,14},{9,1... | collective-permute-start | bytes 1572872 | tf_op jit(solution)/shard_map/ppermute | solution.py:216
  159.2 13.5 %collective-permute-start.41 = (bf16[128,2048]{1,0:T(8,128)(2,1)S(1)}, bf16[128,2048]{1,0:T(8,128)(2,1)S(1)}, u32[]{:S(2)}, u32[]{:S(2)}) collective-permute-start(bf16[128,2048]{1,0:T(8,128)(2,1)S(1)} %add_convert_fusion.6), channel_id=1, source_target_pairs={{0,8},{2,10},{4,12},{6,14},{24,16},{26,18},{28,20},{30,22},{1,9},{... | collective-permute-start | bytes 1572872 | tf_op jit(solution)/shard_map/ppermute | solution.py:216
  164.0 22.4 %copy-start.4 = (f32[128,2048]{1,0:T(8,128)S(1)}, f32[128,2048]{1,0:T(8,128)}, u32[]{:S(2)}) copy-start(f32[128,2048]{1,0:T(8,128)} %get-tuple-element.68) | copy-start | bytes 3145732
  164.1 13.2 %collective-permute-start.46 = (bf16[128,2048]{1,0:T(8,128)(2,1)S(1)}, bf16[128,2048]{1,0:T(8,128)(2,1)S(1)}, u32[]{:S(2)}, u32[]{:S(2)}) collective-permute-start(bf16[128,2048]{1,0:T(8,128)(2,1)S(1)} %add_convert_fusion.1), channel_id=1, source_target_pairs={{0,4},{1,3},{2,6},{3,1},{4,0},{5,7},{6,2},{7,5},{8,12},{9,11},{10,... | collective-permute-start | bytes 1572872 | tf_op jit(solution)/shard_map/ppermute | solution.py:26
  166.4 10.9 %collective-permute-start.45 = (bf16[128,2048]{1,0:T(8,128)(2,1)S(1)}, bf16[128,2048]{1,0:T(8,128)(2,1)S(1)}, u32[]{:S(2)}, u32[]{:S(2)}) collective-permute-start(bf16[128,2048]{1,0:T(8,128)(2,1)S(1)} %add_convert_fusion.3), channel_id=1, source_target_pairs={{0,2},{1,5},{2,0},{3,7},{4,6},{5,1},{6,4},{7,3},{8,10},{9,13},{10,... | collective-permute-start | bytes 1572872 | tf_op jit(solution)/shard_map/ppermute | solution.py:26
  172.8 11.5 %collective-permute-start.43 = (bf16[128,2048]{1,0:T(8,128)(2,1)S(1)}, bf16[128,2048]{1,0:T(8,128)(2,1)S(1)}, u32[]{:S(2)}, u32[]{:S(2)}) collective-permute-start(bf16[128,2048]{1,0:T(8,128)(2,1)S(1)} %add_convert_fusion.4), channel_id=1, source_target_pairs={{8,16},{10,18},{12,20},{14,22},{16,8},{18,10},{20,12},{22,14},{9,1... | collective-permute-start | bytes 1572872 | tf_op jit(solution)/shard_map/ppermute | solution.py:216
  177.2 9.2 %collective-permute-start.42 = (bf16[128,2048]{1,0:T(8,128)(2,1)S(1)}, bf16[128,2048]{1,0:T(8,128)(2,1)S(1)}, u32[]{:S(2)}, u32[]{:S(2)}) collective-permute-start(bf16[128,2048]{1,0:T(8,128)(2,1)S(1)} %add_convert_fusion.5), channel_id=1, source_target_pairs={{0,8},{2,10},{4,12},{6,14},{8,0},{10,2},{12,4},{14,6},{16,24},{18,... | collective-permute-start | bytes 1572872 | tf_op jit(solution)/shard_map/ppermute | solution.py:20
  (9 other events, 42.7 us)

commit v12 on v11

--- a/solution.py
+++ b/solution.py
@@ -231,14 +231,14 @@
     ends2, near2 = shift(near3, OUTWARD), shift(o1, MIDDLE)
     d0, y1 = cross(after(y0, x0), X), cross(after(o1, y0), Y)
 
-    ends3 = shift(after(near2, ends2), OUTWARD)
     o2 = jnp.where(inner, near2, ends2)
+    ends3 = shift(after(near2, o2, d0, y1), OUTWARD)
     x2, y2 = cross(after(o2, d0, weights[0]), X), cross(after(o2, y1, weights[0]), Y)
     run = functools.partial(run, weights)
     p0, px0, py0, pd0 = run([after(o0, o2), x0, y0, d0], (0, X, Y, 3))
 
+    o3 = jnp.where(inner, near3, after(ends3, x2, y2))
     x1 = flip(after(x0, ends3, p0), 4)
-    o3 = jnp.where(inner, near3, ends3)
     x3, y3 = cross(after(o3, x2, p0), X), cross(after(o3, y2, p0), Y)
     p1, py1, p2, px2, py2, p3 = run(
         [after(o1, p0), y1, o2, x2, y2, o3], (4, plane(Y, 4), 8, plane(X, 8), plane(Y, 8), 12)
@@ -266,9 +266,9 @@
 
     p1, py0 = add_small(p1, by_y, to_1), add_small(py0, to_y0)
     p3 = add_small(after(p3, p1), to_3)
-    by_z, by_middle = flip(after(p1, to_3), 4), shift(p3, MIDDLE)
+    by_middle, by_z = shift(p3, MIDDLE), flip(p1, 4)
     by_x, by_y = cross(after(px0, to_y0), X), cross(after(py0, by_y), Y)
-    return add(stream, p0, by_z, by_middle, by_x, by_y)
+    return add(stream, p0, by_x, by_y, by_z, by_middle)
 
 
 def plane(masks, distance):
@@ -279,7 +279,7 @@
     count = lax.axis_size("seq")
 
     def weights(*waits):
-        return assemble([after(half, *waits) for half in halves])
+        return assemble([after(half, gates[-1], *waits) for half in halves])
 
     def run(weights, blocks, masks):
         masks = [mask if isinstance(mask, tuple) else (mask, mask) for mask in masks]

time: 188 us -> 201 us (1.069); the launches traced: 188 us -> 198 us
  waiting for transfers between devices: 77.1 us -> 90.2 us
  starting transfers between devices: 60.9 us -> 57 us
    ppermute x20, waiting for transfers between devices: 42.7 us -> 55.8 us  [cross(): return lax.ppermute(block, ('seq', 'exp'), pairs)]
    ppermute x8, starting transfers between devices: 22.4 us -> 19.8 us  [shift(): lax.ppermute(block, 'seq', [(4 * a + i, 4 * b + i) for a, b in pairs for...]
    ppermute x12, starting transfers between devices: 10.4 us -> 8.1 us  [flip(): return lax.ppermute(block, 'seq', [(i, i ^ mask) for i in range(count)])]
  transfers between devices with their start and end apart: 47 -> 47, of which waited for: 22 -> 24; matrix products, arithmetic and copies ran while one was open for 3% -> 3% of each run, Pallas kernels for 17% -> 17%
where the time goes in v12:
time: 201 us; the launch traced here: 198 us
  waiting for transfers between devices  90.2 us (45%)
  starting transfers between devices  57 us (28%)
  Pallas kernels  37 us (18%)
  local copies, waits for them, and re-layouts  6.87 us (3%)
  other arithmetic  6.54 us (3%)
    ppermute x20, waiting for transfers between devices, cross(): return lax.ppermute(block, ('seq', 'exp'), pairs)  55.8 us
    pallas_call x5, Pallas kernels, expert(): pl.pallas_call(functools.partial(expert_kernel, places, len(gates)), out_...  25.5 us
    ppermute x20, starting transfers between devices, cross(): return lax.ppermute(block, ('seq', 'exp'), pairs)  21.9 us
    ppermute x8, starting transfers between devices, shift(): lax.ppermute(block, 'seq', [(4 * a + i, 4 * b + i) for a, b in pairs for...  19.8 us
    ppermute x12, waiting for transfers between devices, flip(): return lax.ppermute(block, 'seq', [(i, i ^ mask) for i in range(count)])  19.2 us
    ppermute x8, waiting for transfers between devices, shift(): lax.ppermute(block, 'seq', [(4 * a + i, 4 * b + i) for a, b in pairs for...  13.6 us
    ppermute x12, starting transfers between devices, flip(): return lax.ppermute(block, 'seq', [(i, i ^ mask) for i in range(count)])  8.1 us
    ppermute x2, starting transfers between devices, halo(): return (beside, part, lax.ppermute(beside, 'seq', ahead + back))  6.6 us
  transfers between devices with their start and end apart: 47, of which 24 were waited for; matrix products, arithmetic and copies ran while one was open for 3% of the time, Pallas kernels for 17%

profile of v12, /device:TPU:10, one launch (start us, length us, event | category | flops | bytes accessed | tf_op | source)
XLA Modules:
  0.0 198.0 jit_solution(3645311811293462086)
XLA Ops:
  0.5 1.5 collective-permute-start.2
  3.3 3.2 %collective-permute-done.7.refs_5_.refs_7_.refs_4_.refs_3_.refs_2_ = f32[16,128]{1,0:T(8,128)S(1)} collective-permute-done((f32[16,128]{1,0:T(8,128)S(1)}, f32[16,128]{1,0:T(8,128)S(1)}, u32[]{:S(2)}, u32[]{:S(2)}) %collective-permute-start.7) | collective-permute-done | bytes 8224 | tf_op jit(solution)/shard_map/ppermute | solution.py:20
  6.5 2.6 %collective-permute-start.8 = (f32[16,256]{1,0:T(8,128)S(1)}, f32[16,256]{1,0:T(8,128)S(1)}, u32[]{:S(2)}, u32[]{:S(2)}) collective-permute-start(f32[16,256]{1,0:T(8,128)S(1)} %pad_maximum_fusion.2), channel_id=1, source_target_pairs={{0,16},{2,18},{4,20},{6,22},{8,24},{10,26},{12,28},{14,30},{16,0},... | collective-permute-start | bytes 49160 | tf_op jit(solution)/shard_map/ppermute | solution.py:20
  9.3 3.3 %collective-permute-start.1 = (bf16[256,512]{1,0:T(8,128)(2,1)S(1)}, bf16[256,512]{1,0:T(8,128)(2,1)S(1)}, u32[]{:S(2)}, u32[]{:S(2)}) collective-permute-start(bf16[256,512]{1,0:T(8,128)(2,1)S(1)} %collective-permute-done.refs_0_), channel_id=1, source_target_pairs={{0,4},{4,8},{8,12},{12,16},{16,20},{20,24},{24,28},{6,2},{10,6},{1... | collective-permute-start | bytes 786440 | tf_op jit(solution)/shard_map/ppermute | solution.py:329
  12.6 1.9 collective-permute-done.2.refs_3_
  14.6 3.3 %collective-permute-start.3 = (bf16[256,512]{1,0:T(8,128)(2,1)S(1)}, bf16[256,512]{1,0:T(8,128)(2,1)S(1)}, u32[]{:S(2)}, u32[]{:S(2)}) collective-permute-start(bf16[256,512]{1,0:T(8,128)(2,1)S(1)} %collective-permute-done.2.refs_3_), channel_id=1, source_target_pairs={{0,4},{4,8},{8,12},{12,16},{16,20},{20,24},{24,28},{6,2},{10,6},{1... | collective-permute-start | bytes 786440 | tf_op jit(solution)/shard_map/ppermute | solution.py:329
  20.5 4.5 %collective-permute-done.9.refs_7_.refs_9_.refs_6_.refs_5_.refs_4_ = f32[16,512]{1,0:T(8,128)S(1)} collective-permute-done((f32[16,512]{1,0:T(8,128)S(1)}, f32[16,512]{1,0:T(8,128)S(1)}, u32[]{:S(2)}, u32[]{:S(2)}) %collective-permute-start.9) | collective-permute-done | bytes 32800 | tf_op jit(solution)/shard_map/ppermute | solution.py:20
  26.4 4.6 %window_attention.1 = (bf16[128,512]{1,0:T(8,128)(2,1)}, bf16[128,512]{1,0:T(8,128)(2,1)}) custom-call(s32[2]{0:T(128)} %pad_add_fusion.where_ref, bf16[256,512]{1,0:T(8,128)(2,1)} %q_ref.1, s32[1,768]{1,0:T(1,128)} %broadcast_in_dim.21.ids_ref, bf16[256,512]{1,0:T(8,128)(2,1)} %copy-done.5, bf16[256,512]{1,0:T(8,128)(2,1)} %refs_1_.1, ...), custom_call_target="tpu_custom_call" | custom-call | tf_op jit(solution)/shard_map/window_attention/pallas_call | solution.py:97
  33.2 4.3 %project_and_norm.1 = (f32[128,2048]{1,0:T(8,128)}, bf16[128,2048]{1,0:T(8,128)(2,1)}) custom-call(bf16[128,512]{1,0:T(8,128)(2,1)} %get-tuple-element.64.mine_ref, bf16[128,512]{1,0:T(8,128)(2,1)} %copy-done.9, bf16[512,2048]{1,0:T(8,128)(2,1)} %own_w.1, bf16[512,2048]{1,0:T(8,128)(2,1)} %collective-permute-done.4.refs_6_.other_w, ...), custom_call_target="tpu_custom_call" | custom-call | tf_op jit(solution)/shard_map/project_and_norm/pallas_call | solution.py:120
  37.9 4.6 %collective-permute-start.14 = (bf16[128,2048]{1,0:T(8,128)(2,1)}, bf16[128,2048]{1,0:T(8,128)(2,1)}, u32[]{:S(2)}, u32[]{:S(2)}) collective-permute-start(bf16[128,2048]{1,0:T(8,128)(2,1)} %get-tuple-element.70.refs_0_), channel_id=1, source_target_pairs={{8,16},{10,18},{12,20},{14,22},{16,8},{18,10},{20,12},{22,14},{9,1... | collective-permute-start | bytes 1572872 | tf_op jit(solution)/shard_map/ppermute | solution.py:216
  42.5 1.5 collective-permute-start.16
  44.6 7.0 %collective-permute-done.12.refs_0_ = bf16[128,2048]{1,0:T(8,128)(2,1)S(1)} collective-permute-done((bf16[128,2048]{1,0:T(8,128)(2,1)}, bf16[128,2048]{1,0:T(8,128)(2,1)S(1)}, u32[]{:S(2)}, u32[]{:S(2)}) %collective-permute-start.12) | collective-permute-done | bytes 524320 | tf_op jit(solution)/shard_map/ppermute | solution.py:20
  51.6 3.5 %collective-permute-start.13 = (bf16[128,2048]{1,0:T(8,128)(2,1)S(1)}, bf16[128,2048]{1,0:T(8,128)(2,1)}, u32[]{:S(2)}, u32[]{:S(2)}) collective-permute-start(bf16[128,2048]{1,0:T(8,128)(2,1)S(1)} %collective-permute-done.12.refs_0_), channel_id=1, source_target_pairs={{8,16},{10,18},{12,20},{14,22},{16,8},{18,10},{20,12},{22,14},{9,1... | collective-permute-start | bytes 1572872 | tf_op jit(solution)/shard_map/ppermute | solution.py:216
  55.1 2.1 %collective-permute-start.15 = (bf16[128,2048]{1,0:T(8,128)(2,1)}, bf16[128,2048]{1,0:T(8,128)(2,1)}, u32[]{:S(2)}, u32[]{:S(2)}) collective-permute-start(bf16[128,2048]{1,0:T(8,128)(2,1)} %collective-permute-done.14), channel_id=1, source_target_pairs={{8,0},{10,2},{12,4},{14,6},{16,24},{18,26},{20,28},{22,30},{9,1},{... | collective-permute-start | bytes 1572872 | tf_op jit(solution)/shard_map/ppermute | solution.py:216
  57.2 1.4 collective-permute-start.19
  59.3 2.4 %collective-permute-start.20 = (bf16[128,2048]{1,0:T(8,128)(2,1)S(1)}, bf16[128,2048]{1,0:T(8,128)(2,1)S(1)}, u32[]{:S(2)}, u32[]{:S(2)}) collective-permute-start(bf16[128,2048]{1,0:T(8,128)(2,1)S(1)} %collective-permute-done.12.refs_0_), channel_id=1, source_target_pairs={{0,4},{1,3},{2,6},{3,1},{4,0},{5,7},{6,2},{7,5},{8,12},{9,11},{10,... | collective-permute-start | bytes 1572872 | tf_op jit(solution)/shard_map/ppermute | solution.py:26
  61.9 1.4 copy-done
  63.2 1.4 copy-done.1
  64.6 1.4 copy-done.2
  66.0 2.6 %assemble_weights.1 = (bf16[1408,2048]{1,0:T(8,128)(2,1)S(1)}, bf16[704,2048]{1,0:T(8,128)(2,1)S(1)}) custom-call(bf16[352,2048]{1,0:T(8,128)(2,1)S(1)} %bitcast.14, bf16[352,2048]{1,0:T(8,128)(2,1)} %collective-permute-done.5.refs_7_.refs_1_, bf16[352,2048]{1,0:T(8,128)(2,1)S(1)} %bitcast.16, bf16[352,2048]{1,0:T(8,128)(2,1)} %collective-permute-done.10.refs_0_.refs_3_, ...), custom_call_target="tpu_custom_call" | custom-call | tf_op jit(solution)/shard_map/assemble_weights/pallas_call | solution.py:148
  69.8 2.9 %collective-permute-done.18.refs_3_ = bf16[128,2048]{1,0:T(8,128)(2,1)S(1)} collective-permute-done((bf16[128,2048]{1,0:T(8,128)(2,1)S(1)}, bf16[128,2048]{1,0:T(8,128)(2,1)S(1)}, u32[]{:S(2)}, u32[]{:S(2)}) %collective-permute-start.18) | collective-permute-done | bytes 524320 | tf_op jit(solution)/shard_map/ppermute | solution.py:26
  72.7 1.5 collective-permute-start.21
  74.2 1.5 collective-permute-start.23
  76.8 5.6 %expert_rows.5 = (bf16[128,2048]{1,0:T(8,128)(2,1)S(1)}, bf16[128,2048]{1,0:T(8,128)(2,1)S(1)}, bf16[128,2048]{1,0:T(8,128)(2,1)S(1)}, bf16[128,2048]{1,0:T(8,128)(2,1)S(1)}) custom-call(s32[2]{0:T(128)S(1)} %pad_add_fusion.1.where_ref, bf16[128,2048]{1,0:T(8,128)(2,1)S(1)} %copy-done.3, bf16[128,2048]{1,0:T(8,128)(2,1)S(1)} %collective-permute-done.16.refs_1_, ...), custom_call_target="tpu_custom_call" | custom-call | tf_op jit(solution)/shard_map/expert_rows/pallas_call | solution.py:194
  82.5 2.9 %collective-permute-done.21 = bf16[128,2048]{1,0:T(8,128)(2,1)S(1)} collective-permute-done((bf16[128,2048]{1,0:T(8,128)(2,1)}, bf16[128,2048]{1,0:T(8,128)(2,1)S(1)}, u32[]{:S(2)}, u32[]{:S(2)}) %collective-permute-start.21) | collective-permute-done | bytes 524320 | tf_op jit(solution)/shard_map/ppermute | solution.py:216
  85.3 3.6 %collective-permute-done.23.refs_4_ = bf16[128,2048]{1,0:T(8,128)(2,1)S(1)} collective-permute-done((bf16[128,2048]{1,0:T(8,128)(2,1)S(1)}, bf16[128,2048]{1,0:T(8,128)(2,1)S(1)}, u32[]{:S(2)}, u32[]{:S(2)}) %collective-permute-start.23) | collective-permute-done | bytes 524320 | tf_op jit(solution)/shard_map/ppermute | solution.py:26
  91.1 8.1 %expert_rows.6 = (bf16[128,2048]{1,0:T(8,128)(2,1)S(1)}, bf16[128,2048]{1,0:T(8,128)(2,1)S(1)}, bf16[128,2048]{1,0:T(8,128)(2,1)S(1)}, bf16[128,2048]{1,0:T(8,12...) custom-call(s32[2]{0:T(128)S(1)} %pad_add_fusion.1.where_ref, ...), custom_call_target="tpu_custom_call" | custom-call | tf_op jit(solution)/shard_map/expert_rows/pallas_call | solution.py:194
  99.2 4.9 %collective-permute-done.24.refs_0_ = bf16[128,2048]{1,0:T(8,128)(2,1)S(1)} collective-permute-done((bf16[128,2048]{1,0:T(8,128)(2,1)S(1)}, bf16[128,2048]{1,0:T(8,128)(2,1)S(1)}, u32[]{:S(2)}, u32[]{:S(2)}) %collective-permute-start.24) | collective-permute-done | bytes 524320 | tf_op jit(solution)/shard_map/ppermute | solution.py:26
  105.7 5.6 %expert_rows.7 = (bf16[128,2048]{1,0:T(8,128)(2,1)S(1)}, bf16[128,2048]{1,0:T(8,128)(2,1)S(1)}, bf16[128,2048]{1,0:T(8,128)(2,1)S(1)}) custom-call(s32[2]{0:T(128)S(1)} %pad_add_fusion.1.where_ref, bf16[128,2048]{1,0:T(8,128)(2,1)S(1)} %collective-permute-done.24.refs_0_, bf16[128,2048]{1,0:T(8,128)(2,1)S(1)} %collective-permute-done.25.refs_1_, ...), custom_call_target="tpu_custom_call" | custom-call | tf_op jit(solution)/shard_map/expert_rows/pallas_call | solution.py:194
  111.4 6.0 %collective-permute-done.28.refs_0_ = bf16[128,2048]{1,0:T(8,128)(2,1)S(1)} collective-permute-done((bf16[128,2048]{1,0:T(8,128)(2,1)S(1)}, bf16[128,2048]{1,0:T(8,128)(2,1)S(1)}, u32[]{:S(2)}, u32[]{:S(2)}) %collective-permute-start.28) | collective-permute-done | bytes 524320 | tf_op jit(solution)/shard_map/ppermute | solution.py:26
  117.3 3.2 %expert_rows.8 = (bf16[128,2048]{1,0:T(8,128)(2,1)S(1)}, bf16[128,2048]{1,0:T(8,128)(2,1)S(1)}) custom-call(s32[2]{0:T(128)S(1)} %pad_add_fusion.1.where_ref, bf16[128,2048]{1,0:T(8,128)(2,1)S(1)} %collective-permute-done.28.refs_0_, bf16[128,2048]{1,0:T(8,128)(2,1)S(1)} %collective-permute-done.29.refs_1_, ...), custom_call_target="tpu_custom_call" | custom-call | tf_op jit(solution)/shard_map/expert_rows/pallas_call | solution.py:194
  120.6 2.2 %collective-permute-start.32 = (bf16[128,2048]{1,0:T(8,128)(2,1)S(1)}, bf16[128,2048]{1,0:T(8,128)(2,1)S(1)}, u32[]{:S(2)}, u32[]{:S(2)}) collective-permute-start(bf16[128,2048]{1,0:T(8,128)(2,1)S(1)} %get-tuple-element.105), channel_id=1, source_target_pairs={{0,4},{1,3},{2,6},{3,1},{4,0},{5,7},{6,2},{7,5},{8,12},{9,11},{10,... | collective-permute-start | bytes 1572872 | tf_op jit(solution)/shard_map/ppermute | solution.py:26
  123.2 2.9 %expert_rows.9 = bf16[128,2048]{1,0:T(8,128)(2,1)S(1)} custom-call(s32[2]{0:T(128)S(1)} %pad_add_fusion.1.where_ref, bf16[128,2048]{1,0:T(8,128)(2,1)S(1)} %collective-permute-done.27.refs_0_, f32[16,128]{1,0:T(8,128)S(1)} %select_reduce_fusion.refs_4_.refs_6_.refs_3_.refs_2_.refs_1_, ...), custom_call_target="tpu_custom_call" | custom-call | tf_op jit(solution)/shard_map/expert_rows/pallas_call | solution.py:194
  126.2 8.3 %collective-permute-done.32 = bf16[128,2048]{1,0:T(8,128)(2,1)S(1)} collective-permute-done((bf16[128,2048]{1,0:T(8,128)(2,1)S(1)}, bf16[128,2048]{1,0:T(8,128)(2,1)S(1)}, u32[]{:S(2)}, u32[]{:S(2)}) %collective-permute-start.32) | collective-permute-done | bytes 524320 | tf_op jit(solution)/shard_map/ppermute | solution.py:26
  135.9 2.2 %collective-permute-start.38 = (bf16[128,2048]{1,0:T(8,128)(2,1)S(1)}, bf16[128,2048]{1,0:T(8,128)(2,1)S(1)}, u32[]{:S(2)}, u32[]{:S(2)}) collective-permute-start(bf16[128,2048]{1,0:T(8,128)(2,1)S(1)} %get-tuple-element.114), channel_id=1, source_target_pairs={{0,4},{1,3},{2,6},{3,1},{4,0},{5,7},{6,2},{7,5},{8,12},{9,11},{10,... | collective-permute-start | bytes 1572872 | tf_op jit(solution)/shard_map/ppermute | solution.py:26
  139.4 9.8 %collective-permute-done.34 = bf16[128,2048]{1,0:T(8,128)(2,1)S(1)} collective-permute-done((bf16[128,2048]{1,0:T(8,128)(2,1)S(1)}, bf16[128,2048]{1,0:T(8,128)(2,1)S(1)}, u32[]{:S(2)}, u32[]{:S(2)}) %collective-permute-start.34) | collective-permute-done | bytes 524320 | tf_op jit(solution)/shard_map/ppermute | solution.py:26
  149.8 2.0 %collective-permute-start.39 = (bf16[128,2048]{1,0:T(8,128)(2,1)S(1)}, bf16[128,2048]{1,0:T(8,128)(2,1)S(1)}, u32[]{:S(2)}, u32[]{:S(2)}) collective-permute-start(bf16[128,2048]{1,0:T(8,128)(2,1)S(1)} %add_convert_fusion.5), channel_id=1, source_target_pairs={{0,4},{1,3},{2,6},{3,1},{4,0},{5,7},{6,2},{7,5},{8,12},{9,11},{10,... | collective-permute-start | bytes 1572872 | tf_op jit(solution)/shard_map/ppermute | solution.py:26
  152.1 1.3 collective-permute-start.42
  153.5 9.9 %collective-permute-done.35 = bf16[128,2048]{1,0:T(8,128)(2,1)S(1)} collective-permute-done((bf16[128,2048]{1,0:T(8,128)(2,1)S(1)}, bf16[128,2048]{1,0:T(8,128)(2,1)S(1)}, u32[]{:S(2)}, u32[]{:S(2)}) %collective-permute-start.35) | collective-permute-done | bytes 524320 | tf_op jit(solution)/shard_map/ppermute | solution.py:26
  164.8 1.7 collective-permute-done.42
  166.9 1.9 collective-permute-start.43
  170.2 6.7 %collective-permute-done.36 = bf16[128,2048]{1,0:T(8,128)(2,1)S(1)} collective-permute-done((bf16[128,2048]{1,0:T(8,128)(2,1)S(1)}, bf16[128,2048]{1,0:T(8,128)(2,1)S(1)}, u32[]{:S(2)}, u32[]{:S(2)}) %collective-permute-start.36) | collective-permute-done | bytes 524320 | tf_op jit(solution)/shard_map/ppermute | solution.py:26
  177.0 1.6 collective-permute-start.37
  178.8 1.7 collective-permute-done.43
  180.8 1.8 collective-permute-done.45
  182.7 3.6 %collective-permute-start.46 = (bf16[128,2048]{1,0:T(8,128)(2,1)S(1)}, bf16[128,2048]{1,0:T(8,128)(2,1)S(1)}, u32[]{:S(2)}, u32[]{:S(2)}) collective-permute-start(bf16[128,2048]{1,0:T(8,128)(2,1)S(1)} %add_convert_fusion.1), channel_id=1, source_target_pairs={{8,16},{10,18},{12,20},{14,22},{16,8},{18,10},{20,12},{22,14},{9,1... | collective-permute-start | bytes 1572872 | tf_op jit(solution)/shard_map/ppermute | solution.py:216
  186.5 3.5 %collective-permute-done.37 = bf16[128,2048]{1,0:T(8,128)(2,1)S(1)} collective-permute-done((bf16[128,2048]{1,0:T(8,128)(2,1)S(1)}, bf16[128,2048]{1,0:T(8,128)(2,1)S(1)}, u32[]{:S(2)}, u32[]{:S(2)}) %collective-permute-start.37) | collective-permute-done | bytes 524320 | tf_op jit(solution)/shard_map/ppermute | solution.py:26
  189.9 5.5 %collective-permute-done.46 = bf16[128,2048]{1,0:T(8,128)(2,1)S(1)} collective-permute-done((bf16[128,2048]{1,0:T(8,128)(2,1)S(1)}, bf16[128,2048]{1,0:T(8,128)(2,1)S(1)}, u32[]{:S(2)}, u32[]{:S(2)}) %collective-permute-start.46) | collective-permute-done | bytes 524320 | tf_op jit(solution)/shard_map/ppermute | solution.py:216
  (94 shorter events, 26.4 us)
Async XLA Ops:
  0.0 26.3 %collective-permute-start.4 = (bf16[512,2048]{1,0:T(8,128)(2,1)}, bf16[512,2048]{1,0:T(8,128)(2,1)}, u32[]{:S(2)}, u32[]{:S(2)}) collective-permute-start(bf16[512,2048]{1,0:T(8,128)(2,1)} %own_w.1), channel_id=1, source_target_pairs={{0,1},{1,0},{2,3},{3,2},{4,5},{5,4},{6,7},{7,6},{8,9},{9,8},{10,11... | collective-permute-start | bytes 6291464 | tf_op jit(solution)/shard_map/ppermute | solution.py:338
  0.0 9.3 %collective-permute-start = (bf16[256,512]{1,0:T(8,128)(2,1)}, bf16[256,512]{1,0:T(8,128)(2,1)S(1)}, u32[]{:S(2)}, u32[]{:S(2)}) collective-permute-start(bf16[256,512]{1,0:T(8,128)(2,1)} %refs_1_.1), channel_id=1, source_target_pairs={{0,2},{2,0},{4,6},{6,4},{8,10},{10,8},{12,14},{14,12},{16,18},{18,... | collective-permute-start | bytes 786440 | tf_op jit(solution)/shard_map/ppermute | solution.py:20
  0.5 14.0 %collective-permute-start.2 = (bf16[256,512]{1,0:T(8,128)(2,1)}, bf16[256,512]{1,0:T(8,128)(2,1)S(1)}, u32[]{:S(2)}, u32[]{:S(2)}) collective-permute-start(bf16[256,512]{1,0:T(8,128)(2,1)} %refs_4_.1), channel_id=1, source_target_pairs={{0,2},{2,0},{4,6},{6,4},{8,10},{10,8},{12,14},{14,12},{16,18},{18,... | collective-permute-start | bytes 786440 | tf_op jit(solution)/shard_map/ppermute | solution.py:20
  2.7 3.7 %collective-permute-start.7 = (f32[16,128]{1,0:T(8,128)S(1)}, f32[16,128]{1,0:T(8,128)S(1)}, u32[]{:S(2)}, u32[]{:S(2)}) collective-permute-start(f32[16,128]{1,0:T(8,128)S(1)} %select_reduce_fusion.refs_4_.refs_6_.refs_3_.refs_2_.refs_1_), channel_id=1, source_target_pairs={{0,8},{2,10},{4,12},{6,14},{8,0},{10,2},{12,4},{14,6},{16,24},{18,... | collective-permute-start | bytes 24584 | tf_op jit(solution)/shard_map/ppermute | solution.py:20
  3.3 23.1 %collective-permute-start.5 = (bf16[352,2048]{1,0:T(8,128)(2,1)}, bf16[352,2048]{1,0:T(8,128)(2,1)}, u32[]{:S(2)}, u32[]{:S(2)}) collective-permute-start(bf16[352,2048]{1,0:T(8,128)(2,1)} %bitcast.13), channel_id=1, source_target_pairs={{0,1},{1,0},{2,3},{3,2},{4,5},{5,4},{6,7},{7,6},{8,9},{9,8},{10,11... | collective-permute-start | bytes 4325384 | tf_op jit(solution)/shard_map/ppermute | solution.py:340
  6.5 12.2 %collective-permute-start.8 = (f32[16,256]{1,0:T(8,128)S(1)}, f32[16,256]{1,0:T(8,128)S(1)}, u32[]{:S(2)}, u32[]{:S(2)}) collective-permute-start(f32[16,256]{1,0:T(8,128)S(1)} %pad_maximum_fusion.2), channel_id=1, source_target_pairs={{0,16},{2,18},{4,20},{6,22},{8,24},{10,26},{12,28},{14,30},{16,0},... | collective-permute-start | bytes 49160 | tf_op jit(solution)/shard_map/ppermute | solution.py:20
  9.3 15.8 %collective-permute-start.1 = (bf16[256,512]{1,0:T(8,128)(2,1)S(1)}, bf16[256,512]{1,0:T(8,128)(2,1)S(1)}, u32[]{:S(2)}, u32[]{:S(2)}) collective-permute-start(bf16[256,512]{1,0:T(8,128)(2,1)S(1)} %collective-permute-done.refs_0_), channel_id=1, source_target_pairs={{0,4},{4,8},{8,12},{12,16},{16,20},{20,24},{24,28},{6,2},{10,6},{1... | collective-permute-start | bytes 786440 | tf_op jit(solution)/shard_map/ppermute | solution.py:329
  14.6 10.5 %collective-permute-start.3 = (bf16[256,512]{1,0:T(8,128)(2,1)S(1)}, bf16[256,512]{1,0:T(8,128)(2,1)S(1)}, u32[]{:S(2)}, u32[]{:S(2)}) collective-permute-start(bf16[256,512]{1,0:T(8,128)(2,1)S(1)} %collective-permute-done.2.refs_3_), channel_id=1, source_target_pairs={{0,4},{4,8},{8,12},{12,16},{16,20},{20,24},{24,28},{6,2},{10,6},{1... | collective-permute-start | bytes 786440 | tf_op jit(solution)/shard_map/ppermute | solution.py:329
  18.7 6.4 %collective-permute-start.9 = (f32[16,512]{1,0:T(8,128)S(1)}, f32[16,512]{1,0:T(8,128)S(1)}, u32[]{:S(2)}, u32[]{:S(2)}) collective-permute-start(f32[16,512]{1,0:T(8,128)S(1)} %pad_maximum_fusion.1), channel_id=1, source_target_pairs={{0,4},{2,6},{4,0},{6,2},{8,12},{10,14},{12,8},{14,10},{16,20},{18,... | collective-permute-start | bytes 98312 | tf_op jit(solution)/shard_map/ppermute | solution.py:20
  25.8 5.1 %collective-permute-start.10 = (bf16[352,2048]{1,0:T(8,128)(2,1)}, bf16[352,2048]{1,0:T(8,128)(2,1)}, u32[]{:S(2)}, u32[]{:S(2)}) collective-permute-start(bf16[352,2048]{1,0:T(8,128)(2,1)} %bitcast.15), channel_id=1, source_target_pairs={{0,1},{1,0},{2,3},{3,2},{4,5},{5,4},{6,7},{7,6},{8,9},{9,8},{10,11... | collective-permute-start | bytes 4325384 | tf_op jit(solution)/shard_map/ppermute | solution.py:343
  25.8 5.6 %collective-permute-start.11 = (bf16[352,2048]{1,0:T(8,128)(2,1)}, bf16[352,2048]{1,0:T(8,128)(2,1)}, u32[]{:S(2)}, u32[]{:S(2)}) collective-permute-start(bf16[352,2048]{1,0:T(8,128)(2,1)} %bitcast.17), channel_id=1, source_target_pairs={{0,1},{1,0},{2,3},{3,2},{4,5},{5,4},{6,7},{7,6},{8,9},{9,8},{10,11... | collective-permute-start | bytes 4325384 | tf_op jit(solution)/shard_map/ppermute | solution.py:344
  30.9 1.6 collective-permute-start.6
  37.5 14.2 %collective-permute-start.12 = (bf16[128,2048]{1,0:T(8,128)(2,1)}, bf16[128,2048]{1,0:T(8,128)(2,1)S(1)}, u32[]{:S(2)}, u32[]{:S(2)}) collective-permute-start(bf16[128,2048]{1,0:T(8,128)(2,1)} %get-tuple-element.70.refs_0_), channel_id=1, source_target_pairs={{0,8},{2,10},{4,12},{6,14},{8,0},{10,2},{12,4},{14,6},{16,24},{18,... | collective-permute-start | bytes 1572872 | tf_op jit(solution)/shard_map/ppermute | solution.py:20
  37.9 17.2 %collective-permute-start.14 = (bf16[128,2048]{1,0:T(8,128)(2,1)}, bf16[128,2048]{1,0:T(8,128)(2,1)}, u32[]{:S(2)}, u32[]{:S(2)}) collective-permute-start(bf16[128,2048]{1,0:T(8,128)(2,1)} %get-tuple-element.70.refs_0_), channel_id=1, source_target_pairs={{8,16},{10,18},{12,20},{14,22},{16,8},{18,10},{20,12},{22,14},{9,1... | collective-permute-start | bytes 1572872 | tf_op jit(solution)/shard_map/ppermute | solution.py:216
  42.5 16.2 %collective-permute-start.16 = (bf16[128,2048]{1,0:T(8,128)(2,1)}, bf16[128,2048]{1,0:T(8,128)(2,1)S(1)}, u32[]{:S(2)}, u32[]{:S(2)}) collective-permute-start(bf16[128,2048]{1,0:T(8,128)(2,1)} %get-tuple-element.70.refs_0_), channel_id=1, source_target_pairs={{0,2},{1,5},{2,0},{3,7},{4,6},{5,1},{6,4},{7,3},{8,10},{9,13},{10,... | collective-permute-start | bytes 1572872 | tf_op jit(solution)/shard_map/ppermute | solution.py:26
  44.0 14.7 %collective-permute-start.17 = (bf16[128,2048]{1,0:T(8,128)(2,1)}, bf16[128,2048]{1,0:T(8,128)(2,1)S(1)}, u32[]{:S(2)}, u32[]{:S(2)}) collective-permute-start(bf16[128,2048]{1,0:T(8,128)(2,1)} %get-tuple-element.70.refs_0_), channel_id=1, source_target_pairs={{0,4},{1,3},{2,6},{3,1},{4,0},{5,7},{6,2},{7,5},{8,12},{9,11},{10,... | collective-permute-start | bytes 1572872 | tf_op jit(solution)/shard_map/ppermute | solution.py:26
  51.6 17.0 %collective-permute-start.13 = (bf16[128,2048]{1,0:T(8,128)(2,1)S(1)}, bf16[128,2048]{1,0:T(8,128)(2,1)}, u32[]{:S(2)}, u32[]{:S(2)}) collective-permute-start(bf16[128,2048]{1,0:T(8,128)(2,1)S(1)} %collective-permute-done.12.refs_0_), channel_id=1, source_target_pairs={{8,16},{10,18},{12,20},{14,22},{16,8},{18,10},{20,12},{22,14},{9,1... | collective-permute-start | bytes 1572872 | tf_op jit(solution)/shard_map/ppermute | solution.py:216
  55.1 13.5 %collective-permute-start.15 = (bf16[128,2048]{1,0:T(8,128)(2,1)}, bf16[128,2048]{1,0:T(8,128)(2,1)}, u32[]{:S(2)}, u32[]{:S(2)}) collective-permute-start(bf16[128,2048]{1,0:T(8,128)(2,1)} %collective-permute-done.14), channel_id=1, source_target_pairs={{8,0},{10,2},{12,4},{14,6},{16,24},{18,26},{20,28},{22,30},{9,1},{... | collective-permute-start | bytes 1572872 | tf_op jit(solution)/shard_map/ppermute | solution.py:216
  57.2 4.6 %collective-permute-start.19 = (f32[16,1024]{1,0:T(8,128)S(1)}, f32[16,1024]{1,0:T(8,128)S(1)}, u32[]{:S(2)}, u32[]{:S(2)}) collective-permute-start(f32[16,1024]{1,0:T(8,128)S(1)} %pad_maximum_fusion), channel_id=1, source_target_pairs={{0,2},{2,0},{4,6},{6,4},{8,10},{10,8},{12,14},{14,12},{16,18},{18,... | collective-permute-start | bytes 196616 | tf_op jit(solution)/shard_map/ppermute | solution.py:20
  58.7 14.1 %collective-permute-start.18 = (bf16[128,2048]{1,0:T(8,128)(2,1)S(1)}, bf16[128,2048]{1,0:T(8,128)(2,1)S(1)}, u32[]{:S(2)}, u32[]{:S(2)}) collective-permute-start(bf16[128,2048]{1,0:T(8,128)(2,1)S(1)} %collective-permute-done.17.refs_2_), channel_id=1, source_target_pairs={{0,2},{1,5},{2,0},{3,7},{4,6},{5,1},{6,4},{7,3},{8,10},{9,13},{10,... | collective-permute-start | bytes 1572872 | tf_op jit(solution)/shard_map/ppermute | solution.py:26
  59.3 13.5 %collective-permute-start.20 = (bf16[128,2048]{1,0:T(8,128)(2,1)S(1)}, bf16[128,2048]{1,0:T(8,128)(2,1)S(1)}, u32[]{:S(2)}, u32[]{:S(2)}) collective-permute-start(bf16[128,2048]{1,0:T(8,128)(2,1)S(1)} %collective-permute-done.12.refs_0_), channel_id=1, source_target_pairs={{0,4},{1,3},{2,6},{3,1},{4,0},{5,7},{6,2},{7,5},{8,12},{9,11},{10,... | collective-permute-start | bytes 1572872 | tf_op jit(solution)/shard_map/ppermute | solution.py:26
  72.7 12.6 %collective-permute-start.21 = (bf16[128,2048]{1,0:T(8,128)(2,1)}, bf16[128,2048]{1,0:T(8,128)(2,1)S(1)}, u32[]{:S(2)}, u32[]{:S(2)}) collective-permute-start(bf16[128,2048]{1,0:T(8,128)(2,1)} %collective-permute-done.13), channel_id=1, source_target_pairs={{8,0},{10,2},{12,4},{14,6},{16,24},{18,26},{20,28},{22,30},{9,1},{... | collective-permute-start | bytes 1572872 | tf_op jit(solution)/shard_map/ppermute | solution.py:216
  74.2 14.7 %collective-permute-start.23 = (bf16[128,2048]{1,0:T(8,128)(2,1)S(1)}, bf16[128,2048]{1,0:T(8,128)(2,1)S(1)}, u32[]{:S(2)}, u32[]{:S(2)}) collective-permute-start(bf16[128,2048]{1,0:T(8,128)(2,1)S(1)} %broadcast_select_fusion.1.refs_2_), channel_id=1, source_target_pairs={{0,4},{1,3},{2,6},{3,1},{4,0},{5,7},{6,2},{7,5},{8,12},{9,11},{10,... | collective-permute-start | bytes 1572872 | tf_op jit(solution)/shard_map/ppermute | solution.py:26
  75.7 13.2 %collective-permute-start.22 = (bf16[128,2048]{1,0:T(8,128)(2,1)S(1)}, bf16[128,2048]{1,0:T(8,128)(2,1)S(1)}, u32[]{:S(2)}, u32[]{:S(2)}) collective-permute-start(bf16[128,2048]{1,0:T(8,128)(2,1)S(1)} %broadcast_select_fusion.1.refs_2_), channel_id=1, source_target_pairs={{0,2},{1,5},{2,0},{3,7},{4,6},{5,1},{6,4},{7,3},{8,10},{9,13},{10,... | collective-permute-start | bytes 1572872 | tf_op jit(solution)/shard_map/ppermute | solution.py:26
  90.1 14.1 %collective-permute-start.24 = (bf16[128,2048]{1,0:T(8,128)(2,1)S(1)}, bf16[128,2048]{1,0:T(8,128)(2,1)S(1)}, u32[]{:S(2)}, u32[]{:S(2)}) collective-permute-start(bf16[128,2048]{1,0:T(8,128)(2,1)S(1)} %broadcast_select_fusion.refs_5_), channel_id=1, source_target_pairs={{0,2},{1,5},{2,0},{3,7},{4,6},{5,1},{6,4},{7,3},{8,10},{9,13},{10,... | collective-permute-start | bytes 1572872 | tf_op jit(solution)/shard_map/ppermute | solution.py:26
  90.8 13.6 %collective-permute-start.25 = (bf16[128,2048]{1,0:T(8,128)(2,1)S(1)}, bf16[128,2048]{1,0:T(8,128)(2,1)S(1)}, u32[]{:S(2)}, u32[]{:S(2)}) collective-permute-start(bf16[128,2048]{1,0:T(8,128)(2,1)S(1)} %broadcast_select_fusion.refs_5_), channel_id=1, source_target_pairs={{0,4},{1,3},{2,6},{3,1},{4,0},{5,7},{6,2},{7,5},{8,12},{9,11},{10,... | collective-permute-start | bytes 1572872 | tf_op jit(solution)/shard_map/ppermute | solution.py:26
  91.1 14.6 %collective-permute-start.26 = (bf16[128,2048]{1,0:T(8,128)(2,1)S(1)}, bf16[128,2048]{1,0:T(8,128)(2,1)S(1)}, u32[]{:S(2)}, u32[]{:S(2)}) collective-permute-start(bf16[128,2048]{1,0:T(8,128)(2,1)S(1)} %collective-permute-done.16.refs_1_), channel_id=1, source_target_pairs={{0,8},{2,10},{4,12},{6,14},{8,0},{10,2},{12,4},{14,6},{16,24},{18,... | collective-permute-start | bytes 1572872 | tf_op jit(solution)/shard_map/ppermute | solution.py:20
  104.1 13.2 %collective-permute-start.28 = (bf16[128,2048]{1,0:T(8,128)(2,1)S(1)}, bf16[128,2048]{1,0:T(8,128)(2,1)S(1)}, u32[]{:S(2)}, u32[]{:S(2)}) collective-permute-start(bf16[128,2048]{1,0:T(8,128)(2,1)S(1)} %collective-permute-done.23.refs_4_), channel_id=1, source_target_pairs={{0,2},{1,5},{2,0},{3,7},{4,6},{5,1},{6,4},{7,3},{8,10},{9,13},{10,... | collective-permute-start | bytes 1572872 | tf_op jit(solution)/shard_map/ppermute | solution.py:26
  104.4 12.9 %collective-permute-start.29 = (bf16[128,2048]{1,0:T(8,128)(2,1)S(1)}, bf16[128,2048]{1,0:T(8,128)(2,1)S(1)}, u32[]{:S(2)}, u32[]{:S(2)}) collective-permute-start(bf16[128,2048]{1,0:T(8,128)(2,1)S(1)} %collective-permute-done.24.refs_0_), channel_id=1, source_target_pairs={{0,4},{1,3},{2,6},{3,1},{4,0},{5,7},{6,2},{7,5},{8,12},{9,11},{10,... | collective-permute-start | bytes 1572872 | tf_op jit(solution)/shard_map/ppermute | solution.py:26
  105.7 17.4 %collective-permute-start.27 = (bf16[128,2048]{1,0:T(8,128)(2,1)S(1)}, bf16[128,2048]{1,0:T(8,128)(2,1)S(1)}, u32[]{:S(2)}, u32[]{:S(2)}) collective-permute-start(bf16[128,2048]{1,0:T(8,128)(2,1)S(1)} %collective-permute-done.18.refs_3_), channel_id=1, source_target_pairs={{0,8},{2,10},{4,12},{6,14},{8,0},{10,2},{12,4},{14,6},{16,24},{18,... | collective-permute-start | bytes 1572872 | tf_op jit(solution)/shard_map/ppermute | solution.py:20
  120.6 13.9 %collective-permute-start.32 = (bf16[128,2048]{1,0:T(8,128)(2,1)S(1)}, bf16[128,2048]{1,0:T(8,128)(2,1)S(1)}, u32[]{:S(2)}, u32[]{:S(2)}) collective-permute-start(bf16[128,2048]{1,0:T(8,128)(2,1)S(1)} %get-tuple-element.105), channel_id=1, source_target_pairs={{0,4},{1,3},{2,6},{3,1},{4,0},{5,7},{6,2},{7,5},{8,12},{9,11},{10,... | collective-permute-start | bytes 1572872 | tf_op jit(solution)/shard_map/ppermute | solution.py:26
  122.8 11.9 %collective-permute-start.33 = (bf16[128,2048]{1,0:T(8,128)(2,1)S(1)}, bf16[128,2048]{1,0:T(8,128)(2,1)S(1)}, u32[]{:S(2)}, u32[]{:S(2)}) collective-permute-start(bf16[128,2048]{1,0:T(8,128)(2,1)S(1)} %get-tuple-element.100), channel_id=1, source_target_pairs={{0,2},{1,5},{2,0},{3,7},{4,6},{5,1},{6,4},{7,3},{8,10},{9,13},{10,... | collective-permute-start | bytes 1572872 | tf_op jit(solution)/shard_map/ppermute | solution.py:26
  126.1 12.9 %collective-permute-start.30 = (bf16[128,2048]{1,0:T(8,128)(2,1)S(1)}, bf16[128,2048]{1,0:T(8,128)(2,1)S(1)}, u32[]{:S(2)}, u32[]{:S(2)}) collective-permute-start(bf16[128,2048]{1,0:T(8,128)(2,1)S(1)} %expert_rows.9), channel_id=1, source_target_pairs={{0,8},{2,10},{4,12},{6,14},{8,0},{10,2},{12,4},{14,6},{16,24},{18,... | collective-permute-start | bytes 1572872 | tf_op jit(solution)/shard_map/ppermute | solution.py:20
  134.7 14.6 %collective-permute-start.34 = (bf16[128,2048]{1,0:T(8,128)(2,1)S(1)}, bf16[128,2048]{1,0:T(8,128)(2,1)S(1)}, u32[]{:S(2)}, u32[]{:S(2)}) collective-permute-start(bf16[128,2048]{1,0:T(8,128)(2,1)S(1)} %add_convert_fusion.7), channel_id=1, source_target_pairs={{0,2},{1,5},{2,0},{3,7},{4,6},{5,1},{6,4},{7,3},{8,10},{9,13},{10,... | collective-permute-start | bytes 1572872 | tf_op jit(solution)/shard_map/ppermute | solution.py:26
  135.9 14.0 %collective-permute-start.38 = (bf16[128,2048]{1,0:T(8,128)(2,1)S(1)}, bf16[128,2048]{1,0:T(8,128)(2,1)S(1)}, u32[]{:S(2)}, u32[]{:S(2)}) collective-permute-start(bf16[128,2048]{1,0:T(8,128)(2,1)S(1)} %get-tuple-element.114), channel_id=1, source_target_pairs={{0,4},{1,3},{2,6},{3,1},{4,0},{5,7},{6,2},{7,5},{8,12},{9,11},{10,... | collective-permute-start | bytes 1572872 | tf_op jit(solution)/shard_map/ppermute | solution.py:26
  139.0 13.1 %collective-permute-start.31 = (bf16[128,2048]{1,0:T(8,128)(2,1)S(1)}, bf16[128,2048]{1,0:T(8,128)(2,1)S(1)}, u32[]{:S(2)}, u32[]{:S(2)}) collective-permute-start(bf16[128,2048]{1,0:T(8,128)(2,1)S(1)} %get-tuple-element.102), channel_id=1, source_target_pairs={{0,8},{2,10},{4,12},{6,14},{8,0},{10,2},{12,4},{14,6},{16,24},{18,... | collective-permute-start | bytes 1572872 | tf_op jit(solution)/shard_map/ppermute | solution.py:20
  149.2 14.3 %collective-permute-start.35 = (bf16[128,2048]{1,0:T(8,128)(2,1)S(1)}, bf16[128,2048]{1,0:T(8,128)(2,1)S(1)}, u32[]{:S(2)}, u32[]{:S(2)}) collective-permute-start(bf16[128,2048]{1,0:T(8,128)(2,1)S(1)} %get-tuple-element.107), channel_id=1, source_target_pairs={{0,2},{1,5},{2,0},{3,7},{4,6},{5,1},{6,4},{7,3},{8,10},{9,13},{10,... | collective-permute-start | bytes 1572872 | tf_op jit(solution)/shard_map/ppermute | solution.py:26
  149.8 14.8 %collective-permute-start.39 = (bf16[128,2048]{1,0:T(8,128)(2,1)S(1)}, bf16[128,2048]{1,0:T(8,128)(2,1)S(1)}, u32[]{:S(2)}, u32[]{:S(2)}) collective-permute-start(bf16[128,2048]{1,0:T(8,128)(2,1)S(1)} %add_convert_fusion.5), channel_id=1, source_target_pairs={{0,4},{1,3},{2,6},{3,1},{4,0},{5,7},{6,2},{7,5},{8,12},{9,11},{10,... | collective-permute-start | bytes 1572872 | tf_op jit(solution)/shard_map/ppermute | solution.py:26
  152.1 14.4 %collective-permute-start.42 = (bf16[128,2048]{1,0:T(8,128)(2,1)S(1)}, bf16[128,2048]{1,0:T(8,128)(2,1)S(1)}, u32[]{:S(2)}, u32[]{:S(2)}) collective-permute-start(bf16[128,2048]{1,0:T(8,128)(2,1)S(1)} %add_convert_fusion.4), channel_id=1, source_target_pairs={{0,8},{2,10},{4,12},{6,14},{24,16},{26,18},{28,20},{30,22},{1,9},{... | collective-permute-start | bytes 1572872 | tf_op jit(solution)/shard_map/ppermute | solution.py:216
  163.5 13.5 %collective-permute-start.36 = (bf16[128,2048]{1,0:T(8,128)(2,1)S(1)}, bf16[128,2048]{1,0:T(8,128)(2,1)S(1)}, u32[]{:S(2)}, u32[]{:S(2)}) collective-permute-start(bf16[128,2048]{1,0:T(8,128)(2,1)S(1)} %add_convert_fusion.8), channel_id=1, source_target_pairs={{0,2},{1,5},{2,0},{3,7},{4,6},{5,1},{6,4},{7,3},{8,10},{9,13},{10,... | collective-permute-start | bytes 1572872 | tf_op jit(solution)/shard_map/ppermute | solution.py:26
  164.6 14.1 %collective-permute-start.40 = (bf16[128,2048]{1,0:T(8,128)(2,1)S(1)}, bf16[128,2048]{1,0:T(8,128)(2,1)S(1)}, u32[]{:S(2)}, u32[]{:S(2)}) collective-permute-start(bf16[128,2048]{1,0:T(8,128)(2,1)S(1)} %get-tuple-element.116), channel_id=1, source_target_pairs={{0,4},{1,3},{2,6},{3,1},{4,0},{5,7},{6,2},{7,5},{8,12},{9,11},{10,... | collective-permute-start | bytes 1572872 | tf_op jit(solution)/shard_map/ppermute | solution.py:26
  166.9 13.7 %collective-permute-start.43 = (bf16[128,2048]{1,0:T(8,128)(2,1)S(1)}, bf16[128,2048]{1,0:T(8,128)(2,1)S(1)}, u32[]{:S(2)}, u32[]{:S(2)}) collective-permute-start(bf16[128,2048]{1,0:T(8,128)(2,1)S(1)} %add_convert_fusion.3), channel_id=1, source_target_pairs={{8,16},{10,18},{12,20},{14,22},{16,8},{18,10},{20,12},{22,14},{9,1... | collective-permute-start | bytes 1572872 | tf_op jit(solution)/shard_map/ppermute | solution.py:216
  168.9 13.7 %collective-permute-start.45 = (bf16[128,2048]{1,0:T(8,128)(2,1)S(1)}, bf16[128,2048]{1,0:T(8,128)(2,1)S(1)}, u32[]{:S(2)}, u32[]{:S(2)}) collective-permute-start(bf16[128,2048]{1,0:T(8,128)(2,1)S(1)} %add_convert_fusion.3), channel_id=1, source_target_pairs={{0,8},{2,10},{4,12},{6,14},{24,16},{26,18},{28,20},{30,22},{1,9},{... | collective-permute-start | bytes 1572872 | tf_op jit(solution)/shard_map/ppermute | solution.py:216
  177.0 13.0 %collective-permute-start.37 = (bf16[128,2048]{1,0:T(8,128)(2,1)S(1)}, bf16[128,2048]{1,0:T(8,128)(2,1)S(1)}, u32[]{:S(2)}, u32[]{:S(2)}) collective-permute-start(bf16[128,2048]{1,0:T(8,128)(2,1)S(1)} %add_convert_fusion.9), channel_id=1, source_target_pairs={{0,2},{1,5},{2,0},{3,7},{4,6},{5,1},{6,4},{7,3},{8,10},{9,13},{10,... | collective-permute-start | bytes 1572872 | tf_op jit(solution)/shard_map/ppermute | solution.py:26
  178.7 18.0 %copy-start.4 = (f32[128,2048]{1,0:T(8,128)S(1)}, f32[128,2048]{1,0:T(8,128)}, u32[]{:S(2)}) copy-start(f32[128,2048]{1,0:T(8,128)} %get-tuple-element.68) | copy-start | bytes 3145732
  178.7 11.2 %collective-permute-start.41 = (bf16[128,2048]{1,0:T(8,128)(2,1)S(1)}, bf16[128,2048]{1,0:T(8,128)(2,1)S(1)}, u32[]{:S(2)}, u32[]{:S(2)}) collective-permute-start(bf16[128,2048]{1,0:T(8,128)(2,1)S(1)} %add_convert_fusion.6), channel_id=1, source_target_pairs={{0,4},{1,3},{2,6},{3,1},{4,0},{5,7},{6,2},{7,5},{8,12},{9,11},{10,... | collective-permute-start | bytes 1572872 | tf_op jit(solution)/shard_map/ppermute | solution.py:26
  182.7 12.8 %collective-permute-start.46 = (bf16[128,2048]{1,0:T(8,128)(2,1)S(1)}, bf16[128,2048]{1,0:T(8,128)(2,1)S(1)}, u32[]{:S(2)}, u32[]{:S(2)}) collective-permute-start(bf16[128,2048]{1,0:T(8,128)(2,1)S(1)} %add_convert_fusion.1), channel_id=1, source_target_pairs={{8,16},{10,18},{12,20},{14,22},{16,8},{18,10},{20,12},{22,14},{9,1... | collective-permute-start | bytes 1572872 | tf_op jit(solution)/shard_map/ppermute | solution.py:216
  186.4 10.4 %collective-permute-start.44 = (bf16[128,2048]{1,0:T(8,128)(2,1)S(1)}, bf16[128,2048]{1,0:T(8,128)(2,1)S(1)}, u32[]{:S(2)}, u32[]{:S(2)}) collective-permute-start(bf16[128,2048]{1,0:T(8,128)(2,1)S(1)} %add_convert_fusion.2), channel_id=1, source_target_pairs={{0,8},{2,10},{4,12},{6,14},{8,0},{10,2},{12,4},{14,6},{16,24},{18,... | collective-permute-start | bytes 1572872 | tf_op jit(solution)/shard_map/ppermute | solution.py:20
  (9 other events, 43.8 us)

commit v13 on v11

--- a/solution.py
+++ b/solution.py
@@ -179,8 +179,9 @@
         act = (gate / (1.0 + jnp.exp(-gate)) * up).astype(jnp.bfloat16)
         result = jnp.dot(act, down[...], preferred_element_type=jnp.float32)
         for i in group:
-            here, other = (gates_at(place, rows, gates) for place in places[i])
-            here = jnp.where(where_ref[1] == 1, other, here)
+            here = gates_at(places[i][0], rows, gates)
+            if places[i][0] != places[i][1]:
+                here = jnp.where(where_ref[1] == 1, gates_at(places[i][1], rows, gates), here)
             expert = lax.broadcasted_iota(jnp.int32, here.shape, 0)
             chosen = jnp.sum(jnp.where(expert == where_ref[0], here, 0.0), axis=0, keepdims=True)
             chosen = jnp.transpose(jnp.broadcast_to(chosen, (rows, rows)))[:, :1]
@@ -248,16 +249,16 @@
     d2, d3 = cross(after(y2, x3, p1), X), cross(after(x3, y3, p1), Y)
     px3, py3, px1 = run([after(x3, p1), y3, x1], (plane(X, 12), plane(Y, 12), plane(X, 4)))
 
+    to_x0 = flip(after(px1, d1), 4)
     pd2, pd3 = run([after(d2, px3), d3], (11, 15))
     (pd1,) = run([after(d1, pd2)], (7,))
-    to_x3, to_y2, to_d0 = cross(pd3, Y), cross(pd2, X), flip(pd1, 4)
-
-    px3, py2, pd0 = add_small(px3, to_x3), add_small(py2, to_y2), add_small(pd0, to_d0)
+    to_x3, to_y2, to_d0 = cross(pd3, Y), cross(pd2, X), flip(after(pd1, to_x0), 4)
+
+    px3, py2, px0 = add_small(px3, to_x3), add_small(py2, to_y2), add_small(px0, to_x0)
     by_x, by_y = cross(after(px3, to_y2), X), cross(after(py3, to_x3), Y)
-    to_x0 = flip(after(px1, to_d0), 4)
-
-    p3, px0 = add_small(p3, by_x, by_y), add_small(px0, to_x0)
-    to_2 = shift(after(p3, to_x0), INWARD)
+
+    p3, pd0 = add_small(p3, by_x, by_y), add_small(pd0, to_d0)
+    to_2 = shift(after(p3, to_d0), INWARD)
     by_x, by_y = cross(after(px2, by_x), X), cross(after(py2, by_y), Y)
 
     p2 = add_small(p2, by_x, by_y, to_2)

time: 188 us -> 186 us (0.989)
  waiting for transfers between devices: 77.1 us -> 74.8 us
    ppermute x8, waiting for transfers between devices: 12.4 us -> 9.69 us  [shift(): lax.ppermute(block, 'seq', [(4 * a + i, 4 * b + i) for a, b in pairs for...]
  transfers between devices with their start and end apart: 47 -> 47, of which waited for: 22 -> 24; matrix products, arithmetic and copies ran while one was open for 3% -> 3% of each run, Pallas kernels for 17% -> 18%
where the time goes in v13:
time: 186 us; the launch traced here: 185 us
  waiting for transfers between devices  74.8 us (40%)
  starting transfers between devices  60.8 us (33%)
  Pallas kernels  37.1 us (20%)
  local copies, waits for them, and re-layouts  6.87 us (4%)
  other arithmetic  5.45 us (3%)
    ppermute x20, waiting for transfers between devices, cross(): return lax.ppermute(block, ('seq', 'exp'), pairs)  43.5 us
    pallas_call x5, Pallas kernels, expert(): pl.pallas_call(functools.partial(expert_kernel, places, len(gates)), out_...  25.5 us
    ppermute x8, starting transfers between devices, shift(): lax.ppermute(block, 'seq', [(4 * a + i, 4 * b + i) for a, b in pairs for...  22.2 us
    ppermute x20, starting transfers between devices, cross(): return lax.ppermute(block, ('seq', 'exp'), pairs)  21 us
    ppermute x12, waiting for transfers between devices, flip(): return lax.ppermute(block, 'seq', [(i, i ^ mask) for i in range(count)])  20.1 us
    ppermute x12, starting transfers between devices, flip(): return lax.ppermute(block, 'seq', [(i, i ^ mask) for i in range(count)])  10.5 us
    ppermute x8, waiting for transfers between devices, shift(): lax.ppermute(block, 'seq', [(4 * a + i, 4 * b + i) for a, b in pairs for...  9.69 us
    ppermute x2, starting transfers between devices, halo(): return (beside, part, lax.ppermute(beside, 'seq', ahead + back))  6.6 us
  transfers between devices with their start and end apart: 47, of which 24 were waited for; matrix products, arithmetic and copies ran while one was open for 3% of the time, Pallas kernels for 18%

profile of v13, /device:TPU:10, one launch (start us, length us, event | category | flops | bytes accessed | tf_op | source)
XLA Modules:
  0.0 185.4 jit_solution(17565898834827526431)
XLA Ops:
  0.5 1.5 collective-permute-start.2
  3.3 3.2 %collective-permute-done.7.refs_5_.refs_7_.refs_4_.refs_3_.refs_2_ = f32[16,128]{1,0:T(8,128)S(1)} collective-permute-done((f32[16,128]{1,0:T(8,128)S(1)}, f32[16,128]{1,0:T(8,128)S(1)}, u32[]{:S(2)}, u32[]{:S(2)}) %collective-permute-start.7) | collective-permute-done | bytes 8224 | tf_op jit(solution)/shard_map/ppermute | solution.py:20
  6.5 2.6 %collective-permute-start.8 = (f32[16,256]{1,0:T(8,128)S(1)}, f32[16,256]{1,0:T(8,128)S(1)}, u32[]{:S(2)}, u32[]{:S(2)}) collective-permute-start(f32[16,256]{1,0:T(8,128)S(1)} %pad_maximum_fusion.2), channel_id=1, source_target_pairs={{0,16},{2,18},{4,20},{6,22},{8,24},{10,26},{12,28},{14,30},{16,0},... | collective-permute-start | bytes 49160 | tf_op jit(solution)/shard_map/ppermute | solution.py:20
  9.3 3.3 %collective-permute-start.1 = (bf16[256,512]{1,0:T(8,128)(2,1)S(1)}, bf16[256,512]{1,0:T(8,128)(2,1)S(1)}, u32[]{:S(2)}, u32[]{:S(2)}) collective-permute-start(bf16[256,512]{1,0:T(8,128)(2,1)S(1)} %collective-permute-done.refs_0_), channel_id=1, source_target_pairs={{0,4},{4,8},{8,12},{12,16},{16,20},{20,24},{24,28},{6,2},{10,6},{1... | collective-permute-start | bytes 786440 | tf_op jit(solution)/shard_map/ppermute | solution.py:330
  12.6 1.9 %collective-permute-done.2.refs_3_ = bf16[256,512]{1,0:T(8,128)(2,1)S(1)} collective-permute-done((bf16[256,512]{1,0:T(8,128)(2,1)}, bf16[256,512]{1,0:T(8,128)(2,1)S(1)}, u32[]{:S(2)}, u32[]{:S(2)}) %collective-permute-start.2) | collective-permute-done | bytes 262176 | tf_op jit(solution)/shard_map/ppermute | solution.py:20
  14.6 3.3 %collective-permute-start.3 = (bf16[256,512]{1,0:T(8,128)(2,1)S(1)}, bf16[256,512]{1,0:T(8,128)(2,1)S(1)}, u32[]{:S(2)}, u32[]{:S(2)}) collective-permute-start(bf16[256,512]{1,0:T(8,128)(2,1)S(1)} %collective-permute-done.2.refs_3_), channel_id=1, source_target_pairs={{0,4},{4,8},{8,12},{12,16},{16,20},{20,24},{24,28},{6,2},{10,6},{1... | collective-permute-start | bytes 786440 | tf_op jit(solution)/shard_map/ppermute | solution.py:330
  20.5 4.5 %collective-permute-done.9.refs_7_.refs_9_.refs_6_.refs_5_.refs_4_ = f32[16,512]{1,0:T(8,128)S(1)} collective-permute-done((f32[16,512]{1,0:T(8,128)S(1)}, f32[16,512]{1,0:T(8,128)S(1)}, u32[]{:S(2)}, u32[]{:S(2)}) %collective-permute-start.9) | collective-permute-done | bytes 32800 | tf_op jit(solution)/shard_map/ppermute | solution.py:20
  26.4 4.6 %window_attention.1 = (bf16[128,512]{1,0:T(8,128)(2,1)}, bf16[128,512]{1,0:T(8,128)(2,1)}) custom-call(s32[2]{0:T(128)} %pad_add_fusion.where_ref, bf16[256,512]{1,0:T(8,128)(2,1)} %q_ref.1, s32[1,768]{1,0:T(1,128)} %broadcast_in_dim.21.ids_ref, bf16[256,512]{1,0:T(8,128)(2,1)} %copy-done.5, bf16[256,512]{1,0:T(8,128)(2,1)} %refs_1_.1, ...), custom_call_target="tpu_custom_call" | custom-call | tf_op jit(solution)/shard_map/window_attention/pallas_call | solution.py:97
  33.2 4.3 %project_and_norm.1 = (f32[128,2048]{1,0:T(8,128)}, bf16[128,2048]{1,0:T(8,128)(2,1)}) custom-call(bf16[128,512]{1,0:T(8,128)(2,1)} %get-tuple-element.65.mine_ref, bf16[128,512]{1,0:T(8,128)(2,1)} %copy-done.9, bf16[512,2048]{1,0:T(8,128)(2,1)} %own_w.1, bf16[512,2048]{1,0:T(8,128)(2,1)} %collective-permute-done.4.refs_6_.other_w, ...), custom_call_target="tpu_custom_call" | custom-call | tf_op jit(solution)/shard_map/project_and_norm/pallas_call | solution.py:120
  37.9 4.6 %collective-permute-start.14 = (bf16[128,2048]{1,0:T(8,128)(2,1)}, bf16[128,2048]{1,0:T(8,128)(2,1)S(1)}, u32[]{:S(2)}, u32[]{:S(2)}) collective-permute-start(bf16[128,2048]{1,0:T(8,128)(2,1)} %get-tuple-element.71.refs_0_), channel_id=1, source_target_pairs={{8,16},{10,18},{12,20},{14,22},{16,8},{18,10},{20,12},{22,14},{9,1... | collective-permute-start | bytes 1572872 | tf_op jit(solution)/shard_map/ppermute | solution.py:217
  43.4 1.2 collective-permute-start.16
  44.6 7.0 %collective-permute-done.12.refs_0_ = bf16[128,2048]{1,0:T(8,128)(2,1)S(1)} collective-permute-done((bf16[128,2048]{1,0:T(8,128)(2,1)}, bf16[128,2048]{1,0:T(8,128)(2,1)S(1)}, u32[]{:S(2)}, u32[]{:S(2)}) %collective-permute-start.12) | collective-permute-done | bytes 524320 | tf_op jit(solution)/shard_map/ppermute | solution.py:20
  51.6 3.5 %collective-permute-start.13 = (bf16[128,2048]{1,0:T(8,128)(2,1)S(1)}, bf16[128,2048]{1,0:T(8,128)(2,1)}, u32[]{:S(2)}, u32[]{:S(2)}) collective-permute-start(bf16[128,2048]{1,0:T(8,128)(2,1)S(1)} %collective-permute-done.12.refs_0_), channel_id=1, source_target_pairs={{8,16},{10,18},{12,20},{14,22},{16,8},{18,10},{20,12},{22,14},{9,1... | collective-permute-start | bytes 1572872 | tf_op jit(solution)/shard_map/ppermute | solution.py:217
  55.1 2.1 %collective-permute-start.15 = (bf16[128,2048]{1,0:T(8,128)(2,1)S(1)}, bf16[128,2048]{1,0:T(8,128)(2,1)}, u32[]{:S(2)}, u32[]{:S(2)}) collective-permute-start(bf16[128,2048]{1,0:T(8,128)(2,1)S(1)} %collective-permute-done.14), channel_id=1, source_target_pairs={{8,0},{10,2},{12,4},{14,6},{16,24},{18,26},{20,28},{22,30},{9,1},{... | collective-permute-start | bytes 1572872 | tf_op jit(solution)/shard_map/ppermute | solution.py:217
  57.4 1.3 collective-permute-start.18
  59.7 2.0 %collective-permute-start.19 = (f32[16,1024]{1,0:T(8,128)S(1)}, f32[16,1024]{1,0:T(8,128)S(1)}, u32[]{:S(2)}, u32[]{:S(2)}) collective-permute-start(f32[16,1024]{1,0:T(8,128)S(1)} %pad_maximum_fusion), channel_id=1, source_target_pairs={{0,2},{2,0},{4,6},{6,4},{8,10},{10,8},{12,14},{14,12},{16,18},{18,... | collective-permute-start | bytes 196616 | tf_op jit(solution)/shard_map/ppermute | solution.py:20
  61.7 1.4 copy-done
  63.1 1.4 copy-done.1
  64.4 1.4 copy-done.2
  65.8 2.6 %assemble_weights.1 = (bf16[1408,2048]{1,0:T(8,128)(2,1)S(1)}, bf16[704,2048]{1,0:T(8,128)(2,1)S(1)}) custom-call(bf16[352,2048]{1,0:T(8,128)(2,1)S(1)} %bitcast.14, bf16[352,2048]{1,0:T(8,128)(2,1)} %collective-permute-done.5.refs_7_.refs_1_, bf16[352,2048]{1,0:T(8,128)(2,1)S(1)} %bitcast.16, bf16[352,2048]{1,0:T(8,128)(2,1)} %collective-permute-done.10.refs_0_.refs_3_, ...), custom_call_target="tpu_custom_call" | custom-call | tf_op jit(solution)/shard_map/assemble_weights/pallas_call | solution.py:148
  68.5 3.3 %collective-permute-start.23 = (bf16[128,2048]{1,0:T(8,128)(2,1)}, bf16[128,2048]{1,0:T(8,128)(2,1)S(1)}, u32[]{:S(2)}, u32[]{:S(2)}) collective-permute-start(bf16[128,2048]{1,0:T(8,128)(2,1)} %collective-permute-done.13), channel_id=1, source_target_pairs={{8,0},{10,2},{12,4},{14,6},{16,24},{18,26},{20,28},{22,30},{9,1},{... | collective-permute-start | bytes 1572872 | tf_op jit(solution)/shard_map/ppermute | solution.py:217
  72.9 1.5 collective-permute-start.21
  75.6 5.6 %expert_rows.5 = (bf16[128,2048]{1,0:T(8,128)(2,1)S(1)}, bf16[128,2048]{1,0:T(8,128)(2,1)S(1)}, bf16[128,2048]{1,0:T(8,128)(2,1)S(1)}, bf16[128,2048]{1,0:T(8,128)(2,1)S(1)}) custom-call(s32[2]{0:T(128)S(1)} %pad_add_fusion.1.where_ref, bf16[128,2048]{1,0:T(8,128)(2,1)S(1)} %copy-done.3, bf16[128,2048]{1,0:T(8,128)(2,1)S(1)} %collective-permute-done.16.refs_1_, ...), custom_call_target="tpu_custom_call" | custom-call | tf_op jit(solution)/shard_map/expert_rows/pallas_call | solution.py:195
  81.7 5.4 %collective-permute-done.21.refs_3_ = bf16[128,2048]{1,0:T(8,128)(2,1)S(1)} collective-permute-done((bf16[128,2048]{1,0:T(8,128)(2,1)S(1)}, bf16[128,2048]{1,0:T(8,128)(2,1)S(1)}, u32[]{:S(2)}, u32[]{:S(2)}) %collective-permute-start.21) | collective-permute-done | bytes 524320 | tf_op jit(solution)/shard_map/ppermute | solution.py:26
  88.1 8.1 %expert_rows.6 = (bf16[128,2048]{1,0:T(8,128)(2,1)S(1)}, bf16[128,2048]{1,0:T(8,128)(2,1)S(1)}, bf16[128,2048]{1,0:T(8,128)(2,1)S(1)}, bf16[128,2048]{1,0:T(8,12...) custom-call(s32[2]{0:T(128)S(1)} %pad_add_fusion.1.where_ref, ...), custom_call_target="tpu_custom_call" | custom-call | tf_op jit(solution)/shard_map/expert_rows/pallas_call | solution.py:195
  96.2 4.1 %collective-permute-done.24.refs_0_ = bf16[128,2048]{1,0:T(8,128)(2,1)S(1)} collective-permute-done((bf16[128,2048]{1,0:T(8,128)(2,1)S(1)}, bf16[128,2048]{1,0:T(8,128)(2,1)S(1)}, u32[]{:S(2)}, u32[]{:S(2)}) %collective-permute-start.24) | collective-permute-done | bytes 524320 | tf_op jit(solution)/shard_map/ppermute | solution.py:26
  101.4 5.6 %expert_rows.7 = (bf16[128,2048]{1,0:T(8,128)(2,1)S(1)}, bf16[128,2048]{1,0:T(8,128)(2,1)S(1)}, bf16[128,2048]{1,0:T(8,128)(2,1)S(1)}) custom-call(s32[2]{0:T(128)S(1)} %pad_add_fusion.1.where_ref, bf16[128,2048]{1,0:T(8,128)(2,1)S(1)} %collective-permute-done.24.refs_0_, bf16[128,2048]{1,0:T(8,128)(2,1)S(1)} %collective-permute-done.26.refs_1_, ...), custom_call_target="tpu_custom_call" | custom-call | tf_op jit(solution)/shard_map/expert_rows/pallas_call | solution.py:195
  107.0 5.7 %collective-permute-done.25.refs_0_ = bf16[128,2048]{1,0:T(8,128)(2,1)S(1)} collective-permute-done((bf16[128,2048]{1,0:T(8,128)(2,1)S(1)}, bf16[128,2048]{1,0:T(8,128)(2,1)S(1)}, u32[]{:S(2)}, u32[]{:S(2)}) %collective-permute-start.25) | collective-permute-done | bytes 524320 | tf_op jit(solution)/shard_map/ppermute | solution.py:26
  112.7 3.2 %expert_rows.8 = (bf16[128,2048]{1,0:T(8,128)(2,1)S(1)}, bf16[128,2048]{1,0:T(8,128)(2,1)S(1)}) custom-call(s32[2]{0:T(128)S(1)} %pad_add_fusion.1.where_ref, bf16[128,2048]{1,0:T(8,128)(2,1)S(1)} %collective-permute-done.25.refs_0_, bf16[128,2048]{1,0:T(8,128)(2,1)S(1)} %collective-permute-done.28.refs_1_, ...), custom_call_target="tpu_custom_call" | custom-call | tf_op jit(solution)/shard_map/expert_rows/pallas_call | solution.py:195
  117.1 11.0 %collective-permute-done.30 = bf16[128,2048]{1,0:T(8,128)(2,1)S(1)} collective-permute-done((bf16[128,2048]{1,0:T(8,128)(2,1)S(1)}, bf16[128,2048]{1,0:T(8,128)(2,1)S(1)}, u32[]{:S(2)}, u32[]{:S(2)}) %collective-permute-start.30) | collective-permute-done | bytes 524320 | tf_op jit(solution)/shard_map/ppermute | solution.py:26
  128.2 1.1 collective-permute-start.34
  129.6 2.9 %expert_rows.9 = bf16[128,2048]{1,0:T(8,128)(2,1)S(1)} custom-call(s32[2]{0:T(128)S(1)} %pad_add_fusion.1.where_ref, bf16[128,2048]{1,0:T(8,128)(2,1)S(1)} %collective-permute-done.36.refs_0_, f32[16,128]{1,0:T(8,128)S(1)} %select_reduce_fusion.refs_4_.refs_6_.refs_3_.refs_2_.refs_1_, ...), custom_call_target="tpu_custom_call" | custom-call | tf_op jit(solution)/shard_map/expert_rows/pallas_call | solution.py:195
  133.5 6.2 %collective-permute-done.34 = bf16[128,2048]{1,0:T(8,128)(2,1)S(1)} collective-permute-done((bf16[128,2048]{1,0:T(8,128)(2,1)S(1)}, bf16[128,2048]{1,0:T(8,128)(2,1)S(1)}, u32[]{:S(2)}, u32[]{:S(2)}) %collective-permute-start.34) | collective-permute-done | bytes 524320 | tf_op jit(solution)/shard_map/ppermute | solution.py:26
  139.7 1.7 collective-permute-start.35
  141.4 1.4 collective-permute-start.32
  144.1 1.3 collective-permute-start.39
  145.6 6.2 %collective-permute-done.35 = bf16[128,2048]{1,0:T(8,128)(2,1)S(1)} collective-permute-done((bf16[128,2048]{1,0:T(8,128)(2,1)S(1)}, bf16[128,2048]{1,0:T(8,128)(2,1)S(1)}, u32[]{:S(2)}, u32[]{:S(2)}) %collective-permute-start.35) | collective-permute-done | bytes 524320 | tf_op jit(solution)/shard_map/ppermute | solution.py:26
  151.8 1.7 collective-permute-start.44
  154.3 2.5 %collective-permute-start.33 = (bf16[128,2048]{1,0:T(8,128)(2,1)S(1)}, bf16[128,2048]{1,0:T(8,128)(2,1)S(1)}, u32[]{:S(2)}, u32[]{:S(2)}) collective-permute-start(bf16[128,2048]{1,0:T(8,128)(2,1)S(1)} %get-tuple-element.104), channel_id=1, source_target_pairs={{0,4},{1,3},{2,6},{3,1},{4,0},{5,7},{6,2},{7,5},{8,12},{9,11},{10,... | collective-permute-start | bytes 1572872 | tf_op jit(solution)/shard_map/ppermute | solution.py:26
  157.1 1.9 %collective-permute-start.40 = (bf16[128,2048]{1,0:T(8,128)(2,1)S(1)}, bf16[128,2048]{1,0:T(8,128)(2,1)S(1)}, u32[]{:S(2)}, u32[]{:S(2)}) collective-permute-start(bf16[128,2048]{1,0:T(8,128)(2,1)S(1)} %add_convert_fusion.6), channel_id=1, source_target_pairs={{8,16},{10,18},{12,20},{14,22},{16,8},{18,10},{20,12},{22,14},{9,1... | collective-permute-start | bytes 1572872 | tf_op jit(solution)/shard_map/ppermute | solution.py:217
  159.2 1.3 collective-permute-start.41
  160.5 3.4 %collective-permute-done.44 = bf16[128,2048]{1,0:T(8,128)(2,1)S(1)} collective-permute-done((bf16[128,2048]{1,0:T(8,128)(2,1)S(1)}, bf16[128,2048]{1,0:T(8,128)(2,1)S(1)}, u32[]{:S(2)}, u32[]{:S(2)}) %collective-permute-start.44) | collective-permute-done | bytes 524320 | tf_op jit(solution)/shard_map/ppermute | solution.py:26
  164.1 2.3 %collective-permute-start.46 = (bf16[128,2048]{1,0:T(8,128)(2,1)S(1)}, bf16[128,2048]{1,0:T(8,128)(2,1)S(1)}, u32[]{:S(2)}, u32[]{:S(2)}) collective-permute-start(bf16[128,2048]{1,0:T(8,128)(2,1)S(1)} %add_convert_fusion.1), channel_id=1, source_target_pairs={{0,4},{1,3},{2,6},{3,1},{4,0},{5,7},{6,2},{7,5},{8,12},{9,11},{10,... | collective-permute-start | bytes 1572872 | tf_op jit(solution)/shard_map/ppermute | solution.py:26
  168.7 1.8 collective-permute-done.41
  170.7 4.2 %collective-permute-start.43 = (bf16[128,2048]{1,0:T(8,128)(2,1)S(1)}, bf16[128,2048]{1,0:T(8,128)(2,1)S(1)}, u32[]{:S(2)}, u32[]{:S(2)}) collective-permute-start(bf16[128,2048]{1,0:T(8,128)(2,1)S(1)} %add_convert_fusion.4), channel_id=1, source_target_pairs={{8,16},{10,18},{12,20},{14,22},{16,8},{18,10},{20,12},{22,14},{9,1... | collective-permute-start | bytes 1572872 | tf_op jit(solution)/shard_map/ppermute | solution.py:217
  175.5 6.5 %collective-permute-done.43 = bf16[128,2048]{1,0:T(8,128)(2,1)S(1)} collective-permute-done((bf16[128,2048]{1,0:T(8,128)(2,1)S(1)}, bf16[128,2048]{1,0:T(8,128)(2,1)S(1)}, u32[]{:S(2)}, u32[]{:S(2)}) %collective-permute-start.43) | collective-permute-done | bytes 524320 | tf_op jit(solution)/shard_map/ppermute | solution.py:217
  182.0 2.1 %collective-permute-done.42 = bf16[128,2048]{1,0:T(8,128)(2,1)S(1)} collective-permute-done((bf16[128,2048]{1,0:T(8,128)(2,1)S(1)}, bf16[128,2048]{1,0:T(8,128)(2,1)S(1)}, u32[]{:S(2)}, u32[]{:S(2)}) %collective-permute-start.42) | collective-permute-done | bytes 524320 | tf_op jit(solution)/shard_map/ppermute | solution.py:20
  184.1 1.3 add_convert_fusion
  (94 shorter events, 23.8 us)
Async XLA Ops:
  0.0 26.3 %collective-permute-start.4 = (bf16[512,2048]{1,0:T(8,128)(2,1)}, bf16[512,2048]{1,0:T(8,128)(2,1)}, u32[]{:S(2)}, u32[]{:S(2)}) collective-permute-start(bf16[512,2048]{1,0:T(8,128)(2,1)} %own_w.1), channel_id=1, source_target_pairs={{0,1},{1,0},{2,3},{3,2},{4,5},{5,4},{6,7},{7,6},{8,9},{9,8},{10,11... | collective-permute-start | bytes 6291464 | tf_op jit(solution)/shard_map/ppermute | solution.py:339
  0.0 9.3 %collective-permute-start = (bf16[256,512]{1,0:T(8,128)(2,1)}, bf16[256,512]{1,0:T(8,128)(2,1)S(1)}, u32[]{:S(2)}, u32[]{:S(2)}) collective-permute-start(bf16[256,512]{1,0:T(8,128)(2,1)} %refs_1_.1), channel_id=1, source_target_pairs={{0,2},{2,0},{4,6},{6,4},{8,10},{10,8},{12,14},{14,12},{16,18},{18,... | collective-permute-start | bytes 786440 | tf_op jit(solution)/shard_map/ppermute | solution.py:20
  0.5 14.0 %collective-permute-start.2 = (bf16[256,512]{1,0:T(8,128)(2,1)}, bf16[256,512]{1,0:T(8,128)(2,1)S(1)}, u32[]{:S(2)}, u32[]{:S(2)}) collective-permute-start(bf16[256,512]{1,0:T(8,128)(2,1)} %refs_4_.1), channel_id=1, source_target_pairs={{0,2},{2,0},{4,6},{6,4},{8,10},{10,8},{12,14},{14,12},{16,18},{18,... | collective-permute-start | bytes 786440 | tf_op jit(solution)/shard_map/ppermute | solution.py:20
  2.7 3.7 %collective-permute-start.7 = (f32[16,128]{1,0:T(8,128)S(1)}, f32[16,128]{1,0:T(8,128)S(1)}, u32[]{:S(2)}, u32[]{:S(2)}) collective-permute-start(f32[16,128]{1,0:T(8,128)S(1)} %select_reduce_fusion.refs_4_.refs_6_.refs_3_.refs_2_.refs_1_), channel_id=1, source_target_pairs={{0,8},{2,10},{4,12},{6,14},{8,0},{10,2},{12,4},{14,6},{16,24},{18,... | collective-permute-start | bytes 24584 | tf_op jit(solution)/shard_map/ppermute | solution.py:20
  3.3 23.1 %collective-permute-start.5 = (bf16[352,2048]{1,0:T(8,128)(2,1)}, bf16[352,2048]{1,0:T(8,128)(2,1)}, u32[]{:S(2)}, u32[]{:S(2)}) collective-permute-start(bf16[352,2048]{1,0:T(8,128)(2,1)} %bitcast.13), channel_id=1, source_target_pairs={{0,1},{1,0},{2,3},{3,2},{4,5},{5,4},{6,7},{7,6},{8,9},{9,8},{10,11... | collective-permute-start | bytes 4325384 | tf_op jit(solution)/shard_map/ppermute | solution.py:341
  6.5 12.2 %collective-permute-start.8 = (f32[16,256]{1,0:T(8,128)S(1)}, f32[16,256]{1,0:T(8,128)S(1)}, u32[]{:S(2)}, u32[]{:S(2)}) collective-permute-start(f32[16,256]{1,0:T(8,128)S(1)} %pad_maximum_fusion.2), channel_id=1, source_target_pairs={{0,16},{2,18},{4,20},{6,22},{8,24},{10,26},{12,28},{14,30},{16,0},... | collective-permute-start | bytes 49160 | tf_op jit(solution)/shard_map/ppermute | solution.py:20
  9.3 15.8 %collective-permute-start.1 = (bf16[256,512]{1,0:T(8,128)(2,1)S(1)}, bf16[256,512]{1,0:T(8,128)(2,1)S(1)}, u32[]{:S(2)}, u32[]{:S(2)}) collective-permute-start(bf16[256,512]{1,0:T(8,128)(2,1)S(1)} %collective-permute-done.refs_0_), channel_id=1, source_target_pairs={{0,4},{4,8},{8,12},{12,16},{16,20},{20,24},{24,28},{6,2},{10,6},{1... | collective-permute-start | bytes 786440 | tf_op jit(solution)/shard_map/ppermute | solution.py:330
  14.6 10.5 %collective-permute-start.3 = (bf16[256,512]{1,0:T(8,128)(2,1)S(1)}, bf16[256,512]{1,0:T(8,128)(2,1)S(1)}, u32[]{:S(2)}, u32[]{:S(2)}) collective-permute-start(bf16[256,512]{1,0:T(8,128)(2,1)S(1)} %collective-permute-done.2.refs_3_), channel_id=1, source_target_pairs={{0,4},{4,8},{8,12},{12,16},{16,20},{20,24},{24,28},{6,2},{10,6},{1... | collective-permute-start | bytes 786440 | tf_op jit(solution)/shard_map/ppermute | solution.py:330
  18.7 6.4 %collective-permute-start.9 = (f32[16,512]{1,0:T(8,128)S(1)}, f32[16,512]{1,0:T(8,128)S(1)}, u32[]{:S(2)}, u32[]{:S(2)}) collective-permute-start(f32[16,512]{1,0:T(8,128)S(1)} %pad_maximum_fusion.1), channel_id=1, source_target_pairs={{0,4},{2,6},{4,0},{6,2},{8,12},{10,14},{12,8},{14,10},{16,20},{18,... | collective-permute-start | bytes 98312 | tf_op jit(solution)/shard_map/ppermute | solution.py:20
  25.8 5.1 %collective-permute-start.10 = (bf16[352,2048]{1,0:T(8,128)(2,1)}, bf16[352,2048]{1,0:T(8,128)(2,1)}, u32[]{:S(2)}, u32[]{:S(2)}) collective-permute-start(bf16[352,2048]{1,0:T(8,128)(2,1)} %bitcast.15), channel_id=1, source_target_pairs={{0,1},{1,0},{2,3},{3,2},{4,5},{5,4},{6,7},{7,6},{8,9},{9,8},{10,11... | collective-permute-start | bytes 4325384 | tf_op jit(solution)/shard_map/ppermute | solution.py:344
  25.8 5.6 %collective-permute-start.11 = (bf16[352,2048]{1,0:T(8,128)(2,1)}, bf16[352,2048]{1,0:T(8,128)(2,1)}, u32[]{:S(2)}, u32[]{:S(2)}) collective-permute-start(bf16[352,2048]{1,0:T(8,128)(2,1)} %bitcast.17), channel_id=1, source_target_pairs={{0,1},{1,0},{2,3},{3,2},{4,5},{5,4},{6,7},{7,6},{8,9},{9,8},{10,11... | collective-permute-start | bytes 4325384 | tf_op jit(solution)/shard_map/ppermute | solution.py:345
  30.9 1.6 collective-permute-start.6
  37.5 14.2 %collective-permute-start.12 = (bf16[128,2048]{1,0:T(8,128)(2,1)}, bf16[128,2048]{1,0:T(8,128)(2,1)S(1)}, u32[]{:S(2)}, u32[]{:S(2)}) collective-permute-start(bf16[128,2048]{1,0:T(8,128)(2,1)} %get-tuple-element.71.refs_0_), channel_id=1, source_target_pairs={{0,8},{2,10},{4,12},{6,14},{8,0},{10,2},{12,4},{14,6},{16,24},{18,... | collective-permute-start | bytes 1572872 | tf_op jit(solution)/shard_map/ppermute | solution.py:20
  37.9 17.2 %collective-permute-start.14 = (bf16[128,2048]{1,0:T(8,128)(2,1)}, bf16[128,2048]{1,0:T(8,128)(2,1)S(1)}, u32[]{:S(2)}, u32[]{:S(2)}) collective-permute-start(bf16[128,2048]{1,0:T(8,128)(2,1)} %get-tuple-element.71.refs_0_), channel_id=1, source_target_pairs={{8,16},{10,18},{12,20},{14,22},{16,8},{18,10},{20,12},{22,14},{9,1... | collective-permute-start | bytes 1572872 | tf_op jit(solution)/shard_map/ppermute | solution.py:217
  42.5 14.8 %collective-permute-start.17 = (bf16[128,2048]{1,0:T(8,128)(2,1)}, bf16[128,2048]{1,0:T(8,128)(2,1)S(1)}, u32[]{:S(2)}, u32[]{:S(2)}) collective-permute-start(bf16[128,2048]{1,0:T(8,128)(2,1)} %get-tuple-element.71.refs_0_), channel_id=1, source_target_pairs={{0,4},{1,3},{2,6},{3,1},{4,0},{5,7},{6,2},{7,5},{8,12},{9,11},{10,... | collective-permute-start | bytes 1572872 | tf_op jit(solution)/shard_map/ppermute | solution.py:26
  43.4 13.9 %collective-permute-start.16 = (bf16[128,2048]{1,0:T(8,128)(2,1)}, bf16[128,2048]{1,0:T(8,128)(2,1)S(1)}, u32[]{:S(2)}, u32[]{:S(2)}) collective-permute-start(bf16[128,2048]{1,0:T(8,128)(2,1)} %get-tuple-element.71.refs_0_), channel_id=1, source_target_pairs={{0,2},{1,5},{2,0},{3,7},{4,6},{5,1},{6,4},{7,3},{8,10},{9,13},{10,... | collective-permute-start | bytes 1572872 | tf_op jit(solution)/shard_map/ppermute | solution.py:26
  51.6 16.8 %collective-permute-start.13 = (bf16[128,2048]{1,0:T(8,128)(2,1)S(1)}, bf16[128,2048]{1,0:T(8,128)(2,1)}, u32[]{:S(2)}, u32[]{:S(2)}) collective-permute-start(bf16[128,2048]{1,0:T(8,128)(2,1)S(1)} %collective-permute-done.12.refs_0_), channel_id=1, source_target_pairs={{8,16},{10,18},{12,20},{14,22},{16,8},{18,10},{20,12},{22,14},{9,1... | collective-permute-start | bytes 1572872 | tf_op jit(solution)/shard_map/ppermute | solution.py:217
  55.1 13.3 %collective-permute-start.15 = (bf16[128,2048]{1,0:T(8,128)(2,1)S(1)}, bf16[128,2048]{1,0:T(8,128)(2,1)}, u32[]{:S(2)}, u32[]{:S(2)}) collective-permute-start(bf16[128,2048]{1,0:T(8,128)(2,1)S(1)} %collective-permute-done.14), channel_id=1, source_target_pairs={{8,0},{10,2},{12,4},{14,6},{16,24},{18,26},{20,28},{22,30},{9,1},{... | collective-permute-start | bytes 1572872 | tf_op jit(solution)/shard_map/ppermute | solution.py:217
  57.4 15.5 %collective-permute-start.18 = (bf16[128,2048]{1,0:T(8,128)(2,1)S(1)}, bf16[128,2048]{1,0:T(8,128)(2,1)S(1)}, u32[]{:S(2)}, u32[]{:S(2)}) collective-permute-start(bf16[128,2048]{1,0:T(8,128)(2,1)S(1)} %collective-permute-done.17.refs_2_), channel_id=1, source_target_pairs={{0,2},{1,5},{2,0},{3,7},{4,6},{5,1},{6,4},{7,3},{8,10},{9,13},{10,... | collective-permute-start | bytes 1572872 | tf_op jit(solution)/shard_map/ppermute | solution.py:26
  58.7 15.7 %collective-permute-start.20 = (bf16[128,2048]{1,0:T(8,128)(2,1)S(1)}, bf16[128,2048]{1,0:T(8,128)(2,1)S(1)}, u32[]{:S(2)}, u32[]{:S(2)}) collective-permute-start(bf16[128,2048]{1,0:T(8,128)(2,1)S(1)} %collective-permute-done.12.refs_0_), channel_id=1, source_target_pairs={{0,4},{1,3},{2,6},{3,1},{4,0},{5,7},{6,2},{7,5},{8,12},{9,11},{10,... | collective-permute-start | bytes 1572872 | tf_op jit(solution)/shard_map/ppermute | solution.py:26
  59.7 15.8 %collective-permute-start.19 = (f32[16,1024]{1,0:T(8,128)S(1)}, f32[16,1024]{1,0:T(8,128)S(1)}, u32[]{:S(2)}, u32[]{:S(2)}) collective-permute-start(f32[16,1024]{1,0:T(8,128)S(1)} %pad_maximum_fusion), channel_id=1, source_target_pairs={{0,2},{2,0},{4,6},{6,4},{8,10},{10,8},{12,14},{14,12},{16,18},{18,... | collective-permute-start | bytes 196616 | tf_op jit(solution)/shard_map/ppermute | solution.py:20
  68.5 13.1 %collective-permute-start.23 = (bf16[128,2048]{1,0:T(8,128)(2,1)}, bf16[128,2048]{1,0:T(8,128)(2,1)S(1)}, u32[]{:S(2)}, u32[]{:S(2)}) collective-permute-start(bf16[128,2048]{1,0:T(8,128)(2,1)} %collective-permute-done.13), channel_id=1, source_target_pairs={{8,0},{10,2},{12,4},{14,6},{16,24},{18,26},{20,28},{22,30},{9,1},{... | collective-permute-start | bytes 1572872 | tf_op jit(solution)/shard_map/ppermute | solution.py:217
  72.9 14.2 %collective-permute-start.21 = (bf16[128,2048]{1,0:T(8,128)(2,1)S(1)}, bf16[128,2048]{1,0:T(8,128)(2,1)S(1)}, u32[]{:S(2)}, u32[]{:S(2)}) collective-permute-start(bf16[128,2048]{1,0:T(8,128)(2,1)S(1)} %broadcast_select_fusion.1.refs_2_), channel_id=1, source_target_pairs={{0,2},{1,5},{2,0},{3,7},{4,6},{5,1},{6,4},{7,3},{8,10},{9,13},{10,... | collective-permute-start | bytes 1572872 | tf_op jit(solution)/shard_map/ppermute | solution.py:26
  74.4 12.9 %collective-permute-start.22 = (bf16[128,2048]{1,0:T(8,128)(2,1)S(1)}, bf16[128,2048]{1,0:T(8,128)(2,1)S(1)}, u32[]{:S(2)}, u32[]{:S(2)}) collective-permute-start(bf16[128,2048]{1,0:T(8,128)(2,1)S(1)} %broadcast_select_fusion.1.refs_2_), channel_id=1, source_target_pairs={{0,4},{1,3},{2,6},{3,1},{4,0},{5,7},{6,2},{7,5},{8,12},{9,11},{10,... | collective-permute-start | bytes 1572872 | tf_op jit(solution)/shard_map/ppermute | solution.py:26
  87.1 13.3 %collective-permute-start.24 = (bf16[128,2048]{1,0:T(8,128)(2,1)S(1)}, bf16[128,2048]{1,0:T(8,128)(2,1)S(1)}, u32[]{:S(2)}, u32[]{:S(2)}) collective-permute-start(bf16[128,2048]{1,0:T(8,128)(2,1)S(1)} %broadcast_select_fusion.refs_5_), channel_id=1, source_target_pairs={{0,2},{1,5},{2,0},{3,7},{4,6},{5,1},{6,4},{7,3},{8,10},{9,13},{10,... | collective-permute-start | bytes 1572872 | tf_op jit(solution)/shard_map/ppermute | solution.py:26
  87.4 13.3 %collective-permute-start.26 = (bf16[128,2048]{1,0:T(8,128)(2,1)S(1)}, bf16[128,2048]{1,0:T(8,128)(2,1)S(1)}, u32[]{:S(2)}, u32[]{:S(2)}) collective-permute-start(bf16[128,2048]{1,0:T(8,128)(2,1)S(1)} %broadcast_select_fusion.refs_5_), channel_id=1, source_target_pairs={{0,4},{1,3},{2,6},{3,1},{4,0},{5,7},{6,2},{7,5},{8,12},{9,11},{10,... | collective-permute-start | bytes 1572872 | tf_op jit(solution)/shard_map/ppermute | solution.py:26
  88.1 12.5 %collective-permute-start.27 = (bf16[128,2048]{1,0:T(8,128)(2,1)S(1)}, bf16[128,2048]{1,0:T(8,128)(2,1)S(1)}, u32[]{:S(2)}, u32[]{:S(2)}) collective-permute-start(bf16[128,2048]{1,0:T(8,128)(2,1)S(1)} %collective-permute-done.16.refs_1_), channel_id=1, source_target_pairs={{0,8},{2,10},{4,12},{6,14},{8,0},{10,2},{12,4},{14,6},{16,24},{18,... | collective-permute-start | bytes 1572872 | tf_op jit(solution)/shard_map/ppermute | solution.py:20
  100.3 12.4 %collective-permute-start.25 = (bf16[128,2048]{1,0:T(8,128)(2,1)S(1)}, bf16[128,2048]{1,0:T(8,128)(2,1)S(1)}, u32[]{:S(2)}, u32[]{:S(2)}) collective-permute-start(bf16[128,2048]{1,0:T(8,128)(2,1)S(1)} %collective-permute-done.22.refs_4_), channel_id=1, source_target_pairs={{0,2},{1,5},{2,0},{3,7},{4,6},{5,1},{6,4},{7,3},{8,10},{9,13},{10,... | collective-permute-start | bytes 1572872 | tf_op jit(solution)/shard_map/ppermute | solution.py:26
  100.6 12.1 %collective-permute-start.28 = (bf16[128,2048]{1,0:T(8,128)(2,1)S(1)}, bf16[128,2048]{1,0:T(8,128)(2,1)S(1)}, u32[]{:S(2)}, u32[]{:S(2)}) collective-permute-start(bf16[128,2048]{1,0:T(8,128)(2,1)S(1)} %collective-permute-done.24.refs_0_), channel_id=1, source_target_pairs={{0,4},{1,3},{2,6},{3,1},{4,0},{5,7},{6,2},{7,5},{8,12},{9,11},{10,... | collective-permute-start | bytes 1572872 | tf_op jit(solution)/shard_map/ppermute | solution.py:26
  100.6 15.7 %collective-permute-start.36 = (bf16[128,2048]{1,0:T(8,128)(2,1)S(1)}, bf16[128,2048]{1,0:T(8,128)(2,1)S(1)}, u32[]{:S(2)}, u32[]{:S(2)}) collective-permute-start(bf16[128,2048]{1,0:T(8,128)(2,1)S(1)} %collective-permute-done.18.refs_3_), channel_id=1, source_target_pairs={{0,8},{2,10},{4,12},{6,14},{8,0},{10,2},{12,4},{14,6},{16,24},{18,... | collective-permute-start | bytes 1572872 | tf_op jit(solution)/shard_map/ppermute | solution.py:20
  115.9 12.2 %collective-permute-start.30 = (bf16[128,2048]{1,0:T(8,128)(2,1)S(1)}, bf16[128,2048]{1,0:T(8,128)(2,1)S(1)}, u32[]{:S(2)}, u32[]{:S(2)}) collective-permute-start(bf16[128,2048]{1,0:T(8,128)(2,1)S(1)} %get-tuple-element.101), channel_id=1, source_target_pairs={{0,4},{1,3},{2,6},{3,1},{4,0},{5,7},{6,2},{7,5},{8,12},{9,11},{10,... | collective-permute-start | bytes 1572872 | tf_op jit(solution)/shard_map/ppermute | solution.py:26
  116.0 12.2 %collective-permute-start.29 = (bf16[128,2048]{1,0:T(8,128)(2,1)S(1)}, bf16[128,2048]{1,0:T(8,128)(2,1)S(1)}, u32[]{:S(2)}, u32[]{:S(2)}) collective-permute-start(bf16[128,2048]{1,0:T(8,128)(2,1)S(1)} %get-tuple-element.99), channel_id=1, source_target_pairs={{0,2},{1,5},{2,0},{3,7},{4,6},{5,1},{6,4},{7,3},{8,10},{9,13},{10,... | collective-permute-start | bytes 1572872 | tf_op jit(solution)/shard_map/ppermute | solution.py:26
  116.3 16.2 %collective-permute-start.37 = (bf16[128,2048]{1,0:T(8,128)(2,1)S(1)}, bf16[128,2048]{1,0:T(8,128)(2,1)S(1)}, u32[]{:S(2)}, u32[]{:S(2)}) collective-permute-start(bf16[128,2048]{1,0:T(8,128)(2,1)S(1)} %get-tuple-element.113), channel_id=1, source_target_pairs={{0,8},{2,10},{4,12},{6,14},{8,0},{10,2},{12,4},{14,6},{16,24},{18,... | collective-permute-start | bytes 1572872 | tf_op jit(solution)/shard_map/ppermute | solution.py:20
  128.2 11.5 %collective-permute-start.34 = (bf16[128,2048]{1,0:T(8,128)(2,1)S(1)}, bf16[128,2048]{1,0:T(8,128)(2,1)S(1)}, u32[]{:S(2)}, u32[]{:S(2)}) collective-permute-start(bf16[128,2048]{1,0:T(8,128)(2,1)S(1)} %add_convert_fusion.8), channel_id=1, source_target_pairs={{0,2},{1,5},{2,0},{3,7},{4,6},{5,1},{6,4},{7,3},{8,10},{9,13},{10,... | collective-permute-start | bytes 1572872 | tf_op jit(solution)/shard_map/ppermute | solution.py:26
  129.4 12.1 %collective-permute-start.31 = (bf16[128,2048]{1,0:T(8,128)(2,1)S(1)}, bf16[128,2048]{1,0:T(8,128)(2,1)S(1)}, u32[]{:S(2)}, u32[]{:S(2)}) collective-permute-start(bf16[128,2048]{1,0:T(8,128)(2,1)S(1)} %get-tuple-element.102), channel_id=1, source_target_pairs={{0,4},{1,3},{2,6},{3,1},{4,0},{5,7},{6,2},{7,5},{8,12},{9,11},{10,... | collective-permute-start | bytes 1572872 | tf_op jit(solution)/shard_map/ppermute | solution.py:26
  132.6 11.5 %collective-permute-start.38 = (bf16[128,2048]{1,0:T(8,128)(2,1)S(1)}, bf16[128,2048]{1,0:T(8,128)(2,1)S(1)}, u32[]{:S(2)}, u32[]{:S(2)}) collective-permute-start(bf16[128,2048]{1,0:T(8,128)(2,1)S(1)} %expert_rows.9), channel_id=1, source_target_pairs={{0,8},{2,10},{4,12},{6,14},{8,0},{10,2},{12,4},{14,6},{16,24},{18,... | collective-permute-start | bytes 1572872 | tf_op jit(solution)/shard_map/ppermute | solution.py:20
  139.7 12.1 %collective-permute-start.35 = (bf16[128,2048]{1,0:T(8,128)(2,1)S(1)}, bf16[128,2048]{1,0:T(8,128)(2,1)S(1)}, u32[]{:S(2)}, u32[]{:S(2)}) collective-permute-start(bf16[128,2048]{1,0:T(8,128)(2,1)S(1)} %get-tuple-element.108), channel_id=1, source_target_pairs={{0,2},{1,5},{2,0},{3,7},{4,6},{5,1},{6,4},{7,3},{8,10},{9,13},{10,... | collective-permute-start | bytes 1572872 | tf_op jit(solution)/shard_map/ppermute | solution.py:26
  141.4 12.8 %collective-permute-start.32 = (bf16[128,2048]{1,0:T(8,128)(2,1)S(1)}, bf16[128,2048]{1,0:T(8,128)(2,1)S(1)}, u32[]{:S(2)}, u32[]{:S(2)}) collective-permute-start(bf16[128,2048]{1,0:T(8,128)(2,1)S(1)} %add_convert_fusion.9), channel_id=1, source_target_pairs={{0,4},{1,3},{2,6},{3,1},{4,0},{5,7},{6,2},{7,5},{8,12},{9,11},{10,... | collective-permute-start | bytes 1572872 | tf_op jit(solution)/shard_map/ppermute | solution.py:26
  144.1 12.6 %collective-permute-start.39 = (bf16[128,2048]{1,0:T(8,128)(2,1)S(1)}, bf16[128,2048]{1,0:T(8,128)(2,1)S(1)}, u32[]{:S(2)}, u32[]{:S(2)}) collective-permute-start(bf16[128,2048]{1,0:T(8,128)(2,1)S(1)} %add_convert_fusion.7), channel_id=1, source_target_pairs={{0,8},{2,10},{4,12},{6,14},{24,16},{26,18},{28,20},{30,22},{1,9},{... | collective-permute-start | bytes 1572872 | tf_op jit(solution)/shard_map/ppermute | solution.py:217
  151.8 12.1 %collective-permute-start.44 = (bf16[128,2048]{1,0:T(8,128)(2,1)S(1)}, bf16[128,2048]{1,0:T(8,128)(2,1)S(1)}, u32[]{:S(2)}, u32[]{:S(2)}) collective-permute-start(bf16[128,2048]{1,0:T(8,128)(2,1)S(1)} %add_convert_fusion.2), channel_id=1, source_target_pairs={{0,2},{1,5},{2,0},{3,7},{4,6},{5,1},{6,4},{7,3},{8,10},{9,13},{10,... | collective-permute-start | bytes 1572872 | tf_op jit(solution)/shard_map/ppermute | solution.py:26
  154.3 9.8 %collective-permute-start.33 = (bf16[128,2048]{1,0:T(8,128)(2,1)S(1)}, bf16[128,2048]{1,0:T(8,128)(2,1)S(1)}, u32[]{:S(2)}, u32[]{:S(2)}) collective-permute-start(bf16[128,2048]{1,0:T(8,128)(2,1)S(1)} %get-tuple-element.104), channel_id=1, source_target_pairs={{0,4},{1,3},{2,6},{3,1},{4,0},{5,7},{6,2},{7,5},{8,12},{9,11},{10,... | collective-permute-start | bytes 1572872 | tf_op jit(solution)/shard_map/ppermute | solution.py:26
  157.1 11.3 %collective-permute-start.40 = (bf16[128,2048]{1,0:T(8,128)(2,1)S(1)}, bf16[128,2048]{1,0:T(8,128)(2,1)S(1)}, u32[]{:S(2)}, u32[]{:S(2)}) collective-permute-start(bf16[128,2048]{1,0:T(8,128)(2,1)S(1)} %add_convert_fusion.6), channel_id=1, source_target_pairs={{8,16},{10,18},{12,20},{14,22},{16,8},{18,10},{20,12},{22,14},{9,1... | collective-permute-start | bytes 1572872 | tf_op jit(solution)/shard_map/ppermute | solution.py:217
  159.2 11.3 %collective-permute-start.41 = (bf16[128,2048]{1,0:T(8,128)(2,1)S(1)}, bf16[128,2048]{1,0:T(8,128)(2,1)S(1)}, u32[]{:S(2)}, u32[]{:S(2)}) collective-permute-start(bf16[128,2048]{1,0:T(8,128)(2,1)S(1)} %add_convert_fusion.6), channel_id=1, source_target_pairs={{0,8},{2,10},{4,12},{6,14},{24,16},{26,18},{28,20},{30,22},{1,9},{... | collective-permute-start | bytes 1572872 | tf_op jit(solution)/shard_map/ppermute | solution.py:217
  164.0 20.1 %copy-start.4 = (f32[128,2048]{1,0:T(8,128)S(1)}, f32[128,2048]{1,0:T(8,128)}, u32[]{:S(2)}) copy-start(f32[128,2048]{1,0:T(8,128)} %get-tuple-element.69) | copy-start | bytes 3145732
  164.1 11.1 %collective-permute-start.46 = (bf16[128,2048]{1,0:T(8,128)(2,1)S(1)}, bf16[128,2048]{1,0:T(8,128)(2,1)S(1)}, u32[]{:S(2)}, u32[]{:S(2)}) collective-permute-start(bf16[128,2048]{1,0:T(8,128)(2,1)S(1)} %add_convert_fusion.1), channel_id=1, source_target_pairs={{0,4},{1,3},{2,6},{3,1},{4,0},{5,7},{6,2},{7,5},{8,12},{9,11},{10,... | collective-permute-start | bytes 1572872 | tf_op jit(solution)/shard_map/ppermute | solution.py:26
  166.4 9.2 %collective-permute-start.45 = (bf16[128,2048]{1,0:T(8,128)(2,1)S(1)}, bf16[128,2048]{1,0:T(8,128)(2,1)S(1)}, u32[]{:S(2)}, u32[]{:S(2)}) collective-permute-start(bf16[128,2048]{1,0:T(8,128)(2,1)S(1)} %add_convert_fusion.3), channel_id=1, source_target_pairs={{0,2},{1,5},{2,0},{3,7},{4,6},{5,1},{6,4},{7,3},{8,10},{9,13},{10,... | collective-permute-start | bytes 1572872 | tf_op jit(solution)/shard_map/ppermute | solution.py:26
  170.7 11.4 %collective-permute-start.43 = (bf16[128,2048]{1,0:T(8,128)(2,1)S(1)}, bf16[128,2048]{1,0:T(8,128)(2,1)S(1)}, u32[]{:S(2)}, u32[]{:S(2)}) collective-permute-start(bf16[128,2048]{1,0:T(8,128)(2,1)S(1)} %add_convert_fusion.4), channel_id=1, source_target_pairs={{8,16},{10,18},{12,20},{14,22},{16,8},{18,10},{20,12},{22,14},{9,1... | collective-permute-start | bytes 1572872 | tf_op jit(solution)/shard_map/ppermute | solution.py:217
  174.9 9.2 %collective-permute-start.42 = (bf16[128,2048]{1,0:T(8,128)(2,1)S(1)}, bf16[128,2048]{1,0:T(8,128)(2,1)S(1)}, u32[]{:S(2)}, u32[]{:S(2)}) collective-permute-start(bf16[128,2048]{1,0:T(8,128)(2,1)S(1)} %add_convert_fusion.5), channel_id=1, source_target_pairs={{0,8},{2,10},{4,12},{6,14},{8,0},{10,2},{12,4},{14,6},{16,24},{18,... | collective-permute-start | bytes 1572872 | tf_op jit(solution)/shard_map/ppermute | solution.py:20
  (9 other events, 42.7 us)

commit v14 on v13

--- a/solution.py
+++ b/solution.py
@@ -232,7 +232,7 @@
     ends2, near2 = shift(near3, OUTWARD), shift(o1, MIDDLE)
     d0, y1 = cross(after(y0, x0), X), cross(after(o1, y0), Y)
 
-    ends3 = shift(after(near2, ends2), OUTWARD)
+    ends3 = shift(near2, OUTWARD)
     o2 = jnp.where(inner, near2, ends2)
     x2, y2 = cross(after(o2, d0, weights[0]), X), cross(after(o2, y1, weights[0]), Y)
     run = functools.partial(run, weights)

time: 186 us -> 186 us (level)
  starting transfers between devices: 60.8 us -> 57.1 us
  waiting for transfers between devices: 74.8 us -> 77.9 us
    ppermute x20, waiting for transfers between devices: 43.5 us -> 46.6 us  [cross(): return lax.ppermute(block, ('seq', 'exp'), pairs)]
  transfers between devices with their start and end apart: 47 -> 47, of which waited for: 24 -> 25; matrix products, arithmetic and copies ran while one was open for 3% -> 3% of each run, Pallas kernels for 18% -> 18%
where the time goes in v14:
time: 186 us; the launch traced here: 185 us
  waiting for transfers between devices  77.9 us (42%)
  starting transfers between devices  57.1 us (31%)
  Pallas kernels  37.1 us (20%)
  local copies, waits for them, and re-layouts  6.87 us (4%)
  other arithmetic  5.45 us (3%)
    ppermute x20, waiting for transfers between devices, cross(): return lax.ppermute(block, ('seq', 'exp'), pairs)  46.6 us
    pallas_call x5, Pallas kernels, expert(): pl.pallas_call(functools.partial(expert_kernel, places, len(gates)), out_...  25.5 us
    ppermute x8, starting transfers between devices, shift(): lax.ppermute(block, 'seq', [(4 * a + i, 4 * b + i) for a, b in pairs for...  20.4 us
    ppermute x12, waiting for transfers between devices, flip(): return lax.ppermute(block, 'seq', [(i, i ^ mask) for i in range(count)])  20.1 us
    ppermute x20, starting transfers between devices, cross(): return lax.ppermute(block, ('seq', 'exp'), pairs)  19.9 us
    ppermute x12, starting transfers between devices, flip(): return lax.ppermute(block, 'seq', [(i, i ^ mask) for i in range(count)])  9.69 us
    ppermute x8, waiting for transfers between devices, shift(): lax.ppermute(block, 'seq', [(4 * a + i, 4 * b + i) for a, b in pairs for...  9.66 us
    ppermute x2, starting transfers between devices, halo(): return (beside, part, lax.ppermute(beside, 'seq', ahead + back))  6.6 us
  transfers between devices with their start and end apart: 47, of which 25 were waited for; matrix products, arithmetic and copies ran while one was open for 3% of the time, Pallas kernels for 18%

profile of v14, /device:TPU:10, one launch (start us, length us, event | category | flops | bytes accessed | tf_op | source)
XLA Modules:
  0.0 184.7 jit_solution(17102478290136212231)
XLA Ops:
  0.5 1.5 collective-permute-start.2
  3.3 3.2 %collective-permute-done.7.refs_5_.refs_7_.refs_4_.refs_3_.refs_2_ = f32[16,128]{1,0:T(8,128)S(1)} collective-permute-done((f32[16,128]{1,0:T(8,128)S(1)}, f32[16,128]{1,0:T(8,128)S(1)}, u32[]{:S(2)}, u32[]{:S(2)}) %collective-permute-start.7) | collective-permute-done | bytes 8224 | tf_op jit(solution)/shard_map/ppermute | solution.py:20
  6.5 2.6 %collective-permute-start.8 = (f32[16,256]{1,0:T(8,128)S(1)}, f32[16,256]{1,0:T(8,128)S(1)}, u32[]{:S(2)}, u32[]{:S(2)}) collective-permute-start(f32[16,256]{1,0:T(8,128)S(1)} %pad_maximum_fusion.2), channel_id=1, source_target_pairs={{0,16},{2,18},{4,20},{6,22},{8,24},{10,26},{12,28},{14,30},{16,0},... | collective-permute-start | bytes 49160 | tf_op jit(solution)/shard_map/ppermute | solution.py:20
  9.3 3.3 %collective-permute-start.1 = (bf16[256,512]{1,0:T(8,128)(2,1)S(1)}, bf16[256,512]{1,0:T(8,128)(2,1)S(1)}, u32[]{:S(2)}, u32[]{:S(2)}) collective-permute-start(bf16[256,512]{1,0:T(8,128)(2,1)S(1)} %collective-permute-done.refs_0_), channel_id=1, source_target_pairs={{0,4},{4,8},{8,12},{12,16},{16,20},{20,24},{24,28},{6,2},{10,6},{1... | collective-permute-start | bytes 786440 | tf_op jit(solution)/shard_map/ppermute | solution.py:330
  12.6 1.9 %collective-permute-done.2.refs_3_ = bf16[256,512]{1,0:T(8,128)(2,1)S(1)} collective-permute-done((bf16[256,512]{1,0:T(8,128)(2,1)}, bf16[256,512]{1,0:T(8,128)(2,1)S(1)}, u32[]{:S(2)}, u32[]{:S(2)}) %collective-permute-start.2) | collective-permute-done | bytes 262176 | tf_op jit(solution)/shard_map/ppermute | solution.py:20
  14.6 3.3 %collective-permute-start.3 = (bf16[256,512]{1,0:T(8,128)(2,1)S(1)}, bf16[256,512]{1,0:T(8,128)(2,1)S(1)}, u32[]{:S(2)}, u32[]{:S(2)}) collective-permute-start(bf16[256,512]{1,0:T(8,128)(2,1)S(1)} %collective-permute-done.2.refs_3_), channel_id=1, source_target_pairs={{0,4},{4,8},{8,12},{12,16},{16,20},{20,24},{24,28},{6,2},{10,6},{1... | collective-permute-start | bytes 786440 | tf_op jit(solution)/shard_map/ppermute | solution.py:330
  20.5 4.5 %collective-permute-done.9.refs_7_.refs_9_.refs_6_.refs_5_.refs_4_ = f32[16,512]{1,0:T(8,128)S(1)} collective-permute-done((f32[16,512]{1,0:T(8,128)S(1)}, f32[16,512]{1,0:T(8,128)S(1)}, u32[]{:S(2)}, u32[]{:S(2)}) %collective-permute-start.9) | collective-permute-done | bytes 32800 | tf_op jit(solution)/shard_map/ppermute | solution.py:20
  26.4 4.6 %window_attention.1 = (bf16[128,512]{1,0:T(8,128)(2,1)}, bf16[128,512]{1,0:T(8,128)(2,1)}) custom-call(s32[2]{0:T(128)} %pad_add_fusion.where_ref, bf16[256,512]{1,0:T(8,128)(2,1)} %q_ref.1, s32[1,768]{1,0:T(1,128)} %broadcast_in_dim.21.ids_ref, bf16[256,512]{1,0:T(8,128)(2,1)} %copy-done.5, bf16[256,512]{1,0:T(8,128)(2,1)} %refs_1_.1, ...), custom_call_target="tpu_custom_call" | custom-call | tf_op jit(solution)/shard_map/window_attention/pallas_call | solution.py:97
  33.2 4.3 %project_and_norm.1 = (f32[128,2048]{1,0:T(8,128)}, bf16[128,2048]{1,0:T(8,128)(2,1)}) custom-call(bf16[128,512]{1,0:T(8,128)(2,1)} %get-tuple-element.64.mine_ref, bf16[128,512]{1,0:T(8,128)(2,1)} %copy-done.9, bf16[512,2048]{1,0:T(8,128)(2,1)} %own_w.1, bf16[512,2048]{1,0:T(8,128)(2,1)} %collective-permute-done.4.refs_6_.other_w, ...), custom_call_target="tpu_custom_call" | custom-call | tf_op jit(solution)/shard_map/project_and_norm/pallas_call | solution.py:120
  37.9 4.6 %collective-permute-start.14 = (bf16[128,2048]{1,0:T(8,128)(2,1)}, bf16[128,2048]{1,0:T(8,128)(2,1)S(1)}, u32[]{:S(2)}, u32[]{:S(2)}) collective-permute-start(bf16[128,2048]{1,0:T(8,128)(2,1)} %get-tuple-element.70.refs_0_), channel_id=1, source_target_pairs={{8,16},{10,18},{12,20},{14,22},{16,8},{18,10},{20,12},{22,14},{9,1... | collective-permute-start | bytes 1572872 | tf_op jit(solution)/shard_map/ppermute | solution.py:217
  43.4 1.2 collective-permute-start.16
  44.6 7.0 %collective-permute-done.12.refs_0_ = bf16[128,2048]{1,0:T(8,128)(2,1)S(1)} collective-permute-done((bf16[128,2048]{1,0:T(8,128)(2,1)}, bf16[128,2048]{1,0:T(8,128)(2,1)S(1)}, u32[]{:S(2)}, u32[]{:S(2)}) %collective-permute-start.12) | collective-permute-done | bytes 524320 | tf_op jit(solution)/shard_map/ppermute | solution.py:20
  51.6 3.5 %collective-permute-start.13 = (bf16[128,2048]{1,0:T(8,128)(2,1)S(1)}, bf16[128,2048]{1,0:T(8,128)(2,1)}, u32[]{:S(2)}, u32[]{:S(2)}) collective-permute-start(bf16[128,2048]{1,0:T(8,128)(2,1)S(1)} %collective-permute-done.12.refs_0_), channel_id=1, source_target_pairs={{8,16},{10,18},{12,20},{14,22},{16,8},{18,10},{20,12},{22,14},{9,1... | collective-permute-start | bytes 1572872 | tf_op jit(solution)/shard_map/ppermute | solution.py:217
  55.1 2.1 %collective-permute-start.15 = (bf16[128,2048]{1,0:T(8,128)(2,1)S(1)}, bf16[128,2048]{1,0:T(8,128)(2,1)}, u32[]{:S(2)}, u32[]{:S(2)}) collective-permute-start(bf16[128,2048]{1,0:T(8,128)(2,1)S(1)} %collective-permute-done.14), channel_id=1, source_target_pairs={{8,0},{10,2},{12,4},{14,6},{16,24},{18,26},{20,28},{22,30},{9,1},{... | collective-permute-start | bytes 1572872 | tf_op jit(solution)/shard_map/ppermute | solution.py:217
  57.4 1.3 collective-permute-start.18
  59.7 2.0 %collective-permute-start.19 = (f32[16,1024]{1,0:T(8,128)S(1)}, f32[16,1024]{1,0:T(8,128)S(1)}, u32[]{:S(2)}, u32[]{:S(2)}) collective-permute-start(f32[16,1024]{1,0:T(8,128)S(1)} %pad_maximum_fusion), channel_id=1, source_target_pairs={{0,2},{2,0},{4,6},{6,4},{8,10},{10,8},{12,14},{14,12},{16,18},{18,... | collective-permute-start | bytes 196616 | tf_op jit(solution)/shard_map/ppermute | solution.py:20
  61.7 1.4 copy-done
  63.1 1.4 copy-done.1
  64.4 1.4 copy-done.2
  65.8 2.6 %assemble_weights.1 = (bf16[1408,2048]{1,0:T(8,128)(2,1)S(1)}, bf16[704,2048]{1,0:T(8,128)(2,1)S(1)}) custom-call(bf16[352,2048]{1,0:T(8,128)(2,1)S(1)} %bitcast.14, bf16[352,2048]{1,0:T(8,128)(2,1)} %collective-permute-done.5.refs_7_.refs_1_, bf16[352,2048]{1,0:T(8,128)(2,1)S(1)} %bitcast.16, bf16[352,2048]{1,0:T(8,128)(2,1)} %collective-permute-done.10.refs_0_.refs_3_, ...), custom_call_target="tpu_custom_call" | custom-call | tf_op jit(solution)/shard_map/assemble_weights/pallas_call | solution.py:148
  68.5 1.6 collective-permute-start.23
  74.1 5.6 %expert_rows.5 = (bf16[128,2048]{1,0:T(8,128)(2,1)S(1)}, bf16[128,2048]{1,0:T(8,128)(2,1)S(1)}, bf16[128,2048]{1,0:T(8,128)(2,1)S(1)}, bf16[128,2048]{1,0:T(8,128)(2,1)S(1)}) custom-call(s32[2]{0:T(128)S(1)} %pad_add_fusion.1.where_ref, bf16[128,2048]{1,0:T(8,128)(2,1)S(1)} %copy-done.3, bf16[128,2048]{1,0:T(8,128)(2,1)S(1)} %collective-permute-done.16.refs_1_, ...), custom_call_target="tpu_custom_call" | custom-call | tf_op jit(solution)/shard_map/expert_rows/pallas_call | solution.py:195
  80.1 6.1 %collective-permute-done.21.refs_3_ = bf16[128,2048]{1,0:T(8,128)(2,1)S(1)} collective-permute-done((bf16[128,2048]{1,0:T(8,128)(2,1)S(1)}, bf16[128,2048]{1,0:T(8,128)(2,1)S(1)}, u32[]{:S(2)}, u32[]{:S(2)}) %collective-permute-start.21) | collective-permute-done | bytes 524320 | tf_op jit(solution)/shard_map/ppermute | solution.py:26
  86.5 8.1 %expert_rows.6 = (bf16[128,2048]{1,0:T(8,128)(2,1)S(1)}, bf16[128,2048]{1,0:T(8,128)(2,1)S(1)}, bf16[128,2048]{1,0:T(8,128)(2,1)S(1)}, bf16[128,2048]{1,0:T(8,12...) custom-call(s32[2]{0:T(128)S(1)} %pad_add_fusion.1.where_ref, ...), custom_call_target="tpu_custom_call" | custom-call | tf_op jit(solution)/shard_map/expert_rows/pallas_call | solution.py:195
  94.6 4.9 %collective-permute-done.24.refs_0_ = bf16[128,2048]{1,0:T(8,128)(2,1)S(1)} collective-permute-done((bf16[128,2048]{1,0:T(8,128)(2,1)S(1)}, bf16[128,2048]{1,0:T(8,128)(2,1)S(1)}, u32[]{:S(2)}, u32[]{:S(2)}) %collective-permute-start.24) | collective-permute-done | bytes 524320 | tf_op jit(solution)/shard_map/ppermute | solution.py:26
  100.5 5.6 %expert_rows.7 = (bf16[128,2048]{1,0:T(8,128)(2,1)S(1)}, bf16[128,2048]{1,0:T(8,128)(2,1)S(1)}, bf16[128,2048]{1,0:T(8,128)(2,1)S(1)}) custom-call(s32[2]{0:T(128)S(1)} %pad_add_fusion.1.where_ref, bf16[128,2048]{1,0:T(8,128)(2,1)S(1)} %collective-permute-done.24.refs_0_, bf16[128,2048]{1,0:T(8,128)(2,1)S(1)} %collective-permute-done.26.refs_1_, ...), custom_call_target="tpu_custom_call" | custom-call | tf_op jit(solution)/shard_map/expert_rows/pallas_call | solution.py:195
  106.1 5.8 %collective-permute-done.25.refs_0_ = bf16[128,2048]{1,0:T(8,128)(2,1)S(1)} collective-permute-done((bf16[128,2048]{1,0:T(8,128)(2,1)S(1)}, bf16[128,2048]{1,0:T(8,128)(2,1)S(1)}, u32[]{:S(2)}, u32[]{:S(2)}) %collective-permute-start.25) | collective-permute-done | bytes 524320 | tf_op jit(solution)/shard_map/ppermute | solution.py:26
  111.9 3.2 %expert_rows.8 = (bf16[128,2048]{1,0:T(8,128)(2,1)S(1)}, bf16[128,2048]{1,0:T(8,128)(2,1)S(1)}) custom-call(s32[2]{0:T(128)S(1)} %pad_add_fusion.1.where_ref, bf16[128,2048]{1,0:T(8,128)(2,1)S(1)} %collective-permute-done.25.refs_0_, bf16[128,2048]{1,0:T(8,128)(2,1)S(1)} %collective-permute-done.28.refs_1_, ...), custom_call_target="tpu_custom_call" | custom-call | tf_op jit(solution)/shard_map/expert_rows/pallas_call | solution.py:195
  116.3 11.0 %collective-permute-done.30 = bf16[128,2048]{1,0:T(8,128)(2,1)S(1)} collective-permute-done((bf16[128,2048]{1,0:T(8,128)(2,1)S(1)}, bf16[128,2048]{1,0:T(8,128)(2,1)S(1)}, u32[]{:S(2)}, u32[]{:S(2)}) %collective-permute-start.30) | collective-permute-done | bytes 524320 | tf_op jit(solution)/shard_map/ppermute | solution.py:26
  127.4 1.2 collective-permute-start.34
  128.9 2.9 %expert_rows.9 = bf16[128,2048]{1,0:T(8,128)(2,1)S(1)} custom-call(s32[2]{0:T(128)S(1)} %pad_add_fusion.1.where_ref, bf16[128,2048]{1,0:T(8,128)(2,1)S(1)} %collective-permute-done.36.refs_0_, f32[16,128]{1,0:T(8,128)S(1)} %select_reduce_fusion.refs_4_.refs_6_.refs_3_.refs_2_.refs_1_, ...), custom_call_target="tpu_custom_call" | custom-call | tf_op jit(solution)/shard_map/expert_rows/pallas_call | solution.py:195
  132.1 6.9 %collective-permute-done.34 = bf16[128,2048]{1,0:T(8,128)(2,1)S(1)} collective-permute-done((bf16[128,2048]{1,0:T(8,128)(2,1)S(1)}, bf16[128,2048]{1,0:T(8,128)(2,1)S(1)}, u32[]{:S(2)}, u32[]{:S(2)}) %collective-permute-start.34) | collective-permute-done | bytes 524320 | tf_op jit(solution)/shard_map/ppermute | solution.py:26
  139.0 1.7 collective-permute-start.35
  140.7 1.5 collective-permute-start.32
  143.5 1.3 collective-permute-start.39
  144.9 6.2 %collective-permute-done.35 = bf16[128,2048]{1,0:T(8,128)(2,1)S(1)} collective-permute-done((bf16[128,2048]{1,0:T(8,128)(2,1)S(1)}, bf16[128,2048]{1,0:T(8,128)(2,1)S(1)}, u32[]{:S(2)}, u32[]{:S(2)}) %collective-permute-start.35) | collective-permute-done | bytes 524320 | tf_op jit(solution)/shard_map/ppermute | solution.py:26
  151.1 1.7 collective-permute-start.44
  153.7 2.5 %collective-permute-start.33 = (bf16[128,2048]{1,0:T(8,128)(2,1)S(1)}, bf16[128,2048]{1,0:T(8,128)(2,1)S(1)}, u32[]{:S(2)}, u32[]{:S(2)}) collective-permute-start(bf16[128,2048]{1,0:T(8,128)(2,1)S(1)} %get-tuple-element.102), channel_id=1, source_target_pairs={{0,4},{1,3},{2,6},{3,1},{4,0},{5,7},{6,2},{7,5},{8,12},{9,11},{10,... | collective-permute-start | bytes 1572872 | tf_op jit(solution)/shard_map/ppermute | solution.py:26
  156.5 1.9 %collective-permute-start.40 = (bf16[128,2048]{1,0:T(8,128)(2,1)S(1)}, bf16[128,2048]{1,0:T(8,128)(2,1)S(1)}, u32[]{:S(2)}, u32[]{:S(2)}) collective-permute-start(bf16[128,2048]{1,0:T(8,128)(2,1)S(1)} %add_convert_fusion.6), channel_id=1, source_target_pairs={{8,16},{10,18},{12,20},{14,22},{16,8},{18,10},{20,12},{22,14},{9,1... | collective-permute-start | bytes 1572872 | tf_op jit(solution)/shard_map/ppermute | solution.py:217
  158.6 1.3 collective-permute-start.41
  159.9 3.3 %collective-permute-done.44 = bf16[128,2048]{1,0:T(8,128)(2,1)S(1)} collective-permute-done((bf16[128,2048]{1,0:T(8,128)(2,1)S(1)}, bf16[128,2048]{1,0:T(8,128)(2,1)S(1)}, u32[]{:S(2)}, u32[]{:S(2)}) %collective-permute-start.44) | collective-permute-done | bytes 524320 | tf_op jit(solution)/shard_map/ppermute | solution.py:26
  163.4 2.3 %collective-permute-start.46 = (bf16[128,2048]{1,0:T(8,128)(2,1)S(1)}, bf16[128,2048]{1,0:T(8,128)(2,1)S(1)}, u32[]{:S(2)}, u32[]{:S(2)}) collective-permute-start(bf16[128,2048]{1,0:T(8,128)(2,1)S(1)} %add_convert_fusion.1), channel_id=1, source_target_pairs={{0,4},{1,3},{2,6},{3,1},{4,0},{5,7},{6,2},{7,5},{8,12},{9,11},{10,... | collective-permute-start | bytes 1572872 | tf_op jit(solution)/shard_map/ppermute | solution.py:26
  165.7 1.2 collective-permute-start.45
  168.1 1.8 collective-permute-done.41
  170.1 4.1 %collective-permute-start.43 = (bf16[128,2048]{1,0:T(8,128)(2,1)S(1)}, bf16[128,2048]{1,0:T(8,128)(2,1)S(1)}, u32[]{:S(2)}, u32[]{:S(2)}) collective-permute-start(bf16[128,2048]{1,0:T(8,128)(2,1)S(1)} %add_convert_fusion.4), channel_id=1, source_target_pairs={{8,16},{10,18},{12,20},{14,22},{16,8},{18,10},{20,12},{22,14},{9,1... | collective-permute-start | bytes 1572872 | tf_op jit(solution)/shard_map/ppermute | solution.py:217
  174.9 6.5 %collective-permute-done.43 = bf16[128,2048]{1,0:T(8,128)(2,1)S(1)} collective-permute-done((bf16[128,2048]{1,0:T(8,128)(2,1)S(1)}, bf16[128,2048]{1,0:T(8,128)(2,1)S(1)}, u32[]{:S(2)}, u32[]{:S(2)}) %collective-permute-start.43) | collective-permute-done | bytes 524320 | tf_op jit(solution)/shard_map/ppermute | solution.py:217
  181.4 2.1 %collective-permute-done.42 = bf16[128,2048]{1,0:T(8,128)(2,1)S(1)} collective-permute-done((bf16[128,2048]{1,0:T(8,128)(2,1)S(1)}, bf16[128,2048]{1,0:T(8,128)(2,1)S(1)}, u32[]{:S(2)}, u32[]{:S(2)}) %collective-permute-start.42) | collective-permute-done | bytes 524320 | tf_op jit(solution)/shard_map/ppermute | solution.py:20
  183.5 1.3 add_convert_fusion
  (94 shorter events, 22.9 us)
Async XLA Ops:
  0.0 26.3 %collective-permute-start.4 = (bf16[512,2048]{1,0:T(8,128)(2,1)}, bf16[512,2048]{1,0:T(8,128)(2,1)}, u32[]{:S(2)}, u32[]{:S(2)}) collective-permute-start(bf16[512,2048]{1,0:T(8,128)(2,1)} %own_w.1), channel_id=1, source_target_pairs={{0,1},{1,0},{2,3},{3,2},{4,5},{5,4},{6,7},{7,6},{8,9},{9,8},{10,11... | collective-permute-start | bytes 6291464 | tf_op jit(solution)/shard_map/ppermute | solution.py:339
  0.0 9.3 %collective-permute-start = (bf16[256,512]{1,0:T(8,128)(2,1)}, bf16[256,512]{1,0:T(8,128)(2,1)S(1)}, u32[]{:S(2)}, u32[]{:S(2)}) collective-permute-start(bf16[256,512]{1,0:T(8,128)(2,1)} %refs_1_.1), channel_id=1, source_target_pairs={{0,2},{2,0},{4,6},{6,4},{8,10},{10,8},{12,14},{14,12},{16,18},{18,... | collective-permute-start | bytes 786440 | tf_op jit(solution)/shard_map/ppermute | solution.py:20
  0.5 14.0 %collective-permute-start.2 = (bf16[256,512]{1,0:T(8,128)(2,1)}, bf16[256,512]{1,0:T(8,128)(2,1)S(1)}, u32[]{:S(2)}, u32[]{:S(2)}) collective-permute-start(bf16[256,512]{1,0:T(8,128)(2,1)} %refs_4_.1), channel_id=1, source_target_pairs={{0,2},{2,0},{4,6},{6,4},{8,10},{10,8},{12,14},{14,12},{16,18},{18,... | collective-permute-start | bytes 786440 | tf_op jit(solution)/shard_map/ppermute | solution.py:20
  2.7 3.7 %collective-permute-start.7 = (f32[16,128]{1,0:T(8,128)S(1)}, f32[16,128]{1,0:T(8,128)S(1)}, u32[]{:S(2)}, u32[]{:S(2)}) collective-permute-start(f32[16,128]{1,0:T(8,128)S(1)} %select_reduce_fusion.refs_4_.refs_6_.refs_3_.refs_2_.refs_1_), channel_id=1, source_target_pairs={{0,8},{2,10},{4,12},{6,14},{8,0},{10,2},{12,4},{14,6},{16,24},{18,... | collective-permute-start | bytes 24584 | tf_op jit(solution)/shard_map/ppermute | solution.py:20
  3.3 23.1 %collective-permute-start.5 = (bf16[352,2048]{1,0:T(8,128)(2,1)}, bf16[352,2048]{1,0:T(8,128)(2,1)}, u32[]{:S(2)}, u32[]{:S(2)}) collective-permute-start(bf16[352,2048]{1,0:T(8,128)(2,1)} %bitcast.13), channel_id=1, source_target_pairs={{0,1},{1,0},{2,3},{3,2},{4,5},{5,4},{6,7},{7,6},{8,9},{9,8},{10,11... | collective-permute-start | bytes 4325384 | tf_op jit(solution)/shard_map/ppermute | solution.py:341
  6.5 12.2 %collective-permute-start.8 = (f32[16,256]{1,0:T(8,128)S(1)}, f32[16,256]{1,0:T(8,128)S(1)}, u32[]{:S(2)}, u32[]{:S(2)}) collective-permute-start(f32[16,256]{1,0:T(8,128)S(1)} %pad_maximum_fusion.2), channel_id=1, source_target_pairs={{0,16},{2,18},{4,20},{6,22},{8,24},{10,26},{12,28},{14,30},{16,0},... | collective-permute-start | bytes 49160 | tf_op jit(solution)/shard_map/ppermute | solution.py:20
  9.3 15.8 %collective-permute-start.1 = (bf16[256,512]{1,0:T(8,128)(2,1)S(1)}, bf16[256,512]{1,0:T(8,128)(2,1)S(1)}, u32[]{:S(2)}, u32[]{:S(2)}) collective-permute-start(bf16[256,512]{1,0:T(8,128)(2,1)S(1)} %collective-permute-done.refs_0_), channel_id=1, source_target_pairs={{0,4},{4,8},{8,12},{12,16},{16,20},{20,24},{24,28},{6,2},{10,6},{1... | collective-permute-start | bytes 786440 | tf_op jit(solution)/shard_map/ppermute | solution.py:330
  14.6 10.5 %collective-permute-start.3 = (bf16[256,512]{1,0:T(8,128)(2,1)S(1)}, bf16[256,512]{1,0:T(8,128)(2,1)S(1)}, u32[]{:S(2)}, u32[]{:S(2)}) collective-permute-start(bf16[256,512]{1,0:T(8,128)(2,1)S(1)} %collective-permute-done.2.refs_3_), channel_id=1, source_target_pairs={{0,4},{4,8},{8,12},{12,16},{16,20},{20,24},{24,28},{6,2},{10,6},{1... | collective-permute-start | bytes 786440 | tf_op jit(solution)/shard_map/ppermute | solution.py:330
  18.7 6.4 %collective-permute-start.9 = (f32[16,512]{1,0:T(8,128)S(1)}, f32[16,512]{1,0:T(8,128)S(1)}, u32[]{:S(2)}, u32[]{:S(2)}) collective-permute-start(f32[16,512]{1,0:T(8,128)S(1)} %pad_maximum_fusion.1), channel_id=1, source_target_pairs={{0,4},{2,6},{4,0},{6,2},{8,12},{10,14},{12,8},{14,10},{16,20},{18,... | collective-permute-start | bytes 98312 | tf_op jit(solution)/shard_map/ppermute | solution.py:20
  25.8 5.1 %collective-permute-start.10 = (bf16[352,2048]{1,0:T(8,128)(2,1)}, bf16[352,2048]{1,0:T(8,128)(2,1)}, u32[]{:S(2)}, u32[]{:S(2)}) collective-permute-start(bf16[352,2048]{1,0:T(8,128)(2,1)} %bitcast.15), channel_id=1, source_target_pairs={{0,1},{1,0},{2,3},{3,2},{4,5},{5,4},{6,7},{7,6},{8,9},{9,8},{10,11... | collective-permute-start | bytes 4325384 | tf_op jit(solution)/shard_map/ppermute | solution.py:344
  25.8 5.6 %collective-permute-start.11 = (bf16[352,2048]{1,0:T(8,128)(2,1)}, bf16[352,2048]{1,0:T(8,128)(2,1)}, u32[]{:S(2)}, u32[]{:S(2)}) collective-permute-start(bf16[352,2048]{1,0:T(8,128)(2,1)} %bitcast.17), channel_id=1, source_target_pairs={{0,1},{1,0},{2,3},{3,2},{4,5},{5,4},{6,7},{7,6},{8,9},{9,8},{10,11... | collective-permute-start | bytes 4325384 | tf_op jit(solution)/shard_map/ppermute | solution.py:345
  30.9 1.6 collective-permute-start.6
  37.5 14.2 %collective-permute-start.12 = (bf16[128,2048]{1,0:T(8,128)(2,1)}, bf16[128,2048]{1,0:T(8,128)(2,1)S(1)}, u32[]{:S(2)}, u32[]{:S(2)}) collective-permute-start(bf16[128,2048]{1,0:T(8,128)(2,1)} %get-tuple-element.70.refs_0_), channel_id=1, source_target_pairs={{0,8},{2,10},{4,12},{6,14},{8,0},{10,2},{12,4},{14,6},{16,24},{18,... | collective-permute-start | bytes 1572872 | tf_op jit(solution)/shard_map/ppermute | solution.py:20
  37.9 17.2 %collective-permute-start.14 = (bf16[128,2048]{1,0:T(8,128)(2,1)}, bf16[128,2048]{1,0:T(8,128)(2,1)S(1)}, u32[]{:S(2)}, u32[]{:S(2)}) collective-permute-start(bf16[128,2048]{1,0:T(8,128)(2,1)} %get-tuple-element.70.refs_0_), channel_id=1, source_target_pairs={{8,16},{10,18},{12,20},{14,22},{16,8},{18,10},{20,12},{22,14},{9,1... | collective-permute-start | bytes 1572872 | tf_op jit(solution)/shard_map/ppermute | solution.py:217
  42.5 14.8 %collective-permute-start.17 = (bf16[128,2048]{1,0:T(8,128)(2,1)}, bf16[128,2048]{1,0:T(8,128)(2,1)S(1)}, u32[]{:S(2)}, u32[]{:S(2)}) collective-permute-start(bf16[128,2048]{1,0:T(8,128)(2,1)} %get-tuple-element.70.refs_0_), channel_id=1, source_target_pairs={{0,4},{1,3},{2,6},{3,1},{4,0},{5,7},{6,2},{7,5},{8,12},{9,11},{10,... | collective-permute-start | bytes 1572872 | tf_op jit(solution)/shard_map/ppermute | solution.py:26
  43.4 13.9 %collective-permute-start.16 = (bf16[128,2048]{1,0:T(8,128)(2,1)}, bf16[128,2048]{1,0:T(8,128)(2,1)S(1)}, u32[]{:S(2)}, u32[]{:S(2)}) collective-permute-start(bf16[128,2048]{1,0:T(8,128)(2,1)} %get-tuple-element.70.refs_0_), channel_id=1, source_target_pairs={{0,2},{1,5},{2,0},{3,7},{4,6},{5,1},{6,4},{7,3},{8,10},{9,13},{10,... | collective-permute-start | bytes 1572872 | tf_op jit(solution)/shard_map/ppermute | solution.py:26
  51.6 16.8 %collective-permute-start.13 = (bf16[128,2048]{1,0:T(8,128)(2,1)S(1)}, bf16[128,2048]{1,0:T(8,128)(2,1)}, u32[]{:S(2)}, u32[]{:S(2)}) collective-permute-start(bf16[128,2048]{1,0:T(8,128)(2,1)S(1)} %collective-permute-done.12.refs_0_), channel_id=1, source_target_pairs={{8,16},{10,18},{12,20},{14,22},{16,8},{18,10},{20,12},{22,14},{9,1... | collective-permute-start | bytes 1572872 | tf_op jit(solution)/shard_map/ppermute | solution.py:217
  55.1 15.0 %collective-permute-start.15 = (bf16[128,2048]{1,0:T(8,128)(2,1)S(1)}, bf16[128,2048]{1,0:T(8,128)(2,1)}, u32[]{:S(2)}, u32[]{:S(2)}) collective-permute-start(bf16[128,2048]{1,0:T(8,128)(2,1)S(1)} %collective-permute-done.14), channel_id=1, source_target_pairs={{8,0},{10,2},{12,4},{14,6},{16,24},{18,26},{20,28},{22,30},{9,1},{... | collective-permute-start | bytes 1572872 | tf_op jit(solution)/shard_map/ppermute | solution.py:217
  57.4 14.7 %collective-permute-start.18 = (bf16[128,2048]{1,0:T(8,128)(2,1)S(1)}, bf16[128,2048]{1,0:T(8,128)(2,1)S(1)}, u32[]{:S(2)}, u32[]{:S(2)}) collective-permute-start(bf16[128,2048]{1,0:T(8,128)(2,1)S(1)} %collective-permute-done.17.refs_2_), channel_id=1, source_target_pairs={{0,2},{1,5},{2,0},{3,7},{4,6},{5,1},{6,4},{7,3},{8,10},{9,13},{10,... | collective-permute-start | bytes 1572872 | tf_op jit(solution)/shard_map/ppermute | solution.py:26
  58.7 14.6 %collective-permute-start.20 = (bf16[128,2048]{1,0:T(8,128)(2,1)S(1)}, bf16[128,2048]{1,0:T(8,128)(2,1)S(1)}, u32[]{:S(2)}, u32[]{:S(2)}) collective-permute-start(bf16[128,2048]{1,0:T(8,128)(2,1)S(1)} %collective-permute-done.12.refs_0_), channel_id=1, source_target_pairs={{0,4},{1,3},{2,6},{3,1},{4,0},{5,7},{6,2},{7,5},{8,12},{9,11},{10,... | collective-permute-start | bytes 1572872 | tf_op jit(solution)/shard_map/ppermute | solution.py:26
  59.7 14.3 %collective-permute-start.19 = (f32[16,1024]{1,0:T(8,128)S(1)}, f32[16,1024]{1,0:T(8,128)S(1)}, u32[]{:S(2)}, u32[]{:S(2)}) collective-permute-start(f32[16,1024]{1,0:T(8,128)S(1)} %pad_maximum_fusion), channel_id=1, source_target_pairs={{0,2},{2,0},{4,6},{6,4},{8,10},{10,8},{12,14},{14,12},{16,18},{18,... | collective-permute-start | bytes 196616 | tf_op jit(solution)/shard_map/ppermute | solution.py:20
  68.5 11.6 %collective-permute-start.23 = (bf16[128,2048]{1,0:T(8,128)(2,1)}, bf16[128,2048]{1,0:T(8,128)(2,1)S(1)}, u32[]{:S(2)}, u32[]{:S(2)}) collective-permute-start(bf16[128,2048]{1,0:T(8,128)(2,1)} %collective-permute-done.13), channel_id=1, source_target_pairs={{8,0},{10,2},{12,4},{14,6},{16,24},{18,26},{20,28},{22,30},{9,1},{... | collective-permute-start | bytes 1572872 | tf_op jit(solution)/shard_map/ppermute | solution.py:217
  72.1 14.1 %collective-permute-start.21 = (bf16[128,2048]{1,0:T(8,128)(2,1)S(1)}, bf16[128,2048]{1,0:T(8,128)(2,1)S(1)}, u32[]{:S(2)}, u32[]{:S(2)}) collective-permute-start(bf16[128,2048]{1,0:T(8,128)(2,1)S(1)} %broadcast_select_fusion.1.refs_2_), channel_id=1, source_target_pairs={{0,2},{1,5},{2,0},{3,7},{4,6},{5,1},{6,4},{7,3},{8,10},{9,13},{10,... | collective-permute-start | bytes 1572872 | tf_op jit(solution)/shard_map/ppermute | solution.py:26
  73.2 13.2 %collective-permute-start.22 = (bf16[128,2048]{1,0:T(8,128)(2,1)S(1)}, bf16[128,2048]{1,0:T(8,128)(2,1)S(1)}, u32[]{:S(2)}, u32[]{:S(2)}) collective-permute-start(bf16[128,2048]{1,0:T(8,128)(2,1)S(1)} %broadcast_select_fusion.1.refs_2_), channel_id=1, source_target_pairs={{0,4},{1,3},{2,6},{3,1},{4,0},{5,7},{6,2},{7,5},{8,12},{9,11},{10,... | collective-permute-start | bytes 1572872 | tf_op jit(solution)/shard_map/ppermute | solution.py:26
  86.2 13.3 %collective-permute-start.24 = (bf16[128,2048]{1,0:T(8,128)(2,1)S(1)}, bf16[128,2048]{1,0:T(8,128)(2,1)S(1)}, u32[]{:S(2)}, u32[]{:S(2)}) collective-permute-start(bf16[128,2048]{1,0:T(8,128)(2,1)S(1)} %broadcast_select_fusion.refs_5_), channel_id=1, source_target_pairs={{0,2},{1,5},{2,0},{3,7},{4,6},{5,1},{6,4},{7,3},{8,10},{9,13},{10,... | collective-permute-start | bytes 1572872 | tf_op jit(solution)/shard_map/ppermute | solution.py:26
  86.5 13.3 %collective-permute-start.26 = (bf16[128,2048]{1,0:T(8,128)(2,1)S(1)}, bf16[128,2048]{1,0:T(8,128)(2,1)S(1)}, u32[]{:S(2)}, u32[]{:S(2)}) collective-permute-start(bf16[128,2048]{1,0:T(8,128)(2,1)S(1)} %broadcast_select_fusion.refs_5_), channel_id=1, source_target_pairs={{0,4},{1,3},{2,6},{3,1},{4,0},{5,7},{6,2},{7,5},{8,12},{9,11},{10,... | collective-permute-start | bytes 1572872 | tf_op jit(solution)/shard_map/ppermute | solution.py:26
  86.5 13.3 %collective-permute-start.27 = (bf16[128,2048]{1,0:T(8,128)(2,1)S(1)}, bf16[128,2048]{1,0:T(8,128)(2,1)S(1)}, u32[]{:S(2)}, u32[]{:S(2)}) collective-permute-start(bf16[128,2048]{1,0:T(8,128)(2,1)S(1)} %collective-permute-done.16.refs_1_), channel_id=1, source_target_pairs={{0,8},{2,10},{4,12},{6,14},{8,0},{10,2},{12,4},{14,6},{16,24},{18,... | collective-permute-start | bytes 1572872 | tf_op jit(solution)/shard_map/ppermute | solution.py:20
  99.5 12.4 %collective-permute-start.25 = (bf16[128,2048]{1,0:T(8,128)(2,1)S(1)}, bf16[128,2048]{1,0:T(8,128)(2,1)S(1)}, u32[]{:S(2)}, u32[]{:S(2)}) collective-permute-start(bf16[128,2048]{1,0:T(8,128)(2,1)S(1)} %collective-permute-done.22.refs_4_), channel_id=1, source_target_pairs={{0,2},{1,5},{2,0},{3,7},{4,6},{5,1},{6,4},{7,3},{8,10},{9,13},{10,... | collective-permute-start | bytes 1572872 | tf_op jit(solution)/shard_map/ppermute | solution.py:26
  99.8 12.1 %collective-permute-start.28 = (bf16[128,2048]{1,0:T(8,128)(2,1)S(1)}, bf16[128,2048]{1,0:T(8,128)(2,1)S(1)}, u32[]{:S(2)}, u32[]{:S(2)}) collective-permute-start(bf16[128,2048]{1,0:T(8,128)(2,1)S(1)} %collective-permute-done.24.refs_0_), channel_id=1, source_target_pairs={{0,4},{1,3},{2,6},{3,1},{4,0},{5,7},{6,2},{7,5},{8,12},{9,11},{10,... | collective-permute-start | bytes 1572872 | tf_op jit(solution)/shard_map/ppermute | solution.py:26
  99.8 15.8 %collective-permute-start.36 = (bf16[128,2048]{1,0:T(8,128)(2,1)S(1)}, bf16[128,2048]{1,0:T(8,128)(2,1)S(1)}, u32[]{:S(2)}, u32[]{:S(2)}) collective-permute-start(bf16[128,2048]{1,0:T(8,128)(2,1)S(1)} %collective-permute-done.18.refs_3_), channel_id=1, source_target_pairs={{0,8},{2,10},{4,12},{6,14},{8,0},{10,2},{12,4},{14,6},{16,24},{18,... | collective-permute-start | bytes 1572872 | tf_op jit(solution)/shard_map/ppermute | solution.py:20
  115.1 12.2 %collective-permute-start.30 = (bf16[128,2048]{1,0:T(8,128)(2,1)S(1)}, bf16[128,2048]{1,0:T(8,128)(2,1)S(1)}, u32[]{:S(2)}, u32[]{:S(2)}) collective-permute-start(bf16[128,2048]{1,0:T(8,128)(2,1)S(1)} %get-tuple-element.99), channel_id=1, source_target_pairs={{0,4},{1,3},{2,6},{3,1},{4,0},{5,7},{6,2},{7,5},{8,12},{9,11},{10,... | collective-permute-start | bytes 1572872 | tf_op jit(solution)/shard_map/ppermute | solution.py:26
  115.2 12.2 %collective-permute-start.29 = (bf16[128,2048]{1,0:T(8,128)(2,1)S(1)}, bf16[128,2048]{1,0:T(8,128)(2,1)S(1)}, u32[]{:S(2)}, u32[]{:S(2)}) collective-permute-start(bf16[128,2048]{1,0:T(8,128)(2,1)S(1)} %get-tuple-element.97), channel_id=1, source_target_pairs={{0,2},{1,5},{2,0},{3,7},{4,6},{5,1},{6,4},{7,3},{8,10},{9,13},{10,... | collective-permute-start | bytes 1572872 | tf_op jit(solution)/shard_map/ppermute | solution.py:26
  115.6 16.3 %collective-permute-start.37 = (bf16[128,2048]{1,0:T(8,128)(2,1)S(1)}, bf16[128,2048]{1,0:T(8,128)(2,1)S(1)}, u32[]{:S(2)}, u32[]{:S(2)}) collective-permute-start(bf16[128,2048]{1,0:T(8,128)(2,1)S(1)} %get-tuple-element.111), channel_id=1, source_target_pairs={{0,8},{2,10},{4,12},{6,14},{8,0},{10,2},{12,4},{14,6},{16,24},{18,... | collective-permute-start | bytes 1572872 | tf_op jit(solution)/shard_map/ppermute | solution.py:20
  127.4 11.6 %collective-permute-start.34 = (bf16[128,2048]{1,0:T(8,128)(2,1)S(1)}, bf16[128,2048]{1,0:T(8,128)(2,1)S(1)}, u32[]{:S(2)}, u32[]{:S(2)}) collective-permute-start(bf16[128,2048]{1,0:T(8,128)(2,1)S(1)} %add_convert_fusion.8), channel_id=1, source_target_pairs={{0,2},{1,5},{2,0},{3,7},{4,6},{5,1},{6,4},{7,3},{8,10},{9,13},{10,... | collective-permute-start | bytes 1572872 | tf_op jit(solution)/shard_map/ppermute | solution.py:26
  128.7 12.1 %collective-permute-start.31 = (bf16[128,2048]{1,0:T(8,128)(2,1)S(1)}, bf16[128,2048]{1,0:T(8,128)(2,1)S(1)}, u32[]{:S(2)}, u32[]{:S(2)}) collective-permute-start(bf16[128,2048]{1,0:T(8,128)(2,1)S(1)} %get-tuple-element.100), channel_id=1, source_target_pairs={{0,4},{1,3},{2,6},{3,1},{4,0},{5,7},{6,2},{7,5},{8,12},{9,11},{10,... | collective-permute-start | bytes 1572872 | tf_op jit(solution)/shard_map/ppermute | solution.py:26
  131.9 11.6 %collective-permute-start.38 = (bf16[128,2048]{1,0:T(8,128)(2,1)S(1)}, bf16[128,2048]{1,0:T(8,128)(2,1)S(1)}, u32[]{:S(2)}, u32[]{:S(2)}) collective-permute-start(bf16[128,2048]{1,0:T(8,128)(2,1)S(1)} %expert_rows.9), channel_id=1, source_target_pairs={{0,8},{2,10},{4,12},{6,14},{8,0},{10,2},{12,4},{14,6},{16,24},{18,... | collective-permute-start | bytes 1572872 | tf_op jit(solution)/shard_map/ppermute | solution.py:20
  139.0 12.1 %collective-permute-start.35 = (bf16[128,2048]{1,0:T(8,128)(2,1)S(1)}, bf16[128,2048]{1,0:T(8,128)(2,1)S(1)}, u32[]{:S(2)}, u32[]{:S(2)}) collective-permute-start(bf16[128,2048]{1,0:T(8,128)(2,1)S(1)} %get-tuple-element.106), channel_id=1, source_target_pairs={{0,2},{1,5},{2,0},{3,7},{4,6},{5,1},{6,4},{7,3},{8,10},{9,13},{10,... | collective-permute-start | bytes 1572872 | tf_op jit(solution)/shard_map/ppermute | solution.py:26
  140.7 13.0 %collective-permute-start.32 = (bf16[128,2048]{1,0:T(8,128)(2,1)S(1)}, bf16[128,2048]{1,0:T(8,128)(2,1)S(1)}, u32[]{:S(2)}, u32[]{:S(2)}) collective-permute-start(bf16[128,2048]{1,0:T(8,128)(2,1)S(1)} %add_convert_fusion.9), channel_id=1, source_target_pairs={{0,4},{1,3},{2,6},{3,1},{4,0},{5,7},{6,2},{7,5},{8,12},{9,11},{10,... | collective-permute-start | bytes 1572872 | tf_op jit(solution)/shard_map/ppermute | solution.py:26
  143.5 12.7 %collective-permute-start.39 = (bf16[128,2048]{1,0:T(8,128)(2,1)S(1)}, bf16[128,2048]{1,0:T(8,128)(2,1)S(1)}, u32[]{:S(2)}, u32[]{:S(2)}) collective-permute-start(bf16[128,2048]{1,0:T(8,128)(2,1)S(1)} %add_convert_fusion.7), channel_id=1, source_target_pairs={{0,8},{2,10},{4,12},{6,14},{24,16},{26,18},{28,20},{30,22},{1,9},{... | collective-permute-start | bytes 1572872 | tf_op jit(solution)/shard_map/ppermute | solution.py:217
  151.1 12.1 %collective-permute-start.44 = (bf16[128,2048]{1,0:T(8,128)(2,1)S(1)}, bf16[128,2048]{1,0:T(8,128)(2,1)S(1)}, u32[]{:S(2)}, u32[]{:S(2)}) collective-permute-start(bf16[128,2048]{1,0:T(8,128)(2,1)S(1)} %add_convert_fusion.2), channel_id=1, source_target_pairs={{0,2},{1,5},{2,0},{3,7},{4,6},{5,1},{6,4},{7,3},{8,10},{9,13},{10,... | collective-permute-start | bytes 1572872 | tf_op jit(solution)/shard_map/ppermute | solution.py:26
  153.7 9.7 %collective-permute-start.33 = (bf16[128,2048]{1,0:T(8,128)(2,1)S(1)}, bf16[128,2048]{1,0:T(8,128)(2,1)S(1)}, u32[]{:S(2)}, u32[]{:S(2)}) collective-permute-start(bf16[128,2048]{1,0:T(8,128)(2,1)S(1)} %get-tuple-element.102), channel_id=1, source_target_pairs={{0,4},{1,3},{2,6},{3,1},{4,0},{5,7},{6,2},{7,5},{8,12},{9,11},{10,... | collective-permute-start | bytes 1572872 | tf_op jit(solution)/shard_map/ppermute | solution.py:26
  156.5 11.4 %collective-permute-start.40 = (bf16[128,2048]{1,0:T(8,128)(2,1)S(1)}, bf16[128,2048]{1,0:T(8,128)(2,1)S(1)}, u32[]{:S(2)}, u32[]{:S(2)}) collective-permute-start(bf16[128,2048]{1,0:T(8,128)(2,1)S(1)} %add_convert_fusion.6), channel_id=1, source_target_pairs={{8,16},{10,18},{12,20},{14,22},{16,8},{18,10},{20,12},{22,14},{9,1... | collective-permute-start | bytes 1572872 | tf_op jit(solution)/shard_map/ppermute | solution.py:217
  158.6 11.4 %collective-permute-start.41 = (bf16[128,2048]{1,0:T(8,128)(2,1)S(1)}, bf16[128,2048]{1,0:T(8,128)(2,1)S(1)}, u32[]{:S(2)}, u32[]{:S(2)}) collective-permute-start(bf16[128,2048]{1,0:T(8,128)(2,1)S(1)} %add_convert_fusion.6), channel_id=1, source_target_pairs={{0,8},{2,10},{4,12},{6,14},{24,16},{26,18},{28,20},{30,22},{1,9},{... | collective-permute-start | bytes 1572872 | tf_op jit(solution)/shard_map/ppermute | solution.py:217
  163.3 20.2 %copy-start.4 = (f32[128,2048]{1,0:T(8,128)S(1)}, f32[128,2048]{1,0:T(8,128)}, u32[]{:S(2)}) copy-start(f32[128,2048]{1,0:T(8,128)} %get-tuple-element.68) | copy-start | bytes 3145732
  163.4 11.2 %collective-permute-start.46 = (bf16[128,2048]{1,0:T(8,128)(2,1)S(1)}, bf16[128,2048]{1,0:T(8,128)(2,1)S(1)}, u32[]{:S(2)}, u32[]{:S(2)}) collective-permute-start(bf16[128,2048]{1,0:T(8,128)(2,1)S(1)} %add_convert_fusion.1), channel_id=1, source_target_pairs={{0,4},{1,3},{2,6},{3,1},{4,0},{5,7},{6,2},{7,5},{8,12},{9,11},{10,... | collective-permute-start | bytes 1572872 | tf_op jit(solution)/shard_map/ppermute | solution.py:26
  165.7 9.2 %collective-permute-start.45 = (bf16[128,2048]{1,0:T(8,128)(2,1)S(1)}, bf16[128,2048]{1,0:T(8,128)(2,1)S(1)}, u32[]{:S(2)}, u32[]{:S(2)}) collective-permute-start(bf16[128,2048]{1,0:T(8,128)(2,1)S(1)} %add_convert_fusion.3), channel_id=1, source_target_pairs={{0,2},{1,5},{2,0},{3,7},{4,6},{5,1},{6,4},{7,3},{8,10},{9,13},{10,... | collective-permute-start | bytes 1572872 | tf_op jit(solution)/shard_map/ppermute | solution.py:26
  170.1 11.3 %collective-permute-start.43 = (bf16[128,2048]{1,0:T(8,128)(2,1)S(1)}, bf16[128,2048]{1,0:T(8,128)(2,1)S(1)}, u32[]{:S(2)}, u32[]{:S(2)}) collective-permute-start(bf16[128,2048]{1,0:T(8,128)(2,1)S(1)} %add_convert_fusion.4), channel_id=1, source_target_pairs={{8,16},{10,18},{12,20},{14,22},{16,8},{18,10},{20,12},{22,14},{9,1... | collective-permute-start | bytes 1572872 | tf_op jit(solution)/shard_map/ppermute | solution.py:217
  174.2 9.2 %collective-permute-start.42 = (bf16[128,2048]{1,0:T(8,128)(2,1)S(1)}, bf16[128,2048]{1,0:T(8,128)(2,1)S(1)}, u32[]{:S(2)}, u32[]{:S(2)}) collective-permute-start(bf16[128,2048]{1,0:T(8,128)(2,1)S(1)} %add_convert_fusion.5), channel_id=1, source_target_pairs={{0,8},{2,10},{4,12},{6,14},{8,0},{10,2},{12,4},{14,6},{16,24},{18,... | collective-permute-start | bytes 1572872 | tf_op jit(solution)/shard_map/ppermute | solution.py:20
  (9 other events, 41.2 us)

commit v15 on v14

--- a/solution.py
+++ b/solution.py
@@ -267,9 +267,10 @@
 
     p1, py0 = add_small(p1, by_y, to_1), add_small(py0, to_y0)
     p3 = add_small(after(p3, p1), to_3)
-    by_z, by_middle = flip(after(p1, to_3), 4), shift(p3, MIDDLE)
+    by_z, by_middle = flip(p1, 4), shift(p3, MIDDLE)
     by_x, by_y = cross(after(px0, to_y0), X), cross(after(py0, by_y), Y)
-    return add(stream, p0, by_z, by_middle, by_x, by_y)
+    most = after(add(stream, p0, by_x, by_y, by_z))
+    return add(most, by_middle)
 
 
 def plane(masks, distance):

time: 186 us -> 190 us (1.022)
  starting transfers between devices: 57.1 us -> 63 us
  waiting for transfers between devices: 77.9 us -> 75.1 us
    ppermute x20, starting transfers between devices: 19.9 us -> 26.4 us  [cross(): return lax.ppermute(block, ('seq', 'exp'), pairs)]
  transfers between devices with their start and end apart: 47 -> 47, of which waited for: 25 -> 23; matrix products, arithmetic and copies ran while one was open for 3% -> 3% of each run, Pallas kernels for 18% -> 17%
where the time goes in v15:
time: 190 us; the launch traced here: 188 us
  waiting for transfers between devices  75.1 us (40%)
  starting transfers between devices  63 us (33%)
  Pallas kernels  37.1 us (20%)
  local copies, waits for them, and re-layouts  6.87 us (4%)
  other arithmetic  5.52 us (3%)
    ppermute x20, waiting for transfers between devices, cross(): return lax.ppermute(block, ('seq', 'exp'), pairs)  44.9 us
    ppermute x20, starting transfers between devices, cross(): return lax.ppermute(block, ('seq', 'exp'), pairs)  26.4 us
    pallas_call x5, Pallas kernels, expert(): pl.pallas_call(functools.partial(expert_kernel, places, len(gates)), out_...  25.6 us
    ppermute x8, starting transfers between devices, shift(): lax.ppermute(block, 'seq', [(4 * a + i, 4 * b + i) for a, b in pairs for...  21.2 us
    ppermute x12, waiting for transfers between devices, flip(): return lax.ppermute(block, 'seq', [(i, i ^ mask) for i in range(count)])  19.3 us
    ppermute x8, waiting for transfers between devices, shift(): lax.ppermute(block, 'seq', [(4 * a + i, 4 * b + i) for a, b in pairs for...  9.42 us
    ppermute x12, starting transfers between devices, flip(): return lax.ppermute(block, 'seq', [(i, i ^ mask) for i in range(count)])  8.34 us
    ppermute x2, starting transfers between devices, halo(): return (beside, part, lax.ppermute(beside, 'seq', ahead + back))  6.6 us
  transfers between devices with their start and end apart: 47, of which 23 were waited for; matrix products, arithmetic and copies ran while one was open for 3% of the time, Pallas kernels for 17%

profile of v15, /device:TPU:10, one launch (start us, length us, event | category | flops | bytes accessed | tf_op | source)
XLA Modules:
  0.0 188.0 jit_solution(16048146600581223416)
XLA Ops:
  0.5 1.5 collective-permute-start.2
  3.3 3.2 %collective-permute-done.7.refs_5_.refs_7_.refs_4_.refs_3_.refs_2_ = f32[16,128]{1,0:T(8,128)S(1)} collective-permute-done((f32[16,128]{1,0:T(8,128)S(1)}, f32[16,128]{1,0:T(8,128)S(1)}, u32[]{:S(2)}, u32[]{:S(2)}) %collective-permute-start.7) | collective-permute-done | bytes 8224 | tf_op jit(solution)/shard_map/ppermute | solution.py:20
  6.5 2.6 %collective-permute-start.8 = (f32[16,256]{1,0:T(8,128)S(1)}, f32[16,256]{1,0:T(8,128)S(1)}, u32[]{:S(2)}, u32[]{:S(2)}) collective-permute-start(f32[16,256]{1,0:T(8,128)S(1)} %pad_maximum_fusion.2), channel_id=1, source_target_pairs={{0,16},{2,18},{4,20},{6,22},{8,24},{10,26},{12,28},{14,30},{16,0},... | collective-permute-start | bytes 49160 | tf_op jit(solution)/shard_map/ppermute | solution.py:20
  9.3 3.3 %collective-permute-start.1 = (bf16[256,512]{1,0:T(8,128)(2,1)S(1)}, bf16[256,512]{1,0:T(8,128)(2,1)S(1)}, u32[]{:S(2)}, u32[]{:S(2)}) collective-permute-start(bf16[256,512]{1,0:T(8,128)(2,1)S(1)} %collective-permute-done.refs_0_), channel_id=1, source_target_pairs={{0,4},{4,8},{8,12},{12,16},{16,20},{20,24},{24,28},{6,2},{10,6},{1... | collective-permute-start | bytes 786440 | tf_op jit(solution)/shard_map/ppermute | solution.py:331
  12.6 1.9 %collective-permute-done.2.refs_3_ = bf16[256,512]{1,0:T(8,128)(2,1)S(1)} collective-permute-done((bf16[256,512]{1,0:T(8,128)(2,1)}, bf16[256,512]{1,0:T(8,128)(2,1)S(1)}, u32[]{:S(2)}, u32[]{:S(2)}) %collective-permute-start.2) | collective-permute-done | bytes 262176 | tf_op jit(solution)/shard_map/ppermute | solution.py:20
  14.6 3.3 %collective-permute-start.3 = (bf16[256,512]{1,0:T(8,128)(2,1)S(1)}, bf16[256,512]{1,0:T(8,128)(2,1)S(1)}, u32[]{:S(2)}, u32[]{:S(2)}) collective-permute-start(bf16[256,512]{1,0:T(8,128)(2,1)S(1)} %collective-permute-done.2.refs_3_), channel_id=1, source_target_pairs={{0,4},{4,8},{8,12},{12,16},{16,20},{20,24},{24,28},{6,2},{10,6},{1... | collective-permute-start | bytes 786440 | tf_op jit(solution)/shard_map/ppermute | solution.py:331
  20.5 4.5 %collective-permute-done.9.refs_7_.refs_9_.refs_6_.refs_5_.refs_4_ = f32[16,512]{1,0:T(8,128)S(1)} collective-permute-done((f32[16,512]{1,0:T(8,128)S(1)}, f32[16,512]{1,0:T(8,128)S(1)}, u32[]{:S(2)}, u32[]{:S(2)}) %collective-permute-start.9) | collective-permute-done | bytes 32800 | tf_op jit(solution)/shard_map/ppermute | solution.py:20
  26.4 4.6 %window_attention.1 = (bf16[128,512]{1,0:T(8,128)(2,1)}, bf16[128,512]{1,0:T(8,128)(2,1)}) custom-call(s32[2]{0:T(128)} %pad_add_fusion.where_ref, bf16[256,512]{1,0:T(8,128)(2,1)} %q_ref.1, s32[1,768]{1,0:T(1,128)} %broadcast_in_dim.21.ids_ref, bf16[256,512]{1,0:T(8,128)(2,1)} %copy-done.5, bf16[256,512]{1,0:T(8,128)(2,1)} %refs_1_.1, ...), custom_call_target="tpu_custom_call" | custom-call | tf_op jit(solution)/shard_map/window_attention/pallas_call | solution.py:97
  33.2 4.3 %project_and_norm.1 = (f32[128,2048]{1,0:T(8,128)}, bf16[128,2048]{1,0:T(8,128)(2,1)}) custom-call(bf16[128,512]{1,0:T(8,128)(2,1)} %get-tuple-element.63.mine_ref, bf16[128,512]{1,0:T(8,128)(2,1)} %copy-done.9, bf16[512,2048]{1,0:T(8,128)(2,1)} %own_w.1, bf16[512,2048]{1,0:T(8,128)(2,1)} %collective-permute-done.4.refs_6_.other_w, ...), custom_call_target="tpu_custom_call" | custom-call | tf_op jit(solution)/shard_map/project_and_norm/pallas_call | solution.py:120
  37.9 4.6 %collective-permute-start.14 = (bf16[128,2048]{1,0:T(8,128)(2,1)}, bf16[128,2048]{1,0:T(8,128)(2,1)S(1)}, u32[]{:S(2)}, u32[]{:S(2)}) collective-permute-start(bf16[128,2048]{1,0:T(8,128)(2,1)} %get-tuple-element.69.refs_0_), channel_id=1, source_target_pairs={{8,16},{10,18},{12,20},{14,22},{16,8},{18,10},{20,12},{22,14},{9,1... | collective-permute-start | bytes 1572872 | tf_op jit(solution)/shard_map/ppermute | solution.py:217
  44.6 7.0 %collective-permute-done.12.refs_0_ = bf16[128,2048]{1,0:T(8,128)(2,1)S(1)} collective-permute-done((bf16[128,2048]{1,0:T(8,128)(2,1)}, bf16[128,2048]{1,0:T(8,128)(2,1)S(1)}, u32[]{:S(2)}, u32[]{:S(2)}) %collective-permute-start.12) | collective-permute-done | bytes 524320 | tf_op jit(solution)/shard_map/ppermute | solution.py:20
  51.6 3.5 %collective-permute-start.13 = (bf16[128,2048]{1,0:T(8,128)(2,1)S(1)}, bf16[128,2048]{1,0:T(8,128)(2,1)}, u32[]{:S(2)}, u32[]{:S(2)}) collective-permute-start(bf16[128,2048]{1,0:T(8,128)(2,1)S(1)} %collective-permute-done.12.refs_0_), channel_id=1, source_target_pairs={{8,16},{10,18},{12,20},{14,22},{16,8},{18,10},{20,12},{22,14},{9,1... | collective-permute-start | bytes 1572872 | tf_op jit(solution)/shard_map/ppermute | solution.py:217
  55.1 2.1 %collective-permute-start.15 = (bf16[128,2048]{1,0:T(8,128)(2,1)S(1)}, bf16[128,2048]{1,0:T(8,128)(2,1)}, u32[]{:S(2)}, u32[]{:S(2)}) collective-permute-start(bf16[128,2048]{1,0:T(8,128)(2,1)S(1)} %collective-permute-done.14), channel_id=1, source_target_pairs={{8,0},{10,2},{12,4},{14,6},{16,24},{18,26},{20,28},{22,30},{9,1},{... | collective-permute-start | bytes 1572872 | tf_op jit(solution)/shard_map/ppermute | solution.py:217
  57.4 1.3 collective-permute-start.18
  59.7 2.0 %collective-permute-start.19 = (f32[16,1024]{1,0:T(8,128)S(1)}, f32[16,1024]{1,0:T(8,128)S(1)}, u32[]{:S(2)}, u32[]{:S(2)}) collective-permute-start(f32[16,1024]{1,0:T(8,128)S(1)} %pad_maximum_fusion), channel_id=1, source_target_pairs={{0,2},{2,0},{4,6},{6,4},{8,10},{10,8},{12,14},{14,12},{16,18},{18,... | collective-permute-start | bytes 196616 | tf_op jit(solution)/shard_map/ppermute | solution.py:20
  61.7 1.4 copy-done
  63.1 1.4 copy-done.1
  64.4 1.4 copy-done.2
  65.8 2.6 %assemble_weights.1 = (bf16[1408,2048]{1,0:T(8,128)(2,1)S(1)}, bf16[704,2048]{1,0:T(8,128)(2,1)S(1)}) custom-call(bf16[352,2048]{1,0:T(8,128)(2,1)S(1)} %bitcast.14, bf16[352,2048]{1,0:T(8,128)(2,1)} %collective-permute-done.5.refs_7_.refs_1_, bf16[352,2048]{1,0:T(8,128)(2,1)S(1)} %bitcast.16, bf16[352,2048]{1,0:T(8,128)(2,1)} %collective-permute-done.10.refs_0_.refs_3_, ...), custom_call_target="tpu_custom_call" | custom-call | tf_op jit(solution)/shard_map/assemble_weights/pallas_call | solution.py:148
  68.5 1.6 collective-permute-start.20
  74.1 5.6 %expert_rows.5 = (bf16[128,2048]{1,0:T(8,128)(2,1)S(1)}, bf16[128,2048]{1,0:T(8,128)(2,1)S(1)}, bf16[128,2048]{1,0:T(8,128)(2,1)S(1)}, bf16[128,2048]{1,0:T(8,128)(2,1)S(1)}) custom-call(s32[2]{0:T(128)S(1)} %pad_add_fusion.1.where_ref, bf16[128,2048]{1,0:T(8,128)(2,1)S(1)} %copy-done.3, bf16[128,2048]{1,0:T(8,128)(2,1)S(1)} %collective-permute-done.16.refs_1_, ...), custom_call_target="tpu_custom_call" | custom-call | tf_op jit(solution)/shard_map/expert_rows/pallas_call | solution.py:195
  80.1 6.1 %collective-permute-done.21.refs_3_ = bf16[128,2048]{1,0:T(8,128)(2,1)S(1)} collective-permute-done((bf16[128,2048]{1,0:T(8,128)(2,1)S(1)}, bf16[128,2048]{1,0:T(8,128)(2,1)S(1)}, u32[]{:S(2)}, u32[]{:S(2)}) %collective-permute-start.21) | collective-permute-done | bytes 524320 | tf_op jit(solution)/shard_map/ppermute | solution.py:26
  86.5 1.7 collective-permute-start.25
  88.2 8.1 %expert_rows.6 = (bf16[128,2048]{1,0:T(8,128)(2,1)S(1)}, bf16[128,2048]{1,0:T(8,128)(2,1)S(1)}, bf16[128,2048]{1,0:T(8,128)(2,1)S(1)}, bf16[128,2048]{1,0:T(8,12...) custom-call(s32[2]{0:T(128)S(1)} %pad_add_fusion.1.where_ref, ...), custom_call_target="tpu_custom_call" | custom-call | tf_op jit(solution)/shard_map/expert_rows/pallas_call | solution.py:195
  96.4 3.2 %collective-permute-done.22.refs_0_ = bf16[128,2048]{1,0:T(8,128)(2,1)S(1)} collective-permute-done((bf16[128,2048]{1,0:T(8,128)(2,1)S(1)}, bf16[128,2048]{1,0:T(8,128)(2,1)S(1)}, u32[]{:S(2)}, u32[]{:S(2)}) %collective-permute-start.22) | collective-permute-done | bytes 524320 | tf_op jit(solution)/shard_map/ppermute | solution.py:26
  99.8 2.1 %collective-permute-start.30 = (bf16[128,2048]{1,0:T(8,128)(2,1)S(1)}, bf16[128,2048]{1,0:T(8,128)(2,1)S(1)}, u32[]{:S(2)}, u32[]{:S(2)}) collective-permute-start(bf16[128,2048]{1,0:T(8,128)(2,1)S(1)} %collective-permute-done.22.refs_0_), channel_id=1, source_target_pairs={{0,4},{1,3},{2,6},{3,1},{4,0},{5,7},{6,2},{7,5},{8,12},{9,11},{10,... | collective-permute-start | bytes 1572872 | tf_op jit(solution)/shard_map/ppermute | solution.py:26
  101.9 5.7 %expert_rows.7 = (bf16[128,2048]{1,0:T(8,128)(2,1)S(1)}, bf16[128,2048]{1,0:T(8,128)(2,1)S(1)}, bf16[128,2048]{1,0:T(8,128)(2,1)S(1)}) custom-call(s32[2]{0:T(128)S(1)} %pad_add_fusion.1.where_ref, bf16[128,2048]{1,0:T(8,128)(2,1)S(1)} %collective-permute-done.22.refs_0_, bf16[128,2048]{1,0:T(8,128)(2,1)S(1)} %collective-permute-done.25.refs_1_, ...), custom_call_target="tpu_custom_call" | custom-call | tf_op jit(solution)/shard_map/expert_rows/pallas_call | solution.py:195
  107.6 4.4 %collective-permute-done.29.refs_0_ = bf16[128,2048]{1,0:T(8,128)(2,1)S(1)} collective-permute-done((bf16[128,2048]{1,0:T(8,128)(2,1)S(1)}, bf16[128,2048]{1,0:T(8,128)(2,1)S(1)}, u32[]{:S(2)}, u32[]{:S(2)}) %collective-permute-start.29) | collective-permute-done | bytes 524320 | tf_op jit(solution)/shard_map/ppermute | solution.py:26
  112.0 3.2 %expert_rows.8 = (bf16[128,2048]{1,0:T(8,128)(2,1)S(1)}, bf16[128,2048]{1,0:T(8,128)(2,1)S(1)}) custom-call(s32[2]{0:T(128)S(1)} %pad_add_fusion.1.where_ref, bf16[128,2048]{1,0:T(8,128)(2,1)S(1)} %collective-permute-done.29.refs_0_, bf16[128,2048]{1,0:T(8,128)(2,1)S(1)} %collective-permute-done.30.refs_1_, ...), custom_call_target="tpu_custom_call" | custom-call | tf_op jit(solution)/shard_map/expert_rows/pallas_call | solution.py:195
  115.2 2.5 %collective-permute-start.32 = (bf16[128,2048]{1,0:T(8,128)(2,1)S(1)}, bf16[128,2048]{1,0:T(8,128)(2,1)S(1)}, u32[]{:S(2)}, u32[]{:S(2)}) collective-permute-start(bf16[128,2048]{1,0:T(8,128)(2,1)S(1)} %get-tuple-element.103), channel_id=1, source_target_pairs={{0,4},{1,3},{2,6},{3,1},{4,0},{5,7},{6,2},{7,5},{8,12},{9,11},{10,... | collective-permute-start | bytes 1572872 | tf_op jit(solution)/shard_map/ppermute | solution.py:26
  118.0 9.9 %collective-permute-done.32 = bf16[128,2048]{1,0:T(8,128)(2,1)S(1)} collective-permute-done((bf16[128,2048]{1,0:T(8,128)(2,1)S(1)}, bf16[128,2048]{1,0:T(8,128)(2,1)S(1)}, u32[]{:S(2)}, u32[]{:S(2)}) %collective-permute-start.32) | collective-permute-done | bytes 524320 | tf_op jit(solution)/shard_map/ppermute | solution.py:26
  127.9 1.9 %collective-permute-start.38 = (bf16[128,2048]{1,0:T(8,128)(2,1)S(1)}, bf16[128,2048]{1,0:T(8,128)(2,1)S(1)}, u32[]{:S(2)}, u32[]{:S(2)}) collective-permute-start(bf16[128,2048]{1,0:T(8,128)(2,1)S(1)} %get-tuple-element.112), channel_id=1, source_target_pairs={{0,4},{1,3},{2,6},{3,1},{4,0},{5,7},{6,2},{7,5},{8,12},{9,11},{10,... | collective-permute-start | bytes 1572872 | tf_op jit(solution)/shard_map/ppermute | solution.py:26
  129.9 1.6 collective-permute-start.34
  131.5 2.9 %expert_rows.9 = bf16[128,2048]{1,0:T(8,128)(2,1)S(1)} custom-call(s32[2]{0:T(128)S(1)} %pad_add_fusion.1.where_ref, bf16[128,2048]{1,0:T(8,128)(2,1)S(1)} %collective-permute-done.27.refs_0_, f32[16,128]{1,0:T(8,128)S(1)} %select_reduce_fusion.refs_4_.refs_6_.refs_3_.refs_2_.refs_1_, ...), custom_call_target="tpu_custom_call" | custom-call | tf_op jit(solution)/shard_map/expert_rows/pallas_call | solution.py:195
  134.7 5.3 %collective-permute-done.38 = bf16[128,2048]{1,0:T(8,128)(2,1)S(1)} collective-permute-done((bf16[128,2048]{1,0:T(8,128)(2,1)S(1)}, bf16[128,2048]{1,0:T(8,128)(2,1)S(1)}, u32[]{:S(2)}, u32[]{:S(2)}) %collective-permute-start.38) | collective-permute-done | bytes 524320 | tf_op jit(solution)/shard_map/ppermute | solution.py:26
  140.0 2.3 %collective-permute-start.35 = (bf16[128,2048]{1,0:T(8,128)(2,1)S(1)}, bf16[128,2048]{1,0:T(8,128)(2,1)S(1)}, u32[]{:S(2)}, u32[]{:S(2)}) collective-permute-start(bf16[128,2048]{1,0:T(8,128)(2,1)S(1)} %get-tuple-element.105), channel_id=1, source_target_pairs={{0,2},{1,5},{2,0},{3,7},{4,6},{5,1},{6,4},{7,3},{8,10},{9,13},{10,... | collective-permute-start | bytes 1572872 | tf_op jit(solution)/shard_map/ppermute | solution.py:26
  142.3 1.4 collective-permute-start.39
  145.4 7.7 %collective-permute-done.35 = bf16[128,2048]{1,0:T(8,128)(2,1)S(1)} collective-permute-done((bf16[128,2048]{1,0:T(8,128)(2,1)S(1)}, bf16[128,2048]{1,0:T(8,128)(2,1)S(1)}, u32[]{:S(2)}, u32[]{:S(2)}) %collective-permute-start.35) | collective-permute-done | bytes 524320 | tf_op jit(solution)/shard_map/ppermute | solution.py:26
  153.1 1.7 collective-permute-start.36
  157.1 1.9 %collective-permute-start.43 = (bf16[128,2048]{1,0:T(8,128)(2,1)S(1)}, bf16[128,2048]{1,0:T(8,128)(2,1)S(1)}, u32[]{:S(2)}, u32[]{:S(2)}) collective-permute-start(bf16[128,2048]{1,0:T(8,128)(2,1)S(1)} %add_convert_fusion.3), channel_id=1, source_target_pairs={{8,16},{10,18},{12,20},{14,22},{16,8},{18,10},{20,12},{22,14},{9,1... | collective-permute-start | bytes 1572872 | tf_op jit(solution)/shard_map/ppermute | solution.py:217
  159.2 1.3 collective-permute-start.45
  160.5 4.7 %collective-permute-done.36 = bf16[128,2048]{1,0:T(8,128)(2,1)S(1)} collective-permute-done((bf16[128,2048]{1,0:T(8,128)(2,1)S(1)}, bf16[128,2048]{1,0:T(8,128)(2,1)S(1)}, u32[]{:S(2)}, u32[]{:S(2)}) %collective-permute-start.36) | collective-permute-done | bytes 524320 | tf_op jit(solution)/shard_map/ppermute | solution.py:26
  165.2 1.7 collective-permute-start.37
  167.1 2.1 %collective-permute-done.40 = bf16[128,2048]{1,0:T(8,128)(2,1)S(1)} collective-permute-done((bf16[128,2048]{1,0:T(8,128)(2,1)S(1)}, bf16[128,2048]{1,0:T(8,128)(2,1)S(1)}, u32[]{:S(2)}, u32[]{:S(2)}) %collective-permute-start.40) | collective-permute-done | bytes 524320 | tf_op jit(solution)/shard_map/ppermute | solution.py:26
  170.5 4.5 %collective-permute-done.45 = bf16[128,2048]{1,0:T(8,128)(2,1)S(1)} collective-permute-done((bf16[128,2048]{1,0:T(8,128)(2,1)S(1)}, bf16[128,2048]{1,0:T(8,128)(2,1)S(1)}, u32[]{:S(2)}, u32[]{:S(2)}) %collective-permute-start.45) | collective-permute-done | bytes 524320 | tf_op jit(solution)/shard_map/ppermute | solution.py:217
  175.1 4.9 %collective-permute-start.46 = (bf16[128,2048]{1,0:T(8,128)(2,1)S(1)}, bf16[128,2048]{1,0:T(8,128)(2,1)S(1)}, u32[]{:S(2)}, u32[]{:S(2)}) collective-permute-start(bf16[128,2048]{1,0:T(8,128)(2,1)S(1)} %add_convert_fusion.1), channel_id=1, source_target_pairs={{8,16},{10,18},{12,20},{14,22},{16,8},{18,10},{20,12},{22,14},{9,1... | collective-permute-start | bytes 1572872 | tf_op jit(solution)/shard_map/ppermute | solution.py:217
  180.0 2.4 %collective-permute-done.44 = bf16[128,2048]{1,0:T(8,128)(2,1)S(1)} collective-permute-done((bf16[128,2048]{1,0:T(8,128)(2,1)S(1)}, bf16[128,2048]{1,0:T(8,128)(2,1)S(1)}, u32[]{:S(2)}, u32[]{:S(2)}) %collective-permute-start.44) | collective-permute-done | bytes 524320 | tf_op jit(solution)/shard_map/ppermute | solution.py:20
  182.7 4.4 %collective-permute-done.46 = bf16[128,2048]{1,0:T(8,128)(2,1)S(1)} collective-permute-done((bf16[128,2048]{1,0:T(8,128)(2,1)S(1)}, bf16[128,2048]{1,0:T(8,128)(2,1)S(1)}, u32[]{:S(2)}, u32[]{:S(2)}) %collective-permute-start.46) | collective-permute-done | bytes 524320 | tf_op jit(solution)/shard_map/ppermute | solution.py:217
  (95 shorter events, 24.3 us)
Async XLA Ops:
  0.0 26.3 %collective-permute-start.4 = (bf16[512,2048]{1,0:T(8,128)(2,1)}, bf16[512,2048]{1,0:T(8,128)(2,1)}, u32[]{:S(2)}, u32[]{:S(2)}) collective-permute-start(bf16[512,2048]{1,0:T(8,128)(2,1)} %own_w.1), channel_id=1, source_target_pairs={{0,1},{1,0},{2,3},{3,2},{4,5},{5,4},{6,7},{7,6},{8,9},{9,8},{10,11... | collective-permute-start | bytes 6291464 | tf_op jit(solution)/shard_map/ppermute | solution.py:340
  0.0 9.3 %collective-permute-start = (bf16[256,512]{1,0:T(8,128)(2,1)}, bf16[256,512]{1,0:T(8,128)(2,1)S(1)}, u32[]{:S(2)}, u32[]{:S(2)}) collective-permute-start(bf16[256,512]{1,0:T(8,128)(2,1)} %refs_1_.1), channel_id=1, source_target_pairs={{0,2},{2,0},{4,6},{6,4},{8,10},{10,8},{12,14},{14,12},{16,18},{18,... | collective-permute-start | bytes 786440 | tf_op jit(solution)/shard_map/ppermute | solution.py:20
  0.5 14.0 %collective-permute-start.2 = (bf16[256,512]{1,0:T(8,128)(2,1)}, bf16[256,512]{1,0:T(8,128)(2,1)S(1)}, u32[]{:S(2)}, u32[]{:S(2)}) collective-permute-start(bf16[256,512]{1,0:T(8,128)(2,1)} %refs_4_.1), channel_id=1, source_target_pairs={{0,2},{2,0},{4,6},{6,4},{8,10},{10,8},{12,14},{14,12},{16,18},{18,... | collective-permute-start | bytes 786440 | tf_op jit(solution)/shard_map/ppermute | solution.py:20
  2.7 3.7 %collective-permute-start.7 = (f32[16,128]{1,0:T(8,128)S(1)}, f32[16,128]{1,0:T(8,128)S(1)}, u32[]{:S(2)}, u32[]{:S(2)}) collective-permute-start(f32[16,128]{1,0:T(8,128)S(1)} %select_reduce_fusion.refs_4_.refs_6_.refs_3_.refs_2_.refs_1_), channel_id=1, source_target_pairs={{0,8},{2,10},{4,12},{6,14},{8,0},{10,2},{12,4},{14,6},{16,24},{18,... | collective-permute-start | bytes 24584 | tf_op jit(solution)/shard_map/ppermute | solution.py:20
  3.3 23.1 %collective-permute-start.5 = (bf16[352,2048]{1,0:T(8,128)(2,1)}, bf16[352,2048]{1,0:T(8,128)(2,1)}, u32[]{:S(2)}, u32[]{:S(2)}) collective-permute-start(bf16[352,2048]{1,0:T(8,128)(2,1)} %bitcast.13), channel_id=1, source_target_pairs={{0,1},{1,0},{2,3},{3,2},{4,5},{5,4},{6,7},{7,6},{8,9},{9,8},{10,11... | collective-permute-start | bytes 4325384 | tf_op jit(solution)/shard_map/ppermute | solution.py:342
  6.5 12.2 %collective-permute-start.8 = (f32[16,256]{1,0:T(8,128)S(1)}, f32[16,256]{1,0:T(8,128)S(1)}, u32[]{:S(2)}, u32[]{:S(2)}) collective-permute-start(f32[16,256]{1,0:T(8,128)S(1)} %pad_maximum_fusion.2), channel_id=1, source_target_pairs={{0,16},{2,18},{4,20},{6,22},{8,24},{10,26},{12,28},{14,30},{16,0},... | collective-permute-start | bytes 49160 | tf_op jit(solution)/shard_map/ppermute | solution.py:20
  9.3 17.0 %copy-start.5 = (bf16[256,512]{1,0:T(8,128)(2,1)}, bf16[256,512]{1,0:T(8,128)(2,1)S(1)}, u32[]{:S(2)}) copy-start(bf16[256,512]{1,0:T(8,128)(2,1)S(1)} %collective-permute-done.refs_0_) | copy-start | bytes 786436
  9.3 15.8 %collective-permute-start.1 = (bf16[256,512]{1,0:T(8,128)(2,1)S(1)}, bf16[256,512]{1,0:T(8,128)(2,1)S(1)}, u32[]{:S(2)}, u32[]{:S(2)}) collective-permute-start(bf16[256,512]{1,0:T(8,128)(2,1)S(1)} %collective-permute-done.refs_0_), channel_id=1, source_target_pairs={{0,4},{4,8},{8,12},{12,16},{16,20},{20,24},{24,28},{6,2},{10,6},{1... | collective-permute-start | bytes 786440 | tf_op jit(solution)/shard_map/ppermute | solution.py:331
  14.6 10.5 %collective-permute-start.3 = (bf16[256,512]{1,0:T(8,128)(2,1)S(1)}, bf16[256,512]{1,0:T(8,128)(2,1)S(1)}, u32[]{:S(2)}, u32[]{:S(2)}) collective-permute-start(bf16[256,512]{1,0:T(8,128)(2,1)S(1)} %collective-permute-done.2.refs_3_), channel_id=1, source_target_pairs={{0,4},{4,8},{8,12},{12,16},{16,20},{20,24},{24,28},{6,2},{10,6},{1... | collective-permute-start | bytes 786440 | tf_op jit(solution)/shard_map/ppermute | solution.py:331
  18.7 6.4 %collective-permute-start.9 = (f32[16,512]{1,0:T(8,128)S(1)}, f32[16,512]{1,0:T(8,128)S(1)}, u32[]{:S(2)}, u32[]{:S(2)}) collective-permute-start(f32[16,512]{1,0:T(8,128)S(1)} %pad_maximum_fusion.1), channel_id=1, source_target_pairs={{0,4},{2,6},{4,0},{6,2},{8,12},{10,14},{12,8},{14,10},{16,20},{18,... | collective-permute-start | bytes 98312 | tf_op jit(solution)/shard_map/ppermute | solution.py:20
  25.8 5.1 %collective-permute-start.10 = (bf16[352,2048]{1,0:T(8,128)(2,1)}, bf16[352,2048]{1,0:T(8,128)(2,1)}, u32[]{:S(2)}, u32[]{:S(2)}) collective-permute-start(bf16[352,2048]{1,0:T(8,128)(2,1)} %bitcast.15), channel_id=1, source_target_pairs={{0,1},{1,0},{2,3},{3,2},{4,5},{5,4},{6,7},{7,6},{8,9},{9,8},{10,11... | collective-permute-start | bytes 4325384 | tf_op jit(solution)/shard_map/ppermute | solution.py:345
  25.8 5.6 %collective-permute-start.11 = (bf16[352,2048]{1,0:T(8,128)(2,1)}, bf16[352,2048]{1,0:T(8,128)(2,1)}, u32[]{:S(2)}, u32[]{:S(2)}) collective-permute-start(bf16[352,2048]{1,0:T(8,128)(2,1)} %bitcast.17), channel_id=1, source_target_pairs={{0,1},{1,0},{2,3},{3,2},{4,5},{5,4},{6,7},{7,6},{8,9},{9,8},{10,11... | collective-permute-start | bytes 4325384 | tf_op jit(solution)/shard_map/ppermute | solution.py:346
  30.9 1.6 collective-permute-start.6
  37.5 14.2 %collective-permute-start.12 = (bf16[128,2048]{1,0:T(8,128)(2,1)}, bf16[128,2048]{1,0:T(8,128)(2,1)S(1)}, u32[]{:S(2)}, u32[]{:S(2)}) collective-permute-start(bf16[128,2048]{1,0:T(8,128)(2,1)} %get-tuple-element.69.refs_0_), channel_id=1, source_target_pairs={{0,8},{2,10},{4,12},{6,14},{8,0},{10,2},{12,4},{14,6},{16,24},{18,... | collective-permute-start | bytes 1572872 | tf_op jit(solution)/shard_map/ppermute | solution.py:20
  37.9 17.2 %collective-permute-start.14 = (bf16[128,2048]{1,0:T(8,128)(2,1)}, bf16[128,2048]{1,0:T(8,128)(2,1)S(1)}, u32[]{:S(2)}, u32[]{:S(2)}) collective-permute-start(bf16[128,2048]{1,0:T(8,128)(2,1)} %get-tuple-element.69.refs_0_), channel_id=1, source_target_pairs={{8,16},{10,18},{12,20},{14,22},{16,8},{18,10},{20,12},{22,14},{9,1... | collective-permute-start | bytes 1572872 | tf_op jit(solution)/shard_map/ppermute | solution.py:217
  42.5 14.8 %collective-permute-start.17 = (bf16[128,2048]{1,0:T(8,128)(2,1)}, bf16[128,2048]{1,0:T(8,128)(2,1)S(1)}, u32[]{:S(2)}, u32[]{:S(2)}) collective-permute-start(bf16[128,2048]{1,0:T(8,128)(2,1)} %get-tuple-element.69.refs_0_), channel_id=1, source_target_pairs={{0,4},{1,3},{2,6},{3,1},{4,0},{5,7},{6,2},{7,5},{8,12},{9,11},{10,... | collective-permute-start | bytes 1572872 | tf_op jit(solution)/shard_map/ppermute | solution.py:26
  43.4 13.9 %collective-permute-start.16 = (bf16[128,2048]{1,0:T(8,128)(2,1)}, bf16[128,2048]{1,0:T(8,128)(2,1)S(1)}, u32[]{:S(2)}, u32[]{:S(2)}) collective-permute-start(bf16[128,2048]{1,0:T(8,128)(2,1)} %get-tuple-element.69.refs_0_), channel_id=1, source_target_pairs={{0,2},{1,5},{2,0},{3,7},{4,6},{5,1},{6,4},{7,3},{8,10},{9,13},{10,... | collective-permute-start | bytes 1572872 | tf_op jit(solution)/shard_map/ppermute | solution.py:26
  51.6 16.8 %collective-permute-start.13 = (bf16[128,2048]{1,0:T(8,128)(2,1)S(1)}, bf16[128,2048]{1,0:T(8,128)(2,1)}, u32[]{:S(2)}, u32[]{:S(2)}) collective-permute-start(bf16[128,2048]{1,0:T(8,128)(2,1)S(1)} %collective-permute-done.12.refs_0_), channel_id=1, source_target_pairs={{8,16},{10,18},{12,20},{14,22},{16,8},{18,10},{20,12},{22,14},{9,1... | collective-permute-start | bytes 1572872 | tf_op jit(solution)/shard_map/ppermute | solution.py:217
  55.1 15.0 %collective-permute-start.15 = (bf16[128,2048]{1,0:T(8,128)(2,1)S(1)}, bf16[128,2048]{1,0:T(8,128)(2,1)}, u32[]{:S(2)}, u32[]{:S(2)}) collective-permute-start(bf16[128,2048]{1,0:T(8,128)(2,1)S(1)} %collective-permute-done.14), channel_id=1, source_target_pairs={{8,0},{10,2},{12,4},{14,6},{16,24},{18,26},{20,28},{22,30},{9,1},{... | collective-permute-start | bytes 1572872 | tf_op jit(solution)/shard_map/ppermute | solution.py:217
  57.4 14.7 %collective-permute-start.18 = (bf16[128,2048]{1,0:T(8,128)(2,1)S(1)}, bf16[128,2048]{1,0:T(8,128)(2,1)S(1)}, u32[]{:S(2)}, u32[]{:S(2)}) collective-permute-start(bf16[128,2048]{1,0:T(8,128)(2,1)S(1)} %collective-permute-done.17.refs_2_), channel_id=1, source_target_pairs={{0,2},{1,5},{2,0},{3,7},{4,6},{5,1},{6,4},{7,3},{8,10},{9,13},{10,... | collective-permute-start | bytes 1572872 | tf_op jit(solution)/shard_map/ppermute | solution.py:26
  58.7 12.6 %collective-permute-start.23 = (bf16[128,2048]{1,0:T(8,128)(2,1)S(1)}, bf16[128,2048]{1,0:T(8,128)(2,1)S(1)}, u32[]{:S(2)}, u32[]{:S(2)}) collective-permute-start(bf16[128,2048]{1,0:T(8,128)(2,1)S(1)} %collective-permute-done.12.refs_0_), channel_id=1, source_target_pairs={{0,4},{1,3},{2,6},{3,1},{4,0},{5,7},{6,2},{7,5},{8,12},{9,11},{10,... | collective-permute-start | bytes 1572872 | tf_op jit(solution)/shard_map/ppermute | solution.py:26
  59.7 14.3 %collective-permute-start.19 = (f32[16,1024]{1,0:T(8,128)S(1)}, f32[16,1024]{1,0:T(8,128)S(1)}, u32[]{:S(2)}, u32[]{:S(2)}) collective-permute-start(f32[16,1024]{1,0:T(8,128)S(1)} %pad_maximum_fusion), channel_id=1, source_target_pairs={{0,2},{2,0},{4,6},{6,4},{8,10},{10,8},{12,14},{14,12},{16,18},{18,... | collective-permute-start | bytes 196616 | tf_op jit(solution)/shard_map/ppermute | solution.py:20
  68.5 11.6 %collective-permute-start.20 = (bf16[128,2048]{1,0:T(8,128)(2,1)}, bf16[128,2048]{1,0:T(8,128)(2,1)S(1)}, u32[]{:S(2)}, u32[]{:S(2)}) collective-permute-start(bf16[128,2048]{1,0:T(8,128)(2,1)} %collective-permute-done.13), channel_id=1, source_target_pairs={{8,0},{10,2},{12,4},{14,6},{16,24},{18,26},{20,28},{22,30},{9,1},{... | collective-permute-start | bytes 1572872 | tf_op jit(solution)/shard_map/ppermute | solution.py:217
  72.1 14.1 %collective-permute-start.21 = (bf16[128,2048]{1,0:T(8,128)(2,1)S(1)}, bf16[128,2048]{1,0:T(8,128)(2,1)S(1)}, u32[]{:S(2)}, u32[]{:S(2)}) collective-permute-start(bf16[128,2048]{1,0:T(8,128)(2,1)S(1)} %broadcast_select_fusion.1.refs_2_), channel_id=1, source_target_pairs={{0,2},{1,5},{2,0},{3,7},{4,6},{5,1},{6,4},{7,3},{8,10},{9,13},{10,... | collective-permute-start | bytes 1572872 | tf_op jit(solution)/shard_map/ppermute | solution.py:26
  73.2 13.3 %collective-permute-start.24 = (bf16[128,2048]{1,0:T(8,128)(2,1)S(1)}, bf16[128,2048]{1,0:T(8,128)(2,1)S(1)}, u32[]{:S(2)}, u32[]{:S(2)}) collective-permute-start(bf16[128,2048]{1,0:T(8,128)(2,1)S(1)} %broadcast_select_fusion.1.refs_2_), channel_id=1, source_target_pairs={{0,4},{1,3},{2,6},{3,1},{4,0},{5,7},{6,2},{7,5},{8,12},{9,11},{10,... | collective-permute-start | bytes 1572872 | tf_op jit(solution)/shard_map/ppermute | solution.py:26
  86.2 13.3 %collective-permute-start.22 = (bf16[128,2048]{1,0:T(8,128)(2,1)S(1)}, bf16[128,2048]{1,0:T(8,128)(2,1)S(1)}, u32[]{:S(2)}, u32[]{:S(2)}) collective-permute-start(bf16[128,2048]{1,0:T(8,128)(2,1)S(1)} %broadcast_select_fusion.refs_5_), channel_id=1, source_target_pairs={{0,2},{1,5},{2,0},{3,7},{4,6},{5,1},{6,4},{7,3},{8,10},{9,13},{10,... | collective-permute-start | bytes 1572872 | tf_op jit(solution)/shard_map/ppermute | solution.py:26
  86.5 13.3 %collective-permute-start.25 = (bf16[128,2048]{1,0:T(8,128)(2,1)S(1)}, bf16[128,2048]{1,0:T(8,128)(2,1)S(1)}, u32[]{:S(2)}, u32[]{:S(2)}) collective-permute-start(bf16[128,2048]{1,0:T(8,128)(2,1)S(1)} %broadcast_select_fusion.refs_5_), channel_id=1, source_target_pairs={{0,4},{1,3},{2,6},{3,1},{4,0},{5,7},{6,2},{7,5},{8,12},{9,11},{10,... | collective-permute-start | bytes 1572872 | tf_op jit(solution)/shard_map/ppermute | solution.py:26
  88.2 13.7 %collective-permute-start.26 = (bf16[128,2048]{1,0:T(8,128)(2,1)S(1)}, bf16[128,2048]{1,0:T(8,128)(2,1)S(1)}, u32[]{:S(2)}, u32[]{:S(2)}) collective-permute-start(bf16[128,2048]{1,0:T(8,128)(2,1)S(1)} %collective-permute-done.16.refs_1_), channel_id=1, source_target_pairs={{0,8},{2,10},{4,12},{6,14},{8,0},{10,2},{12,4},{14,6},{16,24},{18,... | collective-permute-start | bytes 1572872 | tf_op jit(solution)/shard_map/ppermute | solution.py:20
  99.5 12.4 %collective-permute-start.29 = (bf16[128,2048]{1,0:T(8,128)(2,1)S(1)}, bf16[128,2048]{1,0:T(8,128)(2,1)S(1)}, u32[]{:S(2)}, u32[]{:S(2)}) collective-permute-start(bf16[128,2048]{1,0:T(8,128)(2,1)S(1)} %collective-permute-done.24.refs_4_), channel_id=1, source_target_pairs={{0,2},{1,5},{2,0},{3,7},{4,6},{5,1},{6,4},{7,3},{8,10},{9,13},{10,... | collective-permute-start | bytes 1572872 | tf_op jit(solution)/shard_map/ppermute | solution.py:26
  99.8 12.1 %collective-permute-start.30 = (bf16[128,2048]{1,0:T(8,128)(2,1)S(1)}, bf16[128,2048]{1,0:T(8,128)(2,1)S(1)}, u32[]{:S(2)}, u32[]{:S(2)}) collective-permute-start(bf16[128,2048]{1,0:T(8,128)(2,1)S(1)} %collective-permute-done.22.refs_0_), channel_id=1, source_target_pairs={{0,4},{1,3},{2,6},{3,1},{4,0},{5,7},{6,2},{7,5},{8,12},{9,11},{10,... | collective-permute-start | bytes 1572872 | tf_op jit(solution)/shard_map/ppermute | solution.py:26
  101.9 16.1 %collective-permute-start.27 = (bf16[128,2048]{1,0:T(8,128)(2,1)S(1)}, bf16[128,2048]{1,0:T(8,128)(2,1)S(1)}, u32[]{:S(2)}, u32[]{:S(2)}) collective-permute-start(bf16[128,2048]{1,0:T(8,128)(2,1)S(1)} %collective-permute-done.18.refs_3_), channel_id=1, source_target_pairs={{0,8},{2,10},{4,12},{6,14},{8,0},{10,2},{12,4},{14,6},{16,24},{18,... | collective-permute-start | bytes 1572872 | tf_op jit(solution)/shard_map/ppermute | solution.py:20
  115.2 12.7 %collective-permute-start.32 = (bf16[128,2048]{1,0:T(8,128)(2,1)S(1)}, bf16[128,2048]{1,0:T(8,128)(2,1)S(1)}, u32[]{:S(2)}, u32[]{:S(2)}) collective-permute-start(bf16[128,2048]{1,0:T(8,128)(2,1)S(1)} %get-tuple-element.103), channel_id=1, source_target_pairs={{0,4},{1,3},{2,6},{3,1},{4,0},{5,7},{6,2},{7,5},{8,12},{9,11},{10,... | collective-permute-start | bytes 1572872 | tf_op jit(solution)/shard_map/ppermute | solution.py:26
  117.7 12.2 %collective-permute-start.33 = (bf16[128,2048]{1,0:T(8,128)(2,1)S(1)}, bf16[128,2048]{1,0:T(8,128)(2,1)S(1)}, u32[]{:S(2)}, u32[]{:S(2)}) collective-permute-start(bf16[128,2048]{1,0:T(8,128)(2,1)S(1)} %get-tuple-element.99), channel_id=1, source_target_pairs={{0,2},{1,5},{2,0},{3,7},{4,6},{5,1},{6,4},{7,3},{8,10},{9,13},{10,... | collective-permute-start | bytes 1572872 | tf_op jit(solution)/shard_map/ppermute | solution.py:26
  118.0 16.5 %collective-permute-start.28 = (bf16[128,2048]{1,0:T(8,128)(2,1)S(1)}, bf16[128,2048]{1,0:T(8,128)(2,1)S(1)}, u32[]{:S(2)}, u32[]{:S(2)}) collective-permute-start(bf16[128,2048]{1,0:T(8,128)(2,1)S(1)} %get-tuple-element.93), channel_id=1, source_target_pairs={{0,8},{2,10},{4,12},{6,14},{8,0},{10,2},{12,4},{14,6},{16,24},{18,... | collective-permute-start | bytes 1572872 | tf_op jit(solution)/shard_map/ppermute | solution.py:20
  127.9 12.1 %collective-permute-start.38 = (bf16[128,2048]{1,0:T(8,128)(2,1)S(1)}, bf16[128,2048]{1,0:T(8,128)(2,1)S(1)}, u32[]{:S(2)}, u32[]{:S(2)}) collective-permute-start(bf16[128,2048]{1,0:T(8,128)(2,1)S(1)} %get-tuple-element.112), channel_id=1, source_target_pairs={{0,4},{1,3},{2,6},{3,1},{4,0},{5,7},{6,2},{7,5},{8,12},{9,11},{10,... | collective-permute-start | bytes 1572872 | tf_op jit(solution)/shard_map/ppermute | solution.py:26
  129.9 10.1 %collective-permute-start.34 = (bf16[128,2048]{1,0:T(8,128)(2,1)S(1)}, bf16[128,2048]{1,0:T(8,128)(2,1)S(1)}, u32[]{:S(2)}, u32[]{:S(2)}) collective-permute-start(bf16[128,2048]{1,0:T(8,128)(2,1)S(1)} %add_convert_fusion.7), channel_id=1, source_target_pairs={{0,2},{1,5},{2,0},{3,7},{4,6},{5,1},{6,4},{7,3},{8,10},{9,13},{10,... | collective-permute-start | bytes 1572872 | tf_op jit(solution)/shard_map/ppermute | solution.py:26
  134.4 9.5 %collective-permute-start.31 = (bf16[128,2048]{1,0:T(8,128)(2,1)S(1)}, bf16[128,2048]{1,0:T(8,128)(2,1)S(1)}, u32[]{:S(2)}, u32[]{:S(2)}) collective-permute-start(bf16[128,2048]{1,0:T(8,128)(2,1)S(1)} %expert_rows.9), channel_id=1, source_target_pairs={{0,8},{2,10},{4,12},{6,14},{8,0},{10,2},{12,4},{14,6},{16,24},{18,... | collective-permute-start | bytes 1572872 | tf_op jit(solution)/shard_map/ppermute | solution.py:20
  140.0 13.2 %collective-permute-start.35 = (bf16[128,2048]{1,0:T(8,128)(2,1)S(1)}, bf16[128,2048]{1,0:T(8,128)(2,1)S(1)}, u32[]{:S(2)}, u32[]{:S(2)}) collective-permute-start(bf16[128,2048]{1,0:T(8,128)(2,1)S(1)} %get-tuple-element.105), channel_id=1, source_target_pairs={{0,2},{1,5},{2,0},{3,7},{4,6},{5,1},{6,4},{7,3},{8,10},{9,13},{10,... | collective-permute-start | bytes 1572872 | tf_op jit(solution)/shard_map/ppermute | solution.py:26
  142.3 13.1 %collective-permute-start.39 = (bf16[128,2048]{1,0:T(8,128)(2,1)S(1)}, bf16[128,2048]{1,0:T(8,128)(2,1)S(1)}, u32[]{:S(2)}, u32[]{:S(2)}) collective-permute-start(bf16[128,2048]{1,0:T(8,128)(2,1)S(1)} %add_convert_fusion.5), channel_id=1, source_target_pairs={{0,4},{1,3},{2,6},{3,1},{4,0},{5,7},{6,2},{7,5},{8,12},{9,11},{10,... | collective-permute-start | bytes 1572872 | tf_op jit(solution)/shard_map/ppermute | solution.py:26
  144.0 12.8 %collective-permute-start.42 = (bf16[128,2048]{1,0:T(8,128)(2,1)S(1)}, bf16[128,2048]{1,0:T(8,128)(2,1)S(1)}, u32[]{:S(2)}, u32[]{:S(2)}) collective-permute-start(bf16[128,2048]{1,0:T(8,128)(2,1)S(1)} %add_convert_fusion.4), channel_id=1, source_target_pairs={{0,8},{2,10},{4,12},{6,14},{24,16},{26,18},{28,20},{30,22},{1,9},{... | collective-permute-start | bytes 1572872 | tf_op jit(solution)/shard_map/ppermute | solution.py:217
  153.1 12.1 %collective-permute-start.36 = (bf16[128,2048]{1,0:T(8,128)(2,1)S(1)}, bf16[128,2048]{1,0:T(8,128)(2,1)S(1)}, u32[]{:S(2)}, u32[]{:S(2)}) collective-permute-start(bf16[128,2048]{1,0:T(8,128)(2,1)S(1)} %add_convert_fusion.8), channel_id=1, source_target_pairs={{0,2},{1,5},{2,0},{3,7},{4,6},{5,1},{6,4},{7,3},{8,10},{9,13},{10,... | collective-permute-start | bytes 1572872 | tf_op jit(solution)/shard_map/ppermute | solution.py:26
  155.3 13.9 %collective-permute-start.40 = (bf16[128,2048]{1,0:T(8,128)(2,1)S(1)}, bf16[128,2048]{1,0:T(8,128)(2,1)S(1)}, u32[]{:S(2)}, u32[]{:S(2)}) collective-permute-start(bf16[128,2048]{1,0:T(8,128)(2,1)S(1)} %get-tuple-element.114), channel_id=1, source_target_pairs={{0,4},{1,3},{2,6},{3,1},{4,0},{5,7},{6,2},{7,5},{8,12},{9,11},{10,... | collective-permute-start | bytes 1572872 | tf_op jit(solution)/shard_map/ppermute | solution.py:26
  157.1 13.0 %collective-permute-start.43 = (bf16[128,2048]{1,0:T(8,128)(2,1)S(1)}, bf16[128,2048]{1,0:T(8,128)(2,1)S(1)}, u32[]{:S(2)}, u32[]{:S(2)}) collective-permute-start(bf16[128,2048]{1,0:T(8,128)(2,1)S(1)} %add_convert_fusion.3), channel_id=1, source_target_pairs={{8,16},{10,18},{12,20},{14,22},{16,8},{18,10},{20,12},{22,14},{9,1... | collective-permute-start | bytes 1572872 | tf_op jit(solution)/shard_map/ppermute | solution.py:217
  159.2 15.7 %collective-permute-start.45 = (bf16[128,2048]{1,0:T(8,128)(2,1)S(1)}, bf16[128,2048]{1,0:T(8,128)(2,1)S(1)}, u32[]{:S(2)}, u32[]{:S(2)}) collective-permute-start(bf16[128,2048]{1,0:T(8,128)(2,1)S(1)} %add_convert_fusion.3), channel_id=1, source_target_pairs={{0,8},{2,10},{4,12},{6,14},{24,16},{26,18},{28,20},{30,22},{1,9},{... | collective-permute-start | bytes 1572872 | tf_op jit(solution)/shard_map/ppermute | solution.py:217
  165.2 14.7 %collective-permute-start.37 = (bf16[128,2048]{1,0:T(8,128)(2,1)S(1)}, bf16[128,2048]{1,0:T(8,128)(2,1)S(1)}, u32[]{:S(2)}, u32[]{:S(2)}) collective-permute-start(bf16[128,2048]{1,0:T(8,128)(2,1)S(1)} %add_convert_fusion.9), channel_id=1, source_target_pairs={{0,2},{1,5},{2,0},{3,7},{4,6},{5,1},{6,4},{7,3},{8,10},{9,13},{10,... | collective-permute-start | bytes 1572872 | tf_op jit(solution)/shard_map/ppermute | solution.py:26
  169.2 10.7 %collective-permute-start.41 = (bf16[128,2048]{1,0:T(8,128)(2,1)S(1)}, bf16[128,2048]{1,0:T(8,128)(2,1)S(1)}, u32[]{:S(2)}, u32[]{:S(2)}) collective-permute-start(bf16[128,2048]{1,0:T(8,128)(2,1)S(1)} %add_convert_fusion.6), channel_id=1, source_target_pairs={{0,4},{1,3},{2,6},{3,1},{4,0},{5,7},{6,2},{7,5},{8,12},{9,11},{10,... | collective-permute-start | bytes 1572872 | tf_op jit(solution)/shard_map/ppermute | solution.py:26
  170.4 11.9 %collective-permute-start.44 = (bf16[128,2048]{1,0:T(8,128)(2,1)S(1)}, bf16[128,2048]{1,0:T(8,128)(2,1)S(1)}, u32[]{:S(2)}, u32[]{:S(2)}) collective-permute-start(bf16[128,2048]{1,0:T(8,128)(2,1)S(1)} %add_convert_fusion.2), channel_id=1, source_target_pairs={{0,8},{2,10},{4,12},{6,14},{8,0},{10,2},{12,4},{14,6},{16,24},{18,... | collective-permute-start | bytes 1572872 | tf_op jit(solution)/shard_map/ppermute | solution.py:20
  175.1 12.0 %collective-permute-start.46 = (bf16[128,2048]{1,0:T(8,128)(2,1)S(1)}, bf16[128,2048]{1,0:T(8,128)(2,1)S(1)}, u32[]{:S(2)}, u32[]{:S(2)}) collective-permute-start(bf16[128,2048]{1,0:T(8,128)(2,1)S(1)} %add_convert_fusion.1), channel_id=1, source_target_pairs={{8,16},{10,18},{12,20},{14,22},{16,8},{18,10},{20,12},{22,14},{9,1... | collective-permute-start | bytes 1572872 | tf_op jit(solution)/shard_map/ppermute | solution.py:217
  (9 other events, 39.4 us)

commit v16 on v15

--- a/solution.py
+++ b/solution.py
@@ -267,7 +267,7 @@
 
     p1, py0 = add_small(p1, by_y, to_1), add_small(py0, to_y0)
     p3 = add_small(after(p3, p1), to_3)
-    by_z, by_middle = flip(p1, 4), shift(p3, MIDDLE)
+    by_z, by_middle = flip(after(p1, to_3), 4), shift(p3, MIDDLE)
     by_x, by_y = cross(after(px0, to_y0), X), cross(after(py0, by_y), Y)
     most = after(add(stream, p0, by_x, by_y, by_z))
     return add(most, by_middle)

time: 190 us -> 188 us (0.989)
    ppermute x8, waiting for transfers between devices: 9.42 us -> 5.02 us  [shift(): lax.ppermute(block, 'seq', [(4 * a + i, 4 * b + i) for a, b in pairs for...]
  transfers between devices with their start and end apart: 47 -> 47, of which waited for: 23 -> 24; matrix products, arithmetic and copies ran while one was open for 3% -> 3% of each run, Pallas kernels for 17% -> 18%
where the time goes in v16:
time: 188 us; the launch traced here: 185 us
  waiting for transfers between devices  73.5 us (39%)
  starting transfers between devices  62 us (33%)
  Pallas kernels  37.1 us (20%)
  local copies, waits for them, and re-layouts  6.87 us (4%)
  other arithmetic  5.52 us (3%)
    ppermute x20, waiting for transfers between devices, cross(): return lax.ppermute(block, ('seq', 'exp'), pairs)  46 us
    ppermute x20, starting transfers between devices, cross(): return lax.ppermute(block, ('seq', 'exp'), pairs)  26.4 us
    pallas_call x5, Pallas kernels, expert(): pl.pallas_call(functools.partial(expert_kernel, places, len(gates)), out_...  25.6 us
    ppermute x12, waiting for transfers between devices, flip(): return lax.ppermute(block, 'seq', [(i, i ^ mask) for i in range(count)])  20.9 us
    ppermute x8, starting transfers between devices, shift(): lax.ppermute(block, 'seq', [(4 * a + i, 4 * b + i) for a, b in pairs for...  20.2 us
    ppermute x12, starting transfers between devices, flip(): return lax.ppermute(block, 'seq', [(i, i ^ mask) for i in range(count)])  8.27 us
    ppermute x2, starting transfers between devices, halo(): return (beside, part, lax.ppermute(beside, 'seq', ahead + back))  6.6 us
    unnamed x20, local copies, waits for them, and re-layouts  5.5 us
  transfers between devices with their start and end apart: 47, of which 24 were waited for; matrix products, arithmetic and copies ran while one was open for 3% of the time, Pallas kernels for 18%

profile of v16, /device:TPU:10, one launch (start us, length us, event | category | flops | bytes accessed | tf_op | source)
XLA Modules:
  0.0 185.3 jit_solution(15887357836863541347)
XLA Ops:
  0.5 1.5 collective-permute-start.2
  3.3 3.2 %collective-permute-done.7.refs_5_.refs_7_.refs_4_.refs_3_.refs_2_ = f32[16,128]{1,0:T(8,128)S(1)} collective-permute-done((f32[16,128]{1,0:T(8,128)S(1)}, f32[16,128]{1,0:T(8,128)S(1)}, u32[]{:S(2)}, u32[]{:S(2)}) %collective-permute-start.7) | collective-permute-done | bytes 8224 | tf_op jit(solution)/shard_map/ppermute | solution.py:20
  6.5 2.6 %collective-permute-start.8 = (f32[16,256]{1,0:T(8,128)S(1)}, f32[16,256]{1,0:T(8,128)S(1)}, u32[]{:S(2)}, u32[]{:S(2)}) collective-permute-start(f32[16,256]{1,0:T(8,128)S(1)} %pad_maximum_fusion.2), channel_id=1, source_target_pairs={{0,16},{2,18},{4,20},{6,22},{8,24},{10,26},{12,28},{14,30},{16,0},... | collective-permute-start | bytes 49160 | tf_op jit(solution)/shard_map/ppermute | solution.py:20
  9.3 3.3 %collective-permute-start.1 = (bf16[256,512]{1,0:T(8,128)(2,1)S(1)}, bf16[256,512]{1,0:T(8,128)(2,1)S(1)}, u32[]{:S(2)}, u32[]{:S(2)}) collective-permute-start(bf16[256,512]{1,0:T(8,128)(2,1)S(1)} %collective-permute-done.refs_0_), channel_id=1, source_target_pairs={{0,4},{4,8},{8,12},{12,16},{16,20},{20,24},{24,28},{6,2},{10,6},{1... | collective-permute-start | bytes 786440 | tf_op jit(solution)/shard_map/ppermute | solution.py:331
  12.6 1.9 %collective-permute-done.2.refs_3_ = bf16[256,512]{1,0:T(8,128)(2,1)S(1)} collective-permute-done((bf16[256,512]{1,0:T(8,128)(2,1)}, bf16[256,512]{1,0:T(8,128)(2,1)S(1)}, u32[]{:S(2)}, u32[]{:S(2)}) %collective-permute-start.2) | collective-permute-done | bytes 262176 | tf_op jit(solution)/shard_map/ppermute | solution.py:20
  14.6 3.3 %collective-permute-start.3 = (bf16[256,512]{1,0:T(8,128)(2,1)S(1)}, bf16[256,512]{1,0:T(8,128)(2,1)S(1)}, u32[]{:S(2)}, u32[]{:S(2)}) collective-permute-start(bf16[256,512]{1,0:T(8,128)(2,1)S(1)} %collective-permute-done.2.refs_3_), channel_id=1, source_target_pairs={{0,4},{4,8},{8,12},{12,16},{16,20},{20,24},{24,28},{6,2},{10,6},{1... | collective-permute-start | bytes 786440 | tf_op jit(solution)/shard_map/ppermute | solution.py:331
  20.5 4.5 %collective-permute-done.9.refs_7_.refs_9_.refs_6_.refs_5_.refs_4_ = f32[16,512]{1,0:T(8,128)S(1)} collective-permute-done((f32[16,512]{1,0:T(8,128)S(1)}, f32[16,512]{1,0:T(8,128)S(1)}, u32[]{:S(2)}, u32[]{:S(2)}) %collective-permute-start.9) | collective-permute-done | bytes 32800 | tf_op jit(solution)/shard_map/ppermute | solution.py:20
  26.4 4.6 %window_attention.1 = (bf16[128,512]{1,0:T(8,128)(2,1)}, bf16[128,512]{1,0:T(8,128)(2,1)}) custom-call(s32[2]{0:T(128)} %pad_add_fusion.where_ref, bf16[256,512]{1,0:T(8,128)(2,1)} %q_ref.1, s32[1,768]{1,0:T(1,128)} %broadcast_in_dim.21.ids_ref, bf16[256,512]{1,0:T(8,128)(2,1)} %copy-done.5, bf16[256,512]{1,0:T(8,128)(2,1)} %refs_1_.1, ...), custom_call_target="tpu_custom_call" | custom-call | tf_op jit(solution)/shard_map/window_attention/pallas_call | solution.py:97
  33.2 4.3 %project_and_norm.1 = (f32[128,2048]{1,0:T(8,128)}, bf16[128,2048]{1,0:T(8,128)(2,1)}) custom-call(bf16[128,512]{1,0:T(8,128)(2,1)} %get-tuple-element.64.mine_ref, bf16[128,512]{1,0:T(8,128)(2,1)} %copy-done.9, bf16[512,2048]{1,0:T(8,128)(2,1)} %own_w.1, bf16[512,2048]{1,0:T(8,128)(2,1)} %collective-permute-done.4.refs_6_.other_w, ...), custom_call_target="tpu_custom_call" | custom-call | tf_op jit(solution)/shard_map/project_and_norm/pallas_call | solution.py:120
  37.9 4.6 %collective-permute-start.14 = (bf16[128,2048]{1,0:T(8,128)(2,1)}, bf16[128,2048]{1,0:T(8,128)(2,1)S(1)}, u32[]{:S(2)}, u32[]{:S(2)}) collective-permute-start(bf16[128,2048]{1,0:T(8,128)(2,1)} %get-tuple-element.70.refs_0_), channel_id=1, source_target_pairs={{8,16},{10,18},{12,20},{14,22},{16,8},{18,10},{20,12},{22,14},{9,1... | collective-permute-start | bytes 1572872 | tf_op jit(solution)/shard_map/ppermute | solution.py:217
  44.6 7.0 %collective-permute-done.12.refs_0_ = bf16[128,2048]{1,0:T(8,128)(2,1)S(1)} collective-permute-done((bf16[128,2048]{1,0:T(8,128)(2,1)}, bf16[128,2048]{1,0:T(8,128)(2,1)S(1)}, u32[]{:S(2)}, u32[]{:S(2)}) %collective-permute-start.12) | collective-permute-done | bytes 524320 | tf_op jit(solution)/shard_map/ppermute | solution.py:20
  51.6 3.5 %collective-permute-start.13 = (bf16[128,2048]{1,0:T(8,128)(2,1)S(1)}, bf16[128,2048]{1,0:T(8,128)(2,1)}, u32[]{:S(2)}, u32[]{:S(2)}) collective-permute-start(bf16[128,2048]{1,0:T(8,128)(2,1)S(1)} %collective-permute-done.12.refs_0_), channel_id=1, source_target_pairs={{8,16},{10,18},{12,20},{14,22},{16,8},{18,10},{20,12},{22,14},{9,1... | collective-permute-start | bytes 1572872 | tf_op jit(solution)/shard_map/ppermute | solution.py:217
  55.1 2.1 %collective-permute-start.15 = (bf16[128,2048]{1,0:T(8,128)(2,1)S(1)}, bf16[128,2048]{1,0:T(8,128)(2,1)}, u32[]{:S(2)}, u32[]{:S(2)}) collective-permute-start(bf16[128,2048]{1,0:T(8,128)(2,1)S(1)} %collective-permute-done.14), channel_id=1, source_target_pairs={{8,0},{10,2},{12,4},{14,6},{16,24},{18,26},{20,28},{22,30},{9,1},{... | collective-permute-start | bytes 1572872 | tf_op jit(solution)/shard_map/ppermute | solution.py:217
  57.4 1.3 collective-permute-start.18
  59.7 2.0 %collective-permute-start.19 = (f32[16,1024]{1,0:T(8,128)S(1)}, f32[16,1024]{1,0:T(8,128)S(1)}, u32[]{:S(2)}, u32[]{:S(2)}) collective-permute-start(f32[16,1024]{1,0:T(8,128)S(1)} %pad_maximum_fusion), channel_id=1, source_target_pairs={{0,2},{2,0},{4,6},{6,4},{8,10},{10,8},{12,14},{14,12},{16,18},{18,... | collective-permute-start | bytes 196616 | tf_op jit(solution)/shard_map/ppermute | solution.py:20
  61.7 1.4 copy-done
  63.1 1.4 copy-done.1
  64.4 1.4 copy-done.2
  65.8 2.6 %assemble_weights.1 = (bf16[1408,2048]{1,0:T(8,128)(2,1)S(1)}, bf16[704,2048]{1,0:T(8,128)(2,1)S(1)}) custom-call(bf16[352,2048]{1,0:T(8,128)(2,1)S(1)} %bitcast.14, bf16[352,2048]{1,0:T(8,128)(2,1)} %collective-permute-done.5.refs_7_.refs_1_, bf16[352,2048]{1,0:T(8,128)(2,1)S(1)} %bitcast.16, bf16[352,2048]{1,0:T(8,128)(2,1)} %collective-permute-done.10.refs_0_.refs_3_, ...), custom_call_target="tpu_custom_call" | custom-call | tf_op jit(solution)/shard_map/assemble_weights/pallas_call | solution.py:148
  68.5 1.6 collective-permute-start.20
  74.1 5.6 %expert_rows.5 = (bf16[128,2048]{1,0:T(8,128)(2,1)S(1)}, bf16[128,2048]{1,0:T(8,128)(2,1)S(1)}, bf16[128,2048]{1,0:T(8,128)(2,1)S(1)}, bf16[128,2048]{1,0:T(8,128)(2,1)S(1)}) custom-call(s32[2]{0:T(128)S(1)} %pad_add_fusion.1.where_ref, bf16[128,2048]{1,0:T(8,128)(2,1)S(1)} %copy-done.3, bf16[128,2048]{1,0:T(8,128)(2,1)S(1)} %collective-permute-done.16.refs_1_, ...), custom_call_target="tpu_custom_call" | custom-call | tf_op jit(solution)/shard_map/expert_rows/pallas_call | solution.py:195
  80.1 6.1 %collective-permute-done.21.refs_3_ = bf16[128,2048]{1,0:T(8,128)(2,1)S(1)} collective-permute-done((bf16[128,2048]{1,0:T(8,128)(2,1)S(1)}, bf16[128,2048]{1,0:T(8,128)(2,1)S(1)}, u32[]{:S(2)}, u32[]{:S(2)}) %collective-permute-start.21) | collective-permute-done | bytes 524320 | tf_op jit(solution)/shard_map/ppermute | solution.py:26
  86.5 1.7 collective-permute-start.25
  88.2 8.1 %expert_rows.6 = (bf16[128,2048]{1,0:T(8,128)(2,1)S(1)}, bf16[128,2048]{1,0:T(8,128)(2,1)S(1)}, bf16[128,2048]{1,0:T(8,128)(2,1)S(1)}, bf16[128,2048]{1,0:T(8,12...) custom-call(s32[2]{0:T(128)S(1)} %pad_add_fusion.1.where_ref, ...), custom_call_target="tpu_custom_call" | custom-call | tf_op jit(solution)/shard_map/expert_rows/pallas_call | solution.py:195
  96.4 3.2 %collective-permute-done.22.refs_0_ = bf16[128,2048]{1,0:T(8,128)(2,1)S(1)} collective-permute-done((bf16[128,2048]{1,0:T(8,128)(2,1)S(1)}, bf16[128,2048]{1,0:T(8,128)(2,1)S(1)}, u32[]{:S(2)}, u32[]{:S(2)}) %collective-permute-start.22) | collective-permute-done | bytes 524320 | tf_op jit(solution)/shard_map/ppermute | solution.py:26
  99.8 2.1 %collective-permute-start.30 = (bf16[128,2048]{1,0:T(8,128)(2,1)S(1)}, bf16[128,2048]{1,0:T(8,128)(2,1)S(1)}, u32[]{:S(2)}, u32[]{:S(2)}) collective-permute-start(bf16[128,2048]{1,0:T(8,128)(2,1)S(1)} %collective-permute-done.22.refs_0_), channel_id=1, source_target_pairs={{0,4},{1,3},{2,6},{3,1},{4,0},{5,7},{6,2},{7,5},{8,12},{9,11},{10,... | collective-permute-start | bytes 1572872 | tf_op jit(solution)/shard_map/ppermute | solution.py:26
  101.9 5.7 %expert_rows.7 = (bf16[128,2048]{1,0:T(8,128)(2,1)S(1)}, bf16[128,2048]{1,0:T(8,128)(2,1)S(1)}, bf16[128,2048]{1,0:T(8,128)(2,1)S(1)}) custom-call(s32[2]{0:T(128)S(1)} %pad_add_fusion.1.where_ref, bf16[128,2048]{1,0:T(8,128)(2,1)S(1)} %collective-permute-done.22.refs_0_, bf16[128,2048]{1,0:T(8,128)(2,1)S(1)} %collective-permute-done.25.refs_1_, ...), custom_call_target="tpu_custom_call" | custom-call | tf_op jit(solution)/shard_map/expert_rows/pallas_call | solution.py:195
  107.6 4.4 %collective-permute-done.29.refs_0_ = bf16[128,2048]{1,0:T(8,128)(2,1)S(1)} collective-permute-done((bf16[128,2048]{1,0:T(8,128)(2,1)S(1)}, bf16[128,2048]{1,0:T(8,128)(2,1)S(1)}, u32[]{:S(2)}, u32[]{:S(2)}) %collective-permute-start.29) | collective-permute-done | bytes 524320 | tf_op jit(solution)/shard_map/ppermute | solution.py:26
  112.0 3.2 %expert_rows.8 = (bf16[128,2048]{1,0:T(8,128)(2,1)S(1)}, bf16[128,2048]{1,0:T(8,128)(2,1)S(1)}) custom-call(s32[2]{0:T(128)S(1)} %pad_add_fusion.1.where_ref, bf16[128,2048]{1,0:T(8,128)(2,1)S(1)} %collective-permute-done.29.refs_0_, bf16[128,2048]{1,0:T(8,128)(2,1)S(1)} %collective-permute-done.30.refs_1_, ...), custom_call_target="tpu_custom_call" | custom-call | tf_op jit(solution)/shard_map/expert_rows/pallas_call | solution.py:195
  115.2 2.5 %collective-permute-start.32 = (bf16[128,2048]{1,0:T(8,128)(2,1)S(1)}, bf16[128,2048]{1,0:T(8,128)(2,1)S(1)}, u32[]{:S(2)}, u32[]{:S(2)}) collective-permute-start(bf16[128,2048]{1,0:T(8,128)(2,1)S(1)} %get-tuple-element.104), channel_id=1, source_target_pairs={{0,4},{1,3},{2,6},{3,1},{4,0},{5,7},{6,2},{7,5},{8,12},{9,11},{10,... | collective-permute-start | bytes 1572872 | tf_op jit(solution)/shard_map/ppermute | solution.py:26
  118.0 9.9 %collective-permute-done.32 = bf16[128,2048]{1,0:T(8,128)(2,1)S(1)} collective-permute-done((bf16[128,2048]{1,0:T(8,128)(2,1)S(1)}, bf16[128,2048]{1,0:T(8,128)(2,1)S(1)}, u32[]{:S(2)}, u32[]{:S(2)}) %collective-permute-start.32) | collective-permute-done | bytes 524320 | tf_op jit(solution)/shard_map/ppermute | solution.py:26
  127.9 1.9 %collective-permute-start.38 = (bf16[128,2048]{1,0:T(8,128)(2,1)S(1)}, bf16[128,2048]{1,0:T(8,128)(2,1)S(1)}, u32[]{:S(2)}, u32[]{:S(2)}) collective-permute-start(bf16[128,2048]{1,0:T(8,128)(2,1)S(1)} %get-tuple-element.113), channel_id=1, source_target_pairs={{0,4},{1,3},{2,6},{3,1},{4,0},{5,7},{6,2},{7,5},{8,12},{9,11},{10,... | collective-permute-start | bytes 1572872 | tf_op jit(solution)/shard_map/ppermute | solution.py:26
  129.9 1.6 collective-permute-start.34
  131.5 2.9 %expert_rows.9 = bf16[128,2048]{1,0:T(8,128)(2,1)S(1)} custom-call(s32[2]{0:T(128)S(1)} %pad_add_fusion.1.where_ref, bf16[128,2048]{1,0:T(8,128)(2,1)S(1)} %collective-permute-done.27.refs_0_, f32[16,128]{1,0:T(8,128)S(1)} %select_reduce_fusion.refs_4_.refs_6_.refs_3_.refs_2_.refs_1_, ...), custom_call_target="tpu_custom_call" | custom-call | tf_op jit(solution)/shard_map/expert_rows/pallas_call | solution.py:195
  134.7 5.3 %collective-permute-done.38 = bf16[128,2048]{1,0:T(8,128)(2,1)S(1)} collective-permute-done((bf16[128,2048]{1,0:T(8,128)(2,1)S(1)}, bf16[128,2048]{1,0:T(8,128)(2,1)S(1)}, u32[]{:S(2)}, u32[]{:S(2)}) %collective-permute-start.38) | collective-permute-done | bytes 524320 | tf_op jit(solution)/shard_map/ppermute | solution.py:26
  140.0 2.3 %collective-permute-start.35 = (bf16[128,2048]{1,0:T(8,128)(2,1)S(1)}, bf16[128,2048]{1,0:T(8,128)(2,1)S(1)}, u32[]{:S(2)}, u32[]{:S(2)}) collective-permute-start(bf16[128,2048]{1,0:T(8,128)(2,1)S(1)} %get-tuple-element.106), channel_id=1, source_target_pairs={{0,2},{1,5},{2,0},{3,7},{4,6},{5,1},{6,4},{7,3},{8,10},{9,13},{10,... | collective-permute-start | bytes 1572872 | tf_op jit(solution)/shard_map/ppermute | solution.py:26
  142.3 1.4 collective-permute-start.39
  144.0 1.3 collective-permute-start.42
  145.4 7.7 %collective-permute-done.35 = bf16[128,2048]{1,0:T(8,128)(2,1)S(1)} collective-permute-done((bf16[128,2048]{1,0:T(8,128)(2,1)S(1)}, bf16[128,2048]{1,0:T(8,128)(2,1)S(1)}, u32[]{:S(2)}, u32[]{:S(2)}) %collective-permute-start.35) | collective-permute-done | bytes 524320 | tf_op jit(solution)/shard_map/ppermute | solution.py:26
  153.1 1.7 collective-permute-start.36
  157.1 1.9 %collective-permute-start.43 = (bf16[128,2048]{1,0:T(8,128)(2,1)S(1)}, bf16[128,2048]{1,0:T(8,128)(2,1)S(1)}, u32[]{:S(2)}, u32[]{:S(2)}) collective-permute-start(bf16[128,2048]{1,0:T(8,128)(2,1)S(1)} %add_convert_fusion.3), channel_id=1, source_target_pairs={{8,16},{10,18},{12,20},{14,22},{16,8},{18,10},{20,12},{22,14},{9,1... | collective-permute-start | bytes 1572872 | tf_op jit(solution)/shard_map/ppermute | solution.py:217
  160.5 4.7 %collective-permute-done.36 = bf16[128,2048]{1,0:T(8,128)(2,1)S(1)} collective-permute-done((bf16[128,2048]{1,0:T(8,128)(2,1)S(1)}, bf16[128,2048]{1,0:T(8,128)(2,1)S(1)}, u32[]{:S(2)}, u32[]{:S(2)}) %collective-permute-start.36) | collective-permute-done | bytes 524320 | tf_op jit(solution)/shard_map/ppermute | solution.py:26
  165.2 1.7 collective-permute-start.37
  167.1 2.1 %collective-permute-done.40 = bf16[128,2048]{1,0:T(8,128)(2,1)S(1)} collective-permute-done((bf16[128,2048]{1,0:T(8,128)(2,1)S(1)}, bf16[128,2048]{1,0:T(8,128)(2,1)S(1)}, u32[]{:S(2)}, u32[]{:S(2)}) %collective-permute-start.40) | collective-permute-done | bytes 524320 | tf_op jit(solution)/shard_map/ppermute | solution.py:26
  170.4 2.8 %collective-permute-done.44 = bf16[128,2048]{1,0:T(8,128)(2,1)S(1)} collective-permute-done((bf16[128,2048]{1,0:T(8,128)(2,1)S(1)}, bf16[128,2048]{1,0:T(8,128)(2,1)S(1)}, u32[]{:S(2)}, u32[]{:S(2)}) %collective-permute-start.44) | collective-permute-done | bytes 524320 | tf_op jit(solution)/shard_map/ppermute | solution.py:217
  173.3 3.9 %collective-permute-start.46 = (bf16[128,2048]{1,0:T(8,128)(2,1)S(1)}, bf16[128,2048]{1,0:T(8,128)(2,1)S(1)}, u32[]{:S(2)}, u32[]{:S(2)}) collective-permute-start(bf16[128,2048]{1,0:T(8,128)(2,1)S(1)} %add_convert_fusion.1), channel_id=1, source_target_pairs={{8,16},{10,18},{12,20},{14,22},{16,8},{18,10},{20,12},{22,14},{9,1... | collective-permute-start | bytes 1572872 | tf_op jit(solution)/shard_map/ppermute | solution.py:217
  178.4 3.9 %collective-permute-done.45 = bf16[128,2048]{1,0:T(8,128)(2,1)S(1)} collective-permute-done((bf16[128,2048]{1,0:T(8,128)(2,1)S(1)}, bf16[128,2048]{1,0:T(8,128)(2,1)S(1)}, u32[]{:S(2)}, u32[]{:S(2)}) %collective-permute-start.45) | collective-permute-done | bytes 524320 | tf_op jit(solution)/shard_map/ppermute | solution.py:20
  182.7 1.6 collective-permute-done.46
  (95 shorter events, 25.4 us)
Async XLA Ops:
  0.0 26.3 %collective-permute-start.4 = (bf16[512,2048]{1,0:T(8,128)(2,1)}, bf16[512,2048]{1,0:T(8,128)(2,1)}, u32[]{:S(2)}, u32[]{:S(2)}) collective-permute-start(bf16[512,2048]{1,0:T(8,128)(2,1)} %own_w.1), channel_id=1, source_target_pairs={{0,1},{1,0},{2,3},{3,2},{4,5},{5,4},{6,7},{7,6},{8,9},{9,8},{10,11... | collective-permute-start | bytes 6291464 | tf_op jit(solution)/shard_map/ppermute | solution.py:340
  0.0 9.3 %collective-permute-start = (bf16[256,512]{1,0:T(8,128)(2,1)}, bf16[256,512]{1,0:T(8,128)(2,1)S(1)}, u32[]{:S(2)}, u32[]{:S(2)}) collective-permute-start(bf16[256,512]{1,0:T(8,128)(2,1)} %refs_1_.1), channel_id=1, source_target_pairs={{0,2},{2,0},{4,6},{6,4},{8,10},{10,8},{12,14},{14,12},{16,18},{18,... | collective-permute-start | bytes 786440 | tf_op jit(solution)/shard_map/ppermute | solution.py:20
  0.5 14.0 %collective-permute-start.2 = (bf16[256,512]{1,0:T(8,128)(2,1)}, bf16[256,512]{1,0:T(8,128)(2,1)S(1)}, u32[]{:S(2)}, u32[]{:S(2)}) collective-permute-start(bf16[256,512]{1,0:T(8,128)(2,1)} %refs_4_.1), channel_id=1, source_target_pairs={{0,2},{2,0},{4,6},{6,4},{8,10},{10,8},{12,14},{14,12},{16,18},{18,... | collective-permute-start | bytes 786440 | tf_op jit(solution)/shard_map/ppermute | solution.py:20
  2.7 3.7 %collective-permute-start.7 = (f32[16,128]{1,0:T(8,128)S(1)}, f32[16,128]{1,0:T(8,128)S(1)}, u32[]{:S(2)}, u32[]{:S(2)}) collective-permute-start(f32[16,128]{1,0:T(8,128)S(1)} %select_reduce_fusion.refs_4_.refs_6_.refs_3_.refs_2_.refs_1_), channel_id=1, source_target_pairs={{0,8},{2,10},{4,12},{6,14},{8,0},{10,2},{12,4},{14,6},{16,24},{18,... | collective-permute-start | bytes 24584 | tf_op jit(solution)/shard_map/ppermute | solution.py:20
  3.3 23.1 %collective-permute-start.5 = (bf16[352,2048]{1,0:T(8,128)(2,1)}, bf16[352,2048]{1,0:T(8,128)(2,1)}, u32[]{:S(2)}, u32[]{:S(2)}) collective-permute-start(bf16[352,2048]{1,0:T(8,128)(2,1)} %bitcast.13), channel_id=1, source_target_pairs={{0,1},{1,0},{2,3},{3,2},{4,5},{5,4},{6,7},{7,6},{8,9},{9,8},{10,11... | collective-permute-start | bytes 4325384 | tf_op jit(solution)/shard_map/ppermute | solution.py:342
  6.5 12.2 %collective-permute-start.8 = (f32[16,256]{1,0:T(8,128)S(1)}, f32[16,256]{1,0:T(8,128)S(1)}, u32[]{:S(2)}, u32[]{:S(2)}) collective-permute-start(f32[16,256]{1,0:T(8,128)S(1)} %pad_maximum_fusion.2), channel_id=1, source_target_pairs={{0,16},{2,18},{4,20},{6,22},{8,24},{10,26},{12,28},{14,30},{16,0},... | collective-permute-start | bytes 49160 | tf_op jit(solution)/shard_map/ppermute | solution.py:20
  9.3 17.0 %copy-start.5 = (bf16[256,512]{1,0:T(8,128)(2,1)}, bf16[256,512]{1,0:T(8,128)(2,1)S(1)}, u32[]{:S(2)}) copy-start(bf16[256,512]{1,0:T(8,128)(2,1)S(1)} %collective-permute-done.refs_0_) | copy-start | bytes 786436
  9.3 15.8 %collective-permute-start.1 = (bf16[256,512]{1,0:T(8,128)(2,1)S(1)}, bf16[256,512]{1,0:T(8,128)(2,1)S(1)}, u32[]{:S(2)}, u32[]{:S(2)}) collective-permute-start(bf16[256,512]{1,0:T(8,128)(2,1)S(1)} %collective-permute-done.refs_0_), channel_id=1, source_target_pairs={{0,4},{4,8},{8,12},{12,16},{16,20},{20,24},{24,28},{6,2},{10,6},{1... | collective-permute-start | bytes 786440 | tf_op jit(solution)/shard_map/ppermute | solution.py:331
  14.6 10.5 %collective-permute-start.3 = (bf16[256,512]{1,0:T(8,128)(2,1)S(1)}, bf16[256,512]{1,0:T(8,128)(2,1)S(1)}, u32[]{:S(2)}, u32[]{:S(2)}) collective-permute-start(bf16[256,512]{1,0:T(8,128)(2,1)S(1)} %collective-permute-done.2.refs_3_), channel_id=1, source_target_pairs={{0,4},{4,8},{8,12},{12,16},{16,20},{20,24},{24,28},{6,2},{10,6},{1... | collective-permute-start | bytes 786440 | tf_op jit(solution)/shard_map/ppermute | solution.py:331
  18.7 6.4 %collective-permute-start.9 = (f32[16,512]{1,0:T(8,128)S(1)}, f32[16,512]{1,0:T(8,128)S(1)}, u32[]{:S(2)}, u32[]{:S(2)}) collective-permute-start(f32[16,512]{1,0:T(8,128)S(1)} %pad_maximum_fusion.1), channel_id=1, source_target_pairs={{0,4},{2,6},{4,0},{6,2},{8,12},{10,14},{12,8},{14,10},{16,20},{18,... | collective-permute-start | bytes 98312 | tf_op jit(solution)/shard_map/ppermute | solution.py:20
  25.8 5.1 %collective-permute-start.10 = (bf16[352,2048]{1,0:T(8,128)(2,1)}, bf16[352,2048]{1,0:T(8,128)(2,1)}, u32[]{:S(2)}, u32[]{:S(2)}) collective-permute-start(bf16[352,2048]{1,0:T(8,128)(2,1)} %bitcast.15), channel_id=1, source_target_pairs={{0,1},{1,0},{2,3},{3,2},{4,5},{5,4},{6,7},{7,6},{8,9},{9,8},{10,11... | collective-permute-start | bytes 4325384 | tf_op jit(solution)/shard_map/ppermute | solution.py:345
  25.8 5.6 %collective-permute-start.11 = (bf16[352,2048]{1,0:T(8,128)(2,1)}, bf16[352,2048]{1,0:T(8,128)(2,1)}, u32[]{:S(2)}, u32[]{:S(2)}) collective-permute-start(bf16[352,2048]{1,0:T(8,128)(2,1)} %bitcast.17), channel_id=1, source_target_pairs={{0,1},{1,0},{2,3},{3,2},{4,5},{5,4},{6,7},{7,6},{8,9},{9,8},{10,11... | collective-permute-start | bytes 4325384 | tf_op jit(solution)/shard_map/ppermute | solution.py:346
  30.9 1.6 collective-permute-start.6
  37.5 14.2 %collective-permute-start.12 = (bf16[128,2048]{1,0:T(8,128)(2,1)}, bf16[128,2048]{1,0:T(8,128)(2,1)S(1)}, u32[]{:S(2)}, u32[]{:S(2)}) collective-permute-start(bf16[128,2048]{1,0:T(8,128)(2,1)} %get-tuple-element.70.refs_0_), channel_id=1, source_target_pairs={{0,8},{2,10},{4,12},{6,14},{8,0},{10,2},{12,4},{14,6},{16,24},{18,... | collective-permute-start | bytes 1572872 | tf_op jit(solution)/shard_map/ppermute | solution.py:20
  37.9 17.2 %collective-permute-start.14 = (bf16[128,2048]{1,0:T(8,128)(2,1)}, bf16[128,2048]{1,0:T(8,128)(2,1)S(1)}, u32[]{:S(2)}, u32[]{:S(2)}) collective-permute-start(bf16[128,2048]{1,0:T(8,128)(2,1)} %get-tuple-element.70.refs_0_), channel_id=1, source_target_pairs={{8,16},{10,18},{12,20},{14,22},{16,8},{18,10},{20,12},{22,14},{9,1... | collective-permute-start | bytes 1572872 | tf_op jit(solution)/shard_map/ppermute | solution.py:217
  42.5 14.8 %collective-permute-start.17 = (bf16[128,2048]{1,0:T(8,128)(2,1)}, bf16[128,2048]{1,0:T(8,128)(2,1)S(1)}, u32[]{:S(2)}, u32[]{:S(2)}) collective-permute-start(bf16[128,2048]{1,0:T(8,128)(2,1)} %get-tuple-element.70.refs_0_), channel_id=1, source_target_pairs={{0,4},{1,3},{2,6},{3,1},{4,0},{5,7},{6,2},{7,5},{8,12},{9,11},{10,... | collective-permute-start | bytes 1572872 | tf_op jit(solution)/shard_map/ppermute | solution.py:26
  43.4 13.9 %collective-permute-start.16 = (bf16[128,2048]{1,0:T(8,128)(2,1)}, bf16[128,2048]{1,0:T(8,128)(2,1)S(1)}, u32[]{:S(2)}, u32[]{:S(2)}) collective-permute-start(bf16[128,2048]{1,0:T(8,128)(2,1)} %get-tuple-element.70.refs_0_), channel_id=1, source_target_pairs={{0,2},{1,5},{2,0},{3,7},{4,6},{5,1},{6,4},{7,3},{8,10},{9,13},{10,... | collective-permute-start | bytes 1572872 | tf_op jit(solution)/shard_map/ppermute | solution.py:26
  51.6 16.8 %collective-permute-start.13 = (bf16[128,2048]{1,0:T(8,128)(2,1)S(1)}, bf16[128,2048]{1,0:T(8,128)(2,1)}, u32[]{:S(2)}, u32[]{:S(2)}) collective-permute-start(bf16[128,2048]{1,0:T(8,128)(2,1)S(1)} %collective-permute-done.12.refs_0_), channel_id=1, source_target_pairs={{8,16},{10,18},{12,20},{14,22},{16,8},{18,10},{20,12},{22,14},{9,1... | collective-permute-start | bytes 1572872 | tf_op jit(solution)/shard_map/ppermute | solution.py:217
  55.1 15.0 %collective-permute-start.15 = (bf16[128,2048]{1,0:T(8,128)(2,1)S(1)}, bf16[128,2048]{1,0:T(8,128)(2,1)}, u32[]{:S(2)}, u32[]{:S(2)}) collective-permute-start(bf16[128,2048]{1,0:T(8,128)(2,1)S(1)} %collective-permute-done.14), channel_id=1, source_target_pairs={{8,0},{10,2},{12,4},{14,6},{16,24},{18,26},{20,28},{22,30},{9,1},{... | collective-permute-start | bytes 1572872 | tf_op jit(solution)/shard_map/ppermute | solution.py:217
  57.4 14.7 %collective-permute-start.18 = (bf16[128,2048]{1,0:T(8,128)(2,1)S(1)}, bf16[128,2048]{1,0:T(8,128)(2,1)S(1)}, u32[]{:S(2)}, u32[]{:S(2)}) collective-permute-start(bf16[128,2048]{1,0:T(8,128)(2,1)S(1)} %collective-permute-done.17.refs_2_), channel_id=1, source_target_pairs={{0,2},{1,5},{2,0},{3,7},{4,6},{5,1},{6,4},{7,3},{8,10},{9,13},{10,... | collective-permute-start | bytes 1572872 | tf_op jit(solution)/shard_map/ppermute | solution.py:26
  58.7 12.6 %collective-permute-start.23 = (bf16[128,2048]{1,0:T(8,128)(2,1)S(1)}, bf16[128,2048]{1,0:T(8,128)(2,1)S(1)}, u32[]{:S(2)}, u32[]{:S(2)}) collective-permute-start(bf16[128,2048]{1,0:T(8,128)(2,1)S(1)} %collective-permute-done.12.refs_0_), channel_id=1, source_target_pairs={{0,4},{1,3},{2,6},{3,1},{4,0},{5,7},{6,2},{7,5},{8,12},{9,11},{10,... | collective-permute-start | bytes 1572872 | tf_op jit(solution)/shard_map/ppermute | solution.py:26
  59.7 14.3 %collective-permute-start.19 = (f32[16,1024]{1,0:T(8,128)S(1)}, f32[16,1024]{1,0:T(8,128)S(1)}, u32[]{:S(2)}, u32[]{:S(2)}) collective-permute-start(f32[16,1024]{1,0:T(8,128)S(1)} %pad_maximum_fusion), channel_id=1, source_target_pairs={{0,2},{2,0},{4,6},{6,4},{8,10},{10,8},{12,14},{14,12},{16,18},{18,... | collective-permute-start | bytes 196616 | tf_op jit(solution)/shard_map/ppermute | solution.py:20
  68.5 11.6 %collective-permute-start.20 = (bf16[128,2048]{1,0:T(8,128)(2,1)}, bf16[128,2048]{1,0:T(8,128)(2,1)S(1)}, u32[]{:S(2)}, u32[]{:S(2)}) collective-permute-start(bf16[128,2048]{1,0:T(8,128)(2,1)} %collective-permute-done.13), channel_id=1, source_target_pairs={{8,0},{10,2},{12,4},{14,6},{16,24},{18,26},{20,28},{22,30},{9,1},{... | collective-permute-start | bytes 1572872 | tf_op jit(solution)/shard_map/ppermute | solution.py:217
  72.1 14.1 %collective-permute-start.21 = (bf16[128,2048]{1,0:T(8,128)(2,1)S(1)}, bf16[128,2048]{1,0:T(8,128)(2,1)S(1)}, u32[]{:S(2)}, u32[]{:S(2)}) collective-permute-start(bf16[128,2048]{1,0:T(8,128)(2,1)S(1)} %broadcast_select_fusion.1.refs_2_), channel_id=1, source_target_pairs={{0,2},{1,5},{2,0},{3,7},{4,6},{5,1},{6,4},{7,3},{8,10},{9,13},{10,... | collective-permute-start | bytes 1572872 | tf_op jit(solution)/shard_map/ppermute | solution.py:26
  73.2 13.3 %collective-permute-start.24 = (bf16[128,2048]{1,0:T(8,128)(2,1)S(1)}, bf16[128,2048]{1,0:T(8,128)(2,1)S(1)}, u32[]{:S(2)}, u32[]{:S(2)}) collective-permute-start(bf16[128,2048]{1,0:T(8,128)(2,1)S(1)} %broadcast_select_fusion.1.refs_2_), channel_id=1, source_target_pairs={{0,4},{1,3},{2,6},{3,1},{4,0},{5,7},{6,2},{7,5},{8,12},{9,11},{10,... | collective-permute-start | bytes 1572872 | tf_op jit(solution)/shard_map/ppermute | solution.py:26
  86.2 13.3 %collective-permute-start.22 = (bf16[128,2048]{1,0:T(8,128)(2,1)S(1)}, bf16[128,2048]{1,0:T(8,128)(2,1)S(1)}, u32[]{:S(2)}, u32[]{:S(2)}) collective-permute-start(bf16[128,2048]{1,0:T(8,128)(2,1)S(1)} %broadcast_select_fusion.refs_5_), channel_id=1, source_target_pairs={{0,2},{1,5},{2,0},{3,7},{4,6},{5,1},{6,4},{7,3},{8,10},{9,13},{10,... | collective-permute-start | bytes 1572872 | tf_op jit(solution)/shard_map/ppermute | solution.py:26
  86.5 13.3 %collective-permute-start.25 = (bf16[128,2048]{1,0:T(8,128)(2,1)S(1)}, bf16[128,2048]{1,0:T(8,128)(2,1)S(1)}, u32[]{:S(2)}, u32[]{:S(2)}) collective-permute-start(bf16[128,2048]{1,0:T(8,128)(2,1)S(1)} %broadcast_select_fusion.refs_5_), channel_id=1, source_target_pairs={{0,4},{1,3},{2,6},{3,1},{4,0},{5,7},{6,2},{7,5},{8,12},{9,11},{10,... | collective-permute-start | bytes 1572872 | tf_op jit(solution)/shard_map/ppermute | solution.py:26
  88.2 13.7 %collective-permute-start.26 = (bf16[128,2048]{1,0:T(8,128)(2,1)S(1)}, bf16[128,2048]{1,0:T(8,128)(2,1)S(1)}, u32[]{:S(2)}, u32[]{:S(2)}) collective-permute-start(bf16[128,2048]{1,0:T(8,128)(2,1)S(1)} %collective-permute-done.16.refs_1_), channel_id=1, source_target_pairs={{0,8},{2,10},{4,12},{6,14},{8,0},{10,2},{12,4},{14,6},{16,24},{18,... | collective-permute-start | bytes 1572872 | tf_op jit(solution)/shard_map/ppermute | solution.py:20
  99.5 12.4 %collective-permute-start.29 = (bf16[128,2048]{1,0:T(8,128)(2,1)S(1)}, bf16[128,2048]{1,0:T(8,128)(2,1)S(1)}, u32[]{:S(2)}, u32[]{:S(2)}) collective-permute-start(bf16[128,2048]{1,0:T(8,128)(2,1)S(1)} %collective-permute-done.24.refs_4_), channel_id=1, source_target_pairs={{0,2},{1,5},{2,0},{3,7},{4,6},{5,1},{6,4},{7,3},{8,10},{9,13},{10,... | collective-permute-start | bytes 1572872 | tf_op jit(solution)/shard_map/ppermute | solution.py:26
  99.8 12.1 %collective-permute-start.30 = (bf16[128,2048]{1,0:T(8,128)(2,1)S(1)}, bf16[128,2048]{1,0:T(8,128)(2,1)S(1)}, u32[]{:S(2)}, u32[]{:S(2)}) collective-permute-start(bf16[128,2048]{1,0:T(8,128)(2,1)S(1)} %collective-permute-done.22.refs_0_), channel_id=1, source_target_pairs={{0,4},{1,3},{2,6},{3,1},{4,0},{5,7},{6,2},{7,5},{8,12},{9,11},{10,... | collective-permute-start | bytes 1572872 | tf_op jit(solution)/shard_map/ppermute | solution.py:26
  101.9 16.1 %collective-permute-start.27 = (bf16[128,2048]{1,0:T(8,128)(2,1)S(1)}, bf16[128,2048]{1,0:T(8,128)(2,1)S(1)}, u32[]{:S(2)}, u32[]{:S(2)}) collective-permute-start(bf16[128,2048]{1,0:T(8,128)(2,1)S(1)} %collective-permute-done.18.refs_3_), channel_id=1, source_target_pairs={{0,8},{2,10},{4,12},{6,14},{8,0},{10,2},{12,4},{14,6},{16,24},{18,... | collective-permute-start | bytes 1572872 | tf_op jit(solution)/shard_map/ppermute | solution.py:20
  115.2 12.7 %collective-permute-start.32 = (bf16[128,2048]{1,0:T(8,128)(2,1)S(1)}, bf16[128,2048]{1,0:T(8,128)(2,1)S(1)}, u32[]{:S(2)}, u32[]{:S(2)}) collective-permute-start(bf16[128,2048]{1,0:T(8,128)(2,1)S(1)} %get-tuple-element.104), channel_id=1, source_target_pairs={{0,4},{1,3},{2,6},{3,1},{4,0},{5,7},{6,2},{7,5},{8,12},{9,11},{10,... | collective-permute-start | bytes 1572872 | tf_op jit(solution)/shard_map/ppermute | solution.py:26
  117.7 12.2 %collective-permute-start.33 = (bf16[128,2048]{1,0:T(8,128)(2,1)S(1)}, bf16[128,2048]{1,0:T(8,128)(2,1)S(1)}, u32[]{:S(2)}, u32[]{:S(2)}) collective-permute-start(bf16[128,2048]{1,0:T(8,128)(2,1)S(1)} %get-tuple-element.100), channel_id=1, source_target_pairs={{0,2},{1,5},{2,0},{3,7},{4,6},{5,1},{6,4},{7,3},{8,10},{9,13},{10,... | collective-permute-start | bytes 1572872 | tf_op jit(solution)/shard_map/ppermute | solution.py:26
  118.0 16.5 %collective-permute-start.28 = (bf16[128,2048]{1,0:T(8,128)(2,1)S(1)}, bf16[128,2048]{1,0:T(8,128)(2,1)S(1)}, u32[]{:S(2)}, u32[]{:S(2)}) collective-permute-start(bf16[128,2048]{1,0:T(8,128)(2,1)S(1)} %get-tuple-element.94), channel_id=1, source_target_pairs={{0,8},{2,10},{4,12},{6,14},{8,0},{10,2},{12,4},{14,6},{16,24},{18,... | collective-permute-start | bytes 1572872 | tf_op jit(solution)/shard_map/ppermute | solution.py:20
  127.9 12.1 %collective-permute-start.38 = (bf16[128,2048]{1,0:T(8,128)(2,1)S(1)}, bf16[128,2048]{1,0:T(8,128)(2,1)S(1)}, u32[]{:S(2)}, u32[]{:S(2)}) collective-permute-start(bf16[128,2048]{1,0:T(8,128)(2,1)S(1)} %get-tuple-element.113), channel_id=1, source_target_pairs={{0,4},{1,3},{2,6},{3,1},{4,0},{5,7},{6,2},{7,5},{8,12},{9,11},{10,... | collective-permute-start | bytes 1572872 | tf_op jit(solution)/shard_map/ppermute | solution.py:26
  129.9 10.1 %collective-permute-start.34 = (bf16[128,2048]{1,0:T(8,128)(2,1)S(1)}, bf16[128,2048]{1,0:T(8,128)(2,1)S(1)}, u32[]{:S(2)}, u32[]{:S(2)}) collective-permute-start(bf16[128,2048]{1,0:T(8,128)(2,1)S(1)} %add_convert_fusion.7), channel_id=1, source_target_pairs={{0,2},{1,5},{2,0},{3,7},{4,6},{5,1},{6,4},{7,3},{8,10},{9,13},{10,... | collective-permute-start | bytes 1572872 | tf_op jit(solution)/shard_map/ppermute | solution.py:26
  134.4 9.5 %collective-permute-start.31 = (bf16[128,2048]{1,0:T(8,128)(2,1)S(1)}, bf16[128,2048]{1,0:T(8,128)(2,1)S(1)}, u32[]{:S(2)}, u32[]{:S(2)}) collective-permute-start(bf16[128,2048]{1,0:T(8,128)(2,1)S(1)} %expert_rows.9), channel_id=1, source_target_pairs={{0,8},{2,10},{4,12},{6,14},{8,0},{10,2},{12,4},{14,6},{16,24},{18,... | collective-permute-start | bytes 1572872 | tf_op jit(solution)/shard_map/ppermute | solution.py:20
  140.0 13.2 %collective-permute-start.35 = (bf16[128,2048]{1,0:T(8,128)(2,1)S(1)}, bf16[128,2048]{1,0:T(8,128)(2,1)S(1)}, u32[]{:S(2)}, u32[]{:S(2)}) collective-permute-start(bf16[128,2048]{1,0:T(8,128)(2,1)S(1)} %get-tuple-element.106), channel_id=1, source_target_pairs={{0,2},{1,5},{2,0},{3,7},{4,6},{5,1},{6,4},{7,3},{8,10},{9,13},{10,... | collective-permute-start | bytes 1572872 | tf_op jit(solution)/shard_map/ppermute | solution.py:26
  142.3 13.1 %collective-permute-start.39 = (bf16[128,2048]{1,0:T(8,128)(2,1)S(1)}, bf16[128,2048]{1,0:T(8,128)(2,1)S(1)}, u32[]{:S(2)}, u32[]{:S(2)}) collective-permute-start(bf16[128,2048]{1,0:T(8,128)(2,1)S(1)} %add_convert_fusion.5), channel_id=1, source_target_pairs={{0,4},{1,3},{2,6},{3,1},{4,0},{5,7},{6,2},{7,5},{8,12},{9,11},{10,... | collective-permute-start | bytes 1572872 | tf_op jit(solution)/shard_map/ppermute | solution.py:26
  144.0 12.8 %collective-permute-start.42 = (bf16[128,2048]{1,0:T(8,128)(2,1)S(1)}, bf16[128,2048]{1,0:T(8,128)(2,1)S(1)}, u32[]{:S(2)}, u32[]{:S(2)}) collective-permute-start(bf16[128,2048]{1,0:T(8,128)(2,1)S(1)} %add_convert_fusion.4), channel_id=1, source_target_pairs={{0,8},{2,10},{4,12},{6,14},{24,16},{26,18},{28,20},{30,22},{1,9},{... | collective-permute-start | bytes 1572872 | tf_op jit(solution)/shard_map/ppermute | solution.py:217
  153.1 12.1 %collective-permute-start.36 = (bf16[128,2048]{1,0:T(8,128)(2,1)S(1)}, bf16[128,2048]{1,0:T(8,128)(2,1)S(1)}, u32[]{:S(2)}, u32[]{:S(2)}) collective-permute-start(bf16[128,2048]{1,0:T(8,128)(2,1)S(1)} %add_convert_fusion.8), channel_id=1, source_target_pairs={{0,2},{1,5},{2,0},{3,7},{4,6},{5,1},{6,4},{7,3},{8,10},{9,13},{10,... | collective-permute-start | bytes 1572872 | tf_op jit(solution)/shard_map/ppermute | solution.py:26
  155.3 13.9 %collective-permute-start.40 = (bf16[128,2048]{1,0:T(8,128)(2,1)S(1)}, bf16[128,2048]{1,0:T(8,128)(2,1)S(1)}, u32[]{:S(2)}, u32[]{:S(2)}) collective-permute-start(bf16[128,2048]{1,0:T(8,128)(2,1)S(1)} %get-tuple-element.115), channel_id=1, source_target_pairs={{0,4},{1,3},{2,6},{3,1},{4,0},{5,7},{6,2},{7,5},{8,12},{9,11},{10,... | collective-permute-start | bytes 1572872 | tf_op jit(solution)/shard_map/ppermute | solution.py:26
  157.1 13.0 %collective-permute-start.43 = (bf16[128,2048]{1,0:T(8,128)(2,1)S(1)}, bf16[128,2048]{1,0:T(8,128)(2,1)S(1)}, u32[]{:S(2)}, u32[]{:S(2)}) collective-permute-start(bf16[128,2048]{1,0:T(8,128)(2,1)S(1)} %add_convert_fusion.3), channel_id=1, source_target_pairs={{8,16},{10,18},{12,20},{14,22},{16,8},{18,10},{20,12},{22,14},{9,1... | collective-permute-start | bytes 1572872 | tf_op jit(solution)/shard_map/ppermute | solution.py:217
  159.2 14.0 %collective-permute-start.44 = (bf16[128,2048]{1,0:T(8,128)(2,1)S(1)}, bf16[128,2048]{1,0:T(8,128)(2,1)S(1)}, u32[]{:S(2)}, u32[]{:S(2)}) collective-permute-start(bf16[128,2048]{1,0:T(8,128)(2,1)S(1)} %add_convert_fusion.3), channel_id=1, source_target_pairs={{0,8},{2,10},{4,12},{6,14},{24,16},{26,18},{28,20},{30,22},{1,9},{... | collective-permute-start | bytes 1572872 | tf_op jit(solution)/shard_map/ppermute | solution.py:217
  165.2 12.0 %collective-permute-start.37 = (bf16[128,2048]{1,0:T(8,128)(2,1)S(1)}, bf16[128,2048]{1,0:T(8,128)(2,1)S(1)}, u32[]{:S(2)}, u32[]{:S(2)}) collective-permute-start(bf16[128,2048]{1,0:T(8,128)(2,1)S(1)} %add_convert_fusion.9), channel_id=1, source_target_pairs={{0,2},{1,5},{2,0},{3,7},{4,6},{5,1},{6,4},{7,3},{8,10},{9,13},{10,... | collective-permute-start | bytes 1572872 | tf_op jit(solution)/shard_map/ppermute | solution.py:26
  169.2 9.2 %collective-permute-start.41 = (bf16[128,2048]{1,0:T(8,128)(2,1)S(1)}, bf16[128,2048]{1,0:T(8,128)(2,1)S(1)}, u32[]{:S(2)}, u32[]{:S(2)}) collective-permute-start(bf16[128,2048]{1,0:T(8,128)(2,1)S(1)} %add_convert_fusion.6), channel_id=1, source_target_pairs={{0,4},{1,3},{2,6},{3,1},{4,0},{5,7},{6,2},{7,5},{8,12},{9,11},{10,... | collective-permute-start | bytes 1572872 | tf_op jit(solution)/shard_map/ppermute | solution.py:26
  173.2 9.2 %collective-permute-start.45 = (bf16[128,2048]{1,0:T(8,128)(2,1)S(1)}, bf16[128,2048]{1,0:T(8,128)(2,1)S(1)}, u32[]{:S(2)}, u32[]{:S(2)}) collective-permute-start(bf16[128,2048]{1,0:T(8,128)(2,1)S(1)} %add_convert_fusion.2), channel_id=1, source_target_pairs={{0,8},{2,10},{4,12},{6,14},{8,0},{10,2},{12,4},{14,6},{16,24},{18,... | collective-permute-start | bytes 1572872 | tf_op jit(solution)/shard_map/ppermute | solution.py:20
  173.3 11.1 %collective-permute-start.46 = (bf16[128,2048]{1,0:T(8,128)(2,1)S(1)}, bf16[128,2048]{1,0:T(8,128)(2,1)S(1)}, u32[]{:S(2)}, u32[]{:S(2)}) collective-permute-start(bf16[128,2048]{1,0:T(8,128)(2,1)S(1)} %add_convert_fusion.1), channel_id=1, source_target_pairs={{8,16},{10,18},{12,20},{14,22},{16,8},{18,10},{20,12},{22,14},{9,1... | collective-permute-start | bytes 1572872 | tf_op jit(solution)/shard_map/ppermute | solution.py:217
  (9 other events, 39.5 us)

commit v17 on v14

--- a/solution.py
+++ b/solution.py
@@ -159,16 +159,30 @@
     )(*halves)
 
 
-def gates_at(place, rows, pieces):
-    piece = place.bit_length()
-    at = (place - (1 << piece >> 1)) * rows
-    return pieces[piece][:, at : at + rows]
-
-
-def expert_kernel(places, pieces, where_ref, *refs):
+def own_gates_kernel(where_ref, *refs):
+    at = 0
+    for piece in refs[:-1]:
+        expert = lax.broadcasted_iota(jnp.int32, piece.shape, 0)
+        chosen = jnp.where(expert == where_ref[0], piece[...], 0.0)
+        refs[-1][:, at : at + piece.shape[1]] = jnp.sum(chosen, axis=0, keepdims=True)
+        at += piece.shape[1]
+
+
+def own_gates(where, pieces):
+    width = sum(piece.shape[1] for piece in pieces)
+    return pl.pallas_call(
+        own_gates_kernel,
+        out_shape=jax.ShapeDtypeStruct((1, width), jnp.float32),
+        in_specs=[pl.BlockSpec(memory_space=pltpu.SMEM)] + [VMEM] * len(pieces),
+        out_specs=VMEM,
+        compiler_params=pltpu.CompilerParams(vmem_limit_bytes=8 * 1024 * 1024),
+        name="own_gates",
+    )(where, *pieces)
+
+
+def expert_kernel(places, where_ref, *refs):
     count = len(places)
-    blocks, gates, (gate_up, down) = refs[:count], refs[count : count + pieces], refs[count + pieces :][:2]
-    outs = refs[count + pieces + 2 :]
+    blocks, (gates, gate_up, down), outs = refs[:count], refs[count : count + 3], refs[count + 3 :]
     units = down.shape[0]
     rows = blocks[0].shape[0]
     for first in range(0, count, 2):
@@ -179,11 +193,10 @@
         act = (gate / (1.0 + jnp.exp(-gate)) * up).astype(jnp.bfloat16)
         result = jnp.dot(act, down[...], preferred_element_type=jnp.float32)
         for i in group:
-            here = gates_at(places[i][0], rows, gates)
+            chosen = gates[:, places[i][0] * rows : (places[i][0] + 1) * rows]
             if places[i][0] != places[i][1]:
-                here = jnp.where(where_ref[1] == 1, gates_at(places[i][1], rows, gates), here)
-            expert = lax.broadcasted_iota(jnp.int32, here.shape, 0)
-            chosen = jnp.sum(jnp.where(expert == where_ref[0], here, 0.0), axis=0, keepdims=True)
+                other = gates[:, places[i][1] * rows : (places[i][1] + 1) * rows]
+                chosen = jnp.where(where_ref[1] == 1, other, chosen)
             chosen = jnp.transpose(jnp.broadcast_to(chosen, (rows, rows)))[:, :1]
             part = result[(i - first) * rows : (i - first + 1) * rows]
             outs[i][...] = (part * chosen).astype(jnp.bfloat16)
@@ -193,13 +206,13 @@
     rows, width = blocks[0].shape
     count = len(blocks)
     return pl.pallas_call(
-        functools.partial(expert_kernel, places, len(gates)),
+        functools.partial(expert_kernel, places),
         out_shape=[jax.ShapeDtypeStruct((rows, width), jnp.bfloat16)] * count,
-        in_specs=[pl.BlockSpec(memory_space=pltpu.SMEM)] + [VMEM] * (count + len(gates) + 2),
+        in_specs=[pl.BlockSpec(memory_space=pltpu.SMEM)] + [VMEM] * (count + 3),
         out_specs=[VMEM] * count,
         compiler_params=pltpu.CompilerParams(vmem_limit_bytes=36 * 1024 * 1024),
         name="expert_rows",
-    )(where, *blocks, *gates, *weights)
+    )(where, *blocks, gates, *weights)
 
 
 def add(*terms):
@@ -282,10 +295,12 @@
     def weights(*waits):
         return assemble([after(half, *waits) for half in halves])
 
+    row = own_gates(where, gates)
+
     def run(weights, blocks, masks):
         masks = [mask if isinstance(mask, tuple) else (mask, mask) for mask in masks]
         places = tuple(tuple(place_of(j) for j in mask) for mask in masks)
-        return expert(blocks, places, where, gates, weights)
+        return expert(blocks, places, where, row, weights)
 
     if count == 16:
         return step_layer(normed, stream, run, weights)

time: 186 us -> 186 us (level)
    pallas_call x5 -> x6, Pallas kernels: 25.5 us -> 26 us  [the longest x5 25.4 us: expert(): pl.pallas_call(functools.partial(expert_kernel, places), out_shape=[jax.S...]
  transfers between devices with their start and end apart: 47 -> 47, of which waited for: 25 -> 24; matrix products, arithmetic and copies ran while one was open for 3% -> 3% of each run, Pallas kernels for 18% -> 18%
where the time goes in v17:
time: 186 us; the launch traced here: 185 us
  waiting for transfers between devices  77.6 us (42%)
  starting transfers between devices  57 us (31%)
  Pallas kernels  37.5 us (20%)
  local copies, waits for them, and re-layouts  6.87 us (4%)
  other arithmetic  5.44 us (3%)
    ppermute x20, waiting for transfers between devices, cross(): return lax.ppermute(block, ('seq', 'exp'), pairs)  46.6 us
    pallas_call x5, Pallas kernels, expert(): pl.pallas_call(functools.partial(expert_kernel, places), out_shape=[jax.S...  25.4 us
    ppermute x8, starting transfers between devices, shift(): lax.ppermute(block, 'seq', [(4 * a + i, 4 * b + i) for a, b in pairs for...  20.5 us
    ppermute x12, waiting for transfers between devices, flip(): return lax.ppermute(block, 'seq', [(i, i ^ mask) for i in range(count)])  20 us
    ppermute x20, starting transfers between devices, cross(): return lax.ppermute(block, ('seq', 'exp'), pairs)  19.9 us
    ppermute x12, starting transfers between devices, flip(): return lax.ppermute(block, 'seq', [(i, i ^ mask) for i in range(count)])  9.56 us
    ppermute x8, waiting for transfers between devices, shift(): lax.ppermute(block, 'seq', [(4 * a + i, 4 * b + i) for a, b in pairs for...  9.38 us
    ppermute x2, starting transfers between devices, halo(): return (beside, part, lax.ppermute(beside, 'seq', ahead + back))  6.6 us
  transfers between devices with their start and end apart: 47, of which 24 were waited for; matrix products, arithmetic and copies ran while one was open for 3% of the time, Pallas kernels for 18%

profile of v17, /device:TPU:10, one launch (start us, length us, event | category | flops | bytes accessed | tf_op | source)
XLA Modules:
  0.0 184.7 jit_solution(4473453230193325042)
XLA Ops:
  0.5 1.5 collective-permute-start.2
  3.3 3.2 %collective-permute-done.7.refs_1_ = f32[16,128]{1,0:T(8,128)S(1)} collective-permute-done((f32[16,128]{1,0:T(8,128)S(1)}, f32[16,128]{1,0:T(8,128)S(1)}, u32[]{:S(2)}, u32[]{:S(2)}) %collective-permute-start.7) | collective-permute-done | bytes 8224 | tf_op jit(solution)/shard_map/ppermute | solution.py:20
  6.5 2.6 %collective-permute-start.8 = (f32[16,256]{1,0:T(8,128)S(1)}, f32[16,256]{1,0:T(8,128)S(1)}, u32[]{:S(2)}, u32[]{:S(2)}) collective-permute-start(f32[16,256]{1,0:T(8,128)S(1)} %pad_maximum_fusion.2), channel_id=1, source_target_pairs={{0,16},{2,18},{4,20},{6,22},{8,24},{10,26},{12,28},{14,30},{16,0},... | collective-permute-start | bytes 49160 | tf_op jit(solution)/shard_map/ppermute | solution.py:20
  9.3 3.3 %collective-permute-start.1 = (bf16[256,512]{1,0:T(8,128)(2,1)S(1)}, bf16[256,512]{1,0:T(8,128)(2,1)S(1)}, u32[]{:S(2)}, u32[]{:S(2)}) collective-permute-start(bf16[256,512]{1,0:T(8,128)(2,1)S(1)} %collective-permute-done.refs_0_), channel_id=1, source_target_pairs={{0,4},{4,8},{8,12},{12,16},{16,20},{20,24},{24,28},{6,2},{10,6},{1... | collective-permute-start | bytes 786440 | tf_op jit(solution)/shard_map/ppermute | solution.py:345
  12.6 1.9 %collective-permute-done.2.refs_3_ = bf16[256,512]{1,0:T(8,128)(2,1)S(1)} collective-permute-done((bf16[256,512]{1,0:T(8,128)(2,1)}, bf16[256,512]{1,0:T(8,128)(2,1)S(1)}, u32[]{:S(2)}, u32[]{:S(2)}) %collective-permute-start.2) | collective-permute-done | bytes 262176 | tf_op jit(solution)/shard_map/ppermute | solution.py:20
  14.6 3.3 %collective-permute-start.3 = (bf16[256,512]{1,0:T(8,128)(2,1)S(1)}, bf16[256,512]{1,0:T(8,128)(2,1)S(1)}, u32[]{:S(2)}, u32[]{:S(2)}) collective-permute-start(bf16[256,512]{1,0:T(8,128)(2,1)S(1)} %collective-permute-done.2.refs_3_), channel_id=1, source_target_pairs={{0,4},{4,8},{8,12},{12,16},{16,20},{20,24},{24,28},{6,2},{10,6},{1... | collective-permute-start | bytes 786440 | tf_op jit(solution)/shard_map/ppermute | solution.py:345
  20.5 4.5 %collective-permute-done.9.refs_3_ = f32[16,512]{1,0:T(8,128)S(1)} collective-permute-done((f32[16,512]{1,0:T(8,128)S(1)}, f32[16,512]{1,0:T(8,128)S(1)}, u32[]{:S(2)}, u32[]{:S(2)}) %collective-permute-start.9) | collective-permute-done | bytes 32800 | tf_op jit(solution)/shard_map/ppermute | solution.py:20
  26.4 4.6 %window_attention.1 = (bf16[128,512]{1,0:T(8,128)(2,1)}, bf16[128,512]{1,0:T(8,128)(2,1)}) custom-call(s32[2]{0:T(128)} %pad_add_fusion.where_ref, bf16[256,512]{1,0:T(8,128)(2,1)} %q_ref.1, s32[1,768]{1,0:T(1,128)} %broadcast_in_dim.21.ids_ref, bf16[256,512]{1,0:T(8,128)(2,1)} %copy-done.5, bf16[256,512]{1,0:T(8,128)(2,1)} %refs_1_.1, ...), custom_call_target="tpu_custom_call" | custom-call | tf_op jit(solution)/shard_map/window_attention/pallas_call | solution.py:97
  33.2 4.3 %project_and_norm.1 = (f32[128,2048]{1,0:T(8,128)}, bf16[128,2048]{1,0:T(8,128)(2,1)}) custom-call(bf16[128,512]{1,0:T(8,128)(2,1)} %get-tuple-element.64.mine_ref, bf16[128,512]{1,0:T(8,128)(2,1)} %copy-done.9, bf16[512,2048]{1,0:T(8,128)(2,1)} %own_w.1, bf16[512,2048]{1,0:T(8,128)(2,1)} %collective-permute-done.4.refs_6_.other_w, ...), custom_call_target="tpu_custom_call" | custom-call | tf_op jit(solution)/shard_map/project_and_norm/pallas_call | solution.py:120
  37.9 4.6 %collective-permute-start.14 = (bf16[128,2048]{1,0:T(8,128)(2,1)}, bf16[128,2048]{1,0:T(8,128)(2,1)S(1)}, u32[]{:S(2)}, u32[]{:S(2)}) collective-permute-start(bf16[128,2048]{1,0:T(8,128)(2,1)} %get-tuple-element.70.refs_0_), channel_id=1, source_target_pairs={{8,16},{10,18},{12,20},{14,22},{16,8},{18,10},{20,12},{22,14},{9,1... | collective-permute-start | bytes 1572872 | tf_op jit(solution)/shard_map/ppermute | solution.py:230
  43.4 1.2 collective-permute-start.16
  44.6 7.0 %collective-permute-done.12.refs_0_ = bf16[128,2048]{1,0:T(8,128)(2,1)S(1)} collective-permute-done((bf16[128,2048]{1,0:T(8,128)(2,1)}, bf16[128,2048]{1,0:T(8,128)(2,1)S(1)}, u32[]{:S(2)}, u32[]{:S(2)}) %collective-permute-start.12) | collective-permute-done | bytes 524320 | tf_op jit(solution)/shard_map/ppermute | solution.py:20
  51.6 3.5 %collective-permute-start.13 = (bf16[128,2048]{1,0:T(8,128)(2,1)S(1)}, bf16[128,2048]{1,0:T(8,128)(2,1)}, u32[]{:S(2)}, u32[]{:S(2)}) collective-permute-start(bf16[128,2048]{1,0:T(8,128)(2,1)S(1)} %collective-permute-done.12.refs_0_), channel_id=1, source_target_pairs={{8,16},{10,18},{12,20},{14,22},{16,8},{18,10},{20,12},{22,14},{9,1... | collective-permute-start | bytes 1572872 | tf_op jit(solution)/shard_map/ppermute | solution.py:230
  55.1 2.1 %collective-permute-start.15 = (bf16[128,2048]{1,0:T(8,128)(2,1)S(1)}, bf16[128,2048]{1,0:T(8,128)(2,1)}, u32[]{:S(2)}, u32[]{:S(2)}) collective-permute-start(bf16[128,2048]{1,0:T(8,128)(2,1)S(1)} %collective-permute-done.14), channel_id=1, source_target_pairs={{8,0},{10,2},{12,4},{14,6},{16,24},{18,26},{20,28},{22,30},{9,1},{... | collective-permute-start | bytes 1572872 | tf_op jit(solution)/shard_map/ppermute | solution.py:230
  57.4 1.3 collective-permute-start.18
  59.7 2.0 %collective-permute-start.19 = (f32[16,1024]{1,0:T(8,128)S(1)}, f32[16,1024]{1,0:T(8,128)S(1)}, u32[]{:S(2)}, u32[]{:S(2)}) collective-permute-start(f32[16,1024]{1,0:T(8,128)S(1)} %pad_maximum_fusion), channel_id=1, source_target_pairs={{0,2},{2,0},{4,6},{6,4},{8,10},{10,8},{12,14},{14,12},{16,18},{18,... | collective-permute-start | bytes 196616 | tf_op jit(solution)/shard_map/ppermute | solution.py:20
  61.7 1.4 copy-done
  63.1 1.4 copy-done.1
  64.4 1.4 copy-done.2
  65.8 2.6 %assemble_weights.1 = (bf16[1408,2048]{1,0:T(8,128)(2,1)S(1)}, bf16[704,2048]{1,0:T(8,128)(2,1)S(1)}) custom-call(bf16[352,2048]{1,0:T(8,128)(2,1)S(1)} %bitcast.14, bf16[352,2048]{1,0:T(8,128)(2,1)} %collective-permute-done.5.refs_7_.refs_1_, bf16[352,2048]{1,0:T(8,128)(2,1)S(1)} %bitcast.16, bf16[352,2048]{1,0:T(8,128)(2,1)} %collective-permute-done.10.refs_0_.refs_3_, ...), custom_call_target="tpu_custom_call" | custom-call | tf_op jit(solution)/shard_map/assemble_weights/pallas_call | solution.py:148
  68.5 1.6 collective-permute-start.23
  74.7 5.6 %expert_rows.5 = (bf16[128,2048]{1,0:T(8,128)(2,1)S(1)}, bf16[128,2048]{1,0:T(8,128)(2,1)S(1)}, bf16[128,2048]{1,0:T(8,128)(2,1)S(1)}, bf16[128,2048]{1,0:T(8,128)(2,1)S(1)}) custom-call(s32[2]{0:T(128)S(1)} %pad_add_fusion.1.where_ref, bf16[128,2048]{1,0:T(8,128)(2,1)S(1)} %copy-done.3, bf16[128,2048]{1,0:T(8,128)(2,1)S(1)} %collective-permute-done.16.refs_1_, ...), custom_call_target="tpu_custom_call" | custom-call | tf_op jit(solution)/shard_map/expert_rows/pallas_call | solution.py:208
  80.4 5.8 %collective-permute-done.21.refs_3_ = bf16[128,2048]{1,0:T(8,128)(2,1)S(1)} collective-permute-done((bf16[128,2048]{1,0:T(8,128)(2,1)S(1)}, bf16[128,2048]{1,0:T(8,128)(2,1)S(1)}, u32[]{:S(2)}, u32[]{:S(2)}) %collective-permute-start.21) | collective-permute-done | bytes 524320 | tf_op jit(solution)/shard_map/ppermute | solution.py:26
  86.5 8.1 %expert_rows.6 = (bf16[128,2048]{1,0:T(8,128)(2,1)S(1)}, bf16[128,2048]{1,0:T(8,128)(2,1)S(1)}, bf16[128,2048]{1,0:T(8,128)(2,1)S(1)}, bf16[128,2048]{1,0:T(8,12...) custom-call(s32[2]{0:T(128)S(1)} %pad_add_fusion.1.where_ref, ...), custom_call_target="tpu_custom_call" | custom-call | tf_op jit(solution)/shard_map/expert_rows/pallas_call | solution.py:208
  94.6 5.0 %collective-permute-done.24.refs_0_ = bf16[128,2048]{1,0:T(8,128)(2,1)S(1)} collective-permute-done((bf16[128,2048]{1,0:T(8,128)(2,1)S(1)}, bf16[128,2048]{1,0:T(8,128)(2,1)S(1)}, u32[]{:S(2)}, u32[]{:S(2)}) %collective-permute-start.24) | collective-permute-done | bytes 524320 | tf_op jit(solution)/shard_map/ppermute | solution.py:26
  100.4 5.6 %expert_rows.7 = (bf16[128,2048]{1,0:T(8,128)(2,1)S(1)}, bf16[128,2048]{1,0:T(8,128)(2,1)S(1)}, bf16[128,2048]{1,0:T(8,128)(2,1)S(1)}) custom-call(s32[2]{0:T(128)S(1)} %pad_add_fusion.1.where_ref, bf16[128,2048]{1,0:T(8,128)(2,1)S(1)} %collective-permute-done.24.refs_0_, bf16[128,2048]{1,0:T(8,128)(2,1)S(1)} %collective-permute-done.26.refs_1_, ...), custom_call_target="tpu_custom_call" | custom-call | tf_op jit(solution)/shard_map/expert_rows/pallas_call | solution.py:208
  106.0 5.9 %collective-permute-done.25.refs_0_ = bf16[128,2048]{1,0:T(8,128)(2,1)S(1)} collective-permute-done((bf16[128,2048]{1,0:T(8,128)(2,1)S(1)}, bf16[128,2048]{1,0:T(8,128)(2,1)S(1)}, u32[]{:S(2)}, u32[]{:S(2)}) %collective-permute-start.25) | collective-permute-done | bytes 524320 | tf_op jit(solution)/shard_map/ppermute | solution.py:26
  111.9 3.2 %expert_rows.8 = (bf16[128,2048]{1,0:T(8,128)(2,1)S(1)}, bf16[128,2048]{1,0:T(8,128)(2,1)S(1)}) custom-call(s32[2]{0:T(128)S(1)} %pad_add_fusion.1.where_ref, bf16[128,2048]{1,0:T(8,128)(2,1)S(1)} %collective-permute-done.25.refs_0_, bf16[128,2048]{1,0:T(8,128)(2,1)S(1)} %collective-permute-done.28.refs_1_, ...), custom_call_target="tpu_custom_call" | custom-call | tf_op jit(solution)/shard_map/expert_rows/pallas_call | solution.py:208
  116.2 11.1 %collective-permute-done.30 = bf16[128,2048]{1,0:T(8,128)(2,1)S(1)} collective-permute-done((bf16[128,2048]{1,0:T(8,128)(2,1)S(1)}, bf16[128,2048]{1,0:T(8,128)(2,1)S(1)}, u32[]{:S(2)}, u32[]{:S(2)}) %collective-permute-start.30) | collective-permute-done | bytes 524320 | tf_op jit(solution)/shard_map/ppermute | solution.py:26
  127.4 1.2 collective-permute-start.34
  128.9 2.9 %expert_rows.9 = bf16[128,2048]{1,0:T(8,128)(2,1)S(1)} custom-call(s32[2]{0:T(128)S(1)} %pad_add_fusion.1.where_ref, bf16[128,2048]{1,0:T(8,128)(2,1)S(1)} %collective-permute-done.36.refs_0_, f32[1,2048]{1,0:T(1,128)S(1)} %own_gates.1.refs_4_.refs_6_.refs_3_.refs_2_.refs_1_, ...), custom_call_target="tpu_custom_call" | custom-call | tf_op jit(solution)/shard_map/expert_rows/pallas_call | solution.py:208
  132.1 6.9 %collective-permute-done.34 = bf16[128,2048]{1,0:T(8,128)(2,1)S(1)} collective-permute-done((bf16[128,2048]{1,0:T(8,128)(2,1)S(1)}, bf16[128,2048]{1,0:T(8,128)(2,1)S(1)}, u32[]{:S(2)}, u32[]{:S(2)}) %collective-permute-start.34) | collective-permute-done | bytes 524320 | tf_op jit(solution)/shard_map/ppermute | solution.py:26
  139.0 1.7 collective-permute-start.35
  140.7 1.5 collective-permute-start.32
  143.5 1.3 collective-permute-start.39
  144.9 6.2 %collective-permute-done.35 = bf16[128,2048]{1,0:T(8,128)(2,1)S(1)} collective-permute-done((bf16[128,2048]{1,0:T(8,128)(2,1)S(1)}, bf16[128,2048]{1,0:T(8,128)(2,1)S(1)}, u32[]{:S(2)}, u32[]{:S(2)}) %collective-permute-start.35) | collective-permute-done | bytes 524320 | tf_op jit(solution)/shard_map/ppermute | solution.py:26
  151.1 1.7 collective-permute-start.44
  153.7 2.5 %collective-permute-start.33 = (bf16[128,2048]{1,0:T(8,128)(2,1)S(1)}, bf16[128,2048]{1,0:T(8,128)(2,1)S(1)}, u32[]{:S(2)}, u32[]{:S(2)}) collective-permute-start(bf16[128,2048]{1,0:T(8,128)(2,1)S(1)} %get-tuple-element.102), channel_id=1, source_target_pairs={{0,4},{1,3},{2,6},{3,1},{4,0},{5,7},{6,2},{7,5},{8,12},{9,11},{10,... | collective-permute-start | bytes 1572872 | tf_op jit(solution)/shard_map/ppermute | solution.py:26
  156.5 1.9 %collective-permute-start.40 = (bf16[128,2048]{1,0:T(8,128)(2,1)S(1)}, bf16[128,2048]{1,0:T(8,128)(2,1)S(1)}, u32[]{:S(2)}, u32[]{:S(2)}) collective-permute-start(bf16[128,2048]{1,0:T(8,128)(2,1)S(1)} %add_convert_fusion.6), channel_id=1, source_target_pairs={{8,16},{10,18},{12,20},{14,22},{16,8},{18,10},{20,12},{22,14},{9,1... | collective-permute-start | bytes 1572872 | tf_op jit(solution)/shard_map/ppermute | solution.py:230
  158.6 1.3 collective-permute-start.41
  159.9 3.3 %collective-permute-done.44 = bf16[128,2048]{1,0:T(8,128)(2,1)S(1)} collective-permute-done((bf16[128,2048]{1,0:T(8,128)(2,1)S(1)}, bf16[128,2048]{1,0:T(8,128)(2,1)S(1)}, u32[]{:S(2)}, u32[]{:S(2)}) %collective-permute-start.44) | collective-permute-done | bytes 524320 | tf_op jit(solution)/shard_map/ppermute | solution.py:26
  163.4 2.3 %collective-permute-start.46 = (bf16[128,2048]{1,0:T(8,128)(2,1)S(1)}, bf16[128,2048]{1,0:T(8,128)(2,1)S(1)}, u32[]{:S(2)}, u32[]{:S(2)}) collective-permute-start(bf16[128,2048]{1,0:T(8,128)(2,1)S(1)} %add_convert_fusion.1), channel_id=1, source_target_pairs={{0,4},{1,3},{2,6},{3,1},{4,0},{5,7},{6,2},{7,5},{8,12},{9,11},{10,... | collective-permute-start | bytes 1572872 | tf_op jit(solution)/shard_map/ppermute | solution.py:26
  165.7 1.2 collective-permute-start.45
  168.1 1.8 collective-permute-done.41
  170.1 4.2 %collective-permute-start.43 = (bf16[128,2048]{1,0:T(8,128)(2,1)S(1)}, bf16[128,2048]{1,0:T(8,128)(2,1)S(1)}, u32[]{:S(2)}, u32[]{:S(2)}) collective-permute-start(bf16[128,2048]{1,0:T(8,128)(2,1)S(1)} %add_convert_fusion.4), channel_id=1, source_target_pairs={{8,16},{10,18},{12,20},{14,22},{16,8},{18,10},{20,12},{22,14},{9,1... | collective-permute-start | bytes 1572872 | tf_op jit(solution)/shard_map/ppermute | solution.py:230
  174.8 6.5 %collective-permute-done.43 = bf16[128,2048]{1,0:T(8,128)(2,1)S(1)} collective-permute-done((bf16[128,2048]{1,0:T(8,128)(2,1)S(1)}, bf16[128,2048]{1,0:T(8,128)(2,1)S(1)}, u32[]{:S(2)}, u32[]{:S(2)}) %collective-permute-start.43) | collective-permute-done | bytes 524320 | tf_op jit(solution)/shard_map/ppermute | solution.py:230
  181.4 2.1 %collective-permute-done.42 = bf16[128,2048]{1,0:T(8,128)(2,1)S(1)} collective-permute-done((bf16[128,2048]{1,0:T(8,128)(2,1)S(1)}, bf16[128,2048]{1,0:T(8,128)(2,1)S(1)}, u32[]{:S(2)}, u32[]{:S(2)}) %collective-permute-start.42) | collective-permute-done | bytes 524320 | tf_op jit(solution)/shard_map/ppermute | solution.py:20
  183.5 1.3 add_convert_fusion
  (95 shorter events, 23.0 us)
Async XLA Ops:
  0.0 26.3 %collective-permute-start.4 = (bf16[512,2048]{1,0:T(8,128)(2,1)}, bf16[512,2048]{1,0:T(8,128)(2,1)}, u32[]{:S(2)}, u32[]{:S(2)}) collective-permute-start(bf16[512,2048]{1,0:T(8,128)(2,1)} %own_w.1), channel_id=1, source_target_pairs={{0,1},{1,0},{2,3},{3,2},{4,5},{5,4},{6,7},{7,6},{8,9},{9,8},{10,11... | collective-permute-start | bytes 6291464 | tf_op jit(solution)/shard_map/ppermute | solution.py:354
  0.0 9.3 %collective-permute-start = (bf16[256,512]{1,0:T(8,128)(2,1)}, bf16[256,512]{1,0:T(8,128)(2,1)S(1)}, u32[]{:S(2)}, u32[]{:S(2)}) collective-permute-start(bf16[256,512]{1,0:T(8,128)(2,1)} %refs_1_.1), channel_id=1, source_target_pairs={{0,2},{2,0},{4,6},{6,4},{8,10},{10,8},{12,14},{14,12},{16,18},{18,... | collective-permute-start | bytes 786440 | tf_op jit(solution)/shard_map/ppermute | solution.py:20
  0.5 14.0 %collective-permute-start.2 = (bf16[256,512]{1,0:T(8,128)(2,1)}, bf16[256,512]{1,0:T(8,128)(2,1)S(1)}, u32[]{:S(2)}, u32[]{:S(2)}) collective-permute-start(bf16[256,512]{1,0:T(8,128)(2,1)} %refs_4_.1), channel_id=1, source_target_pairs={{0,2},{2,0},{4,6},{6,4},{8,10},{10,8},{12,14},{14,12},{16,18},{18,... | collective-permute-start | bytes 786440 | tf_op jit(solution)/shard_map/ppermute | solution.py:20
  2.7 3.7 %collective-permute-start.7 = (f32[16,128]{1,0:T(8,128)S(1)}, f32[16,128]{1,0:T(8,128)S(1)}, u32[]{:S(2)}, u32[]{:S(2)}) collective-permute-start(f32[16,128]{1,0:T(8,128)S(1)} %select_reduce_fusion.refs_0_), channel_id=1, source_target_pairs={{0,8},{2,10},{4,12},{6,14},{8,0},{10,2},{12,4},{14,6},{16,24},{18,... | collective-permute-start | bytes 24584 | tf_op jit(solution)/shard_map/ppermute | solution.py:20
  3.3 23.1 %collective-permute-start.5 = (bf16[352,2048]{1,0:T(8,128)(2,1)}, bf16[352,2048]{1,0:T(8,128)(2,1)}, u32[]{:S(2)}, u32[]{:S(2)}) collective-permute-start(bf16[352,2048]{1,0:T(8,128)(2,1)} %bitcast.13), channel_id=1, source_target_pairs={{0,1},{1,0},{2,3},{3,2},{4,5},{5,4},{6,7},{7,6},{8,9},{9,8},{10,11... | collective-permute-start | bytes 4325384 | tf_op jit(solution)/shard_map/ppermute | solution.py:356
  6.5 12.2 %collective-permute-start.8 = (f32[16,256]{1,0:T(8,128)S(1)}, f32[16,256]{1,0:T(8,128)S(1)}, u32[]{:S(2)}, u32[]{:S(2)}) collective-permute-start(f32[16,256]{1,0:T(8,128)S(1)} %pad_maximum_fusion.2), channel_id=1, source_target_pairs={{0,16},{2,18},{4,20},{6,22},{8,24},{10,26},{12,28},{14,30},{16,0},... | collective-permute-start | bytes 49160 | tf_op jit(solution)/shard_map/ppermute | solution.py:20
  9.3 15.8 %collective-permute-start.1 = (bf16[256,512]{1,0:T(8,128)(2,1)S(1)}, bf16[256,512]{1,0:T(8,128)(2,1)S(1)}, u32[]{:S(2)}, u32[]{:S(2)}) collective-permute-start(bf16[256,512]{1,0:T(8,128)(2,1)S(1)} %collective-permute-done.refs_0_), channel_id=1, source_target_pairs={{0,4},{4,8},{8,12},{12,16},{16,20},{20,24},{24,28},{6,2},{10,6},{1... | collective-permute-start | bytes 786440 | tf_op jit(solution)/shard_map/ppermute | solution.py:345
  14.6 10.5 %collective-permute-start.3 = (bf16[256,512]{1,0:T(8,128)(2,1)S(1)}, bf16[256,512]{1,0:T(8,128)(2,1)S(1)}, u32[]{:S(2)}, u32[]{:S(2)}) collective-permute-start(bf16[256,512]{1,0:T(8,128)(2,1)S(1)} %collective-permute-done.2.refs_3_), channel_id=1, source_target_pairs={{0,4},{4,8},{8,12},{12,16},{16,20},{20,24},{24,28},{6,2},{10,6},{1... | collective-permute-start | bytes 786440 | tf_op jit(solution)/shard_map/ppermute | solution.py:345
  18.7 6.4 %collective-permute-start.9 = (f32[16,512]{1,0:T(8,128)S(1)}, f32[16,512]{1,0:T(8,128)S(1)}, u32[]{:S(2)}, u32[]{:S(2)}) collective-permute-start(f32[16,512]{1,0:T(8,128)S(1)} %pad_maximum_fusion.1), channel_id=1, source_target_pairs={{0,4},{2,6},{4,0},{6,2},{8,12},{10,14},{12,8},{14,10},{16,20},{18,... | collective-permute-start | bytes 98312 | tf_op jit(solution)/shard_map/ppermute | solution.py:20
  25.8 5.1 %collective-permute-start.10 = (bf16[352,2048]{1,0:T(8,128)(2,1)}, bf16[352,2048]{1,0:T(8,128)(2,1)}, u32[]{:S(2)}, u32[]{:S(2)}) collective-permute-start(bf16[352,2048]{1,0:T(8,128)(2,1)} %bitcast.15), channel_id=1, source_target_pairs={{0,1},{1,0},{2,3},{3,2},{4,5},{5,4},{6,7},{7,6},{8,9},{9,8},{10,11... | collective-permute-start | bytes 4325384 | tf_op jit(solution)/shard_map/ppermute | solution.py:359
  25.8 5.6 %collective-permute-start.11 = (bf16[352,2048]{1,0:T(8,128)(2,1)}, bf16[352,2048]{1,0:T(8,128)(2,1)}, u32[]{:S(2)}, u32[]{:S(2)}) collective-permute-start(bf16[352,2048]{1,0:T(8,128)(2,1)} %bitcast.17), channel_id=1, source_target_pairs={{0,1},{1,0},{2,3},{3,2},{4,5},{5,4},{6,7},{7,6},{8,9},{9,8},{10,11... | collective-permute-start | bytes 4325384 | tf_op jit(solution)/shard_map/ppermute | solution.py:360
  30.9 1.6 collective-permute-start.6
  37.5 14.2 %collective-permute-start.12 = (bf16[128,2048]{1,0:T(8,128)(2,1)}, bf16[128,2048]{1,0:T(8,128)(2,1)S(1)}, u32[]{:S(2)}, u32[]{:S(2)}) collective-permute-start(bf16[128,2048]{1,0:T(8,128)(2,1)} %get-tuple-element.70.refs_0_), channel_id=1, source_target_pairs={{0,8},{2,10},{4,12},{6,14},{8,0},{10,2},{12,4},{14,6},{16,24},{18,... | collective-permute-start | bytes 1572872 | tf_op jit(solution)/shard_map/ppermute | solution.py:20
  37.9 17.2 %collective-permute-start.14 = (bf16[128,2048]{1,0:T(8,128)(2,1)}, bf16[128,2048]{1,0:T(8,128)(2,1)S(1)}, u32[]{:S(2)}, u32[]{:S(2)}) collective-permute-start(bf16[128,2048]{1,0:T(8,128)(2,1)} %get-tuple-element.70.refs_0_), channel_id=1, source_target_pairs={{8,16},{10,18},{12,20},{14,22},{16,8},{18,10},{20,12},{22,14},{9,1... | collective-permute-start | bytes 1572872 | tf_op jit(solution)/shard_map/ppermute | solution.py:230
  42.5 14.8 %collective-permute-start.17 = (bf16[128,2048]{1,0:T(8,128)(2,1)}, bf16[128,2048]{1,0:T(8,128)(2,1)S(1)}, u32[]{:S(2)}, u32[]{:S(2)}) collective-permute-start(bf16[128,2048]{1,0:T(8,128)(2,1)} %get-tuple-element.70.refs_0_), channel_id=1, source_target_pairs={{0,4},{1,3},{2,6},{3,1},{4,0},{5,7},{6,2},{7,5},{8,12},{9,11},{10,... | collective-permute-start | bytes 1572872 | tf_op jit(solution)/shard_map/ppermute | solution.py:26
  43.4 13.9 %collective-permute-start.16 = (bf16[128,2048]{1,0:T(8,128)(2,1)}, bf16[128,2048]{1,0:T(8,128)(2,1)S(1)}, u32[]{:S(2)}, u32[]{:S(2)}) collective-permute-start(bf16[128,2048]{1,0:T(8,128)(2,1)} %get-tuple-element.70.refs_0_), channel_id=1, source_target_pairs={{0,2},{1,5},{2,0},{3,7},{4,6},{5,1},{6,4},{7,3},{8,10},{9,13},{10,... | collective-permute-start | bytes 1572872 | tf_op jit(solution)/shard_map/ppermute | solution.py:26
  51.6 16.8 %collective-permute-start.13 = (bf16[128,2048]{1,0:T(8,128)(2,1)S(1)}, bf16[128,2048]{1,0:T(8,128)(2,1)}, u32[]{:S(2)}, u32[]{:S(2)}) collective-permute-start(bf16[128,2048]{1,0:T(8,128)(2,1)S(1)} %collective-permute-done.12.refs_0_), channel_id=1, source_target_pairs={{8,16},{10,18},{12,20},{14,22},{16,8},{18,10},{20,12},{22,14},{9,1... | collective-permute-start | bytes 1572872 | tf_op jit(solution)/shard_map/ppermute | solution.py:230
  55.1 15.0 %collective-permute-start.15 = (bf16[128,2048]{1,0:T(8,128)(2,1)S(1)}, bf16[128,2048]{1,0:T(8,128)(2,1)}, u32[]{:S(2)}, u32[]{:S(2)}) collective-permute-start(bf16[128,2048]{1,0:T(8,128)(2,1)S(1)} %collective-permute-done.14), channel_id=1, source_target_pairs={{8,0},{10,2},{12,4},{14,6},{16,24},{18,26},{20,28},{22,30},{9,1},{... | collective-permute-start | bytes 1572872 | tf_op jit(solution)/shard_map/ppermute | solution.py:230
  57.4 14.7 %collective-permute-start.18 = (bf16[128,2048]{1,0:T(8,128)(2,1)S(1)}, bf16[128,2048]{1,0:T(8,128)(2,1)S(1)}, u32[]{:S(2)}, u32[]{:S(2)}) collective-permute-start(bf16[128,2048]{1,0:T(8,128)(2,1)S(1)} %collective-permute-done.17.refs_2_), channel_id=1, source_target_pairs={{0,2},{1,5},{2,0},{3,7},{4,6},{5,1},{6,4},{7,3},{8,10},{9,13},{10,... | collective-permute-start | bytes 1572872 | tf_op jit(solution)/shard_map/ppermute | solution.py:26
  58.7 14.6 %collective-permute-start.20 = (bf16[128,2048]{1,0:T(8,128)(2,1)S(1)}, bf16[128,2048]{1,0:T(8,128)(2,1)S(1)}, u32[]{:S(2)}, u32[]{:S(2)}) collective-permute-start(bf16[128,2048]{1,0:T(8,128)(2,1)S(1)} %collective-permute-done.12.refs_0_), channel_id=1, source_target_pairs={{0,4},{1,3},{2,6},{3,1},{4,0},{5,7},{6,2},{7,5},{8,12},{9,11},{10,... | collective-permute-start | bytes 1572872 | tf_op jit(solution)/shard_map/ppermute | solution.py:26
  59.7 14.3 %collective-permute-start.19 = (f32[16,1024]{1,0:T(8,128)S(1)}, f32[16,1024]{1,0:T(8,128)S(1)}, u32[]{:S(2)}, u32[]{:S(2)}) collective-permute-start(f32[16,1024]{1,0:T(8,128)S(1)} %pad_maximum_fusion), channel_id=1, source_target_pairs={{0,2},{2,0},{4,6},{6,4},{8,10},{10,8},{12,14},{14,12},{16,18},{18,... | collective-permute-start | bytes 196616 | tf_op jit(solution)/shard_map/ppermute | solution.py:20
  68.5 11.8 %collective-permute-start.23 = (bf16[128,2048]{1,0:T(8,128)(2,1)}, bf16[128,2048]{1,0:T(8,128)(2,1)S(1)}, u32[]{:S(2)}, u32[]{:S(2)}) collective-permute-start(bf16[128,2048]{1,0:T(8,128)(2,1)} %collective-permute-done.13), channel_id=1, source_target_pairs={{8,0},{10,2},{12,4},{14,6},{16,24},{18,26},{20,28},{22,30},{9,1},{... | collective-permute-start | bytes 1572872 | tf_op jit(solution)/shard_map/ppermute | solution.py:230
  72.1 14.1 %collective-permute-start.21 = (bf16[128,2048]{1,0:T(8,128)(2,1)S(1)}, bf16[128,2048]{1,0:T(8,128)(2,1)S(1)}, u32[]{:S(2)}, u32[]{:S(2)}) collective-permute-start(bf16[128,2048]{1,0:T(8,128)(2,1)S(1)} %broadcast_select_fusion.1.refs_2_), channel_id=1, source_target_pairs={{0,2},{1,5},{2,0},{3,7},{4,6},{5,1},{6,4},{7,3},{8,10},{9,13},{10,... | collective-permute-start | bytes 1572872 | tf_op jit(solution)/shard_map/ppermute | solution.py:26
  73.2 13.2 %collective-permute-start.22 = (bf16[128,2048]{1,0:T(8,128)(2,1)S(1)}, bf16[128,2048]{1,0:T(8,128)(2,1)S(1)}, u32[]{:S(2)}, u32[]{:S(2)}) collective-permute-start(bf16[128,2048]{1,0:T(8,128)(2,1)S(1)} %broadcast_select_fusion.1.refs_2_), channel_id=1, source_target_pairs={{0,4},{1,3},{2,6},{3,1},{4,0},{5,7},{6,2},{7,5},{8,12},{9,11},{10,... | collective-permute-start | bytes 1572872 | tf_op jit(solution)/shard_map/ppermute | solution.py:26
  86.2 13.3 %collective-permute-start.24 = (bf16[128,2048]{1,0:T(8,128)(2,1)S(1)}, bf16[128,2048]{1,0:T(8,128)(2,1)S(1)}, u32[]{:S(2)}, u32[]{:S(2)}) collective-permute-start(bf16[128,2048]{1,0:T(8,128)(2,1)S(1)} %broadcast_select_fusion.refs_5_), channel_id=1, source_target_pairs={{0,2},{1,5},{2,0},{3,7},{4,6},{5,1},{6,4},{7,3},{8,10},{9,13},{10,... | collective-permute-start | bytes 1572872 | tf_op jit(solution)/shard_map/ppermute | solution.py:26
  86.5 13.3 %collective-permute-start.26 = (bf16[128,2048]{1,0:T(8,128)(2,1)S(1)}, bf16[128,2048]{1,0:T(8,128)(2,1)S(1)}, u32[]{:S(2)}, u32[]{:S(2)}) collective-permute-start(bf16[128,2048]{1,0:T(8,128)(2,1)S(1)} %broadcast_select_fusion.refs_5_), channel_id=1, source_target_pairs={{0,4},{1,3},{2,6},{3,1},{4,0},{5,7},{6,2},{7,5},{8,12},{9,11},{10,... | collective-permute-start | bytes 1572872 | tf_op jit(solution)/shard_map/ppermute | solution.py:26
  86.5 13.3 %collective-permute-start.27 = (bf16[128,2048]{1,0:T(8,128)(2,1)S(1)}, bf16[128,2048]{1,0:T(8,128)(2,1)S(1)}, u32[]{:S(2)}, u32[]{:S(2)}) collective-permute-start(bf16[128,2048]{1,0:T(8,128)(2,1)S(1)} %collective-permute-done.16.refs_1_), channel_id=1, source_target_pairs={{0,8},{2,10},{4,12},{6,14},{8,0},{10,2},{12,4},{14,6},{16,24},{18,... | collective-permute-start | bytes 1572872 | tf_op jit(solution)/shard_map/ppermute | solution.py:20
  99.5 12.4 %collective-permute-start.25 = (bf16[128,2048]{1,0:T(8,128)(2,1)S(1)}, bf16[128,2048]{1,0:T(8,128)(2,1)S(1)}, u32[]{:S(2)}, u32[]{:S(2)}) collective-permute-start(bf16[128,2048]{1,0:T(8,128)(2,1)S(1)} %collective-permute-done.22.refs_4_), channel_id=1, source_target_pairs={{0,2},{1,5},{2,0},{3,7},{4,6},{5,1},{6,4},{7,3},{8,10},{9,13},{10,... | collective-permute-start | bytes 1572872 | tf_op jit(solution)/shard_map/ppermute | solution.py:26
  99.8 12.1 %collective-permute-start.28 = (bf16[128,2048]{1,0:T(8,128)(2,1)S(1)}, bf16[128,2048]{1,0:T(8,128)(2,1)S(1)}, u32[]{:S(2)}, u32[]{:S(2)}) collective-permute-start(bf16[128,2048]{1,0:T(8,128)(2,1)S(1)} %collective-permute-done.24.refs_0_), channel_id=1, source_target_pairs={{0,4},{1,3},{2,6},{3,1},{4,0},{5,7},{6,2},{7,5},{8,12},{9,11},{10,... | collective-permute-start | bytes 1572872 | tf_op jit(solution)/shard_map/ppermute | solution.py:26
  99.8 15.7 %collective-permute-start.36 = (bf16[128,2048]{1,0:T(8,128)(2,1)S(1)}, bf16[128,2048]{1,0:T(8,128)(2,1)S(1)}, u32[]{:S(2)}, u32[]{:S(2)}) collective-permute-start(bf16[128,2048]{1,0:T(8,128)(2,1)S(1)} %collective-permute-done.18.refs_3_), channel_id=1, source_target_pairs={{0,8},{2,10},{4,12},{6,14},{8,0},{10,2},{12,4},{14,6},{16,24},{18,... | collective-permute-start | bytes 1572872 | tf_op jit(solution)/shard_map/ppermute | solution.py:20
  115.1 12.2 %collective-permute-start.30 = (bf16[128,2048]{1,0:T(8,128)(2,1)S(1)}, bf16[128,2048]{1,0:T(8,128)(2,1)S(1)}, u32[]{:S(2)}, u32[]{:S(2)}) collective-permute-start(bf16[128,2048]{1,0:T(8,128)(2,1)S(1)} %get-tuple-element.99), channel_id=1, source_target_pairs={{0,4},{1,3},{2,6},{3,1},{4,0},{5,7},{6,2},{7,5},{8,12},{9,11},{10,... | collective-permute-start | bytes 1572872 | tf_op jit(solution)/shard_map/ppermute | solution.py:26
  115.2 12.2 %collective-permute-start.29 = (bf16[128,2048]{1,0:T(8,128)(2,1)S(1)}, bf16[128,2048]{1,0:T(8,128)(2,1)S(1)}, u32[]{:S(2)}, u32[]{:S(2)}) collective-permute-start(bf16[128,2048]{1,0:T(8,128)(2,1)S(1)} %get-tuple-element.97), channel_id=1, source_target_pairs={{0,2},{1,5},{2,0},{3,7},{4,6},{5,1},{6,4},{7,3},{8,10},{9,13},{10,... | collective-permute-start | bytes 1572872 | tf_op jit(solution)/shard_map/ppermute | solution.py:26
  115.6 16.3 %collective-permute-start.37 = (bf16[128,2048]{1,0:T(8,128)(2,1)S(1)}, bf16[128,2048]{1,0:T(8,128)(2,1)S(1)}, u32[]{:S(2)}, u32[]{:S(2)}) collective-permute-start(bf16[128,2048]{1,0:T(8,128)(2,1)S(1)} %get-tuple-element.111), channel_id=1, source_target_pairs={{0,8},{2,10},{4,12},{6,14},{8,0},{10,2},{12,4},{14,6},{16,24},{18,... | collective-permute-start | bytes 1572872 | tf_op jit(solution)/shard_map/ppermute | solution.py:20
  127.4 11.6 %collective-permute-start.34 = (bf16[128,2048]{1,0:T(8,128)(2,1)S(1)}, bf16[128,2048]{1,0:T(8,128)(2,1)S(1)}, u32[]{:S(2)}, u32[]{:S(2)}) collective-permute-start(bf16[128,2048]{1,0:T(8,128)(2,1)S(1)} %add_convert_fusion.8), channel_id=1, source_target_pairs={{0,2},{1,5},{2,0},{3,7},{4,6},{5,1},{6,4},{7,3},{8,10},{9,13},{10,... | collective-permute-start | bytes 1572872 | tf_op jit(solution)/shard_map/ppermute | solution.py:26
  128.6 12.1 %collective-permute-start.31 = (bf16[128,2048]{1,0:T(8,128)(2,1)S(1)}, bf16[128,2048]{1,0:T(8,128)(2,1)S(1)}, u32[]{:S(2)}, u32[]{:S(2)}) collective-permute-start(bf16[128,2048]{1,0:T(8,128)(2,1)S(1)} %get-tuple-element.100), channel_id=1, source_target_pairs={{0,4},{1,3},{2,6},{3,1},{4,0},{5,7},{6,2},{7,5},{8,12},{9,11},{10,... | collective-permute-start | bytes 1572872 | tf_op jit(solution)/shard_map/ppermute | solution.py:26
  131.9 11.6 %collective-permute-start.38 = (bf16[128,2048]{1,0:T(8,128)(2,1)S(1)}, bf16[128,2048]{1,0:T(8,128)(2,1)S(1)}, u32[]{:S(2)}, u32[]{:S(2)}) collective-permute-start(bf16[128,2048]{1,0:T(8,128)(2,1)S(1)} %expert_rows.9), channel_id=1, source_target_pairs={{0,8},{2,10},{4,12},{6,14},{8,0},{10,2},{12,4},{14,6},{16,24},{18,... | collective-permute-start | bytes 1572872 | tf_op jit(solution)/shard_map/ppermute | solution.py:20
  139.0 12.1 %collective-permute-start.35 = (bf16[128,2048]{1,0:T(8,128)(2,1)S(1)}, bf16[128,2048]{1,0:T(8,128)(2,1)S(1)}, u32[]{:S(2)}, u32[]{:S(2)}) collective-permute-start(bf16[128,2048]{1,0:T(8,128)(2,1)S(1)} %get-tuple-element.106), channel_id=1, source_target_pairs={{0,2},{1,5},{2,0},{3,7},{4,6},{5,1},{6,4},{7,3},{8,10},{9,13},{10,... | collective-permute-start | bytes 1572872 | tf_op jit(solution)/shard_map/ppermute | solution.py:26
  140.7 13.0 %collective-permute-start.32 = (bf16[128,2048]{1,0:T(8,128)(2,1)S(1)}, bf16[128,2048]{1,0:T(8,128)(2,1)S(1)}, u32[]{:S(2)}, u32[]{:S(2)}) collective-permute-start(bf16[128,2048]{1,0:T(8,128)(2,1)S(1)} %add_convert_fusion.9), channel_id=1, source_target_pairs={{0,4},{1,3},{2,6},{3,1},{4,0},{5,7},{6,2},{7,5},{8,12},{9,11},{10,... | collective-permute-start | bytes 1572872 | tf_op jit(solution)/shard_map/ppermute | solution.py:26
  143.5 12.7 %collective-permute-start.39 = (bf16[128,2048]{1,0:T(8,128)(2,1)S(1)}, bf16[128,2048]{1,0:T(8,128)(2,1)S(1)}, u32[]{:S(2)}, u32[]{:S(2)}) collective-permute-start(bf16[128,2048]{1,0:T(8,128)(2,1)S(1)} %add_convert_fusion.7), channel_id=1, source_target_pairs={{0,8},{2,10},{4,12},{6,14},{24,16},{26,18},{28,20},{30,22},{1,9},{... | collective-permute-start | bytes 1572872 | tf_op jit(solution)/shard_map/ppermute | solution.py:230
  151.1 12.1 %collective-permute-start.44 = (bf16[128,2048]{1,0:T(8,128)(2,1)S(1)}, bf16[128,2048]{1,0:T(8,128)(2,1)S(1)}, u32[]{:S(2)}, u32[]{:S(2)}) collective-permute-start(bf16[128,2048]{1,0:T(8,128)(2,1)S(1)} %add_convert_fusion.2), channel_id=1, source_target_pairs={{0,2},{1,5},{2,0},{3,7},{4,6},{5,1},{6,4},{7,3},{8,10},{9,13},{10,... | collective-permute-start | bytes 1572872 | tf_op jit(solution)/shard_map/ppermute | solution.py:26
  153.7 9.7 %collective-permute-start.33 = (bf16[128,2048]{1,0:T(8,128)(2,1)S(1)}, bf16[128,2048]{1,0:T(8,128)(2,1)S(1)}, u32[]{:S(2)}, u32[]{:S(2)}) collective-permute-start(bf16[128,2048]{1,0:T(8,128)(2,1)S(1)} %get-tuple-element.102), channel_id=1, source_target_pairs={{0,4},{1,3},{2,6},{3,1},{4,0},{5,7},{6,2},{7,5},{8,12},{9,11},{10,... | collective-permute-start | bytes 1572872 | tf_op jit(solution)/shard_map/ppermute | solution.py:26
  156.5 11.3 %collective-permute-start.40 = (bf16[128,2048]{1,0:T(8,128)(2,1)S(1)}, bf16[128,2048]{1,0:T(8,128)(2,1)S(1)}, u32[]{:S(2)}, u32[]{:S(2)}) collective-permute-start(bf16[128,2048]{1,0:T(8,128)(2,1)S(1)} %add_convert_fusion.6), channel_id=1, source_target_pairs={{8,16},{10,18},{12,20},{14,22},{16,8},{18,10},{20,12},{22,14},{9,1... | collective-permute-start | bytes 1572872 | tf_op jit(solution)/shard_map/ppermute | solution.py:230
  158.6 11.3 %collective-permute-start.41 = (bf16[128,2048]{1,0:T(8,128)(2,1)S(1)}, bf16[128,2048]{1,0:T(8,128)(2,1)S(1)}, u32[]{:S(2)}, u32[]{:S(2)}) collective-permute-start(bf16[128,2048]{1,0:T(8,128)(2,1)S(1)} %add_convert_fusion.6), channel_id=1, source_target_pairs={{0,8},{2,10},{4,12},{6,14},{24,16},{26,18},{28,20},{30,22},{1,9},{... | collective-permute-start | bytes 1572872 | tf_op jit(solution)/shard_map/ppermute | solution.py:230
  163.3 20.2 %copy-start.4 = (f32[128,2048]{1,0:T(8,128)S(1)}, f32[128,2048]{1,0:T(8,128)}, u32[]{:S(2)}) copy-start(f32[128,2048]{1,0:T(8,128)} %get-tuple-element.68) | copy-start | bytes 3145732
  163.4 11.2 %collective-permute-start.46 = (bf16[128,2048]{1,0:T(8,128)(2,1)S(1)}, bf16[128,2048]{1,0:T(8,128)(2,1)S(1)}, u32[]{:S(2)}, u32[]{:S(2)}) collective-permute-start(bf16[128,2048]{1,0:T(8,128)(2,1)S(1)} %add_convert_fusion.1), channel_id=1, source_target_pairs={{0,4},{1,3},{2,6},{3,1},{4,0},{5,7},{6,2},{7,5},{8,12},{9,11},{10,... | collective-permute-start | bytes 1572872 | tf_op jit(solution)/shard_map/ppermute | solution.py:26
  165.7 9.2 %collective-permute-start.45 = (bf16[128,2048]{1,0:T(8,128)(2,1)S(1)}, bf16[128,2048]{1,0:T(8,128)(2,1)S(1)}, u32[]{:S(2)}, u32[]{:S(2)}) collective-permute-start(bf16[128,2048]{1,0:T(8,128)(2,1)S(1)} %add_convert_fusion.3), channel_id=1, source_target_pairs={{0,2},{1,5},{2,0},{3,7},{4,6},{5,1},{6,4},{7,3},{8,10},{9,13},{10,... | collective-permute-start | bytes 1572872 | tf_op jit(solution)/shard_map/ppermute | solution.py:26
  170.1 11.3 %collective-permute-start.43 = (bf16[128,2048]{1,0:T(8,128)(2,1)S(1)}, bf16[128,2048]{1,0:T(8,128)(2,1)S(1)}, u32[]{:S(2)}, u32[]{:S(2)}) collective-permute-start(bf16[128,2048]{1,0:T(8,128)(2,1)S(1)} %add_convert_fusion.4), channel_id=1, source_target_pairs={{8,16},{10,18},{12,20},{14,22},{16,8},{18,10},{20,12},{22,14},{9,1... | collective-permute-start | bytes 1572872 | tf_op jit(solution)/shard_map/ppermute | solution.py:230
  174.2 9.2 %collective-permute-start.42 = (bf16[128,2048]{1,0:T(8,128)(2,1)S(1)}, bf16[128,2048]{1,0:T(8,128)(2,1)S(1)}, u32[]{:S(2)}, u32[]{:S(2)}) collective-permute-start(bf16[128,2048]{1,0:T(8,128)(2,1)S(1)} %add_convert_fusion.5), channel_id=1, source_target_pairs={{0,8},{2,10},{4,12},{6,14},{8,0},{10,2},{12,4},{14,6},{16,24},{18,... | collective-permute-start | bytes 1572872 | tf_op jit(solution)/shard_map/ppermute | solution.py:20
  (9 other events, 41.8 us)
